TPU v7x, 32 devices: a whole 2x2x4 slice. The times are simulated.
32 devices in a mesh: batch: 2 (over y), orient: 8 (over z, core), cls: 2 (over x), rep: 1.
Axes of the slice: x: 2, y: 2, z: 4, core: 2. Of those that a mesh axis runs over, the one named last changes fastest.
Arguments:
- images: bfloat16 [4, 128, 2, 7296], P(('batch', 'cls'), 'orient', 'rep'), parts along dimension 0, may hold values from -9.5 to 9.5
- defocus: bfloat16 [4, 128], P(('batch', 'cls'), 'orient'), parts along dimension 0, may hold values from 0.5 to 2
- block_ids: int32 [4, 128, 4], P(('batch', 'cls'), 'orient'), parts along dimension 0, may hold values from 0 to 7, all different within a row; in each aligned block of 16 rows (0 to 15, 16 to 31, ..., all dimensions but the last counted through in order) at most 16 rows name the same one
- noise_weight: float32 [7296], replicated, may hold values from 0.02 to 0.2
- panels: bfloat16 [4, 8, 128, 2, 7296], P(('batch', 'cls'), 'orient', None, 'rep'), parts along dimension 0, may hold values from -4 to 4
Outputs:
- posteriors: float32 [4, 8, 128, 256], P(('batch', 'cls'), 'orient', None, 'rep'), parts along dimension 0
There are 2 independent parts, one for each index of `batch`. A program takes and returns all parts, laid end to end along the dimension named above; an argument that names none is the same for every part. Nothing has to cross between parts.
Inputs may be any that keep to these rules, and one draw needn't show every extreme that they name: `block_ids`: each particle names 4 different blocks; among the 16 particles of one index of orient (aligned runs of 16 rows over the first two dimensions) no block is named more than 16 times, and 16 is reached.
All inputs are finite; a program needn't handle non-finite values.
Results may differ from a plain program's by a relative error of at most 0.0215.
Values may be sent and summed in bfloat16 or wider, within the bound.
No kernel may reach another device: no remote copies, remote signals or barrier semaphores. Data moves between devices by JAX's collectives and lax.ppermute only.
A program may use at most 64 MiB of HBM per device.

v0:
```python
import jax
import jax.numpy as jnp
from jax import lax
from jax.sharding import PartitionSpec as P

CTF_PHASE = 40.0
FLOOR = -1e30


def spread_max(member, is_live, values):
    picked = jnp.max(jnp.where(member, values[None, :], FLOOR), axis=1)
    return jnp.where(is_live, picked, 0.0)


def collect_sums(member, expo):
    return jnp.sum(jnp.where(member, jnp.sum(expo, axis=1)[:, None], 0.0), axis=0)


def shards(images, defocus, block_ids, noise_weight, panels):
    per_device = images.shape[1]
    columns = images.shape[3]
    devices = lax.axis_size("orient")
    local_search = block_ids.shape[2]
    slots_each = min(per_device, max(2, 2 * per_device * local_search // devices))
    capacity = slots_each * devices
    everyone = per_device * devices
    all_lists = lax.all_gather(block_ids[0], "orient", axis=0, tiled=True)
    all_rows, all_focus = (
        lax.all_gather(images[0], "orient", axis=0, tiled=True),
        lax.all_gather(defocus[0], "orient", axis=0, tiled=True),
    )
    own_block = lax.axis_index("orient")
    block_hits = (
        jnp.any(all_lists == own_block, axis=1).astype(jnp.int32).reshape(devices, per_device)
    )
    slot_rank = jnp.cumsum(block_hits, axis=1) - block_hits
    places = (jnp.arange(devices, dtype=jnp.int32)[:, None] * slots_each + slot_rank).reshape(
        everyone
    )
    chosen = (places[None, :] == jnp.arange(capacity, dtype=jnp.int32)[:, None]) & (
        block_hits.reshape(everyone)[None, :] == 1
    )
    is_live = jnp.any(chosen, axis=1)
    slot_owner = jnp.sum(
        jnp.where(chosen, jnp.arange(everyone, dtype=jnp.int32)[None, :], 0), axis=1
    )
    slot_rows = jnp.take(all_rows, slot_owner, axis=0)
    slot_focus = jnp.take(all_focus, slot_owner, axis=0).astype(jnp.float32)
    frequency = (jnp.arange(columns, dtype=jnp.float32) + 0.5) / columns
    contrast = -jnp.sin(CTF_PHASE * slot_focus[:, None] * frequency[None, :] + 0.1)
    weighted = contrast * noise_weight[None, :]
    scaled_rows = (weighted[:, None, :] * slot_rows.astype(jnp.float32)).astype(jnp.bfloat16)
    energy = (contrast * weighted).astype(jnp.bfloat16)
    piece = lax.all_gather(panels[:, 0], "cls", axis=0, tiled=True)
    widened = piece.astype(jnp.float32)
    squared = (widened * widened).astype(jnp.bfloat16)
    correlate = jnp.einsum("srk,cjrk->scj", scaled_rows, piece, preferred_element_type=jnp.float32)
    energy_term = jnp.einsum("sk,cjrk->scj", energy, squared, preferred_element_type=jnp.float32)
    terms = correlate - 0.5 * energy_term
    combined = terms.reshape(capacity, -1)
    scores = lax.psum_scatter(combined, "rep", scatter_dimension=1, tiled=True)
    member = (slot_owner[:, None] == jnp.arange(everyone, dtype=jnp.int32)[None, :]) & is_live[
        :, None
    ]
    slot_top = jnp.max(scores, axis=1)
    local_peak = jnp.max(jnp.where(member, slot_top[:, None], FLOOR), axis=0)
    peak = lax.pmax(local_peak, ("orient", "rep"))
    slot_peak = spread_max(member, is_live, peak)
    expo = jnp.where(is_live[:, None], jnp.exp(scores - slot_peak[:, None]), 0.0)
    total = lax.psum(collect_sums(member, expo), ("orient", "rep"))
    slot_total = jnp.where(is_live, jnp.sum(jnp.where(member, total[None, :], 0.0), axis=1), 1.0)
    posterior = expo / slot_total[:, None]
    return posterior.reshape(1, 1, capacity, -1)


def solution(mesh):
    in_specs = (
        P(("batch", "cls"), "orient", "rep", None),
        P(("batch", "cls"), "orient"),
        P(("batch", "cls"), "orient", None),
        P(),
        P(("batch", "cls"), "orient", None, "rep", None),
    )
    out_specs = P(("batch", "cls"), "orient", None, "rep")
    return jax.shard_map(shards, mesh=mesh, in_specs=in_specs, out_specs=out_specs, check_vma=False)
```

profile of v0, /device:TPU:0, one launch (start us, length us, event | category | flops | bytes accessed | tf_op | source)
XLA Modules:
  0.0 208.8 jit_solution(4104390490345364379)
XLA Ops:
  6.5 0.0 all-gather.7.cloned.1.call-start
  6.5 0.7 all-gather.7.cloned.1.call-update
  7.3 0.0 all-gather.9.cloned.1.call-start
  7.3 4.3 %copy.29 = bf16[1,1,128,2,7296]{4,2,3,1,0:T(8,128)(2,1)} copy(bf16[1,1,128,2,7296]{4,3,2,1,0:T(2,128)(2,1)} %param.9) | data formatting | bytes 7471104 | tf_op args[4]
  11.6 0.0 copy-start.4
  11.6 0.0 copy-start.6
  11.6 0.0 copy-start.5
  11.6 0.0 copy-start.3
  11.6 0.0 all-gather.9.cloned.1.call-update
  11.7 0.1 add.65
  11.8 0.1 add.66
  11.8 0.5 copy-done.4
  12.3 0.1 copy.26
  12.4 15.9 %all-gather = s32[1,128,4]{2,0,1:T(1,128)S(1)} all-gather(s32[1,16,4]{2,0,1:T(1,128)S(1)} %copy.26), channel_id=2, replica_groups=mesh['batch'=2,'orient'=8,'cls'=2,'rep'=1] {'orient'}, dimensions={1}, use_global_device_ids=true | all-gather | bytes 2304 | tf_op jit(solution)/shard_map/all_gather | solution.py:27
  28.3 2.4 %compare_reduce_fusion = pred[128]{0:T(512)(128)(4,1)S(1)} fusion(s32[1,128,4]{2,0,1:T(1,128)S(1)} %all-gather, s32[]{:T(128)S(6)} %axis_index.15), kind=kLoop, calls=%fused_computation.23 | loop fusion | flops 896 | bytes 2180 | tf_op jit(solution)/shard_map/reduce_or | solution.py:34
  30.6 0.1 reshape.204
  30.7 0.2 reduce_window_sum.13
  30.9 0.1 reduce_window_sum.14
  31.0 0.0 copy-done.6
  31.0 0.6 dynamic-slice
  32.2 0.0 copy-done.5
  32.2 0.2 dynamic-update-slice
  32.5 17.3 %all-reduce = bf16[128]{0:T(256)(128)(2,1)S(1)} all-reduce(bf16[128]{0:T(256)(128)(2,1)S(1)} %dynamic-update-slice), channel_id=3, replica_groups=mesh['batch'=2,'orient'=8,'cls'=2,'rep'=1] {'orient'}, use_global_device_ids=true, to_apply=%add | all-reduce | flops 128 | bytes 512 | tf_op jit(solution)/shard_map/all_gather | solution.py:30
  49.8 0.1 select_reduce_fusion.5
  50.0 1.2 gather_fusion
  51.2 0.1 fusion.29
  51.3 0.0 copy-done.3
  51.3 13.7 %fusion.5 = f32[128,7296]{1,0:T(8,128)} fusion(f32[7296]{0:T(1024)S(1)} %copy-done.3, f32[7296]{0:T(1024)S(1)} %add_multiply_fusion, f32[128]{0:T(128)S(1)} %get-tuple-element.5), kind=kLoop, calls=%fused_computation.12 | loop fusion | flops 3735552 | bytes 3794432 | tf_op jit(solution)/shard_map/mul | solution.py:51
  65.0 0.0 all-gather.7.cloned.1.call-done
  65.0 14.2 %gather_fusion.1 = bf16[128,2,7296]{2,1,0:T(2,128)(2,1)} fusion(bf16[128,2,7296]{2,1,0:T(2,128)(2,1)} %bitcast.39, s32[1024]{0:T(1024)S(1)} %pad_clamp_fusion), kind=kCustom, calls=%fused_computation.1 | custom fusion | bytes 7471616 | tf_op jit(solution)/shard_map/jit(_take)/gather | solution.py:47
  79.2 70.3 %all-gather.9.cloned.1.call-done = bf16[2,1,128,2,7296]{4,2,3,1,0:T(8,128)(2,1)} async-done(((bf16[1,1,128,2,7296]{4,2,3,1,0:T(8,128)(2,1)}), bf16[2,1,128,2,7296]{4,2,3,1,0:T(8,128)(2,1)}) %all-gather.9.cloned.1.call-update) | async-done | bytes 7471120 | tf_op jit(solution)/shard_map/all_gather | solution.py:54
  149.6 0.0 copy-start.1
  149.6 5.1 %convert_reduce_fusion = bf16[2,128,7296]{2,1,0:T(8,128)(2,1)S(1)} fusion(bf16[2,1,128,2,7296]{4,2,3,1,0:T(8,128)(2,1)} %all-gather.9.cloned.1.call-done), kind=kLoop, calls=%fused_computation.2 | loop fusion | flops 16809984 | bytes 11206656 | tf_op jit(solution)/shard_map/sk,cjrk->scj/reduce_sum | solution.py:58
  154.6 0.0 copy-start
  154.7 13.2 %fusion.24 = f32[128,2,128]{0,2,1:T(8,128)S(1)} fusion(bf16[2,128,7296]{2,1,0:T(8,128)(2,1)S(1)} %convert_reduce_fusion, f32[7296]{0:T(1024)S(1)} %add_multiply_fusion, f32[128]{0:T(128)S(1)} %get-tuple-element.5, f32[7296]{0:T(1024)S(1)} %copy-done.3), kind=kOutput, calls=%fused_computation.22 | convolution fusion | flops 483786752 | bytes 3925504 | tf_op jit(solution)/shard_map/sk,cjrk->scj/dot_general | solution.py:58
  167.9 0.0 copy-done.1
  167.9 0.0 copy-done.2
  167.9 0.0 copy-done
  167.9 2.5 %fusion.34 = (f32[128]{0:T(128)S(1)}, f32[128,2,128]{0,2,1:T(8,128)S(1)}) fusion(f32[128,2,128]{0,2,1:T(8,128)S(1)} %fusion.24, bf16[2,1,128,2,7296]{4,2,3,1,0:T(8,128)(2,1)S(1)} %copy-done, bf16[128,2,7296]{2,1,0:T(2,128)(2,1)S(1)} %copy-done.2, f32[128,7296]{1,0:T(8,128)S(1)} %copy-done.1, pred[128]{0:T(512)(128)(4,1)S(1)} %get-tuple-element.6), kind=kOutput, calls=%fused_computation.50 | convolution fusion | flops 963837824 | bytes 15204992 | tf_op jit(solution)/shard_map/srk,cjrk->scj/dot_general | solution.py:57
  170.4 0.1 copy.30
  170.5 0.1 select_reduce_fusion.4
  170.7 16.3 %pmax.7 = f32[128]{0:T(128)S(1)} all-reduce(f32[128]{0:T(128)S(1)} %select_reduce_fusion.4), channel_id=1, replica_groups=mesh['batch'=2,'orient'=8,'cls'=2,'rep'=1] {'orient','rep'}, use_global_device_ids=true, to_apply=%region_7.8 | all-reduce | flops 128 | bytes 1024 | tf_op jit(solution)/shard_map/pmax | solution.py:67
  187.0 0.2 select_reduce_fusion.3
  187.2 0.1 select_reduce_fusion
  187.3 0.1 select_reduce_fusion.2
  187.4 13.6 %psum.7 = f32[128]{0:T(128)S(1)} all-reduce(f32[128]{0:T(128)S(1)} %select_reduce_fusion.2), channel_id=1, replica_groups=mesh['batch'=2,'orient'=8,'cls'=2,'rep'=1] {'orient','rep'}, use_global_device_ids=true, to_apply=%region_11.12 | all-reduce | flops 128 | bytes 1024 | tf_op jit(solution)/shard_map/psum | solution.py:70
  201.0 0.2 select_reduce_fusion.1
  201.2 0.8 select_divide_fusion
  (11 shorter events, 0.1 us)
Async XLA Ops:
  6.5 58.5 %all-gather.7.cloned.1.call-start = ((), (), s32[]{:S(2)}) async-start(), calls=%async_computation | async-start | bytes 4202496 | tf_op jit(solution)/shard_map/all_gather | solution.py:29
  7.3 142.3 %all-gather.9.cloned.1.call-start = ((), (), s32[]{:S(2)}) async-start(), calls=%async_computation.1 | async-start | bytes 11206656 | tf_op jit(solution)/shard_map/all_gather | solution.py:54
  11.6 0.7 copy-start.4
  11.6 19.3 %copy-start.6 = (u32[32]{0:T(128)S(1)}, u32[32]{0:T(128)}, u32[]{:S(2)}) copy-start(u32[32]{0:T(128)} %constant.68) | copy-start | bytes 388
  11.6 20.6 %copy-start.5 = (bf16[1,16]{1,0:T(2,128)(2,1)S(1)}, bf16[1,16]{1,0:T(2,128)(2,1)}, u32[]{:S(2)}) copy-start(bf16[1,16]{1,0:T(2,128)(2,1)} %param.6) | copy-start | bytes 100
  11.6 39.7 %copy-start.3 = (f32[7296]{0:T(1024)S(1)}, f32[7296]{0:T(1024)}, u32[]{:S(2)}) copy-start(f32[7296]{0:T(1024)} %param.8) | copy-start | bytes 87556
  149.6 18.4 %copy-start.1 = (f32[128,7296]{1,0:T(8,128)S(1)}, f32[128,7296]{1,0:T(8,128)}, u32[]{:S(2)}) copy-start(f32[128,7296]{1,0:T(8,128)} %fusion.5) | copy-start | bytes 11206660
  149.6 18.4 %copy-start.2 = (bf16[128,2,7296]{2,1,0:T(2,128)(2,1)S(1)}, bf16[128,2,7296]{2,1,0:T(2,128)(2,1)}, u32[]{:S(2)}) copy-start(bf16[128,2,7296]{2,1,0:T(2,128)(2,1)} %gather_fusion.1) | copy-start | bytes 11206660
  154.6 13.3 %copy-start = (bf16[2,1,128,2,7296]{4,2,3,1,0:T(8,128)(2,1)S(1)}, bf16[2,1,128,2,7296]{4,2,3,1,0:T(8,128)(2,1)}, u32[]{:S(2)}) copy-start(bf16[2,1,128,2,7296]{4,2,3,1,0:T(8,128)(2,1)} %all-gather.9.cloned.1.call-done) | copy-start | bytes 22413316
Sparse Core Ops, SparseCore 0:
  9.0 46.3 all-gather.6
  56.9 92.5 all-gather.8
where the time goes:
time: 209 us
  waiting for transfers between devices  71.1 us (34%)
  blocking collectives  63.1 us (30%)
  other arithmetic  23.1 us (11%)
  local copies, waits for them, and re-layouts  21.6 us (10%)
  matrix products  15.7 us (8%)
  between operations  14.2 us (7%)
    all_gather x1, waiting for transfers between devices, shards(): piece = lax.all_gather(panels[:, 0], 'cls', axis=0, tiled=True)  70.3 us
    all_gather x1, blocking collectives, shards(): lax.all_gather(defocus[0], 'orient', axis=0, tiled=True)  17.3 us
    pmax x1, blocking collectives, shards(): peak = lax.pmax(local_peak, ('orient', 'rep'))  16.3 us
    all_gather x1, blocking collectives, shards(): all_lists = lax.all_gather(block_ids[0], 'orient', axis=0, tiled=True)  15.9 us
    gather x1, local copies, waits for them, and re-layouts, shards(): slot_rows = jnp.take(all_rows, slot_owner, axis=0)  14.2 us
    mul x1, other arithmetic, shards(): weighted = contrast * noise_weight[None, :]  13.7 us
    psum x1, blocking collectives, shards(): total = lax.psum(collect_sums(member, expo), ('orient', 'rep'))  13.6 us
    dot_general x1, matrix products, shards(): jnp.einsum('sk,cjrk->scj', energy, squared, preferred_element_type=jnp.fl...  13.2 us
  transfers between devices with their start and end apart: 2, of which 1 were waited for; matrix products, arithmetic and copies ran while one was open for 18% of the time, Pallas kernels for 0%

commit v1 on v0

--- a/solution.py
+++ b/solution.py
@@ -1,10 +1,196 @@
+import functools
+
 import jax
 import jax.numpy as jnp
 from jax import lax
+from jax.experimental import pallas as pl
+from jax.experimental.pallas import tpu as pltpu
 from jax.sharding import PartitionSpec as P
 
 CTF_PHASE = 40.0
 FLOOR = -1e30
+LANES = 128
+
+
+def score_kernel(chunks, tiles, columns, *refs):
+    rows = refs[:chunks]
+    meta = refs[chunks : 2 * chunks]
+    noise, own_panel, mate_panel, own_out, mate_out, sin_a, cos_a, sin_b, cos_b = refs[2 * chunks :]
+    step = pl.program_id(0)
+    count = sin_a.shape[0]
+
+    @pl.when(step == 0)
+    def _():
+        focus = jnp.concatenate([m[:, 0:1] for m in meta], axis=0).astype(jnp.float32)
+        rate = CTF_PHASE * focus
+        lane = lax.broadcasted_iota(jnp.int32, (count, LANES), 1).astype(jnp.float32)
+        coarse = rate * (lane * (LANES / columns)) + 0.1
+        fine = rate * ((lane + 0.5) / columns)
+        sin_a[...] = jnp.sin(coarse)
+        cos_a[...] = jnp.cos(coarse)
+        sin_b[...] = jnp.sin(fine)
+        cos_b[...] = jnp.cos(fine)
+        own_out[...] = jnp.zeros_like(own_out)
+        mate_out[...] = jnp.zeros_like(mate_out)
+
+    shift = lax.rem(LANES - step * tiles, LANES)
+    sa = pltpu.roll(sin_a[...], shift, 1)
+    ca = pltpu.roll(cos_a[...], shift, 1)
+    sb = sin_b[...]
+    cb = cos_b[...]
+    scaled_parts, energy_parts = [], []
+    for t in range(tiles):
+        window = slice(t * LANES, (t + 1) * LANES)
+        contrast = -(sa[:, t : t + 1] * cb + ca[:, t : t + 1] * sb)
+        weighted = contrast * noise[:, window]
+        image = jnp.concatenate([r[:, window] for r in rows], axis=0).astype(jnp.float32)
+        scaled_parts.append((weighted * image).astype(jnp.bfloat16))
+        energy_parts.append((-0.5 * (contrast * weighted)).astype(jnp.bfloat16))
+    scaled = jnp.concatenate(scaled_parts, axis=1)
+    energy = jnp.concatenate(energy_parts, axis=1)
+    for panel, out in ((own_panel, own_out), (mate_panel, mate_out)):
+        values = panel[...]
+        wide = values.astype(jnp.float32)
+        squared = (wide * wide).astype(jnp.bfloat16)
+        contract = (((1,), (1,)), ((), ()))
+        out[...] += lax.dot_general(
+            scaled, values, contract, preferred_element_type=jnp.float32
+        ) + lax.dot_general(energy, squared, contract, preferred_element_type=jnp.float32)
+
+
+def partial_scores(chunks, noise, own_panel, mate_panel):
+    each = chunks[0].shape[0]
+    columns = own_panel.shape[1]
+    orientations = own_panel.shape[0]
+    whole = columns // LANES
+    steps = next(s for s in (3, 2, 4, 5, 6, 7, 1) if whole % s == 0)
+    tiles = whole // steps
+    width = tiles * LANES
+    count = each * len(chunks)
+    n = len(chunks)
+    row_spec = pl.BlockSpec((each, width), lambda s: (0, s))
+    meta_spec = pl.BlockSpec((each, LANES), lambda s: (0, whole))
+    panel_spec = pl.BlockSpec((orientations, width), lambda s: (0, s))
+    out_spec = pl.BlockSpec((count, orientations), lambda s: (0, 0))
+    return pl.pallas_call(
+        functools.partial(score_kernel, n, tiles, columns),
+        grid=(steps,),
+        in_specs=[row_spec] * n
+        + [meta_spec] * n
+        + [pl.BlockSpec((1, width), lambda s: (0, s)), panel_spec, panel_spec],
+        out_specs=[out_spec, out_spec],
+        out_shape=[jax.ShapeDtypeStruct((count, orientations), jnp.float32)] * 2,
+        scratch_shapes=[pltpu.VMEM((count, LANES), jnp.float32)] * 4,
+        compiler_params=pltpu.CompilerParams(vmem_limit_bytes=32 * 1024 * 1024),
+        cost_estimate=pl.CostEstimate(
+            flops=8 * count * orientations * columns,
+            bytes_accessed=4 * orientations * columns + 2 * count * columns,
+            transcendentals=4 * count * LANES,
+        ),
+    )(*chunks, *chunks, noise, own_panel, mate_panel)
+
+
+def swap_halves(values, per_device):
+    shape = values.shape
+    split = values.reshape((-1, 2, per_device) + shape[1:])
+    return jnp.flip(split, axis=1).reshape(shape)
+
+
+def chip_shards(images, defocus, block_ids, noise_weight, panels):
+    per_device, halves, columns = images.shape[1:]
+    devices = lax.axis_size("orient")
+    chips = devices // 2
+    groups = lax.axis_size("cls")
+    local_search = block_ids.shape[2]
+    orientations = panels.shape[2]
+    slots_each = min(per_device, max(2, 2 * per_device * local_search // devices))
+    capacity = slots_each * devices
+    place = lax.axis_index("orient")
+    chip, core = place // 2, place % 2
+    first = core == 0
+
+    mate_pairs = [(d, d ^ 1) for d in range(devices)]
+    x_pairs = [(0, 1), (1, 0)]
+
+    def turn(step, cross=False):
+        return [(d, (d + 2 * step) % devices ^ int(cross)) for d in range(devices)]
+
+    facts = jnp.concatenate(
+        [defocus[0][:, None], block_ids[0].astype(jnp.bfloat16)], axis=1
+    )
+    facts = jnp.pad(facts, ((0, 0), (0, LANES - facts.shape[1])))
+    part = [jnp.concatenate([images[0, :, r, :], facts], axis=1) for r in range(2)]
+    kept = jnp.where(first, part[0], part[1])
+    given = jnp.where(first, part[1], part[0])
+    own_chunk = jnp.concatenate([kept, lax.ppermute(given, "orient", mate_pairs)], axis=0)
+
+    chunks = [own_chunk]
+    for step in range(1, chips):
+        chunks.append(lax.ppermute(own_chunk, "orient", turn(step)))
+    other_chunks = [lax.ppermute(c, "cls", x_pairs) for c in chunks]
+
+    sides = [panels[0, 0, :, r, :] for r in range(2)]
+    own_panel = jnp.where(first, sides[0], sides[1])
+    given_panel = jnp.where(first, sides[1], sides[0])
+    mate_panel = lax.ppermute(given_panel, "orient", mate_pairs)
+
+    noise = noise_weight[None, :]
+    here_own, here_mate = partial_scores(chunks, noise, own_panel, mate_panel)
+    there_own, there_mate = partial_scores(other_chunks, noise, own_panel, mate_panel)
+
+    from_mate = lax.ppermute(here_mate, "orient", mate_pairs)
+    from_x = lax.ppermute(there_own, "cls", x_pairs)
+    from_both = lax.ppermute(
+        there_mate,
+        ("orient", "cls"),
+        [(d * 2 + g, (d ^ 1) * 2 + 1 - g) for d in range(devices) for g in range(2)],
+    )
+    mine = here_own + swap_halves(from_mate, per_device)
+    theirs = from_x + swap_halves(from_both, per_device)
+    zero_class = lax.axis_index("cls") == 0
+    scores = jnp.concatenate(
+        [jnp.where(zero_class, mine, theirs), jnp.where(zero_class, theirs, mine)], axis=1
+    )
+
+    everyone = per_device * devices
+    lists = jnp.concatenate([c[:, columns + 1 : columns + 1 + local_search] for c in chunks], axis=0)
+    named = jnp.any(lists.astype(jnp.int32) == place, axis=1)
+    hits = named.astype(jnp.int32).reshape(devices, per_device)
+    rank = jnp.cumsum(hits, axis=1) - hits
+    run = jnp.arange(devices, dtype=jnp.int32)
+    owner = ((chip - run // 2 + chips) % chips) * 2 + (core ^ (run % 2))
+    places = jnp.where(
+        named, (owner[:, None] * slots_each + rank).reshape(everyone), -1
+    )
+    chosen = places[None, :] == jnp.arange(capacity, dtype=jnp.int32)[:, None]
+
+    top = jnp.where(named, jnp.max(scores, axis=1), FLOOR)
+    expo = jnp.where(named[:, None], jnp.exp(scores - top[:, None]), 0.0)
+    total = jnp.sum(expo, axis=1)
+    stats = jnp.stack([top, total])
+    gathered = [stats]
+    for step in range(chips):
+        for cross in (False, True):
+            if step == 0 and not cross:
+                continue
+            got = lax.ppermute(stats, "orient", turn(step, cross))
+            got = got.reshape(2, chips, 2, per_device)
+            got = jnp.roll(got, step, axis=1)
+            if cross:
+                got = jnp.flip(got, axis=2)
+            gathered.append(got.reshape(2, everyone))
+    slots = jnp.dot(
+        chosen.astype(jnp.float32),
+        expo,
+        precision=lax.Precision.HIGHEST,
+        preferred_element_type=jnp.float32,
+    )
+    peak = functools.reduce(jnp.maximum, [s[0] for s in gathered])
+    denominator = functools.reduce(jnp.add, [s[1] * jnp.exp(s[0] - peak) for s in gathered])
+    factor = jnp.exp(top - peak) / denominator
+    slot_factor = jnp.sum(jnp.where(chosen, factor[None, :], 0.0), axis=1)
+    posterior = slots * slot_factor[:, None]
+    return posterior.reshape(1, 1, capacity, -1)
 
 
 def spread_max(member, is_live, values):
@@ -82,4 +268,12 @@
         P(("batch", "cls"), "orient", None, "rep", None),
     )
     out_specs = P(("batch", "cls"), "orient", None, "rep")
-    return jax.shard_map(shards, mesh=mesh, in_specs=in_specs, out_specs=out_specs, check_vma=False)
+    sizes = mesh.shape
+    paired = sizes["rep"] == 1 and sizes["cls"] == 2 and sizes["orient"] % 2 == 0
+    return jax.shard_map(
+        chip_shards if paired else shards,
+        mesh=mesh,
+        in_specs=in_specs,
+        out_specs=out_specs,
+        check_vma=False,
+    )

time: 209 us -> 116 us (0.56)
  blocking collectives: 63.1 us -> 0 us
  starting transfers between devices: 0.04 us -> 30.1 us
  waiting for transfers between devices: 71.1 us -> 43.9 us
  other arithmetic: 23.1 us -> 6.95 us
  matrix products: 15.7 us -> 0.97 us
  between operations: 14.2 us -> 0.39 us
  Pallas kernels: 0 us -> 13.4 us
    all_gather x2 -> x0, waiting for transfers between devices: 70.3 us -> none  [the longest x1 70.3 us: shards(): piece = lax.all_gather(panels[:, 0], 'cls', axis=0, tiled=True)]
    ppermute x0 -> x19, waiting for transfers between devices: none -> 43.9 us  [the longest x3 26.4 us: chip_shards(): chunks.append(lax.ppermute(own_chunk, 'orient', turn(step)))]
    all_gather x2 -> x0, blocking collectives: 33.2 us -> none  [the longest x1 17.3 us: shards(): lax.all_gather(defocus[0], 'orient', axis=0, tiled=True)]
    ppermute x0 -> x19, starting transfers between devices: none -> 30.1 us  [the longest x7 15.6 us: chip_shards(): got = lax.ppermute(stats, 'orient', turn(step, cross))]
    slice x0 -> x30, local copies, waits for them, and re-layouts: none -> 16.5 us  [the longest x1 12.7 us: chip_shards(): sides = [panels[0, 0, :, r, :] for r in range(2)]]
    pmax x1 -> x0, blocking collectives: 16.3 us -> none  [shards(): peak = lax.pmax(local_peak, ('orient', 'rep'))]
    gather x2 -> x0, local copies, waits for them, and re-layouts: 15.4 us -> none  [the longest x1 14.2 us: shards(): slot_rows = jnp.take(all_rows, slot_owner, axis=0)]
    dot_general x2 -> x1, matrix products: 15.7 us -> 0.97 us  [chip_shards(): jnp.dot(chosen.astype(jnp.float32), expo, precision=lax.Precision.HIGHEST...]
  transfers between devices with their start and end apart: 2 -> 19, of which waited for: 1 -> 7; matrix products, arithmetic and copies ran while one was open for 18% -> 19% of each run, Pallas kernels for 0% -> 12%
where the time goes in v1:
time: 116 us
  waiting for transfers between devices  43.9 us (38%)
  starting transfers between devices  30.1 us (26%)
  local copies, waits for them, and re-layouts  20.2 us (17%)
  Pallas kernels  13.4 us (12%)
  other arithmetic  6.95 us (6%)
    ppermute x3, waiting for transfers between devices, chip_shards(): chunks.append(lax.ppermute(own_chunk, 'orient', turn(step)))  26.4 us
    ppermute x7, starting transfers between devices, chip_shards(): got = lax.ppermute(stats, 'orient', turn(step, cross))  15.6 us
    ppermute x4, waiting for transfers between devices, chip_shards(): other_chunks = [lax.ppermute(c, 'cls', x_pairs) for c in chunks]  13.8 us
    pallas_call x2, Pallas kernels, partial_scores(): pl.pallas_call(functools.partial(score_kernel, n, tiles, columns), grid=(...  13.4 us
    slice x1, local copies, waits for them, and re-layouts, chip_shards(): sides = [panels[0, 0, :, r, :] for r in range(2)]  12.7 us
    ppermute x3, starting transfers between devices, chip_shards(): chunks.append(lax.ppermute(own_chunk, 'orient', turn(step)))  6.96 us
    ppermute x4, starting transfers between devices, chip_shards(): other_chunks = [lax.ppermute(c, 'cls', x_pairs) for c in chunks]  5.26 us
    select_n x1, other arithmetic, chip_shards(): given_panel = jnp.where(first, sides[1], sides[0])  5.2 us
  transfers between devices with their start and end apart: 19, of which 7 were waited for; matrix products, arithmetic and copies ran while one was open for 19% of the time, Pallas kernels for 12%

profile of v1, /device:TPU:0, one launch (start us, length us, event | category | flops | bytes accessed | tf_op | source)
XLA Modules:
  0.0 115.8 jit_solution(5578068101655599168)
XLA Ops:
  0.0 2.0 %fusion.32 = (bf16[1,16,1,7296]{3,2,1,0:T(2,128)(2,1)S(1)}, bf16[1,16,1,7296]{3,2,1,0:T(2,128)(2,1)S(1)}) fusion(bf16[1,16,2,7296]{3,2,1,0:T(2,128)(2,1)} %param.5), kind=kLoop, calls=%fused_computation.85 | loop fusion | bytes 933888 | tf_op jit(solution)/shard_map/slice | solution.py:122
  2.0 0.7 convert_bitcast_fusion
  2.7 0.1 copy.24
  2.8 0.7 copy.23
  3.8 0.5 collective-permute-start
  4.3 12.7 %fusion.31 = (bf16[1,1,128,1,7296]{4,3,2,1,0:T(2,128)(2,1)}, bf16[1,1,128,1,7296]{4,3,2,1,0:T(2,128)(2,1)}) fusion(bf16[1,1,128,2,7296]{4,3,2,1,0:T(2,128)(2,1)} %param.9), kind=kLoop, calls=%fused_computation.84 | loop fusion | bytes 7471104 | tf_op jit(solution)/shard_map/slice | solution.py:132
  17.0 5.2 %select_bitcast_fusion = (bf16[128,7296]{1,0:T(8,128)(2,1)}, bf16[128,7296]{1,0:T(8,128)(2,1)S(1)}) fusion(pred[]{:T(512)S(6)} %eq.30, bf16[1,1,128,1,7296]{4,3,2,1,0:T(2,128)(2,1)} %get-tuple-element.22, bf16[1,1,128,1,7296]{4,3,2,1,0:T(2,128)(2,1)} %get-tuple-element.21), kind=kLoop, calls=%fused_computation | loop fusion | flops 1867776 | bytes 7471105 | tf_op jit(solution)/shard_map/jit(_where)/select_n | solution.py:134
  22.4 0.7 copy-done.2
  23.0 3.0 %collective-permute-start.1 = (bf16[32,7424]{1,0:T(8,128)(2,1)S(1)}, bf16[32,7424]{1,0:T(8,128)(2,1)S(1)}, u32[]{:S(2)}, u32[]{:S(2)}) collective-permute-start(bf16[32,7424]{1,0:T(8,128)(2,1)S(1)} %pad_maximum_fusion.refs_0_.refs_4_), channel_id=1, source_target_pairs={{0,4},{2,6},{4,8},{6,10},{8,12},{10,14},{12,0},{14,2},{1,5},{3,7},... | collective-permute-start | bytes 1425416 | tf_op jit(solution)/shard_map/ppermute | solution.py:129
  26.0 2.6 %collective-permute-start.2 = (bf16[32,7424]{1,0:T(8,128)(2,1)S(1)}, bf16[32,7424]{1,0:T(8,128)(2,1)S(1)}, u32[]{:S(2)}, u32[]{:S(2)}) collective-permute-start(bf16[32,7424]{1,0:T(8,128)(2,1)S(1)} %pad_maximum_fusion.refs_0_.refs_4_), channel_id=1, source_target_pairs={{0,8},{2,10},{4,12},{6,14},{8,0},{10,2},{12,4},{14,6},{1,9},{3,11}... | collective-permute-start | bytes 1425416 | tf_op jit(solution)/shard_map/ppermute | solution.py:129
  28.6 1.3 %collective-permute-start.3 = (bf16[32,7424]{1,0:T(8,128)(2,1)S(1)}, bf16[32,7424]{1,0:T(8,128)(2,1)}, u32[]{:S(2)}, u32[]{:S(2)}) collective-permute-start(bf16[32,7424]{1,0:T(8,128)(2,1)S(1)} %pad_maximum_fusion.refs_0_.refs_4_), channel_id=1, source_target_pairs={{0,12},{2,14},{4,0},{6,2},{8,4},{10,6},{12,8},{14,10},{1,13},{3,15... | collective-permute-start | bytes 1425416 | tf_op jit(solution)/shard_map/ppermute | solution.py:129
  30.0 1.5 %collective-permute-start.6 = (bf16[32,7424]{1,0:T(8,128)(2,1)S(1)}, bf16[32,7424]{1,0:T(8,128)(2,1)}, u32[]{:S(2)}, u32[]{:S(2)}) collective-permute-start(bf16[32,7424]{1,0:T(8,128)(2,1)S(1)} %pad_maximum_fusion.refs_0_.refs_4_), channel_id=1, source_target_pairs={{0,1},{1,0},{2,3},{3,2},{4,5},{5,4},{6,7},{7,6},{8,9},{9,8},{10,11... | collective-permute-start | bytes 1425416 | tf_op jit(solution)/shard_map/ppermute | solution.py:130
  31.5 8.4 %collective-permute-done.1.refs_1_.refs_5_ = bf16[32,7424]{1,0:T(8,128)(2,1)S(1)} collective-permute-done((bf16[32,7424]{1,0:T(8,128)(2,1)S(1)}, bf16[32,7424]{1,0:T(8,128)(2,1)S(1)}, u32[]{:S(2)}, u32[]{:S(2)}) %collective-permute-start.1) | collective-permute-done | bytes 475168 | tf_op jit(solution)/shard_map/ppermute | solution.py:129
  39.9 1.7 %collective-permute-start.7 = (bf16[32,7424]{1,0:T(8,128)(2,1)S(1)}, bf16[32,7424]{1,0:T(8,128)(2,1)}, u32[]{:S(2)}, u32[]{:S(2)}) collective-permute-start(bf16[32,7424]{1,0:T(8,128)(2,1)S(1)} %collective-permute-done.1.refs_1_.refs_5_), channel_id=1, source_target_pairs={{0,1},{1,0},{2,3},{3,2},{4,5},{5,4},{6,7},{7,6},{8,9},{9,8},{10,11... | collective-permute-start | bytes 1425416 | tf_op jit(solution)/shard_map/ppermute | solution.py:130
  41.6 18.0 %collective-permute-done.2.refs_2_.refs_6_ = bf16[32,7424]{1,0:T(8,128)(2,1)S(1)} collective-permute-done((bf16[32,7424]{1,0:T(8,128)(2,1)S(1)}, bf16[32,7424]{1,0:T(8,128)(2,1)S(1)}, u32[]{:S(2)}, u32[]{:S(2)}) %collective-permute-start.2) | collective-permute-done | bytes 475168 | tf_op jit(solution)/shard_map/ppermute | solution.py:129
  59.6 1.5 %collective-permute-start.8 = (bf16[32,7424]{1,0:T(8,128)(2,1)S(1)}, bf16[32,7424]{1,0:T(8,128)(2,1)}, u32[]{:S(2)}, u32[]{:S(2)}) collective-permute-start(bf16[32,7424]{1,0:T(8,128)(2,1)S(1)} %collective-permute-done.2.refs_2_.refs_6_), channel_id=1, source_target_pairs={{0,1},{1,0},{2,3},{3,2},{4,5},{5,4},{6,7},{7,6},{8,9},{9,8},{10,11... | collective-permute-start | bytes 1425416 | tf_op jit(solution)/shard_map/ppermute | solution.py:130
  61.1 0.5 collective-permute-start.9
  61.9 6.8 %shard_map.55 = (f32[128,128]{1,0:T(8,128)S(1)}, f32[128,128]{1,0:T(8,128)S(1)}) custom-call(bf16[32,7424]{1,0:T(8,128)(2,1)S(1)} %pad_maximum_fusion.refs_0_.refs_4_, bf16[32,7424]{1,0:T(8,128)(2,1)S(1)} %collective-permute-done.1.refs_1_.refs_5_, bf16[32,7424]{1,0:T(8,128)(2,1)S(1)} %collective-permute-done.2.refs_2_.refs_6_, ...), custom_call_target="tpu_custom_call" | custom-call | flops 956301312 | bytes 5603328 | tf_op jit(solution)/shard_map/pallas_call | solution.py:75
  68.8 4.7 %collective-permute-done.8.refs_2_.refs_6_ = bf16[32,7424]{1,0:T(8,128)(2,1)} collective-permute-done((bf16[32,7424]{1,0:T(8,128)(2,1)S(1)}, bf16[32,7424]{1,0:T(8,128)(2,1)}, u32[]{:S(2)}, u32[]{:S(2)}) %collective-permute-start.8) | collective-permute-done | bytes 475168 | tf_op jit(solution)/shard_map/ppermute | solution.py:130
  73.5 9.1 %collective-permute-done.9.refs_3_.refs_7_ = bf16[32,7424]{1,0:T(8,128)(2,1)} collective-permute-done((bf16[32,7424]{1,0:T(8,128)(2,1)}, bf16[32,7424]{1,0:T(8,128)(2,1)}, u32[]{:S(2)}, u32[]{:S(2)}) %collective-permute-start.9) | collective-permute-done | bytes 475168 | tf_op jit(solution)/shard_map/ppermute | solution.py:130
  82.6 6.6 %shard_map.56 = (f32[128,128]{1,0:T(8,128)S(1)}, f32[128,128]{1,0:T(8,128)S(1)}) custom-call(bf16[32,7424]{1,0:T(8,128)(2,1)} %collective-permute-done.6.refs_0_.refs_4_, bf16[32,7424]{1,0:T(8,128)(2,1)} %collective-permute-done.7.refs_1_.refs_5_, bf16[32,7424]{1,0:T(8,128)(2,1)} %collective-permute-done.8.refs_2_.refs_6_, ...), custom_call_target="tpu_custom_call" | custom-call | flops 956301312 | bytes 5603328 | tf_op jit(solution)/shard_map/pallas_call | solution.py:75
  89.2 0.2 collective-permute-start.11
  89.4 1.4 %collective-permute-start.10 = (f32[128,128]{1,0:T(8,128)S(1)}, f32[128,128]{1,0:T(8,128)S(1)}, u32[]{:S(2)}, u32[]{:S(2)}) collective-permute-start(f32[128,128]{1,0:T(8,128)S(1)} %get-tuple-element.11), channel_id=1, source_target_pairs={{0,1},{1,0},{2,3},{3,2},{4,5},{5,4},{6,7},{7,6},{8,9},{9,8},{10,11... | collective-permute-start | bytes 196616 | tf_op jit(solution)/shard_map/ppermute | solution.py:142
  90.9 0.1 copy.26
  91.1 0.1 copy.27
  91.2 0.1 copy.28
  91.3 0.8 slice.207
  92.1 0.1 copy.29
  92.2 0.1 fusion.19
  92.4 0.2 reduce_window_sum.13
  92.7 0.9 collective-permute-done.11
  93.6 1.5 %collective-permute-done.10 = f32[128,128]{1,0:T(8,128)S(1)} collective-permute-done((f32[128,128]{1,0:T(8,128)S(1)}, f32[128,128]{1,0:T(8,128)S(1)}, u32[]{:S(2)}, u32[]{:S(2)}) %collective-permute-start.10) | collective-permute-done | bytes 65568 | tf_op jit(solution)/shard_map/ppermute | solution.py:142
  95.0 0.1 fusion.30
  95.2 0.2 fusion.3
  95.4 8.2 %collective-permute-start.13 = (f32[2,128]{1,0:T(2,128)S(1)}, f32[2,128]{1,0:T(2,128)S(1)}, u32[]{:S(2)}, u32[]{:S(2)}) collective-permute-start(f32[2,128]{1,0:T(2,128)S(1)} %pad_maximum_fusion.9), channel_id=1, source_target_pairs={{0,4},{2,6},{4,8},{6,10},{8,12},{10,14},{12,0},{14,2},{1,5},{3,7},... | collective-permute-start | bytes 3080 | tf_op jit(solution)/shard_map/ppermute | solution.py:176
  103.5 3.4 %collective-permute-start.15 = (f32[2,128]{1,0:T(2,128)S(1)}, f32[2,128]{1,0:T(2,128)S(1)}, u32[]{:S(2)}, u32[]{:S(2)}) collective-permute-start(f32[2,128]{1,0:T(2,128)S(1)} %pad_maximum_fusion.9), channel_id=1, source_target_pairs={{0,8},{2,10},{4,12},{6,14},{8,0},{10,2},{12,4},{14,6},{1,9},{3,11}... | collective-permute-start | bytes 3080 | tf_op jit(solution)/shard_map/ppermute | solution.py:176
  106.9 2.8 %collective-permute-start.17 = (f32[2,128]{1,0:T(2,128)S(1)}, f32[2,128]{1,0:T(2,128)S(1)}, u32[]{:S(2)}, u32[]{:S(2)}) collective-permute-start(f32[2,128]{1,0:T(2,128)S(1)} %pad_maximum_fusion.9), channel_id=1, source_target_pairs={{0,12},{2,14},{4,0},{6,2},{8,4},{10,6},{12,8},{14,10},{1,13},{3,15... | collective-permute-start | bytes 3080 | tf_op jit(solution)/shard_map/ppermute | solution.py:176
  109.7 1.0 collective-permute-start.18
  110.8 0.1 reshape.294
  110.9 0.2 collective-permute-start.12
  111.2 0.1 reshape.296
  111.5 1.2 %collective-permute-done.18 = f32[2,128]{1,0:T(2,128)S(1)} collective-permute-done((f32[2,128]{1,0:T(2,128)S(1)}, f32[2,128]{1,0:T(2,128)S(1)}, u32[]{:S(2)}, u32[]{:S(2)}) %collective-permute-start.18) | collective-permute-done | bytes 1056 | tf_op jit(solution)/shard_map/ppermute | solution.py:176
  113.3 0.1 reshape.297
  113.9 0.1 squeeze.72
  114.3 0.1 slice.168
  114.4 0.1 squeeze.60
  114.7 0.1 select_reduce_fusion
  114.8 1.0 fusion
  (86 shorter events, 2.8 us)
Async XLA Ops:
  3.8 18.5 %copy-start = (bf16[16,7424]{1,0:T(8,128)(2,1)}, bf16[16,7424]{1,0:T(8,128)(2,1)S(1)}, u32[]{:S(2)}) copy-start(bf16[16,7424]{1,0:T(8,128)(2,1)S(1)} %get-tuple-element.23) | copy-start | bytes 712708
  3.8 18.5 %collective-permute-start = (bf16[16,7424]{1,0:T(8,128)(2,1)S(1)}, bf16[16,7424]{1,0:T(8,128)(2,1)S(1)}, u32[]{:S(2)}, u32[]{:S(2)}) collective-permute-start(bf16[16,7424]{1,0:T(8,128)(2,1)S(1)} %get-tuple-element.24), channel_id=1, source_target_pairs={{0,2},{2,0},{4,6},{6,4},{8,10},{10,8},{12,14},{14,12},{1,3},{3,1},... | collective-permute-start | bytes 712712 | tf_op jit(solution)/shard_map/ppermute | solution.py:125
  17.0 44.8 %copy-start.4 = (f32[7296]{0:T(1024)S(1)}, f32[7296]{0:T(1024)}, u32[]{:S(2)}) copy-start(f32[7296]{0:T(1024)} %param.8) | copy-start | bytes 87556
  22.2 39.6 %collective-permute-start.4 = (bf16[128,7296]{1,0:T(8,128)(2,1)}, bf16[128,7296]{1,0:T(8,128)(2,1)}, u32[]{:S(2)}, u32[]{:S(2)}) collective-permute-start(bf16[128,7296]{1,0:T(8,128)(2,1)} %get-tuple-element.19), channel_id=1, source_target_pairs={{0,2},{2,0},{4,6},{6,4},{8,10},{10,8},{12,14},{14,12},{1,3},{3,1},... | collective-permute-start | bytes 5603336 | tf_op jit(solution)/shard_map/ppermute | solution.py:135
  22.3 0.7 copy-start.2
  23.0 16.9 %collective-permute-start.1 = (bf16[32,7424]{1,0:T(8,128)(2,1)S(1)}, bf16[32,7424]{1,0:T(8,128)(2,1)S(1)}, u32[]{:S(2)}, u32[]{:S(2)}) collective-permute-start(bf16[32,7424]{1,0:T(8,128)(2,1)S(1)} %pad_maximum_fusion.refs_0_.refs_4_), channel_id=1, source_target_pairs={{0,4},{2,6},{4,8},{6,10},{8,12},{10,14},{12,0},{14,2},{1,5},{3,7},... | collective-permute-start | bytes 1425416 | tf_op jit(solution)/shard_map/ppermute | solution.py:129
  26.0 33.6 %collective-permute-start.2 = (bf16[32,7424]{1,0:T(8,128)(2,1)S(1)}, bf16[32,7424]{1,0:T(8,128)(2,1)S(1)}, u32[]{:S(2)}, u32[]{:S(2)}) collective-permute-start(bf16[32,7424]{1,0:T(8,128)(2,1)S(1)} %pad_maximum_fusion.refs_0_.refs_4_), channel_id=1, source_target_pairs={{0,8},{2,10},{4,12},{6,14},{8,0},{10,2},{12,4},{14,6},{1,9},{3,11}... | collective-permute-start | bytes 1425416 | tf_op jit(solution)/shard_map/ppermute | solution.py:129
  28.6 32.5 %collective-permute-start.3 = (bf16[32,7424]{1,0:T(8,128)(2,1)S(1)}, bf16[32,7424]{1,0:T(8,128)(2,1)}, u32[]{:S(2)}, u32[]{:S(2)}) collective-permute-start(bf16[32,7424]{1,0:T(8,128)(2,1)S(1)} %pad_maximum_fusion.refs_0_.refs_4_), channel_id=1, source_target_pairs={{0,12},{2,14},{4,0},{6,2},{8,4},{10,6},{12,8},{14,10},{1,13},{3,15... | collective-permute-start | bytes 1425416 | tf_op jit(solution)/shard_map/ppermute | solution.py:129
  30.0 38.8 %collective-permute-start.6 = (bf16[32,7424]{1,0:T(8,128)(2,1)S(1)}, bf16[32,7424]{1,0:T(8,128)(2,1)}, u32[]{:S(2)}, u32[]{:S(2)}) collective-permute-start(bf16[32,7424]{1,0:T(8,128)(2,1)S(1)} %pad_maximum_fusion.refs_0_.refs_4_), channel_id=1, source_target_pairs={{0,1},{1,0},{2,3},{3,2},{4,5},{5,4},{6,7},{7,6},{8,9},{9,8},{10,11... | collective-permute-start | bytes 1425416 | tf_op jit(solution)/shard_map/ppermute | solution.py:130
  39.9 28.9 %collective-permute-start.7 = (bf16[32,7424]{1,0:T(8,128)(2,1)S(1)}, bf16[32,7424]{1,0:T(8,128)(2,1)}, u32[]{:S(2)}, u32[]{:S(2)}) collective-permute-start(bf16[32,7424]{1,0:T(8,128)(2,1)S(1)} %collective-permute-done.1.refs_1_.refs_5_), channel_id=1, source_target_pairs={{0,1},{1,0},{2,3},{3,2},{4,5},{5,4},{6,7},{7,6},{8,9},{9,8},{10,11... | collective-permute-start | bytes 1425416 | tf_op jit(solution)/shard_map/ppermute | solution.py:130
  59.6 13.9 %collective-permute-start.8 = (bf16[32,7424]{1,0:T(8,128)(2,1)S(1)}, bf16[32,7424]{1,0:T(8,128)(2,1)}, u32[]{:S(2)}, u32[]{:S(2)}) collective-permute-start(bf16[32,7424]{1,0:T(8,128)(2,1)S(1)} %collective-permute-done.2.refs_2_.refs_6_), channel_id=1, source_target_pairs={{0,1},{1,0},{2,3},{3,2},{4,5},{5,4},{6,7},{7,6},{8,9},{9,8},{10,11... | collective-permute-start | bytes 1425416 | tf_op jit(solution)/shard_map/ppermute | solution.py:130
  61.1 21.5 %collective-permute-start.9 = (bf16[32,7424]{1,0:T(8,128)(2,1)}, bf16[32,7424]{1,0:T(8,128)(2,1)}, u32[]{:S(2)}, u32[]{:S(2)}) collective-permute-start(bf16[32,7424]{1,0:T(8,128)(2,1)} %collective-permute-done.3.refs_3_.refs_7_), channel_id=1, source_target_pairs={{0,1},{1,0},{2,3},{3,2},{4,5},{5,4},{6,7},{7,6},{8,9},{9,8},{10,11... | collective-permute-start | bytes 1425416 | tf_op jit(solution)/shard_map/ppermute | solution.py:130
  68.7 22.2 %copy-start.1 = (bf16[16,7424]{1,0:T(8,128)(2,1)S(1)}, bf16[16,7424]{1,0:T(8,128)(2,1)}, u32[]{:S(2)}) copy-start(bf16[16,7424]{1,0:T(8,128)(2,1)} %copy-done) | copy-start | bytes 712708
  68.7 22.2 %copy-start.3 = (bf16[16,7424]{1,0:T(8,128)(2,1)S(1)}, bf16[16,7424]{1,0:T(8,128)(2,1)}, u32[]{:S(2)}) copy-start(bf16[16,7424]{1,0:T(8,128)(2,1)} %copy-done.2) | copy-start | bytes 712708
  68.7 24.0 %collective-permute-start.5 = (f32[128,128]{1,0:T(8,128)S(1)}, f32[128,128]{1,0:T(8,128)S(1)}, u32[]{:S(2)}, u32[]{:S(2)}) collective-permute-start(f32[128,128]{1,0:T(8,128)S(1)} %get-tuple-element.10), channel_id=1, source_target_pairs={{0,2},{2,0},{4,6},{6,4},{8,10},{10,8},{12,14},{14,12},{1,3},{3,1},... | collective-permute-start | bytes 196616 | tf_op jit(solution)/shard_map/ppermute | solution.py:141
  89.2 4.4 %collective-permute-start.11 = (f32[128,128]{1,0:T(8,128)S(1)}, f32[128,128]{1,0:T(8,128)S(1)}, u32[]{:S(2)}, u32[]{:S(2)}) collective-permute-start(f32[128,128]{1,0:T(8,128)S(1)} %get-tuple-element.12), channel_id=1, source_target_pairs={{0,3},{1,2},{2,1},{3,0},{4,7},{5,6},{6,5},{7,4},{8,11},{9,10},{10,... | collective-permute-start | bytes 196616 | tf_op jit(solution)/shard_map/ppermute | solution.py:143
  89.4 5.6 %collective-permute-start.10 = (f32[128,128]{1,0:T(8,128)S(1)}, f32[128,128]{1,0:T(8,128)S(1)}, u32[]{:S(2)}, u32[]{:S(2)}) collective-permute-start(f32[128,128]{1,0:T(8,128)S(1)} %get-tuple-element.11), channel_id=1, source_target_pairs={{0,1},{1,0},{2,3},{3,2},{4,5},{5,4},{6,7},{7,6},{8,9},{9,8},{10,11... | collective-permute-start | bytes 196616 | tf_op jit(solution)/shard_map/ppermute | solution.py:142
  95.4 14.4 %collective-permute-start.13 = (f32[2,128]{1,0:T(2,128)S(1)}, f32[2,128]{1,0:T(2,128)S(1)}, u32[]{:S(2)}, u32[]{:S(2)}) collective-permute-start(f32[2,128]{1,0:T(2,128)S(1)} %pad_maximum_fusion.9), channel_id=1, source_target_pairs={{0,4},{2,6},{4,8},{6,10},{8,12},{10,14},{12,0},{14,2},{1,5},{3,7},... | collective-permute-start | bytes 3080 | tf_op jit(solution)/shard_map/ppermute | solution.py:176
  103.5 7.3 %collective-permute-start.14 = (f32[2,128]{1,0:T(2,128)S(1)}, f32[2,128]{1,0:T(2,128)S(1)}, u32[]{:S(2)}, u32[]{:S(2)}) collective-permute-start(f32[2,128]{1,0:T(2,128)S(1)} %pad_maximum_fusion.9), channel_id=1, source_target_pairs={{0,6},{2,4},{4,10},{6,8},{8,14},{10,12},{12,2},{14,0},{1,7},{3,5},... | collective-permute-start | bytes 3080 | tf_op jit(solution)/shard_map/ppermute | solution.py:176
  103.5 7.7 %collective-permute-start.15 = (f32[2,128]{1,0:T(2,128)S(1)}, f32[2,128]{1,0:T(2,128)S(1)}, u32[]{:S(2)}, u32[]{:S(2)}) collective-permute-start(f32[2,128]{1,0:T(2,128)S(1)} %pad_maximum_fusion.9), channel_id=1, source_target_pairs={{0,8},{2,10},{4,12},{6,14},{8,0},{10,2},{12,4},{14,6},{1,9},{3,11}... | collective-permute-start | bytes 3080 | tf_op jit(solution)/shard_map/ppermute | solution.py:176
  106.9 6.3 %collective-permute-start.16 = (f32[2,128]{1,0:T(2,128)S(1)}, f32[2,128]{1,0:T(2,128)S(1)}, u32[]{:S(2)}, u32[]{:S(2)}) collective-permute-start(f32[2,128]{1,0:T(2,128)S(1)} %pad_maximum_fusion.9), channel_id=1, source_target_pairs={{0,10},{2,8},{4,14},{6,12},{8,2},{10,0},{12,6},{14,4},{1,11},{3,9}... | collective-permute-start | bytes 3080 | tf_op jit(solution)/shard_map/ppermute | solution.py:176
  106.9 4.5 %collective-permute-start.17 = (f32[2,128]{1,0:T(2,128)S(1)}, f32[2,128]{1,0:T(2,128)S(1)}, u32[]{:S(2)}, u32[]{:S(2)}) collective-permute-start(f32[2,128]{1,0:T(2,128)S(1)} %pad_maximum_fusion.9), channel_id=1, source_target_pairs={{0,12},{2,14},{4,0},{6,2},{8,4},{10,6},{12,8},{14,10},{1,13},{3,15... | collective-permute-start | bytes 3080 | tf_op jit(solution)/shard_map/ppermute | solution.py:176
  109.7 3.0 %collective-permute-start.18 = (f32[2,128]{1,0:T(2,128)S(1)}, f32[2,128]{1,0:T(2,128)S(1)}, u32[]{:S(2)}, u32[]{:S(2)}) collective-permute-start(f32[2,128]{1,0:T(2,128)S(1)} %pad_maximum_fusion.9), channel_id=1, source_target_pairs={{0,14},{2,12},{4,2},{6,0},{8,6},{10,4},{12,10},{14,8},{1,15},{3,13... | collective-permute-start | bytes 3080 | tf_op jit(solution)/shard_map/ppermute | solution.py:176
  110.9 3.4 %collective-permute-start.12 = (f32[2,128]{1,0:T(2,128)S(1)}, f32[2,128]{1,0:T(2,128)S(1)}, u32[]{:S(2)}, u32[]{:S(2)}) collective-permute-start(f32[2,128]{1,0:T(2,128)S(1)} %pad_maximum_fusion.9), channel_id=1, source_target_pairs={{0,2},{2,0},{4,6},{6,4},{8,10},{10,8},{12,14},{14,12},{1,3},{3,1},... | collective-permute-start | bytes 3080 | tf_op jit(solution)/shard_map/ppermute | solution.py:176

commit v2 on v0

--- a/solution.py
+++ b/solution.py
@@ -1,10 +1,360 @@
+import functools
+
 import jax
 import jax.numpy as jnp
 from jax import lax
+from jax.experimental import pallas as pl
+from jax.experimental.pallas import tpu as pltpu
 from jax.sharding import PartitionSpec as P
 
 CTF_PHASE = 40.0
 FLOOR = -1e30
+LANES = 128
+VMEM_LIMIT = 32 * 1024 * 1024
+
+
+def sin_cos(angle):
+    turns = jnp.floor(angle * 0.6366197723675814 + 0.5)
+    rest = angle - turns * 1.5703125
+    rest = rest - turns * 4.837512969970703e-4
+    rest = rest - turns * 7.549789948768648e-8
+    square = rest * rest
+    sine = rest + rest * square * (
+        -1.6666654611e-1 + square * (8.3321608736e-3 - square * 1.9515295891e-4)
+    )
+    cosine = (
+        1.0
+        - 0.5 * square
+        + square
+        * square
+        * (4.166664568298827e-2 + square * (-1.388731625493765e-3 + square * 2.443315711809948e-5))
+    )
+    quarter = turns.astype(jnp.int32)
+    odd = (quarter & 1) == 1
+    low = jnp.where(odd, cosine, sine)
+    high = jnp.where(odd, sine, cosine)
+    return (
+        jnp.where((quarter & 2) == 2, -low, low),
+        jnp.where(((quarter + 1) & 2) == 2, -high, high),
+    )
+
+
+def add_scores(rows, meta, noise, panels, outs, tables, tiles, columns):
+    step = pl.program_id(0)
+    sin_a, cos_a, sin_b, cos_b = tables
+    count = sin_a.shape[0]
+
+    @pl.when(step == 0)
+    def _():
+        focus = jnp.concatenate([m[:, 0:1] for m in meta], axis=0).astype(jnp.float32)
+        rate = CTF_PHASE * focus
+        lane = lax.broadcasted_iota(jnp.int32, (count, LANES), 1).astype(jnp.float32)
+        coarse_sin, coarse_cos = sin_cos(rate * (lane * (LANES / columns)) + 0.1)
+        sin_a[...] = -coarse_sin
+        cos_a[...] = -coarse_cos
+        fine_sin, fine_cos = sin_cos(rate * ((lane + 0.5) / columns))
+        sin_b[...] = fine_sin
+        cos_b[...] = fine_cos
+        for out in outs:
+            out[...] = jnp.zeros_like(out)
+
+    shift = lax.rem(LANES - step * tiles, LANES)
+    sa = pltpu.roll(sin_a[...], shift, 1)
+    ca = pltpu.roll(cos_a[...], shift, 1)
+    sb = sin_b[...]
+    cb = cos_b[...]
+    scaled_parts, energy_parts = [], []
+    for t in range(tiles):
+        window = slice(t * LANES, (t + 1) * LANES)
+        contrast = sa[:, t : t + 1] * cb + ca[:, t : t + 1] * sb
+        weighted = contrast * noise[:, window]
+        image = jnp.concatenate([r[:, window] for r in rows], axis=0).astype(jnp.float32)
+        scaled_parts.append((weighted * image).astype(jnp.bfloat16))
+        energy_parts.append((contrast * weighted).astype(jnp.bfloat16))
+    scaled = jnp.concatenate(scaled_parts, axis=1)
+    energy = jnp.concatenate(energy_parts, axis=1)
+    contract = (((1,), (1,)), ((), ()))
+    for panel, out in zip(panels, outs):
+        values = panel[...]
+        squared = values * values
+        correlate = lax.dot_general(scaled, values, contract, preferred_element_type=jnp.float32)
+        power = lax.dot_general(energy, squared, contract, preferred_element_type=jnp.float32)
+        out[...] += correlate - 0.5 * power
+
+
+def batch_kernel(n, tiles, columns, spot, *refs):
+    del spot
+    rows, meta = refs[:n], refs[n : 2 * n]
+    noise, own_panel, mate_panel, own_out, mate_out, fact_out = refs[2 * n : 2 * n + 6]
+    tables = refs[2 * n + 6 :]
+    add_scores(
+        rows, meta, noise, (own_panel, mate_panel), (own_out, mate_out), tables, tiles, columns
+    )
+    fact_out[...] = jnp.concatenate([m[...] for m in meta], axis=0).astype(jnp.float32)
+
+
+def last_kernel(n, tiles, columns, steps, orders, spot, *refs):
+    rows, meta = refs[:n], refs[n : 2 * n]
+    noise, own_panel, mate_panel = refs[2 * n : 2 * n + 3]
+    earlier = refs[2 * n + 3 : 2 * n + 3 + 3 * (len(orders) - 1)]
+    here_own, here_mate, there_own, there_mate, facts, own_sum, mate_sum, *rest = refs[
+        2 * n + 3 + len(earlier) :
+    ]
+    tables, (own_all, mate_all, fact_all) = rest[:4], rest[4:]
+    add_scores(
+        rows, meta, noise, (own_panel, mate_panel), (own_sum, mate_sum), tables, tiles, columns
+    )
+
+    @pl.when(pl.program_id(0) == steps - 1)
+    def _():
+        group, position, core = spot[0], spot[1], spot[2]
+        each = rows[0].shape[0]
+        ring = own_all.shape[0] // (2 * each)
+        half = ring // 2
+        last_facts = jnp.concatenate([m[...] for m in meta], axis=0).astype(jnp.float32)
+        for index, order in enumerate(orders):
+            if index < len(orders) - 1:
+                own, mate, fact = [r[...] for r in earlier[3 * index : 3 * index + 3]]
+            else:
+                own, mate, fact = own_sum[...], mate_sum[...], last_facts
+            for k, (distance, crossed) in enumerate(order):
+                place = lax.rem(position + distance + ring, ring)
+                far = place >= half
+                level = jnp.where(far, ring - 1 - place, place)
+                device = 2 * level + (1 - core if crossed else core)
+                side = jnp.where(far, 1, 0)
+                other = jnp.where(side == group, 0, 1)
+                start = pl.multiple_of((other * ring + device) * each, each)
+                piece = slice(k * each, (k + 1) * each)
+                own_all[pl.ds(start, each), :] = own[piece]
+                mate_all[pl.ds(start, each), :] = mate[piece]
+                fact_all[pl.ds(start, each), :] = fact[piece]
+        everyone = ring * each
+        here_own[...] = own_all[:everyone]
+        here_mate[...] = mate_all[:everyone]
+        there_own[...] = own_all[everyone:]
+        there_mate[...] = mate_all[everyone:]
+        facts[...] = fact_all[:everyone]
+
+
+def score_call(chunks, orders, earlier, spot, noise, sides, mate_panel):
+    each = chunks[0].shape[0]
+    orientations, columns = mate_panel.shape
+    whole = columns // LANES
+    steps = next(s for s in (3, 2, 4, 5, 6, 7, 1) if whole % s == 0)
+    tiles = whole // steps
+    width = tiles * LANES
+    n = len(chunks)
+    count = each * n
+    row_spec = pl.BlockSpec((each, width), lambda s, spot: (0, s))
+    meta_spec = pl.BlockSpec((each, LANES), lambda s, spot: (0, whole))
+    fixed = lambda shape: pl.BlockSpec(shape, lambda s, spot: (0, 0))
+    in_specs = (
+        [row_spec] * n
+        + [meta_spec] * n
+        + [
+            pl.BlockSpec((1, width), lambda s, spot: (0, s)),
+            pl.BlockSpec((None, orientations, width), lambda s, spot: (spot[2], 0, s)),
+            pl.BlockSpec((orientations, width), lambda s, spot: (0, s)),
+        ]
+    )
+    table = [pltpu.VMEM((count, LANES), jnp.float32)] * 4
+    single = jax.ShapeDtypeStruct((count, orientations), jnp.float32)
+    if orders is None:
+        kernel = functools.partial(batch_kernel, n, tiles, columns)
+        out_shape = [single, single, jax.ShapeDtypeStruct((count, LANES), jnp.float32)]
+        scratch = table
+        extra = []
+    else:
+        everyone = each * sum(len(o) for o in orders) // 2
+        kernel = functools.partial(last_kernel, n, tiles, columns, steps, orders)
+        block = jax.ShapeDtypeStruct((everyone, orientations), jnp.float32)
+        out_shape = [block] * 4 + [jax.ShapeDtypeStruct((everyone, LANES), jnp.float32)]
+        sums = pltpu.VMEM((count, orientations), jnp.float32)
+        whole_sums = pltpu.VMEM((2 * everyone, orientations), jnp.float32)
+        scratch = (
+            [sums, sums]
+            + table
+            + [whole_sums, whole_sums, pltpu.VMEM((2 * everyone, LANES), jnp.float32)]
+        )
+        extra = [e for triple in earlier for e in triple]
+        in_specs = in_specs + [fixed(e.shape) for e in extra]
+    return pl.pallas_call(
+        kernel,
+        grid_spec=pltpu.PrefetchScalarGridSpec(
+            num_scalar_prefetch=1,
+            grid=(steps,),
+            in_specs=in_specs,
+            out_specs=[fixed(o.shape) for o in out_shape],
+            scratch_shapes=scratch,
+        ),
+        out_shape=out_shape,
+        compiler_params=pltpu.CompilerParams(vmem_limit_bytes=VMEM_LIMIT),
+        cost_estimate=pl.CostEstimate(
+            flops=8 * max(count, 128) * orientations * columns,
+            bytes_accessed=4 * orientations * columns + 2 * count * columns,
+            transcendentals=0,
+        ),
+    )(spot, *chunks, *chunks, noise, sides, mate_panel, *extra)
+
+
+def stats_kernel(search, slots_each, each, spot, mine, mate, across, both, facts, slots, chosen, stats):
+    group, block = spot[0], spot[3]
+    count = mine.shape[0]
+    same = mine[...] + mate[...]
+    other = across[...] + both[...]
+    first = group == 0
+    scores = jnp.concatenate(
+        [jnp.where(first, same, other), jnp.where(first, other, same)], axis=1
+    )
+    lane = lax.broadcasted_iota(jnp.int32, (count, LANES), 1)
+    row = lax.broadcasted_iota(jnp.int32, (count, LANES), 0)
+    match = (lane >= 1) & (lane <= search) & (facts[...] == block.astype(jnp.float32))
+    hit = jnp.max(jnp.where(match, 1.0, 0.0), axis=1, keepdims=True)
+    named = hit > 0.0
+    line = lax.broadcasted_iota(jnp.int32, (count, count), 0)
+    column = lax.broadcasted_iota(jnp.int32, (count, count), 1)
+    before = (column < line) & (column // each == line // each)
+    rank = jnp.dot(
+        jnp.where(before, 1.0, 0.0).astype(jnp.bfloat16),
+        jnp.broadcast_to(hit, (count, LANES)).astype(jnp.bfloat16),
+        preferred_element_type=jnp.float32,
+    )
+    slot = (row // each) * slots_each + rank.astype(jnp.int32)
+    capacity = chosen.shape[0]
+    if capacity != LANES:
+        slot = jnp.broadcast_to(slot[:, :1], (count, capacity))
+    target = lax.broadcasted_iota(jnp.int32, (count, capacity), 1)
+    taken = jnp.where((slot == target) & named, 1.0, 0.0)
+    top = jnp.where(named, jnp.max(scores, axis=1, keepdims=True), FLOOR)
+    terms = jnp.where(named, jnp.exp(scores - top), 0.0)
+    total = jnp.sum(terms, axis=1, keepdims=True)
+    slots[...] = lax.dot_general(
+        taken,
+        terms,
+        (((0,), (0,)), ((), ())),
+        precision=lax.Precision.HIGHEST,
+        preferred_element_type=jnp.float32,
+    )
+    chosen[...] = taken.T
+    pair = jnp.where(lane == 0, top, jnp.where(lane == 1, total, 0.0))
+    stats[...] = pair.T[: stats.shape[0]]
+
+
+def final_kernel(n, *refs):
+    own, parts, slots, chosen, out = refs[0], refs[1 : 1 + n], refs[1 + n], refs[2 + n], refs[3 + n]
+    tops = [p[0:1, :] for p in parts]
+    peak = functools.reduce(jnp.maximum, tops)
+    total = functools.reduce(jnp.add, [p[1:2, :] * jnp.exp(p[0:1, :] - peak) for p in parts])
+    factor = jnp.exp(own[0:1, :] - peak) / total
+    scale = jnp.sum(chosen[...] * factor, axis=1, keepdims=True)
+    out[...] = slots[...] * scale
+
+
+def chip_shards(images, defocus, block_ids, noise_weight, panels):
+    per_device, halves, columns = images.shape[1:]
+    devices = lax.axis_size("orient")
+    chips = devices // 2
+    ring = 2 * chips
+    everyone = per_device * devices
+    local_search = block_ids.shape[2]
+    orientations = panels.shape[2]
+    slots_each = min(per_device, max(2, 2 * per_device * local_search // devices))
+    capacity = slots_each * devices
+    place = lax.axis_index("orient")
+    group = lax.axis_index("cls")
+    chip, core = place // 2, place % 2
+    position = jnp.where(group == 0, chip, ring - 1 - chip)
+    spot = jnp.stack([group, position, core, place]).astype(jnp.int32)
+    first = core == 0
+
+    mate_pairs = [(d, d ^ 1) for d in range(devices)]
+    x_pairs = [(0, 1), (1, 0)]
+
+    def joint(place, core):
+        place = place % ring
+        far = place >= chips
+        level = ring - 1 - place if far else place
+        return (2 * level + core) * 2 + int(far)
+
+    def forward(values, step):
+        pairs = [(joint(p, c), joint(p + step, c)) for p in range(ring) for c in range(2)]
+        return lax.ppermute(values, ("orient", "cls"), pairs)
+
+    facts = jnp.concatenate([defocus[0][:, None], block_ids[0].astype(jnp.bfloat16)], axis=1)
+    facts = jnp.pad(facts, ((0, 0), (0, LANES - facts.shape[1])))
+    planes = lax.optimization_barrier(jnp.transpose(images[0], (1, 0, 2)))
+    kept = jnp.concatenate([jnp.where(first, planes[0], planes[1]), facts], axis=1)
+    given = jnp.concatenate([jnp.where(first, planes[1], planes[0]), facts], axis=1)
+    got = lax.ppermute(given, "orient", mate_pairs)
+
+    got, panels = lax.optimization_barrier((got, panels))
+    sides = lax.optimization_barrier(jnp.transpose(panels[0, 0], (1, 0, 2)))
+    mate_panel = lax.ppermute(
+        lax.dynamic_index_in_dim(sides, 1 - core, 0, keepdims=False), "orient", mate_pairs
+    )
+
+    batches = [[((0, False), kept), ((0, True), got)]]
+    ahead = {False: kept, True: got}
+    behind = {False: kept, True: got}
+    for step in range(1, chips + 1):
+        arrived = []
+        for crossed in (False, True):
+            if step < chips or not crossed:
+                ahead[crossed] = forward(ahead[crossed], 1)
+                arrived.append(((-step, crossed), ahead[crossed]))
+            if step < chips or crossed:
+                behind[crossed] = forward(behind[crossed], -1)
+                arrived.append(((step, crossed), behind[crossed]))
+        batches.append(arrived)
+    batches = [batches[0] + batches[1]] + batches[2:]
+
+    noise = noise_weight[None, :]
+    orders = [[key for key, _ in batch] for batch in batches]
+    earlier = [
+        score_call([c for _, c in batch], None, None, spot, noise, sides, mate_panel)
+        for batch in batches[:-1]
+    ]
+    here_own, here_mate, there_own, there_mate, own_facts = score_call(
+        [c for _, c in batches[-1]], orders, earlier, spot, noise, sides, mate_panel
+    )
+
+    from_mate = lax.ppermute(here_mate, "orient", mate_pairs)
+    from_x = lax.ppermute(there_own, "cls", x_pairs)
+    from_both = lax.ppermute(
+        there_mate,
+        ("orient", "cls"),
+        [(d * 2 + g, (d ^ 1) * 2 + 1 - g) for d in range(devices) for g in range(2)],
+    )
+    vmem = pl.BlockSpec(memory_space=pltpu.VMEM)
+    slots, chosen, stats = pl.pallas_call(
+        functools.partial(stats_kernel, local_search, slots_each, per_device),
+        in_specs=[pl.BlockSpec(memory_space=pltpu.SMEM)] + [vmem] * 5,
+        out_specs=[vmem] * 3,
+        out_shape=[
+            jax.ShapeDtypeStruct((capacity, 2 * orientations), jnp.float32),
+            jax.ShapeDtypeStruct((capacity, everyone), jnp.float32),
+            jax.ShapeDtypeStruct((8, everyone), jnp.float32),
+        ],
+        compiler_params=pltpu.CompilerParams(vmem_limit_bytes=VMEM_LIMIT),
+    )(spot, here_own, from_mate, from_x, from_both, own_facts)
+
+    mate_stats = lax.ppermute(stats, "orient", mate_pairs)
+    peak = jnp.maximum(stats[0], mate_stats[0])
+    total = stats[1] * jnp.exp(stats[0] - peak) + mate_stats[1] * jnp.exp(mate_stats[0] - peak)
+    pair = jnp.zeros_like(stats).at[0].set(peak).at[1].set(total)
+    pairs = [pair] + [
+        lax.ppermute(pair, "orient", [(d, (d + 2 * s) % devices) for d in range(devices)])
+        for s in range(1, chips)
+    ]
+    posterior = pl.pallas_call(
+        functools.partial(final_kernel, chips),
+        in_specs=[vmem] * (chips + 3),
+        out_specs=vmem,
+        out_shape=jax.ShapeDtypeStruct((capacity, 2 * orientations), jnp.float32),
+        compiler_params=pltpu.CompilerParams(vmem_limit_bytes=VMEM_LIMIT),
+    )(stats, *pairs, slots, chosen)
+    return posterior.reshape(1, 1, capacity, -1)
 
 
 def spread_max(member, is_live, values):
@@ -82,4 +432,12 @@
         P(("batch", "cls"), "orient", None, "rep", None),
     )
     out_specs = P(("batch", "cls"), "orient", None, "rep")
-    return jax.shard_map(shards, mesh=mesh, in_specs=in_specs, out_specs=out_specs, check_vma=False)
+    sizes = mesh.shape
+    paired = sizes["rep"] == 1 and sizes["cls"] == 2 and sizes["orient"] % 2 == 0
+    return jax.shard_map(
+        chip_shards if paired else shards,
+        mesh=mesh,
+        in_specs=in_specs,
+        out_specs=out_specs,
+        check_vma=False,
+    )

time: 209 us -> 85.8 us (0.41)
  blocking collectives: 63.1 us -> 0 us
  waiting for transfers between devices: 71.1 us -> 24.3 us
  Pallas kernels: 0 us -> 24.4 us
  starting transfers between devices: 0.04 us -> 23.8 us
  other arithmetic: 23.1 us -> 0.94 us
  matrix products: 15.7 us -> 0 us
  between operations: 14.2 us -> 0.14 us
  local copies, waits for them, and re-layouts: 21.6 us -> 11.8 us
    all_gather x2 -> x0, waiting for transfers between devices: 70.3 us -> none  [the longest x1 70.3 us: shards(): piece = lax.all_gather(panels[:, 0], 'cls', axis=0, tiled=True)]
    all_gather x2 -> x0, blocking collectives: 33.2 us -> none  [the longest x1 17.3 us: shards(): lax.all_gather(defocus[0], 'orient', axis=0, tiled=True)]
    pallas_call x0 -> x6, Pallas kernels: none -> 24.4 us  [the longest x4 22.5 us: score_call(): pl.pallas_call(kernel, grid_spec=pltpu.PrefetchScalarGridSpec(num_scalar_...]
    ppermute x0 -> x23, waiting for transfers between devices: none -> 24.3 us  [the longest x14 15.9 us: forward(): return lax.ppermute(values, ('orient', 'cls'), pairs)]
    ppermute x0 -> x23, starting transfers between devices: none -> 23.8 us  [the longest x14 15 us: forward(): return lax.ppermute(values, ('orient', 'cls'), pairs)]
    pmax x1 -> x0, blocking collectives: 16.3 us -> none  [shards(): peak = lax.pmax(local_peak, ('orient', 'rep'))]
    dot_general x2 -> x0, matrix products: 15.7 us -> none  [the longest x1 13.2 us: shards(): jnp.einsum('sk,cjrk->scj', energy, squared, preferred_element_type=jnp.fl...]
    gather x2 -> x0, local copies, waits for them, and re-layouts: 15.4 us -> none  [the longest x1 14.2 us: shards(): slot_rows = jnp.take(all_rows, slot_owner, axis=0)]
  transfers between devices with their start and end apart: 2 -> 23, of which waited for: 1 -> 12; matrix products, arithmetic and copies ran while one was open for 18% -> 2% of each run, Pallas kernels for 0% -> 21%
where the time goes in v2:
time: 85.8 us; the launch traced here: 85.3 us
  Pallas kernels  24.4 us (28%)
  waiting for transfers between devices  24.3 us (28%)
  starting transfers between devices  23.8 us (28%)
  local copies, waits for them, and re-layouts  11.8 us (14%)
  other arithmetic  0.94 us (1%)
    pallas_call x4, Pallas kernels, score_call(): pl.pallas_call(kernel, grid_spec=pltpu.PrefetchScalarGridSpec(num_scalar_...  22.5 us
    ppermute x14, waiting for transfers between devices, forward(): return lax.ppermute(values, ('orient', 'cls'), pairs)  15.9 us
    ppermute x14, starting transfers between devices, forward(): return lax.ppermute(values, ('orient', 'cls'), pairs)  15 us
    unnamed x9, local copies, waits for them, and re-layouts  5.68 us
    ppermute x3, starting transfers between devices, chip_shards(): lax.ppermute(pair, 'orient', [(d, (d + 2 * s) % devices) for d in range(d...  5.57 us
    ppermute x1, waiting for transfers between devices, chip_shards(): from_x = lax.ppermute(there_own, 'cls', x_pairs)  2.61 us
    optimization_barrier x1, local copies, waits for them, and re-layouts, chip_shards(): got, panels = lax.optimization_barrier((got, panels))  2.42 us
    ppermute x3, waiting for transfers between devices, chip_shards(): lax.ppermute(pair, 'orient', [(d, (d + 2 * s) % devices) for d in range(d...  2.26 us
  transfers between devices with their start and end apart: 23, of which 12 were waited for; matrix products, arithmetic and copies ran while one was open for 2% of the time, Pallas kernels for 21%

profile of v2, /device:TPU:0, one launch (start us, length us, event | category | flops | bytes accessed | tf_op | source)
XLA Modules:
  0.0 85.3 jit_solution(4853439534811993713)
XLA Ops:
  0.0 1.1 %copy.13 = bf16[1,16,2,7296]{3,1,2,0:T(8,128)(2,1)S(1)} copy(bf16[1,16,2,7296]{3,2,1,0:T(2,128)(2,1)} %param.9) | data formatting | bytes 933888 | tf_op args[0]
  1.1 0.7 convert_bitcast_fusion
  1.8 0.1 copy.8
  1.9 0.7 copy.7
  2.7 0.1 fusion.2
  2.8 0.5 collective-permute-start.4
  3.3 1.1 %collective-permute-done.4.refs_1_.refs_7_ = bf16[16,7424]{1,0:T(8,128)(2,1)S(1)} collective-permute-done((bf16[16,7424]{1,0:T(8,128)(2,1)S(1)}, bf16[16,7424]{1,0:T(8,128)(2,1)S(1)}, u32[]{:S(2)}, u32[]{:S(2)}) %collective-permute-start.4) | collective-permute-done | bytes 237600 | tf_op jit(solution)/shard_map/ppermute | solution.py:289
  4.4 2.4 %copy.12 = bf16[1,1,128,2,7296]{4,2,3,1,0:T(8,128)(2,1)S(1)} copy(bf16[1,1,128,2,7296]{4,3,2,1,0:T(2,128)(2,1)} %param.13) | data formatting | bytes 7471104 | tf_op jit(solution)/shard_map/optimization_barrier | solution.py:291
  6.9 1.4 %dynamic-slice_bitcast_fusion = bf16[128,7296]{1,0:T(8,128)(2,1)} fusion(bf16[2,128,7296]{2,1,0:T(8,128)(2,1)S(1)} %bitcast.24, s32[]{:T(128)S(6)} %select_n.44), kind=kLoop, calls=%fused_computation.1 | loop fusion | bytes 3735556 | tf_op jit(solution)/shard_map/jit(dynamic_index_in_dim)/squeeze | solution.py:294
  8.3 1.8 %copy-done = bf16[1,1,128,2,7296]{4,2,3,1,0:T(8,128)(2,1)} copy-done((bf16[1,1,128,2,7296]{4,2,3,1,0:T(8,128)(2,1)}, bf16[1,1,128,2,7296]{4,2,3,1,0:T(8,128)(2,1)S(1)}, u32[]{:S(2)}) %copy-start) | copy-done | bytes 3735576
  10.1 0.4 collective-permute-start.9
  10.4 2.7 %collective-permute-start = (bf16[16,7424]{1,0:T(8,128)(2,1)S(1)}, bf16[16,7424]{1,0:T(8,128)(2,1)S(1)}, u32[]{:S(2)}, u32[]{:S(2)}) collective-permute-start(bf16[16,7424]{1,0:T(8,128)(2,1)S(1)} %get-tuple-element.72.refs_0_.refs_6_), channel_id=1, source_target_pairs={{0,4},{2,6},{4,8},{6,10},{8,12},{10,14},{12,13},{14,15},{13,9},{15... | collective-permute-start | bytes 712712 | tf_op jit(solution)/shard_map/ppermute | solution.py:282
  13.2 1.9 %collective-permute-start.10 = (bf16[16,7424]{1,0:T(8,128)(2,1)S(1)}, bf16[16,7424]{1,0:T(8,128)(2,1)S(1)}, u32[]{:S(2)}, u32[]{:S(2)}) collective-permute-start(bf16[16,7424]{1,0:T(8,128)(2,1)S(1)} %get-tuple-element.72.refs_0_.refs_6_), channel_id=1, source_target_pairs={{0,1},{2,3},{4,0},{6,2},{8,4},{10,6},{12,8},{14,10},{13,12},{15,14... | collective-permute-start | bytes 712712 | tf_op jit(solution)/shard_map/ppermute | solution.py:282
  15.1 0.1 collective-permute-start.11
  15.2 4.5 %collective-permute-done.refs_2_.refs_8_ = bf16[16,7424]{1,0:T(8,128)(2,1)S(1)} collective-permute-done((bf16[16,7424]{1,0:T(8,128)(2,1)S(1)}, bf16[16,7424]{1,0:T(8,128)(2,1)S(1)}, u32[]{:S(2)}, u32[]{:S(2)}) %collective-permute-start) | collective-permute-done | bytes 237600 | tf_op jit(solution)/shard_map/ppermute | solution.py:282
  19.7 2.1 %collective-permute-start.1 = (bf16[16,7424]{1,0:T(8,128)(2,1)S(1)}, bf16[16,7424]{1,0:T(8,128)(2,1)S(1)}, u32[]{:S(2)}, u32[]{:S(2)}) collective-permute-start(bf16[16,7424]{1,0:T(8,128)(2,1)S(1)} %collective-permute-done.refs_2_.refs_8_), channel_id=1, source_target_pairs={{0,4},{2,6},{4,8},{6,10},{8,12},{10,14},{12,13},{14,15},{13,9},{15... | collective-permute-start | bytes 712712 | tf_op jit(solution)/shard_map/ppermute | solution.py:282
  21.8 0.0 collective-permute-done.5.refs_5_.refs_11_
  21.8 5.1 %collective-permute-done.10.refs_3_.refs_9_ = bf16[16,7424]{1,0:T(8,128)(2,1)S(1)} collective-permute-done((bf16[16,7424]{1,0:T(8,128)(2,1)S(1)}, bf16[16,7424]{1,0:T(8,128)(2,1)S(1)}, u32[]{:S(2)}, u32[]{:S(2)}) %collective-permute-start.10) | collective-permute-done | bytes 237600 | tf_op jit(solution)/shard_map/ppermute | solution.py:282
  26.9 2.0 %collective-permute-start.13 = (bf16[16,7424]{1,0:T(8,128)(2,1)S(1)}, bf16[16,7424]{1,0:T(8,128)(2,1)}, u32[]{:S(2)}, u32[]{:S(2)}) collective-permute-start(bf16[16,7424]{1,0:T(8,128)(2,1)S(1)} %collective-permute-done.11.refs_4_.refs_10_), channel_id=1, source_target_pairs={{0,4},{2,6},{4,8},{6,10},{8,12},{10,14},{12,13},{14,15},{13,9},{15... | collective-permute-start | bytes 712712 | tf_op jit(solution)/shard_map/ppermute | solution.py:282
  28.9 1.0 %collective-permute-done.1.refs_0_.refs_4_ = bf16[16,7424]{1,0:T(8,128)(2,1)S(1)} collective-permute-done((bf16[16,7424]{1,0:T(8,128)(2,1)S(1)}, bf16[16,7424]{1,0:T(8,128)(2,1)S(1)}, u32[]{:S(2)}, u32[]{:S(2)}) %collective-permute-start.1) | collective-permute-done | bytes 237600 | tf_op jit(solution)/shard_map/ppermute | solution.py:282
  29.9 2.1 %collective-permute-start.2 = (bf16[16,7424]{1,0:T(8,128)(2,1)S(1)}, bf16[16,7424]{1,0:T(8,128)(2,1)}, u32[]{:S(2)}, u32[]{:S(2)}) collective-permute-start(bf16[16,7424]{1,0:T(8,128)(2,1)S(1)} %collective-permute-done.1.refs_0_.refs_4_), channel_id=1, source_target_pairs={{0,4},{2,6},{4,8},{6,10},{8,12},{10,14},{12,13},{14,15},{13,9},{15... | collective-permute-start | bytes 712712 | tf_op jit(solution)/shard_map/ppermute | solution.py:282
  31.9 0.1 collective-permute-done.6.refs_3_.refs_7_
  32.1 1.4 %broadcast_in_dim.4.refs_12_.refs_8_.refs_4_ = f32[1,7296]{1,0:T(1,128)} reshape(f32[7296]{0:T(1024)} %param.12) | data formatting | bytes 58368 | tf_op jit(solution)/shard_map/broadcast_in_dim | solution.py:312
  33.5 3.7 %collective-permute-done.12.refs_1_.refs_5_ = bf16[16,7424]{1,0:T(8,128)(2,1)} collective-permute-done((bf16[16,7424]{1,0:T(8,128)(2,1)S(1)}, bf16[16,7424]{1,0:T(8,128)(2,1)}, u32[]{:S(2)}, u32[]{:S(2)}) %collective-permute-start.12) | collective-permute-done | bytes 237600 | tf_op jit(solution)/shard_map/ppermute | solution.py:282
  37.2 2.0 %collective-permute-start.15 = (bf16[16,7424]{1,0:T(8,128)(2,1)}, bf16[16,7424]{1,0:T(8,128)(2,1)S(1)}, u32[]{:S(2)}, u32[]{:S(2)}) collective-permute-start(bf16[16,7424]{1,0:T(8,128)(2,1)} %collective-permute-done.13.refs_2_.refs_6_), channel_id=1, source_target_pairs={{0,4},{2,6},{4,8},{6,10},{8,12},{10,14},{12,13},{14,15},{13,9},{15... | collective-permute-start | bytes 712712 | tf_op jit(solution)/shard_map/ppermute | solution.py:282
  39.2 0.1 pad_add_fusion.spot
  39.3 1.5 %collective-permute-done.2.refs_0_.refs_4_ = bf16[16,7424]{1,0:T(8,128)(2,1)} collective-permute-done((bf16[16,7424]{1,0:T(8,128)(2,1)S(1)}, bf16[16,7424]{1,0:T(8,128)(2,1)}, u32[]{:S(2)}, u32[]{:S(2)}) %collective-permute-start.2) | collective-permute-done | bytes 237600 | tf_op jit(solution)/shard_map/ppermute | solution.py:282
  40.8 2.0 %collective-permute-start.3 = (bf16[16,7424]{1,0:T(8,128)(2,1)}, bf16[16,7424]{1,0:T(8,128)(2,1)S(1)}, u32[]{:S(2)}, u32[]{:S(2)}) collective-permute-start(bf16[16,7424]{1,0:T(8,128)(2,1)} %collective-permute-done.2.refs_0_.refs_4_), channel_id=1, source_target_pairs={{0,4},{2,6},{4,8},{6,10},{8,12},{10,14},{12,13},{14,15},{13,9},{15... | collective-permute-start | bytes 712712 | tf_op jit(solution)/shard_map/ppermute | solution.py:282
  42.8 2.0 %copy-done.1 = bf16[1,1,128,2,7296]{4,2,3,1,0:T(8,128)(2,1)S(1)} copy-done((bf16[1,1,128,2,7296]{4,2,3,1,0:T(8,128)(2,1)S(1)}, bf16[1,1,128,2,7296]{4,2,3,1,0:T(8,128)(2,1)}, u32[]{:S(2)}) %copy-start.1) | copy-done | bytes 3735576
  44.9 0.7 copy-done.3
  45.6 5.9 %shard_map.56 = (f32[64,128]{1,0:T(8,128)S(1)}, f32[64,128]{1,0:T(8,128)S(1)}, f32[64,128]{1,0:T(8,128)S(1)}) custom-call(s32[4]{0:T(128)S(1)} %pad_add_fusion.spot, bf16[16,7424]{1,0:T(8,128)(2,1)S(1)} %collective-permute-done.1.refs_0_.refs_4_, bf16[16,7424]{1,0:T(8,128)(2,1)} %collective-permute-done.12.refs_1_.refs_5_, ...), custom_call_target="tpu_custom_call" | custom-call | flops 956301312 | bytes 4669440 | tf_op jit(solution)/shard_map/pallas_call | solution.py:182
  51.5 6.6 %shard_map.55 = (f32[96,128]{1,0:T(8,128)S(1)}, f32[96,128]{1,0:T(8,128)S(1)}, f32[96,128]{1,0:T(8,128)S(1)}) custom-call(s32[4]{0:T(128)S(1)} %pad_add_fusion.spot, bf16[16,7424]{1,0:T(8,128)(2,1)S(1)} %get-tuple-element.72.refs_0_.refs_6_, bf16[16,7424]{1,0:T(8,128)(2,1)S(1)} %collective-permute-done.4.refs_1_.refs_7_, ...), custom_call_target="tpu_custom_call" | custom-call | flops 956301312 | bytes 5136384 | tf_op jit(solution)/shard_map/pallas_call | solution.py:182
  58.2 5.6 %shard_map.57 = (f32[64,128]{1,0:T(8,128)S(1)}, f32[64,128]{1,0:T(8,128)S(1)}, f32[64,128]{1,0:T(8,128)S(1)}) custom-call(s32[4]{0:T(128)S(1)} %pad_add_fusion.spot, bf16[16,7424]{1,0:T(8,128)(2,1)} %collective-permute-done.2.refs_0_.refs_4_, bf16[16,7424]{1,0:T(8,128)(2,1)S(1)} %collective-permute-done.14.refs_1_.refs_5_, ...), custom_call_target="tpu_custom_call" | custom-call | flops 956301312 | bytes 4669440 | tf_op jit(solution)/shard_map/pallas_call | solution.py:182
  63.8 4.4 %shard_map.58 = (f32[128,128]{1,0:T(8,128)S(1)}, f32[128,128]{1,0:T(8,128)S(1)}, f32[128,128]{1,0:T(8,128)S(1)}, f32[128,128]{1,0:T(8,128)S(1)}, f32[128,128]{1,0:T(8,128)S(1)}) custom-call(s32[4]{0:T(128)S(1)} %pad_add_fusion.spot, bf16[16,7424]{1,0:T(8,128)(2,1)S(1)} %collective-permute-done.3.refs_0_.refs_2_, ...), custom_call_target="tpu_custom_call" | custom-call | flops 956301312 | bytes 4202496 | tf_op jit(solution)/shard_map/pallas_call | solution.py:182
  68.3 0.1 collective-permute-start.16
  68.3 2.0 %collective-permute-start.17 = (f32[128,128]{1,0:T(8,128)S(1)}, f32[128,128]{1,0:T(8,128)S(1)}, u32[]{:S(2)}, u32[]{:S(2)}) collective-permute-start(f32[128,128]{1,0:T(8,128)S(1)} %get-tuple-element.61), channel_id=1, source_target_pairs={{0,1},{1,0},{2,3},{3,2},{4,5},{5,4},{6,7},{7,6},{8,9},{9,8},{10,11... | collective-permute-start | bytes 196616 | tf_op jit(solution)/shard_map/ppermute | solution.py:323
  70.3 0.1 collective-permute-start.18
  70.4 2.6 %collective-permute-done.17.across = f32[128,128]{1,0:T(8,128)S(1)} collective-permute-done((f32[128,128]{1,0:T(8,128)S(1)}, f32[128,128]{1,0:T(8,128)S(1)}, u32[]{:S(2)}, u32[]{:S(2)}) %collective-permute-start.17) | collective-permute-done | bytes 65568 | tf_op jit(solution)/shard_map/ppermute | solution.py:323
  73.0 1.4 %collective-permute-done.18.both = f32[128,128]{1,0:T(8,128)S(1)} collective-permute-done((f32[128,128]{1,0:T(8,128)S(1)}, f32[128,128]{1,0:T(8,128)S(1)}, u32[]{:S(2)}, u32[]{:S(2)}) %collective-permute-start.18) | collective-permute-done | bytes 65568 | tf_op jit(solution)/shard_map/ppermute | solution.py:324
  74.4 1.1 %shard_map.59 = (f32[128,256]{1,0:T(8,128)S(1)}, f32[128,128]{1,0:T(8,128)S(1)}, f32[8,128]{1,0:T(8,128)S(1)}) custom-call(s32[4]{0:T(128)S(1)} %pad_add_fusion.spot, f32[128,128]{1,0:T(8,128)S(1)} %get-tuple-element.59.mine, f32[128,128]{1,0:T(8,128)S(1)} %collective-permute-done.16.mate, f32[128,128]{1,0:T(8,128)S(1)} %collective-permute-done.17.across, ...), custom_call_target="tpu_custom_call" | custom-call | tf_op jit(solution)/shard_map/pallas_call | solution.py:330
  75.5 0.2 collective-permute-start.19
  75.7 1.0 %collective-permute-done.19 = f32[8,128]{1,0:T(8,128)S(1)} collective-permute-done((f32[8,128]{1,0:T(8,128)S(1)}, f32[8,128]{1,0:T(8,128)S(1)}, u32[]{:S(2)}, u32[]{:S(2)}) %collective-permute-start.19) | collective-permute-done | bytes 4128 | tf_op jit(solution)/shard_map/ppermute | solution.py:342
  76.7 1.6 %collective-permute-start.20 = (f32[8,128]{1,0:T(8,128)S(1)}, f32[8,128]{1,0:T(8,128)S(1)}, u32[]{:S(2)}, u32[]{:S(2)}) collective-permute-start(f32[8,128]{1,0:T(8,128)S(1)} %scatter.9.refs_1_), channel_id=1, source_target_pairs={{0,4},{2,6},{4,8},{6,10},{8,12},{10,14},{12,0},{14,2},{1,5},{3,7},... | collective-permute-start | bytes 12296 | tf_op jit(solution)/shard_map/ppermute | solution.py:347
  78.4 2.6 %collective-permute-start.21 = (f32[8,128]{1,0:T(8,128)S(1)}, f32[8,128]{1,0:T(8,128)S(1)}, u32[]{:S(2)}, u32[]{:S(2)}) collective-permute-start(f32[8,128]{1,0:T(8,128)S(1)} %scatter.9.refs_1_), channel_id=1, source_target_pairs={{0,8},{2,10},{4,12},{6,14},{8,0},{10,2},{12,4},{14,6},{1,9},{3,11}... | collective-permute-start | bytes 12296 | tf_op jit(solution)/shard_map/ppermute | solution.py:347
  81.0 1.3 %collective-permute-start.22 = (f32[8,128]{1,0:T(8,128)S(1)}, f32[8,128]{1,0:T(8,128)S(1)}, u32[]{:S(2)}, u32[]{:S(2)}) collective-permute-start(f32[8,128]{1,0:T(8,128)S(1)} %scatter.9.refs_1_), channel_id=1, source_target_pairs={{0,12},{2,14},{4,0},{6,2},{8,4},{10,6},{12,8},{14,10},{1,13},{3,15... | collective-permute-start | bytes 12296 | tf_op jit(solution)/shard_map/ppermute | solution.py:347
  82.3 0.6 collective-permute-done.21.refs_3_
  82.9 1.7 %collective-permute-done.22.refs_4_ = f32[8,128]{1,0:T(8,128)S(1)} collective-permute-done((f32[8,128]{1,0:T(8,128)S(1)}, f32[8,128]{1,0:T(8,128)S(1)}, u32[]{:S(2)}, u32[]{:S(2)}) %collective-permute-start.22) | collective-permute-done | bytes 4128 | tf_op jit(solution)/shard_map/ppermute | solution.py:347
  84.6 0.8 shard_map.60
  (26 shorter events, 0.2 us)
Async XLA Ops:
  2.8 1.6 %collective-permute-start.4 = (bf16[16,7424]{1,0:T(8,128)(2,1)S(1)}, bf16[16,7424]{1,0:T(8,128)(2,1)S(1)}, u32[]{:S(2)}, u32[]{:S(2)}) collective-permute-start(bf16[16,7424]{1,0:T(8,128)(2,1)S(1)} %get-tuple-element.71), channel_id=1, source_target_pairs={{0,2},{2,0},{4,6},{6,4},{8,10},{10,8},{12,14},{14,12},{1,3},{3,1},... | collective-permute-start | bytes 712712 | tf_op jit(solution)/shard_map/ppermute | solution.py:289
  8.3 1.8 %copy-start = (bf16[1,1,128,2,7296]{4,2,3,1,0:T(8,128)(2,1)}, bf16[1,1,128,2,7296]{4,2,3,1,0:T(8,128)(2,1)S(1)}, u32[]{:S(2)}) copy-start(bf16[1,1,128,2,7296]{4,2,3,1,0:T(8,128)(2,1)S(1)} %copy.12) | copy-start | bytes 11206660
  10.1 32.8 %collective-permute-start.9 = (bf16[128,7296]{1,0:T(8,128)(2,1)}, bf16[128,7296]{1,0:T(8,128)(2,1)S(1)}, u32[]{:S(2)}, u32[]{:S(2)}) collective-permute-start(bf16[128,7296]{1,0:T(8,128)(2,1)} %dynamic-slice_bitcast_fusion), channel_id=1, source_target_pairs={{0,2},{2,0},{4,6},{6,4},{8,10},{10,8},{12,14},{14,12},{1,3},{3,1},... | collective-permute-start | bytes 5603336 | tf_op jit(solution)/shard_map/ppermute | solution.py:293
  10.4 9.2 %collective-permute-start = (bf16[16,7424]{1,0:T(8,128)(2,1)S(1)}, bf16[16,7424]{1,0:T(8,128)(2,1)S(1)}, u32[]{:S(2)}, u32[]{:S(2)}) collective-permute-start(bf16[16,7424]{1,0:T(8,128)(2,1)S(1)} %get-tuple-element.72.refs_0_.refs_6_), channel_id=1, source_target_pairs={{0,4},{2,6},{4,8},{6,10},{8,12},{10,14},{12,13},{14,15},{13,9},{15... | collective-permute-start | bytes 712712 | tf_op jit(solution)/shard_map/ppermute | solution.py:282
  13.2 8.6 %collective-permute-start.5 = (bf16[16,7424]{1,0:T(8,128)(2,1)S(1)}, bf16[16,7424]{1,0:T(8,128)(2,1)S(1)}, u32[]{:S(2)}, u32[]{:S(2)}) collective-permute-start(bf16[16,7424]{1,0:T(8,128)(2,1)S(1)} %collective-permute-done.4.refs_1_.refs_7_), channel_id=1, source_target_pairs={{0,1},{2,3},{4,0},{6,2},{8,4},{10,6},{12,8},{14,10},{13,12},{15,14... | collective-permute-start | bytes 712712 | tf_op jit(solution)/shard_map/ppermute | solution.py:282
  13.2 13.7 %collective-permute-start.10 = (bf16[16,7424]{1,0:T(8,128)(2,1)S(1)}, bf16[16,7424]{1,0:T(8,128)(2,1)S(1)}, u32[]{:S(2)}, u32[]{:S(2)}) collective-permute-start(bf16[16,7424]{1,0:T(8,128)(2,1)S(1)} %get-tuple-element.72.refs_0_.refs_6_), channel_id=1, source_target_pairs={{0,1},{2,3},{4,0},{6,2},{8,4},{10,6},{12,8},{14,10},{13,12},{15,14... | collective-permute-start | bytes 712712 | tf_op jit(solution)/shard_map/ppermute | solution.py:282
  15.1 11.8 %collective-permute-start.11 = (bf16[16,7424]{1,0:T(8,128)(2,1)S(1)}, bf16[16,7424]{1,0:T(8,128)(2,1)S(1)}, u32[]{:S(2)}, u32[]{:S(2)}) collective-permute-start(bf16[16,7424]{1,0:T(8,128)(2,1)S(1)} %collective-permute-done.4.refs_1_.refs_7_), channel_id=1, source_target_pairs={{0,4},{2,6},{4,8},{6,10},{8,12},{10,14},{12,13},{14,15},{13,9},{15... | collective-permute-start | bytes 712712 | tf_op jit(solution)/shard_map/ppermute | solution.py:282
  19.7 10.2 %collective-permute-start.1 = (bf16[16,7424]{1,0:T(8,128)(2,1)S(1)}, bf16[16,7424]{1,0:T(8,128)(2,1)S(1)}, u32[]{:S(2)}, u32[]{:S(2)}) collective-permute-start(bf16[16,7424]{1,0:T(8,128)(2,1)S(1)} %collective-permute-done.refs_2_.refs_8_), channel_id=1, source_target_pairs={{0,4},{2,6},{4,8},{6,10},{8,12},{10,14},{12,13},{14,15},{13,9},{15... | collective-permute-start | bytes 712712 | tf_op jit(solution)/shard_map/ppermute | solution.py:282
  21.8 10.3 %collective-permute-start.6 = (bf16[16,7424]{1,0:T(8,128)(2,1)S(1)}, bf16[16,7424]{1,0:T(8,128)(2,1)}, u32[]{:S(2)}, u32[]{:S(2)}) collective-permute-start(bf16[16,7424]{1,0:T(8,128)(2,1)S(1)} %collective-permute-done.5.refs_5_.refs_11_), channel_id=1, source_target_pairs={{0,1},{2,3},{4,0},{6,2},{8,4},{10,6},{12,8},{14,10},{13,12},{15,14... | collective-permute-start | bytes 712712 | tf_op jit(solution)/shard_map/ppermute | solution.py:282
  26.9 10.3 %collective-permute-start.12 = (bf16[16,7424]{1,0:T(8,128)(2,1)S(1)}, bf16[16,7424]{1,0:T(8,128)(2,1)}, u32[]{:S(2)}, u32[]{:S(2)}) collective-permute-start(bf16[16,7424]{1,0:T(8,128)(2,1)S(1)} %collective-permute-done.10.refs_3_.refs_9_), channel_id=1, source_target_pairs={{0,1},{2,3},{4,0},{6,2},{8,4},{10,6},{12,8},{14,10},{13,12},{15,14... | collective-permute-start | bytes 712712 | tf_op jit(solution)/shard_map/ppermute | solution.py:282
  26.9 10.3 %collective-permute-start.13 = (bf16[16,7424]{1,0:T(8,128)(2,1)S(1)}, bf16[16,7424]{1,0:T(8,128)(2,1)}, u32[]{:S(2)}, u32[]{:S(2)}) collective-permute-start(bf16[16,7424]{1,0:T(8,128)(2,1)S(1)} %collective-permute-done.11.refs_4_.refs_10_), channel_id=1, source_target_pairs={{0,4},{2,6},{4,8},{6,10},{8,12},{10,14},{12,13},{14,15},{13,9},{15... | collective-permute-start | bytes 712712 | tf_op jit(solution)/shard_map/ppermute | solution.py:282
  29.9 10.9 %collective-permute-start.2 = (bf16[16,7424]{1,0:T(8,128)(2,1)S(1)}, bf16[16,7424]{1,0:T(8,128)(2,1)}, u32[]{:S(2)}, u32[]{:S(2)}) collective-permute-start(bf16[16,7424]{1,0:T(8,128)(2,1)S(1)} %collective-permute-done.1.refs_0_.refs_4_), channel_id=1, source_target_pairs={{0,4},{2,6},{4,8},{6,10},{8,12},{10,14},{12,13},{14,15},{13,9},{15... | collective-permute-start | bytes 712712 | tf_op jit(solution)/shard_map/ppermute | solution.py:282
  32.1 10.8 %collective-permute-start.7 = (bf16[16,7424]{1,0:T(8,128)(2,1)}, bf16[16,7424]{1,0:T(8,128)(2,1)}, u32[]{:S(2)}, u32[]{:S(2)}) collective-permute-start(bf16[16,7424]{1,0:T(8,128)(2,1)} %collective-permute-done.6.refs_3_.refs_7_), channel_id=1, source_target_pairs={{0,1},{2,3},{4,0},{6,2},{8,4},{10,6},{12,8},{14,10},{13,12},{15,14... | collective-permute-start | bytes 712712 | tf_op jit(solution)/shard_map/ppermute | solution.py:282
  37.2 21.0 %collective-permute-start.14 = (bf16[16,7424]{1,0:T(8,128)(2,1)}, bf16[16,7424]{1,0:T(8,128)(2,1)S(1)}, u32[]{:S(2)}, u32[]{:S(2)}) collective-permute-start(bf16[16,7424]{1,0:T(8,128)(2,1)} %collective-permute-done.12.refs_1_.refs_5_), channel_id=1, source_target_pairs={{0,1},{2,3},{4,0},{6,2},{8,4},{10,6},{12,8},{14,10},{13,12},{15,14... | collective-permute-start | bytes 712712 | tf_op jit(solution)/shard_map/ppermute | solution.py:282
  37.2 21.0 %collective-permute-start.15 = (bf16[16,7424]{1,0:T(8,128)(2,1)}, bf16[16,7424]{1,0:T(8,128)(2,1)S(1)}, u32[]{:S(2)}, u32[]{:S(2)}) collective-permute-start(bf16[16,7424]{1,0:T(8,128)(2,1)} %collective-permute-done.13.refs_2_.refs_6_), channel_id=1, source_target_pairs={{0,4},{2,6},{4,8},{6,10},{8,12},{10,14},{12,13},{14,15},{13,9},{15... | collective-permute-start | bytes 712712 | tf_op jit(solution)/shard_map/ppermute | solution.py:282
  40.8 23.0 %collective-permute-start.3 = (bf16[16,7424]{1,0:T(8,128)(2,1)}, bf16[16,7424]{1,0:T(8,128)(2,1)S(1)}, u32[]{:S(2)}, u32[]{:S(2)}) collective-permute-start(bf16[16,7424]{1,0:T(8,128)(2,1)} %collective-permute-done.2.refs_0_.refs_4_), channel_id=1, source_target_pairs={{0,4},{2,6},{4,8},{6,10},{8,12},{10,14},{12,13},{14,15},{13,9},{15... | collective-permute-start | bytes 712712 | tf_op jit(solution)/shard_map/ppermute | solution.py:282
  42.8 21.0 %collective-permute-start.8 = (bf16[16,7424]{1,0:T(8,128)(2,1)}, bf16[16,7424]{1,0:T(8,128)(2,1)S(1)}, u32[]{:S(2)}, u32[]{:S(2)}) collective-permute-start(bf16[16,7424]{1,0:T(8,128)(2,1)} %collective-permute-done.7.refs_3_.refs_7_), channel_id=1, source_target_pairs={{0,1},{2,3},{4,0},{6,2},{8,4},{10,6},{12,8},{14,10},{13,12},{15,14... | collective-permute-start | bytes 712712 | tf_op jit(solution)/shard_map/ppermute | solution.py:282
  42.8 2.1 %copy-start.1 = (bf16[1,1,128,2,7296]{4,2,3,1,0:T(8,128)(2,1)S(1)}, bf16[1,1,128,2,7296]{4,2,3,1,0:T(8,128)(2,1)}, u32[]{:S(2)}) copy-start(bf16[1,1,128,2,7296]{4,2,3,1,0:T(8,128)(2,1)} %copy-done) | copy-start | bytes 11206660
  44.9 0.7 copy-start.3
  45.6 5.9 %copy-start.2 = (bf16[1,1,128,2,7296]{4,2,3,1,0:T(8,128)(2,1)S(1)}, bf16[1,1,128,2,7296]{4,2,3,1,0:T(8,128)(2,1)}, u32[]{:S(2)}) copy-start(bf16[1,1,128,2,7296]{4,2,3,1,0:T(8,128)(2,1)} %copy-done) | copy-start | bytes 11206660
  68.3 2.2 %collective-permute-start.16 = (f32[128,128]{1,0:T(8,128)S(1)}, f32[128,128]{1,0:T(8,128)S(1)}, u32[]{:S(2)}, u32[]{:S(2)}) collective-permute-start(f32[128,128]{1,0:T(8,128)S(1)} %get-tuple-element.60), channel_id=1, source_target_pairs={{0,2},{2,0},{4,6},{6,4},{8,10},{10,8},{12,14},{14,12},{1,3},{3,1},... | collective-permute-start | bytes 196616 | tf_op jit(solution)/shard_map/ppermute | solution.py:322
  68.3 4.7 %collective-permute-start.17 = (f32[128,128]{1,0:T(8,128)S(1)}, f32[128,128]{1,0:T(8,128)S(1)}, u32[]{:S(2)}, u32[]{:S(2)}) collective-permute-start(f32[128,128]{1,0:T(8,128)S(1)} %get-tuple-element.61), channel_id=1, source_target_pairs={{0,1},{1,0},{2,3},{3,2},{4,5},{5,4},{6,7},{7,6},{8,9},{9,8},{10,11... | collective-permute-start | bytes 196616 | tf_op jit(solution)/shard_map/ppermute | solution.py:323
  70.3 4.0 %collective-permute-start.18 = (f32[128,128]{1,0:T(8,128)S(1)}, f32[128,128]{1,0:T(8,128)S(1)}, u32[]{:S(2)}, u32[]{:S(2)}) collective-permute-start(f32[128,128]{1,0:T(8,128)S(1)} %get-tuple-element.62), channel_id=1, source_target_pairs={{0,3},{1,2},{2,1},{3,0},{4,7},{5,6},{6,5},{7,4},{8,11},{9,10},{10,... | collective-permute-start | bytes 196616 | tf_op jit(solution)/shard_map/ppermute | solution.py:324
  75.5 1.2 %collective-permute-start.19 = (f32[8,128]{1,0:T(8,128)S(1)}, f32[8,128]{1,0:T(8,128)S(1)}, u32[]{:S(2)}, u32[]{:S(2)}) collective-permute-start(f32[8,128]{1,0:T(8,128)S(1)} %get-tuple-element.64.refs_0_), channel_id=1, source_target_pairs={{0,2},{2,0},{4,6},{6,4},{8,10},{10,8},{12,14},{14,12},{1,3},{3,1},... | collective-permute-start | bytes 12296 | tf_op jit(solution)/shard_map/ppermute | solution.py:342
  76.7 5.6 %collective-permute-start.20 = (f32[8,128]{1,0:T(8,128)S(1)}, f32[8,128]{1,0:T(8,128)S(1)}, u32[]{:S(2)}, u32[]{:S(2)}) collective-permute-start(f32[8,128]{1,0:T(8,128)S(1)} %scatter.9.refs_1_), channel_id=1, source_target_pairs={{0,4},{2,6},{4,8},{6,10},{8,12},{10,14},{12,0},{14,2},{1,5},{3,7},... | collective-permute-start | bytes 12296 | tf_op jit(solution)/shard_map/ppermute | solution.py:347
  78.4 4.5 %collective-permute-start.21 = (f32[8,128]{1,0:T(8,128)S(1)}, f32[8,128]{1,0:T(8,128)S(1)}, u32[]{:S(2)}, u32[]{:S(2)}) collective-permute-start(f32[8,128]{1,0:T(8,128)S(1)} %scatter.9.refs_1_), channel_id=1, source_target_pairs={{0,8},{2,10},{4,12},{6,14},{8,0},{10,2},{12,4},{14,6},{1,9},{3,11}... | collective-permute-start | bytes 12296 | tf_op jit(solution)/shard_map/ppermute | solution.py:347
  81.0 3.6 %collective-permute-start.22 = (f32[8,128]{1,0:T(8,128)S(1)}, f32[8,128]{1,0:T(8,128)S(1)}, u32[]{:S(2)}, u32[]{:S(2)}) collective-permute-start(f32[8,128]{1,0:T(8,128)S(1)} %scatter.9.refs_1_), channel_id=1, source_target_pairs={{0,12},{2,14},{4,0},{6,2},{8,4},{10,6},{12,8},{14,10},{1,13},{3,15... | collective-permute-start | bytes 12296 | tf_op jit(solution)/shard_map/ppermute | solution.py:347

commit v3 on v2

--- a/solution.py
+++ b/solution.py
@@ -39,163 +39,145 @@
     )
 
 
-def add_scores(rows, meta, noise, panels, outs, tables, tiles, columns):
-    step = pl.program_id(0)
+def particle_facts(meta):
+    return jnp.concatenate([m[...].astype(jnp.float32).T[: m.shape[0]] for m in meta], axis=0)
+
+
+def add_scores(rows, spot, noise, sides, mate_panel, tables, sums, segments):
+    columns = noise.shape[1]
+    width = columns // segments
+    tiles = width // LANES
     sin_a, cos_a, sin_b, cos_b = tables
     count = sin_a.shape[0]
-
-    @pl.when(step == 0)
-    def _():
-        focus = jnp.concatenate([m[:, 0:1] for m in meta], axis=0).astype(jnp.float32)
-        rate = CTF_PHASE * focus
-        lane = lax.broadcasted_iota(jnp.int32, (count, LANES), 1).astype(jnp.float32)
-        coarse_sin, coarse_cos = sin_cos(rate * (lane * (LANES / columns)) + 0.1)
-        sin_a[...] = -coarse_sin
-        cos_a[...] = -coarse_cos
-        fine_sin, fine_cos = sin_cos(rate * ((lane + 0.5) / columns))
-        sin_b[...] = fine_sin
-        cos_b[...] = fine_cos
-        for out in outs:
-            out[...] = jnp.zeros_like(out)
-
-    shift = lax.rem(LANES - step * tiles, LANES)
-    sa = pltpu.roll(sin_a[...], shift, 1)
-    ca = pltpu.roll(cos_a[...], shift, 1)
-    sb = sin_b[...]
-    cb = cos_b[...]
-    scaled_parts, energy_parts = [], []
-    for t in range(tiles):
-        window = slice(t * LANES, (t + 1) * LANES)
-        contrast = sa[:, t : t + 1] * cb + ca[:, t : t + 1] * sb
-        weighted = contrast * noise[:, window]
-        image = jnp.concatenate([r[:, window] for r in rows], axis=0).astype(jnp.float32)
-        scaled_parts.append((weighted * image).astype(jnp.bfloat16))
-        energy_parts.append((contrast * weighted).astype(jnp.bfloat16))
-    scaled = jnp.concatenate(scaled_parts, axis=1)
-    energy = jnp.concatenate(energy_parts, axis=1)
-    contract = (((1,), (1,)), ((), ()))
-    for panel, out in zip(panels, outs):
-        values = panel[...]
-        squared = values * values
-        correlate = lax.dot_general(scaled, values, contract, preferred_element_type=jnp.float32)
-        power = lax.dot_general(energy, squared, contract, preferred_element_type=jnp.float32)
-        out[...] += correlate - 0.5 * power
-
-
-def batch_kernel(n, tiles, columns, spot, *refs):
-    del spot
-    rows, meta = refs[:n], refs[n : 2 * n]
-    noise, own_panel, mate_panel, own_out, mate_out, fact_out = refs[2 * n : 2 * n + 6]
-    tables = refs[2 * n + 6 :]
-    add_scores(
-        rows, meta, noise, (own_panel, mate_panel), (own_out, mate_out), tables, tiles, columns
-    )
-    fact_out[...] = jnp.concatenate([m[...] for m in meta], axis=0).astype(jnp.float32)
-
-
-def last_kernel(n, tiles, columns, steps, orders, spot, *refs):
-    rows, meta = refs[:n], refs[n : 2 * n]
-    noise, own_panel, mate_panel = refs[2 * n : 2 * n + 3]
-    earlier = refs[2 * n + 3 : 2 * n + 3 + 3 * (len(orders) - 1)]
-    here_own, here_mate, there_own, there_mate, facts, own_sum, mate_sum, *rest = refs[
-        2 * n + 3 + len(earlier) :
-    ]
-    tables, (own_all, mate_all, fact_all) = rest[:4], rest[4:]
-    add_scores(
-        rows, meta, noise, (own_panel, mate_panel), (own_sum, mate_sum), tables, tiles, columns
-    )
-
-    @pl.when(pl.program_id(0) == steps - 1)
-    def _():
-        group, position, core = spot[0], spot[1], spot[2]
-        each = rows[0].shape[0]
-        ring = own_all.shape[0] // (2 * each)
-        half = ring // 2
-        last_facts = jnp.concatenate([m[...] for m in meta], axis=0).astype(jnp.float32)
-        for index, order in enumerate(orders):
-            if index < len(orders) - 1:
-                own, mate, fact = [r[...] for r in earlier[3 * index : 3 * index + 3]]
-            else:
-                own, mate, fact = own_sum[...], mate_sum[...], last_facts
-            for k, (distance, crossed) in enumerate(order):
-                place = lax.rem(position + distance + ring, ring)
-                far = place >= half
-                level = jnp.where(far, ring - 1 - place, place)
-                device = 2 * level + (1 - core if crossed else core)
-                side = jnp.where(far, 1, 0)
-                other = jnp.where(side == group, 0, 1)
-                start = pl.multiple_of((other * ring + device) * each, each)
-                piece = slice(k * each, (k + 1) * each)
-                own_all[pl.ds(start, each), :] = own[piece]
-                mate_all[pl.ds(start, each), :] = mate[piece]
-                fact_all[pl.ds(start, each), :] = fact[piece]
-        everyone = ring * each
-        here_own[...] = own_all[:everyone]
-        here_mate[...] = mate_all[:everyone]
-        there_own[...] = own_all[everyone:]
-        there_mate[...] = mate_all[everyone:]
-        facts[...] = fact_all[:everyone]
+    facts = particle_facts([r.at[:, pl.ds(columns, LANES)] for r in rows])
+    rate = CTF_PHASE * facts[:, 0:1]
+    lane = lax.broadcasted_iota(jnp.int32, (count, LANES), 1).astype(jnp.float32)
+    coarse_sin, coarse_cos = sin_cos(rate * (lane * (LANES / columns)) + 0.1)
+    sin_a[...] = -coarse_sin
+    cos_a[...] = -coarse_cos
+    fine_sin, fine_cos = sin_cos(rate * ((lane + 0.5) / columns))
+    sin_b[...] = fine_sin
+    cos_b[...] = fine_cos
+    for total in sums:
+        total[...] = jnp.zeros_like(total)
+    core = spot[2]
+
+    def segment(index, carry):
+        start = pl.multiple_of(index * width, LANES)
+        shift = lax.rem(LANES - index * tiles, LANES)
+        sa = pltpu.roll(sin_a[...], shift, 1)
+        ca = pltpu.roll(cos_a[...], shift, 1)
+        sb = sin_b[...]
+        cb = cos_b[...]
+        scaled_parts, energy_parts = [], []
+        for t in range(tiles):
+            window = pl.ds(start + t * LANES, LANES)
+            contrast = sa[:, t : t + 1] * cb + ca[:, t : t + 1] * sb
+            weighted = contrast * noise[:, window]
+            image = jnp.concatenate([r[:, window] for r in rows], axis=0).astype(jnp.float32)
+            scaled_parts.append((weighted * image).astype(jnp.bfloat16))
+            energy_parts.append((contrast * weighted).astype(jnp.bfloat16))
+        scaled = jnp.concatenate(scaled_parts, axis=1)
+        energy = jnp.concatenate(energy_parts, axis=1)
+        contract = (((1,), (1,)), ((), ()))
+        whole = pl.ds(start, width)
+        for values, total in ((sides[core, :, whole], sums[0]), (mate_panel[:, whole], sums[1])):
+            squared = values * values
+            correlate = lax.dot_general(
+                values, scaled, contract, preferred_element_type=jnp.float32
+            )
+            power = lax.dot_general(squared, energy, contract, preferred_element_type=jnp.float32)
+            total[...] += correlate - 0.5 * power
+        return carry
+
+    lax.fori_loop(0, segments, segment, 0)
+    return facts
+
+
+def batch_kernel(n, segments, spot, *refs):
+    rows = refs[:n]
+    noise, sides, mate_panel, own_out, mate_out, fact_out = refs[n : n + 6]
+    tables, sums = refs[n + 6 : n + 10], refs[n + 10 :]
+    facts = add_scores(rows, spot, noise, sides, mate_panel, tables, sums, segments)
+    own_out[...] = sums[0][...].T
+    mate_out[...] = sums[1][...].T
+    fact_out[...] = jnp.pad(facts, ((0, 0), (0, LANES - facts.shape[1])))
+
+
+def last_kernel(n, segments, orders, spot, *refs):
+    rows = refs[:n]
+    noise, sides, mate_panel = refs[n : n + 3]
+    earlier = refs[n + 3 : n + 3 + 3 * (len(orders) - 1)]
+    outs = refs[n + 3 + len(earlier) :]
+    here_own, here_mate, there_own, there_mate, facts = outs[:5]
+    tables, sums, (own_all, mate_all, fact_all) = outs[5:9], outs[9:11], outs[11:]
+    last_facts = add_scores(rows, spot, noise, sides, mate_panel, tables, sums, segments)
+    last_facts = jnp.pad(last_facts, ((0, 0), (0, LANES - last_facts.shape[1])))
+    group, position, core = spot[0], spot[1], spot[2]
+    each = rows[0].shape[0]
+    ring = own_all.shape[0] // (2 * each)
+    half = ring // 2
+    for index, order in enumerate(orders):
+        if index < len(orders) - 1:
+            own, mate, fact = [r[...] for r in earlier[3 * index : 3 * index + 3]]
+        else:
+            own, mate, fact = sums[0][...].T, sums[1][...].T, last_facts
+        for k, (distance, crossed) in enumerate(order):
+            place = lax.rem(position + distance + ring, ring)
+            far = place >= half
+            level = jnp.where(far, ring - 1 - place, place)
+            device = 2 * level + (1 - core if crossed else core)
+            side = jnp.where(far, 1, 0)
+            other = jnp.where(side == group, 0, 1)
+            start = pl.multiple_of((other * ring + device) * each, each)
+            piece = slice(k * each, (k + 1) * each)
+            own_all[pl.ds(start, each), :] = own[piece]
+            mate_all[pl.ds(start, each), :] = mate[piece]
+            fact_all[pl.ds(start, each), :] = fact[piece]
+    everyone = ring * each
+    here_own[...] = own_all[:everyone]
+    here_mate[...] = mate_all[:everyone]
+    there_own[...] = own_all[everyone:]
+    there_mate[...] = mate_all[everyone:]
+    facts[...] = fact_all[:everyone]
 
 
 def score_call(chunks, orders, earlier, spot, noise, sides, mate_panel):
     each = chunks[0].shape[0]
     orientations, columns = mate_panel.shape
     whole = columns // LANES
-    steps = next(s for s in (3, 2, 4, 5, 6, 7, 1) if whole % s == 0)
-    tiles = whole // steps
-    width = tiles * LANES
+    segments = next(s for s in (3, 2, 4, 5, 6, 7, 1) if whole % s == 0)
     n = len(chunks)
     count = each * n
-    row_spec = pl.BlockSpec((each, width), lambda s, spot: (0, s))
-    meta_spec = pl.BlockSpec((each, LANES), lambda s, spot: (0, whole))
-    fixed = lambda shape: pl.BlockSpec(shape, lambda s, spot: (0, 0))
-    in_specs = (
-        [row_spec] * n
-        + [meta_spec] * n
-        + [
-            pl.BlockSpec((1, width), lambda s, spot: (0, s)),
-            pl.BlockSpec((None, orientations, width), lambda s, spot: (spot[2], 0, s)),
-            pl.BlockSpec((orientations, width), lambda s, spot: (0, s)),
-        ]
-    )
-    table = [pltpu.VMEM((count, LANES), jnp.float32)] * 4
+    scratch = [pltpu.VMEM((count, LANES), jnp.float32)] * 4
+    scratch += [pltpu.VMEM((orientations, count), jnp.float32)] * 2
     single = jax.ShapeDtypeStruct((count, orientations), jnp.float32)
     if orders is None:
-        kernel = functools.partial(batch_kernel, n, tiles, columns)
+        kernel = functools.partial(batch_kernel, n, segments)
         out_shape = [single, single, jax.ShapeDtypeStruct((count, LANES), jnp.float32)]
-        scratch = table
         extra = []
     else:
         everyone = each * sum(len(o) for o in orders) // 2
-        kernel = functools.partial(last_kernel, n, tiles, columns, steps, orders)
+        kernel = functools.partial(last_kernel, n, segments, orders)
         block = jax.ShapeDtypeStruct((everyone, orientations), jnp.float32)
         out_shape = [block] * 4 + [jax.ShapeDtypeStruct((everyone, LANES), jnp.float32)]
-        sums = pltpu.VMEM((count, orientations), jnp.float32)
         whole_sums = pltpu.VMEM((2 * everyone, orientations), jnp.float32)
-        scratch = (
-            [sums, sums]
-            + table
-            + [whole_sums, whole_sums, pltpu.VMEM((2 * everyone, LANES), jnp.float32)]
-        )
+        scratch += [whole_sums, whole_sums, pltpu.VMEM((2 * everyone, LANES), jnp.float32)]
         extra = [e for triple in earlier for e in triple]
-        in_specs = in_specs + [fixed(e.shape) for e in extra]
+    vmem = pl.BlockSpec(memory_space=pltpu.VMEM)
     return pl.pallas_call(
         kernel,
-        grid_spec=pltpu.PrefetchScalarGridSpec(
-            num_scalar_prefetch=1,
-            grid=(steps,),
-            in_specs=in_specs,
-            out_specs=[fixed(o.shape) for o in out_shape],
-            scratch_shapes=scratch,
-        ),
+        in_specs=[pl.BlockSpec(memory_space=pltpu.SMEM)] + [vmem] * (n + 3 + len(extra)),
+        out_specs=[vmem] * len(out_shape),
         out_shape=out_shape,
+        scratch_shapes=scratch,
         compiler_params=pltpu.CompilerParams(vmem_limit_bytes=VMEM_LIMIT),
         cost_estimate=pl.CostEstimate(
             flops=8 * max(count, 128) * orientations * columns,
             bytes_accessed=4 * orientations * columns + 2 * count * columns,
             transcendentals=0,
         ),
-    )(spot, *chunks, *chunks, noise, sides, mate_panel, *extra)
+    )(spot, *chunks, noise, sides, mate_panel, *extra)
 
 
 def stats_kernel(search, slots_each, each, spot, mine, mate, across, both, facts, slots, chosen, stats):
@@ -281,23 +263,23 @@
         pairs = [(joint(p, c), joint(p + step, c)) for p in range(ring) for c in range(2)]
         return lax.ppermute(values, ("orient", "cls"), pairs)
 
-    facts = jnp.concatenate([defocus[0][:, None], block_ids[0].astype(jnp.bfloat16)], axis=1)
-    facts = jnp.pad(facts, ((0, 0), (0, LANES - facts.shape[1])))
+    facts = jnp.concatenate([defocus, block_ids[0].T.astype(jnp.bfloat16)], axis=0)
+    facts = jnp.pad(facts, ((0, per_device - facts.shape[0]), (0, LANES - per_device)))
     planes = lax.optimization_barrier(jnp.transpose(images[0], (1, 0, 2)))
     kept = jnp.concatenate([jnp.where(first, planes[0], planes[1]), facts], axis=1)
     given = jnp.concatenate([jnp.where(first, planes[1], planes[0]), facts], axis=1)
     got = lax.ppermute(given, "orient", mate_pairs)
 
-    got, panels = lax.optimization_barrier((got, panels))
-    sides = lax.optimization_barrier(jnp.transpose(panels[0, 0], (1, 0, 2)))
-    mate_panel = lax.ppermute(
-        lax.dynamic_index_in_dim(sides, 1 - core, 0, keepdims=False), "orient", mate_pairs
-    )
-
-    batches = [[((0, False), kept), ((0, True), got)]]
+    noise = noise_weight[None, :]
+    waiting = [((0, False), kept), ((0, True), got)]
     ahead = {False: kept, True: got}
     behind = {False: kept, True: got}
+    orders, earlier = [], []
     for step in range(1, chips + 1):
+        if earlier:
+            tie = earlier[-1][2]
+            ahead = {c: lax.optimization_barrier((v, tie))[0] for c, v in ahead.items()}
+            behind = {c: lax.optimization_barrier((v, tie))[0] for c, v in behind.items()}
         arrived = []
         for crossed in (False, True):
             if step < chips or not crossed:
@@ -306,17 +288,22 @@
             if step < chips or crossed:
                 behind[crossed] = forward(behind[crossed], -1)
                 arrived.append(((step, crossed), behind[crossed]))
-        batches.append(arrived)
-    batches = [batches[0] + batches[1]] + batches[2:]
-
-    noise = noise_weight[None, :]
-    orders = [[key for key, _ in batch] for batch in batches]
-    earlier = [
-        score_call([c for _, c in batch], None, None, spot, noise, sides, mate_panel)
-        for batch in batches[:-1]
-    ]
+        if step == 1:
+            _, panels = lax.optimization_barrier((ahead[False], panels))
+            sides = lax.optimization_barrier(jnp.transpose(panels[0, 0], (1, 0, 2)))
+            mate_panel = lax.ppermute(
+                lax.dynamic_index_in_dim(sides, 1 - core, 0, keepdims=False), "orient", mate_pairs
+            )
+        if step > 1:
+            orders.append([key for key, _ in waiting])
+            earlier.append(
+                score_call([c for _, c in waiting], None, None, spot, noise, sides, mate_panel)
+            )
+            waiting = []
+        waiting = waiting + arrived
+    orders.append([key for key, _ in waiting])
     here_own, here_mate, there_own, there_mate, own_facts = score_call(
-        [c for _, c in batches[-1]], orders, earlier, spot, noise, sides, mate_panel
+        [c for _, c in waiting], orders, earlier, spot, noise, sides, mate_panel
     )
 
     from_mate = lax.ppermute(here_mate, "orient", mate_pairs)

time: 85.8 us -> 83.1 us (0.969)
  Pallas kernels: 24.4 us -> 20.2 us
  local copies, waits for them, and re-layouts: 11.8 us -> 9.57 us
  starting transfers between devices: 23.8 us -> 25.8 us
  waiting for transfers between devices: 24.3 us -> 25.5 us
    pallas_call x4, Pallas kernels: 22.5 us -> 18.4 us  [score_call(): pl.pallas_call(kernel, in_specs=[pl.BlockSpec(memory_space=pltpu.SMEM)] +...]
    ppermute x14, starting transfers between devices: 15 us -> 18.6 us  [forward(): return lax.ppermute(values, ('orient', 'cls'), pairs)]
    ppermute x1, waiting for transfers between devices: 1.13 us -> 3.29 us  [chip_shards(): got = lax.ppermute(given, 'orient', mate_pairs)]
    ppermute x3, starting transfers between devices: 5.57 us -> 4.52 us  [chip_shards(): lax.ppermute(pair, 'orient', [(d, (d + 2 * s) % devices) for d in range(d...]
    unnamed x9 -> x7, local copies, waits for them, and re-layouts: 5.68 us -> 4.92 us
  transfers between devices with their start and end apart: 23 -> 23, of which waited for: 12 -> 11; matrix products, arithmetic and copies ran while one was open for 2% -> 1% of each run, Pallas kernels for 21% -> 18%
where the time goes in v3:
time: 83.1 us; the launch traced here: 82.8 us
  starting transfers between devices  25.8 us (31%)
  waiting for transfers between devices  25.5 us (31%)
  Pallas kernels  20.2 us (24%)
  local copies, waits for them, and re-layouts  9.57 us (12%)
  other arithmetic  1.53 us (2%)
    ppermute x14, starting transfers between devices, forward(): return lax.ppermute(values, ('orient', 'cls'), pairs)  18.6 us
    pallas_call x4, Pallas kernels, score_call(): pl.pallas_call(kernel, in_specs=[pl.BlockSpec(memory_space=pltpu.SMEM)] +...  18.4 us
    ppermute x14, waiting for transfers between devices, forward(): return lax.ppermute(values, ('orient', 'cls'), pairs)  15.7 us
    unnamed x7, local copies, waits for them, and re-layouts  4.92 us
    ppermute x3, starting transfers between devices, chip_shards(): lax.ppermute(pair, 'orient', [(d, (d + 2 * s) % devices) for d in range(d...  4.52 us
    ppermute x1, waiting for transfers between devices, chip_shards(): got = lax.ppermute(given, 'orient', mate_pairs)  3.29 us
    ppermute x1, waiting for transfers between devices, chip_shards(): from_x = lax.ppermute(there_own, 'cls', x_pairs)  2.64 us
    optimization_barrier x1, local copies, waits for them, and re-layouts, chip_shards(): _, panels = lax.optimization_barrier((ahead[False], panels))  2.42 us
  transfers between devices with their start and end apart: 23, of which 11 were waited for; matrix products, arithmetic and copies ran while one was open for 1% of the time, Pallas kernels for 18%

profile of v3, /device:TPU:0, one launch (start us, length us, event | category | flops | bytes accessed | tf_op | source)
XLA Modules:
  0.0 82.8 jit_solution(13177705323628965800)
XLA Ops:
  0.0 1.1 %copy.11 = bf16[1,16,2,7296]{3,1,2,0:T(8,128)(2,1)S(1)} copy(bf16[1,16,2,7296]{3,2,1,0:T(2,128)(2,1)} %param.9) | data formatting | bytes 933888 | tf_op args[0]
  1.1 0.7 convert_bitcast_fusion
  1.8 0.7 fusion.5
  2.5 3.1 %collective-permute-start = (bf16[16,7424]{1,0:T(8,128)(2,1)S(1)}, bf16[16,7424]{1,0:T(8,128)(2,1)S(1)}, u32[]{:S(2)}, u32[]{:S(2)}) collective-permute-start(bf16[16,7424]{1,0:T(8,128)(2,1)S(1)} %get-tuple-element.82.refs_0_), channel_id=1, source_target_pairs={{0,4},{2,6},{4,8},{6,10},{8,12},{10,14},{12,13},{14,15},{13,9},{15... | collective-permute-start | bytes 712712 | tf_op jit(solution)/shard_map/ppermute | solution.py:264
  5.6 5.7 %collective-permute-done.refs_2_ = bf16[16,7424]{1,0:T(8,128)(2,1)S(1)} collective-permute-done((bf16[16,7424]{1,0:T(8,128)(2,1)S(1)}, bf16[16,7424]{1,0:T(8,128)(2,1)S(1)}, u32[]{:S(2)}, u32[]{:S(2)}) %collective-permute-start) | collective-permute-done | bytes 237600 | tf_op jit(solution)/shard_map/ppermute | solution.py:264
  11.3 2.4 %copy.10 = bf16[1,1,128,2,7296]{4,2,3,1,0:T(8,128)(2,1)S(1)} copy(bf16[1,1,128,2,7296]{4,3,2,1,0:T(2,128)(2,1)} %param.13) | data formatting | bytes 7471104 | tf_op jit(solution)/shard_map/optimization_barrier | solution.py:292
  13.7 1.4 %dynamic-slice_bitcast_fusion = bf16[128,7296]{1,0:T(8,128)(2,1)} fusion(bf16[2,128,7296]{2,1,0:T(8,128)(2,1)S(1)} %bitcast.25, s32[]{:T(128)S(6)} %select_n.44), kind=kLoop, calls=%fused_computation.1 | loop fusion | bytes 3735556 | tf_op jit(solution)/shard_map/jit(dynamic_index_in_dim)/squeeze | solution.py:295
  15.1 1.8 %copy-done = bf16[1,1,128,2,7296]{4,2,3,1,0:T(8,128)(2,1)} copy-done((bf16[1,1,128,2,7296]{4,2,3,1,0:T(8,128)(2,1)}, bf16[1,1,128,2,7296]{4,2,3,1,0:T(8,128)(2,1)S(1)}, u32[]{:S(2)}) %copy-start) | copy-done | bytes 3735576
  16.9 0.5 collective-permute-start.2
  17.4 3.3 %collective-permute-done.2.refs_1_ = bf16[16,7424]{1,0:T(8,128)(2,1)S(1)} collective-permute-done((bf16[16,7424]{1,0:T(8,128)(2,1)S(1)}, bf16[16,7424]{1,0:T(8,128)(2,1)S(1)}, u32[]{:S(2)}, u32[]{:S(2)}) %collective-permute-start.2) | collective-permute-done | bytes 237600 | tf_op jit(solution)/shard_map/ppermute | solution.py:271
  20.7 1.8 %collective-permute-start.5 = (bf16[16,7424]{1,0:T(8,128)(2,1)S(1)}, bf16[16,7424]{1,0:T(8,128)(2,1)}, u32[]{:S(2)}, u32[]{:S(2)}) collective-permute-start(bf16[16,7424]{1,0:T(8,128)(2,1)S(1)} %collective-permute-done.2.refs_1_), channel_id=1, source_target_pairs={{0,1},{2,3},{4,0},{6,2},{8,4},{10,6},{12,8},{14,10},{13,12},{15,14... | collective-permute-start | bytes 712712 | tf_op jit(solution)/shard_map/ppermute | solution.py:264
  22.5 0.3 collective-permute-start.4
  22.8 1.7 %collective-permute-start.3 = (bf16[16,7424]{1,0:T(8,128)(2,1)S(1)}, bf16[16,7424]{1,0:T(8,128)(2,1)S(1)}, u32[]{:S(2)}, u32[]{:S(2)}) collective-permute-start(bf16[16,7424]{1,0:T(8,128)(2,1)S(1)} %get-tuple-element.82.refs_0_), channel_id=1, source_target_pairs={{0,1},{2,3},{4,0},{6,2},{8,4},{10,6},{12,8},{14,10},{13,12},{15,14... | collective-permute-start | bytes 712712 | tf_op jit(solution)/shard_map/ppermute | solution.py:264
  24.5 4.9 %collective-permute-done.5.refs_5_ = bf16[16,7424]{1,0:T(8,128)(2,1)} collective-permute-done((bf16[16,7424]{1,0:T(8,128)(2,1)S(1)}, bf16[16,7424]{1,0:T(8,128)(2,1)}, u32[]{:S(2)}, u32[]{:S(2)}) %collective-permute-start.5) | collective-permute-done | bytes 237600 | tf_op jit(solution)/shard_map/ppermute | solution.py:264
  29.4 1.8 %collective-permute-start.10 = (bf16[16,7424]{1,0:T(8,128)(2,1)}, bf16[16,7424]{1,0:T(8,128)(2,1)S(1)}, u32[]{:S(2)}, u32[]{:S(2)}) collective-permute-start(bf16[16,7424]{1,0:T(8,128)(2,1)} %collective-permute-done.5.refs_5_), channel_id=1, source_target_pairs={{0,1},{2,3},{4,0},{6,2},{8,4},{10,6},{12,8},{14,10},{13,12},{15,14... | collective-permute-start | bytes 712712 | tf_op jit(solution)/shard_map/ppermute | solution.py:264
  31.2 0.3 collective-permute-start.1
  31.5 0.1 pad_add_fusion.spot
  31.6 1.8 %collective-permute-start.9 = (bf16[16,7424]{1,0:T(8,128)(2,1)S(1)}, bf16[16,7424]{1,0:T(8,128)(2,1)S(1)}, u32[]{:S(2)}, u32[]{:S(2)}) collective-permute-start(bf16[16,7424]{1,0:T(8,128)(2,1)S(1)} %collective-permute-done.4.refs_4_), channel_id=1, source_target_pairs={{0,4},{2,6},{4,8},{6,10},{8,12},{10,14},{12,13},{14,15},{13,9},{15... | collective-permute-start | bytes 712712 | tf_op jit(solution)/shard_map/ppermute | solution.py:264
  33.4 0.8 broadcast_in_dim.4.refs_6_.refs_4_.refs_2_
  34.2 0.3 collective-permute-done.3.refs_3_
  34.4 1.8 %collective-permute-start.8 = (bf16[16,7424]{1,0:T(8,128)(2,1)S(1)}, bf16[16,7424]{1,0:T(8,128)(2,1)S(1)}, u32[]{:S(2)}, u32[]{:S(2)}) collective-permute-start(bf16[16,7424]{1,0:T(8,128)(2,1)S(1)} %collective-permute-done.3.refs_3_), channel_id=1, source_target_pairs={{0,1},{2,3},{4,0},{6,2},{8,4},{10,6},{12,8},{14,10},{13,12},{15,14... | collective-permute-start | bytes 712712 | tf_op jit(solution)/shard_map/ppermute | solution.py:264
  36.2 2.1 %copy-done.1 = bf16[1,1,128,2,7296]{4,2,3,1,0:T(8,128)(2,1)S(1)} copy-done((bf16[1,1,128,2,7296]{4,2,3,1,0:T(8,128)(2,1)S(1)}, bf16[1,1,128,2,7296]{4,2,3,1,0:T(8,128)(2,1)}, u32[]{:S(2)}) %copy-start.1) | copy-done | bytes 3735576
  38.2 5.8 %shard_map.55 = (f32[96,128]{1,0:T(8,128)S(1)}, f32[96,128]{1,0:T(8,128)S(1)}, f32[96,128]{1,0:T(8,128)S(1)}) custom-call(s32[4]{0:T(128)S(1)} %pad_add_fusion.spot, bf16[16,7424]{1,0:T(8,128)(2,1)S(1)} %get-tuple-element.82.refs_0_, bf16[16,7424]{1,0:T(8,128)(2,1)S(1)} %collective-permute-done.2.refs_1_, bf16[16,7424]{1,0:T(8,128)(2,1)S(1)} %collective-permute-done.refs_2_, ...), custom_call_target="tpu_custom_call" | custom-call | flops 956301312 | bytes 5136384 | tf_op jit(solution)/shard_map/pallas_call | solution.py:168
  44.1 1.6 %collective-permute-start.12 = (bf16[16,7424]{1,0:T(8,128)(2,1)S(1)}, bf16[16,7424]{1,0:T(8,128)(2,1)S(1)}, u32[]{:S(2)}, u32[]{:S(2)}) collective-permute-start(bf16[16,7424]{1,0:T(8,128)(2,1)S(1)} %collective-permute-done.10.refs_3_), channel_id=1, source_target_pairs={{0,1},{2,3},{4,0},{6,2},{8,4},{10,6},{12,8},{14,10},{13,12},{15,14... | collective-permute-start | bytes 712712 | tf_op jit(solution)/shard_map/ppermute | solution.py:264
  45.7 0.5 collective-permute-start.7
  46.2 0.3 collective-permute-start.15
  46.4 1.8 %collective-permute-start.14 = (bf16[16,7424]{1,0:T(8,128)(2,1)S(1)}, bf16[16,7424]{1,0:T(8,128)(2,1)S(1)}, u32[]{:S(2)}, u32[]{:S(2)}) collective-permute-start(bf16[16,7424]{1,0:T(8,128)(2,1)S(1)} %collective-permute-done.8.refs_1_), channel_id=1, source_target_pairs={{0,1},{2,3},{4,0},{6,2},{8,4},{10,6},{12,8},{14,10},{13,12},{15,14... | collective-permute-start | bytes 712712 | tf_op jit(solution)/shard_map/ppermute | solution.py:264
  48.2 4.4 %shard_map.56 = (f32[64,128]{1,0:T(8,128)S(1)}, f32[64,128]{1,0:T(8,128)S(1)}, f32[64,128]{1,0:T(8,128)S(1)}) custom-call(s32[4]{0:T(128)S(1)} %pad_add_fusion.spot, bf16[16,7424]{1,0:T(8,128)(2,1)S(1)} %collective-permute-done.1.refs_0_, bf16[16,7424]{1,0:T(8,128)(2,1)S(1)} %collective-permute-done.8.refs_1_, ...), custom_call_target="tpu_custom_call" | custom-call | flops 956301312 | bytes 4669440 | tf_op jit(solution)/shard_map/pallas_call | solution.py:168
  52.6 0.2 collective-permute-done.12.refs_3_
  52.9 1.6 %collective-permute-start.13 = (bf16[16,7424]{1,0:T(8,128)(2,1)S(1)}, bf16[16,7424]{1,0:T(8,128)(2,1)S(1)}, u32[]{:S(2)}, u32[]{:S(2)}) collective-permute-start(bf16[16,7424]{1,0:T(8,128)(2,1)S(1)} %collective-permute-done.12.refs_3_), channel_id=1, source_target_pairs={{0,1},{2,3},{4,0},{6,2},{8,4},{10,6},{12,8},{14,10},{13,12},{15,14... | collective-permute-start | bytes 712712 | tf_op jit(solution)/shard_map/ppermute | solution.py:264
  54.4 0.5 collective-permute-start.11
  54.9 4.6 %collective-permute-done.15.refs_2_ = bf16[16,7424]{1,0:T(8,128)(2,1)S(1)} collective-permute-done((bf16[16,7424]{1,0:T(8,128)(2,1)S(1)}, bf16[16,7424]{1,0:T(8,128)(2,1)S(1)}, u32[]{:S(2)}, u32[]{:S(2)}) %collective-permute-start.15) | collective-permute-done | bytes 237600 | tf_op jit(solution)/shard_map/ppermute | solution.py:264
  59.5 4.4 %shard_map.57 = (f32[64,128]{1,0:T(8,128)S(1)}, f32[64,128]{1,0:T(8,128)S(1)}, f32[64,128]{1,0:T(8,128)S(1)}) custom-call(s32[4]{0:T(128)S(1)} %pad_add_fusion.spot, bf16[16,7424]{1,0:T(8,128)(2,1)S(1)} %collective-permute-done.7.refs_0_, bf16[16,7424]{1,0:T(8,128)(2,1)S(1)} %collective-permute-done.14.refs_1_, ...), custom_call_target="tpu_custom_call" | custom-call | flops 956301312 | bytes 4669440 | tf_op jit(solution)/shard_map/pallas_call | solution.py:168
  63.9 3.8 %shard_map.58 = (f32[128,128]{1,0:T(8,128)S(1)}, f32[128,128]{1,0:T(8,128)S(1)}, f32[128,128]{1,0:T(8,128)S(1)}, f32[128,128]{1,0:T(8,128)S(1)}, f32[128,128]{1,0:T(8,128)S(1)}) custom-call(s32[4]{0:T(128)S(1)} %pad_add_fusion.spot, bf16[16,7424]{1,0:T(8,128)(2,1)S(1)} %collective-permute-done.11.refs_0_, ...), custom_call_target="tpu_custom_call" | custom-call | flops 956301312 | bytes 4202496 | tf_op jit(solution)/shard_map/pallas_call | solution.py:168
  67.7 0.1 collective-permute-start.16
  67.7 1.6 %collective-permute-start.17 = (f32[128,128]{1,0:T(8,128)S(1)}, f32[128,128]{1,0:T(8,128)S(1)}, u32[]{:S(2)}, u32[]{:S(2)}) collective-permute-start(f32[128,128]{1,0:T(8,128)S(1)} %get-tuple-element.71), channel_id=1, source_target_pairs={{0,1},{1,0},{2,3},{3,2},{4,5},{5,4},{6,7},{7,6},{8,9},{9,8},{10,11... | collective-permute-start | bytes 196616 | tf_op jit(solution)/shard_map/ppermute | solution.py:310
  69.4 0.2 collective-permute-start.18
  69.6 2.6 %collective-permute-done.17.across = f32[128,128]{1,0:T(8,128)S(1)} collective-permute-done((f32[128,128]{1,0:T(8,128)S(1)}, f32[128,128]{1,0:T(8,128)S(1)}, u32[]{:S(2)}, u32[]{:S(2)}) %collective-permute-start.17) | collective-permute-done | bytes 65568 | tf_op jit(solution)/shard_map/ppermute | solution.py:310
  72.2 1.2 %collective-permute-done.18.both = f32[128,128]{1,0:T(8,128)S(1)} collective-permute-done((f32[128,128]{1,0:T(8,128)S(1)}, f32[128,128]{1,0:T(8,128)S(1)}, u32[]{:S(2)}, u32[]{:S(2)}) %collective-permute-start.18) | collective-permute-done | bytes 65568 | tf_op jit(solution)/shard_map/ppermute | solution.py:311
  73.4 1.1 %shard_map.59 = (f32[128,256]{1,0:T(8,128)S(1)}, f32[128,128]{1,0:T(8,128)S(1)}, f32[8,128]{1,0:T(8,128)S(1)}) custom-call(s32[4]{0:T(128)S(1)} %pad_add_fusion.spot, f32[128,128]{1,0:T(8,128)S(1)} %get-tuple-element.69.mine, f32[128,128]{1,0:T(8,128)S(1)} %collective-permute-done.16.mate, f32[128,128]{1,0:T(8,128)S(1)} %collective-permute-done.17.across, ...), custom_call_target="tpu_custom_call" | custom-call | tf_op jit(solution)/shard_map/pallas_call | solution.py:317
  74.5 0.2 collective-permute-start.19
  74.7 1.0 %collective-permute-done.19 = f32[8,128]{1,0:T(8,128)S(1)} collective-permute-done((f32[8,128]{1,0:T(8,128)S(1)}, f32[8,128]{1,0:T(8,128)S(1)}, u32[]{:S(2)}, u32[]{:S(2)}) %collective-permute-start.19) | collective-permute-done | bytes 4128 | tf_op jit(solution)/shard_map/ppermute | solution.py:329
  75.8 1.6 %collective-permute-start.20 = (f32[8,128]{1,0:T(8,128)S(1)}, f32[8,128]{1,0:T(8,128)S(1)}, u32[]{:S(2)}, u32[]{:S(2)}) collective-permute-start(f32[8,128]{1,0:T(8,128)S(1)} %scatter.9.refs_1_), channel_id=1, source_target_pairs={{0,4},{2,6},{4,8},{6,10},{8,12},{10,14},{12,0},{14,2},{1,5},{3,7},... | collective-permute-start | bytes 12296 | tf_op jit(solution)/shard_map/ppermute | solution.py:334
  77.4 0.4 collective-permute-start.21
  77.8 2.5 %collective-permute-start.22 = (f32[8,128]{1,0:T(8,128)S(1)}, f32[8,128]{1,0:T(8,128)S(1)}, u32[]{:S(2)}, u32[]{:S(2)}) collective-permute-start(f32[8,128]{1,0:T(8,128)S(1)} %scatter.9.refs_1_), channel_id=1, source_target_pairs={{0,12},{2,14},{4,0},{6,2},{8,4},{10,6},{12,8},{14,10},{1,13},{3,15... | collective-permute-start | bytes 12296 | tf_op jit(solution)/shard_map/ppermute | solution.py:334
  80.3 0.9 %collective-permute-done.20.refs_2_ = f32[8,128]{1,0:T(8,128)S(1)} collective-permute-done((f32[8,128]{1,0:T(8,128)S(1)}, f32[8,128]{1,0:T(8,128)S(1)}, u32[]{:S(2)}, u32[]{:S(2)}) %collective-permute-start.20) | collective-permute-done | bytes 4128 | tf_op jit(solution)/shard_map/ppermute | solution.py:334
  81.2 0.7 collective-permute-done.21.refs_3_
  82.0 0.8 shard_map.60
  (22 shorter events, 0.2 us)
Async XLA Ops:
  2.5 8.8 %collective-permute-start = (bf16[16,7424]{1,0:T(8,128)(2,1)S(1)}, bf16[16,7424]{1,0:T(8,128)(2,1)S(1)}, u32[]{:S(2)}, u32[]{:S(2)}) collective-permute-start(bf16[16,7424]{1,0:T(8,128)(2,1)S(1)} %get-tuple-element.82.refs_0_), channel_id=1, source_target_pairs={{0,4},{2,6},{4,8},{6,10},{8,12},{10,14},{12,13},{14,15},{13,9},{15... | collective-permute-start | bytes 712712 | tf_op jit(solution)/shard_map/ppermute | solution.py:264
  15.1 1.8 %copy-start = (bf16[1,1,128,2,7296]{4,2,3,1,0:T(8,128)(2,1)}, bf16[1,1,128,2,7296]{4,2,3,1,0:T(8,128)(2,1)S(1)}, u32[]{:S(2)}) copy-start(bf16[1,1,128,2,7296]{4,2,3,1,0:T(8,128)(2,1)S(1)} %copy.10) | copy-start | bytes 11206660
  16.9 19.2 %collective-permute-start.6 = (bf16[128,7296]{1,0:T(8,128)(2,1)}, bf16[128,7296]{1,0:T(8,128)(2,1)S(1)}, u32[]{:S(2)}, u32[]{:S(2)}) collective-permute-start(bf16[128,7296]{1,0:T(8,128)(2,1)} %dynamic-slice_bitcast_fusion), channel_id=1, source_target_pairs={{0,2},{2,0},{4,6},{6,4},{8,10},{10,8},{12,14},{14,12},{1,3},{3,1},... | collective-permute-start | bytes 5603336 | tf_op jit(solution)/shard_map/ppermute | solution.py:294
  16.9 3.8 %collective-permute-start.2 = (bf16[16,7424]{1,0:T(8,128)(2,1)S(1)}, bf16[16,7424]{1,0:T(8,128)(2,1)S(1)}, u32[]{:S(2)}, u32[]{:S(2)}) collective-permute-start(bf16[16,7424]{1,0:T(8,128)(2,1)S(1)} %get-tuple-element.81), channel_id=1, source_target_pairs={{0,2},{2,0},{4,6},{6,4},{8,10},{10,8},{12,14},{14,12},{1,3},{3,1},... | collective-permute-start | bytes 712712 | tf_op jit(solution)/shard_map/ppermute | solution.py:271
  20.7 8.7 %collective-permute-start.5 = (bf16[16,7424]{1,0:T(8,128)(2,1)S(1)}, bf16[16,7424]{1,0:T(8,128)(2,1)}, u32[]{:S(2)}, u32[]{:S(2)}) collective-permute-start(bf16[16,7424]{1,0:T(8,128)(2,1)S(1)} %collective-permute-done.2.refs_1_), channel_id=1, source_target_pairs={{0,1},{2,3},{4,0},{6,2},{8,4},{10,6},{12,8},{14,10},{13,12},{15,14... | collective-permute-start | bytes 712712 | tf_op jit(solution)/shard_map/ppermute | solution.py:264
  22.5 9.1 %collective-permute-start.4 = (bf16[16,7424]{1,0:T(8,128)(2,1)S(1)}, bf16[16,7424]{1,0:T(8,128)(2,1)S(1)}, u32[]{:S(2)}, u32[]{:S(2)}) collective-permute-start(bf16[16,7424]{1,0:T(8,128)(2,1)S(1)} %collective-permute-done.2.refs_1_), channel_id=1, source_target_pairs={{0,4},{2,6},{4,8},{6,10},{8,12},{10,14},{12,13},{14,15},{13,9},{15... | collective-permute-start | bytes 712712 | tf_op jit(solution)/shard_map/ppermute | solution.py:264
  22.8 11.7 %collective-permute-start.3 = (bf16[16,7424]{1,0:T(8,128)(2,1)S(1)}, bf16[16,7424]{1,0:T(8,128)(2,1)S(1)}, u32[]{:S(2)}, u32[]{:S(2)}) collective-permute-start(bf16[16,7424]{1,0:T(8,128)(2,1)S(1)} %get-tuple-element.82.refs_0_), channel_id=1, source_target_pairs={{0,1},{2,3},{4,0},{6,2},{8,4},{10,6},{12,8},{14,10},{13,12},{15,14... | collective-permute-start | bytes 712712 | tf_op jit(solution)/shard_map/ppermute | solution.py:264
  29.4 14.6 %collective-permute-start.10 = (bf16[16,7424]{1,0:T(8,128)(2,1)}, bf16[16,7424]{1,0:T(8,128)(2,1)S(1)}, u32[]{:S(2)}, u32[]{:S(2)}) collective-permute-start(bf16[16,7424]{1,0:T(8,128)(2,1)} %collective-permute-done.5.refs_5_), channel_id=1, source_target_pairs={{0,1},{2,3},{4,0},{6,2},{8,4},{10,6},{12,8},{14,10},{13,12},{15,14... | collective-permute-start | bytes 712712 | tf_op jit(solution)/shard_map/ppermute | solution.py:264
  31.2 14.5 %collective-permute-start.1 = (bf16[16,7424]{1,0:T(8,128)(2,1)S(1)}, bf16[16,7424]{1,0:T(8,128)(2,1)S(1)}, u32[]{:S(2)}, u32[]{:S(2)}) collective-permute-start(bf16[16,7424]{1,0:T(8,128)(2,1)S(1)} %collective-permute-done.refs_2_), channel_id=1, source_target_pairs={{0,4},{2,6},{4,8},{6,10},{8,12},{10,14},{12,13},{14,15},{13,9},{15... | collective-permute-start | bytes 712712 | tf_op jit(solution)/shard_map/ppermute | solution.py:264
  31.6 14.6 %collective-permute-start.9 = (bf16[16,7424]{1,0:T(8,128)(2,1)S(1)}, bf16[16,7424]{1,0:T(8,128)(2,1)S(1)}, u32[]{:S(2)}, u32[]{:S(2)}) collective-permute-start(bf16[16,7424]{1,0:T(8,128)(2,1)S(1)} %collective-permute-done.4.refs_4_), channel_id=1, source_target_pairs={{0,4},{2,6},{4,8},{6,10},{8,12},{10,14},{12,13},{14,15},{13,9},{15... | collective-permute-start | bytes 712712 | tf_op jit(solution)/shard_map/ppermute | solution.py:264
  34.4 12.0 %collective-permute-start.8 = (bf16[16,7424]{1,0:T(8,128)(2,1)S(1)}, bf16[16,7424]{1,0:T(8,128)(2,1)S(1)}, u32[]{:S(2)}, u32[]{:S(2)}) collective-permute-start(bf16[16,7424]{1,0:T(8,128)(2,1)S(1)} %collective-permute-done.3.refs_3_), channel_id=1, source_target_pairs={{0,1},{2,3},{4,0},{6,2},{8,4},{10,6},{12,8},{14,10},{13,12},{15,14... | collective-permute-start | bytes 712712 | tf_op jit(solution)/shard_map/ppermute | solution.py:264
  36.2 2.1 %copy-start.1 = (bf16[1,1,128,2,7296]{4,2,3,1,0:T(8,128)(2,1)S(1)}, bf16[1,1,128,2,7296]{4,2,3,1,0:T(8,128)(2,1)}, u32[]{:S(2)}) copy-start(bf16[1,1,128,2,7296]{4,2,3,1,0:T(8,128)(2,1)} %copy-done) | copy-start | bytes 11206660
  38.2 10.0 %copy-start.2 = (bf16[1,1,128,2,7296]{4,2,3,1,0:T(8,128)(2,1)S(1)}, bf16[1,1,128,2,7296]{4,2,3,1,0:T(8,128)(2,1)}, u32[]{:S(2)}) copy-start(bf16[1,1,128,2,7296]{4,2,3,1,0:T(8,128)(2,1)} %copy-done) | copy-start | bytes 11206660
  44.1 8.8 %collective-permute-start.12 = (bf16[16,7424]{1,0:T(8,128)(2,1)S(1)}, bf16[16,7424]{1,0:T(8,128)(2,1)S(1)}, u32[]{:S(2)}, u32[]{:S(2)}) collective-permute-start(bf16[16,7424]{1,0:T(8,128)(2,1)S(1)} %collective-permute-done.10.refs_3_), channel_id=1, source_target_pairs={{0,1},{2,3},{4,0},{6,2},{8,4},{10,6},{12,8},{14,10},{13,12},{15,14... | collective-permute-start | bytes 712712 | tf_op jit(solution)/shard_map/ppermute | solution.py:264
  45.7 8.7 %collective-permute-start.7 = (bf16[16,7424]{1,0:T(8,128)(2,1)S(1)}, bf16[16,7424]{1,0:T(8,128)(2,1)S(1)}, u32[]{:S(2)}, u32[]{:S(2)}) collective-permute-start(bf16[16,7424]{1,0:T(8,128)(2,1)S(1)} %collective-permute-done.1.refs_0_), channel_id=1, source_target_pairs={{0,4},{2,6},{4,8},{6,10},{8,12},{10,14},{12,13},{14,15},{13,9},{15... | collective-permute-start | bytes 712712 | tf_op jit(solution)/shard_map/ppermute | solution.py:264
  46.2 13.3 %collective-permute-start.15 = (bf16[16,7424]{1,0:T(8,128)(2,1)S(1)}, bf16[16,7424]{1,0:T(8,128)(2,1)S(1)}, u32[]{:S(2)}, u32[]{:S(2)}) collective-permute-start(bf16[16,7424]{1,0:T(8,128)(2,1)S(1)} %collective-permute-done.9.refs_2_), channel_id=1, source_target_pairs={{0,4},{2,6},{4,8},{6,10},{8,12},{10,14},{12,13},{14,15},{13,9},{15... | collective-permute-start | bytes 712712 | tf_op jit(solution)/shard_map/ppermute | solution.py:264
  46.4 13.0 %collective-permute-start.14 = (bf16[16,7424]{1,0:T(8,128)(2,1)S(1)}, bf16[16,7424]{1,0:T(8,128)(2,1)S(1)}, u32[]{:S(2)}, u32[]{:S(2)}) collective-permute-start(bf16[16,7424]{1,0:T(8,128)(2,1)S(1)} %collective-permute-done.8.refs_1_), channel_id=1, source_target_pairs={{0,1},{2,3},{4,0},{6,2},{8,4},{10,6},{12,8},{14,10},{13,12},{15,14... | collective-permute-start | bytes 712712 | tf_op jit(solution)/shard_map/ppermute | solution.py:264
  52.9 11.0 %collective-permute-start.13 = (bf16[16,7424]{1,0:T(8,128)(2,1)S(1)}, bf16[16,7424]{1,0:T(8,128)(2,1)S(1)}, u32[]{:S(2)}, u32[]{:S(2)}) collective-permute-start(bf16[16,7424]{1,0:T(8,128)(2,1)S(1)} %collective-permute-done.12.refs_3_), channel_id=1, source_target_pairs={{0,1},{2,3},{4,0},{6,2},{8,4},{10,6},{12,8},{14,10},{13,12},{15,14... | collective-permute-start | bytes 712712 | tf_op jit(solution)/shard_map/ppermute | solution.py:264
  54.4 9.4 %collective-permute-start.11 = (bf16[16,7424]{1,0:T(8,128)(2,1)S(1)}, bf16[16,7424]{1,0:T(8,128)(2,1)S(1)}, u32[]{:S(2)}, u32[]{:S(2)}) collective-permute-start(bf16[16,7424]{1,0:T(8,128)(2,1)S(1)} %collective-permute-done.7.refs_0_), channel_id=1, source_target_pairs={{0,4},{2,6},{4,8},{6,10},{8,12},{10,14},{12,13},{14,15},{13,9},{15... | collective-permute-start | bytes 712712 | tf_op jit(solution)/shard_map/ppermute | solution.py:264
  67.7 1.9 %collective-permute-start.16 = (f32[128,128]{1,0:T(8,128)S(1)}, f32[128,128]{1,0:T(8,128)S(1)}, u32[]{:S(2)}, u32[]{:S(2)}) collective-permute-start(f32[128,128]{1,0:T(8,128)S(1)} %get-tuple-element.70), channel_id=1, source_target_pairs={{0,2},{2,0},{4,6},{6,4},{8,10},{10,8},{12,14},{14,12},{1,3},{3,1},... | collective-permute-start | bytes 196616 | tf_op jit(solution)/shard_map/ppermute | solution.py:309
  67.7 4.5 %collective-permute-start.17 = (f32[128,128]{1,0:T(8,128)S(1)}, f32[128,128]{1,0:T(8,128)S(1)}, u32[]{:S(2)}, u32[]{:S(2)}) collective-permute-start(f32[128,128]{1,0:T(8,128)S(1)} %get-tuple-element.71), channel_id=1, source_target_pairs={{0,1},{1,0},{2,3},{3,2},{4,5},{5,4},{6,7},{7,6},{8,9},{9,8},{10,11... | collective-permute-start | bytes 196616 | tf_op jit(solution)/shard_map/ppermute | solution.py:310
  69.4 4.0 %collective-permute-start.18 = (f32[128,128]{1,0:T(8,128)S(1)}, f32[128,128]{1,0:T(8,128)S(1)}, u32[]{:S(2)}, u32[]{:S(2)}) collective-permute-start(f32[128,128]{1,0:T(8,128)S(1)} %get-tuple-element.72), channel_id=1, source_target_pairs={{0,3},{1,2},{2,1},{3,0},{4,7},{5,6},{6,5},{7,4},{8,11},{9,10},{10,... | collective-permute-start | bytes 196616 | tf_op jit(solution)/shard_map/ppermute | solution.py:311
  74.5 1.2 %collective-permute-start.19 = (f32[8,128]{1,0:T(8,128)S(1)}, f32[8,128]{1,0:T(8,128)S(1)}, u32[]{:S(2)}, u32[]{:S(2)}) collective-permute-start(f32[8,128]{1,0:T(8,128)S(1)} %get-tuple-element.74.refs_0_), channel_id=1, source_target_pairs={{0,2},{2,0},{4,6},{6,4},{8,10},{10,8},{12,14},{14,12},{1,3},{3,1},... | collective-permute-start | bytes 12296 | tf_op jit(solution)/shard_map/ppermute | solution.py:329
  75.8 5.5 %collective-permute-start.20 = (f32[8,128]{1,0:T(8,128)S(1)}, f32[8,128]{1,0:T(8,128)S(1)}, u32[]{:S(2)}, u32[]{:S(2)}) collective-permute-start(f32[8,128]{1,0:T(8,128)S(1)} %scatter.9.refs_1_), channel_id=1, source_target_pairs={{0,4},{2,6},{4,8},{6,10},{8,12},{10,14},{12,0},{14,2},{1,5},{3,7},... | collective-permute-start | bytes 12296 | tf_op jit(solution)/shard_map/ppermute | solution.py:334
  77.4 4.6 %collective-permute-start.21 = (f32[8,128]{1,0:T(8,128)S(1)}, f32[8,128]{1,0:T(8,128)S(1)}, u32[]{:S(2)}, u32[]{:S(2)}) collective-permute-start(f32[8,128]{1,0:T(8,128)S(1)} %scatter.9.refs_1_), channel_id=1, source_target_pairs={{0,8},{2,10},{4,12},{6,14},{8,0},{10,2},{12,4},{14,6},{1,9},{3,11}... | collective-permute-start | bytes 12296 | tf_op jit(solution)/shard_map/ppermute | solution.py:334
  77.8 4.1 %collective-permute-start.22 = (f32[8,128]{1,0:T(8,128)S(1)}, f32[8,128]{1,0:T(8,128)S(1)}, u32[]{:S(2)}, u32[]{:S(2)}) collective-permute-start(f32[8,128]{1,0:T(8,128)S(1)} %scatter.9.refs_1_), channel_id=1, source_target_pairs={{0,12},{2,14},{4,0},{6,2},{8,4},{10,6},{12,8},{14,10},{1,13},{3,15... | collective-permute-start | bytes 12296 | tf_op jit(solution)/shard_map/ppermute | solution.py:334

commit v4 on v3

--- a/solution.py
+++ b/solution.py
@@ -43,40 +43,34 @@
     return jnp.concatenate([m[...].astype(jnp.float32).T[: m.shape[0]] for m in meta], axis=0)
 
 
-def add_scores(rows, spot, noise, sides, mate_panel, tables, sums, segments):
+def add_scores(rows, spot, noise, sides, mate_panel, turn_sin, turn_cos, sums, segments):
     columns = noise.shape[1]
     width = columns // segments
     tiles = width // LANES
-    sin_a, cos_a, sin_b, cos_b = tables
-    count = sin_a.shape[0]
+    count = turn_sin.shape[0]
     facts = particle_facts([r.at[:, pl.ds(columns, LANES)] for r in rows])
-    rate = CTF_PHASE * facts[:, 0:1]
+    rate = jnp.broadcast_to(CTF_PHASE * facts[:, 0:1], (count, LANES))
     lane = lax.broadcasted_iota(jnp.int32, (count, LANES), 1).astype(jnp.float32)
-    coarse_sin, coarse_cos = sin_cos(rate * (lane * (LANES / columns)) + 0.1)
-    sin_a[...] = -coarse_sin
-    cos_a[...] = -coarse_cos
-    fine_sin, fine_cos = sin_cos(rate * ((lane + 0.5) / columns))
-    sin_b[...] = fine_sin
-    cos_b[...] = fine_cos
+    first_sin, first_cos = sin_cos(rate * ((lane + 0.5) / columns) + 0.1)
+    step_sin, step_cos = sin_cos(rate * (LANES / columns))
+    turn_sin[...] = step_sin
+    turn_cos[...] = step_cos
     for total in sums:
         total[...] = jnp.zeros_like(total)
     core = spot[2]
 
     def segment(index, carry):
+        sine, cosine = carry
         start = pl.multiple_of(index * width, LANES)
-        shift = lax.rem(LANES - index * tiles, LANES)
-        sa = pltpu.roll(sin_a[...], shift, 1)
-        ca = pltpu.roll(cos_a[...], shift, 1)
-        sb = sin_b[...]
-        cb = cos_b[...]
         scaled_parts, energy_parts = [], []
         for t in range(tiles):
             window = pl.ds(start + t * LANES, LANES)
-            contrast = sa[:, t : t + 1] * cb + ca[:, t : t + 1] * sb
-            weighted = contrast * noise[:, window]
+            weighted = sine * noise[:, window]
             image = jnp.concatenate([r[:, window] for r in rows], axis=0).astype(jnp.float32)
             scaled_parts.append((weighted * image).astype(jnp.bfloat16))
-            energy_parts.append((contrast * weighted).astype(jnp.bfloat16))
+            energy_parts.append((sine * weighted).astype(jnp.bfloat16))
+            ds, dc = turn_sin[...], turn_cos[...]
+            sine, cosine = sine * dc + cosine * ds, cosine * dc - sine * ds
         scaled = jnp.concatenate(scaled_parts, axis=1)
         energy = jnp.concatenate(energy_parts, axis=1)
         contract = (((1,), (1,)), ((), ()))
@@ -88,34 +82,34 @@
             )
             power = lax.dot_general(squared, energy, contract, preferred_element_type=jnp.float32)
             total[...] += correlate - 0.5 * power
-        return carry
-
-    lax.fori_loop(0, segments, segment, 0)
-    return facts
+        return sine, cosine
+
+    lax.fori_loop(0, segments, segment, (-first_sin, -first_cos))
+    return jnp.pad(facts, ((0, 0), (0, LANES - facts.shape[1])))
 
 
 def batch_kernel(n, segments, spot, *refs):
     rows = refs[:n]
     noise, sides, mate_panel, own_out, mate_out, fact_out = refs[n : n + 6]
-    tables, sums = refs[n + 6 : n + 10], refs[n + 10 :]
-    facts = add_scores(rows, spot, noise, sides, mate_panel, tables, sums, segments)
+    turn_sin, turn_cos, *sums = refs[n + 6 :]
+    fact_out[...] = add_scores(
+        rows, spot, noise, sides, mate_panel, turn_sin, turn_cos, sums, segments
+    )
     own_out[...] = sums[0][...].T
     mate_out[...] = sums[1][...].T
-    fact_out[...] = jnp.pad(facts, ((0, 0), (0, LANES - facts.shape[1])))
 
 
 def last_kernel(n, segments, orders, spot, *refs):
     rows = refs[:n]
     noise, sides, mate_panel = refs[n : n + 3]
     earlier = refs[n + 3 : n + 3 + 3 * (len(orders) - 1)]
-    outs = refs[n + 3 + len(earlier) :]
-    here_own, here_mate, there_own, there_mate, facts = outs[:5]
-    tables, sums, (own_all, mate_all, fact_all) = outs[5:9], outs[9:11], outs[11:]
-    last_facts = add_scores(rows, spot, noise, sides, mate_panel, tables, sums, segments)
-    last_facts = jnp.pad(last_facts, ((0, 0), (0, LANES - last_facts.shape[1])))
-    group, position, core = spot[0], spot[1], spot[2]
+    partial, facts, turn_sin, turn_cos, *sums = refs[n + 3 + len(earlier) :]
+    last_facts = add_scores(
+        rows, spot, noise, sides, mate_panel, turn_sin, turn_cos, sums, segments
+    )
+    position, core = spot[1], spot[2]
     each = rows[0].shape[0]
-    ring = own_all.shape[0] // (2 * each)
+    ring = facts.shape[0] // (2 * each)
     half = ring // 2
     for index, order in enumerate(orders):
         if index < len(orders) - 1:
@@ -127,19 +121,11 @@
             far = place >= half
             level = jnp.where(far, ring - 1 - place, place)
             device = 2 * level + (1 - core if crossed else core)
-            side = jnp.where(far, 1, 0)
-            other = jnp.where(side == group, 0, 1)
-            start = pl.multiple_of((other * ring + device) * each, each)
+            start = pl.multiple_of((jnp.where(far, ring, 0) + device) * each, each)
             piece = slice(k * each, (k + 1) * each)
-            own_all[pl.ds(start, each), :] = own[piece]
-            mate_all[pl.ds(start, each), :] = mate[piece]
-            fact_all[pl.ds(start, each), :] = fact[piece]
-    everyone = ring * each
-    here_own[...] = own_all[:everyone]
-    here_mate[...] = mate_all[:everyone]
-    there_own[...] = own_all[everyone:]
-    there_mate[...] = mate_all[everyone:]
-    facts[...] = fact_all[:everyone]
+            partial[core, pl.ds(start, each), :] = own[piece]
+            partial[1 - core, pl.ds(start, each), :] = mate[piece]
+            facts[pl.ds(start, each), :] = fact[piece]
 
 
 def score_call(chunks, orders, earlier, spot, noise, sides, mate_panel):
@@ -149,7 +135,7 @@
     segments = next(s for s in (3, 2, 4, 5, 6, 7, 1) if whole % s == 0)
     n = len(chunks)
     count = each * n
-    scratch = [pltpu.VMEM((count, LANES), jnp.float32)] * 4
+    scratch = [pltpu.VMEM((count, LANES), jnp.float32)] * 2
     scratch += [pltpu.VMEM((orientations, count), jnp.float32)] * 2
     single = jax.ShapeDtypeStruct((count, orientations), jnp.float32)
     if orders is None:
@@ -157,12 +143,12 @@
         out_shape = [single, single, jax.ShapeDtypeStruct((count, LANES), jnp.float32)]
         extra = []
     else:
-        everyone = each * sum(len(o) for o in orders) // 2
+        everyone = each * sum(len(o) for o in orders)
         kernel = functools.partial(last_kernel, n, segments, orders)
-        block = jax.ShapeDtypeStruct((everyone, orientations), jnp.float32)
-        out_shape = [block] * 4 + [jax.ShapeDtypeStruct((everyone, LANES), jnp.float32)]
-        whole_sums = pltpu.VMEM((2 * everyone, orientations), jnp.float32)
-        scratch += [whole_sums, whole_sums, pltpu.VMEM((2 * everyone, LANES), jnp.float32)]
+        out_shape = [
+            jax.ShapeDtypeStruct((2, everyone, orientations), jnp.float32),
+            jax.ShapeDtypeStruct((everyone, LANES), jnp.float32),
+        ]
         extra = [e for triple in earlier for e in triple]
     vmem = pl.BlockSpec(memory_space=pltpu.VMEM)
     return pl.pallas_call(
@@ -180,20 +166,53 @@
     )(spot, *chunks, noise, sides, mate_panel, *extra)
 
 
-def stats_kernel(search, slots_each, each, spot, mine, mate, across, both, facts, slots, chosen, stats):
-    group, block = spot[0], spot[3]
+def names_block(facts, search, block):
+    lane = lax.broadcasted_iota(jnp.int32, facts.shape, 1)
+    match = (lane >= 1) & (lane <= search) & (facts == block.astype(jnp.float32))
+    return jnp.max(jnp.where(match, 1.0, 0.0), axis=1, keepdims=True) > 0.0
+
+
+def chip_kernel(search, spot, partial, mate, facts, mine, own_stats, across):
+    group, core, place = spot[0], spot[2], spot[3]
     count = mine.shape[0]
-    same = mine[...] + mate[...]
-    other = across[...] + both[...]
+    lane = lax.broadcasted_iota(jnp.int32, (count, LANES), 1)
+    for relative in range(2):
+        side = group if relative == 0 else 1 - group
+        window = pl.ds(pl.multiple_of(side * count, count), count)
+        listed = facts[window, :]
+        masked = []
+        for crossed in range(2):
+            block = core if crossed == 0 else 1 - core
+            scores = partial[block, window, :] + mate[block, window, :]
+            if crossed == 0:
+                if relative == 0:
+                    mine[...] = scores
+                else:
+                    across[:count] = scores
+            named = names_block(listed, search, place - core + block)
+            masked.append(jnp.where(named, scores, FLOOR))
+        top = jnp.max(jnp.maximum(*masked), axis=1, keepdims=True)
+        terms = [jnp.where(m > FLOOR, jnp.exp(m - top), 0.0) for m in masked]
+        total = jnp.sum(terms[0] + terms[1], axis=1, keepdims=True)
+        pair = jnp.where(lane == 0, top, jnp.where(lane == 1, total, 0.0)).T
+        if relative == 0:
+            own_stats[...] = pair[: own_stats.shape[0]]
+        else:
+            across[count:] = pair[: across.shape[0] - count]
+
+
+def slot_kernel(search, slots_each, each, spot, mine, across, pair, facts, slots, chosen):
+    group, place = spot[0], spot[3]
+    count = mine.shape[0]
+    same, other = mine[...], across[:count]
     first = group == 0
     scores = jnp.concatenate(
         [jnp.where(first, same, other), jnp.where(first, other, same)], axis=1
     )
-    lane = lax.broadcasted_iota(jnp.int32, (count, LANES), 1)
+    listed = facts[pl.ds(pl.multiple_of(group * count, count), count), :]
+    named = names_block(listed, search, place)
+    hit = jnp.where(named, 1.0, 0.0)
     row = lax.broadcasted_iota(jnp.int32, (count, LANES), 0)
-    match = (lane >= 1) & (lane <= search) & (facts[...] == block.astype(jnp.float32))
-    hit = jnp.max(jnp.where(match, 1.0, 0.0), axis=1, keepdims=True)
-    named = hit > 0.0
     line = lax.broadcasted_iota(jnp.int32, (count, count), 0)
     column = lax.broadcasted_iota(jnp.int32, (count, count), 1)
     before = (column < line) & (column // each == line // each)
@@ -208,9 +227,8 @@
         slot = jnp.broadcast_to(slot[:, :1], (count, capacity))
     target = lax.broadcasted_iota(jnp.int32, (count, capacity), 1)
     taken = jnp.where((slot == target) & named, 1.0, 0.0)
-    top = jnp.where(named, jnp.max(scores, axis=1, keepdims=True), FLOOR)
+    top = jnp.broadcast_to(pair[0:1, :], (count, count)).T[:, 0:1]
     terms = jnp.where(named, jnp.exp(scores - top), 0.0)
-    total = jnp.sum(terms, axis=1, keepdims=True)
     slots[...] = lax.dot_general(
         taken,
         terms,
@@ -219,16 +237,14 @@
         preferred_element_type=jnp.float32,
     )
     chosen[...] = taken.T
-    pair = jnp.where(lane == 0, top, jnp.where(lane == 1, total, 0.0))
-    stats[...] = pair.T[: stats.shape[0]]
 
 
 def final_kernel(n, *refs):
-    own, parts, slots, chosen, out = refs[0], refs[1 : 1 + n], refs[1 + n], refs[2 + n], refs[3 + n]
-    tops = [p[0:1, :] for p in parts]
-    peak = functools.reduce(jnp.maximum, tops)
-    total = functools.reduce(jnp.add, [p[1:2, :] * jnp.exp(p[0:1, :] - peak) for p in parts])
-    factor = jnp.exp(own[0:1, :] - peak) / total
+    parts, slots, chosen, out = refs[:n], refs[n], refs[n + 1], refs[n + 2]
+    peak = functools.reduce(jnp.maximum, [p[0:1, :] for p in parts])
+    shares = [p[1:2, :] * jnp.exp(p[0:1, :] - peak) for p in parts]
+    total = functools.reduce(jnp.add, shares)
+    factor = jnp.exp(parts[0][0:1, :] - peak) / total
     scale = jnp.sum(chosen[...] * factor, axis=1, keepdims=True)
     out[...] = slots[...] * scale
 
@@ -270,14 +286,19 @@
     given = jnp.concatenate([jnp.where(first, planes[1], planes[0]), facts], axis=1)
     got = lax.ppermute(given, "orient", mate_pairs)
 
+    _, panels = lax.optimization_barrier((got, panels))
+    sides = lax.optimization_barrier(jnp.transpose(panels[0, 0], (1, 0, 2)))
+    given_panel = lax.dynamic_index_in_dim(sides, 1 - core, 0, keepdims=False)
+    mate_panel = lax.ppermute(given_panel, "orient", mate_pairs)
+
     noise = noise_weight[None, :]
     waiting = [((0, False), kept), ((0, True), got)]
     ahead = {False: kept, True: got}
     behind = {False: kept, True: got}
     orders, earlier = [], []
     for step in range(1, chips + 1):
-        if earlier:
-            tie = earlier[-1][2]
+        if step > 1:
+            tie = earlier[-1][2] if earlier else given_panel
             ahead = {c: lax.optimization_barrier((v, tie))[0] for c, v in ahead.items()}
             behind = {c: lax.optimization_barrier((v, tie))[0] for c, v in behind.items()}
         arrived = []
@@ -288,12 +309,6 @@
             if step < chips or crossed:
                 behind[crossed] = forward(behind[crossed], -1)
                 arrived.append(((step, crossed), behind[crossed]))
-        if step == 1:
-            _, panels = lax.optimization_barrier((ahead[False], panels))
-            sides = lax.optimization_barrier(jnp.transpose(panels[0, 0], (1, 0, 2)))
-            mate_panel = lax.ppermute(
-                lax.dynamic_index_in_dim(sides, 1 - core, 0, keepdims=False), "orient", mate_pairs
-            )
         if step > 1:
             orders.append([key for key, _ in waiting])
             earlier.append(
@@ -302,45 +317,52 @@
             waiting = []
         waiting = waiting + arrived
     orders.append([key for key, _ in waiting])
-    here_own, here_mate, there_own, there_mate, own_facts = score_call(
+    partial, all_facts = score_call(
         [c for _, c in waiting], orders, earlier, spot, noise, sides, mate_panel
     )
 
-    from_mate = lax.ppermute(here_mate, "orient", mate_pairs)
-    from_x = lax.ppermute(there_own, "cls", x_pairs)
-    from_both = lax.ppermute(
-        there_mate,
-        ("orient", "cls"),
-        [(d * 2 + g, (d ^ 1) * 2 + 1 - g) for d in range(devices) for g in range(2)],
-    )
+    mate_partial = lax.ppermute(partial, "orient", mate_pairs)
     vmem = pl.BlockSpec(memory_space=pltpu.VMEM)
-    slots, chosen, stats = pl.pallas_call(
-        functools.partial(stats_kernel, local_search, slots_each, per_device),
-        in_specs=[pl.BlockSpec(memory_space=pltpu.SMEM)] + [vmem] * 5,
+    smem = pl.BlockSpec(memory_space=pltpu.SMEM)
+    params = pltpu.CompilerParams(vmem_limit_bytes=VMEM_LIMIT)
+    mine, own_stats, across = pl.pallas_call(
+        functools.partial(chip_kernel, local_search),
+        in_specs=[smem] + [vmem] * 3,
         out_specs=[vmem] * 3,
         out_shape=[
-            jax.ShapeDtypeStruct((capacity, 2 * orientations), jnp.float32),
-            jax.ShapeDtypeStruct((capacity, everyone), jnp.float32),
+            jax.ShapeDtypeStruct((everyone, orientations), jnp.float32),
             jax.ShapeDtypeStruct((8, everyone), jnp.float32),
+            jax.ShapeDtypeStruct((everyone + 8, orientations), jnp.float32),
         ],
-        compiler_params=pltpu.CompilerParams(vmem_limit_bytes=VMEM_LIMIT),
-    )(spot, here_own, from_mate, from_x, from_both, own_facts)
-
-    mate_stats = lax.ppermute(stats, "orient", mate_pairs)
-    peak = jnp.maximum(stats[0], mate_stats[0])
-    total = stats[1] * jnp.exp(stats[0] - peak) + mate_stats[1] * jnp.exp(mate_stats[0] - peak)
-    pair = jnp.zeros_like(stats).at[0].set(peak).at[1].set(total)
+        compiler_params=params,
+    )(spot, partial, mate_partial, all_facts)
+    from_x = lax.ppermute(across, "cls", x_pairs)
+
+    tops = own_stats[0], from_x[everyone]
+    peak = jnp.maximum(*tops)
+    total = own_stats[1] * jnp.exp(tops[0] - peak) + from_x[everyone + 1] * jnp.exp(tops[1] - peak)
+    pair = jnp.pad(jnp.stack([peak, total]), ((0, 6), (0, 0)))
     pairs = [pair] + [
         lax.ppermute(pair, "orient", [(d, (d + 2 * s) % devices) for d in range(devices)])
         for s in range(1, chips)
     ]
+    slots, chosen = pl.pallas_call(
+        functools.partial(slot_kernel, local_search, slots_each, per_device),
+        in_specs=[smem] + [vmem] * 4,
+        out_specs=[vmem] * 2,
+        out_shape=[
+            jax.ShapeDtypeStruct((capacity, 2 * orientations), jnp.float32),
+            jax.ShapeDtypeStruct((capacity, everyone), jnp.float32),
+        ],
+        compiler_params=params,
+    )(spot, mine, from_x, pair, all_facts)
     posterior = pl.pallas_call(
         functools.partial(final_kernel, chips),
-        in_specs=[vmem] * (chips + 3),
+        in_specs=[vmem] * (chips + 2),
         out_specs=vmem,
         out_shape=jax.ShapeDtypeStruct((capacity, 2 * orientations), jnp.float32),
-        compiler_params=pltpu.CompilerParams(vmem_limit_bytes=VMEM_LIMIT),
-    )(stats, *pairs, slots, chosen)
+        compiler_params=params,
+    )(*pairs, slots, chosen)
     return posterior.reshape(1, 1, capacity, -1)
 
 

time: 83.1 us -> 72 us (0.87)
  waiting for transfers between devices: 25.5 us -> 20.8 us
  starting transfers between devices: 25.8 us -> 21.9 us
  Pallas kernels: 20.2 us -> 18.6 us
    ppermute x14, starting transfers between devices: 18.6 us -> 15 us  [forward(): return lax.ppermute(values, ('orient', 'cls'), pairs)]
    pallas_call x4, Pallas kernels: 18.4 us -> 15.8 us  [score_call(): pl.pallas_call(kernel, in_specs=[pl.BlockSpec(memory_space=pltpu.SMEM)] +...]
    ppermute x1, waiting for transfers between devices: 3.29 us -> 1.13 us  [chip_shards(): got = lax.ppermute(given, 'orient', mate_pairs)]
    ppermute x14, waiting for transfers between devices: 15.7 us -> 14.1 us  [forward(): return lax.ppermute(values, ('orient', 'cls'), pairs)]
    ppermute x3, waiting for transfers between devices: 1.66 us -> 0.21 us  [chip_shards(): lax.ppermute(pair, 'orient', [(d, (d + 2 * s) % devices) for d in range(d...]
    ppermute x5 -> x3, starting transfers between devices: 2.17 us -> 0.93 us  [the longest x1 0.49 us: chip_shards(): from_x = lax.ppermute(across, 'cls', x_pairs)]
    ppermute x3, starting transfers between devices: 4.52 us -> 5.48 us  [chip_shards(): lax.ppermute(pair, 'orient', [(d, (d + 2 * s) % devices) for d in range(d...]
    pallas_call x1 -> x2, Pallas kernels: 1.07 us -> 2.02 us  [the longest x1 1.1 us: chip_shards(): pl.pallas_call(functools.partial(slot_kernel, local_search, slots_each, p...]
  transfers between devices with their start and end apart: 23 -> 21, of which waited for: 11 -> 8; matrix products, arithmetic and copies ran while one was open for 1% -> 0% of each run, Pallas kernels for 18% -> 19%
where the time goes in v4:
time: 72 us; the launch traced here: 71.8 us
  starting transfers between devices  21.9 us (30%)
  waiting for transfers between devices  20.8 us (29%)
  Pallas kernels  18.6 us (26%)
  local copies, waits for them, and re-layouts  8.78 us (12%)
  other arithmetic  1.55 us (2%)
    pallas_call x4, Pallas kernels, score_call(): pl.pallas_call(kernel, in_specs=[pl.BlockSpec(memory_space=pltpu.SMEM)] +...  15.8 us
    ppermute x14, starting transfers between devices, forward(): return lax.ppermute(values, ('orient', 'cls'), pairs)  15 us
    ppermute x14, waiting for transfers between devices, forward(): return lax.ppermute(values, ('orient', 'cls'), pairs)  14.1 us
    ppermute x3, starting transfers between devices, chip_shards(): lax.ppermute(pair, 'orient', [(d, (d + 2 * s) % devices) for d in range(d...  5.48 us
    unnamed x9, local copies, waits for them, and re-layouts  4.93 us
    ppermute x1, waiting for transfers between devices, chip_shards(): from_x = lax.ppermute(across, 'cls', x_pairs)  3.86 us
    optimization_barrier x1, local copies, waits for them, and re-layouts, chip_shards(): _, panels = lax.optimization_barrier((got, panels))  2.42 us
    ppermute x1, waiting for transfers between devices, chip_shards(): mate_partial = lax.ppermute(partial, 'orient', mate_pairs)  1.52 us
  transfers between devices with their start and end apart: 21, of which 8 were waited for; matrix products, arithmetic and copies ran while one was open for 0% of the time, Pallas kernels for 19%

profile of v4, /device:TPU:0, one launch (start us, length us, event | category | flops | bytes accessed | tf_op | source)
XLA Modules:
  0.0 71.8 jit_solution(4250477391700147724)
XLA Ops:
  0.0 0.7 convert_bitcast_fusion
  0.7 1.1 %copy.11 = bf16[1,16,2,7296]{3,1,2,0:T(8,128)(2,1)S(1)} copy(bf16[1,16,2,7296]{3,2,1,0:T(2,128)(2,1)} %param.5) | data formatting | bytes 933888 | tf_op args[0]
  1.8 0.7 fusion.5
  2.5 0.5 collective-permute-start.1
  3.0 1.1 %collective-permute-done.1.refs_1_ = bf16[16,7424]{1,0:T(8,128)(2,1)S(1)} collective-permute-done((bf16[16,7424]{1,0:T(8,128)(2,1)S(1)}, bf16[16,7424]{1,0:T(8,128)(2,1)S(1)}, u32[]{:S(2)}, u32[]{:S(2)}) %collective-permute-start.1) | collective-permute-done | bytes 237600 | tf_op jit(solution)/shard_map/ppermute | solution.py:287
  4.2 2.4 %copy.10 = bf16[1,1,128,2,7296]{4,2,3,1,0:T(8,128)(2,1)S(1)} copy(bf16[1,1,128,2,7296]{4,3,2,1,0:T(2,128)(2,1)} %param.9) | data formatting | bytes 7471104 | tf_op jit(solution)/shard_map/optimization_barrier | solution.py:289
  6.6 0.0 copy-start.3
  6.6 1.4 %dynamic-slice_bitcast_fusion = bf16[128,7296]{1,0:T(8,128)(2,1)} fusion(bf16[2,128,7296]{2,1,0:T(8,128)(2,1)S(1)} %bitcast.25, s32[]{:T(128)S(6)} %select_n.44), kind=kLoop, calls=%fused_computation.1 | loop fusion | bytes 3735556 | tf_op jit(solution)/shard_map/jit(dynamic_index_in_dim)/squeeze | solution.py:291
  8.0 1.8 %copy-done = bf16[1,1,128,2,7296]{4,2,3,1,0:T(8,128)(2,1)} copy-done((bf16[1,1,128,2,7296]{4,2,3,1,0:T(8,128)(2,1)}, bf16[1,1,128,2,7296]{4,2,3,1,0:T(8,128)(2,1)S(1)}, u32[]{:S(2)}) %copy-start) | copy-done | bytes 3735576
  9.8 0.4 collective-permute-start.6
  10.2 2.7 %collective-permute-start = (bf16[16,7424]{1,0:T(8,128)(2,1)S(1)}, bf16[16,7424]{1,0:T(8,128)(2,1)}, u32[]{:S(2)}, u32[]{:S(2)}) collective-permute-start(bf16[16,7424]{1,0:T(8,128)(2,1)S(1)} %get-tuple-element.64.refs_0_), channel_id=1, source_target_pairs={{0,4},{2,6},{4,8},{6,10},{8,12},{10,14},{12,13},{14,15},{13,9},{15... | collective-permute-start | bytes 712712 | tf_op jit(solution)/shard_map/ppermute | solution.py:280
  12.9 0.0 collective-permute-start.5
  12.9 1.9 %collective-permute-start.3 = (bf16[16,7424]{1,0:T(8,128)(2,1)S(1)}, bf16[16,7424]{1,0:T(8,128)(2,1)S(1)}, u32[]{:S(2)}, u32[]{:S(2)}) collective-permute-start(bf16[16,7424]{1,0:T(8,128)(2,1)S(1)} %get-tuple-element.64.refs_0_), channel_id=1, source_target_pairs={{0,1},{2,3},{4,0},{6,2},{8,4},{10,6},{12,8},{14,10},{13,12},{15,14... | collective-permute-start | bytes 712712 | tf_op jit(solution)/shard_map/ppermute | solution.py:280
  14.8 0.1 collective-permute-start.4
  15.0 4.6 %collective-permute-done.refs_2_ = bf16[16,7424]{1,0:T(8,128)(2,1)} collective-permute-done((bf16[16,7424]{1,0:T(8,128)(2,1)S(1)}, bf16[16,7424]{1,0:T(8,128)(2,1)}, u32[]{:S(2)}, u32[]{:S(2)}) %collective-permute-start) | collective-permute-done | bytes 237600 | tf_op jit(solution)/shard_map/ppermute | solution.py:280
  19.5 2.1 %collective-permute-start.2 = (bf16[16,7424]{1,0:T(8,128)(2,1)}, bf16[16,7424]{1,0:T(8,128)(2,1)S(1)}, u32[]{:S(2)}, u32[]{:S(2)}) collective-permute-start(bf16[16,7424]{1,0:T(8,128)(2,1)} %collective-permute-done.refs_2_), channel_id=1, source_target_pairs={{0,4},{2,6},{4,8},{6,10},{8,12},{10,14},{12,13},{14,15},{13,9},{15... | collective-permute-start | bytes 712712 | tf_op jit(solution)/shard_map/ppermute | solution.py:280
  21.6 0.0 collective-permute-done.5.refs_5_
  21.6 0.0 collective-permute-start.10
  21.7 0.1 pad_add_fusion.spot
  21.8 4.9 %collective-permute-done.3.refs_3_ = bf16[16,7424]{1,0:T(8,128)(2,1)S(1)} collective-permute-done((bf16[16,7424]{1,0:T(8,128)(2,1)S(1)}, bf16[16,7424]{1,0:T(8,128)(2,1)S(1)}, u32[]{:S(2)}, u32[]{:S(2)}) %collective-permute-start.3) | collective-permute-done | bytes 237600 | tf_op jit(solution)/shard_map/ppermute | solution.py:280
  26.6 2.0 %collective-permute-start.9 = (bf16[16,7424]{1,0:T(8,128)(2,1)S(1)}, bf16[16,7424]{1,0:T(8,128)(2,1)S(1)}, u32[]{:S(2)}, u32[]{:S(2)}) collective-permute-start(bf16[16,7424]{1,0:T(8,128)(2,1)S(1)} %collective-permute-done.4.refs_4_), channel_id=1, source_target_pairs={{0,4},{2,6},{4,8},{6,10},{8,12},{10,14},{12,13},{14,15},{13,9},{15... | collective-permute-start | bytes 712712 | tf_op jit(solution)/shard_map/ppermute | solution.py:280
  28.7 0.0 collective-permute-done.6.refs_8_.refs_6_.refs_4_
  28.7 2.1 %copy-done.1 = bf16[1,1,128,2,7296]{4,2,3,1,0:T(8,128)(2,1)S(1)} copy-done((bf16[1,1,128,2,7296]{4,2,3,1,0:T(8,128)(2,1)S(1)}, bf16[1,1,128,2,7296]{4,2,3,1,0:T(8,128)(2,1)}, u32[]{:S(2)}) %copy-start.1) | copy-done | bytes 3735576
  30.7 4.9 %shard_map.55 = (f32[96,128]{1,0:T(8,128)S(1)}, f32[96,128]{1,0:T(8,128)S(1)}, f32[96,128]{1,0:T(8,128)S(1)}) custom-call(s32[4]{0:T(128)S(1)} %pad_add_fusion.spot, bf16[16,7424]{1,0:T(8,128)(2,1)S(1)} %get-tuple-element.64.refs_0_, bf16[16,7424]{1,0:T(8,128)(2,1)S(1)} %collective-permute-done.1.refs_1_, bf16[16,7424]{1,0:T(8,128)(2,1)} %collective-permute-done.refs_2_, ...), custom_call_target="tpu_custom_call" | custom-call | flops 956301312 | bytes 5136384 | tf_op jit(solution)/shard_map/pallas_call | solution.py:154
  35.6 0.0 collective-permute-done.2.refs_0_
  35.6 1.6 %collective-permute-start.7 = (bf16[16,7424]{1,0:T(8,128)(2,1)S(1)}, bf16[16,7424]{1,0:T(8,128)(2,1)S(1)}, u32[]{:S(2)}, u32[]{:S(2)}) collective-permute-start(bf16[16,7424]{1,0:T(8,128)(2,1)S(1)} %collective-permute-done.2.refs_0_), channel_id=1, source_target_pairs={{0,4},{2,6},{4,8},{6,10},{8,12},{10,14},{12,13},{14,15},{13,9},{15... | collective-permute-start | bytes 712712 | tf_op jit(solution)/shard_map/ppermute | solution.py:280
  37.3 0.4 collective-permute-start.12
  37.7 0.0 collective-permute-done.8.refs_1_
  37.7 0.1 collective-permute-start.14
  37.8 2.0 %collective-permute-start.15 = (bf16[16,7424]{1,0:T(8,128)(2,1)S(1)}, bf16[16,7424]{1,0:T(8,128)(2,1)S(1)}, u32[]{:S(2)}, u32[]{:S(2)}) collective-permute-start(bf16[16,7424]{1,0:T(8,128)(2,1)S(1)} %collective-permute-done.9.refs_2_), channel_id=1, source_target_pairs={{0,4},{2,6},{4,8},{6,10},{8,12},{10,14},{12,13},{14,15},{13,9},{15... | collective-permute-start | bytes 712712 | tf_op jit(solution)/shard_map/ppermute | solution.py:280
  39.7 3.8 %shard_map.56 = (f32[64,128]{1,0:T(8,128)S(1)}, f32[64,128]{1,0:T(8,128)S(1)}, f32[64,128]{1,0:T(8,128)S(1)}) custom-call(s32[4]{0:T(128)S(1)} %pad_add_fusion.spot, bf16[16,7424]{1,0:T(8,128)(2,1)S(1)} %collective-permute-done.2.refs_0_, bf16[16,7424]{1,0:T(8,128)(2,1)S(1)} %collective-permute-done.8.refs_1_, ...), custom_call_target="tpu_custom_call" | custom-call | flops 956301312 | bytes 4669440 | tf_op jit(solution)/shard_map/pallas_call | solution.py:154
  43.5 0.8 %collective-permute-done.7.refs_0_ = bf16[16,7424]{1,0:T(8,128)(2,1)S(1)} collective-permute-done((bf16[16,7424]{1,0:T(8,128)(2,1)S(1)}, bf16[16,7424]{1,0:T(8,128)(2,1)S(1)}, u32[]{:S(2)}, u32[]{:S(2)}) %collective-permute-start.7) | collective-permute-done | bytes 237600 | tf_op jit(solution)/shard_map/ppermute | solution.py:280
  44.3 1.6 %collective-permute-start.11 = (bf16[16,7424]{1,0:T(8,128)(2,1)S(1)}, bf16[16,7424]{1,0:T(8,128)(2,1)S(1)}, u32[]{:S(2)}, u32[]{:S(2)}) collective-permute-start(bf16[16,7424]{1,0:T(8,128)(2,1)S(1)} %collective-permute-done.7.refs_0_), channel_id=1, source_target_pairs={{0,4},{2,6},{4,8},{6,10},{8,12},{10,14},{12,13},{14,15},{13,9},{15... | collective-permute-start | bytes 712712 | tf_op jit(solution)/shard_map/ppermute | solution.py:280
  45.9 0.5 collective-permute-start.13
  46.3 3.8 %collective-permute-done.14.refs_1_ = bf16[16,7424]{1,0:T(8,128)(2,1)S(1)} collective-permute-done((bf16[16,7424]{1,0:T(8,128)(2,1)S(1)}, bf16[16,7424]{1,0:T(8,128)(2,1)S(1)}, u32[]{:S(2)}, u32[]{:S(2)}) %collective-permute-start.14) | collective-permute-done | bytes 237600 | tf_op jit(solution)/shard_map/ppermute | solution.py:280
  50.1 3.7 %shard_map.57 = (f32[64,128]{1,0:T(8,128)S(1)}, f32[64,128]{1,0:T(8,128)S(1)}, f32[64,128]{1,0:T(8,128)S(1)}) custom-call(s32[4]{0:T(128)S(1)} %pad_add_fusion.spot, bf16[16,7424]{1,0:T(8,128)(2,1)S(1)} %collective-permute-done.7.refs_0_, bf16[16,7424]{1,0:T(8,128)(2,1)S(1)} %collective-permute-done.14.refs_1_, ...), custom_call_target="tpu_custom_call" | custom-call | flops 956301312 | bytes 4669440 | tf_op jit(solution)/shard_map/pallas_call | solution.py:154
  53.9 3.4 %shard_map.58 = (f32[2,256,128]{2,1,0:T(8,128)S(1)}, f32[256,128]{1,0:T(8,128)S(1)}) custom-call(s32[4]{0:T(128)S(1)} %pad_add_fusion.spot, bf16[16,7424]{1,0:T(8,128)(2,1)S(1)} %collective-permute-done.11.refs_0_, bf16[16,7424]{1,0:T(8,128)(2,1)S(1)} %collective-permute-done.13.refs_1_, f32[1,7296]{1,0:T(1,128)S(1)} %broadcast_in_dim.3.refs_6_.refs_4_.refs_2_, ...), custom_call_target="tpu_custom_call" | custom-call | flops 956301312 | bytes 4202496 | tf_op jit(solution)/shard_map/pallas_call | solution.py:154
  57.3 0.1 collective-permute-start.16
  57.4 1.5 %collective-permute-done.16.mate = f32[2,256,128]{2,1,0:T(8,128)S(1)} collective-permute-done((f32[2,256,128]{2,1,0:T(8,128)S(1)}, f32[2,256,128]{2,1,0:T(8,128)S(1)}, u32[]{:S(2)}, u32[]{:S(2)}) %collective-permute-start.16) | collective-permute-done | bytes 262176 | tf_op jit(solution)/shard_map/ppermute | solution.py:324
  58.9 0.9 %shard_map.59 = (f32[128,128]{1,0:T(8,128)S(1)}, f32[8,128]{1,0:T(8,128)S(1)}, f32[136,128]{1,0:T(8,128)S(1)}) custom-call(s32[4]{0:T(128)S(1)} %pad_add_fusion.spot, f32[2,256,128]{2,1,0:T(8,128)S(1)} %get-tuple-element.52.partial, f32[2,256,128]{2,1,0:T(8,128)S(1)} %collective-permute-done.16.mate, f32[256,128]{1,0:T(8,128)S(1)} %get-tuple-element.53.facts), custom_call_target="tpu_custom_call" | custom-call | tf_op jit(solution)/shard_map/pallas_call | solution.py:328
  59.8 0.5 collective-permute-start.17
  60.3 3.9 %collective-permute-done.17.across = f32[136,128]{1,0:T(8,128)S(1)} collective-permute-done((f32[136,128]{1,0:T(8,128)S(1)}, f32[136,128]{1,0:T(8,128)S(1)}, u32[]{:S(2)}, u32[]{:S(2)}) %collective-permute-start.17) | collective-permute-done | bytes 69664 | tf_op jit(solution)/shard_map/ppermute | solution.py:339
  64.2 1.6 %collective-permute-start.18 = (f32[8,128]{1,0:T(8,128)S(1)}, f32[8,128]{1,0:T(8,128)S(1)}, u32[]{:S(2)}, u32[]{:S(2)}) collective-permute-start(f32[8,128]{1,0:T(8,128)S(1)} %select_maximum_fusion.pair.refs_0_), channel_id=1, source_target_pairs={{0,4},{2,6},{4,8},{6,10},{8,12},{10,14},{12,0},{14,2},{1,5},{3,7},... | collective-permute-start | bytes 12296 | tf_op jit(solution)/shard_map/ppermute | solution.py:346
  65.8 1.4 %collective-permute-start.19 = (f32[8,128]{1,0:T(8,128)S(1)}, f32[8,128]{1,0:T(8,128)S(1)}, u32[]{:S(2)}, u32[]{:S(2)}) collective-permute-start(f32[8,128]{1,0:T(8,128)S(1)} %select_maximum_fusion.pair.refs_0_), channel_id=1, source_target_pairs={{0,8},{2,10},{4,12},{6,14},{8,0},{10,2},{12,4},{14,6},{1,9},{3,11}... | collective-permute-start | bytes 12296 | tf_op jit(solution)/shard_map/ppermute | solution.py:346
  67.2 2.5 %collective-permute-start.20 = (f32[8,128]{1,0:T(8,128)S(1)}, f32[8,128]{1,0:T(8,128)S(1)}, u32[]{:S(2)}, u32[]{:S(2)}) collective-permute-start(f32[8,128]{1,0:T(8,128)S(1)} %select_maximum_fusion.pair.refs_0_), channel_id=1, source_target_pairs={{0,12},{2,14},{4,0},{6,2},{8,4},{10,6},{12,8},{14,10},{1,13},{3,15... | collective-permute-start | bytes 12296 | tf_op jit(solution)/shard_map/ppermute | solution.py:346
  69.7 1.1 %shard_map.60 = (f32[128,256]{1,0:T(8,128)S(1)}, f32[128,128]{1,0:T(8,128)S(1)}) custom-call(s32[4]{0:T(128)S(1)} %pad_add_fusion.spot, f32[128,128]{1,0:T(8,128)S(1)} %get-tuple-element.56.mine, f32[136,128]{1,0:T(8,128)S(1)} %collective-permute-done.17.across, f32[8,128]{1,0:T(8,128)S(1)} %select_maximum_fusion.pair.refs_0_, ...), custom_call_target="tpu_custom_call" | custom-call | tf_op jit(solution)/shard_map/pallas_call | solution.py:349
  70.8 0.2 collective-permute-done.20.refs_3_
  71.0 0.8 %shard_map.61 = f32[128,256]{1,0:T(8,128)} custom-call(f32[8,128]{1,0:T(8,128)S(1)} %select_maximum_fusion.pair.refs_0_, f32[8,128]{1,0:T(8,128)S(1)} %collective-permute-done.18.refs_1_, f32[8,128]{1,0:T(8,128)S(1)} %collective-permute-done.19.refs_2_, f32[8,128]{1,0:T(8,128)S(1)} %collective-permute-done.20.refs_3_, ...), custom_call_target="tpu_custom_call" | custom-call | tf_op jit(solution)/shard_map/pallas_call | solution.py:359
  (20 shorter events, 0.2 us)
Async XLA Ops:
  2.5 1.6 %collective-permute-start.1 = (bf16[16,7424]{1,0:T(8,128)(2,1)S(1)}, bf16[16,7424]{1,0:T(8,128)(2,1)S(1)}, u32[]{:S(2)}, u32[]{:S(2)}) collective-permute-start(bf16[16,7424]{1,0:T(8,128)(2,1)S(1)} %get-tuple-element.63), channel_id=1, source_target_pairs={{0,2},{2,0},{4,6},{6,4},{8,10},{10,8},{12,14},{14,12},{1,3},{3,1},... | collective-permute-start | bytes 712712 | tf_op jit(solution)/shard_map/ppermute | solution.py:287
  6.6 15.1 %copy-start.3 = (f32[7296]{0:T(1024)S(1)}, f32[7296]{0:T(1024)}, u32[]{:S(2)}) copy-start(f32[7296]{0:T(1024)} %param.8) | copy-start | bytes 87556
  8.0 1.8 %copy-start = (bf16[1,1,128,2,7296]{4,2,3,1,0:T(8,128)(2,1)}, bf16[1,1,128,2,7296]{4,2,3,1,0:T(8,128)(2,1)S(1)}, u32[]{:S(2)}) copy-start(bf16[1,1,128,2,7296]{4,2,3,1,0:T(8,128)(2,1)S(1)} %copy.10) | copy-start | bytes 11206660
  9.8 18.9 %collective-permute-start.6 = (bf16[128,7296]{1,0:T(8,128)(2,1)}, bf16[128,7296]{1,0:T(8,128)(2,1)S(1)}, u32[]{:S(2)}, u32[]{:S(2)}) collective-permute-start(bf16[128,7296]{1,0:T(8,128)(2,1)} %dynamic-slice_bitcast_fusion), channel_id=1, source_target_pairs={{0,2},{2,0},{4,6},{6,4},{8,10},{10,8},{12,14},{14,12},{1,3},{3,1},... | collective-permute-start | bytes 5603336 | tf_op jit(solution)/shard_map/ppermute | solution.py:292
  10.2 9.4 %collective-permute-start = (bf16[16,7424]{1,0:T(8,128)(2,1)S(1)}, bf16[16,7424]{1,0:T(8,128)(2,1)}, u32[]{:S(2)}, u32[]{:S(2)}) collective-permute-start(bf16[16,7424]{1,0:T(8,128)(2,1)S(1)} %get-tuple-element.64.refs_0_), channel_id=1, source_target_pairs={{0,4},{2,6},{4,8},{6,10},{8,12},{10,14},{12,13},{14,15},{13,9},{15... | collective-permute-start | bytes 712712 | tf_op jit(solution)/shard_map/ppermute | solution.py:280
  12.9 8.7 %collective-permute-start.5 = (bf16[16,7424]{1,0:T(8,128)(2,1)S(1)}, bf16[16,7424]{1,0:T(8,128)(2,1)}, u32[]{:S(2)}, u32[]{:S(2)}) collective-permute-start(bf16[16,7424]{1,0:T(8,128)(2,1)S(1)} %collective-permute-done.1.refs_1_), channel_id=1, source_target_pairs={{0,1},{2,3},{4,0},{6,2},{8,4},{10,6},{12,8},{14,10},{13,12},{15,14... | collective-permute-start | bytes 712712 | tf_op jit(solution)/shard_map/ppermute | solution.py:280
  12.9 13.7 %collective-permute-start.3 = (bf16[16,7424]{1,0:T(8,128)(2,1)S(1)}, bf16[16,7424]{1,0:T(8,128)(2,1)S(1)}, u32[]{:S(2)}, u32[]{:S(2)}) collective-permute-start(bf16[16,7424]{1,0:T(8,128)(2,1)S(1)} %get-tuple-element.64.refs_0_), channel_id=1, source_target_pairs={{0,1},{2,3},{4,0},{6,2},{8,4},{10,6},{12,8},{14,10},{13,12},{15,14... | collective-permute-start | bytes 712712 | tf_op jit(solution)/shard_map/ppermute | solution.py:280
  14.8 11.8 %collective-permute-start.4 = (bf16[16,7424]{1,0:T(8,128)(2,1)S(1)}, bf16[16,7424]{1,0:T(8,128)(2,1)S(1)}, u32[]{:S(2)}, u32[]{:S(2)}) collective-permute-start(bf16[16,7424]{1,0:T(8,128)(2,1)S(1)} %collective-permute-done.1.refs_1_), channel_id=1, source_target_pairs={{0,4},{2,6},{4,8},{6,10},{8,12},{10,14},{12,13},{14,15},{13,9},{15... | collective-permute-start | bytes 712712 | tf_op jit(solution)/shard_map/ppermute | solution.py:280
  19.5 16.1 %collective-permute-start.2 = (bf16[16,7424]{1,0:T(8,128)(2,1)}, bf16[16,7424]{1,0:T(8,128)(2,1)S(1)}, u32[]{:S(2)}, u32[]{:S(2)}) collective-permute-start(bf16[16,7424]{1,0:T(8,128)(2,1)} %collective-permute-done.refs_2_), channel_id=1, source_target_pairs={{0,4},{2,6},{4,8},{6,10},{8,12},{10,14},{12,13},{14,15},{13,9},{15... | collective-permute-start | bytes 712712 | tf_op jit(solution)/shard_map/ppermute | solution.py:280
  21.6 15.6 %collective-permute-start.10 = (bf16[16,7424]{1,0:T(8,128)(2,1)}, bf16[16,7424]{1,0:T(8,128)(2,1)S(1)}, u32[]{:S(2)}, u32[]{:S(2)}) collective-permute-start(bf16[16,7424]{1,0:T(8,128)(2,1)} %collective-permute-done.5.refs_5_), channel_id=1, source_target_pairs={{0,1},{2,3},{4,0},{6,2},{8,4},{10,6},{12,8},{14,10},{13,12},{15,14... | collective-permute-start | bytes 712712 | tf_op jit(solution)/shard_map/ppermute | solution.py:280
  26.6 11.1 %collective-permute-start.8 = (bf16[16,7424]{1,0:T(8,128)(2,1)S(1)}, bf16[16,7424]{1,0:T(8,128)(2,1)S(1)}, u32[]{:S(2)}, u32[]{:S(2)}) collective-permute-start(bf16[16,7424]{1,0:T(8,128)(2,1)S(1)} %collective-permute-done.3.refs_3_), channel_id=1, source_target_pairs={{0,1},{2,3},{4,0},{6,2},{8,4},{10,6},{12,8},{14,10},{13,12},{15,14... | collective-permute-start | bytes 712712 | tf_op jit(solution)/shard_map/ppermute | solution.py:280
  26.6 11.1 %collective-permute-start.9 = (bf16[16,7424]{1,0:T(8,128)(2,1)S(1)}, bf16[16,7424]{1,0:T(8,128)(2,1)S(1)}, u32[]{:S(2)}, u32[]{:S(2)}) collective-permute-start(bf16[16,7424]{1,0:T(8,128)(2,1)S(1)} %collective-permute-done.4.refs_4_), channel_id=1, source_target_pairs={{0,4},{2,6},{4,8},{6,10},{8,12},{10,14},{12,13},{14,15},{13,9},{15... | collective-permute-start | bytes 712712 | tf_op jit(solution)/shard_map/ppermute | solution.py:280
  28.7 2.1 %copy-start.1 = (bf16[1,1,128,2,7296]{4,2,3,1,0:T(8,128)(2,1)S(1)}, bf16[1,1,128,2,7296]{4,2,3,1,0:T(8,128)(2,1)}, u32[]{:S(2)}) copy-start(bf16[1,1,128,2,7296]{4,2,3,1,0:T(8,128)(2,1)} %copy-done) | copy-start | bytes 11206660
  30.7 9.0 %copy-start.2 = (bf16[1,1,128,2,7296]{4,2,3,1,0:T(8,128)(2,1)S(1)}, bf16[1,1,128,2,7296]{4,2,3,1,0:T(8,128)(2,1)}, u32[]{:S(2)}) copy-start(bf16[1,1,128,2,7296]{4,2,3,1,0:T(8,128)(2,1)} %copy-done) | copy-start | bytes 11206660
  35.6 8.7 %collective-permute-start.7 = (bf16[16,7424]{1,0:T(8,128)(2,1)S(1)}, bf16[16,7424]{1,0:T(8,128)(2,1)S(1)}, u32[]{:S(2)}, u32[]{:S(2)}) collective-permute-start(bf16[16,7424]{1,0:T(8,128)(2,1)S(1)} %collective-permute-done.2.refs_0_), channel_id=1, source_target_pairs={{0,4},{2,6},{4,8},{6,10},{8,12},{10,14},{12,13},{14,15},{13,9},{15... | collective-permute-start | bytes 712712 | tf_op jit(solution)/shard_map/ppermute | solution.py:280
  37.3 8.6 %collective-permute-start.12 = (bf16[16,7424]{1,0:T(8,128)(2,1)S(1)}, bf16[16,7424]{1,0:T(8,128)(2,1)S(1)}, u32[]{:S(2)}, u32[]{:S(2)}) collective-permute-start(bf16[16,7424]{1,0:T(8,128)(2,1)S(1)} %collective-permute-done.10.refs_3_), channel_id=1, source_target_pairs={{0,1},{2,3},{4,0},{6,2},{8,4},{10,6},{12,8},{14,10},{13,12},{15,14... | collective-permute-start | bytes 712712 | tf_op jit(solution)/shard_map/ppermute | solution.py:280
  37.7 12.4 %collective-permute-start.14 = (bf16[16,7424]{1,0:T(8,128)(2,1)S(1)}, bf16[16,7424]{1,0:T(8,128)(2,1)S(1)}, u32[]{:S(2)}, u32[]{:S(2)}) collective-permute-start(bf16[16,7424]{1,0:T(8,128)(2,1)S(1)} %collective-permute-done.8.refs_1_), channel_id=1, source_target_pairs={{0,1},{2,3},{4,0},{6,2},{8,4},{10,6},{12,8},{14,10},{13,12},{15,14... | collective-permute-start | bytes 712712 | tf_op jit(solution)/shard_map/ppermute | solution.py:280
  37.8 12.3 %collective-permute-start.15 = (bf16[16,7424]{1,0:T(8,128)(2,1)S(1)}, bf16[16,7424]{1,0:T(8,128)(2,1)S(1)}, u32[]{:S(2)}, u32[]{:S(2)}) collective-permute-start(bf16[16,7424]{1,0:T(8,128)(2,1)S(1)} %collective-permute-done.9.refs_2_), channel_id=1, source_target_pairs={{0,4},{2,6},{4,8},{6,10},{8,12},{10,14},{12,13},{14,15},{13,9},{15... | collective-permute-start | bytes 712712 | tf_op jit(solution)/shard_map/ppermute | solution.py:280
  44.3 9.6 %collective-permute-start.11 = (bf16[16,7424]{1,0:T(8,128)(2,1)S(1)}, bf16[16,7424]{1,0:T(8,128)(2,1)S(1)}, u32[]{:S(2)}, u32[]{:S(2)}) collective-permute-start(bf16[16,7424]{1,0:T(8,128)(2,1)S(1)} %collective-permute-done.7.refs_0_), channel_id=1, source_target_pairs={{0,4},{2,6},{4,8},{6,10},{8,12},{10,14},{12,13},{14,15},{13,9},{15... | collective-permute-start | bytes 712712 | tf_op jit(solution)/shard_map/ppermute | solution.py:280
  45.9 8.0 %collective-permute-start.13 = (bf16[16,7424]{1,0:T(8,128)(2,1)S(1)}, bf16[16,7424]{1,0:T(8,128)(2,1)S(1)}, u32[]{:S(2)}, u32[]{:S(2)}) collective-permute-start(bf16[16,7424]{1,0:T(8,128)(2,1)S(1)} %collective-permute-done.12.refs_3_), channel_id=1, source_target_pairs={{0,1},{2,3},{4,0},{6,2},{8,4},{10,6},{12,8},{14,10},{13,12},{15,14... | collective-permute-start | bytes 712712 | tf_op jit(solution)/shard_map/ppermute | solution.py:280
  57.3 1.6 %collective-permute-start.16 = (f32[2,256,128]{2,1,0:T(8,128)S(1)}, f32[2,256,128]{2,1,0:T(8,128)S(1)}, u32[]{:S(2)}, u32[]{:S(2)}) collective-permute-start(f32[2,256,128]{2,1,0:T(8,128)S(1)} %get-tuple-element.52.partial), channel_id=1, source_target_pairs={{0,2},{2,0},{4,6},{6,4},{8,10},{10,8},{12,14},{14,12},{1,3},{3,1},... | collective-permute-start | bytes 786440 | tf_op jit(solution)/shard_map/ppermute | solution.py:324
  59.8 4.3 %collective-permute-start.17 = (f32[136,128]{1,0:T(8,128)S(1)}, f32[136,128]{1,0:T(8,128)S(1)}, u32[]{:S(2)}, u32[]{:S(2)}) collective-permute-start(f32[136,128]{1,0:T(8,128)S(1)} %get-tuple-element.55), channel_id=1, source_target_pairs={{0,1},{1,0},{2,3},{3,2},{4,5},{5,4},{6,7},{7,6},{8,9},{9,8},{10,11... | collective-permute-start | bytes 208904 | tf_op jit(solution)/shard_map/ppermute | solution.py:339
  64.2 6.6 %collective-permute-start.18 = (f32[8,128]{1,0:T(8,128)S(1)}, f32[8,128]{1,0:T(8,128)S(1)}, u32[]{:S(2)}, u32[]{:S(2)}) collective-permute-start(f32[8,128]{1,0:T(8,128)S(1)} %select_maximum_fusion.pair.refs_0_), channel_id=1, source_target_pairs={{0,4},{2,6},{4,8},{6,10},{8,12},{10,14},{12,0},{14,2},{1,5},{3,7},... | collective-permute-start | bytes 12296 | tf_op jit(solution)/shard_map/ppermute | solution.py:346
  65.8 5.0 %collective-permute-start.19 = (f32[8,128]{1,0:T(8,128)S(1)}, f32[8,128]{1,0:T(8,128)S(1)}, u32[]{:S(2)}, u32[]{:S(2)}) collective-permute-start(f32[8,128]{1,0:T(8,128)S(1)} %select_maximum_fusion.pair.refs_0_), channel_id=1, source_target_pairs={{0,8},{2,10},{4,12},{6,14},{8,0},{10,2},{12,4},{14,6},{1,9},{3,11}... | collective-permute-start | bytes 12296 | tf_op jit(solution)/shard_map/ppermute | solution.py:346
  67.2 3.8 %collective-permute-start.20 = (f32[8,128]{1,0:T(8,128)S(1)}, f32[8,128]{1,0:T(8,128)S(1)}, u32[]{:S(2)}, u32[]{:S(2)}) collective-permute-start(f32[8,128]{1,0:T(8,128)S(1)} %select_maximum_fusion.pair.refs_0_), channel_id=1, source_target_pairs={{0,12},{2,14},{4,0},{6,2},{8,4},{10,6},{12,8},{14,10},{1,13},{3,15... | collective-permute-start | bytes 12296 | tf_op jit(solution)/shard_map/ppermute | solution.py:346

commit v5 on v4

--- a/solution.py
+++ b/solution.py
@@ -10,7 +10,7 @@
 CTF_PHASE = 40.0
 FLOOR = -1e30
 LANES = 128
-VMEM_LIMIT = 32 * 1024 * 1024
+VMEM_LIMIT = 8 * 1024 * 1024
 
 
 def sin_cos(angle):
@@ -37,6 +37,18 @@
         jnp.where((quarter & 2) == 2, -low, low),
         jnp.where(((quarter + 1) & 2) == 2, -high, high),
     )
+
+
+def row_kernel(spot, planes, defocus, lists, kept, given, facts):
+    core = spot[2]
+    columns = planes.shape[2]
+    count = defocus.shape[1]
+    facts[...] = jnp.zeros_like(facts)
+    facts[0:1, :count] = defocus[...].astype(jnp.float32)
+    facts[1 : 1 + lists.shape[0], :count] = lists[...].astype(jnp.float32)
+    for half, out in ((core, kept), (1 - core, given)):
+        out[:, :columns] = planes[half]
+        out[:, columns:] = facts[...].astype(out.dtype)
 
 
 def particle_facts(meta):
@@ -279,17 +291,24 @@
         pairs = [(joint(p, c), joint(p + step, c)) for p in range(ring) for c in range(2)]
         return lax.ppermute(values, ("orient", "cls"), pairs)
 
-    facts = jnp.concatenate([defocus, block_ids[0].T.astype(jnp.bfloat16)], axis=0)
-    facts = jnp.pad(facts, ((0, per_device - facts.shape[0]), (0, LANES - per_device)))
+    vmem = pl.BlockSpec(memory_space=pltpu.VMEM)
+    smem = pl.BlockSpec(memory_space=pltpu.SMEM)
+    params = pltpu.CompilerParams(vmem_limit_bytes=VMEM_LIMIT)
     planes = lax.optimization_barrier(jnp.transpose(images[0], (1, 0, 2)))
-    kept = jnp.concatenate([jnp.where(first, planes[0], planes[1]), facts], axis=1)
-    given = jnp.concatenate([jnp.where(first, planes[1], planes[0]), facts], axis=1)
+    row_shape = jax.ShapeDtypeStruct((per_device, columns + LANES), jnp.bfloat16)
+    kept, given = pl.pallas_call(
+        row_kernel,
+        in_specs=[smem] + [vmem] * 3,
+        out_specs=[vmem] * 2,
+        out_shape=[row_shape] * 2,
+        scratch_shapes=[pltpu.VMEM((per_device, LANES), jnp.float32)],
+        compiler_params=params,
+    )(spot, planes, defocus, jnp.transpose(block_ids[0]))
     got = lax.ppermute(given, "orient", mate_pairs)
 
     _, panels = lax.optimization_barrier((got, panels))
     sides = lax.optimization_barrier(jnp.transpose(panels[0, 0], (1, 0, 2)))
     given_panel = lax.dynamic_index_in_dim(sides, 1 - core, 0, keepdims=False)
-    mate_panel = lax.ppermute(given_panel, "orient", mate_pairs)
 
     noise = noise_weight[None, :]
     waiting = [((0, False), kept), ((0, True), got)]
@@ -297,7 +316,7 @@
     behind = {False: kept, True: got}
     orders, earlier = [], []
     for step in range(1, chips + 1):
-        if step > 1:
+        if step == 2 or (earlier and step == chips):
             tie = earlier[-1][2] if earlier else given_panel
             ahead = {c: lax.optimization_barrier((v, tie))[0] for c, v in ahead.items()}
             behind = {c: lax.optimization_barrier((v, tie))[0] for c, v in behind.items()}
@@ -309,7 +328,10 @@
             if step < chips or crossed:
                 behind[crossed] = forward(behind[crossed], -1)
                 arrived.append(((step, crossed), behind[crossed]))
-        if step > 1:
+        if step == 1:
+            given_panel = lax.optimization_barrier((given_panel, *[v for _, v in arrived]))[0]
+            mate_panel = lax.ppermute(given_panel, "orient", mate_pairs)
+        if step in (2, chips):
             orders.append([key for key, _ in waiting])
             earlier.append(
                 score_call([c for _, c in waiting], None, None, spot, noise, sides, mate_panel)
@@ -322,9 +344,6 @@
     )
 
     mate_partial = lax.ppermute(partial, "orient", mate_pairs)
-    vmem = pl.BlockSpec(memory_space=pltpu.VMEM)
-    smem = pl.BlockSpec(memory_space=pltpu.SMEM)
-    params = pltpu.CompilerParams(vmem_limit_bytes=VMEM_LIMIT)
     mine, own_stats, across = pl.pallas_call(
         functools.partial(chip_kernel, local_search),
         in_specs=[smem] + [vmem] * 3,

time: 72 us -> 67.5 us (0.938)
  waiting for transfers between devices: 20.8 us -> 24.9 us
  local copies, waits for them, and re-layouts: 8.78 us -> 4.98 us
  Pallas kernels: 18.6 us -> 15.7 us
  other arithmetic: 1.55 us -> 0.1 us
    ppermute x14, waiting for transfers between devices: 14.1 us -> 19.3 us  [forward(): return lax.ppermute(values, ('orient', 'cls'), pairs)]
    pallas_call x4 -> x3, Pallas kernels: 15.8 us -> 12.3 us  [score_call(): pl.pallas_call(kernel, in_specs=[pl.BlockSpec(memory_space=pltpu.SMEM)] +...]
    unnamed x9 -> x7, local copies, waits for them, and re-layouts: 4.93 us -> 2.41 us
    squeeze x1, local copies, waits for them, and re-layouts: 1.4 us -> 0.12 us  [chip_shards(): given_panel = lax.dynamic_index_in_dim(sides, 1 - core, 0, keepdims=False)]
    ppermute x1, waiting for transfers between devices: 1.13 us -> 0.01 us  [chip_shards(): got = lax.ppermute(given, 'orient', mate_pairs)]
  transfers between devices with their start and end apart: 21 -> 21, of which waited for: 8 -> 10; matrix products, arithmetic and copies ran while one was open for 0% -> 4% of each run, Pallas kernels for 19% -> 15%
where the time goes in v5:
time: 67.5 us; the launch traced here: 67.3 us
  waiting for transfers between devices  24.9 us (37%)
  starting transfers between devices  21.5 us (32%)
  Pallas kernels  15.7 us (23%)
  local copies, waits for them, and re-layouts  4.98 us (7%)
    ppermute x14, waiting for transfers between devices, forward(): return lax.ppermute(values, ('orient', 'cls'), pairs)  19.3 us
    ppermute x14, starting transfers between devices, forward(): return lax.ppermute(values, ('orient', 'cls'), pairs)  14.9 us
    pallas_call x3, Pallas kernels, score_call(): pl.pallas_call(kernel, in_specs=[pl.BlockSpec(memory_space=pltpu.SMEM)] +...  12.3 us
    ppermute x3, starting transfers between devices, chip_shards(): lax.ppermute(pair, 'orient', [(d, (d + 2 * s) % devices) for d in range(d...  5.48 us
    ppermute x1, waiting for transfers between devices, chip_shards(): from_x = lax.ppermute(across, 'cls', x_pairs)  3.86 us
    optimization_barrier x1, local copies, waits for them, and re-layouts, chip_shards(): _, panels = lax.optimization_barrier((got, panels))  2.42 us
    unnamed x7, local copies, waits for them, and re-layouts  2.41 us
    ppermute x1, waiting for transfers between devices, chip_shards(): mate_partial = lax.ppermute(partial, 'orient', mate_pairs)  1.52 us
  transfers between devices with their start and end apart: 21, of which 10 were waited for; matrix products, arithmetic and copies ran while one was open for 4% of the time, Pallas kernels for 15%

profile of v5, /device:TPU:0, one launch (start us, length us, event | category | flops | bytes accessed | tf_op | source)
XLA Modules:
  0.0 67.3 jit_solution(5121392629142134601)
XLA Ops:
  0.0 1.1 %copy.11 = bf16[1,16,2,7296]{3,1,2,0:T(8,128)(2,1)S(1)} copy(bf16[1,16,2,7296]{3,2,1,0:T(2,128)(2,1)} %param.5) | data formatting | bytes 933888 | tf_op args[0]
  1.1 0.1 pad_add_fusion.spot
  1.2 0.7 %copy-done = s32[1,16,4]{1,2,0:T(4,128)S(1)} copy-done((s32[1,16,4]{1,2,0:T(4,128)S(1)}, s32[1,16,4]{1,2,0:T(4,128)}, u32[]{:S(2)}) %copy-start) | copy-done | bytes 280
  1.9 0.7 copy-done.1
  2.5 0.6 shard_map.55
  3.1 0.5 collective-permute-start.1
  3.6 2.6 %collective-permute-start = (bf16[16,7424]{1,0:T(8,128)(2,1)S(1)}, bf16[16,7424]{1,0:T(8,128)(2,1)S(1)}, u32[]{:S(2)}, u32[]{:S(2)}) collective-permute-start(bf16[16,7424]{1,0:T(8,128)(2,1)S(1)} %get-tuple-element.28.refs_0_), channel_id=1, source_target_pairs={{0,4},{2,6},{4,8},{6,10},{8,12},{10,14},{12,13},{14,15},{13,9},{15... | collective-permute-start | bytes 712712 | tf_op jit(solution)/shard_map/ppermute | solution.py:292
  6.3 0.0 collective-permute-start.2
  6.3 0.0 collective-permute-done.1.refs_1_
  6.3 2.4 %copy.10 = bf16[1,1,128,2,7296]{4,2,3,1,0:T(8,128)(2,1)S(1)} copy(bf16[1,1,128,2,7296]{4,3,2,1,0:T(2,128)(2,1)} %param.9) | data formatting | bytes 7471104 | tf_op jit(solution)/shard_map/optimization_barrier | solution.py:309
  8.7 0.0 copy-start.2
  8.7 2.1 %collective-permute-start.3 = (bf16[16,7424]{1,0:T(8,128)(2,1)S(1)}, bf16[16,7424]{1,0:T(8,128)(2,1)S(1)}, u32[]{:S(2)}, u32[]{:S(2)}) collective-permute-start(bf16[16,7424]{1,0:T(8,128)(2,1)S(1)} %collective-permute-done.1.refs_1_), channel_id=1, source_target_pairs={{0,4},{2,6},{4,8},{6,10},{8,12},{10,14},{12,13},{14,15},{13,9},{15... | collective-permute-start | bytes 712712 | tf_op jit(solution)/shard_map/ppermute | solution.py:292
  10.8 0.0 collective-permute-start.4
  10.8 0.1 dynamic-slice_bitcast_fusion
  10.9 1.9 %collective-permute-done.refs_2_ = bf16[16,7424]{1,0:T(8,128)(2,1)S(1)} collective-permute-done((bf16[16,7424]{1,0:T(8,128)(2,1)S(1)}, bf16[16,7424]{1,0:T(8,128)(2,1)S(1)}, u32[]{:S(2)}, u32[]{:S(2)}) %collective-permute-start) | collective-permute-done | bytes 237600 | tf_op jit(solution)/shard_map/ppermute | solution.py:292
  12.8 2.1 %collective-permute-done.2.refs_3_ = bf16[16,7424]{1,0:T(8,128)(2,1)S(1)} collective-permute-done((bf16[16,7424]{1,0:T(8,128)(2,1)S(1)}, bf16[16,7424]{1,0:T(8,128)(2,1)S(1)}, u32[]{:S(2)}, u32[]{:S(2)}) %collective-permute-start.2) | collective-permute-done | bytes 237600 | tf_op jit(solution)/shard_map/ppermute | solution.py:292
  14.9 2.8 %collective-permute-done.3.refs_4_ = bf16[16,7424]{1,0:T(8,128)(2,1)S(1)} collective-permute-done((bf16[16,7424]{1,0:T(8,128)(2,1)S(1)}, bf16[16,7424]{1,0:T(8,128)(2,1)S(1)}, u32[]{:S(2)}, u32[]{:S(2)}) %collective-permute-start.3) | collective-permute-done | bytes 237600 | tf_op jit(solution)/shard_map/ppermute | solution.py:292
  17.6 1.5 %collective-permute-done.4.refs_5_ = bf16[16,7424]{1,0:T(8,128)(2,1)S(1)} collective-permute-done((bf16[16,7424]{1,0:T(8,128)(2,1)S(1)}, bf16[16,7424]{1,0:T(8,128)(2,1)S(1)}, u32[]{:S(2)}, u32[]{:S(2)}) %collective-permute-start.4) | collective-permute-done | bytes 237600 | tf_op jit(solution)/shard_map/ppermute | solution.py:292
  19.2 0.0 collective-permute-start.7
  19.2 1.6 %collective-permute-start.5 = (bf16[16,7424]{1,0:T(8,128)(2,1)S(1)}, bf16[16,7424]{1,0:T(8,128)(2,1)S(1)}, u32[]{:S(2)}, u32[]{:S(2)}) collective-permute-start(bf16[16,7424]{1,0:T(8,128)(2,1)S(1)} %collective-permute-done.refs_2_), channel_id=1, source_target_pairs={{0,4},{2,6},{4,8},{6,10},{8,12},{10,14},{12,13},{14,15},{13,9},{15... | collective-permute-start | bytes 712712 | tf_op jit(solution)/shard_map/ppermute | solution.py:292
  20.8 0.4 collective-permute-start.9
  21.2 0.3 collective-permute-start.12
  21.5 1.7 %collective-permute-start.13 = (bf16[16,7424]{1,0:T(8,128)(2,1)S(1)}, bf16[16,7424]{1,0:T(8,128)(2,1)S(1)}, u32[]{:S(2)}, u32[]{:S(2)}) collective-permute-start(bf16[16,7424]{1,0:T(8,128)(2,1)S(1)} %collective-permute-done.3.refs_4_), channel_id=1, source_target_pairs={{0,4},{2,6},{4,8},{6,10},{8,12},{10,14},{12,13},{14,15},{13,9},{15... | collective-permute-start | bytes 712712 | tf_op jit(solution)/shard_map/ppermute | solution.py:292
  23.2 4.5 %collective-permute-done.5.refs_0_ = bf16[16,7424]{1,0:T(8,128)(2,1)S(1)} collective-permute-done((bf16[16,7424]{1,0:T(8,128)(2,1)S(1)}, bf16[16,7424]{1,0:T(8,128)(2,1)S(1)}, u32[]{:S(2)}, u32[]{:S(2)}) %collective-permute-start.5) | collective-permute-done | bytes 237600 | tf_op jit(solution)/shard_map/ppermute | solution.py:292
  27.8 1.6 %collective-permute-start.6 = (bf16[16,7424]{1,0:T(8,128)(2,1)S(1)}, bf16[16,7424]{1,0:T(8,128)(2,1)S(1)}, u32[]{:S(2)}, u32[]{:S(2)}) collective-permute-start(bf16[16,7424]{1,0:T(8,128)(2,1)S(1)} %collective-permute-done.5.refs_0_), channel_id=1, source_target_pairs={{0,4},{2,6},{4,8},{6,10},{8,12},{10,14},{12,13},{14,15},{13,9},{15... | collective-permute-start | bytes 712712 | tf_op jit(solution)/shard_map/ppermute | solution.py:292
  29.3 0.0 collective-permute-done.9.refs_3_
  29.4 0.4 collective-permute-start.10
  29.9 4.6 %collective-permute-done.12.refs_1_ = bf16[16,7424]{1,0:T(8,128)(2,1)S(1)} collective-permute-done((bf16[16,7424]{1,0:T(8,128)(2,1)S(1)}, bf16[16,7424]{1,0:T(8,128)(2,1)S(1)}, u32[]{:S(2)}, u32[]{:S(2)}) %collective-permute-start.12) | collective-permute-done | bytes 237600 | tf_op jit(solution)/shard_map/ppermute | solution.py:292
  34.5 0.4 collective-permute-start.14
  34.9 1.6 %collective-permute-start.15 = (bf16[16,7424]{1,0:T(8,128)(2,1)S(1)}, bf16[16,7424]{1,0:T(8,128)(2,1)S(1)}, u32[]{:S(2)}, u32[]{:S(2)}) collective-permute-start(bf16[16,7424]{1,0:T(8,128)(2,1)S(1)} %collective-permute-done.13.refs_2_), channel_id=1, source_target_pairs={{0,4},{2,6},{4,8},{6,10},{8,12},{10,14},{12,13},{14,15},{13,9},{15... | collective-permute-start | bytes 712712 | tf_op jit(solution)/shard_map/ppermute | solution.py:292
  36.5 0.0 collective-permute-done.7.refs_8_.refs_10_.refs_4_
  36.5 4.2 %shard_map.56 = (f32[96,128]{1,0:T(8,128)S(1)}, f32[96,128]{1,0:T(8,128)S(1)}, f32[96,128]{1,0:T(8,128)S(1)}) custom-call(s32[4]{0:T(128)S(1)} %pad_add_fusion.spot, bf16[16,7424]{1,0:T(8,128)(2,1)S(1)} %get-tuple-element.28.refs_0_, bf16[16,7424]{1,0:T(8,128)(2,1)S(1)} %collective-permute-done.1.refs_1_, bf16[16,7424]{1,0:T(8,128)(2,1)S(1)} %collective-permute-done.refs_2_, ...), custom_call_target="tpu_custom_call" | custom-call | flops 956301312 | bytes 5136384 | tf_op jit(solution)/shard_map/pallas_call | solution.py:166
  40.8 1.6 %collective-permute-start.8 = (bf16[16,7424]{1,0:T(8,128)(2,1)S(1)}, bf16[16,7424]{1,0:T(8,128)(2,1)S(1)}, u32[]{:S(2)}, u32[]{:S(2)}) collective-permute-start(bf16[16,7424]{1,0:T(8,128)(2,1)S(1)} %collective-permute-done.6.refs_4_), channel_id=1, source_target_pairs={{0,4},{2,6},{4,8},{6,10},{8,12},{10,14},{12,13},{14,15},{13,9},{15... | collective-permute-start | bytes 712712 | tf_op jit(solution)/shard_map/ppermute | solution.py:292
  42.4 0.5 collective-permute-start.11
  42.8 1.8 %collective-permute-done.14.refs_5_ = bf16[16,7424]{1,0:T(8,128)(2,1)S(1)} collective-permute-done((bf16[16,7424]{1,0:T(8,128)(2,1)S(1)}, bf16[16,7424]{1,0:T(8,128)(2,1)S(1)}, u32[]{:S(2)}, u32[]{:S(2)}) %collective-permute-start.14) | collective-permute-done | bytes 237600 | tf_op jit(solution)/shard_map/ppermute | solution.py:292
  44.7 4.7 %shard_map.57 = (f32[128,128]{1,0:T(8,128)S(1)}, f32[128,128]{1,0:T(8,128)S(1)}, f32[128,128]{1,0:T(8,128)S(1)}) custom-call(s32[4]{0:T(128)S(1)} %pad_add_fusion.spot, bf16[16,7424]{1,0:T(8,128)(2,1)S(1)} %collective-permute-done.5.refs_0_, bf16[16,7424]{1,0:T(8,128)(2,1)S(1)} %collective-permute-done.12.refs_1_, ...), custom_call_target="tpu_custom_call" | custom-call | flops 956301312 | bytes 5603328 | tf_op jit(solution)/shard_map/pallas_call | solution.py:166
  49.4 3.4 %shard_map.58 = (f32[2,256,128]{2,1,0:T(8,128)S(1)}, f32[256,128]{1,0:T(8,128)S(1)}) custom-call(s32[4]{0:T(128)S(1)} %pad_add_fusion.spot, bf16[16,7424]{1,0:T(8,128)(2,1)S(1)} %collective-permute-done.8.refs_0_, bf16[16,7424]{1,0:T(8,128)(2,1)S(1)} %collective-permute-done.11.refs_1_, f32[1,7296]{1,0:T(1,128)S(1)} %broadcast_in_dim.3.refs_6_.refs_8_.refs_2_, ...), custom_call_target="tpu_custom_call" | custom-call | flops 956301312 | bytes 4202496 | tf_op jit(solution)/shard_map/pallas_call | solution.py:166
  52.8 0.1 collective-permute-start.16
  52.9 1.5 %collective-permute-done.16.mate = f32[2,256,128]{2,1,0:T(8,128)S(1)} collective-permute-done((f32[2,256,128]{2,1,0:T(8,128)S(1)}, f32[2,256,128]{2,1,0:T(8,128)S(1)}, u32[]{:S(2)}, u32[]{:S(2)}) %collective-permute-start.16) | collective-permute-done | bytes 262176 | tf_op jit(solution)/shard_map/ppermute | solution.py:346
  54.4 0.9 %shard_map.59 = (f32[128,128]{1,0:T(8,128)S(1)}, f32[8,128]{1,0:T(8,128)S(1)}, f32[136,128]{1,0:T(8,128)S(1)}) custom-call(s32[4]{0:T(128)S(1)} %pad_add_fusion.spot, f32[2,256,128]{2,1,0:T(8,128)S(1)} %get-tuple-element.44.partial, f32[2,256,128]{2,1,0:T(8,128)S(1)} %collective-permute-done.16.mate, f32[256,128]{1,0:T(8,128)S(1)} %get-tuple-element.45.facts), custom_call_target="tpu_custom_call" | custom-call | tf_op jit(solution)/shard_map/pallas_call | solution.py:347
  55.3 0.5 collective-permute-start.17
  55.8 3.9 %collective-permute-done.17.across = f32[136,128]{1,0:T(8,128)S(1)} collective-permute-done((f32[136,128]{1,0:T(8,128)S(1)}, f32[136,128]{1,0:T(8,128)S(1)}, u32[]{:S(2)}, u32[]{:S(2)}) %collective-permute-start.17) | collective-permute-done | bytes 69664 | tf_op jit(solution)/shard_map/ppermute | solution.py:358
  59.7 1.6 %collective-permute-start.18 = (f32[8,128]{1,0:T(8,128)S(1)}, f32[8,128]{1,0:T(8,128)S(1)}, u32[]{:S(2)}, u32[]{:S(2)}) collective-permute-start(f32[8,128]{1,0:T(8,128)S(1)} %select_maximum_fusion.pair.refs_0_), channel_id=1, source_target_pairs={{0,4},{2,6},{4,8},{6,10},{8,12},{10,14},{12,0},{14,2},{1,5},{3,7},... | collective-permute-start | bytes 12296 | tf_op jit(solution)/shard_map/ppermute | solution.py:365
  61.3 1.5 %collective-permute-start.19 = (f32[8,128]{1,0:T(8,128)S(1)}, f32[8,128]{1,0:T(8,128)S(1)}, u32[]{:S(2)}, u32[]{:S(2)}) collective-permute-start(f32[8,128]{1,0:T(8,128)S(1)} %select_maximum_fusion.pair.refs_0_), channel_id=1, source_target_pairs={{0,8},{2,10},{4,12},{6,14},{8,0},{10,2},{12,4},{14,6},{1,9},{3,11}... | collective-permute-start | bytes 12296 | tf_op jit(solution)/shard_map/ppermute | solution.py:365
  62.8 2.4 %collective-permute-start.20 = (f32[8,128]{1,0:T(8,128)S(1)}, f32[8,128]{1,0:T(8,128)S(1)}, u32[]{:S(2)}, u32[]{:S(2)}) collective-permute-start(f32[8,128]{1,0:T(8,128)S(1)} %select_maximum_fusion.pair.refs_0_), channel_id=1, source_target_pairs={{0,12},{2,14},{4,0},{6,2},{8,4},{10,6},{12,8},{14,10},{1,13},{3,15... | collective-permute-start | bytes 12296 | tf_op jit(solution)/shard_map/ppermute | solution.py:365
  65.2 1.1 %shard_map.60 = (f32[128,256]{1,0:T(8,128)S(1)}, f32[128,128]{1,0:T(8,128)S(1)}) custom-call(s32[4]{0:T(128)S(1)} %pad_add_fusion.spot, f32[128,128]{1,0:T(8,128)S(1)} %get-tuple-element.48.mine, f32[136,128]{1,0:T(8,128)S(1)} %collective-permute-done.17.across, f32[8,128]{1,0:T(8,128)S(1)} %select_maximum_fusion.pair.refs_0_, ...), custom_call_target="tpu_custom_call" | custom-call | tf_op jit(solution)/shard_map/pallas_call | solution.py:368
  66.3 0.2 collective-permute-done.20.refs_3_
  66.5 0.8 %shard_map.61 = f32[128,256]{1,0:T(8,128)} custom-call(f32[8,128]{1,0:T(8,128)S(1)} %select_maximum_fusion.pair.refs_0_, f32[8,128]{1,0:T(8,128)S(1)} %collective-permute-done.18.refs_1_, f32[8,128]{1,0:T(8,128)S(1)} %collective-permute-done.19.refs_2_, f32[8,128]{1,0:T(8,128)S(1)} %collective-permute-done.20.refs_3_, ...), custom_call_target="tpu_custom_call" | custom-call | tf_op jit(solution)/shard_map/pallas_call | solution.py:378
  (14 shorter events, 0.1 us)
Async XLA Ops:
  1.2 0.7 %copy-start = (s32[1,16,4]{1,2,0:T(4,128)S(1)}, s32[1,16,4]{1,2,0:T(4,128)}, u32[]{:S(2)}) copy-start(s32[1,16,4]{1,2,0:T(4,128)} %param.7) | copy-start | bytes 772
  1.9 0.7 copy-start.1
  3.1 3.2 %collective-permute-start.1 = (bf16[16,7424]{1,0:T(8,128)(2,1)S(1)}, bf16[16,7424]{1,0:T(8,128)(2,1)S(1)}, u32[]{:S(2)}, u32[]{:S(2)}) collective-permute-start(bf16[16,7424]{1,0:T(8,128)(2,1)S(1)} %get-tuple-element.29), channel_id=1, source_target_pairs={{0,2},{2,0},{4,6},{6,4},{8,10},{10,8},{12,14},{14,12},{1,3},{3,1},... | collective-permute-start | bytes 712712 | tf_op jit(solution)/shard_map/ppermute | solution.py:307
  3.6 9.2 %collective-permute-start = (bf16[16,7424]{1,0:T(8,128)(2,1)S(1)}, bf16[16,7424]{1,0:T(8,128)(2,1)S(1)}, u32[]{:S(2)}, u32[]{:S(2)}) collective-permute-start(bf16[16,7424]{1,0:T(8,128)(2,1)S(1)} %get-tuple-element.28.refs_0_), channel_id=1, source_target_pairs={{0,4},{2,6},{4,8},{6,10},{8,12},{10,14},{12,13},{14,15},{13,9},{15... | collective-permute-start | bytes 712712 | tf_op jit(solution)/shard_map/ppermute | solution.py:292
  6.3 8.6 %collective-permute-start.2 = (bf16[16,7424]{1,0:T(8,128)(2,1)S(1)}, bf16[16,7424]{1,0:T(8,128)(2,1)S(1)}, u32[]{:S(2)}, u32[]{:S(2)}) collective-permute-start(bf16[16,7424]{1,0:T(8,128)(2,1)S(1)} %get-tuple-element.28.refs_0_), channel_id=1, source_target_pairs={{0,1},{2,3},{4,0},{6,2},{8,4},{10,6},{12,8},{14,10},{13,12},{15,14... | collective-permute-start | bytes 712712 | tf_op jit(solution)/shard_map/ppermute | solution.py:292
  8.7 21.2 %copy-start.2 = (f32[7296]{0:T(1024)S(1)}, f32[7296]{0:T(1024)}, u32[]{:S(2)}) copy-start(f32[7296]{0:T(1024)} %param.8) | copy-start | bytes 87556
  8.7 8.9 %collective-permute-start.3 = (bf16[16,7424]{1,0:T(8,128)(2,1)S(1)}, bf16[16,7424]{1,0:T(8,128)(2,1)S(1)}, u32[]{:S(2)}, u32[]{:S(2)}) collective-permute-start(bf16[16,7424]{1,0:T(8,128)(2,1)S(1)} %collective-permute-done.1.refs_1_), channel_id=1, source_target_pairs={{0,4},{2,6},{4,8},{6,10},{8,12},{10,14},{12,13},{14,15},{13,9},{15... | collective-permute-start | bytes 712712 | tf_op jit(solution)/shard_map/ppermute | solution.py:292
  10.8 8.4 %collective-permute-start.4 = (bf16[16,7424]{1,0:T(8,128)(2,1)S(1)}, bf16[16,7424]{1,0:T(8,128)(2,1)S(1)}, u32[]{:S(2)}, u32[]{:S(2)}) collective-permute-start(bf16[16,7424]{1,0:T(8,128)(2,1)S(1)} %collective-permute-done.1.refs_1_), channel_id=1, source_target_pairs={{0,1},{2,3},{4,0},{6,2},{8,4},{10,6},{12,8},{14,10},{13,12},{15,14... | collective-permute-start | bytes 712712 | tf_op jit(solution)/shard_map/ppermute | solution.py:292
  19.2 17.3 %collective-permute-start.7 = (bf16[128,7296]{1,0:T(8,128)(2,1)S(1)}, bf16[128,7296]{1,0:T(8,128)(2,1)S(1)}, u32[]{:S(2)}, u32[]{:S(2)}) collective-permute-start(bf16[128,7296]{1,0:T(8,128)(2,1)S(1)} %dynamic-slice_bitcast_fusion), channel_id=1, source_target_pairs={{0,2},{2,0},{4,6},{6,4},{8,10},{10,8},{12,14},{14,12},{1,3},{3,1},... | collective-permute-start | bytes 5603336 | tf_op jit(solution)/shard_map/ppermute | solution.py:333
  19.2 8.6 %collective-permute-start.5 = (bf16[16,7424]{1,0:T(8,128)(2,1)S(1)}, bf16[16,7424]{1,0:T(8,128)(2,1)S(1)}, u32[]{:S(2)}, u32[]{:S(2)}) collective-permute-start(bf16[16,7424]{1,0:T(8,128)(2,1)S(1)} %collective-permute-done.refs_2_), channel_id=1, source_target_pairs={{0,4},{2,6},{4,8},{6,10},{8,12},{10,14},{12,13},{14,15},{13,9},{15... | collective-permute-start | bytes 712712 | tf_op jit(solution)/shard_map/ppermute | solution.py:292
  20.8 8.6 %collective-permute-start.9 = (bf16[16,7424]{1,0:T(8,128)(2,1)S(1)}, bf16[16,7424]{1,0:T(8,128)(2,1)S(1)}, u32[]{:S(2)}, u32[]{:S(2)}) collective-permute-start(bf16[16,7424]{1,0:T(8,128)(2,1)S(1)} %collective-permute-done.4.refs_5_), channel_id=1, source_target_pairs={{0,1},{2,3},{4,0},{6,2},{8,4},{10,6},{12,8},{14,10},{13,12},{15,14... | collective-permute-start | bytes 712712 | tf_op jit(solution)/shard_map/ppermute | solution.py:292
  21.2 13.3 %collective-permute-start.12 = (bf16[16,7424]{1,0:T(8,128)(2,1)S(1)}, bf16[16,7424]{1,0:T(8,128)(2,1)S(1)}, u32[]{:S(2)}, u32[]{:S(2)}) collective-permute-start(bf16[16,7424]{1,0:T(8,128)(2,1)S(1)} %collective-permute-done.2.refs_3_), channel_id=1, source_target_pairs={{0,1},{2,3},{4,0},{6,2},{8,4},{10,6},{12,8},{14,10},{13,12},{15,14... | collective-permute-start | bytes 712712 | tf_op jit(solution)/shard_map/ppermute | solution.py:292
  21.5 13.4 %collective-permute-start.13 = (bf16[16,7424]{1,0:T(8,128)(2,1)S(1)}, bf16[16,7424]{1,0:T(8,128)(2,1)S(1)}, u32[]{:S(2)}, u32[]{:S(2)}) collective-permute-start(bf16[16,7424]{1,0:T(8,128)(2,1)S(1)} %collective-permute-done.3.refs_4_), channel_id=1, source_target_pairs={{0,4},{2,6},{4,8},{6,10},{8,12},{10,14},{12,13},{14,15},{13,9},{15... | collective-permute-start | bytes 712712 | tf_op jit(solution)/shard_map/ppermute | solution.py:292
  27.8 13.0 %collective-permute-start.6 = (bf16[16,7424]{1,0:T(8,128)(2,1)S(1)}, bf16[16,7424]{1,0:T(8,128)(2,1)S(1)}, u32[]{:S(2)}, u32[]{:S(2)}) collective-permute-start(bf16[16,7424]{1,0:T(8,128)(2,1)S(1)} %collective-permute-done.5.refs_0_), channel_id=1, source_target_pairs={{0,4},{2,6},{4,8},{6,10},{8,12},{10,14},{12,13},{14,15},{13,9},{15... | collective-permute-start | bytes 712712 | tf_op jit(solution)/shard_map/ppermute | solution.py:292
  29.4 13.0 %collective-permute-start.10 = (bf16[16,7424]{1,0:T(8,128)(2,1)S(1)}, bf16[16,7424]{1,0:T(8,128)(2,1)S(1)}, u32[]{:S(2)}, u32[]{:S(2)}) collective-permute-start(bf16[16,7424]{1,0:T(8,128)(2,1)S(1)} %collective-permute-done.9.refs_3_), channel_id=1, source_target_pairs={{0,1},{2,3},{4,0},{6,2},{8,4},{10,6},{12,8},{14,10},{13,12},{15,14... | collective-permute-start | bytes 712712 | tf_op jit(solution)/shard_map/ppermute | solution.py:292
  34.5 10.2 %collective-permute-start.14 = (bf16[16,7424]{1,0:T(8,128)(2,1)S(1)}, bf16[16,7424]{1,0:T(8,128)(2,1)S(1)}, u32[]{:S(2)}, u32[]{:S(2)}) collective-permute-start(bf16[16,7424]{1,0:T(8,128)(2,1)S(1)} %collective-permute-done.12.refs_1_), channel_id=1, source_target_pairs={{0,1},{2,3},{4,0},{6,2},{8,4},{10,6},{12,8},{14,10},{13,12},{15,14... | collective-permute-start | bytes 712712 | tf_op jit(solution)/shard_map/ppermute | solution.py:292
  34.9 9.7 %collective-permute-start.15 = (bf16[16,7424]{1,0:T(8,128)(2,1)S(1)}, bf16[16,7424]{1,0:T(8,128)(2,1)S(1)}, u32[]{:S(2)}, u32[]{:S(2)}) collective-permute-start(bf16[16,7424]{1,0:T(8,128)(2,1)S(1)} %collective-permute-done.13.refs_2_), channel_id=1, source_target_pairs={{0,4},{2,6},{4,8},{6,10},{8,12},{10,14},{12,13},{14,15},{13,9},{15... | collective-permute-start | bytes 712712 | tf_op jit(solution)/shard_map/ppermute | solution.py:292
  40.8 8.6 %collective-permute-start.8 = (bf16[16,7424]{1,0:T(8,128)(2,1)S(1)}, bf16[16,7424]{1,0:T(8,128)(2,1)S(1)}, u32[]{:S(2)}, u32[]{:S(2)}) collective-permute-start(bf16[16,7424]{1,0:T(8,128)(2,1)S(1)} %collective-permute-done.6.refs_4_), channel_id=1, source_target_pairs={{0,4},{2,6},{4,8},{6,10},{8,12},{10,14},{12,13},{14,15},{13,9},{15... | collective-permute-start | bytes 712712 | tf_op jit(solution)/shard_map/ppermute | solution.py:292
  42.4 7.0 %collective-permute-start.11 = (bf16[16,7424]{1,0:T(8,128)(2,1)S(1)}, bf16[16,7424]{1,0:T(8,128)(2,1)S(1)}, u32[]{:S(2)}, u32[]{:S(2)}) collective-permute-start(bf16[16,7424]{1,0:T(8,128)(2,1)S(1)} %collective-permute-done.10.refs_7_), channel_id=1, source_target_pairs={{0,1},{2,3},{4,0},{6,2},{8,4},{10,6},{12,8},{14,10},{13,12},{15,14... | collective-permute-start | bytes 712712 | tf_op jit(solution)/shard_map/ppermute | solution.py:292
  52.8 1.6 %collective-permute-start.16 = (f32[2,256,128]{2,1,0:T(8,128)S(1)}, f32[2,256,128]{2,1,0:T(8,128)S(1)}, u32[]{:S(2)}, u32[]{:S(2)}) collective-permute-start(f32[2,256,128]{2,1,0:T(8,128)S(1)} %get-tuple-element.44.partial), channel_id=1, source_target_pairs={{0,2},{2,0},{4,6},{6,4},{8,10},{10,8},{12,14},{14,12},{1,3},{3,1},... | collective-permute-start | bytes 786440 | tf_op jit(solution)/shard_map/ppermute | solution.py:346
  55.3 4.3 %collective-permute-start.17 = (f32[136,128]{1,0:T(8,128)S(1)}, f32[136,128]{1,0:T(8,128)S(1)}, u32[]{:S(2)}, u32[]{:S(2)}) collective-permute-start(f32[136,128]{1,0:T(8,128)S(1)} %get-tuple-element.47), channel_id=1, source_target_pairs={{0,1},{1,0},{2,3},{3,2},{4,5},{5,4},{6,7},{7,6},{8,9},{9,8},{10,11... | collective-permute-start | bytes 208904 | tf_op jit(solution)/shard_map/ppermute | solution.py:358
  59.7 6.6 %collective-permute-start.18 = (f32[8,128]{1,0:T(8,128)S(1)}, f32[8,128]{1,0:T(8,128)S(1)}, u32[]{:S(2)}, u32[]{:S(2)}) collective-permute-start(f32[8,128]{1,0:T(8,128)S(1)} %select_maximum_fusion.pair.refs_0_), channel_id=1, source_target_pairs={{0,4},{2,6},{4,8},{6,10},{8,12},{10,14},{12,0},{14,2},{1,5},{3,7},... | collective-permute-start | bytes 12296 | tf_op jit(solution)/shard_map/ppermute | solution.py:365
  61.3 5.0 %collective-permute-start.19 = (f32[8,128]{1,0:T(8,128)S(1)}, f32[8,128]{1,0:T(8,128)S(1)}, u32[]{:S(2)}, u32[]{:S(2)}) collective-permute-start(f32[8,128]{1,0:T(8,128)S(1)} %select_maximum_fusion.pair.refs_0_), channel_id=1, source_target_pairs={{0,8},{2,10},{4,12},{6,14},{8,0},{10,2},{12,4},{14,6},{1,9},{3,11}... | collective-permute-start | bytes 12296 | tf_op jit(solution)/shard_map/ppermute | solution.py:365
  62.8 3.7 %collective-permute-start.20 = (f32[8,128]{1,0:T(8,128)S(1)}, f32[8,128]{1,0:T(8,128)S(1)}, u32[]{:S(2)}, u32[]{:S(2)}) collective-permute-start(f32[8,128]{1,0:T(8,128)S(1)} %select_maximum_fusion.pair.refs_0_), channel_id=1, source_target_pairs={{0,12},{2,14},{4,0},{6,2},{8,4},{10,6},{12,8},{14,10},{1,13},{3,15... | collective-permute-start | bytes 12296 | tf_op jit(solution)/shard_map/ppermute | solution.py:365

commit v6 on v5

--- a/solution.py
+++ b/solution.py
@@ -304,7 +304,8 @@
         scratch_shapes=[pltpu.VMEM((per_device, LANES), jnp.float32)],
         compiler_params=params,
     )(spot, planes, defocus, jnp.transpose(block_ids[0]))
-    got = lax.ppermute(given, "orient", mate_pairs)
+    with jax.named_scope("mate_rows"):
+        got = lax.ppermute(given, "orient", mate_pairs)
 
     _, panels = lax.optimization_barrier((got, panels))
     sides = lax.optimization_barrier(jnp.transpose(panels[0, 0], (1, 0, 2)))
@@ -314,30 +315,34 @@
     waiting = [((0, False), kept), ((0, True), got)]
     ahead = {False: kept, True: got}
     behind = {False: kept, True: got}
-    orders, earlier = [], []
+    orders, earlier, late = [], [], []
     for step in range(1, chips + 1):
-        if step == 2 or (earlier and step == chips):
-            tie = earlier[-1][2] if earlier else given_panel
+        if step == chips and step > 2:
+            orders.append([key for key, _ in waiting])
+            earlier.append(score([c for _, c in waiting]))
+            waiting = []
+            tie = earlier[-1][2]
             ahead = {c: lax.optimization_barrier((v, tie))[0] for c, v in ahead.items()}
             behind = {c: lax.optimization_barrier((v, tie))[0] for c, v in behind.items()}
-        arrived = []
+        waiting = waiting + late
+        late = []
         for crossed in (False, True):
             if step < chips or not crossed:
-                ahead[crossed] = forward(ahead[crossed], 1)
-                arrived.append(((-step, crossed), ahead[crossed]))
+                with jax.named_scope(f"ahead_{'BA'[not crossed]}{step}"):
+                    ahead[crossed] = forward(ahead[crossed], 1)
+                late.append(((-step, crossed), ahead[crossed]))
             if step < chips or crossed:
-                behind[crossed] = forward(behind[crossed], -1)
-                arrived.append(((step, crossed), behind[crossed]))
-        if step == 1:
-            given_panel = lax.optimization_barrier((given_panel, *[v for _, v in arrived]))[0]
-            mate_panel = lax.ppermute(given_panel, "orient", mate_pairs)
-        if step in (2, chips):
-            orders.append([key for key, _ in waiting])
-            earlier.append(
-                score_call([c for _, c in waiting], None, None, spot, noise, sides, mate_panel)
-            )
-            waiting = []
-        waiting = waiting + arrived
+                with jax.named_scope(f"behind_{'BA'[not crossed]}{step}"):
+                    behind[crossed] = forward(behind[crossed], -1)
+                late.append(((step, crossed), behind[crossed]))
+        if step == 2:
+            given_panel = lax.optimization_barrier((given_panel, *[v for _, v in late]))[0]
+            with jax.named_scope("mate_panel"):
+                mate_panel = lax.ppermute(given_panel, "orient", mate_pairs)
+            score = lambda c: score_call(c, None, None, spot, noise, sides, mate_panel)
+    orders.append([key for key, _ in waiting])
+    earlier.append(score([c for _, c in waiting]))
+    waiting = late
     orders.append([key for key, _ in waiting])
     partial, all_facts = score_call(
         [c for _, c in waiting], orders, earlier, spot, noise, sides, mate_panel

time: 67.5 us -> 67 us (level)
  waiting for transfers between devices: 24.9 us -> 23 us
  starting transfers between devices: 21.5 us -> 22.9 us
    ppermute x14, waiting for transfers between devices: 19.3 us -> 17.7 us  [forward(): return lax.ppermute(values, ('orient', 'cls'), pairs)]
    ppermute x1, waiting for transfers between devices: 3.86 us -> 2.65 us  [chip_shards(): from_x = lax.ppermute(across, 'cls', x_pairs)]
    ppermute x1, starting transfers between devices: 0.49 us -> 1.7 us  [chip_shards(): from_x = lax.ppermute(across, 'cls', x_pairs)]
    ppermute x3, waiting for transfers between devices: 0.21 us -> 1.15 us  [chip_shards(): lax.ppermute(pair, 'orient', [(d, (d + 2 * s) % devices) for d in range(d...]
  transfers between devices with their start and end apart: 21 -> 21, of which waited for: 10 -> 12; matrix products, arithmetic and copies ran while one was open for 4% -> 4% of each run, Pallas kernels for 15% -> 15%
where the time goes in v6:
time: 67 us; the launch traced here: 66.8 us
  waiting for transfers between devices  23 us (34%)
  starting transfers between devices  22.9 us (34%)
  Pallas kernels  15.7 us (23%)
  local copies, waits for them, and re-layouts  4.98 us (7%)
    ppermute x14, waiting for transfers between devices, forward(): return lax.ppermute(values, ('orient', 'cls'), pairs)  17.7 us
    ppermute x14, starting transfers between devices, forward(): return lax.ppermute(values, ('orient', 'cls'), pairs)  14.9 us
    pallas_call x3, Pallas kernels, score_call(): pl.pallas_call(kernel, in_specs=[pl.BlockSpec(memory_space=pltpu.SMEM)] +...  12.3 us
    ppermute x3, starting transfers between devices, chip_shards(): lax.ppermute(pair, 'orient', [(d, (d + 2 * s) % devices) for d in range(d...  5.73 us
    ppermute x1, waiting for transfers between devices, chip_shards(): from_x = lax.ppermute(across, 'cls', x_pairs)  2.65 us
    optimization_barrier x1, local copies, waits for them, and re-layouts, chip_shards(): _, panels = lax.optimization_barrier((got, panels))  2.42 us
    unnamed x7, local copies, waits for them, and re-layouts  2.41 us
    ppermute x1, starting transfers between devices, chip_shards(): from_x = lax.ppermute(across, 'cls', x_pairs)  1.7 us
  transfers between devices with their start and end apart: 21, of which 12 were waited for; matrix products, arithmetic and copies ran while one was open for 4% of the time, Pallas kernels for 15%

profile of v6, /device:TPU:0, one launch (start us, length us, event | category | flops | bytes accessed | tf_op | source)
XLA Modules:
  0.0 66.8 jit_solution(6394478724720006135)
XLA Ops:
  0.0 1.1 %copy.11 = bf16[1,16,2,7296]{3,1,2,0:T(8,128)(2,1)S(1)} copy(bf16[1,16,2,7296]{3,2,1,0:T(2,128)(2,1)} %param.5) | data formatting | bytes 933888 | tf_op args[0]
  1.1 0.1 pad_add_fusion.spot
  1.2 0.7 %copy-done = s32[1,16,4]{1,2,0:T(4,128)S(1)} copy-done((s32[1,16,4]{1,2,0:T(4,128)S(1)}, s32[1,16,4]{1,2,0:T(4,128)}, u32[]{:S(2)}) %copy-start) | copy-done | bytes 280
  1.9 0.7 copy-done.1
  2.5 0.6 shard_map.55
  3.1 0.5 collective-permute-start.3
  3.6 2.6 %collective-permute-start = (bf16[16,7424]{1,0:T(8,128)(2,1)S(1)}, bf16[16,7424]{1,0:T(8,128)(2,1)S(1)}, u32[]{:S(2)}, u32[]{:S(2)}) collective-permute-start(bf16[16,7424]{1,0:T(8,128)(2,1)S(1)} %get-tuple-element.24.refs_0_), channel_id=1, source_target_pairs={{0,4},{2,6},{4,8},{6,10},{8,12},{10,14},{12,13},{14,15},{13,9},{15... | collective-permute-start | bytes 712712 | tf_op jit(solution)/shard_map/ahead_A1/ppermute | solution.py:292
  6.3 2.0 %collective-permute-start.5 = (bf16[16,7424]{1,0:T(8,128)(2,1)S(1)}, bf16[16,7424]{1,0:T(8,128)(2,1)S(1)}, u32[]{:S(2)}, u32[]{:S(2)}) collective-permute-start(bf16[16,7424]{1,0:T(8,128)(2,1)S(1)} %collective-permute-done.3.refs_1_), channel_id=1, source_target_pairs={{0,4},{2,6},{4,8},{6,10},{8,12},{10,14},{12,13},{14,15},{13,9},{15... | collective-permute-start | bytes 712712 | tf_op jit(solution)/shard_map/ahead_B1/ppermute | solution.py:292
  8.3 0.0 collective-permute-start.6
  8.3 2.4 %copy.10 = bf16[1,1,128,2,7296]{4,2,3,1,0:T(8,128)(2,1)S(1)} copy(bf16[1,1,128,2,7296]{4,3,2,1,0:T(2,128)(2,1)} %param.9) | data formatting | bytes 7471104 | tf_op jit(solution)/shard_map/optimization_barrier | solution.py:310
  10.7 0.0 copy-start.2
  10.7 2.1 %collective-permute-done.refs_2_ = bf16[16,7424]{1,0:T(8,128)(2,1)S(1)} collective-permute-done((bf16[16,7424]{1,0:T(8,128)(2,1)S(1)}, bf16[16,7424]{1,0:T(8,128)(2,1)S(1)}, u32[]{:S(2)}, u32[]{:S(2)}) %collective-permute-start) | collective-permute-done | bytes 237600 | tf_op jit(solution)/shard_map/ahead_A1/ppermute | solution.py:292
  12.8 2.0 %collective-permute-start.1 = (bf16[16,7424]{1,0:T(8,128)(2,1)S(1)}, bf16[16,7424]{1,0:T(8,128)(2,1)S(1)}, u32[]{:S(2)}, u32[]{:S(2)}) collective-permute-start(bf16[16,7424]{1,0:T(8,128)(2,1)S(1)} %collective-permute-done.refs_2_), channel_id=1, source_target_pairs={{0,4},{2,6},{4,8},{6,10},{8,12},{10,14},{12,13},{14,15},{13,9},{15... | collective-permute-start | bytes 712712 | tf_op jit(solution)/shard_map/ahead_A2/ppermute | solution.py:292
  14.8 0.0 collective-permute-done.4.refs_3_
  14.9 3.0 %collective-permute-done.5.refs_4_ = bf16[16,7424]{1,0:T(8,128)(2,1)S(1)} collective-permute-done((bf16[16,7424]{1,0:T(8,128)(2,1)S(1)}, bf16[16,7424]{1,0:T(8,128)(2,1)S(1)}, u32[]{:S(2)}, u32[]{:S(2)}) %collective-permute-start.5) | collective-permute-done | bytes 237600 | tf_op jit(solution)/shard_map/ahead_B1/ppermute | solution.py:292
  17.9 2.0 %collective-permute-start.8 = (bf16[16,7424]{1,0:T(8,128)(2,1)S(1)}, bf16[16,7424]{1,0:T(8,128)(2,1)S(1)}, u32[]{:S(2)}, u32[]{:S(2)}) collective-permute-start(bf16[16,7424]{1,0:T(8,128)(2,1)S(1)} %collective-permute-done.5.refs_4_), channel_id=1, source_target_pairs={{0,4},{2,6},{4,8},{6,10},{8,12},{10,14},{12,13},{14,15},{13,9},{15... | collective-permute-start | bytes 712712 | tf_op jit(solution)/shard_map/ahead_B2/ppermute | solution.py:292
  19.9 0.0 collective-permute-done.6.refs_5_
  20.0 0.0 collective-permute-start.9
  20.0 0.1 dynamic-slice_bitcast_fusion
  20.1 2.9 %collective-permute-done.1.refs_6_ = bf16[16,7424]{1,0:T(8,128)(2,1)S(1)} collective-permute-done((bf16[16,7424]{1,0:T(8,128)(2,1)S(1)}, bf16[16,7424]{1,0:T(8,128)(2,1)S(1)}, u32[]{:S(2)}, u32[]{:S(2)}) %collective-permute-start.1) | collective-permute-done | bytes 237600 | tf_op jit(solution)/shard_map/ahead_A2/ppermute | solution.py:292
  23.0 2.1 %collective-permute-done.7.refs_7_ = bf16[16,7424]{1,0:T(8,128)(2,1)S(1)} collective-permute-done((bf16[16,7424]{1,0:T(8,128)(2,1)S(1)}, bf16[16,7424]{1,0:T(8,128)(2,1)S(1)}, u32[]{:S(2)}, u32[]{:S(2)}) %collective-permute-start.7) | collective-permute-done | bytes 237600 | tf_op jit(solution)/shard_map/behind_A2/ppermute | solution.py:292
  25.1 2.8 %collective-permute-done.8.refs_8_ = bf16[16,7424]{1,0:T(8,128)(2,1)S(1)} collective-permute-done((bf16[16,7424]{1,0:T(8,128)(2,1)S(1)}, bf16[16,7424]{1,0:T(8,128)(2,1)S(1)}, u32[]{:S(2)}, u32[]{:S(2)}) %collective-permute-start.8) | collective-permute-done | bytes 237600 | tf_op jit(solution)/shard_map/ahead_B2/ppermute | solution.py:292
  27.8 1.5 %collective-permute-done.9.refs_9_ = bf16[16,7424]{1,0:T(8,128)(2,1)S(1)} collective-permute-done((bf16[16,7424]{1,0:T(8,128)(2,1)S(1)}, bf16[16,7424]{1,0:T(8,128)(2,1)S(1)}, u32[]{:S(2)}, u32[]{:S(2)}) %collective-permute-start.9) | collective-permute-done | bytes 237600 | tf_op jit(solution)/shard_map/behind_B2/ppermute | solution.py:292
  29.4 0.0 collective-permute-start.10
  29.4 0.3 collective-permute-start.12
  29.7 1.7 %collective-permute-start.2 = (bf16[16,7424]{1,0:T(8,128)(2,1)S(1)}, bf16[16,7424]{1,0:T(8,128)(2,1)S(1)}, u32[]{:S(2)}, u32[]{:S(2)}) collective-permute-start(bf16[16,7424]{1,0:T(8,128)(2,1)S(1)} %collective-permute-done.1.refs_6_), channel_id=1, source_target_pairs={{0,4},{2,6},{4,8},{6,10},{8,12},{10,14},{12,13},{14,15},{13,9},{15... | collective-permute-start | bytes 712712 | tf_op jit(solution)/shard_map/ahead_A3/ppermute | solution.py:292
  31.4 0.3 collective-permute-start.14
  31.8 1.7 %collective-permute-start.15 = (bf16[16,7424]{1,0:T(8,128)(2,1)S(1)}, bf16[16,7424]{1,0:T(8,128)(2,1)S(1)}, u32[]{:S(2)}, u32[]{:S(2)}) collective-permute-start(bf16[16,7424]{1,0:T(8,128)(2,1)S(1)} %collective-permute-done.8.refs_8_), channel_id=1, source_target_pairs={{0,4},{2,6},{4,8},{6,10},{8,12},{10,14},{12,13},{14,15},{13,9},{15... | collective-permute-start | bytes 712712 | tf_op jit(solution)/shard_map/ahead_B3/ppermute | solution.py:292
  33.5 5.2 %shard_map.56 = (f32[160,128]{1,0:T(8,128)S(1)}, f32[160,128]{1,0:T(8,128)S(1)}, f32[160,128]{1,0:T(8,128)S(1)}) custom-call(s32[4]{0:T(128)S(1)} %pad_add_fusion.spot, bf16[16,7424]{1,0:T(8,128)(2,1)S(1)} %get-tuple-element.24.refs_0_, bf16[16,7424]{1,0:T(8,128)(2,1)S(1)} %collective-permute-done.3.refs_1_, ...), custom_call_target="tpu_custom_call" | custom-call | flops 1195376640 | bytes 6070272 | tf_op jit(solution)/shard_map/pallas_call | solution.py:166
  38.7 0.3 collective-permute-start.13
  39.0 0.0 collective-permute-done.2.refs_0_
  39.0 1.8 %collective-permute-start.11 = (bf16[16,7424]{1,0:T(8,128)(2,1)S(1)}, bf16[16,7424]{1,0:T(8,128)(2,1)S(1)}, u32[]{:S(2)}, u32[]{:S(2)}) collective-permute-start(bf16[16,7424]{1,0:T(8,128)(2,1)S(1)} %collective-permute-done.2.refs_0_), channel_id=1, source_target_pairs={{0,4},{2,6},{4,8},{6,10},{8,12},{10,14},{12,13},{14,15},{13,9},{15... | collective-permute-start | bytes 712712 | tf_op jit(solution)/shard_map/ahead_A4/ppermute | solution.py:292
  40.8 2.3 %collective-permute-done.14.refs_1_ = bf16[16,7424]{1,0:T(8,128)(2,1)S(1)} collective-permute-done((bf16[16,7424]{1,0:T(8,128)(2,1)S(1)}, bf16[16,7424]{1,0:T(8,128)(2,1)S(1)}, u32[]{:S(2)}, u32[]{:S(2)}) %collective-permute-start.14) | collective-permute-done | bytes 237600 | tf_op jit(solution)/shard_map/behind_A3/ppermute | solution.py:292
  43.0 0.3 collective-permute-done.15.refs_2_
  43.4 3.8 %shard_map.57 = (f32[64,128]{1,0:T(8,128)S(1)}, f32[64,128]{1,0:T(8,128)S(1)}, f32[64,128]{1,0:T(8,128)S(1)}) custom-call(s32[4]{0:T(128)S(1)} %pad_add_fusion.spot, bf16[16,7424]{1,0:T(8,128)(2,1)S(1)} %collective-permute-done.2.refs_0_, bf16[16,7424]{1,0:T(8,128)(2,1)S(1)} %collective-permute-done.14.refs_1_, ...), custom_call_target="tpu_custom_call" | custom-call | flops 956301312 | bytes 4669440 | tf_op jit(solution)/shard_map/pallas_call | solution.py:166
  47.1 0.6 collective-permute-done.13.refs_1_
  47.8 3.4 %shard_map.58 = (f32[2,256,128]{2,1,0:T(8,128)S(1)}, f32[256,128]{1,0:T(8,128)S(1)}) custom-call(s32[4]{0:T(128)S(1)} %pad_add_fusion.spot, bf16[16,7424]{1,0:T(8,128)(2,1)S(1)} %collective-permute-done.11.refs_0_, bf16[16,7424]{1,0:T(8,128)(2,1)S(1)} %collective-permute-done.13.refs_1_, f32[1,7296]{1,0:T(1,128)S(1)} %broadcast_in_dim.3.refs_10_.refs_4_.refs_2_, ...), custom_call_target="tpu_custom_call" | custom-call | flops 956301312 | bytes 4202496 | tf_op jit(solution)/shard_map/pallas_call | solution.py:166
  51.2 0.1 collective-permute-start.16
  51.2 1.5 %collective-permute-done.16.mate = f32[2,256,128]{2,1,0:T(8,128)S(1)} collective-permute-done((f32[2,256,128]{2,1,0:T(8,128)S(1)}, f32[2,256,128]{2,1,0:T(8,128)S(1)}, u32[]{:S(2)}, u32[]{:S(2)}) %collective-permute-start.16) | collective-permute-done | bytes 262176 | tf_op jit(solution)/shard_map/ppermute | solution.py:351
  52.8 0.9 %shard_map.59 = (f32[128,128]{1,0:T(8,128)S(1)}, f32[8,128]{1,0:T(8,128)S(1)}, f32[136,128]{1,0:T(8,128)S(1)}) custom-call(s32[4]{0:T(128)S(1)} %pad_add_fusion.spot, f32[2,256,128]{2,1,0:T(8,128)S(1)} %get-tuple-element.36.partial, f32[2,256,128]{2,1,0:T(8,128)S(1)} %collective-permute-done.16.mate, f32[256,128]{1,0:T(8,128)S(1)} %get-tuple-element.37.facts), custom_call_target="tpu_custom_call" | custom-call | tf_op jit(solution)/shard_map/pallas_call | solution.py:352
  53.7 1.7 %collective-permute-start.17 = (f32[136,128]{1,0:T(8,128)S(1)}, f32[136,128]{1,0:T(8,128)S(1)}, u32[]{:S(2)}, u32[]{:S(2)}) collective-permute-start(f32[136,128]{1,0:T(8,128)S(1)} %get-tuple-element.39), channel_id=1, source_target_pairs={{0,1},{1,0},{2,3},{3,2},{4,5},{5,4},{6,7},{7,6},{8,9},{9,8},{10,11... | collective-permute-start | bytes 208904 | tf_op jit(solution)/shard_map/ppermute | solution.py:363
  55.4 2.7 %collective-permute-done.17.across = f32[136,128]{1,0:T(8,128)S(1)} collective-permute-done((f32[136,128]{1,0:T(8,128)S(1)}, f32[136,128]{1,0:T(8,128)S(1)}, u32[]{:S(2)}, u32[]{:S(2)}) %collective-permute-start.17) | collective-permute-done | bytes 69664 | tf_op jit(solution)/shard_map/ppermute | solution.py:363
  58.1 1.8 %collective-permute-start.18 = (f32[8,128]{1,0:T(8,128)S(1)}, f32[8,128]{1,0:T(8,128)S(1)}, u32[]{:S(2)}, u32[]{:S(2)}) collective-permute-start(f32[8,128]{1,0:T(8,128)S(1)} %select_maximum_fusion.pair.refs_0_), channel_id=1, source_target_pairs={{0,4},{2,6},{4,8},{6,10},{8,12},{10,14},{12,0},{14,2},{1,5},{3,7},... | collective-permute-start | bytes 12296 | tf_op jit(solution)/shard_map/ppermute | solution.py:370
  59.9 2.6 %collective-permute-start.19 = (f32[8,128]{1,0:T(8,128)S(1)}, f32[8,128]{1,0:T(8,128)S(1)}, u32[]{:S(2)}, u32[]{:S(2)}) collective-permute-start(f32[8,128]{1,0:T(8,128)S(1)} %select_maximum_fusion.pair.refs_0_), channel_id=1, source_target_pairs={{0,8},{2,10},{4,12},{6,14},{8,0},{10,2},{12,4},{14,6},{1,9},{3,11}... | collective-permute-start | bytes 12296 | tf_op jit(solution)/shard_map/ppermute | solution.py:370
  62.4 1.3 %collective-permute-start.20 = (f32[8,128]{1,0:T(8,128)S(1)}, f32[8,128]{1,0:T(8,128)S(1)}, u32[]{:S(2)}, u32[]{:S(2)}) collective-permute-start(f32[8,128]{1,0:T(8,128)S(1)} %select_maximum_fusion.pair.refs_0_), channel_id=1, source_target_pairs={{0,12},{2,14},{4,0},{6,2},{8,4},{10,6},{12,8},{14,10},{1,13},{3,15... | collective-permute-start | bytes 12296 | tf_op jit(solution)/shard_map/ppermute | solution.py:370
  63.8 1.1 %shard_map.60 = (f32[128,256]{1,0:T(8,128)S(1)}, f32[128,128]{1,0:T(8,128)S(1)}) custom-call(s32[4]{0:T(128)S(1)} %pad_add_fusion.spot, f32[128,128]{1,0:T(8,128)S(1)} %get-tuple-element.40.mine, f32[136,128]{1,0:T(8,128)S(1)} %collective-permute-done.17.across, f32[8,128]{1,0:T(8,128)S(1)} %select_maximum_fusion.pair.refs_0_, ...), custom_call_target="tpu_custom_call" | custom-call | tf_op jit(solution)/shard_map/pallas_call | solution.py:373
  64.9 1.1 %collective-permute-done.20.refs_3_ = f32[8,128]{1,0:T(8,128)S(1)} collective-permute-done((f32[8,128]{1,0:T(8,128)S(1)}, f32[8,128]{1,0:T(8,128)S(1)}, u32[]{:S(2)}, u32[]{:S(2)}) %collective-permute-start.20) | collective-permute-done | bytes 4128 | tf_op jit(solution)/shard_map/ppermute | solution.py:370
  66.0 0.8 %shard_map.61 = f32[128,256]{1,0:T(8,128)} custom-call(f32[8,128]{1,0:T(8,128)S(1)} %select_maximum_fusion.pair.refs_0_, f32[8,128]{1,0:T(8,128)S(1)} %collective-permute-done.18.refs_1_, f32[8,128]{1,0:T(8,128)S(1)} %collective-permute-done.19.refs_2_, f32[8,128]{1,0:T(8,128)S(1)} %collective-permute-done.20.refs_3_, ...), custom_call_target="tpu_custom_call" | custom-call | tf_op jit(solution)/shard_map/pallas_call | solution.py:383
  (14 shorter events, 0.1 us)
Async XLA Ops:
  1.2 0.7 %copy-start = (s32[1,16,4]{1,2,0:T(4,128)S(1)}, s32[1,16,4]{1,2,0:T(4,128)}, u32[]{:S(2)}) copy-start(s32[1,16,4]{1,2,0:T(4,128)} %param.7) | copy-start | bytes 772
  1.9 0.7 copy-start.1
  3.1 3.2 %collective-permute-start.3 = (bf16[16,7424]{1,0:T(8,128)(2,1)S(1)}, bf16[16,7424]{1,0:T(8,128)(2,1)S(1)}, u32[]{:S(2)}, u32[]{:S(2)}) collective-permute-start(bf16[16,7424]{1,0:T(8,128)(2,1)S(1)} %get-tuple-element.25), channel_id=1, source_target_pairs={{0,2},{2,0},{4,6},{6,4},{8,10},{10,8},{12,14},{14,12},{1,3},{3,1},... | collective-permute-start | bytes 712712 | tf_op jit(solution)/shard_map/mate_rows/ppermute | solution.py:308
  3.6 9.2 %collective-permute-start = (bf16[16,7424]{1,0:T(8,128)(2,1)S(1)}, bf16[16,7424]{1,0:T(8,128)(2,1)S(1)}, u32[]{:S(2)}, u32[]{:S(2)}) collective-permute-start(bf16[16,7424]{1,0:T(8,128)(2,1)S(1)} %get-tuple-element.24.refs_0_), channel_id=1, source_target_pairs={{0,4},{2,6},{4,8},{6,10},{8,12},{10,14},{12,13},{14,15},{13,9},{15... | collective-permute-start | bytes 712712 | tf_op jit(solution)/shard_map/ahead_A1/ppermute | solution.py:292
  6.3 8.6 %collective-permute-start.4 = (bf16[16,7424]{1,0:T(8,128)(2,1)S(1)}, bf16[16,7424]{1,0:T(8,128)(2,1)S(1)}, u32[]{:S(2)}, u32[]{:S(2)}) collective-permute-start(bf16[16,7424]{1,0:T(8,128)(2,1)S(1)} %get-tuple-element.24.refs_0_), channel_id=1, source_target_pairs={{0,1},{2,3},{4,0},{6,2},{8,4},{10,6},{12,8},{14,10},{13,12},{15,14... | collective-permute-start | bytes 712712 | tf_op jit(solution)/shard_map/behind_A1/ppermute | solution.py:292
  6.3 11.6 %collective-permute-start.5 = (bf16[16,7424]{1,0:T(8,128)(2,1)S(1)}, bf16[16,7424]{1,0:T(8,128)(2,1)S(1)}, u32[]{:S(2)}, u32[]{:S(2)}) collective-permute-start(bf16[16,7424]{1,0:T(8,128)(2,1)S(1)} %collective-permute-done.3.refs_1_), channel_id=1, source_target_pairs={{0,4},{2,6},{4,8},{6,10},{8,12},{10,14},{12,13},{14,15},{13,9},{15... | collective-permute-start | bytes 712712 | tf_op jit(solution)/shard_map/ahead_B1/ppermute | solution.py:292
  8.3 11.7 %collective-permute-start.6 = (bf16[16,7424]{1,0:T(8,128)(2,1)S(1)}, bf16[16,7424]{1,0:T(8,128)(2,1)S(1)}, u32[]{:S(2)}, u32[]{:S(2)}) collective-permute-start(bf16[16,7424]{1,0:T(8,128)(2,1)S(1)} %collective-permute-done.3.refs_1_), channel_id=1, source_target_pairs={{0,1},{2,3},{4,0},{6,2},{8,4},{10,6},{12,8},{14,10},{13,12},{15,14... | collective-permute-start | bytes 712712 | tf_op jit(solution)/shard_map/behind_B1/ppermute | solution.py:292
  10.7 20.7 %copy-start.2 = (f32[7296]{0:T(1024)S(1)}, f32[7296]{0:T(1024)}, u32[]{:S(2)}) copy-start(f32[7296]{0:T(1024)} %param.8) | copy-start | bytes 87556
  12.8 10.2 %collective-permute-start.1 = (bf16[16,7424]{1,0:T(8,128)(2,1)S(1)}, bf16[16,7424]{1,0:T(8,128)(2,1)S(1)}, u32[]{:S(2)}, u32[]{:S(2)}) collective-permute-start(bf16[16,7424]{1,0:T(8,128)(2,1)S(1)} %collective-permute-done.refs_2_), channel_id=1, source_target_pairs={{0,4},{2,6},{4,8},{6,10},{8,12},{10,14},{12,13},{14,15},{13,9},{15... | collective-permute-start | bytes 712712 | tf_op jit(solution)/shard_map/ahead_A2/ppermute | solution.py:292
  14.9 10.2 %collective-permute-start.7 = (bf16[16,7424]{1,0:T(8,128)(2,1)S(1)}, bf16[16,7424]{1,0:T(8,128)(2,1)S(1)}, u32[]{:S(2)}, u32[]{:S(2)}) collective-permute-start(bf16[16,7424]{1,0:T(8,128)(2,1)S(1)} %collective-permute-done.4.refs_3_), channel_id=1, source_target_pairs={{0,1},{2,3},{4,0},{6,2},{8,4},{10,6},{12,8},{14,10},{13,12},{15,14... | collective-permute-start | bytes 712712 | tf_op jit(solution)/shard_map/behind_A2/ppermute | solution.py:292
  17.9 9.9 %collective-permute-start.8 = (bf16[16,7424]{1,0:T(8,128)(2,1)S(1)}, bf16[16,7424]{1,0:T(8,128)(2,1)S(1)}, u32[]{:S(2)}, u32[]{:S(2)}) collective-permute-start(bf16[16,7424]{1,0:T(8,128)(2,1)S(1)} %collective-permute-done.5.refs_4_), channel_id=1, source_target_pairs={{0,4},{2,6},{4,8},{6,10},{8,12},{10,14},{12,13},{14,15},{13,9},{15... | collective-permute-start | bytes 712712 | tf_op jit(solution)/shard_map/ahead_B2/ppermute | solution.py:292
  20.0 9.4 %collective-permute-start.9 = (bf16[16,7424]{1,0:T(8,128)(2,1)S(1)}, bf16[16,7424]{1,0:T(8,128)(2,1)S(1)}, u32[]{:S(2)}, u32[]{:S(2)}) collective-permute-start(bf16[16,7424]{1,0:T(8,128)(2,1)S(1)} %collective-permute-done.6.refs_5_), channel_id=1, source_target_pairs={{0,1},{2,3},{4,0},{6,2},{8,4},{10,6},{12,8},{14,10},{13,12},{15,14... | collective-permute-start | bytes 712712 | tf_op jit(solution)/shard_map/behind_B2/ppermute | solution.py:292
  29.4 4.1 %collective-permute-start.10 = (bf16[128,7296]{1,0:T(8,128)(2,1)S(1)}, bf16[128,7296]{1,0:T(8,128)(2,1)S(1)}, u32[]{:S(2)}, u32[]{:S(2)}) collective-permute-start(bf16[128,7296]{1,0:T(8,128)(2,1)S(1)} %dynamic-slice_bitcast_fusion), channel_id=1, source_target_pairs={{0,2},{2,0},{4,6},{6,4},{8,10},{10,8},{12,14},{14,12},{1,3},{3,1},... | collective-permute-start | bytes 5603336 | tf_op jit(solution)/shard_map/mate_panel/ppermute | solution.py:341
  29.4 9.3 %collective-permute-start.12 = (bf16[16,7424]{1,0:T(8,128)(2,1)S(1)}, bf16[16,7424]{1,0:T(8,128)(2,1)S(1)}, u32[]{:S(2)}, u32[]{:S(2)}) collective-permute-start(bf16[16,7424]{1,0:T(8,128)(2,1)S(1)} %collective-permute-done.9.refs_9_), channel_id=1, source_target_pairs={{0,1},{2,3},{4,0},{6,2},{8,4},{10,6},{12,8},{14,10},{13,12},{15,14... | collective-permute-start | bytes 712712 | tf_op jit(solution)/shard_map/behind_B3/ppermute | solution.py:292
  29.7 9.4 %collective-permute-start.2 = (bf16[16,7424]{1,0:T(8,128)(2,1)S(1)}, bf16[16,7424]{1,0:T(8,128)(2,1)S(1)}, u32[]{:S(2)}, u32[]{:S(2)}) collective-permute-start(bf16[16,7424]{1,0:T(8,128)(2,1)S(1)} %collective-permute-done.1.refs_6_), channel_id=1, source_target_pairs={{0,4},{2,6},{4,8},{6,10},{8,12},{10,14},{12,13},{14,15},{13,9},{15... | collective-permute-start | bytes 712712 | tf_op jit(solution)/shard_map/ahead_A3/ppermute | solution.py:292
  31.4 11.6 %collective-permute-start.14 = (bf16[16,7424]{1,0:T(8,128)(2,1)S(1)}, bf16[16,7424]{1,0:T(8,128)(2,1)S(1)}, u32[]{:S(2)}, u32[]{:S(2)}) collective-permute-start(bf16[16,7424]{1,0:T(8,128)(2,1)S(1)} %collective-permute-done.7.refs_7_), channel_id=1, source_target_pairs={{0,1},{2,3},{4,0},{6,2},{8,4},{10,6},{12,8},{14,10},{13,12},{15,14... | collective-permute-start | bytes 712712 | tf_op jit(solution)/shard_map/behind_A3/ppermute | solution.py:292
  31.8 11.6 %collective-permute-start.15 = (bf16[16,7424]{1,0:T(8,128)(2,1)S(1)}, bf16[16,7424]{1,0:T(8,128)(2,1)S(1)}, u32[]{:S(2)}, u32[]{:S(2)}) collective-permute-start(bf16[16,7424]{1,0:T(8,128)(2,1)S(1)} %collective-permute-done.8.refs_8_), channel_id=1, source_target_pairs={{0,4},{2,6},{4,8},{6,10},{8,12},{10,14},{12,13},{14,15},{13,9},{15... | collective-permute-start | bytes 712712 | tf_op jit(solution)/shard_map/ahead_B3/ppermute | solution.py:292
  38.7 9.1 %collective-permute-start.13 = (bf16[16,7424]{1,0:T(8,128)(2,1)S(1)}, bf16[16,7424]{1,0:T(8,128)(2,1)S(1)}, u32[]{:S(2)}, u32[]{:S(2)}) collective-permute-start(bf16[16,7424]{1,0:T(8,128)(2,1)S(1)} %collective-permute-done.12.refs_3_), channel_id=1, source_target_pairs={{0,1},{2,3},{4,0},{6,2},{8,4},{10,6},{12,8},{14,10},{13,12},{15,14... | collective-permute-start | bytes 712712 | tf_op jit(solution)/shard_map/behind_B4/ppermute | solution.py:292
  39.0 8.7 %collective-permute-start.11 = (bf16[16,7424]{1,0:T(8,128)(2,1)S(1)}, bf16[16,7424]{1,0:T(8,128)(2,1)S(1)}, u32[]{:S(2)}, u32[]{:S(2)}) collective-permute-start(bf16[16,7424]{1,0:T(8,128)(2,1)S(1)} %collective-permute-done.2.refs_0_), channel_id=1, source_target_pairs={{0,4},{2,6},{4,8},{6,10},{8,12},{10,14},{12,13},{14,15},{13,9},{15... | collective-permute-start | bytes 712712 | tf_op jit(solution)/shard_map/ahead_A4/ppermute | solution.py:292
  51.2 1.6 %collective-permute-start.16 = (f32[2,256,128]{2,1,0:T(8,128)S(1)}, f32[2,256,128]{2,1,0:T(8,128)S(1)}, u32[]{:S(2)}, u32[]{:S(2)}) collective-permute-start(f32[2,256,128]{2,1,0:T(8,128)S(1)} %get-tuple-element.36.partial), channel_id=1, source_target_pairs={{0,2},{2,0},{4,6},{6,4},{8,10},{10,8},{12,14},{14,12},{1,3},{3,1},... | collective-permute-start | bytes 786440 | tf_op jit(solution)/shard_map/ppermute | solution.py:351
  53.7 4.3 %collective-permute-start.17 = (f32[136,128]{1,0:T(8,128)S(1)}, f32[136,128]{1,0:T(8,128)S(1)}, u32[]{:S(2)}, u32[]{:S(2)}) collective-permute-start(f32[136,128]{1,0:T(8,128)S(1)} %get-tuple-element.39), channel_id=1, source_target_pairs={{0,1},{1,0},{2,3},{3,2},{4,5},{5,4},{6,7},{7,6},{8,9},{9,8},{10,11... | collective-permute-start | bytes 208904 | tf_op jit(solution)/shard_map/ppermute | solution.py:363
  58.1 6.8 %collective-permute-start.18 = (f32[8,128]{1,0:T(8,128)S(1)}, f32[8,128]{1,0:T(8,128)S(1)}, u32[]{:S(2)}, u32[]{:S(2)}) collective-permute-start(f32[8,128]{1,0:T(8,128)S(1)} %select_maximum_fusion.pair.refs_0_), channel_id=1, source_target_pairs={{0,4},{2,6},{4,8},{6,10},{8,12},{10,14},{12,0},{14,2},{1,5},{3,7},... | collective-permute-start | bytes 12296 | tf_op jit(solution)/shard_map/ppermute | solution.py:370
  59.9 5.0 %collective-permute-start.19 = (f32[8,128]{1,0:T(8,128)S(1)}, f32[8,128]{1,0:T(8,128)S(1)}, u32[]{:S(2)}, u32[]{:S(2)}) collective-permute-start(f32[8,128]{1,0:T(8,128)S(1)} %select_maximum_fusion.pair.refs_0_), channel_id=1, source_target_pairs={{0,8},{2,10},{4,12},{6,14},{8,0},{10,2},{12,4},{14,6},{1,9},{3,11}... | collective-permute-start | bytes 12296 | tf_op jit(solution)/shard_map/ppermute | solution.py:370
  62.4 3.6 %collective-permute-start.20 = (f32[8,128]{1,0:T(8,128)S(1)}, f32[8,128]{1,0:T(8,128)S(1)}, u32[]{:S(2)}, u32[]{:S(2)}) collective-permute-start(f32[8,128]{1,0:T(8,128)S(1)} %select_maximum_fusion.pair.refs_0_), channel_id=1, source_target_pairs={{0,12},{2,14},{4,0},{6,2},{8,4},{10,6},{12,8},{14,10},{1,13},{3,15... | collective-permute-start | bytes 12296 | tf_op jit(solution)/shard_map/ppermute | solution.py:370

commit v7 on v6

--- a/solution.py
+++ b/solution.py
@@ -39,15 +39,24 @@
     )
 
 
-def row_kernel(spot, planes, defocus, lists, kept, given, facts):
+def row_kernel(spot, planes, defocus, lists, kept, given, facts, focus, named, sems):
     core = spot[2]
     columns = planes.shape[2]
     count = defocus.shape[1]
+    fetches = [
+        pltpu.make_async_copy(defocus, focus, sems.at[0]),
+        pltpu.make_async_copy(lists, named, sems.at[1]),
+    ]
+    for fetch in fetches:
+        fetch.start()
     facts[...] = jnp.zeros_like(facts)
-    facts[0:1, :count] = defocus[...].astype(jnp.float32)
-    facts[1 : 1 + lists.shape[0], :count] = lists[...].astype(jnp.float32)
     for half, out in ((core, kept), (1 - core, given)):
         out[:, :columns] = planes[half]
+    for fetch in fetches:
+        fetch.wait()
+    facts[0:1, :count] = focus[...].astype(jnp.float32)
+    facts[1 : 1 + lists.shape[0], :count] = named[...].astype(jnp.float32)
+    for out in (kept, given):
         out[:, columns:] = facts[...].astype(out.dtype)
 
 
@@ -102,8 +111,8 @@
 
 def batch_kernel(n, segments, spot, *refs):
     rows = refs[:n]
-    noise, sides, mate_panel, own_out, mate_out, fact_out = refs[n : n + 6]
-    turn_sin, turn_cos, *sums = refs[n + 6 :]
+    noise, sides, mate_panel = refs[n : n + 3]
+    own_out, mate_out, fact_out, turn_sin, turn_cos, *sums = refs[n + 3 :]
     fact_out[...] = add_scores(
         rows, spot, noise, sides, mate_panel, turn_sin, turn_cos, sums, segments
     )
@@ -114,8 +123,9 @@
 def last_kernel(n, segments, orders, spot, *refs):
     rows = refs[:n]
     noise, sides, mate_panel = refs[n : n + 3]
-    earlier = refs[n + 3 : n + 3 + 3 * (len(orders) - 1)]
-    partial, facts, turn_sin, turn_cos, *sums = refs[n + 3 + len(earlier) :]
+    rest = refs[n + 3 :]
+    earlier, rest = rest[: 3 * (len(orders) - 1)], rest[3 * (len(orders) - 1) :]
+    partial, facts, turn_sin, turn_cos, *sums = rest
     last_facts = add_scores(
         rows, spot, noise, sides, mate_panel, turn_sin, turn_cos, sums, segments
     )
@@ -142,7 +152,7 @@
 
 def score_call(chunks, orders, earlier, spot, noise, sides, mate_panel):
     each = chunks[0].shape[0]
-    orientations, columns = mate_panel.shape
+    orientations, columns = sides.shape[1:]
     whole = columns // LANES
     segments = next(s for s in (3, 2, 4, 5, 6, 7, 1) if whole % s == 0)
     n = len(chunks)
@@ -287,8 +297,8 @@
         level = ring - 1 - place if far else place
         return (2 * level + core) * 2 + int(far)
 
-    def forward(values, step):
-        pairs = [(joint(p, c), joint(p + step, c)) for p in range(ring) for c in range(2)]
+    def forward(values, step, cross=0):
+        pairs = [(joint(p, c), joint(p + step, c ^ cross)) for p in range(ring) for c in range(2)]
         return lax.ppermute(values, ("orient", "cls"), pairs)
 
     vmem = pl.BlockSpec(memory_space=pltpu.VMEM)
@@ -298,24 +308,31 @@
     row_shape = jax.ShapeDtypeStruct((per_device, columns + LANES), jnp.bfloat16)
     kept, given = pl.pallas_call(
         row_kernel,
-        in_specs=[smem] + [vmem] * 3,
+        in_specs=[smem, vmem] + [pl.BlockSpec(memory_space=pl.ANY)] * 2,
         out_specs=[vmem] * 2,
         out_shape=[row_shape] * 2,
-        scratch_shapes=[pltpu.VMEM((per_device, LANES), jnp.float32)],
+        scratch_shapes=[
+            pltpu.VMEM((per_device, LANES), jnp.float32),
+            pltpu.VMEM(defocus.shape, defocus.dtype),
+            pltpu.VMEM((local_search, per_device), block_ids.dtype),
+            pltpu.SemaphoreType.DMA((2,)),
+        ],
         compiler_params=params,
     )(spot, planes, defocus, jnp.transpose(block_ids[0]))
     with jax.named_scope("mate_rows"):
         got = lax.ppermute(given, "orient", mate_pairs)
 
-    _, panels = lax.optimization_barrier((got, panels))
     sides = lax.optimization_barrier(jnp.transpose(panels[0, 0], (1, 0, 2)))
     given_panel = lax.dynamic_index_in_dim(sides, 1 - core, 0, keepdims=False)
+    with jax.named_scope("mate_panel"):
+        mate_panel = lax.ppermute(given_panel, "orient", mate_pairs)
 
     noise = noise_weight[None, :]
     waiting = [((0, False), kept), ((0, True), got)]
-    ahead = {False: kept, True: got}
-    behind = {False: kept, True: got}
+    ahead = {False: kept, True: given}
+    behind = {False: kept, True: given}
     orders, earlier, late = [], [], []
+    score = lambda c: score_call(c, None, None, spot, noise, sides, mate_panel)
     for step in range(1, chips + 1):
         if step == chips and step > 2:
             orders.append([key for key, _ in waiting])
@@ -328,18 +345,13 @@
         late = []
         for crossed in (False, True):
             if step < chips or not crossed:
-                with jax.named_scope(f"ahead_{'BA'[not crossed]}{step}"):
-                    ahead[crossed] = forward(ahead[crossed], 1)
+                with jax.named_scope("rows_ahead"):
+                    ahead[crossed] = forward(ahead[crossed], 1, int(crossed and step == 1))
                 late.append(((-step, crossed), ahead[crossed]))
             if step < chips or crossed:
-                with jax.named_scope(f"behind_{'BA'[not crossed]}{step}"):
-                    behind[crossed] = forward(behind[crossed], -1)
+                with jax.named_scope("rows_behind"):
+                    behind[crossed] = forward(behind[crossed], -1, int(crossed and step == 1))
                 late.append(((step, crossed), behind[crossed]))
-        if step == 2:
-            given_panel = lax.optimization_barrier((given_panel, *[v for _, v in late]))[0]
-            with jax.named_scope("mate_panel"):
-                mate_panel = lax.ppermute(given_panel, "orient", mate_pairs)
-            score = lambda c: score_call(c, None, None, spot, noise, sides, mate_panel)
     orders.append([key for key, _ in waiting])
     earlier.append(score([c for _, c in waiting]))
     waiting = late

time: 67 us -> 71.4 us (1.066)
  local copies, waits for them, and re-layouts: 4.98 us -> 9.33 us
    unnamed x7 -> x12, local copies, waits for them, and re-layouts: 2.41 us -> 6.34 us
    squeeze x1, local copies, waits for them, and re-layouts: 0.12 us -> 2.97 us  [chip_shards(): given_panel = lax.dynamic_index_in_dim(sides, 1 - core, 0, keepdims=False)]
    optimization_barrier x1 -> x0, local copies, waits for them, and re-layouts: 2.42 us -> none  [chip_shards(): _, panels = lax.optimization_barrier((got, panels))]
    ppermute x14, waiting for transfers between devices: 17.7 us -> 18.5 us  [forward(): return lax.ppermute(values, ('orient', 'cls'), pairs)]
    ppermute x3, waiting for transfers between devices: 1.15 us -> 0.35 us  [chip_shards(): lax.ppermute(pair, 'orient', [(d, (d + 2 * s) % devices) for d in range(d...]
  transfers between devices with their start and end apart: 21 -> 21, of which waited for: 12 -> 9; matrix products, arithmetic and copies ran while one was open for 4% -> 0% of each run, Pallas kernels for 15% -> 15%
where the time goes in v7:
time: 71.4 us; the launch traced here: 71.2 us
  waiting for transfers between devices  23.1 us (32%)
  starting transfers between devices  22.9 us (32%)
  Pallas kernels  15.7 us (22%)
  local copies, waits for them, and re-layouts  9.33 us (13%)
    ppermute x14, waiting for transfers between devices, forward(): return lax.ppermute(values, ('orient', 'cls'), pairs)  18.5 us
    ppermute x14, starting transfers between devices, forward(): return lax.ppermute(values, ('orient', 'cls'), pairs)  14.9 us
    pallas_call x3, Pallas kernels, score_call(): pl.pallas_call(kernel, in_specs=[pl.BlockSpec(memory_space=pltpu.SMEM)] +...  12.3 us
    unnamed x12, local copies, waits for them, and re-layouts  6.34 us
    ppermute x3, starting transfers between devices, chip_shards(): lax.ppermute(pair, 'orient', [(d, (d + 2 * s) % devices) for d in range(d...  5.31 us
    squeeze x1, local copies, waits for them, and re-layouts, chip_shards(): given_panel = lax.dynamic_index_in_dim(sides, 1 - core, 0, keepdims=False)  2.97 us
    ppermute x1, waiting for transfers between devices, chip_shards(): from_x = lax.ppermute(across, 'cls', x_pairs)  2.74 us
    ppermute x1, starting transfers between devices, chip_shards(): from_x = lax.ppermute(across, 'cls', x_pairs)  1.61 us
  transfers between devices with their start and end apart: 21, of which 9 were waited for; matrix products, arithmetic and copies ran while one was open for 0% of the time, Pallas kernels for 15%

profile of v7, /device:TPU:0, one launch (start us, length us, event | category | flops | bytes accessed | tf_op | source)
XLA Modules:
  0.0 71.2 jit_solution(16442078544103547869)
XLA Ops:
  0.0 4.2 %copy.10 = bf16[1,1,128,2,7296]{4,2,3,1,0:T(8,128)(2,1)} copy(bf16[1,1,128,2,7296]{4,3,2,1,0:T(2,128)(2,1)} %param.9) | data formatting | bytes 7471104 | tf_op args[4]
  4.2 3.0 %dynamic-slice_bitcast_fusion = bf16[128,7296]{1,0:T(8,128)(2,1)} fusion(bf16[2,128,7296]{2,1,0:T(8,128)(2,1)} %bitcast.20, s32[]{:T(128)S(6)} %select_n.21), kind=kLoop, calls=%fused_computation.1 | loop fusion | bytes 3735556 | tf_op jit(solution)/shard_map/jit(dynamic_index_in_dim)/squeeze | solution.py:326
  7.2 0.5 collective-permute-start.10
  7.7 0.1 pad_add_fusion.spot
  7.8 0.6 shard_map.55
  8.4 2.7 %collective-permute-start.6 = (bf16[16,7424]{1,0:T(8,128)(2,1)S(1)}, bf16[16,7424]{1,0:T(8,128)(2,1)S(1)}, u32[]{:S(2)}, u32[]{:S(2)}) collective-permute-start(bf16[16,7424]{1,0:T(8,128)(2,1)S(1)} %get-tuple-element.23), channel_id=1, source_target_pairs={{0,3},{2,1},{4,2},{6,0},{8,6},{10,4},{12,10},{14,8},{13,14},{15,12... | collective-permute-start | bytes 712712 | tf_op jit(solution)/shard_map/rows_behind/ppermute | solution.py:302
  11.1 1.6 %collective-permute-start.4 = (bf16[16,7424]{1,0:T(8,128)(2,1)S(1)}, bf16[16,7424]{1,0:T(8,128)(2,1)S(1)}, u32[]{:S(2)}, u32[]{:S(2)}) collective-permute-start(bf16[16,7424]{1,0:T(8,128)(2,1)S(1)} %get-tuple-element.22.refs_0_), channel_id=1, source_target_pairs={{0,1},{2,3},{4,0},{6,2},{8,4},{10,6},{12,8},{14,10},{13,12},{15,14... | collective-permute-start | bytes 712712 | tf_op jit(solution)/shard_map/rows_behind/ppermute | solution.py:302
  12.7 0.4 collective-permute-start
  13.1 0.0 collective-permute-start.5
  13.1 4.2 %collective-permute-done.6.refs_5_ = bf16[16,7424]{1,0:T(8,128)(2,1)S(1)} collective-permute-done((bf16[16,7424]{1,0:T(8,128)(2,1)S(1)}, bf16[16,7424]{1,0:T(8,128)(2,1)S(1)}, u32[]{:S(2)}, u32[]{:S(2)}) %collective-permute-start.6) | collective-permute-done | bytes 237600 | tf_op jit(solution)/shard_map/rows_behind/ppermute | solution.py:302
  17.3 0.5 collective-permute-start.3
  17.8 4.8 %collective-permute-done.4.refs_3_ = bf16[16,7424]{1,0:T(8,128)(2,1)S(1)} collective-permute-done((bf16[16,7424]{1,0:T(8,128)(2,1)S(1)}, bf16[16,7424]{1,0:T(8,128)(2,1)S(1)}, u32[]{:S(2)}, u32[]{:S(2)}) %collective-permute-start.4) | collective-permute-done | bytes 237600 | tf_op jit(solution)/shard_map/rows_behind/ppermute | solution.py:302
  22.6 1.5 %collective-permute-start.9 = (bf16[16,7424]{1,0:T(8,128)(2,1)S(1)}, bf16[16,7424]{1,0:T(8,128)(2,1)S(1)}, u32[]{:S(2)}, u32[]{:S(2)}) collective-permute-start(bf16[16,7424]{1,0:T(8,128)(2,1)S(1)} %collective-permute-done.6.refs_5_), channel_id=1, source_target_pairs={{0,1},{2,3},{4,0},{6,2},{8,4},{10,6},{12,8},{14,10},{13,12},{15,14... | collective-permute-start | bytes 712712 | tf_op jit(solution)/shard_map/rows_behind/ppermute | solution.py:302
  24.1 0.0 collective-permute-done.refs_2_
  24.1 0.5 collective-permute-start.1
  24.6 1.6 %collective-permute-start.7 = (bf16[16,7424]{1,0:T(8,128)(2,1)S(1)}, bf16[16,7424]{1,0:T(8,128)(2,1)S(1)}, u32[]{:S(2)}, u32[]{:S(2)}) collective-permute-start(bf16[16,7424]{1,0:T(8,128)(2,1)S(1)} %collective-permute-done.4.refs_3_), channel_id=1, source_target_pairs={{0,1},{2,3},{4,0},{6,2},{8,4},{10,6},{12,8},{14,10},{13,12},{15,14... | collective-permute-start | bytes 712712 | tf_op jit(solution)/shard_map/rows_behind/ppermute | solution.py:302
  26.2 0.0 collective-permute-done.3.refs_1_
  26.2 0.5 collective-permute-start.8
  26.7 4.6 %collective-permute-done.9.refs_9_ = bf16[16,7424]{1,0:T(8,128)(2,1)S(1)} collective-permute-done((bf16[16,7424]{1,0:T(8,128)(2,1)S(1)}, bf16[16,7424]{1,0:T(8,128)(2,1)S(1)}, u32[]{:S(2)}, u32[]{:S(2)}) %collective-permute-start.9) | collective-permute-done | bytes 237600 | tf_op jit(solution)/shard_map/rows_behind/ppermute | solution.py:302
  31.3 1.6 %collective-permute-start.12 = (bf16[16,7424]{1,0:T(8,128)(2,1)S(1)}, bf16[16,7424]{1,0:T(8,128)(2,1)S(1)}, u32[]{:S(2)}, u32[]{:S(2)}) collective-permute-start(bf16[16,7424]{1,0:T(8,128)(2,1)S(1)} %collective-permute-done.9.refs_9_), channel_id=1, source_target_pairs={{0,1},{2,3},{4,0},{6,2},{8,4},{10,6},{12,8},{14,10},{13,12},{15,14... | collective-permute-start | bytes 712712 | tf_op jit(solution)/shard_map/rows_behind/ppermute | solution.py:302
  32.9 0.0 collective-permute-done.1.refs_6_
  32.9 0.5 collective-permute-start.2
  33.4 3.0 %collective-permute-done.7.refs_7_ = bf16[16,7424]{1,0:T(8,128)(2,1)S(1)} collective-permute-done((bf16[16,7424]{1,0:T(8,128)(2,1)S(1)}, bf16[16,7424]{1,0:T(8,128)(2,1)S(1)}, u32[]{:S(2)}, u32[]{:S(2)}) %collective-permute-start.7) | collective-permute-done | bytes 237600 | tf_op jit(solution)/shard_map/rows_behind/ppermute | solution.py:302
  36.4 1.6 %collective-permute-start.14 = (bf16[16,7424]{1,0:T(8,128)(2,1)S(1)}, bf16[16,7424]{1,0:T(8,128)(2,1)S(1)}, u32[]{:S(2)}, u32[]{:S(2)}) collective-permute-start(bf16[16,7424]{1,0:T(8,128)(2,1)S(1)} %collective-permute-done.7.refs_7_), channel_id=1, source_target_pairs={{0,1},{2,3},{4,0},{6,2},{8,4},{10,6},{12,8},{14,10},{13,12},{15,14... | collective-permute-start | bytes 712712 | tf_op jit(solution)/shard_map/rows_behind/ppermute | solution.py:302
  38.0 0.0 collective-permute-done.8.refs_8_
  38.0 0.5 collective-permute-start.15
  38.4 2.1 %copy-done = bf16[1,1,128,2,7296]{4,2,3,1,0:T(8,128)(2,1)S(1)} copy-done((bf16[1,1,128,2,7296]{4,2,3,1,0:T(8,128)(2,1)S(1)}, bf16[1,1,128,2,7296]{4,2,3,1,0:T(8,128)(2,1)}, u32[]{:S(2)}) %copy-start) | copy-done | bytes 3735576
  40.5 5.1 %shard_map.56 = (f32[160,128]{1,0:T(8,128)S(1)}, f32[160,128]{1,0:T(8,128)S(1)}, f32[160,128]{1,0:T(8,128)S(1)}) custom-call(s32[4]{0:T(128)S(1)} %pad_add_fusion.spot, bf16[16,7424]{1,0:T(8,128)(2,1)S(1)} %get-tuple-element.22.refs_0_, bf16[16,7424]{1,0:T(8,128)(2,1)S(1)} %collective-permute-done.3.refs_1_, ...), custom_call_target="tpu_custom_call" | custom-call | flops 1195376640 | bytes 6070272 | tf_op jit(solution)/shard_map/pallas_call | solution.py:176
  45.6 0.0 collective-permute-done.12.refs_3_
  45.6 1.6 %collective-permute-start.13 = (bf16[16,7424]{1,0:T(8,128)(2,1)S(1)}, bf16[16,7424]{1,0:T(8,128)(2,1)S(1)}, u32[]{:S(2)}, u32[]{:S(2)}) collective-permute-start(bf16[16,7424]{1,0:T(8,128)(2,1)S(1)} %collective-permute-done.12.refs_3_), channel_id=1, source_target_pairs={{0,1},{2,3},{4,0},{6,2},{8,4},{10,6},{12,8},{14,10},{13,12},{15,14... | collective-permute-start | bytes 712712 | tf_op jit(solution)/shard_map/rows_behind/ppermute | solution.py:302
  47.3 0.5 collective-permute-start.11
  47.7 3.8 %shard_map.57 = (f32[64,128]{1,0:T(8,128)S(1)}, f32[64,128]{1,0:T(8,128)S(1)}, f32[64,128]{1,0:T(8,128)S(1)}) custom-call(s32[4]{0:T(128)S(1)} %pad_add_fusion.spot, bf16[16,7424]{1,0:T(8,128)(2,1)S(1)} %collective-permute-done.2.refs_0_, bf16[16,7424]{1,0:T(8,128)(2,1)S(1)} %collective-permute-done.14.refs_1_, ...), custom_call_target="tpu_custom_call" | custom-call | flops 956301312 | bytes 4669440 | tf_op jit(solution)/shard_map/pallas_call | solution.py:176
  51.5 0.3 collective-permute-done.13.refs_1_
  51.8 1.6 %collective-permute-done.11.refs_0_ = bf16[16,7424]{1,0:T(8,128)(2,1)S(1)} collective-permute-done((bf16[16,7424]{1,0:T(8,128)(2,1)S(1)}, bf16[16,7424]{1,0:T(8,128)(2,1)S(1)}, u32[]{:S(2)}, u32[]{:S(2)}) %collective-permute-start.11) | collective-permute-done | bytes 237600 | tf_op jit(solution)/shard_map/rows_ahead/ppermute | solution.py:302
  53.4 3.4 %shard_map.58 = (f32[2,256,128]{2,1,0:T(8,128)S(1)}, f32[256,128]{1,0:T(8,128)S(1)}) custom-call(s32[4]{0:T(128)S(1)} %pad_add_fusion.spot, bf16[16,7424]{1,0:T(8,128)(2,1)S(1)} %collective-permute-done.11.refs_0_, bf16[16,7424]{1,0:T(8,128)(2,1)S(1)} %collective-permute-done.13.refs_1_, f32[1,7296]{1,0:T(1,128)S(1)} %broadcast_in_dim.3.refs_10_.refs_4_.refs_2_, ...), custom_call_target="tpu_custom_call" | custom-call | flops 956301312 | bytes 4202496 | tf_op jit(solution)/shard_map/pallas_call | solution.py:176
  56.8 0.1 collective-permute-start.16
  56.9 1.5 %collective-permute-done.16.mate = f32[2,256,128]{2,1,0:T(8,128)S(1)} collective-permute-done((f32[2,256,128]{2,1,0:T(8,128)S(1)}, f32[2,256,128]{2,1,0:T(8,128)S(1)}, u32[]{:S(2)}, u32[]{:S(2)}) %collective-permute-start.16) | collective-permute-done | bytes 262176 | tf_op jit(solution)/shard_map/ppermute | solution.py:363
  58.4 0.9 %shard_map.59 = (f32[128,128]{1,0:T(8,128)S(1)}, f32[8,128]{1,0:T(8,128)S(1)}, f32[136,128]{1,0:T(8,128)S(1)}) custom-call(s32[4]{0:T(128)S(1)} %pad_add_fusion.spot, f32[2,256,128]{2,1,0:T(8,128)S(1)} %get-tuple-element.32.partial, f32[2,256,128]{2,1,0:T(8,128)S(1)} %collective-permute-done.16.mate, f32[256,128]{1,0:T(8,128)S(1)} %get-tuple-element.33.facts), custom_call_target="tpu_custom_call" | custom-call | tf_op jit(solution)/shard_map/pallas_call | solution.py:364
  59.3 1.6 %collective-permute-start.17 = (f32[136,128]{1,0:T(8,128)S(1)}, f32[136,128]{1,0:T(8,128)S(1)}, u32[]{:S(2)}, u32[]{:S(2)}) collective-permute-start(f32[136,128]{1,0:T(8,128)S(1)} %get-tuple-element.35), channel_id=1, source_target_pairs={{0,1},{1,0},{2,3},{3,2},{4,5},{5,4},{6,7},{7,6},{8,9},{9,8},{10,11... | collective-permute-start | bytes 208904 | tf_op jit(solution)/shard_map/ppermute | solution.py:375
  60.9 2.7 %collective-permute-done.17.across = f32[136,128]{1,0:T(8,128)S(1)} collective-permute-done((f32[136,128]{1,0:T(8,128)S(1)}, f32[136,128]{1,0:T(8,128)S(1)}, u32[]{:S(2)}, u32[]{:S(2)}) %collective-permute-start.17) | collective-permute-done | bytes 69664 | tf_op jit(solution)/shard_map/ppermute | solution.py:375
  63.7 1.4 %collective-permute-start.18 = (f32[8,128]{1,0:T(8,128)S(1)}, f32[8,128]{1,0:T(8,128)S(1)}, u32[]{:S(2)}, u32[]{:S(2)}) collective-permute-start(f32[8,128]{1,0:T(8,128)S(1)} %select_maximum_fusion.pair.refs_0_), channel_id=1, source_target_pairs={{0,4},{2,6},{4,8},{6,10},{8,12},{10,14},{12,0},{14,2},{1,5},{3,7},... | collective-permute-start | bytes 12296 | tf_op jit(solution)/shard_map/ppermute | solution.py:382
  65.1 1.8 %collective-permute-start.19 = (f32[8,128]{1,0:T(8,128)S(1)}, f32[8,128]{1,0:T(8,128)S(1)}, u32[]{:S(2)}, u32[]{:S(2)}) collective-permute-start(f32[8,128]{1,0:T(8,128)S(1)} %select_maximum_fusion.pair.refs_0_), channel_id=1, source_target_pairs={{0,8},{2,10},{4,12},{6,14},{8,0},{10,2},{12,4},{14,6},{1,9},{3,11}... | collective-permute-start | bytes 12296 | tf_op jit(solution)/shard_map/ppermute | solution.py:382
  66.9 2.1 %collective-permute-start.20 = (f32[8,128]{1,0:T(8,128)S(1)}, f32[8,128]{1,0:T(8,128)S(1)}, u32[]{:S(2)}, u32[]{:S(2)}) collective-permute-start(f32[8,128]{1,0:T(8,128)S(1)} %select_maximum_fusion.pair.refs_0_), channel_id=1, source_target_pairs={{0,12},{2,14},{4,0},{6,2},{8,4},{10,6},{12,8},{14,10},{1,13},{3,15... | collective-permute-start | bytes 12296 | tf_op jit(solution)/shard_map/ppermute | solution.py:382
  69.0 1.1 %shard_map.60 = (f32[128,256]{1,0:T(8,128)S(1)}, f32[128,128]{1,0:T(8,128)S(1)}) custom-call(s32[4]{0:T(128)S(1)} %pad_add_fusion.spot, f32[128,128]{1,0:T(8,128)S(1)} %get-tuple-element.36.mine, f32[136,128]{1,0:T(8,128)S(1)} %collective-permute-done.17.across, f32[8,128]{1,0:T(8,128)S(1)} %select_maximum_fusion.pair.refs_0_, ...), custom_call_target="tpu_custom_call" | custom-call | tf_op jit(solution)/shard_map/pallas_call | solution.py:385
  70.1 0.0 collective-permute-done.18.refs_1_
  70.1 0.0 collective-permute-done.19.refs_2_
  70.1 0.3 collective-permute-done.20.refs_3_
  70.5 0.8 %shard_map.61 = f32[128,256]{1,0:T(8,128)} custom-call(f32[8,128]{1,0:T(8,128)S(1)} %select_maximum_fusion.pair.refs_0_, f32[8,128]{1,0:T(8,128)S(1)} %collective-permute-done.18.refs_1_, f32[8,128]{1,0:T(8,128)S(1)} %collective-permute-done.19.refs_2_, f32[8,128]{1,0:T(8,128)S(1)} %collective-permute-done.20.refs_3_, ...), custom_call_target="tpu_custom_call" | custom-call | tf_op jit(solution)/shard_map/pallas_call | solution.py:395
  (18 shorter events, 0.1 us)
Async XLA Ops:
  4.2 3.4 %copy-start.3 = (bf16[1,16,2,7296]{3,2,1,0:T(2,128)(2,1)S(1)}, bf16[1,16,2,7296]{3,2,1,0:T(2,128)(2,1)}, u32[]{:S(2)}) copy-start(bf16[1,16,2,7296]{3,2,1,0:T(2,128)(2,1)} %param.5) | copy-start | bytes 1400836
  4.2 3.6 %copy-start.1 = (s32[1,16,4]{1,2,0:T(4,128)S(1)}, s32[1,16,4]{1,2,0:T(4,128)}, u32[]{:S(2)}) copy-start(s32[1,16,4]{1,2,0:T(4,128)} %param.7) | copy-start | bytes 772
  4.2 3.6 %copy-start.2 = (bf16[1,16]{1,0:T(2,128)(2,1)S(1)}, bf16[1,16]{1,0:T(2,128)(2,1)}, u32[]{:S(2)}) copy-start(bf16[1,16]{1,0:T(2,128)(2,1)} %defocus.1) | copy-start | bytes 100
  4.2 29.1 %copy-start.4 = (f32[7296]{0:T(1024)S(1)}, f32[7296]{0:T(1024)}, u32[]{:S(2)}) copy-start(f32[7296]{0:T(1024)} %param.8) | copy-start | bytes 87556
  7.2 31.2 %collective-permute-start.10 = (bf16[128,7296]{1,0:T(8,128)(2,1)}, bf16[128,7296]{1,0:T(8,128)(2,1)S(1)}, u32[]{:S(2)}, u32[]{:S(2)}) collective-permute-start(bf16[128,7296]{1,0:T(8,128)(2,1)} %dynamic-slice_bitcast_fusion), channel_id=1, source_target_pairs={{0,2},{2,0},{4,6},{6,4},{8,10},{10,8},{12,14},{14,12},{1,3},{3,1},... | collective-permute-start | bytes 5603336 | tf_op jit(solution)/shard_map/mate_panel/ppermute | solution.py:328
  8.4 8.9 %collective-permute-start.6 = (bf16[16,7424]{1,0:T(8,128)(2,1)S(1)}, bf16[16,7424]{1,0:T(8,128)(2,1)S(1)}, u32[]{:S(2)}, u32[]{:S(2)}) collective-permute-start(bf16[16,7424]{1,0:T(8,128)(2,1)S(1)} %get-tuple-element.23), channel_id=1, source_target_pairs={{0,3},{2,1},{4,2},{6,0},{8,6},{10,4},{12,10},{14,8},{13,14},{15,12... | collective-permute-start | bytes 712712 | tf_op jit(solution)/shard_map/rows_behind/ppermute | solution.py:302
  11.1 11.5 %collective-permute-start.4 = (bf16[16,7424]{1,0:T(8,128)(2,1)S(1)}, bf16[16,7424]{1,0:T(8,128)(2,1)S(1)}, u32[]{:S(2)}, u32[]{:S(2)}) collective-permute-start(bf16[16,7424]{1,0:T(8,128)(2,1)S(1)} %get-tuple-element.22.refs_0_), channel_id=1, source_target_pairs={{0,1},{2,3},{4,0},{6,2},{8,4},{10,6},{12,8},{14,10},{13,12},{15,14... | collective-permute-start | bytes 712712 | tf_op jit(solution)/shard_map/rows_behind/ppermute | solution.py:302
  12.7 11.5 %collective-permute-start = (bf16[16,7424]{1,0:T(8,128)(2,1)S(1)}, bf16[16,7424]{1,0:T(8,128)(2,1)S(1)}, u32[]{:S(2)}, u32[]{:S(2)}) collective-permute-start(bf16[16,7424]{1,0:T(8,128)(2,1)S(1)} %get-tuple-element.22.refs_0_), channel_id=1, source_target_pairs={{0,4},{2,6},{4,8},{6,10},{8,12},{10,14},{12,13},{14,15},{13,9},{15... | collective-permute-start | bytes 712712 | tf_op jit(solution)/shard_map/rows_ahead/ppermute | solution.py:302
  13.1 11.5 %collective-permute-start.5 = (bf16[16,7424]{1,0:T(8,128)(2,1)S(1)}, bf16[16,7424]{1,0:T(8,128)(2,1)S(1)}, u32[]{:S(2)}, u32[]{:S(2)}) collective-permute-start(bf16[16,7424]{1,0:T(8,128)(2,1)S(1)} %get-tuple-element.23), channel_id=1, source_target_pairs={{0,6},{2,4},{4,10},{6,8},{8,14},{10,12},{12,15},{14,13},{13,11},{1... | collective-permute-start | bytes 712712 | tf_op jit(solution)/shard_map/rows_ahead/ppermute | solution.py:302
  17.3 8.9 %collective-permute-start.3 = (bf16[16,7424]{1,0:T(8,128)(2,1)S(1)}, bf16[16,7424]{1,0:T(8,128)(2,1)S(1)}, u32[]{:S(2)}, u32[]{:S(2)}) collective-permute-start(bf16[16,7424]{1,0:T(8,128)(2,1)S(1)} %get-tuple-element.23), channel_id=1, source_target_pairs={{0,2},{2,0},{4,6},{6,4},{8,10},{10,8},{12,14},{14,12},{1,3},{3,1},... | collective-permute-start | bytes 712712 | tf_op jit(solution)/shard_map/mate_rows/ppermute | solution.py:323
  22.6 8.7 %collective-permute-start.9 = (bf16[16,7424]{1,0:T(8,128)(2,1)S(1)}, bf16[16,7424]{1,0:T(8,128)(2,1)S(1)}, u32[]{:S(2)}, u32[]{:S(2)}) collective-permute-start(bf16[16,7424]{1,0:T(8,128)(2,1)S(1)} %collective-permute-done.6.refs_5_), channel_id=1, source_target_pairs={{0,1},{2,3},{4,0},{6,2},{8,4},{10,6},{12,8},{14,10},{13,12},{15,14... | collective-permute-start | bytes 712712 | tf_op jit(solution)/shard_map/rows_behind/ppermute | solution.py:302
  24.1 8.7 %collective-permute-start.1 = (bf16[16,7424]{1,0:T(8,128)(2,1)S(1)}, bf16[16,7424]{1,0:T(8,128)(2,1)S(1)}, u32[]{:S(2)}, u32[]{:S(2)}) collective-permute-start(bf16[16,7424]{1,0:T(8,128)(2,1)S(1)} %collective-permute-done.refs_2_), channel_id=1, source_target_pairs={{0,4},{2,6},{4,8},{6,10},{8,12},{10,14},{12,13},{14,15},{13,9},{15... | collective-permute-start | bytes 712712 | tf_op jit(solution)/shard_map/rows_ahead/ppermute | solution.py:302
  24.6 11.7 %collective-permute-start.7 = (bf16[16,7424]{1,0:T(8,128)(2,1)S(1)}, bf16[16,7424]{1,0:T(8,128)(2,1)S(1)}, u32[]{:S(2)}, u32[]{:S(2)}) collective-permute-start(bf16[16,7424]{1,0:T(8,128)(2,1)S(1)} %collective-permute-done.4.refs_3_), channel_id=1, source_target_pairs={{0,1},{2,3},{4,0},{6,2},{8,4},{10,6},{12,8},{14,10},{13,12},{15,14... | collective-permute-start | bytes 712712 | tf_op jit(solution)/shard_map/rows_behind/ppermute | solution.py:302
  26.2 11.8 %collective-permute-start.8 = (bf16[16,7424]{1,0:T(8,128)(2,1)S(1)}, bf16[16,7424]{1,0:T(8,128)(2,1)S(1)}, u32[]{:S(2)}, u32[]{:S(2)}) collective-permute-start(bf16[16,7424]{1,0:T(8,128)(2,1)S(1)} %collective-permute-done.5.refs_4_), channel_id=1, source_target_pairs={{0,4},{2,6},{4,8},{6,10},{8,12},{10,14},{12,13},{14,15},{13,9},{15... | collective-permute-start | bytes 712712 | tf_op jit(solution)/shard_map/rows_ahead/ppermute | solution.py:302
  31.3 14.4 %collective-permute-start.12 = (bf16[16,7424]{1,0:T(8,128)(2,1)S(1)}, bf16[16,7424]{1,0:T(8,128)(2,1)S(1)}, u32[]{:S(2)}, u32[]{:S(2)}) collective-permute-start(bf16[16,7424]{1,0:T(8,128)(2,1)S(1)} %collective-permute-done.9.refs_9_), channel_id=1, source_target_pairs={{0,1},{2,3},{4,0},{6,2},{8,4},{10,6},{12,8},{14,10},{13,12},{15,14... | collective-permute-start | bytes 712712 | tf_op jit(solution)/shard_map/rows_behind/ppermute | solution.py:302
  32.9 14.4 %collective-permute-start.2 = (bf16[16,7424]{1,0:T(8,128)(2,1)S(1)}, bf16[16,7424]{1,0:T(8,128)(2,1)S(1)}, u32[]{:S(2)}, u32[]{:S(2)}) collective-permute-start(bf16[16,7424]{1,0:T(8,128)(2,1)S(1)} %collective-permute-done.1.refs_6_), channel_id=1, source_target_pairs={{0,4},{2,6},{4,8},{6,10},{8,12},{10,14},{12,13},{14,15},{13,9},{15... | collective-permute-start | bytes 712712 | tf_op jit(solution)/shard_map/rows_ahead/ppermute | solution.py:302
  36.4 11.4 %collective-permute-start.14 = (bf16[16,7424]{1,0:T(8,128)(2,1)S(1)}, bf16[16,7424]{1,0:T(8,128)(2,1)S(1)}, u32[]{:S(2)}, u32[]{:S(2)}) collective-permute-start(bf16[16,7424]{1,0:T(8,128)(2,1)S(1)} %collective-permute-done.7.refs_7_), channel_id=1, source_target_pairs={{0,1},{2,3},{4,0},{6,2},{8,4},{10,6},{12,8},{14,10},{13,12},{15,14... | collective-permute-start | bytes 712712 | tf_op jit(solution)/shard_map/rows_behind/ppermute | solution.py:302
  38.0 9.8 %collective-permute-start.15 = (bf16[16,7424]{1,0:T(8,128)(2,1)S(1)}, bf16[16,7424]{1,0:T(8,128)(2,1)S(1)}, u32[]{:S(2)}, u32[]{:S(2)}) collective-permute-start(bf16[16,7424]{1,0:T(8,128)(2,1)S(1)} %collective-permute-done.8.refs_8_), channel_id=1, source_target_pairs={{0,4},{2,6},{4,8},{6,10},{8,12},{10,14},{12,13},{14,15},{13,9},{15... | collective-permute-start | bytes 712712 | tf_op jit(solution)/shard_map/rows_ahead/ppermute | solution.py:302
  38.4 2.1 %copy-start = (bf16[1,1,128,2,7296]{4,2,3,1,0:T(8,128)(2,1)S(1)}, bf16[1,1,128,2,7296]{4,2,3,1,0:T(8,128)(2,1)}, u32[]{:S(2)}) copy-start(bf16[1,1,128,2,7296]{4,2,3,1,0:T(8,128)(2,1)} %copy.10) | copy-start | bytes 11206660
  45.6 6.2 %collective-permute-start.13 = (bf16[16,7424]{1,0:T(8,128)(2,1)S(1)}, bf16[16,7424]{1,0:T(8,128)(2,1)S(1)}, u32[]{:S(2)}, u32[]{:S(2)}) collective-permute-start(bf16[16,7424]{1,0:T(8,128)(2,1)S(1)} %collective-permute-done.12.refs_3_), channel_id=1, source_target_pairs={{0,1},{2,3},{4,0},{6,2},{8,4},{10,6},{12,8},{14,10},{13,12},{15,14... | collective-permute-start | bytes 712712 | tf_op jit(solution)/shard_map/rows_behind/ppermute | solution.py:302
  47.3 6.1 %collective-permute-start.11 = (bf16[16,7424]{1,0:T(8,128)(2,1)S(1)}, bf16[16,7424]{1,0:T(8,128)(2,1)S(1)}, u32[]{:S(2)}, u32[]{:S(2)}) collective-permute-start(bf16[16,7424]{1,0:T(8,128)(2,1)S(1)} %collective-permute-done.2.refs_0_), channel_id=1, source_target_pairs={{0,4},{2,6},{4,8},{6,10},{8,12},{10,14},{12,13},{14,15},{13,9},{15... | collective-permute-start | bytes 712712 | tf_op jit(solution)/shard_map/rows_ahead/ppermute | solution.py:302
  56.8 1.6 %collective-permute-start.16 = (f32[2,256,128]{2,1,0:T(8,128)S(1)}, f32[2,256,128]{2,1,0:T(8,128)S(1)}, u32[]{:S(2)}, u32[]{:S(2)}) collective-permute-start(f32[2,256,128]{2,1,0:T(8,128)S(1)} %get-tuple-element.32.partial), channel_id=1, source_target_pairs={{0,2},{2,0},{4,6},{6,4},{8,10},{10,8},{12,14},{14,12},{1,3},{3,1},... | collective-permute-start | bytes 786440 | tf_op jit(solution)/shard_map/ppermute | solution.py:363
  59.3 4.3 %collective-permute-start.17 = (f32[136,128]{1,0:T(8,128)S(1)}, f32[136,128]{1,0:T(8,128)S(1)}, u32[]{:S(2)}, u32[]{:S(2)}) collective-permute-start(f32[136,128]{1,0:T(8,128)S(1)} %get-tuple-element.35), channel_id=1, source_target_pairs={{0,1},{1,0},{2,3},{3,2},{4,5},{5,4},{6,7},{7,6},{8,9},{9,8},{10,11... | collective-permute-start | bytes 208904 | tf_op jit(solution)/shard_map/ppermute | solution.py:375
  63.7 6.4 %collective-permute-start.18 = (f32[8,128]{1,0:T(8,128)S(1)}, f32[8,128]{1,0:T(8,128)S(1)}, u32[]{:S(2)}, u32[]{:S(2)}) collective-permute-start(f32[8,128]{1,0:T(8,128)S(1)} %select_maximum_fusion.pair.refs_0_), channel_id=1, source_target_pairs={{0,4},{2,6},{4,8},{6,10},{8,12},{10,14},{12,0},{14,2},{1,5},{3,7},... | collective-permute-start | bytes 12296 | tf_op jit(solution)/shard_map/ppermute | solution.py:382
  65.1 5.1 %collective-permute-start.19 = (f32[8,128]{1,0:T(8,128)S(1)}, f32[8,128]{1,0:T(8,128)S(1)}, u32[]{:S(2)}, u32[]{:S(2)}) collective-permute-start(f32[8,128]{1,0:T(8,128)S(1)} %select_maximum_fusion.pair.refs_0_), channel_id=1, source_target_pairs={{0,8},{2,10},{4,12},{6,14},{8,0},{10,2},{12,4},{14,6},{1,9},{3,11}... | collective-permute-start | bytes 12296 | tf_op jit(solution)/shard_map/ppermute | solution.py:382
  66.9 3.6 %collective-permute-start.20 = (f32[8,128]{1,0:T(8,128)S(1)}, f32[8,128]{1,0:T(8,128)S(1)}, u32[]{:S(2)}, u32[]{:S(2)}) collective-permute-start(f32[8,128]{1,0:T(8,128)S(1)} %select_maximum_fusion.pair.refs_0_), channel_id=1, source_target_pairs={{0,12},{2,14},{4,0},{6,2},{8,4},{10,6},{12,8},{14,10},{1,13},{3,15... | collective-permute-start | bytes 12296 | tf_op jit(solution)/shard_map/ppermute | solution.py:382

commit v8 on v7

--- a/solution.py
+++ b/solution.py
@@ -37,6 +37,11 @@
         jnp.where((quarter & 2) == 2, -low, low),
         jnp.where(((quarter + 1) & 2) == 2, -high, high),
     )
+
+
+def panel_kernel(spot, sides, own, given):
+    own[...] = sides[spot[2]]
+    given[...] = sides[1 - spot[2]]
 
 
 def row_kernel(spot, planes, defocus, lists, kept, given, facts, focus, named, sems):
@@ -64,7 +69,7 @@
     return jnp.concatenate([m[...].astype(jnp.float32).T[: m.shape[0]] for m in meta], axis=0)
 
 
-def add_scores(rows, spot, noise, sides, mate_panel, turn_sin, turn_cos, sums, segments):
+def add_scores(rows, noise, own_panel, mate_panel, turn_sin, turn_cos, sums, segments):
     columns = noise.shape[1]
     width = columns // segments
     tiles = width // LANES
@@ -78,7 +83,6 @@
     turn_cos[...] = step_cos
     for total in sums:
         total[...] = jnp.zeros_like(total)
-    core = spot[2]
 
     def segment(index, carry):
         sine, cosine = carry
@@ -96,7 +100,7 @@
         energy = jnp.concatenate(energy_parts, axis=1)
         contract = (((1,), (1,)), ((), ()))
         whole = pl.ds(start, width)
-        for values, total in ((sides[core, :, whole], sums[0]), (mate_panel[:, whole], sums[1])):
+        for values, total in ((own_panel[:, whole], sums[0]), (mate_panel[:, whole], sums[1])):
             squared = values * values
             correlate = lax.dot_general(
                 values, scaled, contract, preferred_element_type=jnp.float32
@@ -111,10 +115,10 @@
 
 def batch_kernel(n, segments, spot, *refs):
     rows = refs[:n]
-    noise, sides, mate_panel = refs[n : n + 3]
+    noise, own_panel, mate_panel = refs[n : n + 3]
     own_out, mate_out, fact_out, turn_sin, turn_cos, *sums = refs[n + 3 :]
     fact_out[...] = add_scores(
-        rows, spot, noise, sides, mate_panel, turn_sin, turn_cos, sums, segments
+        rows, noise, own_panel, mate_panel, turn_sin, turn_cos, sums, segments
     )
     own_out[...] = sums[0][...].T
     mate_out[...] = sums[1][...].T
@@ -122,12 +126,12 @@
 
 def last_kernel(n, segments, orders, spot, *refs):
     rows = refs[:n]
-    noise, sides, mate_panel = refs[n : n + 3]
+    noise, own_panel, mate_panel = refs[n : n + 3]
     rest = refs[n + 3 :]
     earlier, rest = rest[: 3 * (len(orders) - 1)], rest[3 * (len(orders) - 1) :]
     partial, facts, turn_sin, turn_cos, *sums = rest
     last_facts = add_scores(
-        rows, spot, noise, sides, mate_panel, turn_sin, turn_cos, sums, segments
+        rows, noise, own_panel, mate_panel, turn_sin, turn_cos, sums, segments
     )
     position, core = spot[1], spot[2]
     each = rows[0].shape[0]
@@ -150,9 +154,9 @@
             facts[pl.ds(start, each), :] = fact[piece]
 
 
-def score_call(chunks, orders, earlier, spot, noise, sides, mate_panel):
+def score_call(chunks, orders, earlier, spot, noise, own_panel, mate_panel):
     each = chunks[0].shape[0]
-    orientations, columns = sides.shape[1:]
+    orientations, columns = own_panel.shape
     whole = columns // LANES
     segments = next(s for s in (3, 2, 4, 5, 6, 7, 1) if whole % s == 0)
     n = len(chunks)
@@ -185,7 +189,7 @@
             bytes_accessed=4 * orientations * columns + 2 * count * columns,
             transcendentals=0,
         ),
-    )(spot, *chunks, noise, sides, mate_panel, *extra)
+    )(spot, *chunks, noise, own_panel, mate_panel, *extra)
 
 
 def names_block(facts, search, block):
@@ -194,10 +198,11 @@
     return jnp.max(jnp.where(match, 1.0, 0.0), axis=1, keepdims=True) > 0.0
 
 
-def chip_kernel(search, spot, partial, mate, facts, mine, own_stats, across):
+def chip_kernel(search, spot, partial, mate, facts, mine, across, stats):
     group, core, place = spot[0], spot[2], spot[3]
     count = mine.shape[0]
     lane = lax.broadcasted_iota(jnp.int32, (count, LANES), 1)
+    pairs = []
     for relative in range(2):
         side = group if relative == 0 else 1 - group
         window = pl.ds(pl.multiple_of(side * count, count), count)
@@ -207,26 +212,21 @@
             block = core if crossed == 0 else 1 - core
             scores = partial[block, window, :] + mate[block, window, :]
             if crossed == 0:
-                if relative == 0:
-                    mine[...] = scores
-                else:
-                    across[:count] = scores
+                out = mine if relative == 0 else across
+                out[...] = scores
             named = names_block(listed, search, place - core + block)
             masked.append(jnp.where(named, scores, FLOOR))
         top = jnp.max(jnp.maximum(*masked), axis=1, keepdims=True)
         terms = [jnp.where(m > FLOOR, jnp.exp(m - top), 0.0) for m in masked]
         total = jnp.sum(terms[0] + terms[1], axis=1, keepdims=True)
-        pair = jnp.where(lane == 0, top, jnp.where(lane == 1, total, 0.0)).T
-        if relative == 0:
-            own_stats[...] = pair[: own_stats.shape[0]]
-        else:
-            across[count:] = pair[: across.shape[0] - count]
-
-
-def slot_kernel(search, slots_each, each, spot, mine, across, pair, facts, slots, chosen):
+        pairs.append(jnp.where(lane == relative, top, jnp.where(lane == 2 + relative, total, 0.0)))
+    stats[...] = (pairs[0] + pairs[1]).T[: stats.shape[0]]
+
+
+def slot_kernel(search, slots_each, each, spot, mine, across, facts, slots, chosen, tops):
     group, place = spot[0], spot[3]
     count = mine.shape[0]
-    same, other = mine[...], across[:count]
+    same, other = mine[...], across[...]
     first = group == 0
     scores = jnp.concatenate(
         [jnp.where(first, same, other), jnp.where(first, other, same)], axis=1
@@ -249,7 +249,8 @@
         slot = jnp.broadcast_to(slot[:, :1], (count, capacity))
     target = lax.broadcasted_iota(jnp.int32, (count, capacity), 1)
     taken = jnp.where((slot == target) & named, 1.0, 0.0)
-    top = jnp.broadcast_to(pair[0:1, :], (count, count)).T[:, 0:1]
+    top = jnp.max(scores, axis=1, keepdims=True)
+    tops[...] = jnp.broadcast_to(top, (count, LANES)).T[: tops.shape[0]]
     terms = jnp.where(named, jnp.exp(scores - top), 0.0)
     slots[...] = lax.dot_general(
         taken,
@@ -261,12 +262,12 @@
     chosen[...] = taken.T
 
 
-def final_kernel(n, *refs):
-    parts, slots, chosen, out = refs[:n], refs[n], refs[n + 1], refs[n + 2]
-    peak = functools.reduce(jnp.maximum, [p[0:1, :] for p in parts])
-    shares = [p[1:2, :] * jnp.exp(p[0:1, :] - peak) for p in parts]
-    total = functools.reduce(jnp.add, shares)
-    factor = jnp.exp(parts[0][0:1, :] - peak) / total
+def final_kernel(own, other, tops, slots, chosen, out):
+    peaks = own[0:1, :], other[1:2, :]
+    totals = own[2:3, :], other[3:4, :]
+    peak = jnp.maximum(*peaks)
+    total = totals[0] * jnp.exp(peaks[0] - peak) + totals[1] * jnp.exp(peaks[1] - peak)
+    factor = jnp.exp(jnp.minimum(tops[0:1, :] - peak, 0.0)) / total
     scale = jnp.sum(chosen[...] * factor, axis=1, keepdims=True)
     out[...] = slots[...] * scale
 
@@ -323,7 +324,14 @@
         got = lax.ppermute(given, "orient", mate_pairs)
 
     sides = lax.optimization_barrier(jnp.transpose(panels[0, 0], (1, 0, 2)))
-    given_panel = lax.dynamic_index_in_dim(sides, 1 - core, 0, keepdims=False)
+    panel_shape = jax.ShapeDtypeStruct(sides.shape[1:], sides.dtype)
+    own_panel, given_panel = pl.pallas_call(
+        panel_kernel,
+        in_specs=[smem, vmem],
+        out_specs=[vmem] * 2,
+        out_shape=[panel_shape] * 2,
+        compiler_params=params,
+    )(spot, sides)
     with jax.named_scope("mate_panel"):
         mate_panel = lax.ppermute(given_panel, "orient", mate_pairs)
 
@@ -332,7 +340,7 @@
     ahead = {False: kept, True: given}
     behind = {False: kept, True: given}
     orders, earlier, late = [], [], []
-    score = lambda c: score_call(c, None, None, spot, noise, sides, mate_panel)
+    score = lambda c: score_call(c, None, None, spot, noise, own_panel, mate_panel)
     for step in range(1, chips + 1):
         if step == chips and step > 2:
             orders.append([key for key, _ in waiting])
@@ -357,48 +365,49 @@
     waiting = late
     orders.append([key for key, _ in waiting])
     partial, all_facts = score_call(
-        [c for _, c in waiting], orders, earlier, spot, noise, sides, mate_panel
+        [c for _, c in waiting], orders, earlier, spot, noise, own_panel, mate_panel
     )
 
     mate_partial = lax.ppermute(partial, "orient", mate_pairs)
-    mine, own_stats, across = pl.pallas_call(
+    mine, across, stats = pl.pallas_call(
         functools.partial(chip_kernel, local_search),
         in_specs=[smem] + [vmem] * 3,
         out_specs=[vmem] * 3,
         out_shape=[
             jax.ShapeDtypeStruct((everyone, orientations), jnp.float32),
+            jax.ShapeDtypeStruct((everyone, orientations), jnp.float32),
             jax.ShapeDtypeStruct((8, everyone), jnp.float32),
-            jax.ShapeDtypeStruct((everyone + 8, orientations), jnp.float32),
         ],
         compiler_params=params,
     )(spot, partial, mate_partial, all_facts)
+
     from_x = lax.ppermute(across, "cls", x_pairs)
-
-    tops = own_stats[0], from_x[everyone]
-    peak = jnp.maximum(*tops)
-    total = own_stats[1] * jnp.exp(tops[0] - peak) + from_x[everyone + 1] * jnp.exp(tops[1] - peak)
-    pair = jnp.pad(jnp.stack([peak, total]), ((0, 6), (0, 0)))
-    pairs = [pair] + [
-        lax.ppermute(pair, "orient", [(d, (d + 2 * s) % devices) for d in range(devices)])
+    parts = [stats] + [
+        lax.ppermute(stats, "orient", [(d, (d + 2 * s) % devices) for d in range(devices)])
         for s in range(1, chips)
     ]
-    slots, chosen = pl.pallas_call(
+    peaks = functools.reduce(jnp.maximum, [p[0:2] for p in parts])
+    totals = functools.reduce(jnp.add, [p[2:4] * jnp.exp(p[0:2] - peaks) for p in parts])
+    class_stats = jnp.pad(jnp.concatenate([peaks, totals], axis=0), ((0, 4), (0, 0)))
+    other_stats = lax.ppermute(class_stats, "cls", x_pairs)
+    slots, chosen, tops = pl.pallas_call(
         functools.partial(slot_kernel, local_search, slots_each, per_device),
-        in_specs=[smem] + [vmem] * 4,
-        out_specs=[vmem] * 2,
+        in_specs=[smem] + [vmem] * 3,
+        out_specs=[vmem] * 3,
         out_shape=[
             jax.ShapeDtypeStruct((capacity, 2 * orientations), jnp.float32),
             jax.ShapeDtypeStruct((capacity, everyone), jnp.float32),
+            jax.ShapeDtypeStruct((8, everyone), jnp.float32),
         ],
         compiler_params=params,
-    )(spot, mine, from_x, pair, all_facts)
+    )(spot, mine, from_x, all_facts)
     posterior = pl.pallas_call(
-        functools.partial(final_kernel, chips),
-        in_specs=[vmem] * (chips + 2),
+        final_kernel,
+        in_specs=[vmem] * 5,
         out_specs=vmem,
         out_shape=jax.ShapeDtypeStruct((capacity, 2 * orientations), jnp.float32),
         compiler_params=params,
-    )(*pairs, slots, chosen)
+    )(class_stats, other_stats, tops, slots, chosen)
     return posterior.reshape(1, 1, capacity, -1)
 
 

time: 71.4 us -> 69.7 us (0.976)
  local copies, waits for them, and re-layouts: 9.33 us -> 6.37 us
  starting transfers between devices: 22.9 us -> 24.7 us
  waiting for transfers between devices: 23.1 us -> 21.8 us
    squeeze x1 -> x0, local copies, waits for them, and re-layouts: 2.97 us -> none  [chip_shards(): given_panel = lax.dynamic_index_in_dim(sides, 1 - core, 0, keepdims=False)]
    ppermute x1, waiting for transfers between devices: 2.74 us -> 0.86 us  [chip_shards(): from_x = lax.ppermute(across, 'cls', x_pairs)]
    ppermute x1, starting transfers between devices: 1.61 us -> 2.62 us  [chip_shards(): from_x = lax.ppermute(across, 'cls', x_pairs)]
    pallas_call x1 -> x2, Pallas kernels: 0.77 us -> 1.56 us  [the longest x1 0.79 us: chip_shards(): pl.pallas_call(panel_kernel, in_specs=[smem, vmem], out_specs=[vmem] * 2,...]
    ppermute x3 -> x4, starting transfers between devices: 5.31 us -> 5.87 us  [the longest x3 4.5 us: chip_shards(): lax.ppermute(stats, 'orient', [(d, (d + 2 * s) % devices) for d in range(...]
  transfers between devices with their start and end apart: 21 -> 22, of which waited for: 9 -> 9; matrix products, arithmetic and copies ran while one was open for 0% -> 0% of each run, Pallas kernels for 15% -> 15%
where the time goes in v8:
time: 69.7 us; the launch traced here: 69.5 us
  starting transfers between devices  24.7 us (35%)
  waiting for transfers between devices  21.8 us (31%)
  Pallas kernels  16.4 us (24%)
  local copies, waits for them, and re-layouts  6.37 us (9%)
    ppermute x14, waiting for transfers between devices, forward(): return lax.ppermute(values, ('orient', 'cls'), pairs)  19 us
    ppermute x14, starting transfers between devices, forward(): return lax.ppermute(values, ('orient', 'cls'), pairs)  14.9 us
    pallas_call x3, Pallas kernels, score_call(): pl.pallas_call(kernel, in_specs=[pl.BlockSpec(memory_space=pltpu.SMEM)] +...  12.3 us
    unnamed x12, local copies, waits for them, and re-layouts  6.35 us
    ppermute x3, starting transfers between devices, chip_shards(): lax.ppermute(stats, 'orient', [(d, (d + 2 * s) % devices) for d in range(...  4.5 us
    ppermute x1, starting transfers between devices, chip_shards(): from_x = lax.ppermute(across, 'cls', x_pairs)  2.62 us
    ppermute x1, waiting for transfers between devices, chip_shards(): mate_partial = lax.ppermute(partial, 'orient', mate_pairs)  1.52 us
  transfers between devices with their start and end apart: 22, of which 9 were waited for; matrix products, arithmetic and copies ran while one was open for 0% of the time, Pallas kernels for 15%

profile of v8, /device:TPU:0, one launch (start us, length us, event | category | flops | bytes accessed | tf_op | source)
XLA Modules:
  0.0 69.5 jit_solution(3469909338416370822)
XLA Ops:
  0.0 4.2 %copy.10 = bf16[1,1,128,2,7296]{4,2,3,1,0:T(8,128)(2,1)} copy(bf16[1,1,128,2,7296]{4,3,2,1,0:T(2,128)(2,1)} %param.9) | data formatting | bytes 7471104 | tf_op args[4]
  4.2 0.1 pad_add_fusion.spot
  4.3 2.1 %copy-done = bf16[1,1,128,2,7296]{4,2,3,1,0:T(8,128)(2,1)S(1)} copy-done((bf16[1,1,128,2,7296]{4,2,3,1,0:T(8,128)(2,1)S(1)}, bf16[1,1,128,2,7296]{4,2,3,1,0:T(8,128)(2,1)}, u32[]{:S(2)}) %copy-start) | copy-done | bytes 3735576
  6.4 0.8 %shard_map.56 = (bf16[128,7296]{1,0:T(8,128)(2,1)S(1)}, bf16[128,7296]{1,0:T(8,128)(2,1)S(1)}) custom-call(s32[4]{0:T(128)S(1)} %pad_add_fusion.spot, bf16[2,128,7296]{2,1,0:T(8,128)(2,1)S(1)} %bitcast.18), custom_call_target="tpu_custom_call" | custom-call | tf_op jit(solution)/shard_map/pallas_call | solution.py:328
  7.2 0.5 collective-permute-start.10
  7.8 0.6 shard_map.55
  8.4 2.7 %collective-permute-start.6 = (bf16[16,7424]{1,0:T(8,128)(2,1)S(1)}, bf16[16,7424]{1,0:T(8,128)(2,1)S(1)}, u32[]{:S(2)}, u32[]{:S(2)}) collective-permute-start(bf16[16,7424]{1,0:T(8,128)(2,1)S(1)} %get-tuple-element.26), channel_id=1, source_target_pairs={{0,3},{2,1},{4,2},{6,0},{8,6},{10,4},{12,10},{14,8},{13,14},{15,12... | collective-permute-start | bytes 712712 | tf_op jit(solution)/shard_map/rows_behind/ppermute | solution.py:303
  11.0 1.6 %collective-permute-start.4 = (bf16[16,7424]{1,0:T(8,128)(2,1)S(1)}, bf16[16,7424]{1,0:T(8,128)(2,1)S(1)}, u32[]{:S(2)}, u32[]{:S(2)}) collective-permute-start(bf16[16,7424]{1,0:T(8,128)(2,1)S(1)} %get-tuple-element.25.refs_0_), channel_id=1, source_target_pairs={{0,1},{2,3},{4,0},{6,2},{8,4},{10,6},{12,8},{14,10},{13,12},{15,14... | collective-permute-start | bytes 712712 | tf_op jit(solution)/shard_map/rows_behind/ppermute | solution.py:303
  12.6 0.4 collective-permute-start
  13.1 4.1 %collective-permute-done.6.refs_5_ = bf16[16,7424]{1,0:T(8,128)(2,1)S(1)} collective-permute-done((bf16[16,7424]{1,0:T(8,128)(2,1)S(1)}, bf16[16,7424]{1,0:T(8,128)(2,1)S(1)}, u32[]{:S(2)}, u32[]{:S(2)}) %collective-permute-start.6) | collective-permute-done | bytes 237600 | tf_op jit(solution)/shard_map/rows_behind/ppermute | solution.py:303
  17.1 0.8 %collective-permute-start.3 = (bf16[16,7424]{1,0:T(8,128)(2,1)S(1)}, bf16[16,7424]{1,0:T(8,128)(2,1)S(1)}, u32[]{:S(2)}, u32[]{:S(2)}) collective-permute-start(bf16[16,7424]{1,0:T(8,128)(2,1)S(1)} %get-tuple-element.26), channel_id=1, source_target_pairs={{0,2},{2,0},{4,6},{6,4},{8,10},{10,8},{12,14},{14,12},{1,3},{3,1},... | collective-permute-start | bytes 712712 | tf_op jit(solution)/shard_map/mate_rows/ppermute | solution.py:324
  17.9 4.7 %collective-permute-done.4.refs_3_ = bf16[16,7424]{1,0:T(8,128)(2,1)S(1)} collective-permute-done((bf16[16,7424]{1,0:T(8,128)(2,1)S(1)}, bf16[16,7424]{1,0:T(8,128)(2,1)S(1)}, u32[]{:S(2)}, u32[]{:S(2)}) %collective-permute-start.4) | collective-permute-done | bytes 237600 | tf_op jit(solution)/shard_map/rows_behind/ppermute | solution.py:303
  22.6 1.7 %collective-permute-start.9 = (bf16[16,7424]{1,0:T(8,128)(2,1)S(1)}, bf16[16,7424]{1,0:T(8,128)(2,1)S(1)}, u32[]{:S(2)}, u32[]{:S(2)}) collective-permute-start(bf16[16,7424]{1,0:T(8,128)(2,1)S(1)} %collective-permute-done.6.refs_5_), channel_id=1, source_target_pairs={{0,1},{2,3},{4,0},{6,2},{8,4},{10,6},{12,8},{14,10},{13,12},{15,14... | collective-permute-start | bytes 712712 | tf_op jit(solution)/shard_map/rows_behind/ppermute | solution.py:303
  24.3 0.3 collective-permute-start.1
  24.6 0.0 collective-permute-done.5.refs_4_
  24.6 1.7 %collective-permute-start.7 = (bf16[16,7424]{1,0:T(8,128)(2,1)S(1)}, bf16[16,7424]{1,0:T(8,128)(2,1)S(1)}, u32[]{:S(2)}, u32[]{:S(2)}) collective-permute-start(bf16[16,7424]{1,0:T(8,128)(2,1)S(1)} %collective-permute-done.4.refs_3_), channel_id=1, source_target_pairs={{0,1},{2,3},{4,0},{6,2},{8,4},{10,6},{12,8},{14,10},{13,12},{15,14... | collective-permute-start | bytes 712712 | tf_op jit(solution)/shard_map/rows_behind/ppermute | solution.py:303
  26.3 0.0 collective-permute-done.3.refs_1_
  26.3 0.3 collective-permute-start.8
  26.6 4.6 %collective-permute-done.9.refs_9_ = bf16[16,7424]{1,0:T(8,128)(2,1)S(1)} collective-permute-done((bf16[16,7424]{1,0:T(8,128)(2,1)S(1)}, bf16[16,7424]{1,0:T(8,128)(2,1)S(1)}, u32[]{:S(2)}, u32[]{:S(2)}) %collective-permute-start.9) | collective-permute-done | bytes 237600 | tf_op jit(solution)/shard_map/rows_behind/ppermute | solution.py:303
  31.2 1.7 %collective-permute-start.12 = (bf16[16,7424]{1,0:T(8,128)(2,1)S(1)}, bf16[16,7424]{1,0:T(8,128)(2,1)S(1)}, u32[]{:S(2)}, u32[]{:S(2)}) collective-permute-start(bf16[16,7424]{1,0:T(8,128)(2,1)S(1)} %collective-permute-done.9.refs_9_), channel_id=1, source_target_pairs={{0,1},{2,3},{4,0},{6,2},{8,4},{10,6},{12,8},{14,10},{13,12},{15,14... | collective-permute-start | bytes 712712 | tf_op jit(solution)/shard_map/rows_behind/ppermute | solution.py:303
  32.9 0.0 collective-permute-done.1.refs_6_
  33.0 0.3 collective-permute-start.2
  33.3 3.0 %collective-permute-done.7.refs_7_ = bf16[16,7424]{1,0:T(8,128)(2,1)S(1)} collective-permute-done((bf16[16,7424]{1,0:T(8,128)(2,1)S(1)}, bf16[16,7424]{1,0:T(8,128)(2,1)S(1)}, u32[]{:S(2)}, u32[]{:S(2)}) %collective-permute-start.7) | collective-permute-done | bytes 237600 | tf_op jit(solution)/shard_map/rows_behind/ppermute | solution.py:303
  36.3 1.7 %collective-permute-start.14 = (bf16[16,7424]{1,0:T(8,128)(2,1)S(1)}, bf16[16,7424]{1,0:T(8,128)(2,1)S(1)}, u32[]{:S(2)}, u32[]{:S(2)}) collective-permute-start(bf16[16,7424]{1,0:T(8,128)(2,1)S(1)} %collective-permute-done.7.refs_7_), channel_id=1, source_target_pairs={{0,1},{2,3},{4,0},{6,2},{8,4},{10,6},{12,8},{14,10},{13,12},{15,14... | collective-permute-start | bytes 712712 | tf_op jit(solution)/shard_map/rows_behind/ppermute | solution.py:303
  38.0 0.0 collective-permute-done.8.refs_8_
  38.1 0.3 collective-permute-start.15
  38.4 0.0 collective-permute-done.10.refs_12_.refs_6_.refs_4_
  38.4 5.1 %shard_map.57 = (f32[160,128]{1,0:T(8,128)S(1)}, f32[160,128]{1,0:T(8,128)S(1)}, f32[160,128]{1,0:T(8,128)S(1)}) custom-call(s32[4]{0:T(128)S(1)} %pad_add_fusion.spot, bf16[16,7424]{1,0:T(8,128)(2,1)S(1)} %get-tuple-element.25.refs_0_, bf16[16,7424]{1,0:T(8,128)(2,1)S(1)} %collective-permute-done.3.refs_1_, ...), custom_call_target="tpu_custom_call" | custom-call | flops 1195376640 | bytes 6070272 | tf_op jit(solution)/shard_map/pallas_call | solution.py:180
  43.5 1.8 %collective-permute-start.13 = (bf16[16,7424]{1,0:T(8,128)(2,1)S(1)}, bf16[16,7424]{1,0:T(8,128)(2,1)S(1)}, u32[]{:S(2)}, u32[]{:S(2)}) collective-permute-start(bf16[16,7424]{1,0:T(8,128)(2,1)S(1)} %collective-permute-done.12.refs_3_), channel_id=1, source_target_pairs={{0,1},{2,3},{4,0},{6,2},{8,4},{10,6},{12,8},{14,10},{13,12},{15,14... | collective-permute-start | bytes 712712 | tf_op jit(solution)/shard_map/rows_behind/ppermute | solution.py:303
  45.3 0.0 collective-permute-done.2.refs_0_
  45.3 0.3 collective-permute-start.11
  45.6 0.9 %collective-permute-done.14.refs_1_ = bf16[16,7424]{1,0:T(8,128)(2,1)S(1)} collective-permute-done((bf16[16,7424]{1,0:T(8,128)(2,1)S(1)}, bf16[16,7424]{1,0:T(8,128)(2,1)S(1)}, u32[]{:S(2)}, u32[]{:S(2)}) %collective-permute-start.14) | collective-permute-done | bytes 237600 | tf_op jit(solution)/shard_map/rows_behind/ppermute | solution.py:303
  46.5 1.7 %collective-permute-done.15.refs_2_ = bf16[16,7424]{1,0:T(8,128)(2,1)S(1)} collective-permute-done((bf16[16,7424]{1,0:T(8,128)(2,1)S(1)}, bf16[16,7424]{1,0:T(8,128)(2,1)S(1)}, u32[]{:S(2)}, u32[]{:S(2)}) %collective-permute-start.15) | collective-permute-done | bytes 237600 | tf_op jit(solution)/shard_map/rows_ahead/ppermute | solution.py:303
  48.2 3.7 %shard_map.58 = (f32[64,128]{1,0:T(8,128)S(1)}, f32[64,128]{1,0:T(8,128)S(1)}, f32[64,128]{1,0:T(8,128)S(1)}) custom-call(s32[4]{0:T(128)S(1)} %pad_add_fusion.spot, bf16[16,7424]{1,0:T(8,128)(2,1)S(1)} %collective-permute-done.2.refs_0_, bf16[16,7424]{1,0:T(8,128)(2,1)S(1)} %collective-permute-done.14.refs_1_, ...), custom_call_target="tpu_custom_call" | custom-call | flops 956301312 | bytes 4669440 | tf_op jit(solution)/shard_map/pallas_call | solution.py:180
  52.0 0.0 collective-permute-done.11.refs_0_
  52.0 3.4 %shard_map.59 = (f32[2,256,128]{2,1,0:T(8,128)S(1)}, f32[256,128]{1,0:T(8,128)S(1)}) custom-call(s32[4]{0:T(128)S(1)} %pad_add_fusion.spot, bf16[16,7424]{1,0:T(8,128)(2,1)S(1)} %collective-permute-done.11.refs_0_, bf16[16,7424]{1,0:T(8,128)(2,1)S(1)} %collective-permute-done.13.refs_1_, f32[1,7296]{1,0:T(1,128)S(1)} %broadcast_in_dim.3.refs_10_.refs_4_.refs_2_, ...), custom_call_target="tpu_custom_call" | custom-call | flops 956301312 | bytes 4202496 | tf_op jit(solution)/shard_map/pallas_call | solution.py:180
  55.4 0.1 collective-permute-start.16
  55.5 1.5 %collective-permute-done.16.mate = f32[2,256,128]{2,1,0:T(8,128)S(1)} collective-permute-done((f32[2,256,128]{2,1,0:T(8,128)S(1)}, f32[2,256,128]{2,1,0:T(8,128)S(1)}, u32[]{:S(2)}, u32[]{:S(2)}) %collective-permute-start.16) | collective-permute-done | bytes 262176 | tf_op jit(solution)/shard_map/ppermute | solution.py:371
  57.0 0.9 %shard_map.60 = (f32[128,128]{1,0:T(8,128)S(1)}, f32[128,128]{1,0:T(8,128)S(1)}, f32[8,128]{1,0:T(8,128)S(1)}) custom-call(s32[4]{0:T(128)S(1)} %pad_add_fusion.spot, f32[2,256,128]{2,1,0:T(8,128)S(1)} %get-tuple-element.37.partial, f32[2,256,128]{2,1,0:T(8,128)S(1)} %collective-permute-done.16.mate, f32[256,128]{1,0:T(8,128)S(1)} %get-tuple-element.38.facts), custom_call_target="tpu_custom_call" | custom-call | tf_op jit(solution)/shard_map/pallas_call | solution.py:372
  57.9 0.3 collective-permute-start.17
  58.3 2.8 %collective-permute-start.18 = (f32[8,128]{1,0:T(8,128)S(1)}, f32[8,128]{1,0:T(8,128)S(1)}, u32[]{:S(2)}, u32[]{:S(2)}) collective-permute-start(f32[8,128]{1,0:T(8,128)S(1)} %get-tuple-element.39), channel_id=1, source_target_pairs={{0,8},{2,10},{4,12},{6,14},{8,0},{10,2},{12,4},{14,6},{1,9},{3,11}... | collective-permute-start | bytes 12296 | tf_op jit(solution)/shard_map/ppermute | solution.py:386
  61.1 1.3 %collective-permute-start.19 = (f32[8,128]{1,0:T(8,128)S(1)}, f32[8,128]{1,0:T(8,128)S(1)}, u32[]{:S(2)}, u32[]{:S(2)}) collective-permute-start(f32[8,128]{1,0:T(8,128)S(1)} %get-tuple-element.39), channel_id=1, source_target_pairs={{0,12},{2,14},{4,0},{6,2},{8,4},{10,6},{12,8},{14,10},{1,13},{3,15... | collective-permute-start | bytes 12296 | tf_op jit(solution)/shard_map/ppermute | solution.py:386
  62.4 2.6 %collective-permute-start.21 = (f32[128,128]{1,0:T(8,128)S(1)}, f32[128,128]{1,0:T(8,128)S(1)}, u32[]{:S(2)}, u32[]{:S(2)}) collective-permute-start(f32[128,128]{1,0:T(8,128)S(1)} %get-tuple-element.41), channel_id=1, source_target_pairs={{0,1},{1,0},{2,3},{3,2},{4,5},{5,4},{6,7},{7,6},{8,9},{9,8},{10,11... | collective-permute-start | bytes 196616 | tf_op jit(solution)/shard_map/ppermute | solution.py:384
  65.1 1.4 %collective-permute-start.20 = (f32[8,128]{1,0:T(8,128)S(1)}, f32[8,128]{1,0:T(8,128)S(1)}, u32[]{:S(2)}, u32[]{:S(2)}) collective-permute-start(f32[8,128]{1,0:T(8,128)S(1)} %select_maximum_fusion.own), channel_id=1, source_target_pairs={{0,1},{1,0},{2,3},{3,2},{4,5},{5,4},{6,7},{7,6},{8,9},{9,8},{10,11... | collective-permute-start | bytes 12296 | tf_op jit(solution)/shard_map/ppermute | solution.py:392
  66.5 0.9 %collective-permute-done.21.across = f32[128,128]{1,0:T(8,128)S(1)} collective-permute-done((f32[128,128]{1,0:T(8,128)S(1)}, f32[128,128]{1,0:T(8,128)S(1)}, u32[]{:S(2)}, u32[]{:S(2)}) %collective-permute-start.21) | collective-permute-done | bytes 65568 | tf_op jit(solution)/shard_map/ppermute | solution.py:384
  67.3 1.1 %shard_map.61 = (f32[128,256]{1,0:T(8,128)S(1)}, f32[128,128]{1,0:T(8,128)S(1)}, f32[8,128]{1,0:T(8,128)S(1)}) custom-call(s32[4]{0:T(128)S(1)} %pad_add_fusion.spot, f32[128,128]{1,0:T(8,128)S(1)} %get-tuple-element.40.mine, f32[128,128]{1,0:T(8,128)S(1)} %collective-permute-done.21.across, f32[256,128]{1,0:T(8,128)S(1)} %get-tuple-element.38.facts), custom_call_target="tpu_custom_call" | custom-call | tf_op jit(solution)/shard_map/pallas_call | solution.py:393
  68.4 0.4 collective-permute-done.20.other
  68.8 0.8 %shard_map.62 = f32[128,256]{1,0:T(8,128)} custom-call(f32[8,128]{1,0:T(8,128)S(1)} %select_maximum_fusion.own, f32[8,128]{1,0:T(8,128)S(1)} %collective-permute-done.20.other, f32[8,128]{1,0:T(8,128)S(1)} %get-tuple-element.42.tops, f32[128,256]{1,0:T(8,128)S(1)} %get-tuple-element.43.slots, f32[128,128]{1,0:T(8,128)S(1)} %get-tuple-element.44.chosen), custom_call_target="tpu_custom_call" | custom-call | tf_op jit(solution)/shard_map/pallas_call | solution.py:404
  (20 shorter events, 0.1 us)
Async XLA Ops:
  4.3 2.1 %copy-start = (bf16[1,1,128,2,7296]{4,2,3,1,0:T(8,128)(2,1)S(1)}, bf16[1,1,128,2,7296]{4,2,3,1,0:T(8,128)(2,1)}, u32[]{:S(2)}) copy-start(bf16[1,1,128,2,7296]{4,2,3,1,0:T(8,128)(2,1)} %copy.10) | copy-start | bytes 11206660
  6.4 1.3 %copy-start.3 = (bf16[1,16,2,7296]{3,2,1,0:T(2,128)(2,1)S(1)}, bf16[1,16,2,7296]{3,2,1,0:T(2,128)(2,1)}, u32[]{:S(2)}) copy-start(bf16[1,16,2,7296]{3,2,1,0:T(2,128)(2,1)} %param.5) | copy-start | bytes 1400836
  6.4 1.4 %copy-start.1 = (s32[1,16,4]{1,2,0:T(4,128)S(1)}, s32[1,16,4]{1,2,0:T(4,128)}, u32[]{:S(2)}) copy-start(s32[1,16,4]{1,2,0:T(4,128)} %param.7) | copy-start | bytes 772
  6.4 1.4 %copy-start.2 = (bf16[1,16]{1,0:T(2,128)(2,1)S(1)}, bf16[1,16]{1,0:T(2,128)(2,1)}, u32[]{:S(2)}) copy-start(bf16[1,16]{1,0:T(2,128)(2,1)} %defocus.1) | copy-start | bytes 100
  6.4 26.9 %copy-start.4 = (f32[7296]{0:T(1024)S(1)}, f32[7296]{0:T(1024)}, u32[]{:S(2)}) copy-start(f32[7296]{0:T(1024)} %param.8) | copy-start | bytes 87556
  7.2 31.2 %collective-permute-start.10 = (bf16[128,7296]{1,0:T(8,128)(2,1)S(1)}, bf16[128,7296]{1,0:T(8,128)(2,1)S(1)}, u32[]{:S(2)}, u32[]{:S(2)}) collective-permute-start(bf16[128,7296]{1,0:T(8,128)(2,1)S(1)} %get-tuple-element.28), channel_id=1, source_target_pairs={{0,2},{2,0},{4,6},{6,4},{8,10},{10,8},{12,14},{14,12},{1,3},{3,1},... | collective-permute-start | bytes 5603336 | tf_op jit(solution)/shard_map/mate_panel/ppermute | solution.py:336
  8.4 8.8 %collective-permute-start.6 = (bf16[16,7424]{1,0:T(8,128)(2,1)S(1)}, bf16[16,7424]{1,0:T(8,128)(2,1)S(1)}, u32[]{:S(2)}, u32[]{:S(2)}) collective-permute-start(bf16[16,7424]{1,0:T(8,128)(2,1)S(1)} %get-tuple-element.26), channel_id=1, source_target_pairs={{0,3},{2,1},{4,2},{6,0},{8,6},{10,4},{12,10},{14,8},{13,14},{15,12... | collective-permute-start | bytes 712712 | tf_op jit(solution)/shard_map/rows_behind/ppermute | solution.py:303
  11.0 11.5 %collective-permute-start.4 = (bf16[16,7424]{1,0:T(8,128)(2,1)S(1)}, bf16[16,7424]{1,0:T(8,128)(2,1)S(1)}, u32[]{:S(2)}, u32[]{:S(2)}) collective-permute-start(bf16[16,7424]{1,0:T(8,128)(2,1)S(1)} %get-tuple-element.25.refs_0_), channel_id=1, source_target_pairs={{0,1},{2,3},{4,0},{6,2},{8,4},{10,6},{12,8},{14,10},{13,12},{15,14... | collective-permute-start | bytes 712712 | tf_op jit(solution)/shard_map/rows_behind/ppermute | solution.py:303
  12.6 11.6 %collective-permute-start = (bf16[16,7424]{1,0:T(8,128)(2,1)S(1)}, bf16[16,7424]{1,0:T(8,128)(2,1)S(1)}, u32[]{:S(2)}, u32[]{:S(2)}) collective-permute-start(bf16[16,7424]{1,0:T(8,128)(2,1)S(1)} %get-tuple-element.25.refs_0_), channel_id=1, source_target_pairs={{0,4},{2,6},{4,8},{6,10},{8,12},{10,14},{12,13},{14,15},{13,9},{15... | collective-permute-start | bytes 712712 | tf_op jit(solution)/shard_map/rows_ahead/ppermute | solution.py:303
  13.1 11.5 %collective-permute-start.5 = (bf16[16,7424]{1,0:T(8,128)(2,1)S(1)}, bf16[16,7424]{1,0:T(8,128)(2,1)S(1)}, u32[]{:S(2)}, u32[]{:S(2)}) collective-permute-start(bf16[16,7424]{1,0:T(8,128)(2,1)S(1)} %get-tuple-element.26), channel_id=1, source_target_pairs={{0,6},{2,4},{4,10},{6,8},{8,14},{10,12},{12,15},{14,13},{13,11},{1... | collective-permute-start | bytes 712712 | tf_op jit(solution)/shard_map/rows_ahead/ppermute | solution.py:303
  17.1 9.2 %collective-permute-start.3 = (bf16[16,7424]{1,0:T(8,128)(2,1)S(1)}, bf16[16,7424]{1,0:T(8,128)(2,1)S(1)}, u32[]{:S(2)}, u32[]{:S(2)}) collective-permute-start(bf16[16,7424]{1,0:T(8,128)(2,1)S(1)} %get-tuple-element.26), channel_id=1, source_target_pairs={{0,2},{2,0},{4,6},{6,4},{8,10},{10,8},{12,14},{14,12},{1,3},{3,1},... | collective-permute-start | bytes 712712 | tf_op jit(solution)/shard_map/mate_rows/ppermute | solution.py:324
  22.6 8.7 %collective-permute-start.9 = (bf16[16,7424]{1,0:T(8,128)(2,1)S(1)}, bf16[16,7424]{1,0:T(8,128)(2,1)S(1)}, u32[]{:S(2)}, u32[]{:S(2)}) collective-permute-start(bf16[16,7424]{1,0:T(8,128)(2,1)S(1)} %collective-permute-done.6.refs_5_), channel_id=1, source_target_pairs={{0,1},{2,3},{4,0},{6,2},{8,4},{10,6},{12,8},{14,10},{13,12},{15,14... | collective-permute-start | bytes 712712 | tf_op jit(solution)/shard_map/rows_behind/ppermute | solution.py:303
  24.3 8.7 %collective-permute-start.1 = (bf16[16,7424]{1,0:T(8,128)(2,1)S(1)}, bf16[16,7424]{1,0:T(8,128)(2,1)S(1)}, u32[]{:S(2)}, u32[]{:S(2)}) collective-permute-start(bf16[16,7424]{1,0:T(8,128)(2,1)S(1)} %collective-permute-done.refs_2_), channel_id=1, source_target_pairs={{0,4},{2,6},{4,8},{6,10},{8,12},{10,14},{12,13},{14,15},{13,9},{15... | collective-permute-start | bytes 712712 | tf_op jit(solution)/shard_map/rows_ahead/ppermute | solution.py:303
  24.6 11.7 %collective-permute-start.7 = (bf16[16,7424]{1,0:T(8,128)(2,1)S(1)}, bf16[16,7424]{1,0:T(8,128)(2,1)S(1)}, u32[]{:S(2)}, u32[]{:S(2)}) collective-permute-start(bf16[16,7424]{1,0:T(8,128)(2,1)S(1)} %collective-permute-done.4.refs_3_), channel_id=1, source_target_pairs={{0,1},{2,3},{4,0},{6,2},{8,4},{10,6},{12,8},{14,10},{13,12},{15,14... | collective-permute-start | bytes 712712 | tf_op jit(solution)/shard_map/rows_behind/ppermute | solution.py:303
  26.3 11.8 %collective-permute-start.8 = (bf16[16,7424]{1,0:T(8,128)(2,1)S(1)}, bf16[16,7424]{1,0:T(8,128)(2,1)S(1)}, u32[]{:S(2)}, u32[]{:S(2)}) collective-permute-start(bf16[16,7424]{1,0:T(8,128)(2,1)S(1)} %collective-permute-done.5.refs_4_), channel_id=1, source_target_pairs={{0,4},{2,6},{4,8},{6,10},{8,12},{10,14},{12,13},{14,15},{13,9},{15... | collective-permute-start | bytes 712712 | tf_op jit(solution)/shard_map/rows_ahead/ppermute | solution.py:303
  31.2 12.3 %collective-permute-start.12 = (bf16[16,7424]{1,0:T(8,128)(2,1)S(1)}, bf16[16,7424]{1,0:T(8,128)(2,1)S(1)}, u32[]{:S(2)}, u32[]{:S(2)}) collective-permute-start(bf16[16,7424]{1,0:T(8,128)(2,1)S(1)} %collective-permute-done.9.refs_9_), channel_id=1, source_target_pairs={{0,1},{2,3},{4,0},{6,2},{8,4},{10,6},{12,8},{14,10},{13,12},{15,14... | collective-permute-start | bytes 712712 | tf_op jit(solution)/shard_map/rows_behind/ppermute | solution.py:303
  33.0 12.3 %collective-permute-start.2 = (bf16[16,7424]{1,0:T(8,128)(2,1)S(1)}, bf16[16,7424]{1,0:T(8,128)(2,1)S(1)}, u32[]{:S(2)}, u32[]{:S(2)}) collective-permute-start(bf16[16,7424]{1,0:T(8,128)(2,1)S(1)} %collective-permute-done.1.refs_6_), channel_id=1, source_target_pairs={{0,4},{2,6},{4,8},{6,10},{8,12},{10,14},{12,13},{14,15},{13,9},{15... | collective-permute-start | bytes 712712 | tf_op jit(solution)/shard_map/rows_ahead/ppermute | solution.py:303
  36.3 10.2 %collective-permute-start.14 = (bf16[16,7424]{1,0:T(8,128)(2,1)S(1)}, bf16[16,7424]{1,0:T(8,128)(2,1)S(1)}, u32[]{:S(2)}, u32[]{:S(2)}) collective-permute-start(bf16[16,7424]{1,0:T(8,128)(2,1)S(1)} %collective-permute-done.7.refs_7_), channel_id=1, source_target_pairs={{0,1},{2,3},{4,0},{6,2},{8,4},{10,6},{12,8},{14,10},{13,12},{15,14... | collective-permute-start | bytes 712712 | tf_op jit(solution)/shard_map/rows_behind/ppermute | solution.py:303
  38.1 10.2 %collective-permute-start.15 = (bf16[16,7424]{1,0:T(8,128)(2,1)S(1)}, bf16[16,7424]{1,0:T(8,128)(2,1)S(1)}, u32[]{:S(2)}, u32[]{:S(2)}) collective-permute-start(bf16[16,7424]{1,0:T(8,128)(2,1)S(1)} %collective-permute-done.8.refs_8_), channel_id=1, source_target_pairs={{0,4},{2,6},{4,8},{6,10},{8,12},{10,14},{12,13},{14,15},{13,9},{15... | collective-permute-start | bytes 712712 | tf_op jit(solution)/shard_map/rows_ahead/ppermute | solution.py:303
  43.5 8.5 %collective-permute-start.13 = (bf16[16,7424]{1,0:T(8,128)(2,1)S(1)}, bf16[16,7424]{1,0:T(8,128)(2,1)S(1)}, u32[]{:S(2)}, u32[]{:S(2)}) collective-permute-start(bf16[16,7424]{1,0:T(8,128)(2,1)S(1)} %collective-permute-done.12.refs_3_), channel_id=1, source_target_pairs={{0,1},{2,3},{4,0},{6,2},{8,4},{10,6},{12,8},{14,10},{13,12},{15,14... | collective-permute-start | bytes 712712 | tf_op jit(solution)/shard_map/rows_behind/ppermute | solution.py:303
  45.3 6.7 %collective-permute-start.11 = (bf16[16,7424]{1,0:T(8,128)(2,1)S(1)}, bf16[16,7424]{1,0:T(8,128)(2,1)S(1)}, u32[]{:S(2)}, u32[]{:S(2)}) collective-permute-start(bf16[16,7424]{1,0:T(8,128)(2,1)S(1)} %collective-permute-done.2.refs_0_), channel_id=1, source_target_pairs={{0,4},{2,6},{4,8},{6,10},{8,12},{10,14},{12,13},{14,15},{13,9},{15... | collective-permute-start | bytes 712712 | tf_op jit(solution)/shard_map/rows_ahead/ppermute | solution.py:303
  55.4 1.6 %collective-permute-start.16 = (f32[2,256,128]{2,1,0:T(8,128)S(1)}, f32[2,256,128]{2,1,0:T(8,128)S(1)}, u32[]{:S(2)}, u32[]{:S(2)}) collective-permute-start(f32[2,256,128]{2,1,0:T(8,128)S(1)} %get-tuple-element.37.partial), channel_id=1, source_target_pairs={{0,2},{2,0},{4,6},{6,4},{8,10},{10,8},{12,14},{14,12},{1,3},{3,1},... | collective-permute-start | bytes 786440 | tf_op jit(solution)/shard_map/ppermute | solution.py:371
  57.9 7.1 %collective-permute-start.17 = (f32[8,128]{1,0:T(8,128)S(1)}, f32[8,128]{1,0:T(8,128)S(1)}, u32[]{:S(2)}, u32[]{:S(2)}) collective-permute-start(f32[8,128]{1,0:T(8,128)S(1)} %get-tuple-element.39), channel_id=1, source_target_pairs={{0,4},{2,6},{4,8},{6,10},{8,12},{10,14},{12,0},{14,2},{1,5},{3,7},... | collective-permute-start | bytes 12296 | tf_op jit(solution)/shard_map/ppermute | solution.py:386
  58.3 6.8 %collective-permute-start.18 = (f32[8,128]{1,0:T(8,128)S(1)}, f32[8,128]{1,0:T(8,128)S(1)}, u32[]{:S(2)}, u32[]{:S(2)}) collective-permute-start(f32[8,128]{1,0:T(8,128)S(1)} %get-tuple-element.39), channel_id=1, source_target_pairs={{0,8},{2,10},{4,12},{6,14},{8,0},{10,2},{12,4},{14,6},{1,9},{3,11}... | collective-permute-start | bytes 12296 | tf_op jit(solution)/shard_map/ppermute | solution.py:386
  61.1 4.0 %collective-permute-start.19 = (f32[8,128]{1,0:T(8,128)S(1)}, f32[8,128]{1,0:T(8,128)S(1)}, u32[]{:S(2)}, u32[]{:S(2)}) collective-permute-start(f32[8,128]{1,0:T(8,128)S(1)} %get-tuple-element.39), channel_id=1, source_target_pairs={{0,12},{2,14},{4,0},{6,2},{8,4},{10,6},{12,8},{14,10},{1,13},{3,15... | collective-permute-start | bytes 12296 | tf_op jit(solution)/shard_map/ppermute | solution.py:386
  62.4 4.9 %collective-permute-start.21 = (f32[128,128]{1,0:T(8,128)S(1)}, f32[128,128]{1,0:T(8,128)S(1)}, u32[]{:S(2)}, u32[]{:S(2)}) collective-permute-start(f32[128,128]{1,0:T(8,128)S(1)} %get-tuple-element.41), channel_id=1, source_target_pairs={{0,1},{1,0},{2,3},{3,2},{4,5},{5,4},{6,7},{7,6},{8,9},{9,8},{10,11... | collective-permute-start | bytes 196616 | tf_op jit(solution)/shard_map/ppermute | solution.py:384
  65.1 3.7 %collective-permute-start.20 = (f32[8,128]{1,0:T(8,128)S(1)}, f32[8,128]{1,0:T(8,128)S(1)}, u32[]{:S(2)}, u32[]{:S(2)}) collective-permute-start(f32[8,128]{1,0:T(8,128)S(1)} %select_maximum_fusion.own), channel_id=1, source_target_pairs={{0,1},{1,0},{2,3},{3,2},{4,5},{5,4},{6,7},{7,6},{8,9},{9,8},{10,11... | collective-permute-start | bytes 12296 | tf_op jit(solution)/shard_map/ppermute | solution.py:392

commit v9 on v8

--- a/solution.py
+++ b/solution.py
@@ -11,6 +11,7 @@
 FLOOR = -1e30
 LANES = 128
 VMEM_LIMIT = 8 * 1024 * 1024
+SCHEDULING_WEIGHT = 20 * 10**9
 
 
 def sin_cos(angle):
@@ -42,6 +43,10 @@
 def panel_kernel(spot, sides, own, given):
     own[...] = sides[spot[2]]
     given[...] = sides[1 - spot[2]]
+
+
+def square_kernel(own, squares):
+    squares[...] = own[...] * own[...]
 
 
 def row_kernel(spot, planes, defocus, lists, kept, given, facts, focus, named, sems):
@@ -69,7 +74,7 @@
     return jnp.concatenate([m[...].astype(jnp.float32).T[: m.shape[0]] for m in meta], axis=0)
 
 
-def add_scores(rows, noise, own_panel, mate_panel, turn_sin, turn_cos, sums, segments):
+def add_scores(rows, noise, own_panel, own_squares, mate_panel, turn_sin, turn_cos, sums, segments):
     columns = noise.shape[1]
     width = columns // segments
     tiles = width // LANES
@@ -100,8 +105,11 @@
         energy = jnp.concatenate(energy_parts, axis=1)
         contract = (((1,), (1,)), ((), ()))
         whole = pl.ds(start, width)
-        for values, total in ((own_panel[:, whole], sums[0]), (mate_panel[:, whole], sums[1])):
-            squared = values * values
+        mate = mate_panel[:, whole]
+        for values, squared, total in (
+            (own_panel[:, whole], own_squares[:, whole], sums[0]),
+            (mate, mate * mate, sums[1]),
+        ):
             correlate = lax.dot_general(
                 values, scaled, contract, preferred_element_type=jnp.float32
             )
@@ -115,10 +123,10 @@
 
 def batch_kernel(n, segments, spot, *refs):
     rows = refs[:n]
-    noise, own_panel, mate_panel = refs[n : n + 3]
-    own_out, mate_out, fact_out, turn_sin, turn_cos, *sums = refs[n + 3 :]
+    noise, own_panel, own_squares, mate_panel = refs[n : n + 4]
+    own_out, mate_out, fact_out, turn_sin, turn_cos, *sums = refs[n + 4 :]
     fact_out[...] = add_scores(
-        rows, noise, own_panel, mate_panel, turn_sin, turn_cos, sums, segments
+        rows, noise, own_panel, own_squares, mate_panel, turn_sin, turn_cos, sums, segments
     )
     own_out[...] = sums[0][...].T
     mate_out[...] = sums[1][...].T
@@ -126,12 +134,12 @@
 
 def last_kernel(n, segments, orders, spot, *refs):
     rows = refs[:n]
-    noise, own_panel, mate_panel = refs[n : n + 3]
-    rest = refs[n + 3 :]
+    noise, own_panel, own_squares, mate_panel = refs[n : n + 4]
+    rest = refs[n + 4 :]
     earlier, rest = rest[: 3 * (len(orders) - 1)], rest[3 * (len(orders) - 1) :]
     partial, facts, turn_sin, turn_cos, *sums = rest
     last_facts = add_scores(
-        rows, noise, own_panel, mate_panel, turn_sin, turn_cos, sums, segments
+        rows, noise, own_panel, own_squares, mate_panel, turn_sin, turn_cos, sums, segments
     )
     position, core = spot[1], spot[2]
     each = rows[0].shape[0]
@@ -154,7 +162,7 @@
             facts[pl.ds(start, each), :] = fact[piece]
 
 
-def score_call(chunks, orders, earlier, spot, noise, own_panel, mate_panel):
+def score_call(chunks, orders, earlier, spot, noise, own_panel, squares, mate_panel):
     each = chunks[0].shape[0]
     orientations, columns = own_panel.shape
     whole = columns // LANES
@@ -179,7 +187,7 @@
     vmem = pl.BlockSpec(memory_space=pltpu.VMEM)
     return pl.pallas_call(
         kernel,
-        in_specs=[pl.BlockSpec(memory_space=pltpu.SMEM)] + [vmem] * (n + 3 + len(extra)),
+        in_specs=[pl.BlockSpec(memory_space=pltpu.SMEM)] + [vmem] * (n + 4 + len(extra)),
         out_specs=[vmem] * len(out_shape),
         out_shape=out_shape,
         scratch_shapes=scratch,
@@ -189,7 +197,7 @@
             bytes_accessed=4 * orientations * columns + 2 * count * columns,
             transcendentals=0,
         ),
-    )(spot, *chunks, noise, own_panel, mate_panel, *extra)
+    )(spot, *chunks, noise, own_panel, squares, mate_panel, *extra)
 
 
 def names_block(facts, search, block):
@@ -323,6 +331,7 @@
     with jax.named_scope("mate_rows"):
         got = lax.ppermute(given, "orient", mate_pairs)
 
+    _, panels = lax.optimization_barrier((kept, panels))
     sides = lax.optimization_barrier(jnp.transpose(panels[0, 0], (1, 0, 2)))
     panel_shape = jax.ShapeDtypeStruct(sides.shape[1:], sides.dtype)
     own_panel, given_panel = pl.pallas_call(
@@ -340,7 +349,15 @@
     ahead = {False: kept, True: given}
     behind = {False: kept, True: given}
     orders, earlier, late = [], [], []
-    score = lambda c: score_call(c, None, None, spot, noise, own_panel, mate_panel)
+    squares = pl.pallas_call(
+        square_kernel,
+        in_specs=[vmem],
+        out_specs=vmem,
+        out_shape=panel_shape,
+        compiler_params=params,
+        cost_estimate=pl.CostEstimate(flops=SCHEDULING_WEIGHT, bytes_accessed=0, transcendentals=0),
+    )(own_panel)
+    score = lambda c: score_call(c, None, None, spot, noise, own_panel, squares, mate_panel)
     for step in range(1, chips + 1):
         if step == chips and step > 2:
             orders.append([key for key, _ in waiting])
@@ -349,6 +366,9 @@
             tie = earlier[-1][2]
             ahead = {c: lax.optimization_barrier((v, tie))[0] for c, v in ahead.items()}
             behind = {c: lax.optimization_barrier((v, tie))[0] for c, v in behind.items()}
+        if step == 2:
+            for chain, c in ((ahead, False), (behind, True)):
+                chain[c] = lax.optimization_barrier((chain[c], squares))[0]
         waiting = waiting + late
         late = []
         for crossed in (False, True):
@@ -365,7 +385,7 @@
     waiting = late
     orders.append([key for key, _ in waiting])
     partial, all_facts = score_call(
-        [c for _, c in waiting], orders, earlier, spot, noise, own_panel, mate_panel
+        [c for _, c in waiting], orders, earlier, spot, noise, own_panel, squares, mate_panel
     )
 
     mate_partial = lax.ppermute(partial, "orient", mate_pairs)

time: 69.7 us -> 64.3 us (0.923)
  waiting for transfers between devices: 21.8 us -> 12.4 us
  starting transfers between devices: 24.7 us -> 29.7 us
  local copies, waits for them, and re-layouts: 6.37 us -> 4.85 us
    ppermute x14, waiting for transfers between devices: 19 us -> 9.14 us  [forward(): return lax.ppermute(values, ('orient', 'cls'), pairs)]
    ppermute x14, starting transfers between devices: 14.9 us -> 18.8 us  [forward(): return lax.ppermute(values, ('orient', 'cls'), pairs)]
    unnamed x12 -> x7, local copies, waits for them, and re-layouts: 6.35 us -> 2.41 us
    optimization_barrier x0 -> x1, local copies, waits for them, and re-layouts: none -> 2.42 us  [chip_shards(): _, panels = lax.optimization_barrier((kept, panels))]
    ppermute x3, starting transfers between devices: 4.5 us -> 5.68 us  [chip_shards(): lax.ppermute(stats, 'orient', [(d, (d + 2 * s) % devices) for d in range(...]
    ppermute x1, starting transfers between devices: 2.62 us -> 1.61 us  [chip_shards(): from_x = lax.ppermute(across, 'cls', x_pairs)]
    ppermute x3, waiting for transfers between devices: 0.01 us -> 0.73 us  [chip_shards(): lax.ppermute(stats, 'orient', [(d, (d + 2 * s) % devices) for d in range(...]
  transfers between devices with their start and end apart: 22 -> 22, of which waited for: 9 -> 12; matrix products, arithmetic and copies ran while one was open for 0% -> 4% of each run, Pallas kernels for 15% -> 17%
where the time goes in v9:
time: 64.3 us; the launch traced here: 64.1 us
  starting transfers between devices  29.7 us (46%)
  Pallas kernels  16.9 us (26%)
  waiting for transfers between devices  12.4 us (19%)
  local copies, waits for them, and re-layouts  4.85 us (8%)
    ppermute x14, starting transfers between devices, forward(): return lax.ppermute(values, ('orient', 'cls'), pairs)  18.8 us
    pallas_call x3, Pallas kernels, score_call(): pl.pallas_call(kernel, in_specs=[pl.BlockSpec(memory_space=pltpu.SMEM)] +...  12.6 us
    ppermute x14, waiting for transfers between devices, forward(): return lax.ppermute(values, ('orient', 'cls'), pairs)  9.14 us
    ppermute x3, starting transfers between devices, chip_shards(): lax.ppermute(stats, 'orient', [(d, (d + 2 * s) % devices) for d in range(...  5.68 us
    optimization_barrier x1, local copies, waits for them, and re-layouts, chip_shards(): _, panels = lax.optimization_barrier((kept, panels))  2.42 us
    unnamed x7, local copies, waits for them, and re-layouts  2.41 us
    ppermute x1, starting transfers between devices, chip_shards(): from_x = lax.ppermute(across, 'cls', x_pairs)  1.61 us
    ppermute x1, starting transfers between devices, chip_shards(): other_stats = lax.ppermute(class_stats, 'cls', x_pairs)  1.59 us
  transfers between devices with their start and end apart: 22, of which 12 were waited for; matrix products, arithmetic and copies ran while one was open for 4% of the time, Pallas kernels for 17%

profile of v9, /device:TPU:0, one launch (start us, length us, event | category | flops | bytes accessed | tf_op | source)
XLA Modules:
  0.0 64.1 jit_solution(1844713596346613452)
XLA Ops:
  0.0 1.1 %copy.11 = bf16[1,16,2,7296]{3,1,2,0:T(8,128)(2,1)S(1)} copy(bf16[1,16,2,7296]{3,2,1,0:T(2,128)(2,1)} %param.5) | data formatting | bytes 933888 | tf_op args[0]
  1.1 0.1 pad_add_fusion.spot
  1.2 0.7 %copy-done = s32[1,16,4]{1,2,0:T(4,128)S(1)} copy-done((s32[1,16,4]{1,2,0:T(4,128)S(1)}, s32[1,16,4]{1,2,0:T(4,128)}, u32[]{:S(2)}) %copy-start) | copy-done | bytes 280
  1.9 0.7 %copy-done.1 = bf16[1,16]{1,0:T(2,128)(2,1)S(1)} copy-done((bf16[1,16]{1,0:T(2,128)(2,1)S(1)}, bf16[1,16]{1,0:T(2,128)(2,1)}, u32[]{:S(2)}) %copy-start.1) | copy-done | bytes 56
  2.5 0.6 shard_map.55
  3.1 2.4 %collective-permute-start.6 = (bf16[16,7424]{1,0:T(8,128)(2,1)S(1)}, bf16[16,7424]{1,0:T(8,128)(2,1)S(1)}, u32[]{:S(2)}, u32[]{:S(2)}) collective-permute-start(bf16[16,7424]{1,0:T(8,128)(2,1)S(1)} %get-tuple-element.32), channel_id=1, source_target_pairs={{0,3},{2,1},{4,2},{6,0},{8,6},{10,4},{12,10},{14,8},{13,14},{15,12... | collective-permute-start | bytes 712712 | tf_op jit(solution)/shard_map/rows_behind/ppermute | solution.py:311
  5.6 0.7 %collective-permute-start = (bf16[16,7424]{1,0:T(8,128)(2,1)S(1)}, bf16[16,7424]{1,0:T(8,128)(2,1)S(1)}, u32[]{:S(2)}, u32[]{:S(2)}) collective-permute-start(bf16[16,7424]{1,0:T(8,128)(2,1)S(1)} %get-tuple-element.28.refs_0_), channel_id=1, source_target_pairs={{0,4},{2,6},{4,8},{6,10},{8,12},{10,14},{12,13},{14,15},{13,9},{15... | collective-permute-start | bytes 712712 | tf_op jit(solution)/shard_map/rows_ahead/ppermute | solution.py:311
  6.3 1.3 %collective-permute-start.4 = (bf16[16,7424]{1,0:T(8,128)(2,1)S(1)}, bf16[16,7424]{1,0:T(8,128)(2,1)S(1)}, u32[]{:S(2)}, u32[]{:S(2)}) collective-permute-start(bf16[16,7424]{1,0:T(8,128)(2,1)S(1)} %get-tuple-element.28.refs_0_), channel_id=1, source_target_pairs={{0,1},{2,3},{4,0},{6,2},{8,4},{10,6},{12,8},{14,10},{13,12},{15,14... | collective-permute-start | bytes 712712 | tf_op jit(solution)/shard_map/rows_behind/ppermute | solution.py:311
  7.6 0.1 collective-permute-start.5
  7.7 0.7 %collective-permute-start.3 = (bf16[16,7424]{1,0:T(8,128)(2,1)S(1)}, bf16[16,7424]{1,0:T(8,128)(2,1)S(1)}, u32[]{:S(2)}, u32[]{:S(2)}) collective-permute-start(bf16[16,7424]{1,0:T(8,128)(2,1)S(1)} %get-tuple-element.32), channel_id=1, source_target_pairs={{0,2},{2,0},{4,6},{6,4},{8,10},{10,8},{12,14},{14,12},{1,3},{3,1},... | collective-permute-start | bytes 712712 | tf_op jit(solution)/shard_map/mate_rows/ppermute | solution.py:332
  8.4 2.4 %copy.10 = bf16[1,1,128,2,7296]{4,2,3,1,0:T(8,128)(2,1)S(1)} copy(bf16[1,1,128,2,7296]{4,3,2,1,0:T(2,128)(2,1)} %param.9) | data formatting | bytes 7471104 | tf_op jit(solution)/shard_map/optimization_barrier | solution.py:334
  10.8 0.8 %shard_map.56 = (bf16[128,7296]{1,0:T(8,128)(2,1)S(1)}, bf16[128,7296]{1,0:T(8,128)(2,1)S(1)}) custom-call(s32[4]{0:T(128)S(1)} %pad_add_fusion.spot, bf16[2,128,7296]{2,1,0:T(8,128)(2,1)S(1)} %bitcast.18), custom_call_target="tpu_custom_call" | custom-call | tf_op jit(solution)/shard_map/pallas_call | solution.py:337
  11.6 0.1 collective-permute-done.6.refs_5_
  11.7 1.2 %collective-permute-start.10 = (bf16[128,7296]{1,0:T(8,128)(2,1)S(1)}, bf16[128,7296]{1,0:T(8,128)(2,1)S(1)}, u32[]{:S(2)}, u32[]{:S(2)}) collective-permute-start(bf16[128,7296]{1,0:T(8,128)(2,1)S(1)} %get-tuple-element.34), channel_id=1, source_target_pairs={{0,2},{2,0},{4,6},{6,4},{8,10},{10,8},{12,14},{14,12},{1,3},{3,1},... | collective-permute-start | bytes 5603336 | tf_op jit(solution)/shard_map/mate_panel/ppermute | solution.py:345
  12.9 0.1 shard_map.57.refs_12_.refs_6_.refs_4_
  13.1 1.2 %collective-permute-done.refs_2_ = bf16[16,7424]{1,0:T(8,128)(2,1)S(1)} collective-permute-done((bf16[16,7424]{1,0:T(8,128)(2,1)S(1)}, bf16[16,7424]{1,0:T(8,128)(2,1)S(1)}, u32[]{:S(2)}, u32[]{:S(2)}) %collective-permute-start) | collective-permute-done | bytes 237600 | tf_op jit(solution)/shard_map/rows_ahead/ppermute | solution.py:311
  14.2 1.6 %collective-permute-start.9 = (bf16[16,7424]{1,0:T(8,128)(2,1)S(1)}, bf16[16,7424]{1,0:T(8,128)(2,1)S(1)}, u32[]{:S(2)}, u32[]{:S(2)}) collective-permute-start(bf16[16,7424]{1,0:T(8,128)(2,1)S(1)} %collective-permute-done.6.refs_5_), channel_id=1, source_target_pairs={{0,1},{2,3},{4,0},{6,2},{8,4},{10,6},{12,8},{14,10},{13,12},{15,14... | collective-permute-start | bytes 712712 | tf_op jit(solution)/shard_map/rows_behind/ppermute | solution.py:311
  15.8 2.0 %collective-permute-done.4.refs_3_ = bf16[16,7424]{1,0:T(8,128)(2,1)S(1)} collective-permute-done((bf16[16,7424]{1,0:T(8,128)(2,1)S(1)}, bf16[16,7424]{1,0:T(8,128)(2,1)S(1)}, u32[]{:S(2)}, u32[]{:S(2)}) %collective-permute-start.4) | collective-permute-done | bytes 237600 | tf_op jit(solution)/shard_map/rows_behind/ppermute | solution.py:311
  17.7 1.8 %collective-permute-start.1 = (bf16[16,7424]{1,0:T(8,128)(2,1)S(1)}, bf16[16,7424]{1,0:T(8,128)(2,1)S(1)}, u32[]{:S(2)}, u32[]{:S(2)}) collective-permute-start(bf16[16,7424]{1,0:T(8,128)(2,1)S(1)} %collective-permute-done.refs_2_), channel_id=1, source_target_pairs={{0,4},{2,6},{4,8},{6,10},{8,12},{10,14},{12,13},{14,15},{13,9},{15... | collective-permute-start | bytes 712712 | tf_op jit(solution)/shard_map/rows_ahead/ppermute | solution.py:311
  19.5 0.8 %collective-permute-start.7 = (bf16[16,7424]{1,0:T(8,128)(2,1)S(1)}, bf16[16,7424]{1,0:T(8,128)(2,1)S(1)}, u32[]{:S(2)}, u32[]{:S(2)}) collective-permute-start(bf16[16,7424]{1,0:T(8,128)(2,1)S(1)} %collective-permute-done.4.refs_3_), channel_id=1, source_target_pairs={{0,1},{2,3},{4,0},{6,2},{8,4},{10,6},{12,8},{14,10},{13,12},{15,14... | collective-permute-start | bytes 712712 | tf_op jit(solution)/shard_map/rows_behind/ppermute | solution.py:311
  20.3 1.2 %collective-permute-start.8 = (bf16[16,7424]{1,0:T(8,128)(2,1)S(1)}, bf16[16,7424]{1,0:T(8,128)(2,1)S(1)}, u32[]{:S(2)}, u32[]{:S(2)}) collective-permute-start(bf16[16,7424]{1,0:T(8,128)(2,1)S(1)} %collective-permute-done.5.refs_4_), channel_id=1, source_target_pairs={{0,4},{2,6},{4,8},{6,10},{8,12},{10,14},{12,13},{14,15},{13,9},{15... | collective-permute-start | bytes 712712 | tf_op jit(solution)/shard_map/rows_ahead/ppermute | solution.py:311
  21.5 1.0 %collective-permute-done.9.refs_9_ = bf16[16,7424]{1,0:T(8,128)(2,1)S(1)} collective-permute-done((bf16[16,7424]{1,0:T(8,128)(2,1)S(1)}, bf16[16,7424]{1,0:T(8,128)(2,1)S(1)}, u32[]{:S(2)}, u32[]{:S(2)}) %collective-permute-start.9) | collective-permute-done | bytes 237600 | tf_op jit(solution)/shard_map/rows_behind/ppermute | solution.py:311
  22.5 2.0 %collective-permute-start.12 = (bf16[16,7424]{1,0:T(8,128)(2,1)S(1)}, bf16[16,7424]{1,0:T(8,128)(2,1)S(1)}, u32[]{:S(2)}, u32[]{:S(2)}) collective-permute-start(bf16[16,7424]{1,0:T(8,128)(2,1)S(1)} %collective-permute-done.9.refs_9_), channel_id=1, source_target_pairs={{0,1},{2,3},{4,0},{6,2},{8,4},{10,6},{12,8},{14,10},{13,12},{15,14... | collective-permute-start | bytes 712712 | tf_op jit(solution)/shard_map/rows_behind/ppermute | solution.py:311
  24.5 1.9 %collective-permute-done.1.refs_6_ = bf16[16,7424]{1,0:T(8,128)(2,1)S(1)} collective-permute-done((bf16[16,7424]{1,0:T(8,128)(2,1)S(1)}, bf16[16,7424]{1,0:T(8,128)(2,1)S(1)}, u32[]{:S(2)}, u32[]{:S(2)}) %collective-permute-start.1) | collective-permute-done | bytes 237600 | tf_op jit(solution)/shard_map/rows_ahead/ppermute | solution.py:311
  26.4 1.8 %collective-permute-start.2 = (bf16[16,7424]{1,0:T(8,128)(2,1)S(1)}, bf16[16,7424]{1,0:T(8,128)(2,1)S(1)}, u32[]{:S(2)}, u32[]{:S(2)}) collective-permute-start(bf16[16,7424]{1,0:T(8,128)(2,1)S(1)} %collective-permute-done.1.refs_6_), channel_id=1, source_target_pairs={{0,4},{2,6},{4,8},{6,10},{8,12},{10,14},{12,13},{14,15},{13,9},{15... | collective-permute-start | bytes 712712 | tf_op jit(solution)/shard_map/rows_ahead/ppermute | solution.py:311
  28.2 1.4 %collective-permute-start.14 = (bf16[16,7424]{1,0:T(8,128)(2,1)S(1)}, bf16[16,7424]{1,0:T(8,128)(2,1)S(1)}, u32[]{:S(2)}, u32[]{:S(2)}) collective-permute-start(bf16[16,7424]{1,0:T(8,128)(2,1)S(1)} %collective-permute-done.7.refs_7_), channel_id=1, source_target_pairs={{0,1},{2,3},{4,0},{6,2},{8,4},{10,6},{12,8},{14,10},{13,12},{15,14... | collective-permute-start | bytes 712712 | tf_op jit(solution)/shard_map/rows_behind/ppermute | solution.py:311
  29.6 1.9 %collective-permute-done.8.refs_8_ = bf16[16,7424]{1,0:T(8,128)(2,1)S(1)} collective-permute-done((bf16[16,7424]{1,0:T(8,128)(2,1)S(1)}, bf16[16,7424]{1,0:T(8,128)(2,1)S(1)}, u32[]{:S(2)}, u32[]{:S(2)}) %collective-permute-start.8) | collective-permute-done | bytes 237600 | tf_op jit(solution)/shard_map/rows_ahead/ppermute | solution.py:311
  31.5 1.8 %collective-permute-start.15 = (bf16[16,7424]{1,0:T(8,128)(2,1)S(1)}, bf16[16,7424]{1,0:T(8,128)(2,1)S(1)}, u32[]{:S(2)}, u32[]{:S(2)}) collective-permute-start(bf16[16,7424]{1,0:T(8,128)(2,1)S(1)} %collective-permute-done.8.refs_8_), channel_id=1, source_target_pairs={{0,4},{2,6},{4,8},{6,10},{8,12},{10,14},{12,13},{14,15},{13,9},{15... | collective-permute-start | bytes 712712 | tf_op jit(solution)/shard_map/rows_ahead/ppermute | solution.py:311
  33.3 5.4 %shard_map.58 = (f32[160,128]{1,0:T(8,128)S(1)}, f32[160,128]{1,0:T(8,128)S(1)}, f32[160,128]{1,0:T(8,128)S(1)}) custom-call(s32[4]{0:T(128)S(1)} %pad_add_fusion.spot, bf16[16,7424]{1,0:T(8,128)(2,1)S(1)} %get-tuple-element.28.refs_0_, bf16[16,7424]{1,0:T(8,128)(2,1)S(1)} %collective-permute-done.3.refs_1_, ...), custom_call_target="tpu_custom_call" | custom-call | flops 1195376640 | bytes 6070272 | tf_op jit(solution)/shard_map/pallas_call | solution.py:188
  38.7 0.3 collective-permute-start.13
  39.1 1.8 %collective-permute-start.11 = (bf16[16,7424]{1,0:T(8,128)(2,1)S(1)}, bf16[16,7424]{1,0:T(8,128)(2,1)S(1)}, u32[]{:S(2)}, u32[]{:S(2)}) collective-permute-start(bf16[16,7424]{1,0:T(8,128)(2,1)S(1)} %collective-permute-done.2.refs_0_), channel_id=1, source_target_pairs={{0,4},{2,6},{4,8},{6,10},{8,12},{10,14},{12,13},{14,15},{13,9},{15... | collective-permute-start | bytes 712712 | tf_op jit(solution)/shard_map/rows_ahead/ppermute | solution.py:311
  40.8 0.9 %collective-permute-done.15.refs_2_ = bf16[16,7424]{1,0:T(8,128)(2,1)S(1)} collective-permute-done((bf16[16,7424]{1,0:T(8,128)(2,1)S(1)}, bf16[16,7424]{1,0:T(8,128)(2,1)S(1)}, u32[]{:S(2)}, u32[]{:S(2)}) %collective-permute-start.15) | collective-permute-done | bytes 237600 | tf_op jit(solution)/shard_map/rows_ahead/ppermute | solution.py:311
  41.7 3.8 %shard_map.59 = (f32[64,128]{1,0:T(8,128)S(1)}, f32[64,128]{1,0:T(8,128)S(1)}, f32[64,128]{1,0:T(8,128)S(1)}) custom-call(s32[4]{0:T(128)S(1)} %pad_add_fusion.spot, bf16[16,7424]{1,0:T(8,128)(2,1)S(1)} %collective-permute-done.2.refs_0_, bf16[16,7424]{1,0:T(8,128)(2,1)S(1)} %collective-permute-done.14.refs_1_, ...), custom_call_target="tpu_custom_call" | custom-call | flops 956301312 | bytes 4669440 | tf_op jit(solution)/shard_map/pallas_call | solution.py:188
  45.5 0.2 collective-permute-done.11.refs_0_
  45.7 3.4 %shard_map.60 = (f32[2,256,128]{2,1,0:T(8,128)S(1)}, f32[256,128]{1,0:T(8,128)S(1)}) custom-call(s32[4]{0:T(128)S(1)} %pad_add_fusion.spot, bf16[16,7424]{1,0:T(8,128)(2,1)S(1)} %collective-permute-done.11.refs_0_, bf16[16,7424]{1,0:T(8,128)(2,1)S(1)} %collective-permute-done.13.refs_1_, f32[1,7296]{1,0:T(1,128)S(1)} %broadcast_in_dim.3.refs_10_.refs_4_.refs_2_, ...), custom_call_target="tpu_custom_call" | custom-call | flops 956301312 | bytes 4202496 | tf_op jit(solution)/shard_map/pallas_call | solution.py:188
  49.1 0.1 collective-permute-start.16
  49.2 1.5 %collective-permute-done.16.mate = f32[2,256,128]{2,1,0:T(8,128)S(1)} collective-permute-done((f32[2,256,128]{2,1,0:T(8,128)S(1)}, f32[2,256,128]{2,1,0:T(8,128)S(1)}, u32[]{:S(2)}, u32[]{:S(2)}) %collective-permute-start.16) | collective-permute-done | bytes 262176 | tf_op jit(solution)/shard_map/ppermute | solution.py:391
  50.7 0.9 %shard_map.61 = (f32[128,128]{1,0:T(8,128)S(1)}, f32[128,128]{1,0:T(8,128)S(1)}, f32[8,128]{1,0:T(8,128)S(1)}) custom-call(s32[4]{0:T(128)S(1)} %pad_add_fusion.spot, f32[2,256,128]{2,1,0:T(8,128)S(1)} %get-tuple-element.43.partial, f32[2,256,128]{2,1,0:T(8,128)S(1)} %collective-permute-done.16.mate, f32[256,128]{1,0:T(8,128)S(1)} %get-tuple-element.44.facts), custom_call_target="tpu_custom_call" | custom-call | tf_op jit(solution)/shard_map/pallas_call | solution.py:392
  51.6 1.7 %collective-permute-start.17 = (f32[8,128]{1,0:T(8,128)S(1)}, f32[8,128]{1,0:T(8,128)S(1)}, u32[]{:S(2)}, u32[]{:S(2)}) collective-permute-start(f32[8,128]{1,0:T(8,128)S(1)} %get-tuple-element.45), channel_id=1, source_target_pairs={{0,4},{2,6},{4,8},{6,10},{8,12},{10,14},{12,0},{14,2},{1,5},{3,7},... | collective-permute-start | bytes 12296 | tf_op jit(solution)/shard_map/ppermute | solution.py:406
  53.3 2.7 %collective-permute-start.18 = (f32[8,128]{1,0:T(8,128)S(1)}, f32[8,128]{1,0:T(8,128)S(1)}, u32[]{:S(2)}, u32[]{:S(2)}) collective-permute-start(f32[8,128]{1,0:T(8,128)S(1)} %get-tuple-element.45), channel_id=1, source_target_pairs={{0,8},{2,10},{4,12},{6,14},{8,0},{10,2},{12,4},{14,6},{1,9},{3,11}... | collective-permute-start | bytes 12296 | tf_op jit(solution)/shard_map/ppermute | solution.py:406
  56.0 1.3 %collective-permute-start.19 = (f32[8,128]{1,0:T(8,128)S(1)}, f32[8,128]{1,0:T(8,128)S(1)}, u32[]{:S(2)}, u32[]{:S(2)}) collective-permute-start(f32[8,128]{1,0:T(8,128)S(1)} %get-tuple-element.45), channel_id=1, source_target_pairs={{0,12},{2,14},{4,0},{6,2},{8,4},{10,6},{12,8},{14,10},{1,13},{3,15... | collective-permute-start | bytes 12296 | tf_op jit(solution)/shard_map/ppermute | solution.py:406
  57.3 1.6 %collective-permute-start.21 = (f32[128,128]{1,0:T(8,128)S(1)}, f32[128,128]{1,0:T(8,128)S(1)}, u32[]{:S(2)}, u32[]{:S(2)}) collective-permute-start(f32[128,128]{1,0:T(8,128)S(1)} %get-tuple-element.47), channel_id=1, source_target_pairs={{0,1},{1,0},{2,3},{3,2},{4,5},{5,4},{6,7},{7,6},{8,9},{9,8},{10,11... | collective-permute-start | bytes 196616 | tf_op jit(solution)/shard_map/ppermute | solution.py:404
  58.9 0.7 %collective-permute-done.19 = f32[8,128]{1,0:T(8,128)S(1)} collective-permute-done((f32[8,128]{1,0:T(8,128)S(1)}, f32[8,128]{1,0:T(8,128)S(1)}, u32[]{:S(2)}, u32[]{:S(2)}) %collective-permute-start.19) | collective-permute-done | bytes 4128 | tf_op jit(solution)/shard_map/ppermute | solution.py:406
  59.6 1.6 %collective-permute-start.20 = (f32[8,128]{1,0:T(8,128)S(1)}, f32[8,128]{1,0:T(8,128)S(1)}, u32[]{:S(2)}, u32[]{:S(2)}) collective-permute-start(f32[8,128]{1,0:T(8,128)S(1)} %select_maximum_fusion.own), channel_id=1, source_target_pairs={{0,1},{1,0},{2,3},{3,2},{4,5},{5,4},{6,7},{7,6},{8,9},{9,8},{10,11... | collective-permute-start | bytes 12296 | tf_op jit(solution)/shard_map/ppermute | solution.py:412
  61.2 0.3 collective-permute-done.21.across
  61.5 1.1 %shard_map.62 = (f32[128,256]{1,0:T(8,128)S(1)}, f32[128,128]{1,0:T(8,128)S(1)}, f32[8,128]{1,0:T(8,128)S(1)}) custom-call(s32[4]{0:T(128)S(1)} %pad_add_fusion.spot, f32[128,128]{1,0:T(8,128)S(1)} %get-tuple-element.46.mine, f32[128,128]{1,0:T(8,128)S(1)} %collective-permute-done.21.across, f32[256,128]{1,0:T(8,128)S(1)} %get-tuple-element.44.facts), custom_call_target="tpu_custom_call" | custom-call | tf_op jit(solution)/shard_map/pallas_call | solution.py:413
  62.6 0.7 %collective-permute-done.20.other = f32[8,128]{1,0:T(8,128)S(1)} collective-permute-done((f32[8,128]{1,0:T(8,128)S(1)}, f32[8,128]{1,0:T(8,128)S(1)}, u32[]{:S(2)}, u32[]{:S(2)}) %collective-permute-start.20) | collective-permute-done | bytes 4128 | tf_op jit(solution)/shard_map/ppermute | solution.py:412
  63.3 0.8 %shard_map.63 = f32[128,256]{1,0:T(8,128)} custom-call(f32[8,128]{1,0:T(8,128)S(1)} %select_maximum_fusion.own, f32[8,128]{1,0:T(8,128)S(1)} %collective-permute-done.20.other, f32[8,128]{1,0:T(8,128)S(1)} %get-tuple-element.48.tops, f32[128,256]{1,0:T(8,128)S(1)} %get-tuple-element.49.slots, f32[128,128]{1,0:T(8,128)S(1)} %get-tuple-element.50.chosen), custom_call_target="tpu_custom_call" | custom-call | tf_op jit(solution)/shard_map/pallas_call | solution.py:424
  (17 shorter events, 0.1 us)
Async XLA Ops:
  1.2 0.7 %copy-start = (s32[1,16,4]{1,2,0:T(4,128)S(1)}, s32[1,16,4]{1,2,0:T(4,128)}, u32[]{:S(2)}) copy-start(s32[1,16,4]{1,2,0:T(4,128)} %param.7) | copy-start | bytes 772
  1.9 0.7 %copy-start.1 = (bf16[1,16]{1,0:T(2,128)(2,1)S(1)}, bf16[1,16]{1,0:T(2,128)(2,1)}, u32[]{:S(2)}) copy-start(bf16[1,16]{1,0:T(2,128)(2,1)} %defocus.1) | copy-start | bytes 100
  3.1 8.6 %collective-permute-start.6 = (bf16[16,7424]{1,0:T(8,128)(2,1)S(1)}, bf16[16,7424]{1,0:T(8,128)(2,1)S(1)}, u32[]{:S(2)}, u32[]{:S(2)}) collective-permute-start(bf16[16,7424]{1,0:T(8,128)(2,1)S(1)} %get-tuple-element.32), channel_id=1, source_target_pairs={{0,3},{2,1},{4,2},{6,0},{8,6},{10,4},{12,10},{14,8},{13,14},{15,12... | collective-permute-start | bytes 712712 | tf_op jit(solution)/shard_map/rows_behind/ppermute | solution.py:311
  5.6 8.7 %collective-permute-start = (bf16[16,7424]{1,0:T(8,128)(2,1)S(1)}, bf16[16,7424]{1,0:T(8,128)(2,1)S(1)}, u32[]{:S(2)}, u32[]{:S(2)}) collective-permute-start(bf16[16,7424]{1,0:T(8,128)(2,1)S(1)} %get-tuple-element.28.refs_0_), channel_id=1, source_target_pairs={{0,4},{2,6},{4,8},{6,10},{8,12},{10,14},{12,13},{14,15},{13,9},{15... | collective-permute-start | bytes 712712 | tf_op jit(solution)/shard_map/rows_ahead/ppermute | solution.py:311
  6.3 11.5 %collective-permute-start.4 = (bf16[16,7424]{1,0:T(8,128)(2,1)S(1)}, bf16[16,7424]{1,0:T(8,128)(2,1)S(1)}, u32[]{:S(2)}, u32[]{:S(2)}) collective-permute-start(bf16[16,7424]{1,0:T(8,128)(2,1)S(1)} %get-tuple-element.28.refs_0_), channel_id=1, source_target_pairs={{0,1},{2,3},{4,0},{6,2},{8,4},{10,6},{12,8},{14,10},{13,12},{15,14... | collective-permute-start | bytes 712712 | tf_op jit(solution)/shard_map/rows_behind/ppermute | solution.py:311
  7.6 11.9 %collective-permute-start.5 = (bf16[16,7424]{1,0:T(8,128)(2,1)S(1)}, bf16[16,7424]{1,0:T(8,128)(2,1)S(1)}, u32[]{:S(2)}, u32[]{:S(2)}) collective-permute-start(bf16[16,7424]{1,0:T(8,128)(2,1)S(1)} %get-tuple-element.32), channel_id=1, source_target_pairs={{0,6},{2,4},{4,10},{6,8},{8,14},{10,12},{12,15},{14,13},{13,11},{1... | collective-permute-start | bytes 712712 | tf_op jit(solution)/shard_map/rows_ahead/ppermute | solution.py:311
  7.7 12.6 %collective-permute-start.3 = (bf16[16,7424]{1,0:T(8,128)(2,1)S(1)}, bf16[16,7424]{1,0:T(8,128)(2,1)S(1)}, u32[]{:S(2)}, u32[]{:S(2)}) collective-permute-start(bf16[16,7424]{1,0:T(8,128)(2,1)S(1)} %get-tuple-element.32), channel_id=1, source_target_pairs={{0,2},{2,0},{4,6},{6,4},{8,10},{10,8},{12,14},{14,12},{1,3},{3,1},... | collective-permute-start | bytes 712712 | tf_op jit(solution)/shard_map/mate_rows/ppermute | solution.py:332
  11.7 21.5 %collective-permute-start.10 = (bf16[128,7296]{1,0:T(8,128)(2,1)S(1)}, bf16[128,7296]{1,0:T(8,128)(2,1)S(1)}, u32[]{:S(2)}, u32[]{:S(2)}) collective-permute-start(bf16[128,7296]{1,0:T(8,128)(2,1)S(1)} %get-tuple-element.34), channel_id=1, source_target_pairs={{0,2},{2,0},{4,6},{6,4},{8,10},{10,8},{12,14},{14,12},{1,3},{3,1},... | collective-permute-start | bytes 5603336 | tf_op jit(solution)/shard_map/mate_panel/ppermute | solution.py:345
  12.9 15.2 %copy-start.2 = (f32[7296]{0:T(1024)S(1)}, f32[7296]{0:T(1024)}, u32[]{:S(2)}) copy-start(f32[7296]{0:T(1024)} %param.8) | copy-start | bytes 87556
  14.2 8.3 %collective-permute-start.9 = (bf16[16,7424]{1,0:T(8,128)(2,1)S(1)}, bf16[16,7424]{1,0:T(8,128)(2,1)S(1)}, u32[]{:S(2)}, u32[]{:S(2)}) collective-permute-start(bf16[16,7424]{1,0:T(8,128)(2,1)S(1)} %collective-permute-done.6.refs_5_), channel_id=1, source_target_pairs={{0,1},{2,3},{4,0},{6,2},{8,4},{10,6},{12,8},{14,10},{13,12},{15,14... | collective-permute-start | bytes 712712 | tf_op jit(solution)/shard_map/rows_behind/ppermute | solution.py:311
  17.7 8.7 %collective-permute-start.1 = (bf16[16,7424]{1,0:T(8,128)(2,1)S(1)}, bf16[16,7424]{1,0:T(8,128)(2,1)S(1)}, u32[]{:S(2)}, u32[]{:S(2)}) collective-permute-start(bf16[16,7424]{1,0:T(8,128)(2,1)S(1)} %collective-permute-done.refs_2_), channel_id=1, source_target_pairs={{0,4},{2,6},{4,8},{6,10},{8,12},{10,14},{12,13},{14,15},{13,9},{15... | collective-permute-start | bytes 712712 | tf_op jit(solution)/shard_map/rows_ahead/ppermute | solution.py:311
  19.5 8.7 %collective-permute-start.7 = (bf16[16,7424]{1,0:T(8,128)(2,1)S(1)}, bf16[16,7424]{1,0:T(8,128)(2,1)S(1)}, u32[]{:S(2)}, u32[]{:S(2)}) collective-permute-start(bf16[16,7424]{1,0:T(8,128)(2,1)S(1)} %collective-permute-done.4.refs_3_), channel_id=1, source_target_pairs={{0,1},{2,3},{4,0},{6,2},{8,4},{10,6},{12,8},{14,10},{13,12},{15,14... | collective-permute-start | bytes 712712 | tf_op jit(solution)/shard_map/rows_behind/ppermute | solution.py:311
  20.3 11.2 %collective-permute-start.8 = (bf16[16,7424]{1,0:T(8,128)(2,1)S(1)}, bf16[16,7424]{1,0:T(8,128)(2,1)S(1)}, u32[]{:S(2)}, u32[]{:S(2)}) collective-permute-start(bf16[16,7424]{1,0:T(8,128)(2,1)S(1)} %collective-permute-done.5.refs_4_), channel_id=1, source_target_pairs={{0,4},{2,6},{4,8},{6,10},{8,12},{10,14},{12,13},{14,15},{13,9},{15... | collective-permute-start | bytes 712712 | tf_op jit(solution)/shard_map/rows_ahead/ppermute | solution.py:311
  22.5 16.2 %collective-permute-start.12 = (bf16[16,7424]{1,0:T(8,128)(2,1)S(1)}, bf16[16,7424]{1,0:T(8,128)(2,1)S(1)}, u32[]{:S(2)}, u32[]{:S(2)}) collective-permute-start(bf16[16,7424]{1,0:T(8,128)(2,1)S(1)} %collective-permute-done.9.refs_9_), channel_id=1, source_target_pairs={{0,1},{2,3},{4,0},{6,2},{8,4},{10,6},{12,8},{14,10},{13,12},{15,14... | collective-permute-start | bytes 712712 | tf_op jit(solution)/shard_map/rows_behind/ppermute | solution.py:311
  26.4 12.6 %collective-permute-start.2 = (bf16[16,7424]{1,0:T(8,128)(2,1)S(1)}, bf16[16,7424]{1,0:T(8,128)(2,1)S(1)}, u32[]{:S(2)}, u32[]{:S(2)}) collective-permute-start(bf16[16,7424]{1,0:T(8,128)(2,1)S(1)} %collective-permute-done.1.refs_6_), channel_id=1, source_target_pairs={{0,4},{2,6},{4,8},{6,10},{8,12},{10,14},{12,13},{14,15},{13,9},{15... | collective-permute-start | bytes 712712 | tf_op jit(solution)/shard_map/rows_ahead/ppermute | solution.py:311
  28.2 12.6 %collective-permute-start.14 = (bf16[16,7424]{1,0:T(8,128)(2,1)S(1)}, bf16[16,7424]{1,0:T(8,128)(2,1)S(1)}, u32[]{:S(2)}, u32[]{:S(2)}) collective-permute-start(bf16[16,7424]{1,0:T(8,128)(2,1)S(1)} %collective-permute-done.7.refs_7_), channel_id=1, source_target_pairs={{0,1},{2,3},{4,0},{6,2},{8,4},{10,6},{12,8},{14,10},{13,12},{15,14... | collective-permute-start | bytes 712712 | tf_op jit(solution)/shard_map/rows_behind/ppermute | solution.py:311
  31.5 10.2 %collective-permute-start.15 = (bf16[16,7424]{1,0:T(8,128)(2,1)S(1)}, bf16[16,7424]{1,0:T(8,128)(2,1)S(1)}, u32[]{:S(2)}, u32[]{:S(2)}) collective-permute-start(bf16[16,7424]{1,0:T(8,128)(2,1)S(1)} %collective-permute-done.8.refs_8_), channel_id=1, source_target_pairs={{0,4},{2,6},{4,8},{6,10},{8,12},{10,14},{12,13},{14,15},{13,9},{15... | collective-permute-start | bytes 712712 | tf_op jit(solution)/shard_map/rows_ahead/ppermute | solution.py:311
  38.7 6.7 %collective-permute-start.13 = (bf16[16,7424]{1,0:T(8,128)(2,1)S(1)}, bf16[16,7424]{1,0:T(8,128)(2,1)S(1)}, u32[]{:S(2)}, u32[]{:S(2)}) collective-permute-start(bf16[16,7424]{1,0:T(8,128)(2,1)S(1)} %collective-permute-done.12.refs_3_), channel_id=1, source_target_pairs={{0,1},{2,3},{4,0},{6,2},{8,4},{10,6},{12,8},{14,10},{13,12},{15,14... | collective-permute-start | bytes 712712 | tf_op jit(solution)/shard_map/rows_behind/ppermute | solution.py:311
  39.1 6.6 %collective-permute-start.11 = (bf16[16,7424]{1,0:T(8,128)(2,1)S(1)}, bf16[16,7424]{1,0:T(8,128)(2,1)S(1)}, u32[]{:S(2)}, u32[]{:S(2)}) collective-permute-start(bf16[16,7424]{1,0:T(8,128)(2,1)S(1)} %collective-permute-done.2.refs_0_), channel_id=1, source_target_pairs={{0,4},{2,6},{4,8},{6,10},{8,12},{10,14},{12,13},{14,15},{13,9},{15... | collective-permute-start | bytes 712712 | tf_op jit(solution)/shard_map/rows_ahead/ppermute | solution.py:311
  49.1 1.6 %collective-permute-start.16 = (f32[2,256,128]{2,1,0:T(8,128)S(1)}, f32[2,256,128]{2,1,0:T(8,128)S(1)}, u32[]{:S(2)}, u32[]{:S(2)}) collective-permute-start(f32[2,256,128]{2,1,0:T(8,128)S(1)} %get-tuple-element.43.partial), channel_id=1, source_target_pairs={{0,2},{2,0},{4,6},{6,4},{8,10},{10,8},{12,14},{14,12},{1,3},{3,1},... | collective-permute-start | bytes 786440 | tf_op jit(solution)/shard_map/ppermute | solution.py:391
  51.6 7.3 %collective-permute-start.17 = (f32[8,128]{1,0:T(8,128)S(1)}, f32[8,128]{1,0:T(8,128)S(1)}, u32[]{:S(2)}, u32[]{:S(2)}) collective-permute-start(f32[8,128]{1,0:T(8,128)S(1)} %get-tuple-element.45), channel_id=1, source_target_pairs={{0,4},{2,6},{4,8},{6,10},{8,12},{10,14},{12,0},{14,2},{1,5},{3,7},... | collective-permute-start | bytes 12296 | tf_op jit(solution)/shard_map/ppermute | solution.py:406
  53.3 5.6 %collective-permute-start.18 = (f32[8,128]{1,0:T(8,128)S(1)}, f32[8,128]{1,0:T(8,128)S(1)}, u32[]{:S(2)}, u32[]{:S(2)}) collective-permute-start(f32[8,128]{1,0:T(8,128)S(1)} %get-tuple-element.45), channel_id=1, source_target_pairs={{0,8},{2,10},{4,12},{6,14},{8,0},{10,2},{12,4},{14,6},{1,9},{3,11}... | collective-permute-start | bytes 12296 | tf_op jit(solution)/shard_map/ppermute | solution.py:406
  56.0 3.6 %collective-permute-start.19 = (f32[8,128]{1,0:T(8,128)S(1)}, f32[8,128]{1,0:T(8,128)S(1)}, u32[]{:S(2)}, u32[]{:S(2)}) collective-permute-start(f32[8,128]{1,0:T(8,128)S(1)} %get-tuple-element.45), channel_id=1, source_target_pairs={{0,12},{2,14},{4,0},{6,2},{8,4},{10,6},{12,8},{14,10},{1,13},{3,15... | collective-permute-start | bytes 12296 | tf_op jit(solution)/shard_map/ppermute | solution.py:406
  57.3 4.3 %collective-permute-start.21 = (f32[128,128]{1,0:T(8,128)S(1)}, f32[128,128]{1,0:T(8,128)S(1)}, u32[]{:S(2)}, u32[]{:S(2)}) collective-permute-start(f32[128,128]{1,0:T(8,128)S(1)} %get-tuple-element.47), channel_id=1, source_target_pairs={{0,1},{1,0},{2,3},{3,2},{4,5},{5,4},{6,7},{7,6},{8,9},{9,8},{10,11... | collective-permute-start | bytes 196616 | tf_op jit(solution)/shard_map/ppermute | solution.py:404
  59.6 3.7 %collective-permute-start.20 = (f32[8,128]{1,0:T(8,128)S(1)}, f32[8,128]{1,0:T(8,128)S(1)}, u32[]{:S(2)}, u32[]{:S(2)}) collective-permute-start(f32[8,128]{1,0:T(8,128)S(1)} %select_maximum_fusion.own), channel_id=1, source_target_pairs={{0,1},{1,0},{2,3},{3,2},{4,5},{5,4},{6,7},{7,6},{8,9},{9,8},{10,11... | collective-permute-start | bytes 12296 | tf_op jit(solution)/shard_map/ppermute | solution.py:412

commit v10 on v9

--- a/solution.py
+++ b/solution.py
@@ -317,7 +317,7 @@
     row_shape = jax.ShapeDtypeStruct((per_device, columns + LANES), jnp.bfloat16)
     kept, given = pl.pallas_call(
         row_kernel,
-        in_specs=[smem, vmem] + [pl.BlockSpec(memory_space=pl.ANY)] * 2,
+        in_specs=[smem, vmem] + [pl.BlockSpec(memory_space=pltpu.HBM)] * 2,
         out_specs=[vmem] * 2,
         out_shape=[row_shape] * 2,
         scratch_shapes=[
@@ -359,13 +359,12 @@
     )(own_panel)
     score = lambda c: score_call(c, None, None, spot, noise, own_panel, squares, mate_panel)
     for step in range(1, chips + 1):
-        if step == chips and step > 2:
+        if step == 3:
             orders.append([key for key, _ in waiting])
             earlier.append(score([c for _, c in waiting]))
             waiting = []
-            tie = earlier[-1][2]
-            ahead = {c: lax.optimization_barrier((v, tie))[0] for c, v in ahead.items()}
-            behind = {c: lax.optimization_barrier((v, tie))[0] for c, v in behind.items()}
+            for chain, c in ((ahead, False), (behind, True)):
+                chain[c] = lax.optimization_barrier((chain[c], earlier[-1][2]))[0]
         if step == 2:
             for chain, c in ((ahead, False), (behind, True)):
                 chain[c] = lax.optimization_barrier((chain[c], squares))[0]
@@ -402,13 +401,13 @@
     )(spot, partial, mate_partial, all_facts)
 
     from_x = lax.ppermute(across, "cls", x_pairs)
-    parts = [stats] + [
-        lax.ppermute(stats, "orient", [(d, (d + 2 * s) % devices) for d in range(devices)])
-        for s in range(1, chips)
-    ]
-    peaks = functools.reduce(jnp.maximum, [p[0:2] for p in parts])
-    totals = functools.reduce(jnp.add, [p[2:4] * jnp.exp(p[0:2] - peaks) for p in parts])
-    class_stats = jnp.pad(jnp.concatenate([peaks, totals], axis=0), ((0, 4), (0, 0)))
+    class_stats = stats
+    for bit in range(chips.bit_length() - 1):
+        pairs = [(d, d ^ (2 << bit)) for d in range(devices)]
+        both = class_stats, lax.ppermute(class_stats, "orient", pairs)
+        peaks = jnp.maximum(both[0][0:2], both[1][0:2])
+        totals = sum(v[2:4] * jnp.exp(v[0:2] - peaks) for v in both)
+        class_stats = jnp.pad(jnp.concatenate([peaks, totals], axis=0), ((0, 4), (0, 0)))
     other_stats = lax.ppermute(class_stats, "cls", x_pairs)
     slots, chosen, tops = pl.pallas_call(
         functools.partial(slot_kernel, local_search, slots_each, per_device),
@@ -507,7 +506,7 @@
     )
     out_specs = P(("batch", "cls"), "orient", None, "rep")
     sizes = mesh.shape
-    paired = sizes["rep"] == 1 and sizes["cls"] == 2 and sizes["orient"] % 2 == 0
+    paired = sizes["rep"] == 1 and sizes["cls"] == 2 and sizes["orient"] in (4, 8, 16, 32)
     return jax.shard_map(
         chip_shards if paired else shards,
         mesh=mesh,

time: 64.3 us -> 63.6 us (0.989)
  starting transfers between devices: 29.7 us -> 24.8 us
  waiting for transfers between devices: 12.4 us -> 16.9 us
    ppermute x3 -> x2, starting transfers between devices: 5.68 us -> 2.38 us  [chip_shards(): both = (class_stats, lax.ppermute(class_stats, 'orient', pairs))]
    ppermute x14, starting transfers between devices: 18.8 us -> 16.3 us  [forward(): return lax.ppermute(values, ('orient', 'cls'), pairs)]
    ppermute x3 -> x2, waiting for transfers between devices: 0.73 us -> 3.27 us  [chip_shards(): both = (class_stats, lax.ppermute(class_stats, 'orient', pairs))]
    ppermute x14, waiting for transfers between devices: 9.14 us -> 11.1 us  [forward(): return lax.ppermute(values, ('orient', 'cls'), pairs)]
    ppermute x1, starting transfers between devices: 1.61 us -> 2.56 us  [chip_shards(): from_x = lax.ppermute(across, 'cls', x_pairs)]
  transfers between devices with their start and end apart: 22 -> 21, of which waited for: 12 -> 12; matrix products, arithmetic and copies ran while one was open for 4% -> 4% of each run, Pallas kernels for 17% -> 17%
where the time goes in v10:
time: 63.6 us; the launch traced here: 63.4 us
  starting transfers between devices  24.8 us (39%)
  waiting for transfers between devices  16.9 us (27%)
  Pallas kernels  16.5 us (26%)
  local copies, waits for them, and re-layouts  4.85 us (8%)
    ppermute x14, starting transfers between devices, forward(): return lax.ppermute(values, ('orient', 'cls'), pairs)  16.3 us
    pallas_call x3, Pallas kernels, score_call(): pl.pallas_call(kernel, in_specs=[pl.BlockSpec(memory_space=pltpu.SMEM)] +...  12.3 us
    ppermute x14, waiting for transfers between devices, forward(): return lax.ppermute(values, ('orient', 'cls'), pairs)  11.1 us
    ppermute x2, waiting for transfers between devices, chip_shards(): both = (class_stats, lax.ppermute(class_stats, 'orient', pairs))  3.27 us
    ppermute x1, starting transfers between devices, chip_shards(): from_x = lax.ppermute(across, 'cls', x_pairs)  2.56 us
    optimization_barrier x1, local copies, waits for them, and re-layouts, chip_shards(): _, panels = lax.optimization_barrier((kept, panels))  2.42 us
    unnamed x7, local copies, waits for them, and re-layouts  2.41 us
    ppermute x2, starting transfers between devices, chip_shards(): both = (class_stats, lax.ppermute(class_stats, 'orient', pairs))  2.38 us
  transfers between devices with their start and end apart: 21, of which 12 were waited for; matrix products, arithmetic and copies ran while one was open for 4% of the time, Pallas kernels for 17%

profile of v10, /device:TPU:0, one launch (start us, length us, event | category | flops | bytes accessed | tf_op | source)
XLA Modules:
  0.0 63.4 jit_solution(18093393778209917345)
XLA Ops:
  0.0 1.1 %copy.11 = bf16[1,16,2,7296]{3,1,2,0:T(8,128)(2,1)S(1)} copy(bf16[1,16,2,7296]{3,2,1,0:T(2,128)(2,1)} %param.5) | data formatting | bytes 933888 | tf_op args[0]
  1.1 0.1 pad_add_fusion.spot
  1.2 0.7 %copy-done = s32[1,16,4]{1,2,0:T(4,128)S(1)} copy-done((s32[1,16,4]{1,2,0:T(4,128)S(1)}, s32[1,16,4]{1,2,0:T(4,128)}, u32[]{:S(2)}) %copy-start) | copy-done | bytes 280
  1.9 0.7 %copy-done.1 = bf16[1,16]{1,0:T(2,128)(2,1)S(1)} copy-done((bf16[1,16]{1,0:T(2,128)(2,1)S(1)}, bf16[1,16]{1,0:T(2,128)(2,1)}, u32[]{:S(2)}) %copy-start.1) | copy-done | bytes 56
  2.5 0.6 shard_map.55
  3.1 2.4 %collective-permute-start.5 = (bf16[16,7424]{1,0:T(8,128)(2,1)S(1)}, bf16[16,7424]{1,0:T(8,128)(2,1)S(1)}, u32[]{:S(2)}, u32[]{:S(2)}) collective-permute-start(bf16[16,7424]{1,0:T(8,128)(2,1)S(1)} %get-tuple-element.32), channel_id=1, source_target_pairs={{0,3},{2,1},{4,2},{6,0},{8,6},{10,4},{12,10},{14,8},{13,14},{15,12... | collective-permute-start | bytes 712712 | tf_op jit(solution)/shard_map/rows_behind/ppermute | solution.py:311
  5.6 0.7 %collective-permute-start.2 = (bf16[16,7424]{1,0:T(8,128)(2,1)S(1)}, bf16[16,7424]{1,0:T(8,128)(2,1)S(1)}, u32[]{:S(2)}, u32[]{:S(2)}) collective-permute-start(bf16[16,7424]{1,0:T(8,128)(2,1)S(1)} %get-tuple-element.32), channel_id=1, source_target_pairs={{0,2},{2,0},{4,6},{6,4},{8,10},{10,8},{12,14},{14,12},{1,3},{3,1},... | collective-permute-start | bytes 712712 | tf_op jit(solution)/shard_map/mate_rows/ppermute | solution.py:332
  6.2 0.1 collective-permute-start
  6.3 1.9 %collective-permute-start.3 = (bf16[16,7424]{1,0:T(8,128)(2,1)S(1)}, bf16[16,7424]{1,0:T(8,128)(2,1)S(1)}, u32[]{:S(2)}, u32[]{:S(2)}) collective-permute-start(bf16[16,7424]{1,0:T(8,128)(2,1)S(1)} %get-tuple-element.28.refs_0_), channel_id=1, source_target_pairs={{0,1},{2,3},{4,0},{6,2},{8,4},{10,6},{12,8},{14,10},{13,12},{15,14... | collective-permute-start | bytes 712712 | tf_op jit(solution)/shard_map/rows_behind/ppermute | solution.py:311
  8.3 2.4 %copy.10 = bf16[1,1,128,2,7296]{4,2,3,1,0:T(8,128)(2,1)S(1)} copy(bf16[1,1,128,2,7296]{4,3,2,1,0:T(2,128)(2,1)} %param.9) | data formatting | bytes 7471104 | tf_op jit(solution)/shard_map/optimization_barrier | solution.py:334
  10.7 0.8 %shard_map.56 = (bf16[128,7296]{1,0:T(8,128)(2,1)S(1)}, bf16[128,7296]{1,0:T(8,128)(2,1)S(1)}) custom-call(s32[4]{0:T(128)S(1)} %pad_add_fusion.spot, bf16[2,128,7296]{2,1,0:T(8,128)(2,1)S(1)} %bitcast.18), custom_call_target="tpu_custom_call" | custom-call | tf_op jit(solution)/shard_map/pallas_call | solution.py:337
  11.5 0.2 collective-permute-done.5.refs_5_
  11.7 1.2 %collective-permute-start.6 = (bf16[128,7296]{1,0:T(8,128)(2,1)S(1)}, bf16[128,7296]{1,0:T(8,128)(2,1)S(1)}, u32[]{:S(2)}, u32[]{:S(2)}) collective-permute-start(bf16[128,7296]{1,0:T(8,128)(2,1)S(1)} %get-tuple-element.33), channel_id=1, source_target_pairs={{0,2},{2,0},{4,6},{6,4},{8,10},{10,8},{12,14},{14,12},{1,3},{3,1},... | collective-permute-start | bytes 5603336 | tf_op jit(solution)/shard_map/mate_panel/ppermute | solution.py:345
  12.9 0.1 shard_map.57.refs_8_.refs_10_.refs_4_
  13.1 1.8 %collective-permute-done.refs_2_ = bf16[16,7424]{1,0:T(8,128)(2,1)S(1)} collective-permute-done((bf16[16,7424]{1,0:T(8,128)(2,1)S(1)}, bf16[16,7424]{1,0:T(8,128)(2,1)S(1)}, u32[]{:S(2)}, u32[]{:S(2)}) %collective-permute-start) | collective-permute-done | bytes 237600 | tf_op jit(solution)/shard_map/rows_ahead/ppermute | solution.py:311
  14.9 1.6 %collective-permute-start.9 = (bf16[16,7424]{1,0:T(8,128)(2,1)S(1)}, bf16[16,7424]{1,0:T(8,128)(2,1)S(1)}, u32[]{:S(2)}, u32[]{:S(2)}) collective-permute-start(bf16[16,7424]{1,0:T(8,128)(2,1)S(1)} %collective-permute-done.5.refs_5_), channel_id=1, source_target_pairs={{0,1},{2,3},{4,0},{6,2},{8,4},{10,6},{12,8},{14,10},{13,12},{15,14... | collective-permute-start | bytes 712712 | tf_op jit(solution)/shard_map/rows_behind/ppermute | solution.py:311
  16.5 0.0 collective-permute-done.2.refs_1_
  16.5 0.5 collective-permute-start.1
  16.9 1.0 %collective-permute-done.3.refs_3_ = bf16[16,7424]{1,0:T(8,128)(2,1)S(1)} collective-permute-done((bf16[16,7424]{1,0:T(8,128)(2,1)S(1)}, bf16[16,7424]{1,0:T(8,128)(2,1)S(1)}, u32[]{:S(2)}, u32[]{:S(2)}) %collective-permute-start.3) | collective-permute-done | bytes 237600 | tf_op jit(solution)/shard_map/rows_behind/ppermute | solution.py:311
  17.9 1.4 %collective-permute-start.12 = (bf16[16,7424]{1,0:T(8,128)(2,1)S(1)}, bf16[16,7424]{1,0:T(8,128)(2,1)S(1)}, u32[]{:S(2)}, u32[]{:S(2)}) collective-permute-start(bf16[16,7424]{1,0:T(8,128)(2,1)S(1)} %collective-permute-done.3.refs_3_), channel_id=1, source_target_pairs={{0,1},{2,3},{4,0},{6,2},{8,4},{10,6},{12,8},{14,10},{13,12},{15,14... | collective-permute-start | bytes 712712 | tf_op jit(solution)/shard_map/rows_behind/ppermute | solution.py:311
  19.3 0.0 collective-permute-done.4.refs_4_
  19.3 0.6 collective-permute-start.13
  19.9 4.2 %shard_map.58 = (f32[96,128]{1,0:T(8,128)S(1)}, f32[96,128]{1,0:T(8,128)S(1)}, f32[96,128]{1,0:T(8,128)S(1)}) custom-call(s32[4]{0:T(128)S(1)} %pad_add_fusion.spot, bf16[16,7424]{1,0:T(8,128)(2,1)S(1)} %get-tuple-element.28.refs_0_, bf16[16,7424]{1,0:T(8,128)(2,1)S(1)} %collective-permute-done.2.refs_1_, bf16[16,7424]{1,0:T(8,128)(2,1)S(1)} %collective-permute-done.refs_2_, ...), custom_call_target="tpu_custom_call" | custom-call | flops 956301312 | bytes 5136384 | tf_op jit(solution)/shard_map/pallas_call | solution.py:188
  24.2 1.4 %collective-permute-start.10 = (bf16[16,7424]{1,0:T(8,128)(2,1)S(1)}, bf16[16,7424]{1,0:T(8,128)(2,1)S(1)}, u32[]{:S(2)}, u32[]{:S(2)}) collective-permute-start(bf16[16,7424]{1,0:T(8,128)(2,1)S(1)} %collective-permute-done.9.refs_3_), channel_id=1, source_target_pairs={{0,1},{2,3},{4,0},{6,2},{8,4},{10,6},{12,8},{14,10},{13,12},{15,14... | collective-permute-start | bytes 712712 | tf_op jit(solution)/shard_map/rows_behind/ppermute | solution.py:311
  25.6 0.6 collective-permute-start.7
  26.2 1.4 %collective-permute-done.12.refs_1_ = bf16[16,7424]{1,0:T(8,128)(2,1)S(1)} collective-permute-done((bf16[16,7424]{1,0:T(8,128)(2,1)S(1)}, bf16[16,7424]{1,0:T(8,128)(2,1)S(1)}, u32[]{:S(2)}, u32[]{:S(2)}) %collective-permute-start.12) | collective-permute-done | bytes 237600 | tf_op jit(solution)/shard_map/rows_behind/ppermute | solution.py:311
  27.7 2.5 %collective-permute-start.14 = (bf16[16,7424]{1,0:T(8,128)(2,1)S(1)}, bf16[16,7424]{1,0:T(8,128)(2,1)S(1)}, u32[]{:S(2)}, u32[]{:S(2)}) collective-permute-start(bf16[16,7424]{1,0:T(8,128)(2,1)S(1)} %collective-permute-done.12.refs_1_), channel_id=1, source_target_pairs={{0,1},{2,3},{4,0},{6,2},{8,4},{10,6},{12,8},{14,10},{13,12},{15,14... | collective-permute-start | bytes 712712 | tf_op jit(solution)/shard_map/rows_behind/ppermute | solution.py:311
  30.2 0.4 collective-permute-start.15
  30.6 2.3 %collective-permute-done.10.refs_7_ = bf16[16,7424]{1,0:T(8,128)(2,1)S(1)} collective-permute-done((bf16[16,7424]{1,0:T(8,128)(2,1)S(1)}, bf16[16,7424]{1,0:T(8,128)(2,1)S(1)}, u32[]{:S(2)}, u32[]{:S(2)}) %collective-permute-start.10) | collective-permute-done | bytes 237600 | tf_op jit(solution)/shard_map/rows_behind/ppermute | solution.py:311
  32.8 2.4 %collective-permute-start.11 = (bf16[16,7424]{1,0:T(8,128)(2,1)S(1)}, bf16[16,7424]{1,0:T(8,128)(2,1)S(1)}, u32[]{:S(2)}, u32[]{:S(2)}) collective-permute-start(bf16[16,7424]{1,0:T(8,128)(2,1)S(1)} %collective-permute-done.10.refs_7_), channel_id=1, source_target_pairs={{0,1},{2,3},{4,0},{6,2},{8,4},{10,6},{12,8},{14,10},{13,12},{15,14... | collective-permute-start | bytes 712712 | tf_op jit(solution)/shard_map/rows_behind/ppermute | solution.py:311
  35.3 0.4 collective-permute-start.8
  35.7 2.3 %collective-permute-done.14.refs_5_ = bf16[16,7424]{1,0:T(8,128)(2,1)S(1)} collective-permute-done((bf16[16,7424]{1,0:T(8,128)(2,1)S(1)}, bf16[16,7424]{1,0:T(8,128)(2,1)S(1)}, u32[]{:S(2)}, u32[]{:S(2)}) %collective-permute-start.14) | collective-permute-done | bytes 237600 | tf_op jit(solution)/shard_map/rows_behind/ppermute | solution.py:311
  37.9 2.2 %collective-permute-done.15.refs_6_ = bf16[16,7424]{1,0:T(8,128)(2,1)S(1)} collective-permute-done((bf16[16,7424]{1,0:T(8,128)(2,1)S(1)}, bf16[16,7424]{1,0:T(8,128)(2,1)S(1)}, u32[]{:S(2)}, u32[]{:S(2)}) %collective-permute-start.15) | collective-permute-done | bytes 237600 | tf_op jit(solution)/shard_map/rows_ahead/ppermute | solution.py:311
  40.1 4.7 %shard_map.59 = (f32[128,128]{1,0:T(8,128)S(1)}, f32[128,128]{1,0:T(8,128)S(1)}, f32[128,128]{1,0:T(8,128)S(1)}) custom-call(s32[4]{0:T(128)S(1)} %pad_add_fusion.spot, bf16[16,7424]{1,0:T(8,128)(2,1)S(1)} %collective-permute-done.1.refs_0_, bf16[16,7424]{1,0:T(8,128)(2,1)S(1)} %collective-permute-done.12.refs_1_, ...), custom_call_target="tpu_custom_call" | custom-call | flops 956301312 | bytes 5603328 | tf_op jit(solution)/shard_map/pallas_call | solution.py:188
  44.8 3.4 %shard_map.60 = (f32[2,256,128]{2,1,0:T(8,128)S(1)}, f32[256,128]{1,0:T(8,128)S(1)}) custom-call(s32[4]{0:T(128)S(1)} %pad_add_fusion.spot, bf16[16,7424]{1,0:T(8,128)(2,1)S(1)} %collective-permute-done.8.refs_0_, bf16[16,7424]{1,0:T(8,128)(2,1)S(1)} %collective-permute-done.11.refs_1_, f32[1,7296]{1,0:T(1,128)S(1)} %broadcast_in_dim.3.refs_6_.refs_8_.refs_2_, ...), custom_call_target="tpu_custom_call" | custom-call | flops 956301312 | bytes 4202496 | tf_op jit(solution)/shard_map/pallas_call | solution.py:188
  48.2 0.1 collective-permute-start.16
  48.3 1.5 %collective-permute-done.16.mate = f32[2,256,128]{2,1,0:T(8,128)S(1)} collective-permute-done((f32[2,256,128]{2,1,0:T(8,128)S(1)}, f32[2,256,128]{2,1,0:T(8,128)S(1)}, u32[]{:S(2)}, u32[]{:S(2)}) %collective-permute-start.16) | collective-permute-done | bytes 262176 | tf_op jit(solution)/shard_map/ppermute | solution.py:390
  49.8 0.9 %shard_map.61 = (f32[128,128]{1,0:T(8,128)S(1)}, f32[128,128]{1,0:T(8,128)S(1)}, f32[8,128]{1,0:T(8,128)S(1)}) custom-call(s32[4]{0:T(128)S(1)} %pad_add_fusion.spot, f32[2,256,128]{2,1,0:T(8,128)S(1)} %get-tuple-element.43.partial, f32[2,256,128]{2,1,0:T(8,128)S(1)} %collective-permute-done.16.mate, f32[256,128]{1,0:T(8,128)S(1)} %get-tuple-element.44.facts), custom_call_target="tpu_custom_call" | custom-call | tf_op jit(solution)/shard_map/pallas_call | solution.py:391
  50.7 0.7 %collective-permute-start.17 = (f32[8,128]{1,0:T(8,128)S(1)}, f32[8,128]{1,0:T(8,128)S(1)}, u32[]{:S(2)}, u32[]{:S(2)}) collective-permute-start(f32[8,128]{1,0:T(8,128)S(1)} %get-tuple-element.45), channel_id=1, source_target_pairs={{0,4},{2,6},{4,0},{6,2},{8,12},{10,14},{12,8},{14,10},{1,5},{3,7},... | collective-permute-start | bytes 12296 | tf_op jit(solution)/shard_map/ppermute | solution.py:407
  51.4 2.9 %collective-permute-done.17 = f32[8,128]{1,0:T(8,128)S(1)} collective-permute-done((f32[8,128]{1,0:T(8,128)S(1)}, f32[8,128]{1,0:T(8,128)S(1)}, u32[]{:S(2)}, u32[]{:S(2)}) %collective-permute-start.17) | collective-permute-done | bytes 4128 | tf_op jit(solution)/shard_map/ppermute | solution.py:407
  54.3 1.7 %collective-permute-start.18 = (f32[8,128]{1,0:T(8,128)S(1)}, f32[8,128]{1,0:T(8,128)S(1)}, u32[]{:S(2)}, u32[]{:S(2)}) collective-permute-start(f32[8,128]{1,0:T(8,128)S(1)} %fusion.2), channel_id=1, source_target_pairs={{0,8},{2,10},{4,12},{6,14},{8,0},{10,2},{12,4},{14,6},{1,9},{3,11}... | collective-permute-start | bytes 12296 | tf_op jit(solution)/shard_map/ppermute | solution.py:407
  56.0 2.6 %collective-permute-start.20 = (f32[128,128]{1,0:T(8,128)S(1)}, f32[128,128]{1,0:T(8,128)S(1)}, u32[]{:S(2)}, u32[]{:S(2)}) collective-permute-start(f32[128,128]{1,0:T(8,128)S(1)} %get-tuple-element.47), channel_id=1, source_target_pairs={{0,1},{1,0},{2,3},{3,2},{4,5},{5,4},{6,7},{7,6},{8,9},{9,8},{10,11... | collective-permute-start | bytes 196616 | tf_op jit(solution)/shard_map/ppermute | solution.py:403
  58.6 0.3 collective-permute-done.18
  58.9 1.6 %collective-permute-start.19 = (f32[8,128]{1,0:T(8,128)S(1)}, f32[8,128]{1,0:T(8,128)S(1)}, u32[]{:S(2)}, u32[]{:S(2)}) collective-permute-start(f32[8,128]{1,0:T(8,128)S(1)} %select_maximum_fusion.own), channel_id=1, source_target_pairs={{0,1},{1,0},{2,3},{3,2},{4,5},{5,4},{6,7},{7,6},{8,9},{9,8},{10,11... | collective-permute-start | bytes 12296 | tf_op jit(solution)/shard_map/ppermute | solution.py:411
  60.6 0.2 collective-permute-done.20.across
  60.8 1.1 %shard_map.62 = (f32[128,256]{1,0:T(8,128)S(1)}, f32[128,128]{1,0:T(8,128)S(1)}, f32[8,128]{1,0:T(8,128)S(1)}) custom-call(s32[4]{0:T(128)S(1)} %pad_add_fusion.spot, f32[128,128]{1,0:T(8,128)S(1)} %get-tuple-element.46.mine, f32[128,128]{1,0:T(8,128)S(1)} %collective-permute-done.20.across, f32[256,128]{1,0:T(8,128)S(1)} %get-tuple-element.44.facts), custom_call_target="tpu_custom_call" | custom-call | tf_op jit(solution)/shard_map/pallas_call | solution.py:412
  61.9 0.7 %collective-permute-done.19.other = f32[8,128]{1,0:T(8,128)S(1)} collective-permute-done((f32[8,128]{1,0:T(8,128)S(1)}, f32[8,128]{1,0:T(8,128)S(1)}, u32[]{:S(2)}, u32[]{:S(2)}) %collective-permute-start.19) | collective-permute-done | bytes 4128 | tf_op jit(solution)/shard_map/ppermute | solution.py:411
  62.6 0.8 %shard_map.63 = f32[128,256]{1,0:T(8,128)} custom-call(f32[8,128]{1,0:T(8,128)S(1)} %select_maximum_fusion.own, f32[8,128]{1,0:T(8,128)S(1)} %collective-permute-done.19.other, f32[8,128]{1,0:T(8,128)S(1)} %get-tuple-element.48.tops, f32[128,256]{1,0:T(8,128)S(1)} %get-tuple-element.49.slots, f32[128,128]{1,0:T(8,128)S(1)} %get-tuple-element.50.chosen), custom_call_target="tpu_custom_call" | custom-call | tf_op jit(solution)/shard_map/pallas_call | solution.py:423
  (17 shorter events, 0.1 us)
Async XLA Ops:
  1.2 0.7 %copy-start = (s32[1,16,4]{1,2,0:T(4,128)S(1)}, s32[1,16,4]{1,2,0:T(4,128)}, u32[]{:S(2)}) copy-start(s32[1,16,4]{1,2,0:T(4,128)} %param.7) | copy-start | bytes 772
  1.9 0.7 %copy-start.1 = (bf16[1,16]{1,0:T(2,128)(2,1)S(1)}, bf16[1,16]{1,0:T(2,128)(2,1)}, u32[]{:S(2)}) copy-start(bf16[1,16]{1,0:T(2,128)(2,1)} %defocus.1) | copy-start | bytes 100
  3.1 8.6 %collective-permute-start.5 = (bf16[16,7424]{1,0:T(8,128)(2,1)S(1)}, bf16[16,7424]{1,0:T(8,128)(2,1)S(1)}, u32[]{:S(2)}, u32[]{:S(2)}) collective-permute-start(bf16[16,7424]{1,0:T(8,128)(2,1)S(1)} %get-tuple-element.32), channel_id=1, source_target_pairs={{0,3},{2,1},{4,2},{6,0},{8,6},{10,4},{12,10},{14,8},{13,14},{15,12... | collective-permute-start | bytes 712712 | tf_op jit(solution)/shard_map/rows_behind/ppermute | solution.py:311
  5.6 10.9 %collective-permute-start.2 = (bf16[16,7424]{1,0:T(8,128)(2,1)S(1)}, bf16[16,7424]{1,0:T(8,128)(2,1)S(1)}, u32[]{:S(2)}, u32[]{:S(2)}) collective-permute-start(bf16[16,7424]{1,0:T(8,128)(2,1)S(1)} %get-tuple-element.32), channel_id=1, source_target_pairs={{0,2},{2,0},{4,6},{6,4},{8,10},{10,8},{12,14},{14,12},{1,3},{3,1},... | collective-permute-start | bytes 712712 | tf_op jit(solution)/shard_map/mate_rows/ppermute | solution.py:332
  6.2 8.6 %collective-permute-start = (bf16[16,7424]{1,0:T(8,128)(2,1)S(1)}, bf16[16,7424]{1,0:T(8,128)(2,1)S(1)}, u32[]{:S(2)}, u32[]{:S(2)}) collective-permute-start(bf16[16,7424]{1,0:T(8,128)(2,1)S(1)} %get-tuple-element.28.refs_0_), channel_id=1, source_target_pairs={{0,4},{2,6},{4,8},{6,10},{8,12},{10,14},{12,13},{14,15},{13,9},{15... | collective-permute-start | bytes 712712 | tf_op jit(solution)/shard_map/rows_ahead/ppermute | solution.py:311
  6.3 11.6 %collective-permute-start.3 = (bf16[16,7424]{1,0:T(8,128)(2,1)S(1)}, bf16[16,7424]{1,0:T(8,128)(2,1)S(1)}, u32[]{:S(2)}, u32[]{:S(2)}) collective-permute-start(bf16[16,7424]{1,0:T(8,128)(2,1)S(1)} %get-tuple-element.28.refs_0_), channel_id=1, source_target_pairs={{0,1},{2,3},{4,0},{6,2},{8,4},{10,6},{12,8},{14,10},{13,12},{15,14... | collective-permute-start | bytes 712712 | tf_op jit(solution)/shard_map/rows_behind/ppermute | solution.py:311
  8.3 11.0 %collective-permute-start.4 = (bf16[16,7424]{1,0:T(8,128)(2,1)S(1)}, bf16[16,7424]{1,0:T(8,128)(2,1)S(1)}, u32[]{:S(2)}, u32[]{:S(2)}) collective-permute-start(bf16[16,7424]{1,0:T(8,128)(2,1)S(1)} %get-tuple-element.32), channel_id=1, source_target_pairs={{0,6},{2,4},{4,10},{6,8},{8,14},{10,12},{12,15},{14,13},{13,11},{1... | collective-permute-start | bytes 712712 | tf_op jit(solution)/shard_map/rows_ahead/ppermute | solution.py:311
  11.7 8.2 %collective-permute-start.6 = (bf16[128,7296]{1,0:T(8,128)(2,1)S(1)}, bf16[128,7296]{1,0:T(8,128)(2,1)S(1)}, u32[]{:S(2)}, u32[]{:S(2)}) collective-permute-start(bf16[128,7296]{1,0:T(8,128)(2,1)S(1)} %get-tuple-element.33), channel_id=1, source_target_pairs={{0,2},{2,0},{4,6},{6,4},{8,10},{10,8},{12,14},{14,12},{1,3},{3,1},... | collective-permute-start | bytes 5603336 | tf_op jit(solution)/shard_map/mate_panel/ppermute | solution.py:345
  12.9 4.0 %copy-start.2 = (f32[7296]{0:T(1024)S(1)}, f32[7296]{0:T(1024)}, u32[]{:S(2)}) copy-start(f32[7296]{0:T(1024)} %param.8) | copy-start | bytes 87556
  14.9 9.3 %collective-permute-start.9 = (bf16[16,7424]{1,0:T(8,128)(2,1)S(1)}, bf16[16,7424]{1,0:T(8,128)(2,1)S(1)}, u32[]{:S(2)}, u32[]{:S(2)}) collective-permute-start(bf16[16,7424]{1,0:T(8,128)(2,1)S(1)} %collective-permute-done.5.refs_5_), channel_id=1, source_target_pairs={{0,1},{2,3},{4,0},{6,2},{8,4},{10,6},{12,8},{14,10},{13,12},{15,14... | collective-permute-start | bytes 712712 | tf_op jit(solution)/shard_map/rows_behind/ppermute | solution.py:311
  16.5 9.2 %collective-permute-start.1 = (bf16[16,7424]{1,0:T(8,128)(2,1)S(1)}, bf16[16,7424]{1,0:T(8,128)(2,1)S(1)}, u32[]{:S(2)}, u32[]{:S(2)}) collective-permute-start(bf16[16,7424]{1,0:T(8,128)(2,1)S(1)} %collective-permute-done.refs_2_), channel_id=1, source_target_pairs={{0,4},{2,6},{4,8},{6,10},{8,12},{10,14},{12,13},{14,15},{13,9},{15... | collective-permute-start | bytes 712712 | tf_op jit(solution)/shard_map/rows_ahead/ppermute | solution.py:311
  17.9 9.8 %collective-permute-start.12 = (bf16[16,7424]{1,0:T(8,128)(2,1)S(1)}, bf16[16,7424]{1,0:T(8,128)(2,1)S(1)}, u32[]{:S(2)}, u32[]{:S(2)}) collective-permute-start(bf16[16,7424]{1,0:T(8,128)(2,1)S(1)} %collective-permute-done.3.refs_3_), channel_id=1, source_target_pairs={{0,1},{2,3},{4,0},{6,2},{8,4},{10,6},{12,8},{14,10},{13,12},{15,14... | collective-permute-start | bytes 712712 | tf_op jit(solution)/shard_map/rows_behind/ppermute | solution.py:311
  19.3 10.9 %collective-permute-start.13 = (bf16[16,7424]{1,0:T(8,128)(2,1)S(1)}, bf16[16,7424]{1,0:T(8,128)(2,1)S(1)}, u32[]{:S(2)}, u32[]{:S(2)}) collective-permute-start(bf16[16,7424]{1,0:T(8,128)(2,1)S(1)} %collective-permute-done.4.refs_4_), channel_id=1, source_target_pairs={{0,4},{2,6},{4,8},{6,10},{8,12},{10,14},{12,13},{14,15},{13,9},{15... | collective-permute-start | bytes 712712 | tf_op jit(solution)/shard_map/rows_ahead/ppermute | solution.py:311
  24.2 8.7 %collective-permute-start.10 = (bf16[16,7424]{1,0:T(8,128)(2,1)S(1)}, bf16[16,7424]{1,0:T(8,128)(2,1)S(1)}, u32[]{:S(2)}, u32[]{:S(2)}) collective-permute-start(bf16[16,7424]{1,0:T(8,128)(2,1)S(1)} %collective-permute-done.9.refs_3_), channel_id=1, source_target_pairs={{0,1},{2,3},{4,0},{6,2},{8,4},{10,6},{12,8},{14,10},{13,12},{15,14... | collective-permute-start | bytes 712712 | tf_op jit(solution)/shard_map/rows_behind/ppermute | solution.py:311
  25.6 9.6 %collective-permute-start.7 = (bf16[16,7424]{1,0:T(8,128)(2,1)S(1)}, bf16[16,7424]{1,0:T(8,128)(2,1)S(1)}, u32[]{:S(2)}, u32[]{:S(2)}) collective-permute-start(bf16[16,7424]{1,0:T(8,128)(2,1)S(1)} %collective-permute-done.1.refs_0_), channel_id=1, source_target_pairs={{0,4},{2,6},{4,8},{6,10},{8,12},{10,14},{12,13},{14,15},{13,9},{15... | collective-permute-start | bytes 712712 | tf_op jit(solution)/shard_map/rows_ahead/ppermute | solution.py:311
  27.7 10.2 %collective-permute-start.14 = (bf16[16,7424]{1,0:T(8,128)(2,1)S(1)}, bf16[16,7424]{1,0:T(8,128)(2,1)S(1)}, u32[]{:S(2)}, u32[]{:S(2)}) collective-permute-start(bf16[16,7424]{1,0:T(8,128)(2,1)S(1)} %collective-permute-done.12.refs_1_), channel_id=1, source_target_pairs={{0,1},{2,3},{4,0},{6,2},{8,4},{10,6},{12,8},{14,10},{13,12},{15,14... | collective-permute-start | bytes 712712 | tf_op jit(solution)/shard_map/rows_behind/ppermute | solution.py:311
  30.2 9.9 %collective-permute-start.15 = (bf16[16,7424]{1,0:T(8,128)(2,1)S(1)}, bf16[16,7424]{1,0:T(8,128)(2,1)S(1)}, u32[]{:S(2)}, u32[]{:S(2)}) collective-permute-start(bf16[16,7424]{1,0:T(8,128)(2,1)S(1)} %collective-permute-done.13.refs_2_), channel_id=1, source_target_pairs={{0,4},{2,6},{4,8},{6,10},{8,12},{10,14},{12,13},{14,15},{13,9},{15... | collective-permute-start | bytes 712712 | tf_op jit(solution)/shard_map/rows_ahead/ppermute | solution.py:311
  32.8 11.9 %collective-permute-start.11 = (bf16[16,7424]{1,0:T(8,128)(2,1)S(1)}, bf16[16,7424]{1,0:T(8,128)(2,1)S(1)}, u32[]{:S(2)}, u32[]{:S(2)}) collective-permute-start(bf16[16,7424]{1,0:T(8,128)(2,1)S(1)} %collective-permute-done.10.refs_7_), channel_id=1, source_target_pairs={{0,1},{2,3},{4,0},{6,2},{8,4},{10,6},{12,8},{14,10},{13,12},{15,14... | collective-permute-start | bytes 712712 | tf_op jit(solution)/shard_map/rows_behind/ppermute | solution.py:311
  35.3 9.5 %collective-permute-start.8 = (bf16[16,7424]{1,0:T(8,128)(2,1)S(1)}, bf16[16,7424]{1,0:T(8,128)(2,1)S(1)}, u32[]{:S(2)}, u32[]{:S(2)}) collective-permute-start(bf16[16,7424]{1,0:T(8,128)(2,1)S(1)} %collective-permute-done.7.refs_4_), channel_id=1, source_target_pairs={{0,4},{2,6},{4,8},{6,10},{8,12},{10,14},{12,13},{14,15},{13,9},{15... | collective-permute-start | bytes 712712 | tf_op jit(solution)/shard_map/rows_ahead/ppermute | solution.py:311
  48.2 1.6 %collective-permute-start.16 = (f32[2,256,128]{2,1,0:T(8,128)S(1)}, f32[2,256,128]{2,1,0:T(8,128)S(1)}, u32[]{:S(2)}, u32[]{:S(2)}) collective-permute-start(f32[2,256,128]{2,1,0:T(8,128)S(1)} %get-tuple-element.43.partial), channel_id=1, source_target_pairs={{0,2},{2,0},{4,6},{6,4},{8,10},{10,8},{12,14},{14,12},{1,3},{3,1},... | collective-permute-start | bytes 786440 | tf_op jit(solution)/shard_map/ppermute | solution.py:390
  50.7 3.6 %collective-permute-start.17 = (f32[8,128]{1,0:T(8,128)S(1)}, f32[8,128]{1,0:T(8,128)S(1)}, u32[]{:S(2)}, u32[]{:S(2)}) collective-permute-start(f32[8,128]{1,0:T(8,128)S(1)} %get-tuple-element.45), channel_id=1, source_target_pairs={{0,4},{2,6},{4,0},{6,2},{8,12},{10,14},{12,8},{14,10},{1,5},{3,7},... | collective-permute-start | bytes 12296 | tf_op jit(solution)/shard_map/ppermute | solution.py:407
  54.3 4.6 %collective-permute-start.18 = (f32[8,128]{1,0:T(8,128)S(1)}, f32[8,128]{1,0:T(8,128)S(1)}, u32[]{:S(2)}, u32[]{:S(2)}) collective-permute-start(f32[8,128]{1,0:T(8,128)S(1)} %fusion.2), channel_id=1, source_target_pairs={{0,8},{2,10},{4,12},{6,14},{8,0},{10,2},{12,4},{14,6},{1,9},{3,11}... | collective-permute-start | bytes 12296 | tf_op jit(solution)/shard_map/ppermute | solution.py:407
  56.0 4.8 %collective-permute-start.20 = (f32[128,128]{1,0:T(8,128)S(1)}, f32[128,128]{1,0:T(8,128)S(1)}, u32[]{:S(2)}, u32[]{:S(2)}) collective-permute-start(f32[128,128]{1,0:T(8,128)S(1)} %get-tuple-element.47), channel_id=1, source_target_pairs={{0,1},{1,0},{2,3},{3,2},{4,5},{5,4},{6,7},{7,6},{8,9},{9,8},{10,11... | collective-permute-start | bytes 196616 | tf_op jit(solution)/shard_map/ppermute | solution.py:403
  58.9 3.7 %collective-permute-start.19 = (f32[8,128]{1,0:T(8,128)S(1)}, f32[8,128]{1,0:T(8,128)S(1)}, u32[]{:S(2)}, u32[]{:S(2)}) collective-permute-start(f32[8,128]{1,0:T(8,128)S(1)} %select_maximum_fusion.own), channel_id=1, source_target_pairs={{0,1},{1,0},{2,3},{3,2},{4,5},{5,4},{6,7},{7,6},{8,9},{9,8},{10,11... | collective-permute-start | bytes 12296 | tf_op jit(solution)/shard_map/ppermute | solution.py:411

commit v11 on v10

--- a/solution.py
+++ b/solution.py
@@ -49,25 +49,14 @@
     squares[...] = own[...] * own[...]
 
 
-def row_kernel(spot, planes, defocus, lists, kept, given, facts, focus, named, sems):
+def row_kernel(spot, planes, facts, kept, given, padded):
     core = spot[2]
     columns = planes.shape[2]
-    count = defocus.shape[1]
-    fetches = [
-        pltpu.make_async_copy(defocus, focus, sems.at[0]),
-        pltpu.make_async_copy(lists, named, sems.at[1]),
-    ]
-    for fetch in fetches:
-        fetch.start()
-    facts[...] = jnp.zeros_like(facts)
+    padded[...] = jnp.zeros_like(padded)
+    padded[: facts.shape[0], : facts.shape[1]] = facts[...]
     for half, out in ((core, kept), (1 - core, given)):
         out[:, :columns] = planes[half]
-    for fetch in fetches:
-        fetch.wait()
-    facts[0:1, :count] = focus[...].astype(jnp.float32)
-    facts[1 : 1 + lists.shape[0], :count] = named[...].astype(jnp.float32)
-    for out in (kept, given):
-        out[:, columns:] = facts[...].astype(out.dtype)
+        out[:, columns:] = padded[...].astype(out.dtype)
 
 
 def particle_facts(meta):
@@ -270,11 +259,11 @@
     chosen[...] = taken.T
 
 
-def final_kernel(own, other, tops, slots, chosen, out):
-    peaks = own[0:1, :], other[1:2, :]
-    totals = own[2:3, :], other[3:4, :]
-    peak = jnp.maximum(*peaks)
-    total = totals[0] * jnp.exp(peaks[0] - peak) + totals[1] * jnp.exp(peaks[1] - peak)
+def final_kernel(n, *refs):
+    parts, (tops, slots, chosen, out) = refs[:n], refs[n:]
+    peak = functools.reduce(jnp.maximum, [p[0:1, :] for p in parts])
+    shares = [p[1:2, :] * jnp.exp(p[0:1, :] - peak) for p in parts]
+    total = functools.reduce(jnp.add, shares)
     factor = jnp.exp(jnp.minimum(tops[0:1, :] - peak, 0.0)) / total
     scale = jnp.sum(chosen[...] * factor, axis=1, keepdims=True)
     out[...] = slots[...] * scale
@@ -315,19 +304,15 @@
     params = pltpu.CompilerParams(vmem_limit_bytes=VMEM_LIMIT)
     planes = lax.optimization_barrier(jnp.transpose(images[0], (1, 0, 2)))
     row_shape = jax.ShapeDtypeStruct((per_device, columns + LANES), jnp.bfloat16)
+    facts = jnp.concatenate([defocus, jnp.transpose(block_ids[0])], axis=0, dtype=jnp.float32)
     kept, given = pl.pallas_call(
         row_kernel,
-        in_specs=[smem, vmem] + [pl.BlockSpec(memory_space=pltpu.HBM)] * 2,
+        in_specs=[smem, vmem, vmem],
         out_specs=[vmem] * 2,
         out_shape=[row_shape] * 2,
-        scratch_shapes=[
-            pltpu.VMEM((per_device, LANES), jnp.float32),
-            pltpu.VMEM(defocus.shape, defocus.dtype),
-            pltpu.VMEM((local_search, per_device), block_ids.dtype),
-            pltpu.SemaphoreType.DMA((2,)),
-        ],
+        scratch_shapes=[pltpu.VMEM((per_device, LANES), jnp.float32)],
         compiler_params=params,
-    )(spot, planes, defocus, jnp.transpose(block_ids[0]))
+    )(spot, planes, facts)
     with jax.named_scope("mate_rows"):
         got = lax.ppermute(given, "orient", mate_pairs)
 
@@ -400,15 +385,16 @@
         compiler_params=params,
     )(spot, partial, mate_partial, all_facts)
 
+    x_stats = lax.ppermute(stats, "cls", x_pairs)
+    across, _ = lax.optimization_barrier((across, stats))
     from_x = lax.ppermute(across, "cls", x_pairs)
-    class_stats = stats
-    for bit in range(chips.bit_length() - 1):
-        pairs = [(d, d ^ (2 << bit)) for d in range(devices)]
-        both = class_stats, lax.ppermute(class_stats, "orient", pairs)
-        peaks = jnp.maximum(both[0][0:2], both[1][0:2])
-        totals = sum(v[2:4] * jnp.exp(v[0:2] - peaks) for v in both)
-        class_stats = jnp.pad(jnp.concatenate([peaks, totals], axis=0), ((0, 4), (0, 0)))
-    other_stats = lax.ppermute(class_stats, "cls", x_pairs)
+    peak = jnp.maximum(stats[0], x_stats[1])
+    total = stats[2] * jnp.exp(stats[0] - peak) + x_stats[3] * jnp.exp(x_stats[1] - peak)
+    pair = jnp.pad(jnp.stack([peak, total]), ((0, 6), (0, 0)))
+    parts = [pair] + [
+        lax.ppermute(pair, "orient", [(d, (d + 2 * s) % devices) for d in range(devices)])
+        for s in range(1, chips)
+    ]
     slots, chosen, tops = pl.pallas_call(
         functools.partial(slot_kernel, local_search, slots_each, per_device),
         in_specs=[smem] + [vmem] * 3,
@@ -421,12 +407,12 @@
         compiler_params=params,
     )(spot, mine, from_x, all_facts)
     posterior = pl.pallas_call(
-        final_kernel,
-        in_specs=[vmem] * 5,
+        functools.partial(final_kernel, chips),
+        in_specs=[vmem] * (chips + 3),
         out_specs=vmem,
         out_shape=jax.ShapeDtypeStruct((capacity, 2 * orientations), jnp.float32),
         compiler_params=params,
-    )(class_stats, other_stats, tops, slots, chosen)
+    )(*parts, tops, slots, chosen)
     return posterior.reshape(1, 1, capacity, -1)
 
 

time: 63.6 us -> 62.1 us (0.976)
  waiting for transfers between devices: 16.9 us -> 14.9 us
  other arithmetic: 0.12 us -> 1.45 us
  local copies, waits for them, and re-layouts: 4.85 us -> 3.52 us
    ppermute x3 -> x4, starting transfers between devices: 4.03 us -> 6.74 us  [the longest x3 5.13 us: chip_shards(): lax.ppermute(pair, 'orient', [(d, (d + 2 * s) % devices) for d in range(d...]
    ppermute x1, starting transfers between devices: 2.56 us -> 0.45 us  [chip_shards(): from_x = lax.ppermute(across, 'cls', x_pairs)]
    ppermute x3 -> x4, waiting for transfers between devices: 3.99 us -> 2.2 us  [the longest x1 1.58 us: chip_shards(): x_stats = lax.ppermute(stats, 'cls', x_pairs)]
    convert_element_type x0 -> x2, other arithmetic: none -> 1.34 us  [chip_shards(): jnp.concatenate([defocus, jnp.transpose(block_ids[0])], axis=0, dtype=jnp...]
    unnamed x7 -> x3, local copies, waits for them, and re-layouts: 2.41 us -> 1.07 us
  transfers between devices with their start and end apart: 21 -> 22, of which waited for: 12 -> 10; matrix products, arithmetic and copies ran while one was open for 4% -> 4% of each run, Pallas kernels for 17% -> 18%
where the time goes in v11:
time: 62.1 us; the launch traced here: 61.9 us
  starting transfers between devices  25.4 us (41%)
  Pallas kernels  16.5 us (27%)
  waiting for transfers between devices  14.9 us (24%)
  local copies, waits for them, and re-layouts  3.52 us (6%)
  other arithmetic  1.45 us (2%)
    ppermute x14, starting transfers between devices, forward(): return lax.ppermute(values, ('orient', 'cls'), pairs)  16.3 us
    pallas_call x3, Pallas kernels, score_call(): pl.pallas_call(kernel, in_specs=[pl.BlockSpec(memory_space=pltpu.SMEM)] +...  12.3 us
    ppermute x14, waiting for transfers between devices, forward(): return lax.ppermute(values, ('orient', 'cls'), pairs)  11.1 us
    ppermute x3, starting transfers between devices, chip_shards(): lax.ppermute(pair, 'orient', [(d, (d + 2 * s) % devices) for d in range(d...  5.13 us
    optimization_barrier x1, local copies, waits for them, and re-layouts, chip_shards(): _, panels = lax.optimization_barrier((kept, panels))  2.42 us
    ppermute x1, starting transfers between devices, chip_shards(): x_stats = lax.ppermute(stats, 'cls', x_pairs)  1.61 us
    ppermute x1, waiting for transfers between devices, chip_shards(): x_stats = lax.ppermute(stats, 'cls', x_pairs)  1.58 us
    ppermute x1, waiting for transfers between devices, chip_shards(): mate_partial = lax.ppermute(partial, 'orient', mate_pairs)  1.52 us
  transfers between devices with their start and end apart: 22, of which 10 were waited for; matrix products, arithmetic and copies ran while one was open for 4% of the time, Pallas kernels for 18%

profile of v11, /device:TPU:0, one launch (start us, length us, event | category | flops | bytes accessed | tf_op | source)
XLA Modules:
  0.0 61.9 jit_solution(6352067023814121714)
XLA Ops:
  0.0 1.1 %copy.11 = bf16[1,16,2,7296]{3,1,2,0:T(8,128)(2,1)S(1)} copy(bf16[1,16,2,7296]{3,2,1,0:T(2,128)(2,1)} %param.5) | data formatting | bytes 933888 | tf_op args[0]
  1.1 0.7 %convert_bitcast_fusion = f32[4,16]{1,0:T(4,128)S(1)} fusion(s32[1,16,4]{1,2,0:T(4,128)} %param.7), kind=kLoop, calls=%fused_computation.5 | loop fusion | flops 64 | bytes 512 | tf_op jit(solution)/shard_map/convert_element_type | solution.py:307
  1.8 0.7 %convert_element_type.14 = f32[1,16]{1,0:T(1,128)S(1)} convert(bf16[1,16]{1,0:T(2,128)(2,1)} %param.6) | non-fusion elementwise | flops 16 | bytes 96 | tf_op jit(solution)/shard_map/convert_element_type | solution.py:307
  2.4 0.1 pad_add_fusion.spot
  2.5 0.6 shard_map.55
  3.1 2.4 %collective-permute-start.5 = (bf16[16,7424]{1,0:T(8,128)(2,1)S(1)}, bf16[16,7424]{1,0:T(8,128)(2,1)S(1)}, u32[]{:S(2)}, u32[]{:S(2)}) collective-permute-start(bf16[16,7424]{1,0:T(8,128)(2,1)S(1)} %get-tuple-element.33), channel_id=1, source_target_pairs={{0,3},{2,1},{4,2},{6,0},{8,6},{10,4},{12,10},{14,8},{13,14},{15,12... | collective-permute-start | bytes 712712 | tf_op jit(solution)/shard_map/rows_behind/ppermute | solution.py:300
  5.5 0.7 %collective-permute-start.2 = (bf16[16,7424]{1,0:T(8,128)(2,1)S(1)}, bf16[16,7424]{1,0:T(8,128)(2,1)S(1)}, u32[]{:S(2)}, u32[]{:S(2)}) collective-permute-start(bf16[16,7424]{1,0:T(8,128)(2,1)S(1)} %get-tuple-element.33), channel_id=1, source_target_pairs={{0,2},{2,0},{4,6},{6,4},{8,10},{10,8},{12,14},{14,12},{1,3},{3,1},... | collective-permute-start | bytes 712712 | tf_op jit(solution)/shard_map/mate_rows/ppermute | solution.py:317
  6.2 0.1 collective-permute-start
  6.3 1.9 %collective-permute-start.3 = (bf16[16,7424]{1,0:T(8,128)(2,1)S(1)}, bf16[16,7424]{1,0:T(8,128)(2,1)S(1)}, u32[]{:S(2)}, u32[]{:S(2)}) collective-permute-start(bf16[16,7424]{1,0:T(8,128)(2,1)S(1)} %get-tuple-element.29.refs_0_), channel_id=1, source_target_pairs={{0,1},{2,3},{4,0},{6,2},{8,4},{10,6},{12,8},{14,10},{13,12},{15,14... | collective-permute-start | bytes 712712 | tf_op jit(solution)/shard_map/rows_behind/ppermute | solution.py:300
  8.2 0.0 collective-permute-start.4
  8.2 2.4 %copy.10 = bf16[1,1,128,2,7296]{4,2,3,1,0:T(8,128)(2,1)S(1)} copy(bf16[1,1,128,2,7296]{4,3,2,1,0:T(2,128)(2,1)} %param.9) | data formatting | bytes 7471104 | tf_op jit(solution)/shard_map/optimization_barrier | solution.py:319
  10.7 0.8 %shard_map.56 = (bf16[128,7296]{1,0:T(8,128)(2,1)S(1)}, bf16[128,7296]{1,0:T(8,128)(2,1)S(1)}) custom-call(s32[4]{0:T(128)S(1)} %pad_add_fusion.spot, bf16[2,128,7296]{2,1,0:T(8,128)(2,1)S(1)} %bitcast.19), custom_call_target="tpu_custom_call" | custom-call | tf_op jit(solution)/shard_map/pallas_call | solution.py:322
  11.5 0.2 collective-permute-done.5.refs_5_
  11.7 1.2 %collective-permute-start.6 = (bf16[128,7296]{1,0:T(8,128)(2,1)S(1)}, bf16[128,7296]{1,0:T(8,128)(2,1)S(1)}, u32[]{:S(2)}, u32[]{:S(2)}) collective-permute-start(bf16[128,7296]{1,0:T(8,128)(2,1)S(1)} %get-tuple-element.34), channel_id=1, source_target_pairs={{0,2},{2,0},{4,6},{6,4},{8,10},{10,8},{12,14},{14,12},{1,3},{3,1},... | collective-permute-start | bytes 5603336 | tf_op jit(solution)/shard_map/mate_panel/ppermute | solution.py:330
  12.9 0.1 shard_map.57.refs_8_.refs_10_.refs_4_
  13.0 1.8 %collective-permute-done.refs_2_ = bf16[16,7424]{1,0:T(8,128)(2,1)S(1)} collective-permute-done((bf16[16,7424]{1,0:T(8,128)(2,1)S(1)}, bf16[16,7424]{1,0:T(8,128)(2,1)S(1)}, u32[]{:S(2)}, u32[]{:S(2)}) %collective-permute-start) | collective-permute-done | bytes 237600 | tf_op jit(solution)/shard_map/rows_ahead/ppermute | solution.py:300
  14.8 1.6 %collective-permute-start.9 = (bf16[16,7424]{1,0:T(8,128)(2,1)S(1)}, bf16[16,7424]{1,0:T(8,128)(2,1)S(1)}, u32[]{:S(2)}, u32[]{:S(2)}) collective-permute-start(bf16[16,7424]{1,0:T(8,128)(2,1)S(1)} %collective-permute-done.5.refs_5_), channel_id=1, source_target_pairs={{0,1},{2,3},{4,0},{6,2},{8,4},{10,6},{12,8},{14,10},{13,12},{15,14... | collective-permute-start | bytes 712712 | tf_op jit(solution)/shard_map/rows_behind/ppermute | solution.py:300
  16.4 0.0 collective-permute-done.2.refs_1_
  16.4 0.5 collective-permute-start.1
  16.9 1.0 %collective-permute-done.3.refs_3_ = bf16[16,7424]{1,0:T(8,128)(2,1)S(1)} collective-permute-done((bf16[16,7424]{1,0:T(8,128)(2,1)S(1)}, bf16[16,7424]{1,0:T(8,128)(2,1)S(1)}, u32[]{:S(2)}, u32[]{:S(2)}) %collective-permute-start.3) | collective-permute-done | bytes 237600 | tf_op jit(solution)/shard_map/rows_behind/ppermute | solution.py:300
  17.9 1.4 %collective-permute-start.12 = (bf16[16,7424]{1,0:T(8,128)(2,1)S(1)}, bf16[16,7424]{1,0:T(8,128)(2,1)S(1)}, u32[]{:S(2)}, u32[]{:S(2)}) collective-permute-start(bf16[16,7424]{1,0:T(8,128)(2,1)S(1)} %collective-permute-done.3.refs_3_), channel_id=1, source_target_pairs={{0,1},{2,3},{4,0},{6,2},{8,4},{10,6},{12,8},{14,10},{13,12},{15,14... | collective-permute-start | bytes 712712 | tf_op jit(solution)/shard_map/rows_behind/ppermute | solution.py:300
  19.3 0.0 collective-permute-done.4.refs_4_
  19.3 0.6 %collective-permute-start.13 = (bf16[16,7424]{1,0:T(8,128)(2,1)S(1)}, bf16[16,7424]{1,0:T(8,128)(2,1)S(1)}, u32[]{:S(2)}, u32[]{:S(2)}) collective-permute-start(bf16[16,7424]{1,0:T(8,128)(2,1)S(1)} %collective-permute-done.4.refs_4_), channel_id=1, source_target_pairs={{0,4},{2,6},{4,8},{6,10},{8,12},{10,14},{12,13},{14,15},{13,9},{15... | collective-permute-start | bytes 712712 | tf_op jit(solution)/shard_map/rows_ahead/ppermute | solution.py:300
  19.9 4.2 %shard_map.58 = (f32[96,128]{1,0:T(8,128)S(1)}, f32[96,128]{1,0:T(8,128)S(1)}, f32[96,128]{1,0:T(8,128)S(1)}) custom-call(s32[4]{0:T(128)S(1)} %pad_add_fusion.spot, bf16[16,7424]{1,0:T(8,128)(2,1)S(1)} %get-tuple-element.29.refs_0_, bf16[16,7424]{1,0:T(8,128)(2,1)S(1)} %collective-permute-done.2.refs_1_, bf16[16,7424]{1,0:T(8,128)(2,1)S(1)} %collective-permute-done.refs_2_, ...), custom_call_target="tpu_custom_call" | custom-call | flops 956301312 | bytes 5136384 | tf_op jit(solution)/shard_map/pallas_call | solution.py:177
  24.1 1.4 %collective-permute-start.10 = (bf16[16,7424]{1,0:T(8,128)(2,1)S(1)}, bf16[16,7424]{1,0:T(8,128)(2,1)S(1)}, u32[]{:S(2)}, u32[]{:S(2)}) collective-permute-start(bf16[16,7424]{1,0:T(8,128)(2,1)S(1)} %collective-permute-done.9.refs_3_), channel_id=1, source_target_pairs={{0,1},{2,3},{4,0},{6,2},{8,4},{10,6},{12,8},{14,10},{13,12},{15,14... | collective-permute-start | bytes 712712 | tf_op jit(solution)/shard_map/rows_behind/ppermute | solution.py:300
  25.6 0.6 %collective-permute-start.7 = (bf16[16,7424]{1,0:T(8,128)(2,1)S(1)}, bf16[16,7424]{1,0:T(8,128)(2,1)S(1)}, u32[]{:S(2)}, u32[]{:S(2)}) collective-permute-start(bf16[16,7424]{1,0:T(8,128)(2,1)S(1)} %collective-permute-done.1.refs_0_), channel_id=1, source_target_pairs={{0,4},{2,6},{4,8},{6,10},{8,12},{10,14},{12,13},{14,15},{13,9},{15... | collective-permute-start | bytes 712712 | tf_op jit(solution)/shard_map/rows_ahead/ppermute | solution.py:300
  26.2 1.4 %collective-permute-done.12.refs_1_ = bf16[16,7424]{1,0:T(8,128)(2,1)S(1)} collective-permute-done((bf16[16,7424]{1,0:T(8,128)(2,1)S(1)}, bf16[16,7424]{1,0:T(8,128)(2,1)S(1)}, u32[]{:S(2)}, u32[]{:S(2)}) %collective-permute-start.12) | collective-permute-done | bytes 237600 | tf_op jit(solution)/shard_map/rows_behind/ppermute | solution.py:300
  27.6 2.5 %collective-permute-start.14 = (bf16[16,7424]{1,0:T(8,128)(2,1)S(1)}, bf16[16,7424]{1,0:T(8,128)(2,1)S(1)}, u32[]{:S(2)}, u32[]{:S(2)}) collective-permute-start(bf16[16,7424]{1,0:T(8,128)(2,1)S(1)} %collective-permute-done.12.refs_1_), channel_id=1, source_target_pairs={{0,1},{2,3},{4,0},{6,2},{8,4},{10,6},{12,8},{14,10},{13,12},{15,14... | collective-permute-start | bytes 712712 | tf_op jit(solution)/shard_map/rows_behind/ppermute | solution.py:300
  30.1 0.4 collective-permute-start.15
  30.5 2.3 %collective-permute-done.10.refs_7_ = bf16[16,7424]{1,0:T(8,128)(2,1)S(1)} collective-permute-done((bf16[16,7424]{1,0:T(8,128)(2,1)S(1)}, bf16[16,7424]{1,0:T(8,128)(2,1)S(1)}, u32[]{:S(2)}, u32[]{:S(2)}) %collective-permute-start.10) | collective-permute-done | bytes 237600 | tf_op jit(solution)/shard_map/rows_behind/ppermute | solution.py:300
  32.8 2.4 %collective-permute-start.11 = (bf16[16,7424]{1,0:T(8,128)(2,1)S(1)}, bf16[16,7424]{1,0:T(8,128)(2,1)S(1)}, u32[]{:S(2)}, u32[]{:S(2)}) collective-permute-start(bf16[16,7424]{1,0:T(8,128)(2,1)S(1)} %collective-permute-done.10.refs_7_), channel_id=1, source_target_pairs={{0,1},{2,3},{4,0},{6,2},{8,4},{10,6},{12,8},{14,10},{13,12},{15,14... | collective-permute-start | bytes 712712 | tf_op jit(solution)/shard_map/rows_behind/ppermute | solution.py:300
  35.2 0.4 collective-permute-start.8
  35.6 2.3 %collective-permute-done.14.refs_5_ = bf16[16,7424]{1,0:T(8,128)(2,1)S(1)} collective-permute-done((bf16[16,7424]{1,0:T(8,128)(2,1)S(1)}, bf16[16,7424]{1,0:T(8,128)(2,1)S(1)}, u32[]{:S(2)}, u32[]{:S(2)}) %collective-permute-start.14) | collective-permute-done | bytes 237600 | tf_op jit(solution)/shard_map/rows_behind/ppermute | solution.py:300
  37.9 2.2 %collective-permute-done.15.refs_6_ = bf16[16,7424]{1,0:T(8,128)(2,1)S(1)} collective-permute-done((bf16[16,7424]{1,0:T(8,128)(2,1)S(1)}, bf16[16,7424]{1,0:T(8,128)(2,1)S(1)}, u32[]{:S(2)}, u32[]{:S(2)}) %collective-permute-start.15) | collective-permute-done | bytes 237600 | tf_op jit(solution)/shard_map/rows_ahead/ppermute | solution.py:300
  40.0 4.7 %shard_map.59 = (f32[128,128]{1,0:T(8,128)S(1)}, f32[128,128]{1,0:T(8,128)S(1)}, f32[128,128]{1,0:T(8,128)S(1)}) custom-call(s32[4]{0:T(128)S(1)} %pad_add_fusion.spot, bf16[16,7424]{1,0:T(8,128)(2,1)S(1)} %collective-permute-done.1.refs_0_, bf16[16,7424]{1,0:T(8,128)(2,1)S(1)} %collective-permute-done.12.refs_1_, ...), custom_call_target="tpu_custom_call" | custom-call | flops 956301312 | bytes 5603328 | tf_op jit(solution)/shard_map/pallas_call | solution.py:177
  44.7 3.4 %shard_map.60 = (f32[2,256,128]{2,1,0:T(8,128)S(1)}, f32[256,128]{1,0:T(8,128)S(1)}) custom-call(s32[4]{0:T(128)S(1)} %pad_add_fusion.spot, bf16[16,7424]{1,0:T(8,128)(2,1)S(1)} %collective-permute-done.8.refs_0_, bf16[16,7424]{1,0:T(8,128)(2,1)S(1)} %collective-permute-done.11.refs_1_, f32[1,7296]{1,0:T(1,128)S(1)} %broadcast_in_dim.3.refs_6_.refs_8_.refs_2_, ...), custom_call_target="tpu_custom_call" | custom-call | flops 956301312 | bytes 4202496 | tf_op jit(solution)/shard_map/pallas_call | solution.py:177
  48.1 0.1 collective-permute-start.16
  48.2 1.5 %collective-permute-done.16.mate = f32[2,256,128]{2,1,0:T(8,128)S(1)} collective-permute-done((f32[2,256,128]{2,1,0:T(8,128)S(1)}, f32[2,256,128]{2,1,0:T(8,128)S(1)}, u32[]{:S(2)}, u32[]{:S(2)}) %collective-permute-start.16) | collective-permute-done | bytes 262176 | tf_op jit(solution)/shard_map/ppermute | solution.py:375
  49.8 0.9 %shard_map.61 = (f32[128,128]{1,0:T(8,128)S(1)}, f32[128,128]{1,0:T(8,128)S(1)}, f32[8,128]{1,0:T(8,128)S(1)}) custom-call(s32[4]{0:T(128)S(1)} %pad_add_fusion.spot, f32[2,256,128]{2,1,0:T(8,128)S(1)} %get-tuple-element.44.partial, f32[2,256,128]{2,1,0:T(8,128)S(1)} %collective-permute-done.16.mate, f32[256,128]{1,0:T(8,128)S(1)} %get-tuple-element.45.facts), custom_call_target="tpu_custom_call" | custom-call | tf_op jit(solution)/shard_map/pallas_call | solution.py:376
  50.6 1.6 %collective-permute-start.17 = (f32[8,128]{1,0:T(8,128)S(1)}, f32[8,128]{1,0:T(8,128)S(1)}, u32[]{:S(2)}, u32[]{:S(2)}) collective-permute-start(f32[8,128]{1,0:T(8,128)S(1)} %get-tuple-element.46), channel_id=1, source_target_pairs={{0,1},{1,0},{2,3},{3,2},{4,5},{5,4},{6,7},{7,6},{8,9},{9,8},{10,11... | collective-permute-start | bytes 12296 | tf_op jit(solution)/shard_map/ppermute | solution.py:388
  52.2 0.4 collective-permute-start.21
  52.7 1.6 %collective-permute-done.17 = f32[8,128]{1,0:T(8,128)S(1)} collective-permute-done((f32[8,128]{1,0:T(8,128)S(1)}, f32[8,128]{1,0:T(8,128)S(1)}, u32[]{:S(2)}, u32[]{:S(2)}) %collective-permute-start.17) | collective-permute-done | bytes 4128 | tf_op jit(solution)/shard_map/ppermute | solution.py:388
  54.3 1.2 %collective-permute-start.18 = (f32[8,128]{1,0:T(8,128)S(1)}, f32[8,128]{1,0:T(8,128)S(1)}, u32[]{:S(2)}, u32[]{:S(2)}) collective-permute-start(f32[8,128]{1,0:T(8,128)S(1)} %select_maximum_fusion.refs_0_), channel_id=1, source_target_pairs={{0,4},{2,6},{4,8},{6,10},{8,12},{10,14},{12,0},{14,2},{1,5},{3,7},... | collective-permute-start | bytes 12296 | tf_op jit(solution)/shard_map/ppermute | solution.py:395
  55.5 2.0 %collective-permute-start.19 = (f32[8,128]{1,0:T(8,128)S(1)}, f32[8,128]{1,0:T(8,128)S(1)}, u32[]{:S(2)}, u32[]{:S(2)}) collective-permute-start(f32[8,128]{1,0:T(8,128)S(1)} %select_maximum_fusion.refs_0_), channel_id=1, source_target_pairs={{0,8},{2,10},{4,12},{6,14},{8,0},{10,2},{12,4},{14,6},{1,9},{3,11}... | collective-permute-start | bytes 12296 | tf_op jit(solution)/shard_map/ppermute | solution.py:395
  57.5 1.9 %collective-permute-start.20 = (f32[8,128]{1,0:T(8,128)S(1)}, f32[8,128]{1,0:T(8,128)S(1)}, u32[]{:S(2)}, u32[]{:S(2)}) collective-permute-start(f32[8,128]{1,0:T(8,128)S(1)} %select_maximum_fusion.refs_0_), channel_id=1, source_target_pairs={{0,12},{2,14},{4,0},{6,2},{8,4},{10,6},{12,8},{14,10},{1,13},{3,15... | collective-permute-start | bytes 12296 | tf_op jit(solution)/shard_map/ppermute | solution.py:395
  59.4 1.1 %shard_map.62 = (f32[128,256]{1,0:T(8,128)S(1)}, f32[128,128]{1,0:T(8,128)S(1)}, f32[8,128]{1,0:T(8,128)S(1)}) custom-call(s32[4]{0:T(128)S(1)} %pad_add_fusion.spot, f32[128,128]{1,0:T(8,128)S(1)} %get-tuple-element.47.mine, f32[128,128]{1,0:T(8,128)S(1)} %collective-permute-done.21.across, f32[256,128]{1,0:T(8,128)S(1)} %get-tuple-element.45.facts), custom_call_target="tpu_custom_call" | custom-call | tf_op jit(solution)/shard_map/pallas_call | solution.py:398
  60.5 0.6 collective-permute-done.20.refs_3_
  61.1 0.8 %shard_map.63 = f32[128,256]{1,0:T(8,128)} custom-call(f32[8,128]{1,0:T(8,128)S(1)} %select_maximum_fusion.refs_0_, f32[8,128]{1,0:T(8,128)S(1)} %collective-permute-done.18.refs_1_, f32[8,128]{1,0:T(8,128)S(1)} %collective-permute-done.19.refs_2_, f32[8,128]{1,0:T(8,128)S(1)} %collective-permute-done.20.refs_3_, f32[8,128]{1,0:T(8,128)S(1)} %get-tuple-element.50.refs_4_, ...), custom_call_target="tpu_custom_call" | custom-call | tf_op jit(solution)/shard_map/pallas_call | solution.py:409
  (16 shorter events, 0.1 us)
Async XLA Ops:
  3.1 8.6 %collective-permute-start.5 = (bf16[16,7424]{1,0:T(8,128)(2,1)S(1)}, bf16[16,7424]{1,0:T(8,128)(2,1)S(1)}, u32[]{:S(2)}, u32[]{:S(2)}) collective-permute-start(bf16[16,7424]{1,0:T(8,128)(2,1)S(1)} %get-tuple-element.33), channel_id=1, source_target_pairs={{0,3},{2,1},{4,2},{6,0},{8,6},{10,4},{12,10},{14,8},{13,14},{15,12... | collective-permute-start | bytes 712712 | tf_op jit(solution)/shard_map/rows_behind/ppermute | solution.py:300
  5.5 10.9 %collective-permute-start.2 = (bf16[16,7424]{1,0:T(8,128)(2,1)S(1)}, bf16[16,7424]{1,0:T(8,128)(2,1)S(1)}, u32[]{:S(2)}, u32[]{:S(2)}) collective-permute-start(bf16[16,7424]{1,0:T(8,128)(2,1)S(1)} %get-tuple-element.33), channel_id=1, source_target_pairs={{0,2},{2,0},{4,6},{6,4},{8,10},{10,8},{12,14},{14,12},{1,3},{3,1},... | collective-permute-start | bytes 712712 | tf_op jit(solution)/shard_map/mate_rows/ppermute | solution.py:317
  6.2 8.6 %collective-permute-start = (bf16[16,7424]{1,0:T(8,128)(2,1)S(1)}, bf16[16,7424]{1,0:T(8,128)(2,1)S(1)}, u32[]{:S(2)}, u32[]{:S(2)}) collective-permute-start(bf16[16,7424]{1,0:T(8,128)(2,1)S(1)} %get-tuple-element.29.refs_0_), channel_id=1, source_target_pairs={{0,4},{2,6},{4,8},{6,10},{8,12},{10,14},{12,13},{14,15},{13,9},{15... | collective-permute-start | bytes 712712 | tf_op jit(solution)/shard_map/rows_ahead/ppermute | solution.py:300
  6.3 11.6 %collective-permute-start.3 = (bf16[16,7424]{1,0:T(8,128)(2,1)S(1)}, bf16[16,7424]{1,0:T(8,128)(2,1)S(1)}, u32[]{:S(2)}, u32[]{:S(2)}) collective-permute-start(bf16[16,7424]{1,0:T(8,128)(2,1)S(1)} %get-tuple-element.29.refs_0_), channel_id=1, source_target_pairs={{0,1},{2,3},{4,0},{6,2},{8,4},{10,6},{12,8},{14,10},{13,12},{15,14... | collective-permute-start | bytes 712712 | tf_op jit(solution)/shard_map/rows_behind/ppermute | solution.py:300
  8.2 11.0 %collective-permute-start.4 = (bf16[16,7424]{1,0:T(8,128)(2,1)S(1)}, bf16[16,7424]{1,0:T(8,128)(2,1)S(1)}, u32[]{:S(2)}, u32[]{:S(2)}) collective-permute-start(bf16[16,7424]{1,0:T(8,128)(2,1)S(1)} %get-tuple-element.33), channel_id=1, source_target_pairs={{0,6},{2,4},{4,10},{6,8},{8,14},{10,12},{12,15},{14,13},{13,11},{1... | collective-permute-start | bytes 712712 | tf_op jit(solution)/shard_map/rows_ahead/ppermute | solution.py:300
  11.7 8.2 %collective-permute-start.6 = (bf16[128,7296]{1,0:T(8,128)(2,1)S(1)}, bf16[128,7296]{1,0:T(8,128)(2,1)S(1)}, u32[]{:S(2)}, u32[]{:S(2)}) collective-permute-start(bf16[128,7296]{1,0:T(8,128)(2,1)S(1)} %get-tuple-element.34), channel_id=1, source_target_pairs={{0,2},{2,0},{4,6},{6,4},{8,10},{10,8},{12,14},{14,12},{1,3},{3,1},... | collective-permute-start | bytes 5603336 | tf_op jit(solution)/shard_map/mate_panel/ppermute | solution.py:330
  12.9 4.0 %copy-start = (f32[7296]{0:T(1024)S(1)}, f32[7296]{0:T(1024)}, u32[]{:S(2)}) copy-start(f32[7296]{0:T(1024)} %param.8) | copy-start | bytes 87556
  14.8 9.3 %collective-permute-start.9 = (bf16[16,7424]{1,0:T(8,128)(2,1)S(1)}, bf16[16,7424]{1,0:T(8,128)(2,1)S(1)}, u32[]{:S(2)}, u32[]{:S(2)}) collective-permute-start(bf16[16,7424]{1,0:T(8,128)(2,1)S(1)} %collective-permute-done.5.refs_5_), channel_id=1, source_target_pairs={{0,1},{2,3},{4,0},{6,2},{8,4},{10,6},{12,8},{14,10},{13,12},{15,14... | collective-permute-start | bytes 712712 | tf_op jit(solution)/shard_map/rows_behind/ppermute | solution.py:300
  16.4 9.2 %collective-permute-start.1 = (bf16[16,7424]{1,0:T(8,128)(2,1)S(1)}, bf16[16,7424]{1,0:T(8,128)(2,1)S(1)}, u32[]{:S(2)}, u32[]{:S(2)}) collective-permute-start(bf16[16,7424]{1,0:T(8,128)(2,1)S(1)} %collective-permute-done.refs_2_), channel_id=1, source_target_pairs={{0,4},{2,6},{4,8},{6,10},{8,12},{10,14},{12,13},{14,15},{13,9},{15... | collective-permute-start | bytes 712712 | tf_op jit(solution)/shard_map/rows_ahead/ppermute | solution.py:300
  17.9 9.8 %collective-permute-start.12 = (bf16[16,7424]{1,0:T(8,128)(2,1)S(1)}, bf16[16,7424]{1,0:T(8,128)(2,1)S(1)}, u32[]{:S(2)}, u32[]{:S(2)}) collective-permute-start(bf16[16,7424]{1,0:T(8,128)(2,1)S(1)} %collective-permute-done.3.refs_3_), channel_id=1, source_target_pairs={{0,1},{2,3},{4,0},{6,2},{8,4},{10,6},{12,8},{14,10},{13,12},{15,14... | collective-permute-start | bytes 712712 | tf_op jit(solution)/shard_map/rows_behind/ppermute | solution.py:300
  19.3 10.9 %collective-permute-start.13 = (bf16[16,7424]{1,0:T(8,128)(2,1)S(1)}, bf16[16,7424]{1,0:T(8,128)(2,1)S(1)}, u32[]{:S(2)}, u32[]{:S(2)}) collective-permute-start(bf16[16,7424]{1,0:T(8,128)(2,1)S(1)} %collective-permute-done.4.refs_4_), channel_id=1, source_target_pairs={{0,4},{2,6},{4,8},{6,10},{8,12},{10,14},{12,13},{14,15},{13,9},{15... | collective-permute-start | bytes 712712 | tf_op jit(solution)/shard_map/rows_ahead/ppermute | solution.py:300
  24.1 8.7 %collective-permute-start.10 = (bf16[16,7424]{1,0:T(8,128)(2,1)S(1)}, bf16[16,7424]{1,0:T(8,128)(2,1)S(1)}, u32[]{:S(2)}, u32[]{:S(2)}) collective-permute-start(bf16[16,7424]{1,0:T(8,128)(2,1)S(1)} %collective-permute-done.9.refs_3_), channel_id=1, source_target_pairs={{0,1},{2,3},{4,0},{6,2},{8,4},{10,6},{12,8},{14,10},{13,12},{15,14... | collective-permute-start | bytes 712712 | tf_op jit(solution)/shard_map/rows_behind/ppermute | solution.py:300
  25.6 9.6 %collective-permute-start.7 = (bf16[16,7424]{1,0:T(8,128)(2,1)S(1)}, bf16[16,7424]{1,0:T(8,128)(2,1)S(1)}, u32[]{:S(2)}, u32[]{:S(2)}) collective-permute-start(bf16[16,7424]{1,0:T(8,128)(2,1)S(1)} %collective-permute-done.1.refs_0_), channel_id=1, source_target_pairs={{0,4},{2,6},{4,8},{6,10},{8,12},{10,14},{12,13},{14,15},{13,9},{15... | collective-permute-start | bytes 712712 | tf_op jit(solution)/shard_map/rows_ahead/ppermute | solution.py:300
  27.6 10.2 %collective-permute-start.14 = (bf16[16,7424]{1,0:T(8,128)(2,1)S(1)}, bf16[16,7424]{1,0:T(8,128)(2,1)S(1)}, u32[]{:S(2)}, u32[]{:S(2)}) collective-permute-start(bf16[16,7424]{1,0:T(8,128)(2,1)S(1)} %collective-permute-done.12.refs_1_), channel_id=1, source_target_pairs={{0,1},{2,3},{4,0},{6,2},{8,4},{10,6},{12,8},{14,10},{13,12},{15,14... | collective-permute-start | bytes 712712 | tf_op jit(solution)/shard_map/rows_behind/ppermute | solution.py:300
  30.1 9.9 %collective-permute-start.15 = (bf16[16,7424]{1,0:T(8,128)(2,1)S(1)}, bf16[16,7424]{1,0:T(8,128)(2,1)S(1)}, u32[]{:S(2)}, u32[]{:S(2)}) collective-permute-start(bf16[16,7424]{1,0:T(8,128)(2,1)S(1)} %collective-permute-done.13.refs_2_), channel_id=1, source_target_pairs={{0,4},{2,6},{4,8},{6,10},{8,12},{10,14},{12,13},{14,15},{13,9},{15... | collective-permute-start | bytes 712712 | tf_op jit(solution)/shard_map/rows_ahead/ppermute | solution.py:300
  32.8 11.9 %collective-permute-start.11 = (bf16[16,7424]{1,0:T(8,128)(2,1)S(1)}, bf16[16,7424]{1,0:T(8,128)(2,1)S(1)}, u32[]{:S(2)}, u32[]{:S(2)}) collective-permute-start(bf16[16,7424]{1,0:T(8,128)(2,1)S(1)} %collective-permute-done.10.refs_7_), channel_id=1, source_target_pairs={{0,1},{2,3},{4,0},{6,2},{8,4},{10,6},{12,8},{14,10},{13,12},{15,14... | collective-permute-start | bytes 712712 | tf_op jit(solution)/shard_map/rows_behind/ppermute | solution.py:300
  35.2 9.5 %collective-permute-start.8 = (bf16[16,7424]{1,0:T(8,128)(2,1)S(1)}, bf16[16,7424]{1,0:T(8,128)(2,1)S(1)}, u32[]{:S(2)}, u32[]{:S(2)}) collective-permute-start(bf16[16,7424]{1,0:T(8,128)(2,1)S(1)} %collective-permute-done.7.refs_4_), channel_id=1, source_target_pairs={{0,4},{2,6},{4,8},{6,10},{8,12},{10,14},{12,13},{14,15},{13,9},{15... | collective-permute-start | bytes 712712 | tf_op jit(solution)/shard_map/rows_ahead/ppermute | solution.py:300
  48.1 1.6 %collective-permute-start.16 = (f32[2,256,128]{2,1,0:T(8,128)S(1)}, f32[2,256,128]{2,1,0:T(8,128)S(1)}, u32[]{:S(2)}, u32[]{:S(2)}) collective-permute-start(f32[2,256,128]{2,1,0:T(8,128)S(1)} %get-tuple-element.44.partial), channel_id=1, source_target_pairs={{0,2},{2,0},{4,6},{6,4},{8,10},{10,8},{12,14},{14,12},{1,3},{3,1},... | collective-permute-start | bytes 786440 | tf_op jit(solution)/shard_map/ppermute | solution.py:375
  50.6 3.6 %collective-permute-start.17 = (f32[8,128]{1,0:T(8,128)S(1)}, f32[8,128]{1,0:T(8,128)S(1)}, u32[]{:S(2)}, u32[]{:S(2)}) collective-permute-start(f32[8,128]{1,0:T(8,128)S(1)} %get-tuple-element.46), channel_id=1, source_target_pairs={{0,1},{1,0},{2,3},{3,2},{4,5},{5,4},{6,7},{7,6},{8,9},{9,8},{10,11... | collective-permute-start | bytes 12296 | tf_op jit(solution)/shard_map/ppermute | solution.py:388
  52.2 7.2 %collective-permute-start.21 = (f32[128,128]{1,0:T(8,128)S(1)}, f32[128,128]{1,0:T(8,128)S(1)}, u32[]{:S(2)}, u32[]{:S(2)}) collective-permute-start(f32[128,128]{1,0:T(8,128)S(1)} %get-tuple-element.49), channel_id=1, source_target_pairs={{0,1},{1,0},{2,3},{3,2},{4,5},{5,4},{6,7},{7,6},{8,9},{9,8},{10,11... | collective-permute-start | bytes 196616 | tf_op jit(solution)/shard_map/ppermute | solution.py:390
  54.3 6.2 %collective-permute-start.18 = (f32[8,128]{1,0:T(8,128)S(1)}, f32[8,128]{1,0:T(8,128)S(1)}, u32[]{:S(2)}, u32[]{:S(2)}) collective-permute-start(f32[8,128]{1,0:T(8,128)S(1)} %select_maximum_fusion.refs_0_), channel_id=1, source_target_pairs={{0,4},{2,6},{4,8},{6,10},{8,12},{10,14},{12,0},{14,2},{1,5},{3,7},... | collective-permute-start | bytes 12296 | tf_op jit(solution)/shard_map/ppermute | solution.py:395
  55.5 5.0 %collective-permute-start.19 = (f32[8,128]{1,0:T(8,128)S(1)}, f32[8,128]{1,0:T(8,128)S(1)}, u32[]{:S(2)}, u32[]{:S(2)}) collective-permute-start(f32[8,128]{1,0:T(8,128)S(1)} %select_maximum_fusion.refs_0_), channel_id=1, source_target_pairs={{0,8},{2,10},{4,12},{6,14},{8,0},{10,2},{12,4},{14,6},{1,9},{3,11}... | collective-permute-start | bytes 12296 | tf_op jit(solution)/shard_map/ppermute | solution.py:395
  57.5 3.6 %collective-permute-start.20 = (f32[8,128]{1,0:T(8,128)S(1)}, f32[8,128]{1,0:T(8,128)S(1)}, u32[]{:S(2)}, u32[]{:S(2)}) collective-permute-start(f32[8,128]{1,0:T(8,128)S(1)} %select_maximum_fusion.refs_0_), channel_id=1, source_target_pairs={{0,12},{2,14},{4,0},{6,2},{8,4},{10,6},{12,8},{14,10},{1,13},{3,15... | collective-permute-start | bytes 12296 | tf_op jit(solution)/shard_map/ppermute | solution.py:395

commit v12 on v11

--- a/solution.py
+++ b/solution.py
@@ -391,10 +391,15 @@
     peak = jnp.maximum(stats[0], x_stats[1])
     total = stats[2] * jnp.exp(stats[0] - peak) + x_stats[3] * jnp.exp(x_stats[1] - peak)
     pair = jnp.pad(jnp.stack([peak, total]), ((0, 6), (0, 0)))
-    parts = [pair] + [
-        lax.ppermute(pair, "orient", [(d, (d + 2 * s) % devices) for d in range(devices)])
-        for s in range(1, chips)
-    ]
+    if chips == 4:
+        near = lax.ppermute(pair, "orient", [(d, d ^ (2 << d % 2)) for d in range(devices)])
+        far = lax.ppermute(pair, "orient", [(d, d ^ 6) for d in range(devices)])
+        parts = [pair, near, lax.ppermute(near, "orient", mate_pairs), far]
+    else:
+        parts = [pair] + [
+            lax.ppermute(pair, "orient", [(d, (d + 2 * s) % devices) for d in range(devices)])
+            for s in range(1, chips)
+        ]
     slots, chosen, tops = pl.pallas_call(
         functools.partial(slot_kernel, local_search, slots_each, per_device),
         in_specs=[smem] + [vmem] * 3,

time: 62.1 us -> 61.9 us (level)
  starting transfers between devices: 25.4 us -> 24 us
  waiting for transfers between devices: 14.9 us -> 16.1 us
    ppermute x3, starting transfers between devices: 5.13 us -> 3.68 us  [the longest x1 2.48 us: chip_shards(): far = lax.ppermute(pair, 'orient', [(d, d ^ 6) for d in range(devices)])]
    ppermute x3, waiting for transfers between devices: 0.62 us -> 1.84 us  [the longest x1 1.84 us: chip_shards(): far = lax.ppermute(pair, 'orient', [(d, d ^ 6) for d in range(devices)])]
where the time goes in v12:
time: 61.9 us; the launch traced here: 61.7 us
  starting transfers between devices  24 us (39%)
  Pallas kernels  16.5 us (27%)
  waiting for transfers between devices  16.1 us (26%)
  local copies, waits for them, and re-layouts  3.52 us (6%)
  other arithmetic  1.45 us (2%)
    ppermute x14, starting transfers between devices, forward(): return lax.ppermute(values, ('orient', 'cls'), pairs)  16.3 us
    pallas_call x3, Pallas kernels, score_call(): pl.pallas_call(kernel, in_specs=[pl.BlockSpec(memory_space=pltpu.SMEM)] +...  12.3 us
    ppermute x14, waiting for transfers between devices, forward(): return lax.ppermute(values, ('orient', 'cls'), pairs)  11.1 us
    ppermute x1, starting transfers between devices, chip_shards(): far = lax.ppermute(pair, 'orient', [(d, d ^ 6) for d in range(devices)])  2.48 us
    optimization_barrier x1, local copies, waits for them, and re-layouts, chip_shards(): _, panels = lax.optimization_barrier((kept, panels))  2.42 us
    ppermute x1, waiting for transfers between devices, chip_shards(): far = lax.ppermute(pair, 'orient', [(d, d ^ 6) for d in range(devices)])  1.84 us
    ppermute x1, starting transfers between devices, chip_shards(): x_stats = lax.ppermute(stats, 'cls', x_pairs)  1.61 us
    ppermute x1, waiting for transfers between devices, chip_shards(): x_stats = lax.ppermute(stats, 'cls', x_pairs)  1.58 us
  transfers between devices with their start and end apart: 22, of which 10 were waited for; matrix products, arithmetic and copies ran while one was open for 4% of the time, Pallas kernels for 18%

profile of v12, /device:TPU:0, one launch (start us, length us, event | category | flops | bytes accessed | tf_op | source)
XLA Modules:
  0.0 61.7 jit_solution(10017739085084107624)
XLA Ops:
  0.0 1.1 %copy.11 = bf16[1,16,2,7296]{3,1,2,0:T(8,128)(2,1)S(1)} copy(bf16[1,16,2,7296]{3,2,1,0:T(2,128)(2,1)} %param.5) | data formatting | bytes 933888 | tf_op args[0]
  1.1 0.7 %convert_bitcast_fusion = f32[4,16]{1,0:T(4,128)S(1)} fusion(s32[1,16,4]{1,2,0:T(4,128)} %param.7), kind=kLoop, calls=%fused_computation.5 | loop fusion | flops 64 | bytes 512 | tf_op jit(solution)/shard_map/convert_element_type | solution.py:307
  1.8 0.7 %convert_element_type.14 = f32[1,16]{1,0:T(1,128)S(1)} convert(bf16[1,16]{1,0:T(2,128)(2,1)} %param.6) | non-fusion elementwise | flops 16 | bytes 96 | tf_op jit(solution)/shard_map/convert_element_type | solution.py:307
  2.4 0.1 pad_add_fusion.spot
  2.5 0.6 shard_map.55
  3.1 2.4 %collective-permute-start.5 = (bf16[16,7424]{1,0:T(8,128)(2,1)S(1)}, bf16[16,7424]{1,0:T(8,128)(2,1)S(1)}, u32[]{:S(2)}, u32[]{:S(2)}) collective-permute-start(bf16[16,7424]{1,0:T(8,128)(2,1)S(1)} %get-tuple-element.33), channel_id=1, source_target_pairs={{0,3},{2,1},{4,2},{6,0},{8,6},{10,4},{12,10},{14,8},{13,14},{15,12... | collective-permute-start | bytes 712712 | tf_op jit(solution)/shard_map/rows_behind/ppermute | solution.py:300
  5.5 0.7 %collective-permute-start.2 = (bf16[16,7424]{1,0:T(8,128)(2,1)S(1)}, bf16[16,7424]{1,0:T(8,128)(2,1)S(1)}, u32[]{:S(2)}, u32[]{:S(2)}) collective-permute-start(bf16[16,7424]{1,0:T(8,128)(2,1)S(1)} %get-tuple-element.33), channel_id=1, source_target_pairs={{0,2},{2,0},{4,6},{6,4},{8,10},{10,8},{12,14},{14,12},{1,3},{3,1},... | collective-permute-start | bytes 712712 | tf_op jit(solution)/shard_map/mate_rows/ppermute | solution.py:317
  6.2 0.1 collective-permute-start
  6.3 1.9 %collective-permute-start.3 = (bf16[16,7424]{1,0:T(8,128)(2,1)S(1)}, bf16[16,7424]{1,0:T(8,128)(2,1)S(1)}, u32[]{:S(2)}, u32[]{:S(2)}) collective-permute-start(bf16[16,7424]{1,0:T(8,128)(2,1)S(1)} %get-tuple-element.29.refs_0_), channel_id=1, source_target_pairs={{0,1},{2,3},{4,0},{6,2},{8,4},{10,6},{12,8},{14,10},{13,12},{15,14... | collective-permute-start | bytes 712712 | tf_op jit(solution)/shard_map/rows_behind/ppermute | solution.py:300
  8.2 0.0 collective-permute-start.4
  8.2 2.4 %copy.10 = bf16[1,1,128,2,7296]{4,2,3,1,0:T(8,128)(2,1)S(1)} copy(bf16[1,1,128,2,7296]{4,3,2,1,0:T(2,128)(2,1)} %param.9) | data formatting | bytes 7471104 | tf_op jit(solution)/shard_map/optimization_barrier | solution.py:319
  10.7 0.8 %shard_map.56 = (bf16[128,7296]{1,0:T(8,128)(2,1)S(1)}, bf16[128,7296]{1,0:T(8,128)(2,1)S(1)}) custom-call(s32[4]{0:T(128)S(1)} %pad_add_fusion.spot, bf16[2,128,7296]{2,1,0:T(8,128)(2,1)S(1)} %bitcast.19), custom_call_target="tpu_custom_call" | custom-call | tf_op jit(solution)/shard_map/pallas_call | solution.py:322
  11.5 0.2 collective-permute-done.5.refs_5_
  11.7 1.2 %collective-permute-start.6 = (bf16[128,7296]{1,0:T(8,128)(2,1)S(1)}, bf16[128,7296]{1,0:T(8,128)(2,1)S(1)}, u32[]{:S(2)}, u32[]{:S(2)}) collective-permute-start(bf16[128,7296]{1,0:T(8,128)(2,1)S(1)} %get-tuple-element.34), channel_id=1, source_target_pairs={{0,2},{2,0},{4,6},{6,4},{8,10},{10,8},{12,14},{14,12},{1,3},{3,1},... | collective-permute-start | bytes 5603336 | tf_op jit(solution)/shard_map/mate_panel/ppermute | solution.py:330
  12.9 0.1 shard_map.57.refs_8_.refs_10_.refs_4_
  13.0 1.8 %collective-permute-done.refs_2_ = bf16[16,7424]{1,0:T(8,128)(2,1)S(1)} collective-permute-done((bf16[16,7424]{1,0:T(8,128)(2,1)S(1)}, bf16[16,7424]{1,0:T(8,128)(2,1)S(1)}, u32[]{:S(2)}, u32[]{:S(2)}) %collective-permute-start) | collective-permute-done | bytes 237600 | tf_op jit(solution)/shard_map/rows_ahead/ppermute | solution.py:300
  14.8 1.6 %collective-permute-start.9 = (bf16[16,7424]{1,0:T(8,128)(2,1)S(1)}, bf16[16,7424]{1,0:T(8,128)(2,1)S(1)}, u32[]{:S(2)}, u32[]{:S(2)}) collective-permute-start(bf16[16,7424]{1,0:T(8,128)(2,1)S(1)} %collective-permute-done.5.refs_5_), channel_id=1, source_target_pairs={{0,1},{2,3},{4,0},{6,2},{8,4},{10,6},{12,8},{14,10},{13,12},{15,14... | collective-permute-start | bytes 712712 | tf_op jit(solution)/shard_map/rows_behind/ppermute | solution.py:300
  16.4 0.0 collective-permute-done.2.refs_1_
  16.4 0.5 collective-permute-start.1
  16.9 1.0 %collective-permute-done.3.refs_3_ = bf16[16,7424]{1,0:T(8,128)(2,1)S(1)} collective-permute-done((bf16[16,7424]{1,0:T(8,128)(2,1)S(1)}, bf16[16,7424]{1,0:T(8,128)(2,1)S(1)}, u32[]{:S(2)}, u32[]{:S(2)}) %collective-permute-start.3) | collective-permute-done | bytes 237600 | tf_op jit(solution)/shard_map/rows_behind/ppermute | solution.py:300
  17.9 1.4 %collective-permute-start.12 = (bf16[16,7424]{1,0:T(8,128)(2,1)S(1)}, bf16[16,7424]{1,0:T(8,128)(2,1)S(1)}, u32[]{:S(2)}, u32[]{:S(2)}) collective-permute-start(bf16[16,7424]{1,0:T(8,128)(2,1)S(1)} %collective-permute-done.3.refs_3_), channel_id=1, source_target_pairs={{0,1},{2,3},{4,0},{6,2},{8,4},{10,6},{12,8},{14,10},{13,12},{15,14... | collective-permute-start | bytes 712712 | tf_op jit(solution)/shard_map/rows_behind/ppermute | solution.py:300
  19.3 0.0 collective-permute-done.4.refs_4_
  19.3 0.6 %collective-permute-start.13 = (bf16[16,7424]{1,0:T(8,128)(2,1)S(1)}, bf16[16,7424]{1,0:T(8,128)(2,1)S(1)}, u32[]{:S(2)}, u32[]{:S(2)}) collective-permute-start(bf16[16,7424]{1,0:T(8,128)(2,1)S(1)} %collective-permute-done.4.refs_4_), channel_id=1, source_target_pairs={{0,4},{2,6},{4,8},{6,10},{8,12},{10,14},{12,13},{14,15},{13,9},{15... | collective-permute-start | bytes 712712 | tf_op jit(solution)/shard_map/rows_ahead/ppermute | solution.py:300
  19.9 0.0 collective-permute-done.6.refs_9_.refs_11_.refs_5_
  19.9 4.2 %shard_map.58 = (f32[96,128]{1,0:T(8,128)S(1)}, f32[96,128]{1,0:T(8,128)S(1)}, f32[96,128]{1,0:T(8,128)S(1)}) custom-call(s32[4]{0:T(128)S(1)} %pad_add_fusion.spot, bf16[16,7424]{1,0:T(8,128)(2,1)S(1)} %get-tuple-element.29.refs_0_, bf16[16,7424]{1,0:T(8,128)(2,1)S(1)} %collective-permute-done.2.refs_1_, bf16[16,7424]{1,0:T(8,128)(2,1)S(1)} %collective-permute-done.refs_2_, ...), custom_call_target="tpu_custom_call" | custom-call | flops 956301312 | bytes 5136384 | tf_op jit(solution)/shard_map/pallas_call | solution.py:177
  24.1 1.4 %collective-permute-start.10 = (bf16[16,7424]{1,0:T(8,128)(2,1)S(1)}, bf16[16,7424]{1,0:T(8,128)(2,1)S(1)}, u32[]{:S(2)}, u32[]{:S(2)}) collective-permute-start(bf16[16,7424]{1,0:T(8,128)(2,1)S(1)} %collective-permute-done.9.refs_3_), channel_id=1, source_target_pairs={{0,1},{2,3},{4,0},{6,2},{8,4},{10,6},{12,8},{14,10},{13,12},{15,14... | collective-permute-start | bytes 712712 | tf_op jit(solution)/shard_map/rows_behind/ppermute | solution.py:300
  25.6 0.6 %collective-permute-start.7 = (bf16[16,7424]{1,0:T(8,128)(2,1)S(1)}, bf16[16,7424]{1,0:T(8,128)(2,1)S(1)}, u32[]{:S(2)}, u32[]{:S(2)}) collective-permute-start(bf16[16,7424]{1,0:T(8,128)(2,1)S(1)} %collective-permute-done.1.refs_0_), channel_id=1, source_target_pairs={{0,4},{2,6},{4,8},{6,10},{8,12},{10,14},{12,13},{14,15},{13,9},{15... | collective-permute-start | bytes 712712 | tf_op jit(solution)/shard_map/rows_ahead/ppermute | solution.py:300
  26.2 1.4 %collective-permute-done.12.refs_1_ = bf16[16,7424]{1,0:T(8,128)(2,1)S(1)} collective-permute-done((bf16[16,7424]{1,0:T(8,128)(2,1)S(1)}, bf16[16,7424]{1,0:T(8,128)(2,1)S(1)}, u32[]{:S(2)}, u32[]{:S(2)}) %collective-permute-start.12) | collective-permute-done | bytes 237600 | tf_op jit(solution)/shard_map/rows_behind/ppermute | solution.py:300
  27.6 2.5 %collective-permute-start.14 = (bf16[16,7424]{1,0:T(8,128)(2,1)S(1)}, bf16[16,7424]{1,0:T(8,128)(2,1)S(1)}, u32[]{:S(2)}, u32[]{:S(2)}) collective-permute-start(bf16[16,7424]{1,0:T(8,128)(2,1)S(1)} %collective-permute-done.12.refs_1_), channel_id=1, source_target_pairs={{0,1},{2,3},{4,0},{6,2},{8,4},{10,6},{12,8},{14,10},{13,12},{15,14... | collective-permute-start | bytes 712712 | tf_op jit(solution)/shard_map/rows_behind/ppermute | solution.py:300
  30.1 0.4 collective-permute-start.15
  30.5 2.3 %collective-permute-done.10.refs_7_ = bf16[16,7424]{1,0:T(8,128)(2,1)S(1)} collective-permute-done((bf16[16,7424]{1,0:T(8,128)(2,1)S(1)}, bf16[16,7424]{1,0:T(8,128)(2,1)S(1)}, u32[]{:S(2)}, u32[]{:S(2)}) %collective-permute-start.10) | collective-permute-done | bytes 237600 | tf_op jit(solution)/shard_map/rows_behind/ppermute | solution.py:300
  32.8 2.4 %collective-permute-start.11 = (bf16[16,7424]{1,0:T(8,128)(2,1)S(1)}, bf16[16,7424]{1,0:T(8,128)(2,1)S(1)}, u32[]{:S(2)}, u32[]{:S(2)}) collective-permute-start(bf16[16,7424]{1,0:T(8,128)(2,1)S(1)} %collective-permute-done.10.refs_7_), channel_id=1, source_target_pairs={{0,1},{2,3},{4,0},{6,2},{8,4},{10,6},{12,8},{14,10},{13,12},{15,14... | collective-permute-start | bytes 712712 | tf_op jit(solution)/shard_map/rows_behind/ppermute | solution.py:300
  35.2 0.4 collective-permute-start.8
  35.6 2.3 %collective-permute-done.14.refs_5_ = bf16[16,7424]{1,0:T(8,128)(2,1)S(1)} collective-permute-done((bf16[16,7424]{1,0:T(8,128)(2,1)S(1)}, bf16[16,7424]{1,0:T(8,128)(2,1)S(1)}, u32[]{:S(2)}, u32[]{:S(2)}) %collective-permute-start.14) | collective-permute-done | bytes 237600 | tf_op jit(solution)/shard_map/rows_behind/ppermute | solution.py:300
  37.9 2.2 %collective-permute-done.15.refs_6_ = bf16[16,7424]{1,0:T(8,128)(2,1)S(1)} collective-permute-done((bf16[16,7424]{1,0:T(8,128)(2,1)S(1)}, bf16[16,7424]{1,0:T(8,128)(2,1)S(1)}, u32[]{:S(2)}, u32[]{:S(2)}) %collective-permute-start.15) | collective-permute-done | bytes 237600 | tf_op jit(solution)/shard_map/rows_ahead/ppermute | solution.py:300
  40.0 4.7 %shard_map.59 = (f32[128,128]{1,0:T(8,128)S(1)}, f32[128,128]{1,0:T(8,128)S(1)}, f32[128,128]{1,0:T(8,128)S(1)}) custom-call(s32[4]{0:T(128)S(1)} %pad_add_fusion.spot, bf16[16,7424]{1,0:T(8,128)(2,1)S(1)} %collective-permute-done.1.refs_0_, bf16[16,7424]{1,0:T(8,128)(2,1)S(1)} %collective-permute-done.12.refs_1_, ...), custom_call_target="tpu_custom_call" | custom-call | flops 956301312 | bytes 5603328 | tf_op jit(solution)/shard_map/pallas_call | solution.py:177
  44.7 3.4 %shard_map.60 = (f32[2,256,128]{2,1,0:T(8,128)S(1)}, f32[256,128]{1,0:T(8,128)S(1)}) custom-call(s32[4]{0:T(128)S(1)} %pad_add_fusion.spot, bf16[16,7424]{1,0:T(8,128)(2,1)S(1)} %collective-permute-done.8.refs_0_, bf16[16,7424]{1,0:T(8,128)(2,1)S(1)} %collective-permute-done.11.refs_1_, f32[1,7296]{1,0:T(1,128)S(1)} %broadcast_in_dim.3.refs_6_.refs_8_.refs_2_, ...), custom_call_target="tpu_custom_call" | custom-call | flops 956301312 | bytes 4202496 | tf_op jit(solution)/shard_map/pallas_call | solution.py:177
  48.1 0.1 collective-permute-start.16
  48.2 1.5 %collective-permute-done.16.mate = f32[2,256,128]{2,1,0:T(8,128)S(1)} collective-permute-done((f32[2,256,128]{2,1,0:T(8,128)S(1)}, f32[2,256,128]{2,1,0:T(8,128)S(1)}, u32[]{:S(2)}, u32[]{:S(2)}) %collective-permute-start.16) | collective-permute-done | bytes 262176 | tf_op jit(solution)/shard_map/ppermute | solution.py:375
  49.8 0.9 %shard_map.61 = (f32[128,128]{1,0:T(8,128)S(1)}, f32[128,128]{1,0:T(8,128)S(1)}, f32[8,128]{1,0:T(8,128)S(1)}) custom-call(s32[4]{0:T(128)S(1)} %pad_add_fusion.spot, f32[2,256,128]{2,1,0:T(8,128)S(1)} %get-tuple-element.44.partial, f32[2,256,128]{2,1,0:T(8,128)S(1)} %collective-permute-done.16.mate, f32[256,128]{1,0:T(8,128)S(1)} %get-tuple-element.45.facts), custom_call_target="tpu_custom_call" | custom-call | tf_op jit(solution)/shard_map/pallas_call | solution.py:376
  50.6 1.6 %collective-permute-start.17 = (f32[8,128]{1,0:T(8,128)S(1)}, f32[8,128]{1,0:T(8,128)S(1)}, u32[]{:S(2)}, u32[]{:S(2)}) collective-permute-start(f32[8,128]{1,0:T(8,128)S(1)} %get-tuple-element.46), channel_id=1, source_target_pairs={{0,1},{1,0},{2,3},{3,2},{4,5},{5,4},{6,7},{7,6},{8,9},{9,8},{10,11... | collective-permute-start | bytes 12296 | tf_op jit(solution)/shard_map/ppermute | solution.py:388
  52.2 0.4 collective-permute-start.21
  52.7 1.6 %collective-permute-done.17 = f32[8,128]{1,0:T(8,128)S(1)} collective-permute-done((f32[8,128]{1,0:T(8,128)S(1)}, f32[8,128]{1,0:T(8,128)S(1)}, u32[]{:S(2)}, u32[]{:S(2)}) %collective-permute-start.17) | collective-permute-done | bytes 4128 | tf_op jit(solution)/shard_map/ppermute | solution.py:388
  54.3 1.2 %collective-permute-start.18 = (f32[8,128]{1,0:T(8,128)S(1)}, f32[8,128]{1,0:T(8,128)S(1)}, u32[]{:S(2)}, u32[]{:S(2)}) collective-permute-start(f32[8,128]{1,0:T(8,128)S(1)} %select_maximum_fusion.refs_0_), channel_id=1, source_target_pairs={{0,4},{2,10},{4,0},{6,14},{8,12},{10,2},{12,8},{14,6},{1,5},{3,11}... | collective-permute-start | bytes 12296 | tf_op jit(solution)/shard_map/ppermute | solution.py:395
  55.5 2.5 %collective-permute-start.20 = (f32[8,128]{1,0:T(8,128)S(1)}, f32[8,128]{1,0:T(8,128)S(1)}, u32[]{:S(2)}, u32[]{:S(2)}) collective-permute-start(f32[8,128]{1,0:T(8,128)S(1)} %select_maximum_fusion.refs_0_), channel_id=1, source_target_pairs={{0,12},{2,14},{4,8},{6,10},{8,4},{10,6},{12,0},{14,2},{1,13},{3,15... | collective-permute-start | bytes 12296 | tf_op jit(solution)/shard_map/ppermute | solution.py:396
  58.0 1.1 %shard_map.62 = (f32[128,256]{1,0:T(8,128)S(1)}, f32[128,128]{1,0:T(8,128)S(1)}, f32[8,128]{1,0:T(8,128)S(1)}) custom-call(s32[4]{0:T(128)S(1)} %pad_add_fusion.spot, f32[128,128]{1,0:T(8,128)S(1)} %get-tuple-element.47.mine, f32[128,128]{1,0:T(8,128)S(1)} %collective-permute-done.21.across, f32[256,128]{1,0:T(8,128)S(1)} %get-tuple-element.45.facts), custom_call_target="tpu_custom_call" | custom-call | tf_op jit(solution)/shard_map/pallas_call | solution.py:403
  59.1 1.8 %collective-permute-done.20.refs_3_ = f32[8,128]{1,0:T(8,128)S(1)} collective-permute-done((f32[8,128]{1,0:T(8,128)S(1)}, f32[8,128]{1,0:T(8,128)S(1)}, u32[]{:S(2)}, u32[]{:S(2)}) %collective-permute-start.20) | collective-permute-done | bytes 4128 | tf_op jit(solution)/shard_map/ppermute | solution.py:396
  60.9 0.8 %shard_map.63 = f32[128,256]{1,0:T(8,128)} custom-call(f32[8,128]{1,0:T(8,128)S(1)} %select_maximum_fusion.refs_0_, f32[8,128]{1,0:T(8,128)S(1)} %collective-permute-done.18.refs_1_, f32[8,128]{1,0:T(8,128)S(1)} %collective-permute-done.19.refs_2_, f32[8,128]{1,0:T(8,128)S(1)} %collective-permute-done.20.refs_3_, f32[8,128]{1,0:T(8,128)S(1)} %get-tuple-element.50.refs_4_, ...), custom_call_target="tpu_custom_call" | custom-call | tf_op jit(solution)/shard_map/pallas_call | solution.py:414
  (16 shorter events, 0.1 us)
Async XLA Ops:
  3.1 8.6 %collective-permute-start.5 = (bf16[16,7424]{1,0:T(8,128)(2,1)S(1)}, bf16[16,7424]{1,0:T(8,128)(2,1)S(1)}, u32[]{:S(2)}, u32[]{:S(2)}) collective-permute-start(bf16[16,7424]{1,0:T(8,128)(2,1)S(1)} %get-tuple-element.33), channel_id=1, source_target_pairs={{0,3},{2,1},{4,2},{6,0},{8,6},{10,4},{12,10},{14,8},{13,14},{15,12... | collective-permute-start | bytes 712712 | tf_op jit(solution)/shard_map/rows_behind/ppermute | solution.py:300
  5.5 10.9 %collective-permute-start.2 = (bf16[16,7424]{1,0:T(8,128)(2,1)S(1)}, bf16[16,7424]{1,0:T(8,128)(2,1)S(1)}, u32[]{:S(2)}, u32[]{:S(2)}) collective-permute-start(bf16[16,7424]{1,0:T(8,128)(2,1)S(1)} %get-tuple-element.33), channel_id=1, source_target_pairs={{0,2},{2,0},{4,6},{6,4},{8,10},{10,8},{12,14},{14,12},{1,3},{3,1},... | collective-permute-start | bytes 712712 | tf_op jit(solution)/shard_map/mate_rows/ppermute | solution.py:317
  6.2 8.6 %collective-permute-start = (bf16[16,7424]{1,0:T(8,128)(2,1)S(1)}, bf16[16,7424]{1,0:T(8,128)(2,1)S(1)}, u32[]{:S(2)}, u32[]{:S(2)}) collective-permute-start(bf16[16,7424]{1,0:T(8,128)(2,1)S(1)} %get-tuple-element.29.refs_0_), channel_id=1, source_target_pairs={{0,4},{2,6},{4,8},{6,10},{8,12},{10,14},{12,13},{14,15},{13,9},{15... | collective-permute-start | bytes 712712 | tf_op jit(solution)/shard_map/rows_ahead/ppermute | solution.py:300
  6.3 11.6 %collective-permute-start.3 = (bf16[16,7424]{1,0:T(8,128)(2,1)S(1)}, bf16[16,7424]{1,0:T(8,128)(2,1)S(1)}, u32[]{:S(2)}, u32[]{:S(2)}) collective-permute-start(bf16[16,7424]{1,0:T(8,128)(2,1)S(1)} %get-tuple-element.29.refs_0_), channel_id=1, source_target_pairs={{0,1},{2,3},{4,0},{6,2},{8,4},{10,6},{12,8},{14,10},{13,12},{15,14... | collective-permute-start | bytes 712712 | tf_op jit(solution)/shard_map/rows_behind/ppermute | solution.py:300
  8.2 11.0 %collective-permute-start.4 = (bf16[16,7424]{1,0:T(8,128)(2,1)S(1)}, bf16[16,7424]{1,0:T(8,128)(2,1)S(1)}, u32[]{:S(2)}, u32[]{:S(2)}) collective-permute-start(bf16[16,7424]{1,0:T(8,128)(2,1)S(1)} %get-tuple-element.33), channel_id=1, source_target_pairs={{0,6},{2,4},{4,10},{6,8},{8,14},{10,12},{12,15},{14,13},{13,11},{1... | collective-permute-start | bytes 712712 | tf_op jit(solution)/shard_map/rows_ahead/ppermute | solution.py:300
  11.7 8.2 %collective-permute-start.6 = (bf16[128,7296]{1,0:T(8,128)(2,1)S(1)}, bf16[128,7296]{1,0:T(8,128)(2,1)S(1)}, u32[]{:S(2)}, u32[]{:S(2)}) collective-permute-start(bf16[128,7296]{1,0:T(8,128)(2,1)S(1)} %get-tuple-element.34), channel_id=1, source_target_pairs={{0,2},{2,0},{4,6},{6,4},{8,10},{10,8},{12,14},{14,12},{1,3},{3,1},... | collective-permute-start | bytes 5603336 | tf_op jit(solution)/shard_map/mate_panel/ppermute | solution.py:330
  12.9 4.0 %copy-start = (f32[7296]{0:T(1024)S(1)}, f32[7296]{0:T(1024)}, u32[]{:S(2)}) copy-start(f32[7296]{0:T(1024)} %param.8) | copy-start | bytes 87556
  14.8 9.3 %collective-permute-start.9 = (bf16[16,7424]{1,0:T(8,128)(2,1)S(1)}, bf16[16,7424]{1,0:T(8,128)(2,1)S(1)}, u32[]{:S(2)}, u32[]{:S(2)}) collective-permute-start(bf16[16,7424]{1,0:T(8,128)(2,1)S(1)} %collective-permute-done.5.refs_5_), channel_id=1, source_target_pairs={{0,1},{2,3},{4,0},{6,2},{8,4},{10,6},{12,8},{14,10},{13,12},{15,14... | collective-permute-start | bytes 712712 | tf_op jit(solution)/shard_map/rows_behind/ppermute | solution.py:300
  16.4 9.2 %collective-permute-start.1 = (bf16[16,7424]{1,0:T(8,128)(2,1)S(1)}, bf16[16,7424]{1,0:T(8,128)(2,1)S(1)}, u32[]{:S(2)}, u32[]{:S(2)}) collective-permute-start(bf16[16,7424]{1,0:T(8,128)(2,1)S(1)} %collective-permute-done.refs_2_), channel_id=1, source_target_pairs={{0,4},{2,6},{4,8},{6,10},{8,12},{10,14},{12,13},{14,15},{13,9},{15... | collective-permute-start | bytes 712712 | tf_op jit(solution)/shard_map/rows_ahead/ppermute | solution.py:300
  17.9 9.8 %collective-permute-start.12 = (bf16[16,7424]{1,0:T(8,128)(2,1)S(1)}, bf16[16,7424]{1,0:T(8,128)(2,1)S(1)}, u32[]{:S(2)}, u32[]{:S(2)}) collective-permute-start(bf16[16,7424]{1,0:T(8,128)(2,1)S(1)} %collective-permute-done.3.refs_3_), channel_id=1, source_target_pairs={{0,1},{2,3},{4,0},{6,2},{8,4},{10,6},{12,8},{14,10},{13,12},{15,14... | collective-permute-start | bytes 712712 | tf_op jit(solution)/shard_map/rows_behind/ppermute | solution.py:300
  19.3 10.9 %collective-permute-start.13 = (bf16[16,7424]{1,0:T(8,128)(2,1)S(1)}, bf16[16,7424]{1,0:T(8,128)(2,1)S(1)}, u32[]{:S(2)}, u32[]{:S(2)}) collective-permute-start(bf16[16,7424]{1,0:T(8,128)(2,1)S(1)} %collective-permute-done.4.refs_4_), channel_id=1, source_target_pairs={{0,4},{2,6},{4,8},{6,10},{8,12},{10,14},{12,13},{14,15},{13,9},{15... | collective-permute-start | bytes 712712 | tf_op jit(solution)/shard_map/rows_ahead/ppermute | solution.py:300
  24.1 8.7 %collective-permute-start.10 = (bf16[16,7424]{1,0:T(8,128)(2,1)S(1)}, bf16[16,7424]{1,0:T(8,128)(2,1)S(1)}, u32[]{:S(2)}, u32[]{:S(2)}) collective-permute-start(bf16[16,7424]{1,0:T(8,128)(2,1)S(1)} %collective-permute-done.9.refs_3_), channel_id=1, source_target_pairs={{0,1},{2,3},{4,0},{6,2},{8,4},{10,6},{12,8},{14,10},{13,12},{15,14... | collective-permute-start | bytes 712712 | tf_op jit(solution)/shard_map/rows_behind/ppermute | solution.py:300
  25.6 9.6 %collective-permute-start.7 = (bf16[16,7424]{1,0:T(8,128)(2,1)S(1)}, bf16[16,7424]{1,0:T(8,128)(2,1)S(1)}, u32[]{:S(2)}, u32[]{:S(2)}) collective-permute-start(bf16[16,7424]{1,0:T(8,128)(2,1)S(1)} %collective-permute-done.1.refs_0_), channel_id=1, source_target_pairs={{0,4},{2,6},{4,8},{6,10},{8,12},{10,14},{12,13},{14,15},{13,9},{15... | collective-permute-start | bytes 712712 | tf_op jit(solution)/shard_map/rows_ahead/ppermute | solution.py:300
  27.6 10.2 %collective-permute-start.14 = (bf16[16,7424]{1,0:T(8,128)(2,1)S(1)}, bf16[16,7424]{1,0:T(8,128)(2,1)S(1)}, u32[]{:S(2)}, u32[]{:S(2)}) collective-permute-start(bf16[16,7424]{1,0:T(8,128)(2,1)S(1)} %collective-permute-done.12.refs_1_), channel_id=1, source_target_pairs={{0,1},{2,3},{4,0},{6,2},{8,4},{10,6},{12,8},{14,10},{13,12},{15,14... | collective-permute-start | bytes 712712 | tf_op jit(solution)/shard_map/rows_behind/ppermute | solution.py:300
  30.1 9.9 %collective-permute-start.15 = (bf16[16,7424]{1,0:T(8,128)(2,1)S(1)}, bf16[16,7424]{1,0:T(8,128)(2,1)S(1)}, u32[]{:S(2)}, u32[]{:S(2)}) collective-permute-start(bf16[16,7424]{1,0:T(8,128)(2,1)S(1)} %collective-permute-done.13.refs_2_), channel_id=1, source_target_pairs={{0,4},{2,6},{4,8},{6,10},{8,12},{10,14},{12,13},{14,15},{13,9},{15... | collective-permute-start | bytes 712712 | tf_op jit(solution)/shard_map/rows_ahead/ppermute | solution.py:300
  32.8 11.9 %collective-permute-start.11 = (bf16[16,7424]{1,0:T(8,128)(2,1)S(1)}, bf16[16,7424]{1,0:T(8,128)(2,1)S(1)}, u32[]{:S(2)}, u32[]{:S(2)}) collective-permute-start(bf16[16,7424]{1,0:T(8,128)(2,1)S(1)} %collective-permute-done.10.refs_7_), channel_id=1, source_target_pairs={{0,1},{2,3},{4,0},{6,2},{8,4},{10,6},{12,8},{14,10},{13,12},{15,14... | collective-permute-start | bytes 712712 | tf_op jit(solution)/shard_map/rows_behind/ppermute | solution.py:300
  35.2 9.5 %collective-permute-start.8 = (bf16[16,7424]{1,0:T(8,128)(2,1)S(1)}, bf16[16,7424]{1,0:T(8,128)(2,1)S(1)}, u32[]{:S(2)}, u32[]{:S(2)}) collective-permute-start(bf16[16,7424]{1,0:T(8,128)(2,1)S(1)} %collective-permute-done.7.refs_4_), channel_id=1, source_target_pairs={{0,4},{2,6},{4,8},{6,10},{8,12},{10,14},{12,13},{14,15},{13,9},{15... | collective-permute-start | bytes 712712 | tf_op jit(solution)/shard_map/rows_ahead/ppermute | solution.py:300
  48.1 1.6 %collective-permute-start.16 = (f32[2,256,128]{2,1,0:T(8,128)S(1)}, f32[2,256,128]{2,1,0:T(8,128)S(1)}, u32[]{:S(2)}, u32[]{:S(2)}) collective-permute-start(f32[2,256,128]{2,1,0:T(8,128)S(1)} %get-tuple-element.44.partial), channel_id=1, source_target_pairs={{0,2},{2,0},{4,6},{6,4},{8,10},{10,8},{12,14},{14,12},{1,3},{3,1},... | collective-permute-start | bytes 786440 | tf_op jit(solution)/shard_map/ppermute | solution.py:375
  50.6 3.6 %collective-permute-start.17 = (f32[8,128]{1,0:T(8,128)S(1)}, f32[8,128]{1,0:T(8,128)S(1)}, u32[]{:S(2)}, u32[]{:S(2)}) collective-permute-start(f32[8,128]{1,0:T(8,128)S(1)} %get-tuple-element.46), channel_id=1, source_target_pairs={{0,1},{1,0},{2,3},{3,2},{4,5},{5,4},{6,7},{7,6},{8,9},{9,8},{10,11... | collective-permute-start | bytes 12296 | tf_op jit(solution)/shard_map/ppermute | solution.py:388
  52.2 5.7 %collective-permute-start.21 = (f32[128,128]{1,0:T(8,128)S(1)}, f32[128,128]{1,0:T(8,128)S(1)}, u32[]{:S(2)}, u32[]{:S(2)}) collective-permute-start(f32[128,128]{1,0:T(8,128)S(1)} %get-tuple-element.49), channel_id=1, source_target_pairs={{0,1},{1,0},{2,3},{3,2},{4,5},{5,4},{6,7},{7,6},{8,9},{9,8},{10,11... | collective-permute-start | bytes 196616 | tf_op jit(solution)/shard_map/ppermute | solution.py:390
  54.3 3.7 %collective-permute-start.18 = (f32[8,128]{1,0:T(8,128)S(1)}, f32[8,128]{1,0:T(8,128)S(1)}, u32[]{:S(2)}, u32[]{:S(2)}) collective-permute-start(f32[8,128]{1,0:T(8,128)S(1)} %select_maximum_fusion.refs_0_), channel_id=1, source_target_pairs={{0,4},{2,10},{4,0},{6,14},{8,12},{10,2},{12,8},{14,6},{1,5},{3,11}... | collective-permute-start | bytes 12296 | tf_op jit(solution)/shard_map/ppermute | solution.py:395
  55.5 5.4 %collective-permute-start.20 = (f32[8,128]{1,0:T(8,128)S(1)}, f32[8,128]{1,0:T(8,128)S(1)}, u32[]{:S(2)}, u32[]{:S(2)}) collective-permute-start(f32[8,128]{1,0:T(8,128)S(1)} %select_maximum_fusion.refs_0_), channel_id=1, source_target_pairs={{0,12},{2,14},{4,8},{6,10},{8,4},{10,6},{12,0},{14,2},{1,13},{3,15... | collective-permute-start | bytes 12296 | tf_op jit(solution)/shard_map/ppermute | solution.py:396
  58.0 2.9 %collective-permute-start.19 = (f32[8,128]{1,0:T(8,128)S(1)}, f32[8,128]{1,0:T(8,128)S(1)}, u32[]{:S(2)}, u32[]{:S(2)}) collective-permute-start(f32[8,128]{1,0:T(8,128)S(1)} %collective-permute-done.18.refs_1_), channel_id=1, source_target_pairs={{0,2},{2,0},{4,6},{6,4},{8,10},{10,8},{12,14},{14,12},{1,3},{3,1},... | collective-permute-start | bytes 12296 | tf_op jit(solution)/shard_map/ppermute | solution.py:397

commit v13 on v12

--- a/solution.py
+++ b/solution.py
@@ -47,16 +47,6 @@
 
 def square_kernel(own, squares):
     squares[...] = own[...] * own[...]
-
-
-def row_kernel(spot, planes, facts, kept, given, padded):
-    core = spot[2]
-    columns = planes.shape[2]
-    padded[...] = jnp.zeros_like(padded)
-    padded[: facts.shape[0], : facts.shape[1]] = facts[...]
-    for half, out in ((core, kept), (1 - core, given)):
-        out[:, :columns] = planes[half]
-        out[:, columns:] = padded[...].astype(out.dtype)
 
 
 def particle_facts(meta):
@@ -155,7 +145,7 @@
     each = chunks[0].shape[0]
     orientations, columns = own_panel.shape
     whole = columns // LANES
-    segments = next(s for s in (3, 2, 4, 5, 6, 7, 1) if whole % s == 0)
+    segments = 1
     n = len(chunks)
     count = each * n
     scratch = [pltpu.VMEM((count, LANES), jnp.float32)] * 2
@@ -284,7 +274,6 @@
     chip, core = place // 2, place % 2
     position = jnp.where(group == 0, chip, ring - 1 - chip)
     spot = jnp.stack([group, position, core, place]).astype(jnp.int32)
-    first = core == 0
 
     mate_pairs = [(d, d ^ 1) for d in range(devices)]
     x_pairs = [(0, 1), (1, 0)]
@@ -302,20 +291,12 @@
     vmem = pl.BlockSpec(memory_space=pltpu.VMEM)
     smem = pl.BlockSpec(memory_space=pltpu.SMEM)
     params = pltpu.CompilerParams(vmem_limit_bytes=VMEM_LIMIT)
+    first = core == 0
     planes = lax.optimization_barrier(jnp.transpose(images[0], (1, 0, 2)))
-    row_shape = jax.ShapeDtypeStruct((per_device, columns + LANES), jnp.bfloat16)
-    facts = jnp.concatenate([defocus, jnp.transpose(block_ids[0])], axis=0, dtype=jnp.float32)
-    kept, given = pl.pallas_call(
-        row_kernel,
-        in_specs=[smem, vmem, vmem],
-        out_specs=[vmem] * 2,
-        out_shape=[row_shape] * 2,
-        scratch_shapes=[pltpu.VMEM((per_device, LANES), jnp.float32)],
-        compiler_params=params,
-    )(spot, planes, facts)
-    with jax.named_scope("mate_rows"):
-        got = lax.ppermute(given, "orient", mate_pairs)
-
+    facts = jnp.concatenate([defocus, jnp.transpose(block_ids[0]).astype(jnp.bfloat16)], axis=0)
+    facts = jnp.pad(facts, ((0, per_device - facts.shape[0]), (0, LANES - per_device)))
+    kept = jnp.concatenate([jnp.where(first, planes[0], planes[1]), facts], axis=1)
+    given = jnp.concatenate([jnp.where(first, planes[1], planes[0]), facts], axis=1)
     _, panels = lax.optimization_barrier((kept, panels))
     sides = lax.optimization_barrier(jnp.transpose(panels[0, 0], (1, 0, 2)))
     panel_shape = jax.ShapeDtypeStruct(sides.shape[1:], sides.dtype)
@@ -330,7 +311,7 @@
         mate_panel = lax.ppermute(given_panel, "orient", mate_pairs)
 
     noise = noise_weight[None, :]
-    waiting = [((0, False), kept), ((0, True), got)]
+    waiting = []
     ahead = {False: kept, True: given}
     behind = {False: kept, True: given}
     orders, earlier, late = [], [], []
@@ -364,6 +345,11 @@
                 with jax.named_scope("rows_behind"):
                     behind[crossed] = forward(behind[crossed], -1, int(crossed and step == 1))
                 late.append(((step, crossed), behind[crossed]))
+        if step == 1:
+            late_given, _ = lax.optimization_barrier((given, kept))
+            with jax.named_scope("mate_rows"):
+                got = lax.ppermute(late_given, "orient", mate_pairs)
+            late = [((0, False), kept), ((0, True), got)] + late
     orders.append([key for key, _ in waiting])
     earlier.append(score([c for _, c in waiting]))
     waiting = late

time: 61.9 us -> 63.9 us (1.032)
  local copies, waits for them, and re-layouts: 3.52 us -> 7.39 us
  Pallas kernels: 16.5 us -> 14.8 us
    ppermute x1, waiting for transfers between devices: 0.01 us -> 2.12 us  [chip_shards(): got = lax.ppermute(late_given, 'orient', mate_pairs)]
    unnamed x3 -> x7, local copies, waits for them, and re-layouts: 1.07 us -> 3.15 us
    optimization_barrier x1, local copies, waits for them, and re-layouts: 2.42 us -> 4.22 us  [chip_shards(): _, panels = lax.optimization_barrier((kept, panels))]
    ppermute x14, waiting for transfers between devices: 11.1 us -> 9.63 us  [forward(): return lax.ppermute(values, ('orient', 'cls'), pairs)]
    pallas_call x3, Pallas kernels: 12.3 us -> 11.1 us  [score_call(): pl.pallas_call(kernel, in_specs=[pl.BlockSpec(memory_space=pltpu.SMEM)] +...]
    convert_element_type x2 -> x1, other arithmetic: 1.34 us -> 0.69 us  [chip_shards(): jnp.transpose(block_ids[0]).astype(jnp.bfloat16)]
  transfers between devices with their start and end apart: 22 -> 22, of which waited for: 10 -> 11; matrix products, arithmetic and copies ran while one was open for 4% -> 7% of each run, Pallas kernels for 18% -> 16%
where the time goes in v13:
time: 63.9 us; the launch traced here: 63.7 us
  starting transfers between devices  23.8 us (37%)
  waiting for transfers between devices  16.7 us (26%)
  Pallas kernels  14.8 us (23%)
  local copies, waits for them, and re-layouts  7.39 us (12%)
  other arithmetic  0.89 us (1%)
    ppermute x14, starting transfers between devices, forward(): return lax.ppermute(values, ('orient', 'cls'), pairs)  16.7 us
    pallas_call x3, Pallas kernels, score_call(): pl.pallas_call(kernel, in_specs=[pl.BlockSpec(memory_space=pltpu.SMEM)] +...  11.1 us
    ppermute x14, waiting for transfers between devices, forward(): return lax.ppermute(values, ('orient', 'cls'), pairs)  9.63 us
    optimization_barrier x1, local copies, waits for them, and re-layouts, chip_shards(): _, panels = lax.optimization_barrier((kept, panels))  4.22 us
    unnamed x7, local copies, waits for them, and re-layouts  3.15 us
    ppermute x1, starting transfers between devices, chip_shards(): far = lax.ppermute(pair, 'orient', [(d, d ^ 6) for d in range(devices)])  2.48 us
    ppermute x1, waiting for transfers between devices, chip_shards(): got = lax.ppermute(late_given, 'orient', mate_pairs)  2.12 us
    ppermute x1, waiting for transfers between devices, chip_shards(): far = lax.ppermute(pair, 'orient', [(d, d ^ 6) for d in range(devices)])  1.84 us
  transfers between devices with their start and end apart: 22, of which 11 were waited for; matrix products, arithmetic and copies ran while one was open for 7% of the time, Pallas kernels for 16%

profile of v13, /device:TPU:0, one launch (start us, length us, event | category | flops | bytes accessed | tf_op | source)
XLA Modules:
  0.0 63.7 jit_solution(2890812140040096279)
XLA Ops:
  0.0 1.1 %copy.11 = bf16[1,16,2,7296]{3,1,2,0:T(8,128)(2,1)S(1)} copy(bf16[1,16,2,7296]{3,2,1,0:T(2,128)(2,1)} %param.5) | data formatting | bytes 933888 | tf_op args[0]
  1.1 0.7 %convert_bitcast_fusion = bf16[4,16]{1,0:T(4,128)(2,1)S(1)} fusion(s32[1,16,4]{1,2,0:T(4,128)} %param.7), kind=kLoop, calls=%fused_computation.16 | loop fusion | flops 64 | bytes 384 | tf_op jit(solution)/shard_map/convert_element_type | solution.py:296
  1.9 2.4 %collective-permute-start.5 = (bf16[16,7424]{1,0:T(8,128)(2,1)S(1)}, bf16[16,7424]{1,0:T(8,128)(2,1)S(1)}, u32[]{:S(2)}, u32[]{:S(2)}) collective-permute-start(bf16[16,7424]{1,0:T(8,128)(2,1)S(1)} %get-tuple-element.55), channel_id=1, source_target_pairs={{0,3},{2,1},{4,2},{6,0},{8,6},{10,4},{12,10},{14,8},{13,14},{15,12... | collective-permute-start | bytes 712712 | tf_op jit(solution)/shard_map/rows_behind/ppermute | solution.py:289
  4.3 0.7 %collective-permute-start = (bf16[16,7424]{1,0:T(8,128)(2,1)S(1)}, bf16[16,7424]{1,0:T(8,128)(2,1)S(1)}, u32[]{:S(2)}, u32[]{:S(2)}) collective-permute-start(bf16[16,7424]{1,0:T(8,128)(2,1)S(1)} %get-tuple-element.56.refs_0_), channel_id=1, source_target_pairs={{0,4},{2,6},{4,8},{6,10},{8,12},{10,14},{12,13},{14,15},{13,9},{15... | collective-permute-start | bytes 712712 | tf_op jit(solution)/shard_map/rows_ahead/ppermute | solution.py:289
  5.0 1.3 %collective-permute-start.3 = (bf16[16,7424]{1,0:T(8,128)(2,1)S(1)}, bf16[16,7424]{1,0:T(8,128)(2,1)S(1)}, u32[]{:S(2)}, u32[]{:S(2)}) collective-permute-start(bf16[16,7424]{1,0:T(8,128)(2,1)S(1)} %get-tuple-element.56.refs_0_), channel_id=1, source_target_pairs={{0,1},{2,3},{4,0},{6,2},{8,4},{10,6},{12,8},{14,10},{13,12},{15,14... | collective-permute-start | bytes 712712 | tf_op jit(solution)/shard_map/rows_behind/ppermute | solution.py:289
  6.4 0.1 collective-permute-start.4
  6.4 4.2 %copy.10 = bf16[1,1,128,2,7296]{4,2,3,1,0:T(8,128)(2,1)} copy(bf16[1,1,128,2,7296]{4,3,2,1,0:T(2,128)(2,1)} %param.9) | data formatting | bytes 7471104 | tf_op jit(solution)/shard_map/optimization_barrier | solution.py:300
  10.7 0.1 pad_add_fusion.spot
  10.7 2.1 %copy-done = bf16[1,1,128,2,7296]{4,2,3,1,0:T(8,128)(2,1)S(1)} copy-done((bf16[1,1,128,2,7296]{4,2,3,1,0:T(8,128)(2,1)S(1)}, bf16[1,1,128,2,7296]{4,2,3,1,0:T(8,128)(2,1)}, u32[]{:S(2)}) %copy-start) | copy-done | bytes 3735576
  12.8 0.8 %shard_map.55 = (bf16[128,7296]{1,0:T(8,128)(2,1)S(1)}, bf16[128,7296]{1,0:T(8,128)(2,1)S(1)}) custom-call(s32[4]{0:T(128)S(1)} %pad_add_fusion.spot, bf16[2,128,7296]{2,1,0:T(8,128)(2,1)S(1)} %bitcast.23), custom_call_target="tpu_custom_call" | custom-call | tf_op jit(solution)/shard_map/pallas_call | solution.py:303
  13.6 0.8 %collective-permute-start.6 = (bf16[128,7296]{1,0:T(8,128)(2,1)S(1)}, bf16[128,7296]{1,0:T(8,128)(2,1)S(1)}, u32[]{:S(2)}, u32[]{:S(2)}) collective-permute-start(bf16[128,7296]{1,0:T(8,128)(2,1)S(1)} %get-tuple-element.32), channel_id=1, source_target_pairs={{0,2},{2,0},{4,6},{6,4},{8,10},{10,8},{12,14},{14,12},{1,3},{3,1},... | collective-permute-start | bytes 5603336 | tf_op jit(solution)/shard_map/mate_panel/ppermute | solution.py:311
  14.4 0.0 collective-permute-done.5.refs_5_
  14.4 0.1 collective-permute-start.2
  14.5 0.1 shard_map.56.refs_8_.refs_10_.refs_4_
  14.6 1.4 %collective-permute-start.9 = (bf16[16,7424]{1,0:T(8,128)(2,1)S(1)}, bf16[16,7424]{1,0:T(8,128)(2,1)S(1)}, u32[]{:S(2)}, u32[]{:S(2)}) collective-permute-start(bf16[16,7424]{1,0:T(8,128)(2,1)S(1)} %collective-permute-done.5.refs_5_), channel_id=1, source_target_pairs={{0,1},{2,3},{4,0},{6,2},{8,4},{10,6},{12,8},{14,10},{13,12},{15,14... | collective-permute-start | bytes 712712 | tf_op jit(solution)/shard_map/rows_behind/ppermute | solution.py:289
  16.1 2.1 %collective-permute-done.2.refs_1_ = bf16[16,7424]{1,0:T(8,128)(2,1)S(1)} collective-permute-done((bf16[16,7424]{1,0:T(8,128)(2,1)S(1)}, bf16[16,7424]{1,0:T(8,128)(2,1)S(1)}, u32[]{:S(2)}, u32[]{:S(2)}) %collective-permute-start.2) | collective-permute-done | bytes 237600 | tf_op jit(solution)/shard_map/mate_rows/ppermute | solution.py:351
  18.2 1.6 %collective-permute-start.1 = (bf16[16,7424]{1,0:T(8,128)(2,1)S(1)}, bf16[16,7424]{1,0:T(8,128)(2,1)S(1)}, u32[]{:S(2)}, u32[]{:S(2)}) collective-permute-start(bf16[16,7424]{1,0:T(8,128)(2,1)S(1)} %collective-permute-done.refs_2_), channel_id=1, source_target_pairs={{0,4},{2,6},{4,8},{6,10},{8,12},{10,14},{12,13},{14,15},{13,9},{15... | collective-permute-start | bytes 712712 | tf_op jit(solution)/shard_map/rows_ahead/ppermute | solution.py:289
  19.8 0.5 collective-permute-start.12
  20.3 1.6 %collective-permute-start.13 = (bf16[16,7424]{1,0:T(8,128)(2,1)S(1)}, bf16[16,7424]{1,0:T(8,128)(2,1)S(1)}, u32[]{:S(2)}, u32[]{:S(2)}) collective-permute-start(bf16[16,7424]{1,0:T(8,128)(2,1)S(1)} %collective-permute-done.4.refs_4_), channel_id=1, source_target_pairs={{0,4},{2,6},{4,8},{6,10},{8,12},{10,14},{12,13},{14,15},{13,9},{15... | collective-permute-start | bytes 712712 | tf_op jit(solution)/shard_map/rows_ahead/ppermute | solution.py:289
  21.9 0.0 collective-permute-done.6.refs_9_.refs_11_.refs_5_
  21.9 3.8 %shard_map.57 = (f32[96,128]{1,0:T(8,128)S(1)}, f32[96,128]{1,0:T(8,128)S(1)}, f32[96,128]{1,0:T(8,128)S(1)}) custom-call(s32[4]{0:T(128)S(1)} %pad_add_fusion.spot, bf16[16,7424]{1,0:T(8,128)(2,1)S(1)} %get-tuple-element.56.refs_0_, bf16[16,7424]{1,0:T(8,128)(2,1)S(1)} %collective-permute-done.2.refs_1_, bf16[16,7424]{1,0:T(8,128)(2,1)S(1)} %collective-permute-done.refs_2_, ...), custom_call_target="tpu_custom_call" | custom-call | flops 956301312 | bytes 5136384 | tf_op jit(solution)/shard_map/pallas_call | solution.py:167
  25.8 0.0 collective-permute-done.9.refs_3_
  25.8 0.5 collective-permute-start.10
  26.3 0.5 collective-permute-done.1.refs_0_
  26.8 1.6 %collective-permute-start.7 = (bf16[16,7424]{1,0:T(8,128)(2,1)S(1)}, bf16[16,7424]{1,0:T(8,128)(2,1)S(1)}, u32[]{:S(2)}, u32[]{:S(2)}) collective-permute-start(bf16[16,7424]{1,0:T(8,128)(2,1)S(1)} %collective-permute-done.1.refs_0_), channel_id=1, source_target_pairs={{0,4},{2,6},{4,8},{6,10},{8,12},{10,14},{12,13},{14,15},{13,9},{15... | collective-permute-start | bytes 712712 | tf_op jit(solution)/shard_map/rows_ahead/ppermute | solution.py:289
  28.4 1.4 %collective-permute-start.14 = (bf16[16,7424]{1,0:T(8,128)(2,1)S(1)}, bf16[16,7424]{1,0:T(8,128)(2,1)S(1)}, u32[]{:S(2)}, u32[]{:S(2)}) collective-permute-start(bf16[16,7424]{1,0:T(8,128)(2,1)S(1)} %collective-permute-done.12.refs_1_), channel_id=1, source_target_pairs={{0,1},{2,3},{4,0},{6,2},{8,4},{10,6},{12,8},{14,10},{13,12},{15,14... | collective-permute-start | bytes 712712 | tf_op jit(solution)/shard_map/rows_behind/ppermute | solution.py:289
  29.8 2.1 %collective-permute-done.13.refs_2_ = bf16[16,7424]{1,0:T(8,128)(2,1)S(1)} collective-permute-done((bf16[16,7424]{1,0:T(8,128)(2,1)S(1)}, bf16[16,7424]{1,0:T(8,128)(2,1)S(1)}, u32[]{:S(2)}, u32[]{:S(2)}) %collective-permute-start.13) | collective-permute-done | bytes 237600 | tf_op jit(solution)/shard_map/rows_ahead/ppermute | solution.py:289
  31.9 1.6 %collective-permute-start.15 = (bf16[16,7424]{1,0:T(8,128)(2,1)S(1)}, bf16[16,7424]{1,0:T(8,128)(2,1)S(1)}, u32[]{:S(2)}, u32[]{:S(2)}) collective-permute-start(bf16[16,7424]{1,0:T(8,128)(2,1)S(1)} %collective-permute-done.13.refs_2_), channel_id=1, source_target_pairs={{0,4},{2,6},{4,8},{6,10},{8,12},{10,14},{12,13},{14,15},{13,9},{15... | collective-permute-start | bytes 712712 | tf_op jit(solution)/shard_map/rows_ahead/ppermute | solution.py:289
  33.5 1.0 %collective-permute-done.10.refs_7_ = bf16[16,7424]{1,0:T(8,128)(2,1)S(1)} collective-permute-done((bf16[16,7424]{1,0:T(8,128)(2,1)S(1)}, bf16[16,7424]{1,0:T(8,128)(2,1)S(1)}, u32[]{:S(2)}, u32[]{:S(2)}) %collective-permute-start.10) | collective-permute-done | bytes 237600 | tf_op jit(solution)/shard_map/rows_behind/ppermute | solution.py:289
  34.5 0.5 collective-permute-start.11
  35.0 2.0 %collective-permute-done.7.refs_4_ = bf16[16,7424]{1,0:T(8,128)(2,1)S(1)} collective-permute-done((bf16[16,7424]{1,0:T(8,128)(2,1)S(1)}, bf16[16,7424]{1,0:T(8,128)(2,1)S(1)}, u32[]{:S(2)}, u32[]{:S(2)}) %collective-permute-start.7) | collective-permute-done | bytes 237600 | tf_op jit(solution)/shard_map/rows_ahead/ppermute | solution.py:289
  37.0 1.6 %collective-permute-start.8 = (bf16[16,7424]{1,0:T(8,128)(2,1)S(1)}, bf16[16,7424]{1,0:T(8,128)(2,1)S(1)}, u32[]{:S(2)}, u32[]{:S(2)}) collective-permute-start(bf16[16,7424]{1,0:T(8,128)(2,1)S(1)} %collective-permute-done.7.refs_4_), channel_id=1, source_target_pairs={{0,4},{2,6},{4,8},{6,10},{8,12},{10,14},{12,13},{14,15},{13,9},{15... | collective-permute-start | bytes 712712 | tf_op jit(solution)/shard_map/rows_ahead/ppermute | solution.py:289
  38.6 1.0 %collective-permute-done.14.refs_5_ = bf16[16,7424]{1,0:T(8,128)(2,1)S(1)} collective-permute-done((bf16[16,7424]{1,0:T(8,128)(2,1)S(1)}, bf16[16,7424]{1,0:T(8,128)(2,1)S(1)}, u32[]{:S(2)}, u32[]{:S(2)}) %collective-permute-start.14) | collective-permute-done | bytes 237600 | tf_op jit(solution)/shard_map/rows_behind/ppermute | solution.py:289
  39.6 2.5 %collective-permute-done.15.refs_6_ = bf16[16,7424]{1,0:T(8,128)(2,1)S(1)} collective-permute-done((bf16[16,7424]{1,0:T(8,128)(2,1)S(1)}, bf16[16,7424]{1,0:T(8,128)(2,1)S(1)}, u32[]{:S(2)}, u32[]{:S(2)}) %collective-permute-start.15) | collective-permute-done | bytes 237600 | tf_op jit(solution)/shard_map/rows_ahead/ppermute | solution.py:289
  42.1 4.2 %shard_map.58 = (f32[128,128]{1,0:T(8,128)S(1)}, f32[128,128]{1,0:T(8,128)S(1)}, f32[128,128]{1,0:T(8,128)S(1)}) custom-call(s32[4]{0:T(128)S(1)} %pad_add_fusion.spot, bf16[16,7424]{1,0:T(8,128)(2,1)S(1)} %collective-permute-done.1.refs_0_, bf16[16,7424]{1,0:T(8,128)(2,1)S(1)} %collective-permute-done.12.refs_1_, ...), custom_call_target="tpu_custom_call" | custom-call | flops 956301312 | bytes 5603328 | tf_op jit(solution)/shard_map/pallas_call | solution.py:167
  46.3 0.4 collective-permute-done.8.refs_0_
  46.6 3.1 %shard_map.59 = (f32[2,256,128]{2,1,0:T(8,128)S(1)}, f32[256,128]{1,0:T(8,128)S(1)}) custom-call(s32[4]{0:T(128)S(1)} %pad_add_fusion.spot, bf16[16,7424]{1,0:T(8,128)(2,1)S(1)} %collective-permute-done.8.refs_0_, bf16[16,7424]{1,0:T(8,128)(2,1)S(1)} %collective-permute-done.11.refs_1_, f32[1,7296]{1,0:T(1,128)S(1)} %broadcast_in_dim.3.refs_6_.refs_8_.refs_2_, ...), custom_call_target="tpu_custom_call" | custom-call | flops 956301312 | bytes 4202496 | tf_op jit(solution)/shard_map/pallas_call | solution.py:167
  49.7 0.0 collective-permute-start.16
  49.8 1.5 %collective-permute-done.16.mate = f32[2,256,128]{2,1,0:T(8,128)S(1)} collective-permute-done((f32[2,256,128]{2,1,0:T(8,128)S(1)}, f32[2,256,128]{2,1,0:T(8,128)S(1)}, u32[]{:S(2)}, u32[]{:S(2)}) %collective-permute-start.16) | collective-permute-done | bytes 262176 | tf_op jit(solution)/shard_map/ppermute | solution.py:361
  51.3 0.9 %shard_map.60 = (f32[128,128]{1,0:T(8,128)S(1)}, f32[128,128]{1,0:T(8,128)S(1)}, f32[8,128]{1,0:T(8,128)S(1)}) custom-call(s32[4]{0:T(128)S(1)} %pad_add_fusion.spot, f32[2,256,128]{2,1,0:T(8,128)S(1)} %get-tuple-element.42.partial, f32[2,256,128]{2,1,0:T(8,128)S(1)} %collective-permute-done.16.mate, f32[256,128]{1,0:T(8,128)S(1)} %get-tuple-element.43.facts), custom_call_target="tpu_custom_call" | custom-call | tf_op jit(solution)/shard_map/pallas_call | solution.py:362
  52.2 1.4 %collective-permute-start.17 = (f32[8,128]{1,0:T(8,128)S(1)}, f32[8,128]{1,0:T(8,128)S(1)}, u32[]{:S(2)}, u32[]{:S(2)}) collective-permute-start(f32[8,128]{1,0:T(8,128)S(1)} %get-tuple-element.44), channel_id=1, source_target_pairs={{0,1},{1,0},{2,3},{3,2},{4,5},{5,4},{6,7},{7,6},{8,9},{9,8},{10,11... | collective-permute-start | bytes 12296 | tf_op jit(solution)/shard_map/ppermute | solution.py:374
  53.5 0.7 %collective-permute-start.21 = (f32[128,128]{1,0:T(8,128)S(1)}, f32[128,128]{1,0:T(8,128)S(1)}, u32[]{:S(2)}, u32[]{:S(2)}) collective-permute-start(f32[128,128]{1,0:T(8,128)S(1)} %get-tuple-element.47), channel_id=1, source_target_pairs={{0,1},{1,0},{2,3},{3,2},{4,5},{5,4},{6,7},{7,6},{8,9},{9,8},{10,11... | collective-permute-start | bytes 196616 | tf_op jit(solution)/shard_map/ppermute | solution.py:376
  54.3 1.6 %collective-permute-done.17 = f32[8,128]{1,0:T(8,128)S(1)} collective-permute-done((f32[8,128]{1,0:T(8,128)S(1)}, f32[8,128]{1,0:T(8,128)S(1)}, u32[]{:S(2)}, u32[]{:S(2)}) %collective-permute-start.17) | collective-permute-done | bytes 4128 | tf_op jit(solution)/shard_map/ppermute | solution.py:374
  55.9 1.6 %collective-permute-start.18 = (f32[8,128]{1,0:T(8,128)S(1)}, f32[8,128]{1,0:T(8,128)S(1)}, u32[]{:S(2)}, u32[]{:S(2)}) collective-permute-start(f32[8,128]{1,0:T(8,128)S(1)} %select_maximum_fusion.refs_0_), channel_id=1, source_target_pairs={{0,4},{2,10},{4,0},{6,14},{8,12},{10,2},{12,8},{14,6},{1,5},{3,11}... | collective-permute-start | bytes 12296 | tf_op jit(solution)/shard_map/ppermute | solution.py:381
  57.5 2.5 %collective-permute-start.20 = (f32[8,128]{1,0:T(8,128)S(1)}, f32[8,128]{1,0:T(8,128)S(1)}, u32[]{:S(2)}, u32[]{:S(2)}) collective-permute-start(f32[8,128]{1,0:T(8,128)S(1)} %select_maximum_fusion.refs_0_), channel_id=1, source_target_pairs={{0,12},{2,14},{4,8},{6,10},{8,4},{10,6},{12,0},{14,2},{1,13},{3,15... | collective-permute-start | bytes 12296 | tf_op jit(solution)/shard_map/ppermute | solution.py:382
  60.0 1.1 %shard_map.61 = (f32[128,256]{1,0:T(8,128)S(1)}, f32[128,128]{1,0:T(8,128)S(1)}, f32[8,128]{1,0:T(8,128)S(1)}) custom-call(s32[4]{0:T(128)S(1)} %pad_add_fusion.spot, f32[128,128]{1,0:T(8,128)S(1)} %get-tuple-element.45.mine, f32[128,128]{1,0:T(8,128)S(1)} %collective-permute-done.21.across, f32[256,128]{1,0:T(8,128)S(1)} %get-tuple-element.43.facts), custom_call_target="tpu_custom_call" | custom-call | tf_op jit(solution)/shard_map/pallas_call | solution.py:389
  61.1 1.8 %collective-permute-done.20.refs_3_ = f32[8,128]{1,0:T(8,128)S(1)} collective-permute-done((f32[8,128]{1,0:T(8,128)S(1)}, f32[8,128]{1,0:T(8,128)S(1)}, u32[]{:S(2)}, u32[]{:S(2)}) %collective-permute-start.20) | collective-permute-done | bytes 4128 | tf_op jit(solution)/shard_map/ppermute | solution.py:382
  62.9 0.8 %shard_map.62 = f32[128,256]{1,0:T(8,128)} custom-call(f32[8,128]{1,0:T(8,128)S(1)} %select_maximum_fusion.refs_0_, f32[8,128]{1,0:T(8,128)S(1)} %collective-permute-done.18.refs_1_, f32[8,128]{1,0:T(8,128)S(1)} %collective-permute-done.19.refs_2_, f32[8,128]{1,0:T(8,128)S(1)} %collective-permute-done.20.refs_3_, f32[8,128]{1,0:T(8,128)S(1)} %get-tuple-element.48.refs_4_, ...), custom_call_target="tpu_custom_call" | custom-call | tf_op jit(solution)/shard_map/pallas_call | solution.py:400
  (20 shorter events, 0.2 us)
Async XLA Ops:
  0.0 1.8 %copy-start.2 = (bf16[1,16]{1,0:T(2,128)(2,1)S(1)}, bf16[1,16]{1,0:T(2,128)(2,1)}, u32[]{:S(2)}) copy-start(bf16[1,16]{1,0:T(2,128)(2,1)} %param.6) | copy-start | bytes 100
  1.9 12.5 %collective-permute-start.5 = (bf16[16,7424]{1,0:T(8,128)(2,1)S(1)}, bf16[16,7424]{1,0:T(8,128)(2,1)S(1)}, u32[]{:S(2)}, u32[]{:S(2)}) collective-permute-start(bf16[16,7424]{1,0:T(8,128)(2,1)S(1)} %get-tuple-element.55), channel_id=1, source_target_pairs={{0,3},{2,1},{4,2},{6,0},{8,6},{10,4},{12,10},{14,8},{13,14},{15,12... | collective-permute-start | bytes 712712 | tf_op jit(solution)/shard_map/rows_behind/ppermute | solution.py:289
  4.3 10.3 %collective-permute-start = (bf16[16,7424]{1,0:T(8,128)(2,1)S(1)}, bf16[16,7424]{1,0:T(8,128)(2,1)S(1)}, u32[]{:S(2)}, u32[]{:S(2)}) collective-permute-start(bf16[16,7424]{1,0:T(8,128)(2,1)S(1)} %get-tuple-element.56.refs_0_), channel_id=1, source_target_pairs={{0,4},{2,6},{4,8},{6,10},{8,12},{10,14},{12,13},{14,15},{13,9},{15... | collective-permute-start | bytes 712712 | tf_op jit(solution)/shard_map/rows_ahead/ppermute | solution.py:289
  5.0 14.8 %collective-permute-start.3 = (bf16[16,7424]{1,0:T(8,128)(2,1)S(1)}, bf16[16,7424]{1,0:T(8,128)(2,1)S(1)}, u32[]{:S(2)}, u32[]{:S(2)}) collective-permute-start(bf16[16,7424]{1,0:T(8,128)(2,1)S(1)} %get-tuple-element.56.refs_0_), channel_id=1, source_target_pairs={{0,1},{2,3},{4,0},{6,2},{8,4},{10,6},{12,8},{14,10},{13,12},{15,14... | collective-permute-start | bytes 712712 | tf_op jit(solution)/shard_map/rows_behind/ppermute | solution.py:289
  6.4 14.0 %collective-permute-start.4 = (bf16[16,7424]{1,0:T(8,128)(2,1)S(1)}, bf16[16,7424]{1,0:T(8,128)(2,1)S(1)}, u32[]{:S(2)}, u32[]{:S(2)}) collective-permute-start(bf16[16,7424]{1,0:T(8,128)(2,1)S(1)} %get-tuple-element.55), channel_id=1, source_target_pairs={{0,6},{2,4},{4,10},{6,8},{8,14},{10,12},{12,15},{14,13},{13,11},{1... | collective-permute-start | bytes 712712 | tf_op jit(solution)/shard_map/rows_ahead/ppermute | solution.py:289
  10.7 2.1 %copy-start = (bf16[1,1,128,2,7296]{4,2,3,1,0:T(8,128)(2,1)S(1)}, bf16[1,1,128,2,7296]{4,2,3,1,0:T(8,128)(2,1)}, u32[]{:S(2)}) copy-start(bf16[1,1,128,2,7296]{4,2,3,1,0:T(8,128)(2,1)} %copy.10) | copy-start | bytes 11206660
  13.6 8.3 %collective-permute-start.6 = (bf16[128,7296]{1,0:T(8,128)(2,1)S(1)}, bf16[128,7296]{1,0:T(8,128)(2,1)S(1)}, u32[]{:S(2)}, u32[]{:S(2)}) collective-permute-start(bf16[128,7296]{1,0:T(8,128)(2,1)S(1)} %get-tuple-element.32), channel_id=1, source_target_pairs={{0,2},{2,0},{4,6},{6,4},{8,10},{10,8},{12,14},{14,12},{1,3},{3,1},... | collective-permute-start | bytes 5603336 | tf_op jit(solution)/shard_map/mate_panel/ppermute | solution.py:311
  14.4 3.8 %collective-permute-start.2 = (bf16[16,7424]{1,0:T(8,128)(2,1)S(1)}, bf16[16,7424]{1,0:T(8,128)(2,1)S(1)}, u32[]{:S(2)}, u32[]{:S(2)}) collective-permute-start(bf16[16,7424]{1,0:T(8,128)(2,1)S(1)} %get-tuple-element.55), channel_id=1, source_target_pairs={{0,2},{2,0},{4,6},{6,4},{8,10},{10,8},{12,14},{14,12},{1,3},{3,1},... | collective-permute-start | bytes 712712 | tf_op jit(solution)/shard_map/mate_rows/ppermute | solution.py:351
  14.5 5.3 %copy-start.1 = (f32[7296]{0:T(1024)S(1)}, f32[7296]{0:T(1024)}, u32[]{:S(2)}) copy-start(f32[7296]{0:T(1024)} %param.8) | copy-start | bytes 87556
  14.6 11.1 %collective-permute-start.9 = (bf16[16,7424]{1,0:T(8,128)(2,1)S(1)}, bf16[16,7424]{1,0:T(8,128)(2,1)S(1)}, u32[]{:S(2)}, u32[]{:S(2)}) collective-permute-start(bf16[16,7424]{1,0:T(8,128)(2,1)S(1)} %collective-permute-done.5.refs_5_), channel_id=1, source_target_pairs={{0,1},{2,3},{4,0},{6,2},{8,4},{10,6},{12,8},{14,10},{13,12},{15,14... | collective-permute-start | bytes 712712 | tf_op jit(solution)/shard_map/rows_behind/ppermute | solution.py:289
  18.2 8.6 %collective-permute-start.1 = (bf16[16,7424]{1,0:T(8,128)(2,1)S(1)}, bf16[16,7424]{1,0:T(8,128)(2,1)S(1)}, u32[]{:S(2)}, u32[]{:S(2)}) collective-permute-start(bf16[16,7424]{1,0:T(8,128)(2,1)S(1)} %collective-permute-done.refs_2_), channel_id=1, source_target_pairs={{0,4},{2,6},{4,8},{6,10},{8,12},{10,14},{12,13},{14,15},{13,9},{15... | collective-permute-start | bytes 712712 | tf_op jit(solution)/shard_map/rows_ahead/ppermute | solution.py:289
  19.8 8.6 %collective-permute-start.12 = (bf16[16,7424]{1,0:T(8,128)(2,1)S(1)}, bf16[16,7424]{1,0:T(8,128)(2,1)S(1)}, u32[]{:S(2)}, u32[]{:S(2)}) collective-permute-start(bf16[16,7424]{1,0:T(8,128)(2,1)S(1)} %collective-permute-done.3.refs_3_), channel_id=1, source_target_pairs={{0,1},{2,3},{4,0},{6,2},{8,4},{10,6},{12,8},{14,10},{13,12},{15,14... | collective-permute-start | bytes 712712 | tf_op jit(solution)/shard_map/rows_behind/ppermute | solution.py:289
  20.3 11.6 %collective-permute-start.13 = (bf16[16,7424]{1,0:T(8,128)(2,1)S(1)}, bf16[16,7424]{1,0:T(8,128)(2,1)S(1)}, u32[]{:S(2)}, u32[]{:S(2)}) collective-permute-start(bf16[16,7424]{1,0:T(8,128)(2,1)S(1)} %collective-permute-done.4.refs_4_), channel_id=1, source_target_pairs={{0,4},{2,6},{4,8},{6,10},{8,12},{10,14},{12,13},{14,15},{13,9},{15... | collective-permute-start | bytes 712712 | tf_op jit(solution)/shard_map/rows_ahead/ppermute | solution.py:289
  25.8 8.8 %collective-permute-start.10 = (bf16[16,7424]{1,0:T(8,128)(2,1)S(1)}, bf16[16,7424]{1,0:T(8,128)(2,1)S(1)}, u32[]{:S(2)}, u32[]{:S(2)}) collective-permute-start(bf16[16,7424]{1,0:T(8,128)(2,1)S(1)} %collective-permute-done.9.refs_3_), channel_id=1, source_target_pairs={{0,1},{2,3},{4,0},{6,2},{8,4},{10,6},{12,8},{14,10},{13,12},{15,14... | collective-permute-start | bytes 712712 | tf_op jit(solution)/shard_map/rows_behind/ppermute | solution.py:289
  26.8 10.2 %collective-permute-start.7 = (bf16[16,7424]{1,0:T(8,128)(2,1)S(1)}, bf16[16,7424]{1,0:T(8,128)(2,1)S(1)}, u32[]{:S(2)}, u32[]{:S(2)}) collective-permute-start(bf16[16,7424]{1,0:T(8,128)(2,1)S(1)} %collective-permute-done.1.refs_0_), channel_id=1, source_target_pairs={{0,4},{2,6},{4,8},{6,10},{8,12},{10,14},{12,13},{14,15},{13,9},{15... | collective-permute-start | bytes 712712 | tf_op jit(solution)/shard_map/rows_ahead/ppermute | solution.py:289
  28.4 11.2 %collective-permute-start.14 = (bf16[16,7424]{1,0:T(8,128)(2,1)S(1)}, bf16[16,7424]{1,0:T(8,128)(2,1)S(1)}, u32[]{:S(2)}, u32[]{:S(2)}) collective-permute-start(bf16[16,7424]{1,0:T(8,128)(2,1)S(1)} %collective-permute-done.12.refs_1_), channel_id=1, source_target_pairs={{0,1},{2,3},{4,0},{6,2},{8,4},{10,6},{12,8},{14,10},{13,12},{15,14... | collective-permute-start | bytes 712712 | tf_op jit(solution)/shard_map/rows_behind/ppermute | solution.py:289
  31.9 10.2 %collective-permute-start.15 = (bf16[16,7424]{1,0:T(8,128)(2,1)S(1)}, bf16[16,7424]{1,0:T(8,128)(2,1)S(1)}, u32[]{:S(2)}, u32[]{:S(2)}) collective-permute-start(bf16[16,7424]{1,0:T(8,128)(2,1)S(1)} %collective-permute-done.13.refs_2_), channel_id=1, source_target_pairs={{0,4},{2,6},{4,8},{6,10},{8,12},{10,14},{12,13},{14,15},{13,9},{15... | collective-permute-start | bytes 712712 | tf_op jit(solution)/shard_map/rows_ahead/ppermute | solution.py:289
  34.5 11.7 %collective-permute-start.11 = (bf16[16,7424]{1,0:T(8,128)(2,1)S(1)}, bf16[16,7424]{1,0:T(8,128)(2,1)S(1)}, u32[]{:S(2)}, u32[]{:S(2)}) collective-permute-start(bf16[16,7424]{1,0:T(8,128)(2,1)S(1)} %collective-permute-done.10.refs_7_), channel_id=1, source_target_pairs={{0,1},{2,3},{4,0},{6,2},{8,4},{10,6},{12,8},{14,10},{13,12},{15,14... | collective-permute-start | bytes 712712 | tf_op jit(solution)/shard_map/rows_behind/ppermute | solution.py:289
  37.0 9.6 %collective-permute-start.8 = (bf16[16,7424]{1,0:T(8,128)(2,1)S(1)}, bf16[16,7424]{1,0:T(8,128)(2,1)S(1)}, u32[]{:S(2)}, u32[]{:S(2)}) collective-permute-start(bf16[16,7424]{1,0:T(8,128)(2,1)S(1)} %collective-permute-done.7.refs_4_), channel_id=1, source_target_pairs={{0,4},{2,6},{4,8},{6,10},{8,12},{10,14},{12,13},{14,15},{13,9},{15... | collective-permute-start | bytes 712712 | tf_op jit(solution)/shard_map/rows_ahead/ppermute | solution.py:289
  49.7 1.6 %collective-permute-start.16 = (f32[2,256,128]{2,1,0:T(8,128)S(1)}, f32[2,256,128]{2,1,0:T(8,128)S(1)}, u32[]{:S(2)}, u32[]{:S(2)}) collective-permute-start(f32[2,256,128]{2,1,0:T(8,128)S(1)} %get-tuple-element.42.partial), channel_id=1, source_target_pairs={{0,2},{2,0},{4,6},{6,4},{8,10},{10,8},{12,14},{14,12},{1,3},{3,1},... | collective-permute-start | bytes 786440 | tf_op jit(solution)/shard_map/ppermute | solution.py:361
  52.2 3.6 %collective-permute-start.17 = (f32[8,128]{1,0:T(8,128)S(1)}, f32[8,128]{1,0:T(8,128)S(1)}, u32[]{:S(2)}, u32[]{:S(2)}) collective-permute-start(f32[8,128]{1,0:T(8,128)S(1)} %get-tuple-element.44), channel_id=1, source_target_pairs={{0,1},{1,0},{2,3},{3,2},{4,5},{5,4},{6,7},{7,6},{8,9},{9,8},{10,11... | collective-permute-start | bytes 12296 | tf_op jit(solution)/shard_map/ppermute | solution.py:374
  53.5 6.4 %collective-permute-start.21 = (f32[128,128]{1,0:T(8,128)S(1)}, f32[128,128]{1,0:T(8,128)S(1)}, u32[]{:S(2)}, u32[]{:S(2)}) collective-permute-start(f32[128,128]{1,0:T(8,128)S(1)} %get-tuple-element.47), channel_id=1, source_target_pairs={{0,1},{1,0},{2,3},{3,2},{4,5},{5,4},{6,7},{7,6},{8,9},{9,8},{10,11... | collective-permute-start | bytes 196616 | tf_op jit(solution)/shard_map/ppermute | solution.py:376
  55.9 4.1 %collective-permute-start.18 = (f32[8,128]{1,0:T(8,128)S(1)}, f32[8,128]{1,0:T(8,128)S(1)}, u32[]{:S(2)}, u32[]{:S(2)}) collective-permute-start(f32[8,128]{1,0:T(8,128)S(1)} %select_maximum_fusion.refs_0_), channel_id=1, source_target_pairs={{0,4},{2,10},{4,0},{6,14},{8,12},{10,2},{12,8},{14,6},{1,5},{3,11}... | collective-permute-start | bytes 12296 | tf_op jit(solution)/shard_map/ppermute | solution.py:381
  57.5 5.4 %collective-permute-start.20 = (f32[8,128]{1,0:T(8,128)S(1)}, f32[8,128]{1,0:T(8,128)S(1)}, u32[]{:S(2)}, u32[]{:S(2)}) collective-permute-start(f32[8,128]{1,0:T(8,128)S(1)} %select_maximum_fusion.refs_0_), channel_id=1, source_target_pairs={{0,12},{2,14},{4,8},{6,10},{8,4},{10,6},{12,0},{14,2},{1,13},{3,15... | collective-permute-start | bytes 12296 | tf_op jit(solution)/shard_map/ppermute | solution.py:382
  60.0 2.9 %collective-permute-start.19 = (f32[8,128]{1,0:T(8,128)S(1)}, f32[8,128]{1,0:T(8,128)S(1)}, u32[]{:S(2)}, u32[]{:S(2)}) collective-permute-start(f32[8,128]{1,0:T(8,128)S(1)} %collective-permute-done.18.refs_1_), channel_id=1, source_target_pairs={{0,2},{2,0},{4,6},{6,4},{8,10},{10,8},{12,14},{14,12},{1,3},{3,1},... | collective-permute-start | bytes 12296 | tf_op jit(solution)/shard_map/ppermute | solution.py:383

commit v14 on v13

--- a/solution.py
+++ b/solution.py
@@ -47,6 +47,14 @@
 
 def square_kernel(own, squares):
     squares[...] = own[...] * own[...]
+
+
+def row_kernel(spot, planes, facts, kept, given):
+    core = spot[2]
+    columns = planes.shape[2]
+    for half, out in ((core, kept), (1 - core, given)):
+        out[:, :columns] = planes[half]
+        out[:, columns:] = facts[...]
 
 
 def particle_facts(meta):
@@ -291,12 +299,18 @@
     vmem = pl.BlockSpec(memory_space=pltpu.VMEM)
     smem = pl.BlockSpec(memory_space=pltpu.SMEM)
     params = pltpu.CompilerParams(vmem_limit_bytes=VMEM_LIMIT)
-    first = core == 0
     planes = lax.optimization_barrier(jnp.transpose(images[0], (1, 0, 2)))
     facts = jnp.concatenate([defocus, jnp.transpose(block_ids[0]).astype(jnp.bfloat16)], axis=0)
     facts = jnp.pad(facts, ((0, per_device - facts.shape[0]), (0, LANES - per_device)))
-    kept = jnp.concatenate([jnp.where(first, planes[0], planes[1]), facts], axis=1)
-    given = jnp.concatenate([jnp.where(first, planes[1], planes[0]), facts], axis=1)
+    row_shape = jax.ShapeDtypeStruct((per_device, columns + LANES), jnp.bfloat16)
+    kept, given = pl.pallas_call(
+        row_kernel,
+        in_specs=[smem, vmem, vmem],
+        out_specs=[vmem] * 2,
+        out_shape=[row_shape] * 2,
+        compiler_params=params,
+    )(spot, planes, facts)
+
     _, panels = lax.optimization_barrier((kept, panels))
     sides = lax.optimization_barrier(jnp.transpose(panels[0, 0], (1, 0, 2)))
     panel_shape = jax.ShapeDtypeStruct(sides.shape[1:], sides.dtype)

time: 63.9 us -> 61.3 us (0.959)
  local copies, waits for them, and re-layouts: 7.39 us -> 3.52 us
  starting transfers between devices: 23.8 us -> 24.8 us
  waiting for transfers between devices: 16.7 us -> 15.9 us
    ppermute x1, waiting for transfers between devices: 2.12 us -> 0.01 us  [chip_shards(): got = lax.ppermute(late_given, 'orient', mate_pairs)]
    unnamed x7 -> x3, local copies, waits for them, and re-layouts: 3.15 us -> 1.07 us
    optimization_barrier x1, local copies, waits for them, and re-layouts: 4.22 us -> 2.42 us  [chip_shards(): _, panels = lax.optimization_barrier((kept, panels))]
    ppermute x14, waiting for transfers between devices: 9.63 us -> 10.9 us  [forward(): return lax.ppermute(values, ('orient', 'cls'), pairs)]
    ppermute x1, starting transfers between devices: 0.09 us -> 1.2 us  [chip_shards(): got = lax.ppermute(late_given, 'orient', mate_pairs)]
    concatenate x1, other arithmetic: 0.01 us -> 0.66 us  [chip_shards(): jnp.concatenate([defocus, jnp.transpose(block_ids[0]).astype(jnp.bfloat16...]
  transfers between devices with their start and end apart: 22 -> 22, of which waited for: 11 -> 10; matrix products, arithmetic and copies ran while one was open for 7% -> 4% of each run, Pallas kernels for 16% -> 16%
where the time goes in v14:
time: 61.3 us; the launch traced here: 61 us
  starting transfers between devices  24.8 us (40%)
  waiting for transfers between devices  15.9 us (26%)
  Pallas kernels  15.3 us (25%)
  local copies, waits for them, and re-layouts  3.52 us (6%)
  other arithmetic  1.45 us (2%)
    ppermute x14, starting transfers between devices, forward(): return lax.ppermute(values, ('orient', 'cls'), pairs)  17.1 us
    pallas_call x3, Pallas kernels, score_call(): pl.pallas_call(kernel, in_specs=[pl.BlockSpec(memory_space=pltpu.SMEM)] +...  11 us
    ppermute x14, waiting for transfers between devices, forward(): return lax.ppermute(values, ('orient', 'cls'), pairs)  10.9 us
    ppermute x1, starting transfers between devices, chip_shards(): far = lax.ppermute(pair, 'orient', [(d, d ^ 6) for d in range(devices)])  2.47 us
    optimization_barrier x1, local copies, waits for them, and re-layouts, chip_shards(): _, panels = lax.optimization_barrier((kept, panels))  2.42 us
    ppermute x1, waiting for transfers between devices, chip_shards(): far = lax.ppermute(pair, 'orient', [(d, d ^ 6) for d in range(devices)])  1.85 us
    ppermute x1, starting transfers between devices, chip_shards(): x_stats = lax.ppermute(stats, 'cls', x_pairs)  1.62 us
    ppermute x1, waiting for transfers between devices, chip_shards(): x_stats = lax.ppermute(stats, 'cls', x_pairs)  1.58 us
  transfers between devices with their start and end apart: 22, of which 10 were waited for; matrix products, arithmetic and copies ran while one was open for 4% of the time, Pallas kernels for 16%

profile of v14, /device:TPU:0, one launch (start us, length us, event | category | flops | bytes accessed | tf_op | source)
XLA Modules:
  0.0 61.0 jit_solution(6694892869460577513)
XLA Ops:
  0.0 1.1 %copy.11 = bf16[1,16,2,7296]{3,1,2,0:T(8,128)(2,1)S(1)} copy(bf16[1,16,2,7296]{3,2,1,0:T(2,128)(2,1)} %param.5) | data formatting | bytes 933888 | tf_op args[0]
  1.1 0.7 %convert_bitcast_fusion = bf16[4,16]{1,0:T(4,128)(2,1)S(1)} fusion(s32[1,16,4]{1,2,0:T(4,128)} %param.7), kind=kLoop, calls=%fused_computation.12 | loop fusion | flops 64 | bytes 384 | tf_op jit(solution)/shard_map/convert_element_type | solution.py:303
  1.8 0.7 %fusion.5.facts = bf16[16,128]{1,0:T(8,128)(2,1)S(1)} fusion(bf16[4,16]{1,0:T(4,128)(2,1)S(1)} %convert_bitcast_fusion, bf16[1,16]{1,0:T(2,128)(2,1)} %param.6), kind=kLoop, calls=%fused_computation.9 | loop fusion | flops 22528 | bytes 4256 | tf_op jit(solution)/shard_map/concatenate | solution.py:303
  2.4 0.1 pad_add_fusion.spot
  2.5 0.6 shard_map.55
  3.1 2.4 %collective-permute-start.5 = (bf16[16,7424]{1,0:T(8,128)(2,1)S(1)}, bf16[16,7424]{1,0:T(8,128)(2,1)S(1)}, u32[]{:S(2)}, u32[]{:S(2)}) collective-permute-start(bf16[16,7424]{1,0:T(8,128)(2,1)S(1)} %get-tuple-element.35), channel_id=1, source_target_pairs={{0,3},{2,1},{4,2},{6,0},{8,6},{10,4},{12,10},{14,8},{13,14},{15,12... | collective-permute-start | bytes 712712 | tf_op jit(solution)/shard_map/rows_behind/ppermute | solution.py:297
  5.5 0.7 %collective-permute-start = (bf16[16,7424]{1,0:T(8,128)(2,1)S(1)}, bf16[16,7424]{1,0:T(8,128)(2,1)S(1)}, u32[]{:S(2)}, u32[]{:S(2)}) collective-permute-start(bf16[16,7424]{1,0:T(8,128)(2,1)S(1)} %get-tuple-element.30.refs_0_), channel_id=1, source_target_pairs={{0,4},{2,6},{4,8},{6,10},{8,12},{10,14},{12,13},{14,15},{13,9},{15... | collective-permute-start | bytes 712712 | tf_op jit(solution)/shard_map/rows_ahead/ppermute | solution.py:297
  6.2 1.3 %collective-permute-start.3 = (bf16[16,7424]{1,0:T(8,128)(2,1)S(1)}, bf16[16,7424]{1,0:T(8,128)(2,1)S(1)}, u32[]{:S(2)}, u32[]{:S(2)}) collective-permute-start(bf16[16,7424]{1,0:T(8,128)(2,1)S(1)} %get-tuple-element.30.refs_0_), channel_id=1, source_target_pairs={{0,1},{2,3},{4,0},{6,2},{8,4},{10,6},{12,8},{14,10},{13,12},{15,14... | collective-permute-start | bytes 712712 | tf_op jit(solution)/shard_map/rows_behind/ppermute | solution.py:297
  7.5 0.1 collective-permute-start.4
  7.6 2.4 %copy.10 = bf16[1,1,128,2,7296]{4,2,3,1,0:T(8,128)(2,1)S(1)} copy(bf16[1,1,128,2,7296]{4,3,2,1,0:T(2,128)(2,1)} %param.9) | data formatting | bytes 7471104 | tf_op jit(solution)/shard_map/optimization_barrier | solution.py:314
  10.1 0.8 %shard_map.56 = (bf16[128,7296]{1,0:T(8,128)(2,1)S(1)}, bf16[128,7296]{1,0:T(8,128)(2,1)S(1)}) custom-call(s32[4]{0:T(128)S(1)} %pad_add_fusion.spot, bf16[2,128,7296]{2,1,0:T(8,128)(2,1)S(1)} %bitcast.19), custom_call_target="tpu_custom_call" | custom-call | tf_op jit(solution)/shard_map/pallas_call | solution.py:317
  10.9 0.8 %collective-permute-start.6 = (bf16[128,7296]{1,0:T(8,128)(2,1)S(1)}, bf16[128,7296]{1,0:T(8,128)(2,1)S(1)}, u32[]{:S(2)}, u32[]{:S(2)}) collective-permute-start(bf16[128,7296]{1,0:T(8,128)(2,1)S(1)} %get-tuple-element.36), channel_id=1, source_target_pairs={{0,2},{2,0},{4,6},{6,4},{8,10},{10,8},{12,14},{14,12},{1,3},{3,1},... | collective-permute-start | bytes 5603336 | tf_op jit(solution)/shard_map/mate_panel/ppermute | solution.py:325
  11.7 0.0 collective-permute-done.5.refs_5_
  11.7 1.2 %collective-permute-start.2 = (bf16[16,7424]{1,0:T(8,128)(2,1)S(1)}, bf16[16,7424]{1,0:T(8,128)(2,1)S(1)}, u32[]{:S(2)}, u32[]{:S(2)}) collective-permute-start(bf16[16,7424]{1,0:T(8,128)(2,1)S(1)} %get-tuple-element.35), channel_id=1, source_target_pairs={{0,2},{2,0},{4,6},{6,4},{8,10},{10,8},{12,14},{14,12},{1,3},{3,1},... | collective-permute-start | bytes 712712 | tf_op jit(solution)/shard_map/mate_rows/ppermute | solution.py:365
  12.9 0.1 shard_map.57.refs_8_.refs_10_.refs_4_
  13.0 1.2 %collective-permute-done.refs_2_ = bf16[16,7424]{1,0:T(8,128)(2,1)S(1)} collective-permute-done((bf16[16,7424]{1,0:T(8,128)(2,1)S(1)}, bf16[16,7424]{1,0:T(8,128)(2,1)S(1)}, u32[]{:S(2)}, u32[]{:S(2)}) %collective-permute-start) | collective-permute-done | bytes 237600 | tf_op jit(solution)/shard_map/rows_ahead/ppermute | solution.py:297
  14.2 1.6 %collective-permute-start.9 = (bf16[16,7424]{1,0:T(8,128)(2,1)S(1)}, bf16[16,7424]{1,0:T(8,128)(2,1)S(1)}, u32[]{:S(2)}, u32[]{:S(2)}) collective-permute-start(bf16[16,7424]{1,0:T(8,128)(2,1)S(1)} %collective-permute-done.5.refs_5_), channel_id=1, source_target_pairs={{0,1},{2,3},{4,0},{6,2},{8,4},{10,6},{12,8},{14,10},{13,12},{15,14... | collective-permute-start | bytes 712712 | tf_op jit(solution)/shard_map/rows_behind/ppermute | solution.py:297
  15.7 0.0 collective-permute-done.2.refs_1_
  15.7 1.3 %collective-permute-start.1 = (bf16[16,7424]{1,0:T(8,128)(2,1)S(1)}, bf16[16,7424]{1,0:T(8,128)(2,1)S(1)}, u32[]{:S(2)}, u32[]{:S(2)}) collective-permute-start(bf16[16,7424]{1,0:T(8,128)(2,1)S(1)} %collective-permute-done.refs_2_), channel_id=1, source_target_pairs={{0,4},{2,6},{4,8},{6,10},{8,12},{10,14},{12,13},{14,15},{13,9},{15... | collective-permute-start | bytes 712712 | tf_op jit(solution)/shard_map/rows_ahead/ppermute | solution.py:297
  17.1 0.6 %collective-permute-done.3.refs_3_ = bf16[16,7424]{1,0:T(8,128)(2,1)S(1)} collective-permute-done((bf16[16,7424]{1,0:T(8,128)(2,1)S(1)}, bf16[16,7424]{1,0:T(8,128)(2,1)S(1)}, u32[]{:S(2)}, u32[]{:S(2)}) %collective-permute-start.3) | collective-permute-done | bytes 237600 | tf_op jit(solution)/shard_map/rows_behind/ppermute | solution.py:297
  17.7 1.6 %collective-permute-start.12 = (bf16[16,7424]{1,0:T(8,128)(2,1)S(1)}, bf16[16,7424]{1,0:T(8,128)(2,1)S(1)}, u32[]{:S(2)}, u32[]{:S(2)}) collective-permute-start(bf16[16,7424]{1,0:T(8,128)(2,1)S(1)} %collective-permute-done.3.refs_3_), channel_id=1, source_target_pairs={{0,1},{2,3},{4,0},{6,2},{8,4},{10,6},{12,8},{14,10},{13,12},{15,14... | collective-permute-start | bytes 712712 | tf_op jit(solution)/shard_map/rows_behind/ppermute | solution.py:297
  19.3 0.0 collective-permute-done.4.refs_4_
  19.3 0.5 collective-permute-start.13
  19.7 3.8 %shard_map.58 = (f32[96,128]{1,0:T(8,128)S(1)}, f32[96,128]{1,0:T(8,128)S(1)}, f32[96,128]{1,0:T(8,128)S(1)}) custom-call(s32[4]{0:T(128)S(1)} %pad_add_fusion.spot, bf16[16,7424]{1,0:T(8,128)(2,1)S(1)} %get-tuple-element.30.refs_0_, bf16[16,7424]{1,0:T(8,128)(2,1)S(1)} %collective-permute-done.2.refs_1_, bf16[16,7424]{1,0:T(8,128)(2,1)S(1)} %collective-permute-done.refs_2_, ...), custom_call_target="tpu_custom_call" | custom-call | flops 956301312 | bytes 5136384 | tf_op jit(solution)/shard_map/pallas_call | solution.py:175
  23.6 1.6 %collective-permute-start.10 = (bf16[16,7424]{1,0:T(8,128)(2,1)S(1)}, bf16[16,7424]{1,0:T(8,128)(2,1)S(1)}, u32[]{:S(2)}, u32[]{:S(2)}) collective-permute-start(bf16[16,7424]{1,0:T(8,128)(2,1)S(1)} %collective-permute-done.9.refs_3_), channel_id=1, source_target_pairs={{0,1},{2,3},{4,0},{6,2},{8,4},{10,6},{12,8},{14,10},{13,12},{15,14... | collective-permute-start | bytes 712712 | tf_op jit(solution)/shard_map/rows_behind/ppermute | solution.py:297
  25.2 0.5 collective-permute-start.7
  25.7 2.3 %collective-permute-done.12.refs_1_ = bf16[16,7424]{1,0:T(8,128)(2,1)S(1)} collective-permute-done((bf16[16,7424]{1,0:T(8,128)(2,1)S(1)}, bf16[16,7424]{1,0:T(8,128)(2,1)S(1)}, u32[]{:S(2)}, u32[]{:S(2)}) %collective-permute-start.12) | collective-permute-done | bytes 237600 | tf_op jit(solution)/shard_map/rows_behind/ppermute | solution.py:297
  28.0 1.6 %collective-permute-start.14 = (bf16[16,7424]{1,0:T(8,128)(2,1)S(1)}, bf16[16,7424]{1,0:T(8,128)(2,1)S(1)}, u32[]{:S(2)}, u32[]{:S(2)}) collective-permute-start(bf16[16,7424]{1,0:T(8,128)(2,1)S(1)} %collective-permute-done.12.refs_1_), channel_id=1, source_target_pairs={{0,1},{2,3},{4,0},{6,2},{8,4},{10,6},{12,8},{14,10},{13,12},{15,14... | collective-permute-start | bytes 712712 | tf_op jit(solution)/shard_map/rows_behind/ppermute | solution.py:297
  29.6 1.2 %collective-permute-start.15 = (bf16[16,7424]{1,0:T(8,128)(2,1)S(1)}, bf16[16,7424]{1,0:T(8,128)(2,1)S(1)}, u32[]{:S(2)}, u32[]{:S(2)}) collective-permute-start(bf16[16,7424]{1,0:T(8,128)(2,1)S(1)} %collective-permute-done.13.refs_2_), channel_id=1, source_target_pairs={{0,4},{2,6},{4,8},{6,10},{8,12},{10,14},{12,13},{14,15},{13,9},{15... | collective-permute-start | bytes 712712 | tf_op jit(solution)/shard_map/rows_ahead/ppermute | solution.py:297
  30.7 2.3 %collective-permute-done.10.refs_7_ = bf16[16,7424]{1,0:T(8,128)(2,1)S(1)} collective-permute-done((bf16[16,7424]{1,0:T(8,128)(2,1)S(1)}, bf16[16,7424]{1,0:T(8,128)(2,1)S(1)}, u32[]{:S(2)}, u32[]{:S(2)}) %collective-permute-start.10) | collective-permute-done | bytes 237600 | tf_op jit(solution)/shard_map/rows_behind/ppermute | solution.py:297
  33.1 1.6 %collective-permute-start.11 = (bf16[16,7424]{1,0:T(8,128)(2,1)S(1)}, bf16[16,7424]{1,0:T(8,128)(2,1)S(1)}, u32[]{:S(2)}, u32[]{:S(2)}) collective-permute-start(bf16[16,7424]{1,0:T(8,128)(2,1)S(1)} %collective-permute-done.10.refs_7_), channel_id=1, source_target_pairs={{0,1},{2,3},{4,0},{6,2},{8,4},{10,6},{12,8},{14,10},{13,12},{15,14... | collective-permute-start | bytes 712712 | tf_op jit(solution)/shard_map/rows_behind/ppermute | solution.py:297
  34.7 1.2 %collective-permute-start.8 = (bf16[16,7424]{1,0:T(8,128)(2,1)S(1)}, bf16[16,7424]{1,0:T(8,128)(2,1)S(1)}, u32[]{:S(2)}, u32[]{:S(2)}) collective-permute-start(bf16[16,7424]{1,0:T(8,128)(2,1)S(1)} %collective-permute-done.7.refs_4_), channel_id=1, source_target_pairs={{0,4},{2,6},{4,8},{6,10},{8,12},{10,14},{12,13},{14,15},{13,9},{15... | collective-permute-start | bytes 712712 | tf_op jit(solution)/shard_map/rows_ahead/ppermute | solution.py:297
  35.8 2.3 %collective-permute-done.14.refs_5_ = bf16[16,7424]{1,0:T(8,128)(2,1)S(1)} collective-permute-done((bf16[16,7424]{1,0:T(8,128)(2,1)S(1)}, bf16[16,7424]{1,0:T(8,128)(2,1)S(1)}, u32[]{:S(2)}, u32[]{:S(2)}) %collective-permute-start.14) | collective-permute-done | bytes 237600 | tf_op jit(solution)/shard_map/rows_behind/ppermute | solution.py:297
  38.2 1.6 %collective-permute-done.15.refs_6_ = bf16[16,7424]{1,0:T(8,128)(2,1)S(1)} collective-permute-done((bf16[16,7424]{1,0:T(8,128)(2,1)S(1)}, bf16[16,7424]{1,0:T(8,128)(2,1)S(1)}, u32[]{:S(2)}, u32[]{:S(2)}) %collective-permute-start.15) | collective-permute-done | bytes 237600 | tf_op jit(solution)/shard_map/rows_ahead/ppermute | solution.py:297
  39.7 4.1 %shard_map.59 = (f32[128,128]{1,0:T(8,128)S(1)}, f32[128,128]{1,0:T(8,128)S(1)}, f32[128,128]{1,0:T(8,128)S(1)}) custom-call(s32[4]{0:T(128)S(1)} %pad_add_fusion.spot, bf16[16,7424]{1,0:T(8,128)(2,1)S(1)} %collective-permute-done.1.refs_0_, bf16[16,7424]{1,0:T(8,128)(2,1)S(1)} %collective-permute-done.12.refs_1_, ...), custom_call_target="tpu_custom_call" | custom-call | flops 956301312 | bytes 5603328 | tf_op jit(solution)/shard_map/pallas_call | solution.py:175
  43.9 0.5 collective-permute-done.8.refs_0_
  44.4 3.1 %shard_map.60 = (f32[2,256,128]{2,1,0:T(8,128)S(1)}, f32[256,128]{1,0:T(8,128)S(1)}) custom-call(s32[4]{0:T(128)S(1)} %pad_add_fusion.spot, bf16[16,7424]{1,0:T(8,128)(2,1)S(1)} %collective-permute-done.8.refs_0_, bf16[16,7424]{1,0:T(8,128)(2,1)S(1)} %collective-permute-done.11.refs_1_, f32[1,7296]{1,0:T(1,128)S(1)} %broadcast_in_dim.3.refs_6_.refs_8_.refs_2_, ...), custom_call_target="tpu_custom_call" | custom-call | flops 956301312 | bytes 4202496 | tf_op jit(solution)/shard_map/pallas_call | solution.py:175
  47.5 0.0 collective-permute-start.16
  47.6 1.5 %collective-permute-done.16.mate = f32[2,256,128]{2,1,0:T(8,128)S(1)} collective-permute-done((f32[2,256,128]{2,1,0:T(8,128)S(1)}, f32[2,256,128]{2,1,0:T(8,128)S(1)}, u32[]{:S(2)}, u32[]{:S(2)}) %collective-permute-start.16) | collective-permute-done | bytes 262176 | tf_op jit(solution)/shard_map/ppermute | solution.py:375
  49.1 0.9 %shard_map.61 = (f32[128,128]{1,0:T(8,128)S(1)}, f32[128,128]{1,0:T(8,128)S(1)}, f32[8,128]{1,0:T(8,128)S(1)}) custom-call(s32[4]{0:T(128)S(1)} %pad_add_fusion.spot, f32[2,256,128]{2,1,0:T(8,128)S(1)} %get-tuple-element.46.partial, f32[2,256,128]{2,1,0:T(8,128)S(1)} %collective-permute-done.16.mate, f32[256,128]{1,0:T(8,128)S(1)} %get-tuple-element.47.facts), custom_call_target="tpu_custom_call" | custom-call | tf_op jit(solution)/shard_map/pallas_call | solution.py:376
  50.0 1.6 %collective-permute-start.17 = (f32[8,128]{1,0:T(8,128)S(1)}, f32[8,128]{1,0:T(8,128)S(1)}, u32[]{:S(2)}, u32[]{:S(2)}) collective-permute-start(f32[8,128]{1,0:T(8,128)S(1)} %get-tuple-element.48), channel_id=1, source_target_pairs={{0,1},{1,0},{2,3},{3,2},{4,5},{5,4},{6,7},{7,6},{8,9},{9,8},{10,11... | collective-permute-start | bytes 12296 | tf_op jit(solution)/shard_map/ppermute | solution.py:388
  51.6 0.4 collective-permute-start.21
  52.0 1.6 %collective-permute-done.17 = f32[8,128]{1,0:T(8,128)S(1)} collective-permute-done((f32[8,128]{1,0:T(8,128)S(1)}, f32[8,128]{1,0:T(8,128)S(1)}, u32[]{:S(2)}, u32[]{:S(2)}) %collective-permute-start.17) | collective-permute-done | bytes 4128 | tf_op jit(solution)/shard_map/ppermute | solution.py:388
  53.7 1.2 %collective-permute-start.18 = (f32[8,128]{1,0:T(8,128)S(1)}, f32[8,128]{1,0:T(8,128)S(1)}, u32[]{:S(2)}, u32[]{:S(2)}) collective-permute-start(f32[8,128]{1,0:T(8,128)S(1)} %select_maximum_fusion.refs_0_), channel_id=1, source_target_pairs={{0,4},{2,10},{4,0},{6,14},{8,12},{10,2},{12,8},{14,6},{1,5},{3,11}... | collective-permute-start | bytes 12296 | tf_op jit(solution)/shard_map/ppermute | solution.py:395
  54.9 2.5 %collective-permute-start.20 = (f32[8,128]{1,0:T(8,128)S(1)}, f32[8,128]{1,0:T(8,128)S(1)}, u32[]{:S(2)}, u32[]{:S(2)}) collective-permute-start(f32[8,128]{1,0:T(8,128)S(1)} %select_maximum_fusion.refs_0_), channel_id=1, source_target_pairs={{0,12},{2,14},{4,8},{6,10},{8,4},{10,6},{12,0},{14,2},{1,13},{3,15... | collective-permute-start | bytes 12296 | tf_op jit(solution)/shard_map/ppermute | solution.py:396
  57.3 1.1 %shard_map.62 = (f32[128,256]{1,0:T(8,128)S(1)}, f32[128,128]{1,0:T(8,128)S(1)}, f32[8,128]{1,0:T(8,128)S(1)}) custom-call(s32[4]{0:T(128)S(1)} %pad_add_fusion.spot, f32[128,128]{1,0:T(8,128)S(1)} %get-tuple-element.49.mine, f32[128,128]{1,0:T(8,128)S(1)} %collective-permute-done.21.across, f32[256,128]{1,0:T(8,128)S(1)} %get-tuple-element.47.facts), custom_call_target="tpu_custom_call" | custom-call | tf_op jit(solution)/shard_map/pallas_call | solution.py:403
  58.4 1.8 %collective-permute-done.20.refs_3_ = f32[8,128]{1,0:T(8,128)S(1)} collective-permute-done((f32[8,128]{1,0:T(8,128)S(1)}, f32[8,128]{1,0:T(8,128)S(1)}, u32[]{:S(2)}, u32[]{:S(2)}) %collective-permute-start.20) | collective-permute-done | bytes 4128 | tf_op jit(solution)/shard_map/ppermute | solution.py:396
  60.3 0.8 %shard_map.63 = f32[128,256]{1,0:T(8,128)} custom-call(f32[8,128]{1,0:T(8,128)S(1)} %select_maximum_fusion.refs_0_, f32[8,128]{1,0:T(8,128)S(1)} %collective-permute-done.18.refs_1_, f32[8,128]{1,0:T(8,128)S(1)} %collective-permute-done.19.refs_2_, f32[8,128]{1,0:T(8,128)S(1)} %collective-permute-done.20.refs_3_, f32[8,128]{1,0:T(8,128)S(1)} %get-tuple-element.52.refs_4_, ...), custom_call_target="tpu_custom_call" | custom-call | tf_op jit(solution)/shard_map/pallas_call | solution.py:414
  (15 shorter events, 0.1 us)
Async XLA Ops:
  3.1 8.6 %collective-permute-start.5 = (bf16[16,7424]{1,0:T(8,128)(2,1)S(1)}, bf16[16,7424]{1,0:T(8,128)(2,1)S(1)}, u32[]{:S(2)}, u32[]{:S(2)}) collective-permute-start(bf16[16,7424]{1,0:T(8,128)(2,1)S(1)} %get-tuple-element.35), channel_id=1, source_target_pairs={{0,3},{2,1},{4,2},{6,0},{8,6},{10,4},{12,10},{14,8},{13,14},{15,12... | collective-permute-start | bytes 712712 | tf_op jit(solution)/shard_map/rows_behind/ppermute | solution.py:297
  5.5 8.7 %collective-permute-start = (bf16[16,7424]{1,0:T(8,128)(2,1)S(1)}, bf16[16,7424]{1,0:T(8,128)(2,1)S(1)}, u32[]{:S(2)}, u32[]{:S(2)}) collective-permute-start(bf16[16,7424]{1,0:T(8,128)(2,1)S(1)} %get-tuple-element.30.refs_0_), channel_id=1, source_target_pairs={{0,4},{2,6},{4,8},{6,10},{8,12},{10,14},{12,13},{14,15},{13,9},{15... | collective-permute-start | bytes 712712 | tf_op jit(solution)/shard_map/rows_ahead/ppermute | solution.py:297
  6.2 11.5 %collective-permute-start.3 = (bf16[16,7424]{1,0:T(8,128)(2,1)S(1)}, bf16[16,7424]{1,0:T(8,128)(2,1)S(1)}, u32[]{:S(2)}, u32[]{:S(2)}) collective-permute-start(bf16[16,7424]{1,0:T(8,128)(2,1)S(1)} %get-tuple-element.30.refs_0_), channel_id=1, source_target_pairs={{0,1},{2,3},{4,0},{6,2},{8,4},{10,6},{12,8},{14,10},{13,12},{15,14... | collective-permute-start | bytes 712712 | tf_op jit(solution)/shard_map/rows_behind/ppermute | solution.py:297
  7.5 11.7 %collective-permute-start.4 = (bf16[16,7424]{1,0:T(8,128)(2,1)S(1)}, bf16[16,7424]{1,0:T(8,128)(2,1)S(1)}, u32[]{:S(2)}, u32[]{:S(2)}) collective-permute-start(bf16[16,7424]{1,0:T(8,128)(2,1)S(1)} %get-tuple-element.35), channel_id=1, source_target_pairs={{0,6},{2,4},{4,10},{6,8},{8,14},{10,12},{12,15},{14,13},{13,11},{1... | collective-permute-start | bytes 712712 | tf_op jit(solution)/shard_map/rows_ahead/ppermute | solution.py:297
  10.9 8.9 %collective-permute-start.6 = (bf16[128,7296]{1,0:T(8,128)(2,1)S(1)}, bf16[128,7296]{1,0:T(8,128)(2,1)S(1)}, u32[]{:S(2)}, u32[]{:S(2)}) collective-permute-start(bf16[128,7296]{1,0:T(8,128)(2,1)S(1)} %get-tuple-element.36), channel_id=1, source_target_pairs={{0,2},{2,0},{4,6},{6,4},{8,10},{10,8},{12,14},{14,12},{1,3},{3,1},... | collective-permute-start | bytes 5603336 | tf_op jit(solution)/shard_map/mate_panel/ppermute | solution.py:325
  11.7 4.1 %collective-permute-start.2 = (bf16[16,7424]{1,0:T(8,128)(2,1)S(1)}, bf16[16,7424]{1,0:T(8,128)(2,1)S(1)}, u32[]{:S(2)}, u32[]{:S(2)}) collective-permute-start(bf16[16,7424]{1,0:T(8,128)(2,1)S(1)} %get-tuple-element.35), channel_id=1, source_target_pairs={{0,2},{2,0},{4,6},{6,4},{8,10},{10,8},{12,14},{14,12},{1,3},{3,1},... | collective-permute-start | bytes 712712 | tf_op jit(solution)/shard_map/mate_rows/ppermute | solution.py:365
  12.9 4.2 %copy-start = (f32[7296]{0:T(1024)S(1)}, f32[7296]{0:T(1024)}, u32[]{:S(2)}) copy-start(f32[7296]{0:T(1024)} %param.8) | copy-start | bytes 87556
  14.2 9.4 %collective-permute-start.9 = (bf16[16,7424]{1,0:T(8,128)(2,1)S(1)}, bf16[16,7424]{1,0:T(8,128)(2,1)S(1)}, u32[]{:S(2)}, u32[]{:S(2)}) collective-permute-start(bf16[16,7424]{1,0:T(8,128)(2,1)S(1)} %collective-permute-done.5.refs_5_), channel_id=1, source_target_pairs={{0,1},{2,3},{4,0},{6,2},{8,4},{10,6},{12,8},{14,10},{13,12},{15,14... | collective-permute-start | bytes 712712 | tf_op jit(solution)/shard_map/rows_behind/ppermute | solution.py:297
  15.7 9.4 %collective-permute-start.1 = (bf16[16,7424]{1,0:T(8,128)(2,1)S(1)}, bf16[16,7424]{1,0:T(8,128)(2,1)S(1)}, u32[]{:S(2)}, u32[]{:S(2)}) collective-permute-start(bf16[16,7424]{1,0:T(8,128)(2,1)S(1)} %collective-permute-done.refs_2_), channel_id=1, source_target_pairs={{0,4},{2,6},{4,8},{6,10},{8,12},{10,14},{12,13},{14,15},{13,9},{15... | collective-permute-start | bytes 712712 | tf_op jit(solution)/shard_map/rows_ahead/ppermute | solution.py:297
  17.7 10.3 %collective-permute-start.12 = (bf16[16,7424]{1,0:T(8,128)(2,1)S(1)}, bf16[16,7424]{1,0:T(8,128)(2,1)S(1)}, u32[]{:S(2)}, u32[]{:S(2)}) collective-permute-start(bf16[16,7424]{1,0:T(8,128)(2,1)S(1)} %collective-permute-done.3.refs_3_), channel_id=1, source_target_pairs={{0,1},{2,3},{4,0},{6,2},{8,4},{10,6},{12,8},{14,10},{13,12},{15,14... | collective-permute-start | bytes 712712 | tf_op jit(solution)/shard_map/rows_behind/ppermute | solution.py:297
  19.3 10.3 %collective-permute-start.13 = (bf16[16,7424]{1,0:T(8,128)(2,1)S(1)}, bf16[16,7424]{1,0:T(8,128)(2,1)S(1)}, u32[]{:S(2)}, u32[]{:S(2)}) collective-permute-start(bf16[16,7424]{1,0:T(8,128)(2,1)S(1)} %collective-permute-done.4.refs_4_), channel_id=1, source_target_pairs={{0,4},{2,6},{4,8},{6,10},{8,12},{10,14},{12,13},{14,15},{13,9},{15... | collective-permute-start | bytes 712712 | tf_op jit(solution)/shard_map/rows_ahead/ppermute | solution.py:297
  23.6 9.5 %collective-permute-start.10 = (bf16[16,7424]{1,0:T(8,128)(2,1)S(1)}, bf16[16,7424]{1,0:T(8,128)(2,1)S(1)}, u32[]{:S(2)}, u32[]{:S(2)}) collective-permute-start(bf16[16,7424]{1,0:T(8,128)(2,1)S(1)} %collective-permute-done.9.refs_3_), channel_id=1, source_target_pairs={{0,1},{2,3},{4,0},{6,2},{8,4},{10,6},{12,8},{14,10},{13,12},{15,14... | collective-permute-start | bytes 712712 | tf_op jit(solution)/shard_map/rows_behind/ppermute | solution.py:297
  25.2 9.5 %collective-permute-start.7 = (bf16[16,7424]{1,0:T(8,128)(2,1)S(1)}, bf16[16,7424]{1,0:T(8,128)(2,1)S(1)}, u32[]{:S(2)}, u32[]{:S(2)}) collective-permute-start(bf16[16,7424]{1,0:T(8,128)(2,1)S(1)} %collective-permute-done.1.refs_0_), channel_id=1, source_target_pairs={{0,4},{2,6},{4,8},{6,10},{8,12},{10,14},{12,13},{14,15},{13,9},{15... | collective-permute-start | bytes 712712 | tf_op jit(solution)/shard_map/rows_ahead/ppermute | solution.py:297
  28.0 10.2 %collective-permute-start.14 = (bf16[16,7424]{1,0:T(8,128)(2,1)S(1)}, bf16[16,7424]{1,0:T(8,128)(2,1)S(1)}, u32[]{:S(2)}, u32[]{:S(2)}) collective-permute-start(bf16[16,7424]{1,0:T(8,128)(2,1)S(1)} %collective-permute-done.12.refs_1_), channel_id=1, source_target_pairs={{0,1},{2,3},{4,0},{6,2},{8,4},{10,6},{12,8},{14,10},{13,12},{15,14... | collective-permute-start | bytes 712712 | tf_op jit(solution)/shard_map/rows_behind/ppermute | solution.py:297
  29.6 10.2 %collective-permute-start.15 = (bf16[16,7424]{1,0:T(8,128)(2,1)S(1)}, bf16[16,7424]{1,0:T(8,128)(2,1)S(1)}, u32[]{:S(2)}, u32[]{:S(2)}) collective-permute-start(bf16[16,7424]{1,0:T(8,128)(2,1)S(1)} %collective-permute-done.13.refs_2_), channel_id=1, source_target_pairs={{0,4},{2,6},{4,8},{6,10},{8,12},{10,14},{12,13},{14,15},{13,9},{15... | collective-permute-start | bytes 712712 | tf_op jit(solution)/shard_map/rows_ahead/ppermute | solution.py:297
  33.1 10.8 %collective-permute-start.11 = (bf16[16,7424]{1,0:T(8,128)(2,1)S(1)}, bf16[16,7424]{1,0:T(8,128)(2,1)S(1)}, u32[]{:S(2)}, u32[]{:S(2)}) collective-permute-start(bf16[16,7424]{1,0:T(8,128)(2,1)S(1)} %collective-permute-done.10.refs_7_), channel_id=1, source_target_pairs={{0,1},{2,3},{4,0},{6,2},{8,4},{10,6},{12,8},{14,10},{13,12},{15,14... | collective-permute-start | bytes 712712 | tf_op jit(solution)/shard_map/rows_behind/ppermute | solution.py:297
  34.7 9.8 %collective-permute-start.8 = (bf16[16,7424]{1,0:T(8,128)(2,1)S(1)}, bf16[16,7424]{1,0:T(8,128)(2,1)S(1)}, u32[]{:S(2)}, u32[]{:S(2)}) collective-permute-start(bf16[16,7424]{1,0:T(8,128)(2,1)S(1)} %collective-permute-done.7.refs_4_), channel_id=1, source_target_pairs={{0,4},{2,6},{4,8},{6,10},{8,12},{10,14},{12,13},{14,15},{13,9},{15... | collective-permute-start | bytes 712712 | tf_op jit(solution)/shard_map/rows_ahead/ppermute | solution.py:297
  47.5 1.6 %collective-permute-start.16 = (f32[2,256,128]{2,1,0:T(8,128)S(1)}, f32[2,256,128]{2,1,0:T(8,128)S(1)}, u32[]{:S(2)}, u32[]{:S(2)}) collective-permute-start(f32[2,256,128]{2,1,0:T(8,128)S(1)} %get-tuple-element.46.partial), channel_id=1, source_target_pairs={{0,2},{2,0},{4,6},{6,4},{8,10},{10,8},{12,14},{14,12},{1,3},{3,1},... | collective-permute-start | bytes 786440 | tf_op jit(solution)/shard_map/ppermute | solution.py:375
  50.0 3.6 %collective-permute-start.17 = (f32[8,128]{1,0:T(8,128)S(1)}, f32[8,128]{1,0:T(8,128)S(1)}, u32[]{:S(2)}, u32[]{:S(2)}) collective-permute-start(f32[8,128]{1,0:T(8,128)S(1)} %get-tuple-element.48), channel_id=1, source_target_pairs={{0,1},{1,0},{2,3},{3,2},{4,5},{5,4},{6,7},{7,6},{8,9},{9,8},{10,11... | collective-permute-start | bytes 12296 | tf_op jit(solution)/shard_map/ppermute | solution.py:388
  51.6 5.7 %collective-permute-start.21 = (f32[128,128]{1,0:T(8,128)S(1)}, f32[128,128]{1,0:T(8,128)S(1)}, u32[]{:S(2)}, u32[]{:S(2)}) collective-permute-start(f32[128,128]{1,0:T(8,128)S(1)} %get-tuple-element.51), channel_id=1, source_target_pairs={{0,1},{1,0},{2,3},{3,2},{4,5},{5,4},{6,7},{7,6},{8,9},{9,8},{10,11... | collective-permute-start | bytes 196616 | tf_op jit(solution)/shard_map/ppermute | solution.py:390
  53.7 3.7 %collective-permute-start.18 = (f32[8,128]{1,0:T(8,128)S(1)}, f32[8,128]{1,0:T(8,128)S(1)}, u32[]{:S(2)}, u32[]{:S(2)}) collective-permute-start(f32[8,128]{1,0:T(8,128)S(1)} %select_maximum_fusion.refs_0_), channel_id=1, source_target_pairs={{0,4},{2,10},{4,0},{6,14},{8,12},{10,2},{12,8},{14,6},{1,5},{3,11}... | collective-permute-start | bytes 12296 | tf_op jit(solution)/shard_map/ppermute | solution.py:395
  54.9 5.4 %collective-permute-start.20 = (f32[8,128]{1,0:T(8,128)S(1)}, f32[8,128]{1,0:T(8,128)S(1)}, u32[]{:S(2)}, u32[]{:S(2)}) collective-permute-start(f32[8,128]{1,0:T(8,128)S(1)} %select_maximum_fusion.refs_0_), channel_id=1, source_target_pairs={{0,12},{2,14},{4,8},{6,10},{8,4},{10,6},{12,0},{14,2},{1,13},{3,15... | collective-permute-start | bytes 12296 | tf_op jit(solution)/shard_map/ppermute | solution.py:396
  57.3 2.9 %collective-permute-start.19 = (f32[8,128]{1,0:T(8,128)S(1)}, f32[8,128]{1,0:T(8,128)S(1)}, u32[]{:S(2)}, u32[]{:S(2)}) collective-permute-start(f32[8,128]{1,0:T(8,128)S(1)} %collective-permute-done.18.refs_1_), channel_id=1, source_target_pairs={{0,2},{2,0},{4,6},{6,4},{8,10},{10,8},{12,14},{14,12},{1,3},{3,1},... | collective-permute-start | bytes 12296 | tf_op jit(solution)/shard_map/ppermute | solution.py:397

commit v15 on v14

--- a/solution.py
+++ b/solution.py
@@ -391,15 +391,6 @@
     peak = jnp.maximum(stats[0], x_stats[1])
     total = stats[2] * jnp.exp(stats[0] - peak) + x_stats[3] * jnp.exp(x_stats[1] - peak)
     pair = jnp.pad(jnp.stack([peak, total]), ((0, 6), (0, 0)))
-    if chips == 4:
-        near = lax.ppermute(pair, "orient", [(d, d ^ (2 << d % 2)) for d in range(devices)])
-        far = lax.ppermute(pair, "orient", [(d, d ^ 6) for d in range(devices)])
-        parts = [pair, near, lax.ppermute(near, "orient", mate_pairs), far]
-    else:
-        parts = [pair] + [
-            lax.ppermute(pair, "orient", [(d, (d + 2 * s) % devices) for d in range(devices)])
-            for s in range(1, chips)
-        ]
     slots, chosen, tops = pl.pallas_call(
         functools.partial(slot_kernel, local_search, slots_each, per_device),
         in_specs=[smem] + [vmem] * 3,
@@ -411,6 +402,16 @@
         ],
         compiler_params=params,
     )(spot, mine, from_x, all_facts)
+    if chips == 4:
+        near = lax.ppermute(pair, "orient", [(d, d ^ (2 << d % 2)) for d in range(devices)])
+        far = lax.ppermute(pair, "orient", [(d, d ^ 6) for d in range(devices)])
+        near, tops = lax.optimization_barrier((near, tops))
+        parts = [pair, near, lax.ppermute(near, "orient", mate_pairs), far]
+    else:
+        parts = [pair] + [
+            lax.ppermute(pair, "orient", [(d, (d + 2 * s) % devices) for d in range(devices)])
+            for s in range(1, chips)
+        ]
     posterior = pl.pallas_call(
         functools.partial(final_kernel, chips),
         in_specs=[vmem] * (chips + 3),

time: 61.3 us -> 61.3 us (level)
  no operation moved by 1% of the time
where the time goes in v15:
time: 61.3 us; the launch traced here: 61 us
  starting transfers between devices  24.9 us (41%)
  waiting for transfers between devices  15.8 us (26%)
  Pallas kernels  15.3 us (25%)
  local copies, waits for them, and re-layouts  3.52 us (6%)
  other arithmetic  1.45 us (2%)
    ppermute x14, starting transfers between devices, forward(): return lax.ppermute(values, ('orient', 'cls'), pairs)  17.1 us
    pallas_call x3, Pallas kernels, score_call(): pl.pallas_call(kernel, in_specs=[pl.BlockSpec(memory_space=pltpu.SMEM)] +...  11 us
    ppermute x14, waiting for transfers between devices, forward(): return lax.ppermute(values, ('orient', 'cls'), pairs)  10.9 us
    ppermute x1, starting transfers between devices, chip_shards(): far = lax.ppermute(pair, 'orient', [(d, d ^ 6) for d in range(devices)])  2.47 us
    optimization_barrier x1, local copies, waits for them, and re-layouts, chip_shards(): _, panels = lax.optimization_barrier((kept, panels))  2.42 us
    ppermute x1, waiting for transfers between devices, chip_shards(): far = lax.ppermute(pair, 'orient', [(d, d ^ 6) for d in range(devices)])  1.76 us
    ppermute x1, starting transfers between devices, chip_shards(): x_stats = lax.ppermute(stats, 'cls', x_pairs)  1.62 us
    ppermute x1, waiting for transfers between devices, chip_shards(): x_stats = lax.ppermute(stats, 'cls', x_pairs)  1.58 us
  transfers between devices with their start and end apart: 22, of which 10 were waited for; matrix products, arithmetic and copies ran while one was open for 4% of the time, Pallas kernels for 16%

profile of v15, /device:TPU:0, one launch (start us, length us, event | category | flops | bytes accessed | tf_op | source)
XLA Modules:
  0.0 61.0 jit_solution(10486872179826216503)
XLA Ops:
  0.0 1.1 %copy.11 = bf16[1,16,2,7296]{3,1,2,0:T(8,128)(2,1)S(1)} copy(bf16[1,16,2,7296]{3,2,1,0:T(2,128)(2,1)} %param.5) | data formatting | bytes 933888 | tf_op args[0]
  1.1 0.7 %convert_bitcast_fusion = bf16[4,16]{1,0:T(4,128)(2,1)S(1)} fusion(s32[1,16,4]{1,2,0:T(4,128)} %param.7), kind=kLoop, calls=%fused_computation.12 | loop fusion | flops 64 | bytes 384 | tf_op jit(solution)/shard_map/convert_element_type | solution.py:303
  1.8 0.7 %fusion.5.facts = bf16[16,128]{1,0:T(8,128)(2,1)S(1)} fusion(bf16[4,16]{1,0:T(4,128)(2,1)S(1)} %convert_bitcast_fusion, bf16[1,16]{1,0:T(2,128)(2,1)} %param.6), kind=kLoop, calls=%fused_computation.9 | loop fusion | flops 22528 | bytes 4256 | tf_op jit(solution)/shard_map/concatenate | solution.py:303
  2.4 0.1 pad_add_fusion.spot
  2.5 0.6 shard_map.55
  3.1 2.4 %collective-permute-start.5 = (bf16[16,7424]{1,0:T(8,128)(2,1)S(1)}, bf16[16,7424]{1,0:T(8,128)(2,1)S(1)}, u32[]{:S(2)}, u32[]{:S(2)}) collective-permute-start(bf16[16,7424]{1,0:T(8,128)(2,1)S(1)} %get-tuple-element.37), channel_id=1, source_target_pairs={{0,3},{2,1},{4,2},{6,0},{8,6},{10,4},{12,10},{14,8},{13,14},{15,12... | collective-permute-start | bytes 712712 | tf_op jit(solution)/shard_map/rows_behind/ppermute | solution.py:297
  5.5 0.7 %collective-permute-start = (bf16[16,7424]{1,0:T(8,128)(2,1)S(1)}, bf16[16,7424]{1,0:T(8,128)(2,1)S(1)}, u32[]{:S(2)}, u32[]{:S(2)}) collective-permute-start(bf16[16,7424]{1,0:T(8,128)(2,1)S(1)} %get-tuple-element.32.refs_0_), channel_id=1, source_target_pairs={{0,4},{2,6},{4,8},{6,10},{8,12},{10,14},{12,13},{14,15},{13,9},{15... | collective-permute-start | bytes 712712 | tf_op jit(solution)/shard_map/rows_ahead/ppermute | solution.py:297
  6.2 1.3 %collective-permute-start.3 = (bf16[16,7424]{1,0:T(8,128)(2,1)S(1)}, bf16[16,7424]{1,0:T(8,128)(2,1)S(1)}, u32[]{:S(2)}, u32[]{:S(2)}) collective-permute-start(bf16[16,7424]{1,0:T(8,128)(2,1)S(1)} %get-tuple-element.32.refs_0_), channel_id=1, source_target_pairs={{0,1},{2,3},{4,0},{6,2},{8,4},{10,6},{12,8},{14,10},{13,12},{15,14... | collective-permute-start | bytes 712712 | tf_op jit(solution)/shard_map/rows_behind/ppermute | solution.py:297
  7.5 0.1 collective-permute-start.4
  7.6 2.4 %copy.10 = bf16[1,1,128,2,7296]{4,2,3,1,0:T(8,128)(2,1)S(1)} copy(bf16[1,1,128,2,7296]{4,3,2,1,0:T(2,128)(2,1)} %param.9) | data formatting | bytes 7471104 | tf_op jit(solution)/shard_map/optimization_barrier | solution.py:314
  10.1 0.8 %shard_map.56 = (bf16[128,7296]{1,0:T(8,128)(2,1)S(1)}, bf16[128,7296]{1,0:T(8,128)(2,1)S(1)}) custom-call(s32[4]{0:T(128)S(1)} %pad_add_fusion.spot, bf16[2,128,7296]{2,1,0:T(8,128)(2,1)S(1)} %bitcast.19), custom_call_target="tpu_custom_call" | custom-call | tf_op jit(solution)/shard_map/pallas_call | solution.py:317
  10.9 0.8 %collective-permute-start.6 = (bf16[128,7296]{1,0:T(8,128)(2,1)S(1)}, bf16[128,7296]{1,0:T(8,128)(2,1)S(1)}, u32[]{:S(2)}, u32[]{:S(2)}) collective-permute-start(bf16[128,7296]{1,0:T(8,128)(2,1)S(1)} %get-tuple-element.38), channel_id=1, source_target_pairs={{0,2},{2,0},{4,6},{6,4},{8,10},{10,8},{12,14},{14,12},{1,3},{3,1},... | collective-permute-start | bytes 5603336 | tf_op jit(solution)/shard_map/mate_panel/ppermute | solution.py:325
  11.7 0.0 collective-permute-done.5.refs_5_
  11.7 1.2 %collective-permute-start.2 = (bf16[16,7424]{1,0:T(8,128)(2,1)S(1)}, bf16[16,7424]{1,0:T(8,128)(2,1)S(1)}, u32[]{:S(2)}, u32[]{:S(2)}) collective-permute-start(bf16[16,7424]{1,0:T(8,128)(2,1)S(1)} %get-tuple-element.37), channel_id=1, source_target_pairs={{0,2},{2,0},{4,6},{6,4},{8,10},{10,8},{12,14},{14,12},{1,3},{3,1},... | collective-permute-start | bytes 712712 | tf_op jit(solution)/shard_map/mate_rows/ppermute | solution.py:365
  12.9 0.1 shard_map.57.refs_8_.refs_10_.refs_4_
  13.0 1.2 %collective-permute-done.refs_2_ = bf16[16,7424]{1,0:T(8,128)(2,1)S(1)} collective-permute-done((bf16[16,7424]{1,0:T(8,128)(2,1)S(1)}, bf16[16,7424]{1,0:T(8,128)(2,1)S(1)}, u32[]{:S(2)}, u32[]{:S(2)}) %collective-permute-start) | collective-permute-done | bytes 237600 | tf_op jit(solution)/shard_map/rows_ahead/ppermute | solution.py:297
  14.2 1.6 %collective-permute-start.9 = (bf16[16,7424]{1,0:T(8,128)(2,1)S(1)}, bf16[16,7424]{1,0:T(8,128)(2,1)S(1)}, u32[]{:S(2)}, u32[]{:S(2)}) collective-permute-start(bf16[16,7424]{1,0:T(8,128)(2,1)S(1)} %collective-permute-done.5.refs_5_), channel_id=1, source_target_pairs={{0,1},{2,3},{4,0},{6,2},{8,4},{10,6},{12,8},{14,10},{13,12},{15,14... | collective-permute-start | bytes 712712 | tf_op jit(solution)/shard_map/rows_behind/ppermute | solution.py:297
  15.7 0.0 collective-permute-done.2.refs_1_
  15.7 1.3 %collective-permute-start.1 = (bf16[16,7424]{1,0:T(8,128)(2,1)S(1)}, bf16[16,7424]{1,0:T(8,128)(2,1)S(1)}, u32[]{:S(2)}, u32[]{:S(2)}) collective-permute-start(bf16[16,7424]{1,0:T(8,128)(2,1)S(1)} %collective-permute-done.refs_2_), channel_id=1, source_target_pairs={{0,4},{2,6},{4,8},{6,10},{8,12},{10,14},{12,13},{14,15},{13,9},{15... | collective-permute-start | bytes 712712 | tf_op jit(solution)/shard_map/rows_ahead/ppermute | solution.py:297
  17.1 0.6 %collective-permute-done.3.refs_3_ = bf16[16,7424]{1,0:T(8,128)(2,1)S(1)} collective-permute-done((bf16[16,7424]{1,0:T(8,128)(2,1)S(1)}, bf16[16,7424]{1,0:T(8,128)(2,1)S(1)}, u32[]{:S(2)}, u32[]{:S(2)}) %collective-permute-start.3) | collective-permute-done | bytes 237600 | tf_op jit(solution)/shard_map/rows_behind/ppermute | solution.py:297
  17.7 1.6 %collective-permute-start.12 = (bf16[16,7424]{1,0:T(8,128)(2,1)S(1)}, bf16[16,7424]{1,0:T(8,128)(2,1)S(1)}, u32[]{:S(2)}, u32[]{:S(2)}) collective-permute-start(bf16[16,7424]{1,0:T(8,128)(2,1)S(1)} %collective-permute-done.3.refs_3_), channel_id=1, source_target_pairs={{0,1},{2,3},{4,0},{6,2},{8,4},{10,6},{12,8},{14,10},{13,12},{15,14... | collective-permute-start | bytes 712712 | tf_op jit(solution)/shard_map/rows_behind/ppermute | solution.py:297
  19.3 0.5 collective-permute-start.13
  19.7 3.8 %shard_map.58 = (f32[96,128]{1,0:T(8,128)S(1)}, f32[96,128]{1,0:T(8,128)S(1)}, f32[96,128]{1,0:T(8,128)S(1)}) custom-call(s32[4]{0:T(128)S(1)} %pad_add_fusion.spot, bf16[16,7424]{1,0:T(8,128)(2,1)S(1)} %get-tuple-element.32.refs_0_, bf16[16,7424]{1,0:T(8,128)(2,1)S(1)} %collective-permute-done.2.refs_1_, bf16[16,7424]{1,0:T(8,128)(2,1)S(1)} %collective-permute-done.refs_2_, ...), custom_call_target="tpu_custom_call" | custom-call | flops 956301312 | bytes 5136384 | tf_op jit(solution)/shard_map/pallas_call | solution.py:175
  23.6 1.6 %collective-permute-start.10 = (bf16[16,7424]{1,0:T(8,128)(2,1)S(1)}, bf16[16,7424]{1,0:T(8,128)(2,1)S(1)}, u32[]{:S(2)}, u32[]{:S(2)}) collective-permute-start(bf16[16,7424]{1,0:T(8,128)(2,1)S(1)} %collective-permute-done.9.refs_3_), channel_id=1, source_target_pairs={{0,1},{2,3},{4,0},{6,2},{8,4},{10,6},{12,8},{14,10},{13,12},{15,14... | collective-permute-start | bytes 712712 | tf_op jit(solution)/shard_map/rows_behind/ppermute | solution.py:297
  25.2 0.5 collective-permute-start.7
  25.7 2.3 %collective-permute-done.12.refs_1_ = bf16[16,7424]{1,0:T(8,128)(2,1)S(1)} collective-permute-done((bf16[16,7424]{1,0:T(8,128)(2,1)S(1)}, bf16[16,7424]{1,0:T(8,128)(2,1)S(1)}, u32[]{:S(2)}, u32[]{:S(2)}) %collective-permute-start.12) | collective-permute-done | bytes 237600 | tf_op jit(solution)/shard_map/rows_behind/ppermute | solution.py:297
  28.0 1.6 %collective-permute-start.14 = (bf16[16,7424]{1,0:T(8,128)(2,1)S(1)}, bf16[16,7424]{1,0:T(8,128)(2,1)S(1)}, u32[]{:S(2)}, u32[]{:S(2)}) collective-permute-start(bf16[16,7424]{1,0:T(8,128)(2,1)S(1)} %collective-permute-done.12.refs_1_), channel_id=1, source_target_pairs={{0,1},{2,3},{4,0},{6,2},{8,4},{10,6},{12,8},{14,10},{13,12},{15,14... | collective-permute-start | bytes 712712 | tf_op jit(solution)/shard_map/rows_behind/ppermute | solution.py:297
  29.6 1.2 %collective-permute-start.15 = (bf16[16,7424]{1,0:T(8,128)(2,1)S(1)}, bf16[16,7424]{1,0:T(8,128)(2,1)S(1)}, u32[]{:S(2)}, u32[]{:S(2)}) collective-permute-start(bf16[16,7424]{1,0:T(8,128)(2,1)S(1)} %collective-permute-done.13.refs_2_), channel_id=1, source_target_pairs={{0,4},{2,6},{4,8},{6,10},{8,12},{10,14},{12,13},{14,15},{13,9},{15... | collective-permute-start | bytes 712712 | tf_op jit(solution)/shard_map/rows_ahead/ppermute | solution.py:297
  30.7 2.3 %collective-permute-done.10.refs_7_ = bf16[16,7424]{1,0:T(8,128)(2,1)S(1)} collective-permute-done((bf16[16,7424]{1,0:T(8,128)(2,1)S(1)}, bf16[16,7424]{1,0:T(8,128)(2,1)S(1)}, u32[]{:S(2)}, u32[]{:S(2)}) %collective-permute-start.10) | collective-permute-done | bytes 237600 | tf_op jit(solution)/shard_map/rows_behind/ppermute | solution.py:297
  33.1 1.6 %collective-permute-start.11 = (bf16[16,7424]{1,0:T(8,128)(2,1)S(1)}, bf16[16,7424]{1,0:T(8,128)(2,1)S(1)}, u32[]{:S(2)}, u32[]{:S(2)}) collective-permute-start(bf16[16,7424]{1,0:T(8,128)(2,1)S(1)} %collective-permute-done.10.refs_7_), channel_id=1, source_target_pairs={{0,1},{2,3},{4,0},{6,2},{8,4},{10,6},{12,8},{14,10},{13,12},{15,14... | collective-permute-start | bytes 712712 | tf_op jit(solution)/shard_map/rows_behind/ppermute | solution.py:297
  34.7 1.2 %collective-permute-start.8 = (bf16[16,7424]{1,0:T(8,128)(2,1)S(1)}, bf16[16,7424]{1,0:T(8,128)(2,1)S(1)}, u32[]{:S(2)}, u32[]{:S(2)}) collective-permute-start(bf16[16,7424]{1,0:T(8,128)(2,1)S(1)} %collective-permute-done.7.refs_4_), channel_id=1, source_target_pairs={{0,4},{2,6},{4,8},{6,10},{8,12},{10,14},{12,13},{14,15},{13,9},{15... | collective-permute-start | bytes 712712 | tf_op jit(solution)/shard_map/rows_ahead/ppermute | solution.py:297
  35.8 2.3 %collective-permute-done.14.refs_5_ = bf16[16,7424]{1,0:T(8,128)(2,1)S(1)} collective-permute-done((bf16[16,7424]{1,0:T(8,128)(2,1)S(1)}, bf16[16,7424]{1,0:T(8,128)(2,1)S(1)}, u32[]{:S(2)}, u32[]{:S(2)}) %collective-permute-start.14) | collective-permute-done | bytes 237600 | tf_op jit(solution)/shard_map/rows_behind/ppermute | solution.py:297
  38.2 1.6 %collective-permute-done.15.refs_6_ = bf16[16,7424]{1,0:T(8,128)(2,1)S(1)} collective-permute-done((bf16[16,7424]{1,0:T(8,128)(2,1)S(1)}, bf16[16,7424]{1,0:T(8,128)(2,1)S(1)}, u32[]{:S(2)}, u32[]{:S(2)}) %collective-permute-start.15) | collective-permute-done | bytes 237600 | tf_op jit(solution)/shard_map/rows_ahead/ppermute | solution.py:297
  39.7 4.1 %shard_map.59 = (f32[128,128]{1,0:T(8,128)S(1)}, f32[128,128]{1,0:T(8,128)S(1)}, f32[128,128]{1,0:T(8,128)S(1)}) custom-call(s32[4]{0:T(128)S(1)} %pad_add_fusion.spot, bf16[16,7424]{1,0:T(8,128)(2,1)S(1)} %collective-permute-done.1.refs_0_, bf16[16,7424]{1,0:T(8,128)(2,1)S(1)} %collective-permute-done.12.refs_1_, ...), custom_call_target="tpu_custom_call" | custom-call | flops 956301312 | bytes 5603328 | tf_op jit(solution)/shard_map/pallas_call | solution.py:175
  43.9 0.5 collective-permute-done.8.refs_0_
  44.4 3.1 %shard_map.60 = (f32[2,256,128]{2,1,0:T(8,128)S(1)}, f32[256,128]{1,0:T(8,128)S(1)}) custom-call(s32[4]{0:T(128)S(1)} %pad_add_fusion.spot, bf16[16,7424]{1,0:T(8,128)(2,1)S(1)} %collective-permute-done.8.refs_0_, bf16[16,7424]{1,0:T(8,128)(2,1)S(1)} %collective-permute-done.11.refs_1_, f32[1,7296]{1,0:T(1,128)S(1)} %broadcast_in_dim.3.refs_6_.refs_8_.refs_2_, ...), custom_call_target="tpu_custom_call" | custom-call | flops 956301312 | bytes 4202496 | tf_op jit(solution)/shard_map/pallas_call | solution.py:175
  47.5 0.0 collective-permute-start.16
  47.6 1.5 %collective-permute-done.16.mate = f32[2,256,128]{2,1,0:T(8,128)S(1)} collective-permute-done((f32[2,256,128]{2,1,0:T(8,128)S(1)}, f32[2,256,128]{2,1,0:T(8,128)S(1)}, u32[]{:S(2)}, u32[]{:S(2)}) %collective-permute-start.16) | collective-permute-done | bytes 262176 | tf_op jit(solution)/shard_map/ppermute | solution.py:375
  49.1 0.9 %shard_map.61 = (f32[128,128]{1,0:T(8,128)S(1)}, f32[128,128]{1,0:T(8,128)S(1)}, f32[8,128]{1,0:T(8,128)S(1)}) custom-call(s32[4]{0:T(128)S(1)} %pad_add_fusion.spot, f32[2,256,128]{2,1,0:T(8,128)S(1)} %get-tuple-element.48.partial, f32[2,256,128]{2,1,0:T(8,128)S(1)} %collective-permute-done.16.mate, f32[256,128]{1,0:T(8,128)S(1)} %get-tuple-element.49.facts), custom_call_target="tpu_custom_call" | custom-call | tf_op jit(solution)/shard_map/pallas_call | solution.py:376
  50.0 1.6 %collective-permute-start.17 = (f32[8,128]{1,0:T(8,128)S(1)}, f32[8,128]{1,0:T(8,128)S(1)}, u32[]{:S(2)}, u32[]{:S(2)}) collective-permute-start(f32[8,128]{1,0:T(8,128)S(1)} %get-tuple-element.50), channel_id=1, source_target_pairs={{0,1},{1,0},{2,3},{3,2},{4,5},{5,4},{6,7},{7,6},{8,9},{9,8},{10,11... | collective-permute-start | bytes 12296 | tf_op jit(solution)/shard_map/ppermute | solution.py:388
  51.6 0.4 collective-permute-start.19
  52.0 1.6 %collective-permute-done.17 = f32[8,128]{1,0:T(8,128)S(1)} collective-permute-done((f32[8,128]{1,0:T(8,128)S(1)}, f32[8,128]{1,0:T(8,128)S(1)}, u32[]{:S(2)}, u32[]{:S(2)}) %collective-permute-start.17) | collective-permute-done | bytes 4128 | tf_op jit(solution)/shard_map/ppermute | solution.py:388
  53.7 1.2 %collective-permute-start.18 = (f32[8,128]{1,0:T(8,128)S(1)}, f32[8,128]{1,0:T(8,128)S(1)}, u32[]{:S(2)}, u32[]{:S(2)}) collective-permute-start(f32[8,128]{1,0:T(8,128)S(1)} %select_maximum_fusion.refs_0_), channel_id=1, source_target_pairs={{0,4},{2,10},{4,0},{6,14},{8,12},{10,2},{12,8},{14,6},{1,5},{3,11}... | collective-permute-start | bytes 12296 | tf_op jit(solution)/shard_map/ppermute | solution.py:406
  54.9 2.5 %collective-permute-start.21 = (f32[8,128]{1,0:T(8,128)S(1)}, f32[8,128]{1,0:T(8,128)S(1)}, u32[]{:S(2)}, u32[]{:S(2)}) collective-permute-start(f32[8,128]{1,0:T(8,128)S(1)} %select_maximum_fusion.refs_0_), channel_id=1, source_target_pairs={{0,12},{2,14},{4,8},{6,10},{8,4},{10,6},{12,0},{14,2},{1,13},{3,15... | collective-permute-start | bytes 12296 | tf_op jit(solution)/shard_map/ppermute | solution.py:407
  57.3 1.1 %shard_map.62 = (f32[128,256]{1,0:T(8,128)S(1)}, f32[128,128]{1,0:T(8,128)S(1)}, f32[8,128]{1,0:T(8,128)S(1)}) custom-call(s32[4]{0:T(128)S(1)} %pad_add_fusion.spot, f32[128,128]{1,0:T(8,128)S(1)} %get-tuple-element.51.mine, f32[128,128]{1,0:T(8,128)S(1)} %collective-permute-done.19.across, f32[256,128]{1,0:T(8,128)S(1)} %get-tuple-element.49.facts), custom_call_target="tpu_custom_call" | custom-call | tf_op jit(solution)/shard_map/pallas_call | solution.py:394
  58.4 0.1 collective-permute-start.20
  58.5 1.8 %collective-permute-done.21.refs_3_ = f32[8,128]{1,0:T(8,128)S(1)} collective-permute-done((f32[8,128]{1,0:T(8,128)S(1)}, f32[8,128]{1,0:T(8,128)S(1)}, u32[]{:S(2)}, u32[]{:S(2)}) %collective-permute-start.21) | collective-permute-done | bytes 4128 | tf_op jit(solution)/shard_map/ppermute | solution.py:407
  60.3 0.8 %shard_map.63 = f32[128,256]{1,0:T(8,128)} custom-call(f32[8,128]{1,0:T(8,128)S(1)} %select_maximum_fusion.refs_0_, f32[8,128]{1,0:T(8,128)S(1)} %collective-permute-done.18.refs_1_, f32[8,128]{1,0:T(8,128)S(1)} %collective-permute-done.20.refs_2_, f32[8,128]{1,0:T(8,128)S(1)} %collective-permute-done.21.refs_3_, f32[8,128]{1,0:T(8,128)S(1)} %get-tuple-element.56.refs_4_, ...), custom_call_target="tpu_custom_call" | custom-call | tf_op jit(solution)/shard_map/pallas_call | solution.py:415
  (15 shorter events, 0.1 us)
Async XLA Ops:
  3.1 8.6 %collective-permute-start.5 = (bf16[16,7424]{1,0:T(8,128)(2,1)S(1)}, bf16[16,7424]{1,0:T(8,128)(2,1)S(1)}, u32[]{:S(2)}, u32[]{:S(2)}) collective-permute-start(bf16[16,7424]{1,0:T(8,128)(2,1)S(1)} %get-tuple-element.37), channel_id=1, source_target_pairs={{0,3},{2,1},{4,2},{6,0},{8,6},{10,4},{12,10},{14,8},{13,14},{15,12... | collective-permute-start | bytes 712712 | tf_op jit(solution)/shard_map/rows_behind/ppermute | solution.py:297
  5.5 8.7 %collective-permute-start = (bf16[16,7424]{1,0:T(8,128)(2,1)S(1)}, bf16[16,7424]{1,0:T(8,128)(2,1)S(1)}, u32[]{:S(2)}, u32[]{:S(2)}) collective-permute-start(bf16[16,7424]{1,0:T(8,128)(2,1)S(1)} %get-tuple-element.32.refs_0_), channel_id=1, source_target_pairs={{0,4},{2,6},{4,8},{6,10},{8,12},{10,14},{12,13},{14,15},{13,9},{15... | collective-permute-start | bytes 712712 | tf_op jit(solution)/shard_map/rows_ahead/ppermute | solution.py:297
  6.2 11.5 %collective-permute-start.3 = (bf16[16,7424]{1,0:T(8,128)(2,1)S(1)}, bf16[16,7424]{1,0:T(8,128)(2,1)S(1)}, u32[]{:S(2)}, u32[]{:S(2)}) collective-permute-start(bf16[16,7424]{1,0:T(8,128)(2,1)S(1)} %get-tuple-element.32.refs_0_), channel_id=1, source_target_pairs={{0,1},{2,3},{4,0},{6,2},{8,4},{10,6},{12,8},{14,10},{13,12},{15,14... | collective-permute-start | bytes 712712 | tf_op jit(solution)/shard_map/rows_behind/ppermute | solution.py:297
  7.5 11.7 %collective-permute-start.4 = (bf16[16,7424]{1,0:T(8,128)(2,1)S(1)}, bf16[16,7424]{1,0:T(8,128)(2,1)S(1)}, u32[]{:S(2)}, u32[]{:S(2)}) collective-permute-start(bf16[16,7424]{1,0:T(8,128)(2,1)S(1)} %get-tuple-element.37), channel_id=1, source_target_pairs={{0,6},{2,4},{4,10},{6,8},{8,14},{10,12},{12,15},{14,13},{13,11},{1... | collective-permute-start | bytes 712712 | tf_op jit(solution)/shard_map/rows_ahead/ppermute | solution.py:297
  10.9 8.9 %collective-permute-start.6 = (bf16[128,7296]{1,0:T(8,128)(2,1)S(1)}, bf16[128,7296]{1,0:T(8,128)(2,1)S(1)}, u32[]{:S(2)}, u32[]{:S(2)}) collective-permute-start(bf16[128,7296]{1,0:T(8,128)(2,1)S(1)} %get-tuple-element.38), channel_id=1, source_target_pairs={{0,2},{2,0},{4,6},{6,4},{8,10},{10,8},{12,14},{14,12},{1,3},{3,1},... | collective-permute-start | bytes 5603336 | tf_op jit(solution)/shard_map/mate_panel/ppermute | solution.py:325
  11.7 4.1 %collective-permute-start.2 = (bf16[16,7424]{1,0:T(8,128)(2,1)S(1)}, bf16[16,7424]{1,0:T(8,128)(2,1)S(1)}, u32[]{:S(2)}, u32[]{:S(2)}) collective-permute-start(bf16[16,7424]{1,0:T(8,128)(2,1)S(1)} %get-tuple-element.37), channel_id=1, source_target_pairs={{0,2},{2,0},{4,6},{6,4},{8,10},{10,8},{12,14},{14,12},{1,3},{3,1},... | collective-permute-start | bytes 712712 | tf_op jit(solution)/shard_map/mate_rows/ppermute | solution.py:365
  12.9 4.2 %copy-start = (f32[7296]{0:T(1024)S(1)}, f32[7296]{0:T(1024)}, u32[]{:S(2)}) copy-start(f32[7296]{0:T(1024)} %param.8) | copy-start | bytes 87556
  14.2 9.4 %collective-permute-start.9 = (bf16[16,7424]{1,0:T(8,128)(2,1)S(1)}, bf16[16,7424]{1,0:T(8,128)(2,1)S(1)}, u32[]{:S(2)}, u32[]{:S(2)}) collective-permute-start(bf16[16,7424]{1,0:T(8,128)(2,1)S(1)} %collective-permute-done.5.refs_5_), channel_id=1, source_target_pairs={{0,1},{2,3},{4,0},{6,2},{8,4},{10,6},{12,8},{14,10},{13,12},{15,14... | collective-permute-start | bytes 712712 | tf_op jit(solution)/shard_map/rows_behind/ppermute | solution.py:297
  15.7 9.4 %collective-permute-start.1 = (bf16[16,7424]{1,0:T(8,128)(2,1)S(1)}, bf16[16,7424]{1,0:T(8,128)(2,1)S(1)}, u32[]{:S(2)}, u32[]{:S(2)}) collective-permute-start(bf16[16,7424]{1,0:T(8,128)(2,1)S(1)} %collective-permute-done.refs_2_), channel_id=1, source_target_pairs={{0,4},{2,6},{4,8},{6,10},{8,12},{10,14},{12,13},{14,15},{13,9},{15... | collective-permute-start | bytes 712712 | tf_op jit(solution)/shard_map/rows_ahead/ppermute | solution.py:297
  17.7 10.3 %collective-permute-start.12 = (bf16[16,7424]{1,0:T(8,128)(2,1)S(1)}, bf16[16,7424]{1,0:T(8,128)(2,1)S(1)}, u32[]{:S(2)}, u32[]{:S(2)}) collective-permute-start(bf16[16,7424]{1,0:T(8,128)(2,1)S(1)} %collective-permute-done.3.refs_3_), channel_id=1, source_target_pairs={{0,1},{2,3},{4,0},{6,2},{8,4},{10,6},{12,8},{14,10},{13,12},{15,14... | collective-permute-start | bytes 712712 | tf_op jit(solution)/shard_map/rows_behind/ppermute | solution.py:297
  19.3 10.3 %collective-permute-start.13 = (bf16[16,7424]{1,0:T(8,128)(2,1)S(1)}, bf16[16,7424]{1,0:T(8,128)(2,1)S(1)}, u32[]{:S(2)}, u32[]{:S(2)}) collective-permute-start(bf16[16,7424]{1,0:T(8,128)(2,1)S(1)} %collective-permute-done.4.refs_4_), channel_id=1, source_target_pairs={{0,4},{2,6},{4,8},{6,10},{8,12},{10,14},{12,13},{14,15},{13,9},{15... | collective-permute-start | bytes 712712 | tf_op jit(solution)/shard_map/rows_ahead/ppermute | solution.py:297
  23.6 9.5 %collective-permute-start.10 = (bf16[16,7424]{1,0:T(8,128)(2,1)S(1)}, bf16[16,7424]{1,0:T(8,128)(2,1)S(1)}, u32[]{:S(2)}, u32[]{:S(2)}) collective-permute-start(bf16[16,7424]{1,0:T(8,128)(2,1)S(1)} %collective-permute-done.9.refs_3_), channel_id=1, source_target_pairs={{0,1},{2,3},{4,0},{6,2},{8,4},{10,6},{12,8},{14,10},{13,12},{15,14... | collective-permute-start | bytes 712712 | tf_op jit(solution)/shard_map/rows_behind/ppermute | solution.py:297
  25.2 9.5 %collective-permute-start.7 = (bf16[16,7424]{1,0:T(8,128)(2,1)S(1)}, bf16[16,7424]{1,0:T(8,128)(2,1)S(1)}, u32[]{:S(2)}, u32[]{:S(2)}) collective-permute-start(bf16[16,7424]{1,0:T(8,128)(2,1)S(1)} %collective-permute-done.1.refs_0_), channel_id=1, source_target_pairs={{0,4},{2,6},{4,8},{6,10},{8,12},{10,14},{12,13},{14,15},{13,9},{15... | collective-permute-start | bytes 712712 | tf_op jit(solution)/shard_map/rows_ahead/ppermute | solution.py:297
  28.0 10.2 %collective-permute-start.14 = (bf16[16,7424]{1,0:T(8,128)(2,1)S(1)}, bf16[16,7424]{1,0:T(8,128)(2,1)S(1)}, u32[]{:S(2)}, u32[]{:S(2)}) collective-permute-start(bf16[16,7424]{1,0:T(8,128)(2,1)S(1)} %collective-permute-done.12.refs_1_), channel_id=1, source_target_pairs={{0,1},{2,3},{4,0},{6,2},{8,4},{10,6},{12,8},{14,10},{13,12},{15,14... | collective-permute-start | bytes 712712 | tf_op jit(solution)/shard_map/rows_behind/ppermute | solution.py:297
  29.6 10.2 %collective-permute-start.15 = (bf16[16,7424]{1,0:T(8,128)(2,1)S(1)}, bf16[16,7424]{1,0:T(8,128)(2,1)S(1)}, u32[]{:S(2)}, u32[]{:S(2)}) collective-permute-start(bf16[16,7424]{1,0:T(8,128)(2,1)S(1)} %collective-permute-done.13.refs_2_), channel_id=1, source_target_pairs={{0,4},{2,6},{4,8},{6,10},{8,12},{10,14},{12,13},{14,15},{13,9},{15... | collective-permute-start | bytes 712712 | tf_op jit(solution)/shard_map/rows_ahead/ppermute | solution.py:297
  33.1 10.8 %collective-permute-start.11 = (bf16[16,7424]{1,0:T(8,128)(2,1)S(1)}, bf16[16,7424]{1,0:T(8,128)(2,1)S(1)}, u32[]{:S(2)}, u32[]{:S(2)}) collective-permute-start(bf16[16,7424]{1,0:T(8,128)(2,1)S(1)} %collective-permute-done.10.refs_7_), channel_id=1, source_target_pairs={{0,1},{2,3},{4,0},{6,2},{8,4},{10,6},{12,8},{14,10},{13,12},{15,14... | collective-permute-start | bytes 712712 | tf_op jit(solution)/shard_map/rows_behind/ppermute | solution.py:297
  34.7 9.8 %collective-permute-start.8 = (bf16[16,7424]{1,0:T(8,128)(2,1)S(1)}, bf16[16,7424]{1,0:T(8,128)(2,1)S(1)}, u32[]{:S(2)}, u32[]{:S(2)}) collective-permute-start(bf16[16,7424]{1,0:T(8,128)(2,1)S(1)} %collective-permute-done.7.refs_4_), channel_id=1, source_target_pairs={{0,4},{2,6},{4,8},{6,10},{8,12},{10,14},{12,13},{14,15},{13,9},{15... | collective-permute-start | bytes 712712 | tf_op jit(solution)/shard_map/rows_ahead/ppermute | solution.py:297
  47.5 1.6 %collective-permute-start.16 = (f32[2,256,128]{2,1,0:T(8,128)S(1)}, f32[2,256,128]{2,1,0:T(8,128)S(1)}, u32[]{:S(2)}, u32[]{:S(2)}) collective-permute-start(f32[2,256,128]{2,1,0:T(8,128)S(1)} %get-tuple-element.48.partial), channel_id=1, source_target_pairs={{0,2},{2,0},{4,6},{6,4},{8,10},{10,8},{12,14},{14,12},{1,3},{3,1},... | collective-permute-start | bytes 786440 | tf_op jit(solution)/shard_map/ppermute | solution.py:375
  50.0 3.6 %collective-permute-start.17 = (f32[8,128]{1,0:T(8,128)S(1)}, f32[8,128]{1,0:T(8,128)S(1)}, u32[]{:S(2)}, u32[]{:S(2)}) collective-permute-start(f32[8,128]{1,0:T(8,128)S(1)} %get-tuple-element.50), channel_id=1, source_target_pairs={{0,1},{1,0},{2,3},{3,2},{4,5},{5,4},{6,7},{7,6},{8,9},{9,8},{10,11... | collective-permute-start | bytes 12296 | tf_op jit(solution)/shard_map/ppermute | solution.py:388
  51.6 5.7 %collective-permute-start.19 = (f32[128,128]{1,0:T(8,128)S(1)}, f32[128,128]{1,0:T(8,128)S(1)}, u32[]{:S(2)}, u32[]{:S(2)}) collective-permute-start(f32[128,128]{1,0:T(8,128)S(1)} %get-tuple-element.53), channel_id=1, source_target_pairs={{0,1},{1,0},{2,3},{3,2},{4,5},{5,4},{6,7},{7,6},{8,9},{9,8},{10,11... | collective-permute-start | bytes 196616 | tf_op jit(solution)/shard_map/ppermute | solution.py:390
  53.7 4.8 %collective-permute-start.18 = (f32[8,128]{1,0:T(8,128)S(1)}, f32[8,128]{1,0:T(8,128)S(1)}, u32[]{:S(2)}, u32[]{:S(2)}) collective-permute-start(f32[8,128]{1,0:T(8,128)S(1)} %select_maximum_fusion.refs_0_), channel_id=1, source_target_pairs={{0,4},{2,10},{4,0},{6,14},{8,12},{10,2},{12,8},{14,6},{1,5},{3,11}... | collective-permute-start | bytes 12296 | tf_op jit(solution)/shard_map/ppermute | solution.py:406
  54.9 5.4 %collective-permute-start.21 = (f32[8,128]{1,0:T(8,128)S(1)}, f32[8,128]{1,0:T(8,128)S(1)}, u32[]{:S(2)}, u32[]{:S(2)}) collective-permute-start(f32[8,128]{1,0:T(8,128)S(1)} %select_maximum_fusion.refs_0_), channel_id=1, source_target_pairs={{0,12},{2,14},{4,8},{6,10},{8,4},{10,6},{12,0},{14,2},{1,13},{3,15... | collective-permute-start | bytes 12296 | tf_op jit(solution)/shard_map/ppermute | solution.py:407
  58.4 1.8 %collective-permute-start.20 = (f32[8,128]{1,0:T(8,128)S(1)}, f32[8,128]{1,0:T(8,128)S(1)}, u32[]{:S(2)}, u32[]{:S(2)}) collective-permute-start(f32[8,128]{1,0:T(8,128)S(1)} %collective-permute-done.18.refs_1_), channel_id=1, source_target_pairs={{0,2},{2,0},{4,6},{6,4},{8,10},{10,8},{12,14},{14,12},{1,3},{3,1},... | collective-permute-start | bytes 12296 | tf_op jit(solution)/shard_map/ppermute | solution.py:409

commit v16 on v14

--- a/solution.py
+++ b/solution.py
@@ -391,15 +391,6 @@
     peak = jnp.maximum(stats[0], x_stats[1])
     total = stats[2] * jnp.exp(stats[0] - peak) + x_stats[3] * jnp.exp(x_stats[1] - peak)
     pair = jnp.pad(jnp.stack([peak, total]), ((0, 6), (0, 0)))
-    if chips == 4:
-        near = lax.ppermute(pair, "orient", [(d, d ^ (2 << d % 2)) for d in range(devices)])
-        far = lax.ppermute(pair, "orient", [(d, d ^ 6) for d in range(devices)])
-        parts = [pair, near, lax.ppermute(near, "orient", mate_pairs), far]
-    else:
-        parts = [pair] + [
-            lax.ppermute(pair, "orient", [(d, (d + 2 * s) % devices) for d in range(devices)])
-            for s in range(1, chips)
-        ]
     slots, chosen, tops = pl.pallas_call(
         functools.partial(slot_kernel, local_search, slots_each, per_device),
         in_specs=[smem] + [vmem] * 3,
@@ -411,6 +402,10 @@
         ],
         compiler_params=params,
     )(spot, mine, from_x, all_facts)
+    parts = [pair] + [
+        lax.ppermute(pair, "orient", [(d, d ^ (2 * s)) for d in range(devices)])
+        for s in reversed(range(1, chips))
+    ]
     posterior = pl.pallas_call(
         functools.partial(final_kernel, chips),
         in_specs=[vmem] * (chips + 3),

time: 61.3 us -> 62.2 us (1.015)
  starting transfers between devices: 24.8 us -> 25.6 us
    ppermute x3, starting transfers between devices: 3.67 us -> 4.45 us  [chip_shards(): lax.ppermute(pair, 'orient', [(d, d ^ 2 * s) for d in range(devices)])]
where the time goes in v16:
time: 62.2 us; the launch traced here: 62 us
  starting transfers between devices  25.6 us (41%)
  waiting for transfers between devices  16 us (26%)
  Pallas kernels  15.3 us (25%)
  local copies, waits for them, and re-layouts  3.52 us (6%)
  other arithmetic  1.45 us (2%)
    ppermute x14, starting transfers between devices, forward(): return lax.ppermute(values, ('orient', 'cls'), pairs)  17.1 us
    pallas_call x3, Pallas kernels, score_call(): pl.pallas_call(kernel, in_specs=[pl.BlockSpec(memory_space=pltpu.SMEM)] +...  11 us
    ppermute x14, waiting for transfers between devices, forward(): return lax.ppermute(values, ('orient', 'cls'), pairs)  10.9 us
    ppermute x3, starting transfers between devices, chip_shards(): lax.ppermute(pair, 'orient', [(d, d ^ 2 * s) for d in range(devices)])  4.45 us
    optimization_barrier x1, local copies, waits for them, and re-layouts, chip_shards(): _, panels = lax.optimization_barrier((kept, panels))  2.42 us
    ppermute x3, waiting for transfers between devices, chip_shards(): lax.ppermute(pair, 'orient', [(d, d ^ 2 * s) for d in range(devices)])  2 us
    ppermute x1, starting transfers between devices, chip_shards(): x_stats = lax.ppermute(stats, 'cls', x_pairs)  1.62 us
    ppermute x1, waiting for transfers between devices, chip_shards(): x_stats = lax.ppermute(stats, 'cls', x_pairs)  1.58 us
  transfers between devices with their start and end apart: 22, of which 10 were waited for; matrix products, arithmetic and copies ran while one was open for 4% of the time, Pallas kernels for 16%

profile of v16, /device:TPU:0, one launch (start us, length us, event | category | flops | bytes accessed | tf_op | source)
XLA Modules:
  0.0 62.0 jit_solution(1351340963598669842)
XLA Ops:
  0.0 1.1 %copy.11 = bf16[1,16,2,7296]{3,1,2,0:T(8,128)(2,1)S(1)} copy(bf16[1,16,2,7296]{3,2,1,0:T(2,128)(2,1)} %param.5) | data formatting | bytes 933888 | tf_op args[0]
  1.1 0.7 %convert_bitcast_fusion = bf16[4,16]{1,0:T(4,128)(2,1)S(1)} fusion(s32[1,16,4]{1,2,0:T(4,128)} %param.7), kind=kLoop, calls=%fused_computation.12 | loop fusion | flops 64 | bytes 384 | tf_op jit(solution)/shard_map/convert_element_type | solution.py:303
  1.8 0.7 %fusion.5.facts = bf16[16,128]{1,0:T(8,128)(2,1)S(1)} fusion(bf16[4,16]{1,0:T(4,128)(2,1)S(1)} %convert_bitcast_fusion, bf16[1,16]{1,0:T(2,128)(2,1)} %param.6), kind=kLoop, calls=%fused_computation.9 | loop fusion | flops 22528 | bytes 4256 | tf_op jit(solution)/shard_map/concatenate | solution.py:303
  2.4 0.1 pad_add_fusion.spot
  2.5 0.6 shard_map.55
  3.1 2.4 %collective-permute-start.5 = (bf16[16,7424]{1,0:T(8,128)(2,1)S(1)}, bf16[16,7424]{1,0:T(8,128)(2,1)S(1)}, u32[]{:S(2)}, u32[]{:S(2)}) collective-permute-start(bf16[16,7424]{1,0:T(8,128)(2,1)S(1)} %get-tuple-element.35), channel_id=1, source_target_pairs={{0,3},{2,1},{4,2},{6,0},{8,6},{10,4},{12,10},{14,8},{13,14},{15,12... | collective-permute-start | bytes 712712 | tf_op jit(solution)/shard_map/rows_behind/ppermute | solution.py:297
  5.5 0.7 %collective-permute-start = (bf16[16,7424]{1,0:T(8,128)(2,1)S(1)}, bf16[16,7424]{1,0:T(8,128)(2,1)S(1)}, u32[]{:S(2)}, u32[]{:S(2)}) collective-permute-start(bf16[16,7424]{1,0:T(8,128)(2,1)S(1)} %get-tuple-element.30.refs_0_), channel_id=1, source_target_pairs={{0,4},{2,6},{4,8},{6,10},{8,12},{10,14},{12,13},{14,15},{13,9},{15... | collective-permute-start | bytes 712712 | tf_op jit(solution)/shard_map/rows_ahead/ppermute | solution.py:297
  6.2 1.3 %collective-permute-start.3 = (bf16[16,7424]{1,0:T(8,128)(2,1)S(1)}, bf16[16,7424]{1,0:T(8,128)(2,1)S(1)}, u32[]{:S(2)}, u32[]{:S(2)}) collective-permute-start(bf16[16,7424]{1,0:T(8,128)(2,1)S(1)} %get-tuple-element.30.refs_0_), channel_id=1, source_target_pairs={{0,1},{2,3},{4,0},{6,2},{8,4},{10,6},{12,8},{14,10},{13,12},{15,14... | collective-permute-start | bytes 712712 | tf_op jit(solution)/shard_map/rows_behind/ppermute | solution.py:297
  7.5 0.1 collective-permute-start.4
  7.6 2.4 %copy.10 = bf16[1,1,128,2,7296]{4,2,3,1,0:T(8,128)(2,1)S(1)} copy(bf16[1,1,128,2,7296]{4,3,2,1,0:T(2,128)(2,1)} %param.9) | data formatting | bytes 7471104 | tf_op jit(solution)/shard_map/optimization_barrier | solution.py:314
  10.1 0.8 %shard_map.56 = (bf16[128,7296]{1,0:T(8,128)(2,1)S(1)}, bf16[128,7296]{1,0:T(8,128)(2,1)S(1)}) custom-call(s32[4]{0:T(128)S(1)} %pad_add_fusion.spot, bf16[2,128,7296]{2,1,0:T(8,128)(2,1)S(1)} %bitcast.19), custom_call_target="tpu_custom_call" | custom-call | tf_op jit(solution)/shard_map/pallas_call | solution.py:317
  10.9 0.8 %collective-permute-start.6 = (bf16[128,7296]{1,0:T(8,128)(2,1)S(1)}, bf16[128,7296]{1,0:T(8,128)(2,1)S(1)}, u32[]{:S(2)}, u32[]{:S(2)}) collective-permute-start(bf16[128,7296]{1,0:T(8,128)(2,1)S(1)} %get-tuple-element.36), channel_id=1, source_target_pairs={{0,2},{2,0},{4,6},{6,4},{8,10},{10,8},{12,14},{14,12},{1,3},{3,1},... | collective-permute-start | bytes 5603336 | tf_op jit(solution)/shard_map/mate_panel/ppermute | solution.py:325
  11.7 0.0 collective-permute-done.5.refs_5_
  11.7 1.2 %collective-permute-start.2 = (bf16[16,7424]{1,0:T(8,128)(2,1)S(1)}, bf16[16,7424]{1,0:T(8,128)(2,1)S(1)}, u32[]{:S(2)}, u32[]{:S(2)}) collective-permute-start(bf16[16,7424]{1,0:T(8,128)(2,1)S(1)} %get-tuple-element.35), channel_id=1, source_target_pairs={{0,2},{2,0},{4,6},{6,4},{8,10},{10,8},{12,14},{14,12},{1,3},{3,1},... | collective-permute-start | bytes 712712 | tf_op jit(solution)/shard_map/mate_rows/ppermute | solution.py:365
  12.9 0.1 shard_map.57.refs_8_.refs_10_.refs_4_
  13.0 1.2 %collective-permute-done.refs_2_ = bf16[16,7424]{1,0:T(8,128)(2,1)S(1)} collective-permute-done((bf16[16,7424]{1,0:T(8,128)(2,1)S(1)}, bf16[16,7424]{1,0:T(8,128)(2,1)S(1)}, u32[]{:S(2)}, u32[]{:S(2)}) %collective-permute-start) | collective-permute-done | bytes 237600 | tf_op jit(solution)/shard_map/rows_ahead/ppermute | solution.py:297
  14.2 1.6 %collective-permute-start.9 = (bf16[16,7424]{1,0:T(8,128)(2,1)S(1)}, bf16[16,7424]{1,0:T(8,128)(2,1)S(1)}, u32[]{:S(2)}, u32[]{:S(2)}) collective-permute-start(bf16[16,7424]{1,0:T(8,128)(2,1)S(1)} %collective-permute-done.5.refs_5_), channel_id=1, source_target_pairs={{0,1},{2,3},{4,0},{6,2},{8,4},{10,6},{12,8},{14,10},{13,12},{15,14... | collective-permute-start | bytes 712712 | tf_op jit(solution)/shard_map/rows_behind/ppermute | solution.py:297
  15.7 1.3 %collective-permute-start.1 = (bf16[16,7424]{1,0:T(8,128)(2,1)S(1)}, bf16[16,7424]{1,0:T(8,128)(2,1)S(1)}, u32[]{:S(2)}, u32[]{:S(2)}) collective-permute-start(bf16[16,7424]{1,0:T(8,128)(2,1)S(1)} %collective-permute-done.refs_2_), channel_id=1, source_target_pairs={{0,4},{2,6},{4,8},{6,10},{8,12},{10,14},{12,13},{14,15},{13,9},{15... | collective-permute-start | bytes 712712 | tf_op jit(solution)/shard_map/rows_ahead/ppermute | solution.py:297
  17.1 0.6 %collective-permute-done.3.refs_3_ = bf16[16,7424]{1,0:T(8,128)(2,1)S(1)} collective-permute-done((bf16[16,7424]{1,0:T(8,128)(2,1)S(1)}, bf16[16,7424]{1,0:T(8,128)(2,1)S(1)}, u32[]{:S(2)}, u32[]{:S(2)}) %collective-permute-start.3) | collective-permute-done | bytes 237600 | tf_op jit(solution)/shard_map/rows_behind/ppermute | solution.py:297
  17.7 1.6 %collective-permute-start.12 = (bf16[16,7424]{1,0:T(8,128)(2,1)S(1)}, bf16[16,7424]{1,0:T(8,128)(2,1)S(1)}, u32[]{:S(2)}, u32[]{:S(2)}) collective-permute-start(bf16[16,7424]{1,0:T(8,128)(2,1)S(1)} %collective-permute-done.3.refs_3_), channel_id=1, source_target_pairs={{0,1},{2,3},{4,0},{6,2},{8,4},{10,6},{12,8},{14,10},{13,12},{15,14... | collective-permute-start | bytes 712712 | tf_op jit(solution)/shard_map/rows_behind/ppermute | solution.py:297
  19.3 0.0 collective-permute-done.4.refs_4_
  19.3 0.5 collective-permute-start.13
  19.7 3.8 %shard_map.58 = (f32[96,128]{1,0:T(8,128)S(1)}, f32[96,128]{1,0:T(8,128)S(1)}, f32[96,128]{1,0:T(8,128)S(1)}) custom-call(s32[4]{0:T(128)S(1)} %pad_add_fusion.spot, bf16[16,7424]{1,0:T(8,128)(2,1)S(1)} %get-tuple-element.30.refs_0_, bf16[16,7424]{1,0:T(8,128)(2,1)S(1)} %collective-permute-done.2.refs_1_, bf16[16,7424]{1,0:T(8,128)(2,1)S(1)} %collective-permute-done.refs_2_, ...), custom_call_target="tpu_custom_call" | custom-call | flops 956301312 | bytes 5136384 | tf_op jit(solution)/shard_map/pallas_call | solution.py:175
  23.6 0.0 collective-permute-done.9.refs_3_
  23.6 1.6 %collective-permute-start.10 = (bf16[16,7424]{1,0:T(8,128)(2,1)S(1)}, bf16[16,7424]{1,0:T(8,128)(2,1)S(1)}, u32[]{:S(2)}, u32[]{:S(2)}) collective-permute-start(bf16[16,7424]{1,0:T(8,128)(2,1)S(1)} %collective-permute-done.9.refs_3_), channel_id=1, source_target_pairs={{0,1},{2,3},{4,0},{6,2},{8,4},{10,6},{12,8},{14,10},{13,12},{15,14... | collective-permute-start | bytes 712712 | tf_op jit(solution)/shard_map/rows_behind/ppermute | solution.py:297
  25.2 0.5 collective-permute-start.7
  25.7 2.3 %collective-permute-done.12.refs_1_ = bf16[16,7424]{1,0:T(8,128)(2,1)S(1)} collective-permute-done((bf16[16,7424]{1,0:T(8,128)(2,1)S(1)}, bf16[16,7424]{1,0:T(8,128)(2,1)S(1)}, u32[]{:S(2)}, u32[]{:S(2)}) %collective-permute-start.12) | collective-permute-done | bytes 237600 | tf_op jit(solution)/shard_map/rows_behind/ppermute | solution.py:297
  28.0 1.6 %collective-permute-start.14 = (bf16[16,7424]{1,0:T(8,128)(2,1)S(1)}, bf16[16,7424]{1,0:T(8,128)(2,1)S(1)}, u32[]{:S(2)}, u32[]{:S(2)}) collective-permute-start(bf16[16,7424]{1,0:T(8,128)(2,1)S(1)} %collective-permute-done.12.refs_1_), channel_id=1, source_target_pairs={{0,1},{2,3},{4,0},{6,2},{8,4},{10,6},{12,8},{14,10},{13,12},{15,14... | collective-permute-start | bytes 712712 | tf_op jit(solution)/shard_map/rows_behind/ppermute | solution.py:297
  29.6 1.2 %collective-permute-start.15 = (bf16[16,7424]{1,0:T(8,128)(2,1)S(1)}, bf16[16,7424]{1,0:T(8,128)(2,1)S(1)}, u32[]{:S(2)}, u32[]{:S(2)}) collective-permute-start(bf16[16,7424]{1,0:T(8,128)(2,1)S(1)} %collective-permute-done.13.refs_2_), channel_id=1, source_target_pairs={{0,4},{2,6},{4,8},{6,10},{8,12},{10,14},{12,13},{14,15},{13,9},{15... | collective-permute-start | bytes 712712 | tf_op jit(solution)/shard_map/rows_ahead/ppermute | solution.py:297
  30.7 2.3 %collective-permute-done.10.refs_7_ = bf16[16,7424]{1,0:T(8,128)(2,1)S(1)} collective-permute-done((bf16[16,7424]{1,0:T(8,128)(2,1)S(1)}, bf16[16,7424]{1,0:T(8,128)(2,1)S(1)}, u32[]{:S(2)}, u32[]{:S(2)}) %collective-permute-start.10) | collective-permute-done | bytes 237600 | tf_op jit(solution)/shard_map/rows_behind/ppermute | solution.py:297
  33.1 1.6 %collective-permute-start.11 = (bf16[16,7424]{1,0:T(8,128)(2,1)S(1)}, bf16[16,7424]{1,0:T(8,128)(2,1)S(1)}, u32[]{:S(2)}, u32[]{:S(2)}) collective-permute-start(bf16[16,7424]{1,0:T(8,128)(2,1)S(1)} %collective-permute-done.10.refs_7_), channel_id=1, source_target_pairs={{0,1},{2,3},{4,0},{6,2},{8,4},{10,6},{12,8},{14,10},{13,12},{15,14... | collective-permute-start | bytes 712712 | tf_op jit(solution)/shard_map/rows_behind/ppermute | solution.py:297
  34.7 1.2 %collective-permute-start.8 = (bf16[16,7424]{1,0:T(8,128)(2,1)S(1)}, bf16[16,7424]{1,0:T(8,128)(2,1)S(1)}, u32[]{:S(2)}, u32[]{:S(2)}) collective-permute-start(bf16[16,7424]{1,0:T(8,128)(2,1)S(1)} %collective-permute-done.7.refs_4_), channel_id=1, source_target_pairs={{0,4},{2,6},{4,8},{6,10},{8,12},{10,14},{12,13},{14,15},{13,9},{15... | collective-permute-start | bytes 712712 | tf_op jit(solution)/shard_map/rows_ahead/ppermute | solution.py:297
  35.8 2.3 %collective-permute-done.14.refs_5_ = bf16[16,7424]{1,0:T(8,128)(2,1)S(1)} collective-permute-done((bf16[16,7424]{1,0:T(8,128)(2,1)S(1)}, bf16[16,7424]{1,0:T(8,128)(2,1)S(1)}, u32[]{:S(2)}, u32[]{:S(2)}) %collective-permute-start.14) | collective-permute-done | bytes 237600 | tf_op jit(solution)/shard_map/rows_behind/ppermute | solution.py:297
  38.2 1.6 %collective-permute-done.15.refs_6_ = bf16[16,7424]{1,0:T(8,128)(2,1)S(1)} collective-permute-done((bf16[16,7424]{1,0:T(8,128)(2,1)S(1)}, bf16[16,7424]{1,0:T(8,128)(2,1)S(1)}, u32[]{:S(2)}, u32[]{:S(2)}) %collective-permute-start.15) | collective-permute-done | bytes 237600 | tf_op jit(solution)/shard_map/rows_ahead/ppermute | solution.py:297
  39.7 4.1 %shard_map.59 = (f32[128,128]{1,0:T(8,128)S(1)}, f32[128,128]{1,0:T(8,128)S(1)}, f32[128,128]{1,0:T(8,128)S(1)}) custom-call(s32[4]{0:T(128)S(1)} %pad_add_fusion.spot, bf16[16,7424]{1,0:T(8,128)(2,1)S(1)} %collective-permute-done.1.refs_0_, bf16[16,7424]{1,0:T(8,128)(2,1)S(1)} %collective-permute-done.12.refs_1_, ...), custom_call_target="tpu_custom_call" | custom-call | flops 956301312 | bytes 5603328 | tf_op jit(solution)/shard_map/pallas_call | solution.py:175
  43.9 0.5 collective-permute-done.8.refs_0_
  44.4 3.1 %shard_map.60 = (f32[2,256,128]{2,1,0:T(8,128)S(1)}, f32[256,128]{1,0:T(8,128)S(1)}) custom-call(s32[4]{0:T(128)S(1)} %pad_add_fusion.spot, bf16[16,7424]{1,0:T(8,128)(2,1)S(1)} %collective-permute-done.8.refs_0_, bf16[16,7424]{1,0:T(8,128)(2,1)S(1)} %collective-permute-done.11.refs_1_, f32[1,7296]{1,0:T(1,128)S(1)} %broadcast_in_dim.3.refs_6_.refs_8_.refs_2_, ...), custom_call_target="tpu_custom_call" | custom-call | flops 956301312 | bytes 4202496 | tf_op jit(solution)/shard_map/pallas_call | solution.py:175
  47.5 0.0 collective-permute-start.16
  47.6 1.5 %collective-permute-done.16.mate = f32[2,256,128]{2,1,0:T(8,128)S(1)} collective-permute-done((f32[2,256,128]{2,1,0:T(8,128)S(1)}, f32[2,256,128]{2,1,0:T(8,128)S(1)}, u32[]{:S(2)}, u32[]{:S(2)}) %collective-permute-start.16) | collective-permute-done | bytes 262176 | tf_op jit(solution)/shard_map/ppermute | solution.py:375
  49.1 0.9 %shard_map.61 = (f32[128,128]{1,0:T(8,128)S(1)}, f32[128,128]{1,0:T(8,128)S(1)}, f32[8,128]{1,0:T(8,128)S(1)}) custom-call(s32[4]{0:T(128)S(1)} %pad_add_fusion.spot, f32[2,256,128]{2,1,0:T(8,128)S(1)} %get-tuple-element.46.partial, f32[2,256,128]{2,1,0:T(8,128)S(1)} %collective-permute-done.16.mate, f32[256,128]{1,0:T(8,128)S(1)} %get-tuple-element.47.facts), custom_call_target="tpu_custom_call" | custom-call | tf_op jit(solution)/shard_map/pallas_call | solution.py:376
  50.0 1.6 %collective-permute-start.17 = (f32[8,128]{1,0:T(8,128)S(1)}, f32[8,128]{1,0:T(8,128)S(1)}, u32[]{:S(2)}, u32[]{:S(2)}) collective-permute-start(f32[8,128]{1,0:T(8,128)S(1)} %get-tuple-element.48), channel_id=1, source_target_pairs={{0,1},{1,0},{2,3},{3,2},{4,5},{5,4},{6,7},{7,6},{8,9},{9,8},{10,11... | collective-permute-start | bytes 12296 | tf_op jit(solution)/shard_map/ppermute | solution.py:388
  51.6 0.4 collective-permute-start.21
  52.0 1.6 %collective-permute-done.17 = f32[8,128]{1,0:T(8,128)S(1)} collective-permute-done((f32[8,128]{1,0:T(8,128)S(1)}, f32[8,128]{1,0:T(8,128)S(1)}, u32[]{:S(2)}, u32[]{:S(2)}) %collective-permute-start.17) | collective-permute-done | bytes 4128 | tf_op jit(solution)/shard_map/ppermute | solution.py:388
  53.7 3.0 %collective-permute-start.18 = (f32[8,128]{1,0:T(8,128)S(1)}, f32[8,128]{1,0:T(8,128)S(1)}, u32[]{:S(2)}, u32[]{:S(2)}) collective-permute-start(f32[8,128]{1,0:T(8,128)S(1)} %select_maximum_fusion.refs_0_), channel_id=1, source_target_pairs={{0,12},{2,14},{4,8},{6,10},{8,4},{10,6},{12,0},{14,2},{1,13},{3,15... | collective-permute-start | bytes 12296 | tf_op jit(solution)/shard_map/ppermute | solution.py:406
  56.7 1.4 %collective-permute-start.20 = (f32[8,128]{1,0:T(8,128)S(1)}, f32[8,128]{1,0:T(8,128)S(1)}, u32[]{:S(2)}, u32[]{:S(2)}) collective-permute-start(f32[8,128]{1,0:T(8,128)S(1)} %select_maximum_fusion.refs_0_), channel_id=1, source_target_pairs={{0,4},{2,6},{4,0},{6,2},{8,12},{10,14},{12,8},{14,10},{1,5},{3,7},... | collective-permute-start | bytes 12296 | tf_op jit(solution)/shard_map/ppermute | solution.py:406
  58.1 1.1 %shard_map.62 = (f32[128,256]{1,0:T(8,128)S(1)}, f32[128,128]{1,0:T(8,128)S(1)}, f32[8,128]{1,0:T(8,128)S(1)}) custom-call(s32[4]{0:T(128)S(1)} %pad_add_fusion.spot, f32[128,128]{1,0:T(8,128)S(1)} %get-tuple-element.49.mine, f32[128,128]{1,0:T(8,128)S(1)} %collective-permute-done.21.across, f32[256,128]{1,0:T(8,128)S(1)} %get-tuple-element.47.facts), custom_call_target="tpu_custom_call" | custom-call | tf_op jit(solution)/shard_map/pallas_call | solution.py:394
  59.2 2.0 %collective-permute-done.19.refs_2_ = f32[8,128]{1,0:T(8,128)S(1)} collective-permute-done((f32[8,128]{1,0:T(8,128)S(1)}, f32[8,128]{1,0:T(8,128)S(1)}, u32[]{:S(2)}, u32[]{:S(2)}) %collective-permute-start.19) | collective-permute-done | bytes 4128 | tf_op jit(solution)/shard_map/ppermute | solution.py:406
  61.2 0.8 %shard_map.63 = f32[128,256]{1,0:T(8,128)} custom-call(f32[8,128]{1,0:T(8,128)S(1)} %select_maximum_fusion.refs_0_, f32[8,128]{1,0:T(8,128)S(1)} %collective-permute-done.18.refs_1_, f32[8,128]{1,0:T(8,128)S(1)} %collective-permute-done.19.refs_2_, f32[8,128]{1,0:T(8,128)S(1)} %collective-permute-done.20.refs_3_, f32[8,128]{1,0:T(8,128)S(1)} %get-tuple-element.52.refs_4_, ...), custom_call_target="tpu_custom_call" | custom-call | tf_op jit(solution)/shard_map/pallas_call | solution.py:409
  (15 shorter events, 0.1 us)
Async XLA Ops:
  3.1 8.6 %collective-permute-start.5 = (bf16[16,7424]{1,0:T(8,128)(2,1)S(1)}, bf16[16,7424]{1,0:T(8,128)(2,1)S(1)}, u32[]{:S(2)}, u32[]{:S(2)}) collective-permute-start(bf16[16,7424]{1,0:T(8,128)(2,1)S(1)} %get-tuple-element.35), channel_id=1, source_target_pairs={{0,3},{2,1},{4,2},{6,0},{8,6},{10,4},{12,10},{14,8},{13,14},{15,12... | collective-permute-start | bytes 712712 | tf_op jit(solution)/shard_map/rows_behind/ppermute | solution.py:297
  5.5 8.7 %collective-permute-start = (bf16[16,7424]{1,0:T(8,128)(2,1)S(1)}, bf16[16,7424]{1,0:T(8,128)(2,1)S(1)}, u32[]{:S(2)}, u32[]{:S(2)}) collective-permute-start(bf16[16,7424]{1,0:T(8,128)(2,1)S(1)} %get-tuple-element.30.refs_0_), channel_id=1, source_target_pairs={{0,4},{2,6},{4,8},{6,10},{8,12},{10,14},{12,13},{14,15},{13,9},{15... | collective-permute-start | bytes 712712 | tf_op jit(solution)/shard_map/rows_ahead/ppermute | solution.py:297
  6.2 11.5 %collective-permute-start.3 = (bf16[16,7424]{1,0:T(8,128)(2,1)S(1)}, bf16[16,7424]{1,0:T(8,128)(2,1)S(1)}, u32[]{:S(2)}, u32[]{:S(2)}) collective-permute-start(bf16[16,7424]{1,0:T(8,128)(2,1)S(1)} %get-tuple-element.30.refs_0_), channel_id=1, source_target_pairs={{0,1},{2,3},{4,0},{6,2},{8,4},{10,6},{12,8},{14,10},{13,12},{15,14... | collective-permute-start | bytes 712712 | tf_op jit(solution)/shard_map/rows_behind/ppermute | solution.py:297
  7.5 11.7 %collective-permute-start.4 = (bf16[16,7424]{1,0:T(8,128)(2,1)S(1)}, bf16[16,7424]{1,0:T(8,128)(2,1)S(1)}, u32[]{:S(2)}, u32[]{:S(2)}) collective-permute-start(bf16[16,7424]{1,0:T(8,128)(2,1)S(1)} %get-tuple-element.35), channel_id=1, source_target_pairs={{0,6},{2,4},{4,10},{6,8},{8,14},{10,12},{12,15},{14,13},{13,11},{1... | collective-permute-start | bytes 712712 | tf_op jit(solution)/shard_map/rows_ahead/ppermute | solution.py:297
  10.9 8.9 %collective-permute-start.6 = (bf16[128,7296]{1,0:T(8,128)(2,1)S(1)}, bf16[128,7296]{1,0:T(8,128)(2,1)S(1)}, u32[]{:S(2)}, u32[]{:S(2)}) collective-permute-start(bf16[128,7296]{1,0:T(8,128)(2,1)S(1)} %get-tuple-element.36), channel_id=1, source_target_pairs={{0,2},{2,0},{4,6},{6,4},{8,10},{10,8},{12,14},{14,12},{1,3},{3,1},... | collective-permute-start | bytes 5603336 | tf_op jit(solution)/shard_map/mate_panel/ppermute | solution.py:325
  11.7 4.1 %collective-permute-start.2 = (bf16[16,7424]{1,0:T(8,128)(2,1)S(1)}, bf16[16,7424]{1,0:T(8,128)(2,1)S(1)}, u32[]{:S(2)}, u32[]{:S(2)}) collective-permute-start(bf16[16,7424]{1,0:T(8,128)(2,1)S(1)} %get-tuple-element.35), channel_id=1, source_target_pairs={{0,2},{2,0},{4,6},{6,4},{8,10},{10,8},{12,14},{14,12},{1,3},{3,1},... | collective-permute-start | bytes 712712 | tf_op jit(solution)/shard_map/mate_rows/ppermute | solution.py:365
  12.9 4.2 %copy-start = (f32[7296]{0:T(1024)S(1)}, f32[7296]{0:T(1024)}, u32[]{:S(2)}) copy-start(f32[7296]{0:T(1024)} %param.8) | copy-start | bytes 87556
  14.2 9.4 %collective-permute-start.9 = (bf16[16,7424]{1,0:T(8,128)(2,1)S(1)}, bf16[16,7424]{1,0:T(8,128)(2,1)S(1)}, u32[]{:S(2)}, u32[]{:S(2)}) collective-permute-start(bf16[16,7424]{1,0:T(8,128)(2,1)S(1)} %collective-permute-done.5.refs_5_), channel_id=1, source_target_pairs={{0,1},{2,3},{4,0},{6,2},{8,4},{10,6},{12,8},{14,10},{13,12},{15,14... | collective-permute-start | bytes 712712 | tf_op jit(solution)/shard_map/rows_behind/ppermute | solution.py:297
  15.7 9.4 %collective-permute-start.1 = (bf16[16,7424]{1,0:T(8,128)(2,1)S(1)}, bf16[16,7424]{1,0:T(8,128)(2,1)S(1)}, u32[]{:S(2)}, u32[]{:S(2)}) collective-permute-start(bf16[16,7424]{1,0:T(8,128)(2,1)S(1)} %collective-permute-done.refs_2_), channel_id=1, source_target_pairs={{0,4},{2,6},{4,8},{6,10},{8,12},{10,14},{12,13},{14,15},{13,9},{15... | collective-permute-start | bytes 712712 | tf_op jit(solution)/shard_map/rows_ahead/ppermute | solution.py:297
  17.7 10.3 %collective-permute-start.12 = (bf16[16,7424]{1,0:T(8,128)(2,1)S(1)}, bf16[16,7424]{1,0:T(8,128)(2,1)S(1)}, u32[]{:S(2)}, u32[]{:S(2)}) collective-permute-start(bf16[16,7424]{1,0:T(8,128)(2,1)S(1)} %collective-permute-done.3.refs_3_), channel_id=1, source_target_pairs={{0,1},{2,3},{4,0},{6,2},{8,4},{10,6},{12,8},{14,10},{13,12},{15,14... | collective-permute-start | bytes 712712 | tf_op jit(solution)/shard_map/rows_behind/ppermute | solution.py:297
  19.3 10.3 %collective-permute-start.13 = (bf16[16,7424]{1,0:T(8,128)(2,1)S(1)}, bf16[16,7424]{1,0:T(8,128)(2,1)S(1)}, u32[]{:S(2)}, u32[]{:S(2)}) collective-permute-start(bf16[16,7424]{1,0:T(8,128)(2,1)S(1)} %collective-permute-done.4.refs_4_), channel_id=1, source_target_pairs={{0,4},{2,6},{4,8},{6,10},{8,12},{10,14},{12,13},{14,15},{13,9},{15... | collective-permute-start | bytes 712712 | tf_op jit(solution)/shard_map/rows_ahead/ppermute | solution.py:297
  23.6 9.5 %collective-permute-start.10 = (bf16[16,7424]{1,0:T(8,128)(2,1)S(1)}, bf16[16,7424]{1,0:T(8,128)(2,1)S(1)}, u32[]{:S(2)}, u32[]{:S(2)}) collective-permute-start(bf16[16,7424]{1,0:T(8,128)(2,1)S(1)} %collective-permute-done.9.refs_3_), channel_id=1, source_target_pairs={{0,1},{2,3},{4,0},{6,2},{8,4},{10,6},{12,8},{14,10},{13,12},{15,14... | collective-permute-start | bytes 712712 | tf_op jit(solution)/shard_map/rows_behind/ppermute | solution.py:297
  25.2 9.5 %collective-permute-start.7 = (bf16[16,7424]{1,0:T(8,128)(2,1)S(1)}, bf16[16,7424]{1,0:T(8,128)(2,1)S(1)}, u32[]{:S(2)}, u32[]{:S(2)}) collective-permute-start(bf16[16,7424]{1,0:T(8,128)(2,1)S(1)} %collective-permute-done.1.refs_0_), channel_id=1, source_target_pairs={{0,4},{2,6},{4,8},{6,10},{8,12},{10,14},{12,13},{14,15},{13,9},{15... | collective-permute-start | bytes 712712 | tf_op jit(solution)/shard_map/rows_ahead/ppermute | solution.py:297
  28.0 10.2 %collective-permute-start.14 = (bf16[16,7424]{1,0:T(8,128)(2,1)S(1)}, bf16[16,7424]{1,0:T(8,128)(2,1)S(1)}, u32[]{:S(2)}, u32[]{:S(2)}) collective-permute-start(bf16[16,7424]{1,0:T(8,128)(2,1)S(1)} %collective-permute-done.12.refs_1_), channel_id=1, source_target_pairs={{0,1},{2,3},{4,0},{6,2},{8,4},{10,6},{12,8},{14,10},{13,12},{15,14... | collective-permute-start | bytes 712712 | tf_op jit(solution)/shard_map/rows_behind/ppermute | solution.py:297
  29.6 10.2 %collective-permute-start.15 = (bf16[16,7424]{1,0:T(8,128)(2,1)S(1)}, bf16[16,7424]{1,0:T(8,128)(2,1)S(1)}, u32[]{:S(2)}, u32[]{:S(2)}) collective-permute-start(bf16[16,7424]{1,0:T(8,128)(2,1)S(1)} %collective-permute-done.13.refs_2_), channel_id=1, source_target_pairs={{0,4},{2,6},{4,8},{6,10},{8,12},{10,14},{12,13},{14,15},{13,9},{15... | collective-permute-start | bytes 712712 | tf_op jit(solution)/shard_map/rows_ahead/ppermute | solution.py:297
  33.1 10.8 %collective-permute-start.11 = (bf16[16,7424]{1,0:T(8,128)(2,1)S(1)}, bf16[16,7424]{1,0:T(8,128)(2,1)S(1)}, u32[]{:S(2)}, u32[]{:S(2)}) collective-permute-start(bf16[16,7424]{1,0:T(8,128)(2,1)S(1)} %collective-permute-done.10.refs_7_), channel_id=1, source_target_pairs={{0,1},{2,3},{4,0},{6,2},{8,4},{10,6},{12,8},{14,10},{13,12},{15,14... | collective-permute-start | bytes 712712 | tf_op jit(solution)/shard_map/rows_behind/ppermute | solution.py:297
  34.7 9.8 %collective-permute-start.8 = (bf16[16,7424]{1,0:T(8,128)(2,1)S(1)}, bf16[16,7424]{1,0:T(8,128)(2,1)S(1)}, u32[]{:S(2)}, u32[]{:S(2)}) collective-permute-start(bf16[16,7424]{1,0:T(8,128)(2,1)S(1)} %collective-permute-done.7.refs_4_), channel_id=1, source_target_pairs={{0,4},{2,6},{4,8},{6,10},{8,12},{10,14},{12,13},{14,15},{13,9},{15... | collective-permute-start | bytes 712712 | tf_op jit(solution)/shard_map/rows_ahead/ppermute | solution.py:297
  47.5 1.6 %collective-permute-start.16 = (f32[2,256,128]{2,1,0:T(8,128)S(1)}, f32[2,256,128]{2,1,0:T(8,128)S(1)}, u32[]{:S(2)}, u32[]{:S(2)}) collective-permute-start(f32[2,256,128]{2,1,0:T(8,128)S(1)} %get-tuple-element.46.partial), channel_id=1, source_target_pairs={{0,2},{2,0},{4,6},{6,4},{8,10},{10,8},{12,14},{14,12},{1,3},{3,1},... | collective-permute-start | bytes 786440 | tf_op jit(solution)/shard_map/ppermute | solution.py:375
  50.0 3.6 %collective-permute-start.17 = (f32[8,128]{1,0:T(8,128)S(1)}, f32[8,128]{1,0:T(8,128)S(1)}, u32[]{:S(2)}, u32[]{:S(2)}) collective-permute-start(f32[8,128]{1,0:T(8,128)S(1)} %get-tuple-element.48), channel_id=1, source_target_pairs={{0,1},{1,0},{2,3},{3,2},{4,5},{5,4},{6,7},{7,6},{8,9},{9,8},{10,11... | collective-permute-start | bytes 12296 | tf_op jit(solution)/shard_map/ppermute | solution.py:388
  51.6 6.5 %collective-permute-start.21 = (f32[128,128]{1,0:T(8,128)S(1)}, f32[128,128]{1,0:T(8,128)S(1)}, u32[]{:S(2)}, u32[]{:S(2)}) collective-permute-start(f32[128,128]{1,0:T(8,128)S(1)} %get-tuple-element.51), channel_id=1, source_target_pairs={{0,1},{1,0},{2,3},{3,2},{4,5},{5,4},{6,7},{7,6},{8,9},{9,8},{10,11... | collective-permute-start | bytes 196616 | tf_op jit(solution)/shard_map/ppermute | solution.py:390
  53.7 5.5 %collective-permute-start.18 = (f32[8,128]{1,0:T(8,128)S(1)}, f32[8,128]{1,0:T(8,128)S(1)}, u32[]{:S(2)}, u32[]{:S(2)}) collective-permute-start(f32[8,128]{1,0:T(8,128)S(1)} %select_maximum_fusion.refs_0_), channel_id=1, source_target_pairs={{0,12},{2,14},{4,8},{6,10},{8,4},{10,6},{12,0},{14,2},{1,13},{3,15... | collective-permute-start | bytes 12296 | tf_op jit(solution)/shard_map/ppermute | solution.py:406
  56.7 4.5 %collective-permute-start.19 = (f32[8,128]{1,0:T(8,128)S(1)}, f32[8,128]{1,0:T(8,128)S(1)}, u32[]{:S(2)}, u32[]{:S(2)}) collective-permute-start(f32[8,128]{1,0:T(8,128)S(1)} %select_maximum_fusion.refs_0_), channel_id=1, source_target_pairs={{0,8},{2,10},{4,12},{6,14},{8,0},{10,2},{12,4},{14,6},{1,9},{3,11}... | collective-permute-start | bytes 12296 | tf_op jit(solution)/shard_map/ppermute | solution.py:406
  56.7 4.5 %collective-permute-start.20 = (f32[8,128]{1,0:T(8,128)S(1)}, f32[8,128]{1,0:T(8,128)S(1)}, u32[]{:S(2)}, u32[]{:S(2)}) collective-permute-start(f32[8,128]{1,0:T(8,128)S(1)} %select_maximum_fusion.refs_0_), channel_id=1, source_target_pairs={{0,4},{2,6},{4,0},{6,2},{8,12},{10,14},{12,8},{14,10},{1,5},{3,7},... | collective-permute-start | bytes 12296 | tf_op jit(solution)/shard_map/ppermute | solution.py:406

commit v17 on v15

--- a/solution.py
+++ b/solution.py
@@ -10,7 +10,7 @@
 CTF_PHASE = 40.0
 FLOOR = -1e30
 LANES = 128
-VMEM_LIMIT = 8 * 1024 * 1024
+VMEM_LIMIT = 5 * 1024 * 1024
 SCHEDULING_WEIGHT = 20 * 10**9
 
 
@@ -47,14 +47,6 @@
 
 def square_kernel(own, squares):
     squares[...] = own[...] * own[...]
-
-
-def row_kernel(spot, planes, facts, kept, given):
-    core = spot[2]
-    columns = planes.shape[2]
-    for half, out in ((core, kept), (1 - core, given)):
-        out[:, :columns] = planes[half]
-        out[:, columns:] = facts[...]
 
 
 def particle_facts(meta):
@@ -299,18 +291,12 @@
     vmem = pl.BlockSpec(memory_space=pltpu.VMEM)
     smem = pl.BlockSpec(memory_space=pltpu.SMEM)
     params = pltpu.CompilerParams(vmem_limit_bytes=VMEM_LIMIT)
+    first = core == 0
     planes = lax.optimization_barrier(jnp.transpose(images[0], (1, 0, 2)))
     facts = jnp.concatenate([defocus, jnp.transpose(block_ids[0]).astype(jnp.bfloat16)], axis=0)
     facts = jnp.pad(facts, ((0, per_device - facts.shape[0]), (0, LANES - per_device)))
-    row_shape = jax.ShapeDtypeStruct((per_device, columns + LANES), jnp.bfloat16)
-    kept, given = pl.pallas_call(
-        row_kernel,
-        in_specs=[smem, vmem, vmem],
-        out_specs=[vmem] * 2,
-        out_shape=[row_shape] * 2,
-        compiler_params=params,
-    )(spot, planes, facts)
-
+    kept = jnp.concatenate([jnp.where(first, planes[0], planes[1]), facts], axis=1)
+    given = jnp.concatenate([jnp.where(first, planes[1], planes[0]), facts], axis=1)
     _, panels = lax.optimization_barrier((kept, panels))
     sides = lax.optimization_barrier(jnp.transpose(panels[0, 0], (1, 0, 2)))
     panel_shape = jax.ShapeDtypeStruct(sides.shape[1:], sides.dtype)

time: 61.3 us -> 63.9 us (1.042)
  local copies, waits for them, and re-layouts: 3.52 us -> 7.39 us
  starting transfers between devices: 24.9 us -> 23.9 us
  waiting for transfers between devices: 15.8 us -> 16.6 us
    ppermute x1, waiting for transfers between devices: 0.01 us -> 2.12 us  [chip_shards(): got = lax.ppermute(late_given, 'orient', mate_pairs)]
    unnamed x3 -> x7, local copies, waits for them, and re-layouts: 1.07 us -> 3.15 us
    optimization_barrier x1, local copies, waits for them, and re-layouts: 2.42 us -> 4.22 us  [chip_shards(): _, panels = lax.optimization_barrier((kept, panels))]
    ppermute x14, waiting for transfers between devices: 10.9 us -> 9.63 us  [forward(): return lax.ppermute(values, ('orient', 'cls'), pairs)]
    ppermute x1, starting transfers between devices: 1.2 us -> 0.09 us  [chip_shards(): got = lax.ppermute(late_given, 'orient', mate_pairs)]
    concatenate x1, other arithmetic: 0.66 us -> 0.01 us  [chip_shards(): jnp.concatenate([defocus, jnp.transpose(block_ids[0]).astype(jnp.bfloat16...]
  transfers between devices with their start and end apart: 22 -> 22, of which waited for: 10 -> 11; matrix products, arithmetic and copies ran while one was open for 4% -> 7% of each run, Pallas kernels for 16% -> 16%
where the time goes in v17:
time: 63.9 us; the launch traced here: 63.7 us
  starting transfers between devices  23.9 us (37%)
  waiting for transfers between devices  16.6 us (26%)
  Pallas kernels  14.8 us (23%)
  local copies, waits for them, and re-layouts  7.39 us (12%)
  other arithmetic  0.89 us (1%)
    ppermute x14, starting transfers between devices, forward(): return lax.ppermute(values, ('orient', 'cls'), pairs)  16.7 us
    pallas_call x3, Pallas kernels, score_call(): pl.pallas_call(kernel, in_specs=[pl.BlockSpec(memory_space=pltpu.SMEM)] +...  11.1 us
    ppermute x14, waiting for transfers between devices, forward(): return lax.ppermute(values, ('orient', 'cls'), pairs)  9.63 us
    optimization_barrier x1, local copies, waits for them, and re-layouts, chip_shards(): _, panels = lax.optimization_barrier((kept, panels))  4.22 us
    unnamed x7, local copies, waits for them, and re-layouts  3.15 us
    ppermute x1, starting transfers between devices, chip_shards(): far = lax.ppermute(pair, 'orient', [(d, d ^ 6) for d in range(devices)])  2.48 us
    ppermute x1, waiting for transfers between devices, chip_shards(): got = lax.ppermute(late_given, 'orient', mate_pairs)  2.12 us
    ppermute x1, waiting for transfers between devices, chip_shards(): far = lax.ppermute(pair, 'orient', [(d, d ^ 6) for d in range(devices)])  1.76 us
  transfers between devices with their start and end apart: 22, of which 11 were waited for; matrix products, arithmetic and copies ran while one was open for 7% of the time, Pallas kernels for 16%

profile of v17, /device:TPU:0, one launch (start us, length us, event | category | flops | bytes accessed | tf_op | source)
XLA Modules:
  0.0 63.7 jit_solution(8534728872397063148)
XLA Ops:
  0.0 1.1 %copy.11 = bf16[1,16,2,7296]{3,1,2,0:T(8,128)(2,1)S(1)} copy(bf16[1,16,2,7296]{3,2,1,0:T(2,128)(2,1)} %param.5) | data formatting | bytes 933888 | tf_op args[0]
  1.1 0.7 %convert_bitcast_fusion = bf16[4,16]{1,0:T(4,128)(2,1)S(1)} fusion(s32[1,16,4]{1,2,0:T(4,128)} %param.7), kind=kLoop, calls=%fused_computation.16 | loop fusion | flops 64 | bytes 384 | tf_op jit(solution)/shard_map/convert_element_type | solution.py:296
  1.9 2.4 %collective-permute-start.5 = (bf16[16,7424]{1,0:T(8,128)(2,1)S(1)}, bf16[16,7424]{1,0:T(8,128)(2,1)S(1)}, u32[]{:S(2)}, u32[]{:S(2)}) collective-permute-start(bf16[16,7424]{1,0:T(8,128)(2,1)S(1)} %get-tuple-element.59), channel_id=1, source_target_pairs={{0,3},{2,1},{4,2},{6,0},{8,6},{10,4},{12,10},{14,8},{13,14},{15,12... | collective-permute-start | bytes 712712 | tf_op jit(solution)/shard_map/rows_behind/ppermute | solution.py:289
  4.3 0.7 %collective-permute-start = (bf16[16,7424]{1,0:T(8,128)(2,1)S(1)}, bf16[16,7424]{1,0:T(8,128)(2,1)S(1)}, u32[]{:S(2)}, u32[]{:S(2)}) collective-permute-start(bf16[16,7424]{1,0:T(8,128)(2,1)S(1)} %get-tuple-element.60.refs_0_), channel_id=1, source_target_pairs={{0,4},{2,6},{4,8},{6,10},{8,12},{10,14},{12,13},{14,15},{13,9},{15... | collective-permute-start | bytes 712712 | tf_op jit(solution)/shard_map/rows_ahead/ppermute | solution.py:289
  5.0 1.3 %collective-permute-start.3 = (bf16[16,7424]{1,0:T(8,128)(2,1)S(1)}, bf16[16,7424]{1,0:T(8,128)(2,1)S(1)}, u32[]{:S(2)}, u32[]{:S(2)}) collective-permute-start(bf16[16,7424]{1,0:T(8,128)(2,1)S(1)} %get-tuple-element.60.refs_0_), channel_id=1, source_target_pairs={{0,1},{2,3},{4,0},{6,2},{8,4},{10,6},{12,8},{14,10},{13,12},{15,14... | collective-permute-start | bytes 712712 | tf_op jit(solution)/shard_map/rows_behind/ppermute | solution.py:289
  6.4 0.1 collective-permute-start.4
  6.4 4.2 %copy.10 = bf16[1,1,128,2,7296]{4,2,3,1,0:T(8,128)(2,1)} copy(bf16[1,1,128,2,7296]{4,3,2,1,0:T(2,128)(2,1)} %param.9) | data formatting | bytes 7471104 | tf_op jit(solution)/shard_map/optimization_barrier | solution.py:300
  10.7 0.1 pad_add_fusion.spot
  10.7 2.1 %copy-done = bf16[1,1,128,2,7296]{4,2,3,1,0:T(8,128)(2,1)S(1)} copy-done((bf16[1,1,128,2,7296]{4,2,3,1,0:T(8,128)(2,1)S(1)}, bf16[1,1,128,2,7296]{4,2,3,1,0:T(8,128)(2,1)}, u32[]{:S(2)}) %copy-start) | copy-done | bytes 3735576
  12.8 0.8 %shard_map.55 = (bf16[128,7296]{1,0:T(8,128)(2,1)S(1)}, bf16[128,7296]{1,0:T(8,128)(2,1)S(1)}) custom-call(s32[4]{0:T(128)S(1)} %pad_add_fusion.spot, bf16[2,128,7296]{2,1,0:T(8,128)(2,1)S(1)} %bitcast.23), custom_call_target="tpu_custom_call" | custom-call | tf_op jit(solution)/shard_map/pallas_call | solution.py:303
  13.6 0.8 %collective-permute-start.6 = (bf16[128,7296]{1,0:T(8,128)(2,1)S(1)}, bf16[128,7296]{1,0:T(8,128)(2,1)S(1)}, u32[]{:S(2)}, u32[]{:S(2)}) collective-permute-start(bf16[128,7296]{1,0:T(8,128)(2,1)S(1)} %get-tuple-element.34), channel_id=1, source_target_pairs={{0,2},{2,0},{4,6},{6,4},{8,10},{10,8},{12,14},{14,12},{1,3},{3,1},... | collective-permute-start | bytes 5603336 | tf_op jit(solution)/shard_map/mate_panel/ppermute | solution.py:311
  14.4 0.1 collective-permute-start.2
  14.5 0.1 shard_map.56.refs_8_.refs_10_.refs_4_
  14.6 1.4 %collective-permute-start.9 = (bf16[16,7424]{1,0:T(8,128)(2,1)S(1)}, bf16[16,7424]{1,0:T(8,128)(2,1)S(1)}, u32[]{:S(2)}, u32[]{:S(2)}) collective-permute-start(bf16[16,7424]{1,0:T(8,128)(2,1)S(1)} %collective-permute-done.5.refs_5_), channel_id=1, source_target_pairs={{0,1},{2,3},{4,0},{6,2},{8,4},{10,6},{12,8},{14,10},{13,12},{15,14... | collective-permute-start | bytes 712712 | tf_op jit(solution)/shard_map/rows_behind/ppermute | solution.py:289
  16.1 2.1 %collective-permute-done.2.refs_1_ = bf16[16,7424]{1,0:T(8,128)(2,1)S(1)} collective-permute-done((bf16[16,7424]{1,0:T(8,128)(2,1)S(1)}, bf16[16,7424]{1,0:T(8,128)(2,1)S(1)}, u32[]{:S(2)}, u32[]{:S(2)}) %collective-permute-start.2) | collective-permute-done | bytes 237600 | tf_op jit(solution)/shard_map/mate_rows/ppermute | solution.py:351
  18.2 1.6 %collective-permute-start.1 = (bf16[16,7424]{1,0:T(8,128)(2,1)S(1)}, bf16[16,7424]{1,0:T(8,128)(2,1)S(1)}, u32[]{:S(2)}, u32[]{:S(2)}) collective-permute-start(bf16[16,7424]{1,0:T(8,128)(2,1)S(1)} %collective-permute-done.refs_2_), channel_id=1, source_target_pairs={{0,4},{2,6},{4,8},{6,10},{8,12},{10,14},{12,13},{14,15},{13,9},{15... | collective-permute-start | bytes 712712 | tf_op jit(solution)/shard_map/rows_ahead/ppermute | solution.py:289
  19.8 0.5 collective-permute-start.12
  20.3 1.6 %collective-permute-start.13 = (bf16[16,7424]{1,0:T(8,128)(2,1)S(1)}, bf16[16,7424]{1,0:T(8,128)(2,1)S(1)}, u32[]{:S(2)}, u32[]{:S(2)}) collective-permute-start(bf16[16,7424]{1,0:T(8,128)(2,1)S(1)} %collective-permute-done.4.refs_4_), channel_id=1, source_target_pairs={{0,4},{2,6},{4,8},{6,10},{8,12},{10,14},{12,13},{14,15},{13,9},{15... | collective-permute-start | bytes 712712 | tf_op jit(solution)/shard_map/rows_ahead/ppermute | solution.py:289
  21.9 0.0 collective-permute-done.6.refs_9_.refs_11_.refs_5_
  21.9 3.8 %shard_map.57 = (f32[96,128]{1,0:T(8,128)S(1)}, f32[96,128]{1,0:T(8,128)S(1)}, f32[96,128]{1,0:T(8,128)S(1)}) custom-call(s32[4]{0:T(128)S(1)} %pad_add_fusion.spot, bf16[16,7424]{1,0:T(8,128)(2,1)S(1)} %get-tuple-element.60.refs_0_, bf16[16,7424]{1,0:T(8,128)(2,1)S(1)} %collective-permute-done.2.refs_1_, bf16[16,7424]{1,0:T(8,128)(2,1)S(1)} %collective-permute-done.refs_2_, ...), custom_call_target="tpu_custom_call" | custom-call | flops 956301312 | bytes 5136384 | tf_op jit(solution)/shard_map/pallas_call | solution.py:167
  25.8 0.0 collective-permute-done.9.refs_3_
  25.8 0.5 collective-permute-start.10
  26.3 0.5 collective-permute-done.1.refs_0_
  26.8 1.6 %collective-permute-start.7 = (bf16[16,7424]{1,0:T(8,128)(2,1)S(1)}, bf16[16,7424]{1,0:T(8,128)(2,1)S(1)}, u32[]{:S(2)}, u32[]{:S(2)}) collective-permute-start(bf16[16,7424]{1,0:T(8,128)(2,1)S(1)} %collective-permute-done.1.refs_0_), channel_id=1, source_target_pairs={{0,4},{2,6},{4,8},{6,10},{8,12},{10,14},{12,13},{14,15},{13,9},{15... | collective-permute-start | bytes 712712 | tf_op jit(solution)/shard_map/rows_ahead/ppermute | solution.py:289
  28.4 1.4 %collective-permute-start.14 = (bf16[16,7424]{1,0:T(8,128)(2,1)S(1)}, bf16[16,7424]{1,0:T(8,128)(2,1)S(1)}, u32[]{:S(2)}, u32[]{:S(2)}) collective-permute-start(bf16[16,7424]{1,0:T(8,128)(2,1)S(1)} %collective-permute-done.12.refs_1_), channel_id=1, source_target_pairs={{0,1},{2,3},{4,0},{6,2},{8,4},{10,6},{12,8},{14,10},{13,12},{15,14... | collective-permute-start | bytes 712712 | tf_op jit(solution)/shard_map/rows_behind/ppermute | solution.py:289
  29.8 2.1 %collective-permute-done.13.refs_2_ = bf16[16,7424]{1,0:T(8,128)(2,1)S(1)} collective-permute-done((bf16[16,7424]{1,0:T(8,128)(2,1)S(1)}, bf16[16,7424]{1,0:T(8,128)(2,1)S(1)}, u32[]{:S(2)}, u32[]{:S(2)}) %collective-permute-start.13) | collective-permute-done | bytes 237600 | tf_op jit(solution)/shard_map/rows_ahead/ppermute | solution.py:289
  31.9 1.6 %collective-permute-start.15 = (bf16[16,7424]{1,0:T(8,128)(2,1)S(1)}, bf16[16,7424]{1,0:T(8,128)(2,1)S(1)}, u32[]{:S(2)}, u32[]{:S(2)}) collective-permute-start(bf16[16,7424]{1,0:T(8,128)(2,1)S(1)} %collective-permute-done.13.refs_2_), channel_id=1, source_target_pairs={{0,4},{2,6},{4,8},{6,10},{8,12},{10,14},{12,13},{14,15},{13,9},{15... | collective-permute-start | bytes 712712 | tf_op jit(solution)/shard_map/rows_ahead/ppermute | solution.py:289
  33.5 1.0 %collective-permute-done.10.refs_7_ = bf16[16,7424]{1,0:T(8,128)(2,1)S(1)} collective-permute-done((bf16[16,7424]{1,0:T(8,128)(2,1)S(1)}, bf16[16,7424]{1,0:T(8,128)(2,1)S(1)}, u32[]{:S(2)}, u32[]{:S(2)}) %collective-permute-start.10) | collective-permute-done | bytes 237600 | tf_op jit(solution)/shard_map/rows_behind/ppermute | solution.py:289
  34.5 0.5 collective-permute-start.11
  35.0 2.0 %collective-permute-done.7.refs_4_ = bf16[16,7424]{1,0:T(8,128)(2,1)S(1)} collective-permute-done((bf16[16,7424]{1,0:T(8,128)(2,1)S(1)}, bf16[16,7424]{1,0:T(8,128)(2,1)S(1)}, u32[]{:S(2)}, u32[]{:S(2)}) %collective-permute-start.7) | collective-permute-done | bytes 237600 | tf_op jit(solution)/shard_map/rows_ahead/ppermute | solution.py:289
  37.0 1.6 %collective-permute-start.8 = (bf16[16,7424]{1,0:T(8,128)(2,1)S(1)}, bf16[16,7424]{1,0:T(8,128)(2,1)S(1)}, u32[]{:S(2)}, u32[]{:S(2)}) collective-permute-start(bf16[16,7424]{1,0:T(8,128)(2,1)S(1)} %collective-permute-done.7.refs_4_), channel_id=1, source_target_pairs={{0,4},{2,6},{4,8},{6,10},{8,12},{10,14},{12,13},{14,15},{13,9},{15... | collective-permute-start | bytes 712712 | tf_op jit(solution)/shard_map/rows_ahead/ppermute | solution.py:289
  38.6 1.0 %collective-permute-done.14.refs_5_ = bf16[16,7424]{1,0:T(8,128)(2,1)S(1)} collective-permute-done((bf16[16,7424]{1,0:T(8,128)(2,1)S(1)}, bf16[16,7424]{1,0:T(8,128)(2,1)S(1)}, u32[]{:S(2)}, u32[]{:S(2)}) %collective-permute-start.14) | collective-permute-done | bytes 237600 | tf_op jit(solution)/shard_map/rows_behind/ppermute | solution.py:289
  39.6 2.5 %collective-permute-done.15.refs_6_ = bf16[16,7424]{1,0:T(8,128)(2,1)S(1)} collective-permute-done((bf16[16,7424]{1,0:T(8,128)(2,1)S(1)}, bf16[16,7424]{1,0:T(8,128)(2,1)S(1)}, u32[]{:S(2)}, u32[]{:S(2)}) %collective-permute-start.15) | collective-permute-done | bytes 237600 | tf_op jit(solution)/shard_map/rows_ahead/ppermute | solution.py:289
  42.1 4.2 %shard_map.58 = (f32[128,128]{1,0:T(8,128)S(1)}, f32[128,128]{1,0:T(8,128)S(1)}, f32[128,128]{1,0:T(8,128)S(1)}) custom-call(s32[4]{0:T(128)S(1)} %pad_add_fusion.spot, bf16[16,7424]{1,0:T(8,128)(2,1)S(1)} %collective-permute-done.1.refs_0_, bf16[16,7424]{1,0:T(8,128)(2,1)S(1)} %collective-permute-done.12.refs_1_, ...), custom_call_target="tpu_custom_call" | custom-call | flops 956301312 | bytes 5603328 | tf_op jit(solution)/shard_map/pallas_call | solution.py:167
  46.3 0.4 collective-permute-done.8.refs_0_
  46.6 3.1 %shard_map.59 = (f32[2,256,128]{2,1,0:T(8,128)S(1)}, f32[256,128]{1,0:T(8,128)S(1)}) custom-call(s32[4]{0:T(128)S(1)} %pad_add_fusion.spot, bf16[16,7424]{1,0:T(8,128)(2,1)S(1)} %collective-permute-done.8.refs_0_, bf16[16,7424]{1,0:T(8,128)(2,1)S(1)} %collective-permute-done.11.refs_1_, f32[1,7296]{1,0:T(1,128)S(1)} %broadcast_in_dim.3.refs_6_.refs_8_.refs_2_, ...), custom_call_target="tpu_custom_call" | custom-call | flops 956301312 | bytes 4202496 | tf_op jit(solution)/shard_map/pallas_call | solution.py:167
  49.7 0.0 collective-permute-start.16
  49.8 1.5 %collective-permute-done.16.mate = f32[2,256,128]{2,1,0:T(8,128)S(1)} collective-permute-done((f32[2,256,128]{2,1,0:T(8,128)S(1)}, f32[2,256,128]{2,1,0:T(8,128)S(1)}, u32[]{:S(2)}, u32[]{:S(2)}) %collective-permute-start.16) | collective-permute-done | bytes 262176 | tf_op jit(solution)/shard_map/ppermute | solution.py:361
  51.3 0.9 %shard_map.60 = (f32[128,128]{1,0:T(8,128)S(1)}, f32[128,128]{1,0:T(8,128)S(1)}, f32[8,128]{1,0:T(8,128)S(1)}) custom-call(s32[4]{0:T(128)S(1)} %pad_add_fusion.spot, f32[2,256,128]{2,1,0:T(8,128)S(1)} %get-tuple-element.44.partial, f32[2,256,128]{2,1,0:T(8,128)S(1)} %collective-permute-done.16.mate, f32[256,128]{1,0:T(8,128)S(1)} %get-tuple-element.45.facts), custom_call_target="tpu_custom_call" | custom-call | tf_op jit(solution)/shard_map/pallas_call | solution.py:362
  52.2 1.4 %collective-permute-start.17 = (f32[8,128]{1,0:T(8,128)S(1)}, f32[8,128]{1,0:T(8,128)S(1)}, u32[]{:S(2)}, u32[]{:S(2)}) collective-permute-start(f32[8,128]{1,0:T(8,128)S(1)} %get-tuple-element.46), channel_id=1, source_target_pairs={{0,1},{1,0},{2,3},{3,2},{4,5},{5,4},{6,7},{7,6},{8,9},{9,8},{10,11... | collective-permute-start | bytes 12296 | tf_op jit(solution)/shard_map/ppermute | solution.py:374
  53.5 0.7 %collective-permute-start.19 = (f32[128,128]{1,0:T(8,128)S(1)}, f32[128,128]{1,0:T(8,128)S(1)}, u32[]{:S(2)}, u32[]{:S(2)}) collective-permute-start(f32[128,128]{1,0:T(8,128)S(1)} %get-tuple-element.49), channel_id=1, source_target_pairs={{0,1},{1,0},{2,3},{3,2},{4,5},{5,4},{6,7},{7,6},{8,9},{9,8},{10,11... | collective-permute-start | bytes 196616 | tf_op jit(solution)/shard_map/ppermute | solution.py:376
  54.3 1.6 %collective-permute-done.17 = f32[8,128]{1,0:T(8,128)S(1)} collective-permute-done((f32[8,128]{1,0:T(8,128)S(1)}, f32[8,128]{1,0:T(8,128)S(1)}, u32[]{:S(2)}, u32[]{:S(2)}) %collective-permute-start.17) | collective-permute-done | bytes 4128 | tf_op jit(solution)/shard_map/ppermute | solution.py:374
  55.9 1.6 %collective-permute-start.18 = (f32[8,128]{1,0:T(8,128)S(1)}, f32[8,128]{1,0:T(8,128)S(1)}, u32[]{:S(2)}, u32[]{:S(2)}) collective-permute-start(f32[8,128]{1,0:T(8,128)S(1)} %select_maximum_fusion.refs_0_), channel_id=1, source_target_pairs={{0,4},{2,10},{4,0},{6,14},{8,12},{10,2},{12,8},{14,6},{1,5},{3,11}... | collective-permute-start | bytes 12296 | tf_op jit(solution)/shard_map/ppermute | solution.py:392
  57.5 2.5 %collective-permute-start.21 = (f32[8,128]{1,0:T(8,128)S(1)}, f32[8,128]{1,0:T(8,128)S(1)}, u32[]{:S(2)}, u32[]{:S(2)}) collective-permute-start(f32[8,128]{1,0:T(8,128)S(1)} %select_maximum_fusion.refs_0_), channel_id=1, source_target_pairs={{0,12},{2,14},{4,8},{6,10},{8,4},{10,6},{12,0},{14,2},{1,13},{3,15... | collective-permute-start | bytes 12296 | tf_op jit(solution)/shard_map/ppermute | solution.py:393
  60.0 1.1 %shard_map.61 = (f32[128,256]{1,0:T(8,128)S(1)}, f32[128,128]{1,0:T(8,128)S(1)}, f32[8,128]{1,0:T(8,128)S(1)}) custom-call(s32[4]{0:T(128)S(1)} %pad_add_fusion.spot, f32[128,128]{1,0:T(8,128)S(1)} %get-tuple-element.47.mine, f32[128,128]{1,0:T(8,128)S(1)} %collective-permute-done.19.across, f32[256,128]{1,0:T(8,128)S(1)} %get-tuple-element.45.facts), custom_call_target="tpu_custom_call" | custom-call | tf_op jit(solution)/shard_map/pallas_call | solution.py:380
  61.1 0.1 collective-permute-start.20
  61.2 1.8 %collective-permute-done.21.refs_3_ = f32[8,128]{1,0:T(8,128)S(1)} collective-permute-done((f32[8,128]{1,0:T(8,128)S(1)}, f32[8,128]{1,0:T(8,128)S(1)}, u32[]{:S(2)}, u32[]{:S(2)}) %collective-permute-start.21) | collective-permute-done | bytes 4128 | tf_op jit(solution)/shard_map/ppermute | solution.py:393
  62.9 0.8 %shard_map.62 = f32[128,256]{1,0:T(8,128)} custom-call(f32[8,128]{1,0:T(8,128)S(1)} %select_maximum_fusion.refs_0_, f32[8,128]{1,0:T(8,128)S(1)} %collective-permute-done.18.refs_1_, f32[8,128]{1,0:T(8,128)S(1)} %collective-permute-done.20.refs_2_, f32[8,128]{1,0:T(8,128)S(1)} %collective-permute-done.21.refs_3_, f32[8,128]{1,0:T(8,128)S(1)} %get-tuple-element.52.refs_4_, ...), custom_call_target="tpu_custom_call" | custom-call | tf_op jit(solution)/shard_map/pallas_call | solution.py:401
  (20 shorter events, 0.2 us)
Async XLA Ops:
  0.0 1.8 %copy-start.2 = (bf16[1,16]{1,0:T(2,128)(2,1)S(1)}, bf16[1,16]{1,0:T(2,128)(2,1)}, u32[]{:S(2)}) copy-start(bf16[1,16]{1,0:T(2,128)(2,1)} %param.6) | copy-start | bytes 100
  1.9 12.5 %collective-permute-start.5 = (bf16[16,7424]{1,0:T(8,128)(2,1)S(1)}, bf16[16,7424]{1,0:T(8,128)(2,1)S(1)}, u32[]{:S(2)}, u32[]{:S(2)}) collective-permute-start(bf16[16,7424]{1,0:T(8,128)(2,1)S(1)} %get-tuple-element.59), channel_id=1, source_target_pairs={{0,3},{2,1},{4,2},{6,0},{8,6},{10,4},{12,10},{14,8},{13,14},{15,12... | collective-permute-start | bytes 712712 | tf_op jit(solution)/shard_map/rows_behind/ppermute | solution.py:289
  4.3 10.3 %collective-permute-start = (bf16[16,7424]{1,0:T(8,128)(2,1)S(1)}, bf16[16,7424]{1,0:T(8,128)(2,1)S(1)}, u32[]{:S(2)}, u32[]{:S(2)}) collective-permute-start(bf16[16,7424]{1,0:T(8,128)(2,1)S(1)} %get-tuple-element.60.refs_0_), channel_id=1, source_target_pairs={{0,4},{2,6},{4,8},{6,10},{8,12},{10,14},{12,13},{14,15},{13,9},{15... | collective-permute-start | bytes 712712 | tf_op jit(solution)/shard_map/rows_ahead/ppermute | solution.py:289
  5.0 14.8 %collective-permute-start.3 = (bf16[16,7424]{1,0:T(8,128)(2,1)S(1)}, bf16[16,7424]{1,0:T(8,128)(2,1)S(1)}, u32[]{:S(2)}, u32[]{:S(2)}) collective-permute-start(bf16[16,7424]{1,0:T(8,128)(2,1)S(1)} %get-tuple-element.60.refs_0_), channel_id=1, source_target_pairs={{0,1},{2,3},{4,0},{6,2},{8,4},{10,6},{12,8},{14,10},{13,12},{15,14... | collective-permute-start | bytes 712712 | tf_op jit(solution)/shard_map/rows_behind/ppermute | solution.py:289
  6.4 14.0 %collective-permute-start.4 = (bf16[16,7424]{1,0:T(8,128)(2,1)S(1)}, bf16[16,7424]{1,0:T(8,128)(2,1)S(1)}, u32[]{:S(2)}, u32[]{:S(2)}) collective-permute-start(bf16[16,7424]{1,0:T(8,128)(2,1)S(1)} %get-tuple-element.59), channel_id=1, source_target_pairs={{0,6},{2,4},{4,10},{6,8},{8,14},{10,12},{12,15},{14,13},{13,11},{1... | collective-permute-start | bytes 712712 | tf_op jit(solution)/shard_map/rows_ahead/ppermute | solution.py:289
  10.7 2.1 %copy-start = (bf16[1,1,128,2,7296]{4,2,3,1,0:T(8,128)(2,1)S(1)}, bf16[1,1,128,2,7296]{4,2,3,1,0:T(8,128)(2,1)}, u32[]{:S(2)}) copy-start(bf16[1,1,128,2,7296]{4,2,3,1,0:T(8,128)(2,1)} %copy.10) | copy-start | bytes 11206660
  13.6 8.3 %collective-permute-start.6 = (bf16[128,7296]{1,0:T(8,128)(2,1)S(1)}, bf16[128,7296]{1,0:T(8,128)(2,1)S(1)}, u32[]{:S(2)}, u32[]{:S(2)}) collective-permute-start(bf16[128,7296]{1,0:T(8,128)(2,1)S(1)} %get-tuple-element.34), channel_id=1, source_target_pairs={{0,2},{2,0},{4,6},{6,4},{8,10},{10,8},{12,14},{14,12},{1,3},{3,1},... | collective-permute-start | bytes 5603336 | tf_op jit(solution)/shard_map/mate_panel/ppermute | solution.py:311
  14.4 3.8 %collective-permute-start.2 = (bf16[16,7424]{1,0:T(8,128)(2,1)S(1)}, bf16[16,7424]{1,0:T(8,128)(2,1)S(1)}, u32[]{:S(2)}, u32[]{:S(2)}) collective-permute-start(bf16[16,7424]{1,0:T(8,128)(2,1)S(1)} %get-tuple-element.59), channel_id=1, source_target_pairs={{0,2},{2,0},{4,6},{6,4},{8,10},{10,8},{12,14},{14,12},{1,3},{3,1},... | collective-permute-start | bytes 712712 | tf_op jit(solution)/shard_map/mate_rows/ppermute | solution.py:351
  14.5 5.3 %copy-start.1 = (f32[7296]{0:T(1024)S(1)}, f32[7296]{0:T(1024)}, u32[]{:S(2)}) copy-start(f32[7296]{0:T(1024)} %param.8) | copy-start | bytes 87556
  14.6 11.1 %collective-permute-start.9 = (bf16[16,7424]{1,0:T(8,128)(2,1)S(1)}, bf16[16,7424]{1,0:T(8,128)(2,1)S(1)}, u32[]{:S(2)}, u32[]{:S(2)}) collective-permute-start(bf16[16,7424]{1,0:T(8,128)(2,1)S(1)} %collective-permute-done.5.refs_5_), channel_id=1, source_target_pairs={{0,1},{2,3},{4,0},{6,2},{8,4},{10,6},{12,8},{14,10},{13,12},{15,14... | collective-permute-start | bytes 712712 | tf_op jit(solution)/shard_map/rows_behind/ppermute | solution.py:289
  18.2 8.6 %collective-permute-start.1 = (bf16[16,7424]{1,0:T(8,128)(2,1)S(1)}, bf16[16,7424]{1,0:T(8,128)(2,1)S(1)}, u32[]{:S(2)}, u32[]{:S(2)}) collective-permute-start(bf16[16,7424]{1,0:T(8,128)(2,1)S(1)} %collective-permute-done.refs_2_), channel_id=1, source_target_pairs={{0,4},{2,6},{4,8},{6,10},{8,12},{10,14},{12,13},{14,15},{13,9},{15... | collective-permute-start | bytes 712712 | tf_op jit(solution)/shard_map/rows_ahead/ppermute | solution.py:289
  19.8 8.6 %collective-permute-start.12 = (bf16[16,7424]{1,0:T(8,128)(2,1)S(1)}, bf16[16,7424]{1,0:T(8,128)(2,1)S(1)}, u32[]{:S(2)}, u32[]{:S(2)}) collective-permute-start(bf16[16,7424]{1,0:T(8,128)(2,1)S(1)} %collective-permute-done.3.refs_3_), channel_id=1, source_target_pairs={{0,1},{2,3},{4,0},{6,2},{8,4},{10,6},{12,8},{14,10},{13,12},{15,14... | collective-permute-start | bytes 712712 | tf_op jit(solution)/shard_map/rows_behind/ppermute | solution.py:289
  20.3 11.6 %collective-permute-start.13 = (bf16[16,7424]{1,0:T(8,128)(2,1)S(1)}, bf16[16,7424]{1,0:T(8,128)(2,1)S(1)}, u32[]{:S(2)}, u32[]{:S(2)}) collective-permute-start(bf16[16,7424]{1,0:T(8,128)(2,1)S(1)} %collective-permute-done.4.refs_4_), channel_id=1, source_target_pairs={{0,4},{2,6},{4,8},{6,10},{8,12},{10,14},{12,13},{14,15},{13,9},{15... | collective-permute-start | bytes 712712 | tf_op jit(solution)/shard_map/rows_ahead/ppermute | solution.py:289
  25.8 8.8 %collective-permute-start.10 = (bf16[16,7424]{1,0:T(8,128)(2,1)S(1)}, bf16[16,7424]{1,0:T(8,128)(2,1)S(1)}, u32[]{:S(2)}, u32[]{:S(2)}) collective-permute-start(bf16[16,7424]{1,0:T(8,128)(2,1)S(1)} %collective-permute-done.9.refs_3_), channel_id=1, source_target_pairs={{0,1},{2,3},{4,0},{6,2},{8,4},{10,6},{12,8},{14,10},{13,12},{15,14... | collective-permute-start | bytes 712712 | tf_op jit(solution)/shard_map/rows_behind/ppermute | solution.py:289
  26.8 10.2 %collective-permute-start.7 = (bf16[16,7424]{1,0:T(8,128)(2,1)S(1)}, bf16[16,7424]{1,0:T(8,128)(2,1)S(1)}, u32[]{:S(2)}, u32[]{:S(2)}) collective-permute-start(bf16[16,7424]{1,0:T(8,128)(2,1)S(1)} %collective-permute-done.1.refs_0_), channel_id=1, source_target_pairs={{0,4},{2,6},{4,8},{6,10},{8,12},{10,14},{12,13},{14,15},{13,9},{15... | collective-permute-start | bytes 712712 | tf_op jit(solution)/shard_map/rows_ahead/ppermute | solution.py:289
  28.4 11.2 %collective-permute-start.14 = (bf16[16,7424]{1,0:T(8,128)(2,1)S(1)}, bf16[16,7424]{1,0:T(8,128)(2,1)S(1)}, u32[]{:S(2)}, u32[]{:S(2)}) collective-permute-start(bf16[16,7424]{1,0:T(8,128)(2,1)S(1)} %collective-permute-done.12.refs_1_), channel_id=1, source_target_pairs={{0,1},{2,3},{4,0},{6,2},{8,4},{10,6},{12,8},{14,10},{13,12},{15,14... | collective-permute-start | bytes 712712 | tf_op jit(solution)/shard_map/rows_behind/ppermute | solution.py:289
  31.9 10.2 %collective-permute-start.15 = (bf16[16,7424]{1,0:T(8,128)(2,1)S(1)}, bf16[16,7424]{1,0:T(8,128)(2,1)S(1)}, u32[]{:S(2)}, u32[]{:S(2)}) collective-permute-start(bf16[16,7424]{1,0:T(8,128)(2,1)S(1)} %collective-permute-done.13.refs_2_), channel_id=1, source_target_pairs={{0,4},{2,6},{4,8},{6,10},{8,12},{10,14},{12,13},{14,15},{13,9},{15... | collective-permute-start | bytes 712712 | tf_op jit(solution)/shard_map/rows_ahead/ppermute | solution.py:289
  34.5 11.7 %collective-permute-start.11 = (bf16[16,7424]{1,0:T(8,128)(2,1)S(1)}, bf16[16,7424]{1,0:T(8,128)(2,1)S(1)}, u32[]{:S(2)}, u32[]{:S(2)}) collective-permute-start(bf16[16,7424]{1,0:T(8,128)(2,1)S(1)} %collective-permute-done.10.refs_7_), channel_id=1, source_target_pairs={{0,1},{2,3},{4,0},{6,2},{8,4},{10,6},{12,8},{14,10},{13,12},{15,14... | collective-permute-start | bytes 712712 | tf_op jit(solution)/shard_map/rows_behind/ppermute | solution.py:289
  37.0 9.6 %collective-permute-start.8 = (bf16[16,7424]{1,0:T(8,128)(2,1)S(1)}, bf16[16,7424]{1,0:T(8,128)(2,1)S(1)}, u32[]{:S(2)}, u32[]{:S(2)}) collective-permute-start(bf16[16,7424]{1,0:T(8,128)(2,1)S(1)} %collective-permute-done.7.refs_4_), channel_id=1, source_target_pairs={{0,4},{2,6},{4,8},{6,10},{8,12},{10,14},{12,13},{14,15},{13,9},{15... | collective-permute-start | bytes 712712 | tf_op jit(solution)/shard_map/rows_ahead/ppermute | solution.py:289
  49.7 1.6 %collective-permute-start.16 = (f32[2,256,128]{2,1,0:T(8,128)S(1)}, f32[2,256,128]{2,1,0:T(8,128)S(1)}, u32[]{:S(2)}, u32[]{:S(2)}) collective-permute-start(f32[2,256,128]{2,1,0:T(8,128)S(1)} %get-tuple-element.44.partial), channel_id=1, source_target_pairs={{0,2},{2,0},{4,6},{6,4},{8,10},{10,8},{12,14},{14,12},{1,3},{3,1},... | collective-permute-start | bytes 786440 | tf_op jit(solution)/shard_map/ppermute | solution.py:361
  52.2 3.6 %collective-permute-start.17 = (f32[8,128]{1,0:T(8,128)S(1)}, f32[8,128]{1,0:T(8,128)S(1)}, u32[]{:S(2)}, u32[]{:S(2)}) collective-permute-start(f32[8,128]{1,0:T(8,128)S(1)} %get-tuple-element.46), channel_id=1, source_target_pairs={{0,1},{1,0},{2,3},{3,2},{4,5},{5,4},{6,7},{7,6},{8,9},{9,8},{10,11... | collective-permute-start | bytes 12296 | tf_op jit(solution)/shard_map/ppermute | solution.py:374
  53.5 6.4 %collective-permute-start.19 = (f32[128,128]{1,0:T(8,128)S(1)}, f32[128,128]{1,0:T(8,128)S(1)}, u32[]{:S(2)}, u32[]{:S(2)}) collective-permute-start(f32[128,128]{1,0:T(8,128)S(1)} %get-tuple-element.49), channel_id=1, source_target_pairs={{0,1},{1,0},{2,3},{3,2},{4,5},{5,4},{6,7},{7,6},{8,9},{9,8},{10,11... | collective-permute-start | bytes 196616 | tf_op jit(solution)/shard_map/ppermute | solution.py:376
  55.9 5.2 %collective-permute-start.18 = (f32[8,128]{1,0:T(8,128)S(1)}, f32[8,128]{1,0:T(8,128)S(1)}, u32[]{:S(2)}, u32[]{:S(2)}) collective-permute-start(f32[8,128]{1,0:T(8,128)S(1)} %select_maximum_fusion.refs_0_), channel_id=1, source_target_pairs={{0,4},{2,10},{4,0},{6,14},{8,12},{10,2},{12,8},{14,6},{1,5},{3,11}... | collective-permute-start | bytes 12296 | tf_op jit(solution)/shard_map/ppermute | solution.py:392
  57.5 5.4 %collective-permute-start.21 = (f32[8,128]{1,0:T(8,128)S(1)}, f32[8,128]{1,0:T(8,128)S(1)}, u32[]{:S(2)}, u32[]{:S(2)}) collective-permute-start(f32[8,128]{1,0:T(8,128)S(1)} %select_maximum_fusion.refs_0_), channel_id=1, source_target_pairs={{0,12},{2,14},{4,8},{6,10},{8,4},{10,6},{12,0},{14,2},{1,13},{3,15... | collective-permute-start | bytes 12296 | tf_op jit(solution)/shard_map/ppermute | solution.py:393
  61.1 1.8 %collective-permute-start.20 = (f32[8,128]{1,0:T(8,128)S(1)}, f32[8,128]{1,0:T(8,128)S(1)}, u32[]{:S(2)}, u32[]{:S(2)}) collective-permute-start(f32[8,128]{1,0:T(8,128)S(1)} %collective-permute-done.18.refs_1_), channel_id=1, source_target_pairs={{0,2},{2,0},{4,6},{6,4},{8,10},{10,8},{12,14},{14,12},{1,3},{3,1},... | collective-permute-start | bytes 12296 | tf_op jit(solution)/shard_map/ppermute | solution.py:395

commit v18 on v15

--- a/solution.py
+++ b/solution.py
@@ -311,7 +311,10 @@
         compiler_params=params,
     )(spot, planes, facts)
 
-    _, panels = lax.optimization_barrier((kept, panels))
+    with jax.named_scope("mate_rows"):
+        got = lax.ppermute(given, "orient", mate_pairs)
+
+    _, panels = lax.optimization_barrier((got, panels))
     sides = lax.optimization_barrier(jnp.transpose(panels[0, 0], (1, 0, 2)))
     panel_shape = jax.ShapeDtypeStruct(sides.shape[1:], sides.dtype)
     own_panel, given_panel = pl.pallas_call(
@@ -325,7 +328,7 @@
         mate_panel = lax.ppermute(given_panel, "orient", mate_pairs)
 
     noise = noise_weight[None, :]
-    waiting = []
+    waiting = [((0, False), kept), ((0, True), got)]
     ahead = {False: kept, True: given}
     behind = {False: kept, True: given}
     orders, earlier, late = [], [], []
@@ -346,7 +349,7 @@
             for chain, c in ((ahead, False), (behind, True)):
                 chain[c] = lax.optimization_barrier((chain[c], earlier[-1][2]))[0]
         if step == 2:
-            for chain, c in ((ahead, False), (behind, True)):
+            for chain, c in ((ahead, False), (behind, False)):
                 chain[c] = lax.optimization_barrier((chain[c], squares))[0]
         waiting = waiting + late
         late = []
@@ -359,11 +362,6 @@
                 with jax.named_scope("rows_behind"):
                     behind[crossed] = forward(behind[crossed], -1, int(crossed and step == 1))
                 late.append(((step, crossed), behind[crossed]))
-        if step == 1:
-            late_given, _ = lax.optimization_barrier((given, kept))
-            with jax.named_scope("mate_rows"):
-                got = lax.ppermute(late_given, "orient", mate_pairs)
-            late = [((0, False), kept), ((0, True), got)] + late
     orders.append([key for key, _ in waiting])
     earlier.append(score([c for _, c in waiting]))
     waiting = late

time: 61.3 us -> 61.4 us (level)
  waiting for transfers between devices: 15.8 us -> 19.7 us
  starting transfers between devices: 24.9 us -> 21.1 us
    ppermute x14, waiting for transfers between devices: 10.9 us -> 14.8 us  [forward(): return lax.ppermute(values, ('orient', 'cls'), pairs)]
    ppermute x14, starting transfers between devices: 17.1 us -> 14.4 us  [forward(): return lax.ppermute(values, ('orient', 'cls'), pairs)]
    ppermute x1, starting transfers between devices: 1.2 us -> 0.52 us  [chip_shards(): got = lax.ppermute(given, 'orient', mate_pairs)]
  transfers between devices with their start and end apart: 22 -> 22, of which waited for: 10 -> 11; matrix products, arithmetic and copies ran while one was open for 4% -> 4% of each run, Pallas kernels for 16% -> 16%
where the time goes in v18:
time: 61.4 us; the launch traced here: 61.1 us
  starting transfers between devices  21.1 us (34%)
  waiting for transfers between devices  19.7 us (32%)
  Pallas kernels  15.3 us (25%)
  local copies, waits for them, and re-layouts  3.52 us (6%)
  other arithmetic  1.45 us (2%)
    ppermute x14, waiting for transfers between devices, forward(): return lax.ppermute(values, ('orient', 'cls'), pairs)  14.8 us
    ppermute x14, starting transfers between devices, forward(): return lax.ppermute(values, ('orient', 'cls'), pairs)  14.4 us
    pallas_call x3, Pallas kernels, score_call(): pl.pallas_call(kernel, in_specs=[pl.BlockSpec(memory_space=pltpu.SMEM)] +...  11.1 us
    ppermute x1, starting transfers between devices, chip_shards(): far = lax.ppermute(pair, 'orient', [(d, d ^ 6) for d in range(devices)])  2.47 us
    optimization_barrier x1, local copies, waits for them, and re-layouts, chip_shards(): _, panels = lax.optimization_barrier((got, panels))  2.42 us
    ppermute x1, waiting for transfers between devices, chip_shards(): far = lax.ppermute(pair, 'orient', [(d, d ^ 6) for d in range(devices)])  1.77 us
    ppermute x1, starting transfers between devices, chip_shards(): x_stats = lax.ppermute(stats, 'cls', x_pairs)  1.61 us
    ppermute x1, waiting for transfers between devices, chip_shards(): x_stats = lax.ppermute(stats, 'cls', x_pairs)  1.58 us
  transfers between devices with their start and end apart: 22, of which 11 were waited for; matrix products, arithmetic and copies ran while one was open for 4% of the time, Pallas kernels for 16%

profile of v18, /device:TPU:0, one launch (start us, length us, event | category | flops | bytes accessed | tf_op | source)
XLA Modules:
  0.0 61.1 jit_solution(17674597449598782084)
XLA Ops:
  0.0 1.1 %copy.11 = bf16[1,16,2,7296]{3,1,2,0:T(8,128)(2,1)S(1)} copy(bf16[1,16,2,7296]{3,2,1,0:T(2,128)(2,1)} %param.5) | data formatting | bytes 933888 | tf_op args[0]
  1.1 0.7 %convert_bitcast_fusion = bf16[4,16]{1,0:T(4,128)(2,1)S(1)} fusion(s32[1,16,4]{1,2,0:T(4,128)} %param.7), kind=kLoop, calls=%fused_computation.12 | loop fusion | flops 64 | bytes 384 | tf_op jit(solution)/shard_map/convert_element_type | solution.py:303
  1.8 0.7 %fusion.5.facts = bf16[16,128]{1,0:T(8,128)(2,1)S(1)} fusion(bf16[4,16]{1,0:T(4,128)(2,1)S(1)} %convert_bitcast_fusion, bf16[1,16]{1,0:T(2,128)(2,1)} %param.6), kind=kLoop, calls=%fused_computation.9 | loop fusion | flops 22528 | bytes 4256 | tf_op jit(solution)/shard_map/concatenate | solution.py:303
  2.4 0.1 pad_add_fusion.spot
  2.5 0.6 shard_map.55
  3.1 0.5 collective-permute-start.1
  3.6 2.6 %collective-permute-start.5 = (bf16[16,7424]{1,0:T(8,128)(2,1)S(1)}, bf16[16,7424]{1,0:T(8,128)(2,1)S(1)}, u32[]{:S(2)}, u32[]{:S(2)}) collective-permute-start(bf16[16,7424]{1,0:T(8,128)(2,1)S(1)} %get-tuple-element.32), channel_id=1, source_target_pairs={{0,3},{2,1},{4,2},{6,0},{8,6},{10,4},{12,10},{14,8},{13,14},{15,12... | collective-permute-start | bytes 712712 | tf_op jit(solution)/shard_map/rows_behind/ppermute | solution.py:297
  6.2 0.1 collective-permute-start
  6.3 1.9 %collective-permute-start.3 = (bf16[16,7424]{1,0:T(8,128)(2,1)S(1)}, bf16[16,7424]{1,0:T(8,128)(2,1)S(1)}, u32[]{:S(2)}, u32[]{:S(2)}) collective-permute-start(bf16[16,7424]{1,0:T(8,128)(2,1)S(1)} %get-tuple-element.31.refs_0_), channel_id=1, source_target_pairs={{0,1},{2,3},{4,0},{6,2},{8,4},{10,6},{12,8},{14,10},{13,12},{15,14... | collective-permute-start | bytes 712712 | tf_op jit(solution)/shard_map/rows_behind/ppermute | solution.py:297
  8.2 2.4 %copy.10 = bf16[1,1,128,2,7296]{4,2,3,1,0:T(8,128)(2,1)S(1)} copy(bf16[1,1,128,2,7296]{4,3,2,1,0:T(2,128)(2,1)} %param.9) | data formatting | bytes 7471104 | tf_op jit(solution)/shard_map/optimization_barrier | solution.py:317
  10.7 0.8 %shard_map.56 = (bf16[128,7296]{1,0:T(8,128)(2,1)S(1)}, bf16[128,7296]{1,0:T(8,128)(2,1)S(1)}) custom-call(s32[4]{0:T(128)S(1)} %pad_add_fusion.spot, bf16[2,128,7296]{2,1,0:T(8,128)(2,1)S(1)} %bitcast.19), custom_call_target="tpu_custom_call" | custom-call | tf_op jit(solution)/shard_map/pallas_call | solution.py:320
  11.5 0.3 collective-permute-start.6
  11.8 0.6 collective-permute-done.5.refs_5_
  12.4 1.5 %collective-permute-start.9 = (bf16[16,7424]{1,0:T(8,128)(2,1)S(1)}, bf16[16,7424]{1,0:T(8,128)(2,1)S(1)}, u32[]{:S(2)}, u32[]{:S(2)}) collective-permute-start(bf16[16,7424]{1,0:T(8,128)(2,1)S(1)} %collective-permute-done.5.refs_5_), channel_id=1, source_target_pairs={{0,1},{2,3},{4,0},{6,2},{8,4},{10,6},{12,8},{14,10},{13,12},{15,14... | collective-permute-start | bytes 712712 | tf_op jit(solution)/shard_map/rows_behind/ppermute | solution.py:297
  13.9 0.1 shard_map.57.refs_8_.refs_10_.refs_4_
  14.0 0.8 %collective-permute-done.refs_2_ = bf16[16,7424]{1,0:T(8,128)(2,1)S(1)} collective-permute-done((bf16[16,7424]{1,0:T(8,128)(2,1)S(1)}, bf16[16,7424]{1,0:T(8,128)(2,1)S(1)}, u32[]{:S(2)}, u32[]{:S(2)}) %collective-permute-start) | collective-permute-done | bytes 237600 | tf_op jit(solution)/shard_map/rows_ahead/ppermute | solution.py:297
  14.8 0.1 collective-permute-start.2
  15.0 3.0 %collective-permute-done.3.refs_3_ = bf16[16,7424]{1,0:T(8,128)(2,1)S(1)} collective-permute-done((bf16[16,7424]{1,0:T(8,128)(2,1)S(1)}, bf16[16,7424]{1,0:T(8,128)(2,1)S(1)}, u32[]{:S(2)}, u32[]{:S(2)}) %collective-permute-start.3) | collective-permute-done | bytes 237600 | tf_op jit(solution)/shard_map/rows_behind/ppermute | solution.py:297
  18.0 1.9 %collective-permute-start.12 = (bf16[16,7424]{1,0:T(8,128)(2,1)S(1)}, bf16[16,7424]{1,0:T(8,128)(2,1)S(1)}, u32[]{:S(2)}, u32[]{:S(2)}) collective-permute-start(bf16[16,7424]{1,0:T(8,128)(2,1)S(1)} %collective-permute-done.3.refs_3_), channel_id=1, source_target_pairs={{0,1},{2,3},{4,0},{6,2},{8,4},{10,6},{12,8},{14,10},{13,12},{15,14... | collective-permute-start | bytes 712712 | tf_op jit(solution)/shard_map/rows_behind/ppermute | solution.py:297
  19.9 0.1 collective-permute-start.13
  20.0 3.8 %shard_map.58 = (f32[96,128]{1,0:T(8,128)S(1)}, f32[96,128]{1,0:T(8,128)S(1)}, f32[96,128]{1,0:T(8,128)S(1)}) custom-call(s32[4]{0:T(128)S(1)} %pad_add_fusion.spot, bf16[16,7424]{1,0:T(8,128)(2,1)S(1)} %get-tuple-element.31.refs_0_, bf16[16,7424]{1,0:T(8,128)(2,1)S(1)} %collective-permute-done.1.refs_1_, bf16[16,7424]{1,0:T(8,128)(2,1)S(1)} %collective-permute-done.refs_2_, ...), custom_call_target="tpu_custom_call" | custom-call | flops 956301312 | bytes 5136384 | tf_op jit(solution)/shard_map/pallas_call | solution.py:175
  23.8 2.0 %collective-permute-start.10 = (bf16[16,7424]{1,0:T(8,128)(2,1)S(1)}, bf16[16,7424]{1,0:T(8,128)(2,1)S(1)}, u32[]{:S(2)}, u32[]{:S(2)}) collective-permute-start(bf16[16,7424]{1,0:T(8,128)(2,1)S(1)} %collective-permute-done.9.refs_3_), channel_id=1, source_target_pairs={{0,1},{2,3},{4,0},{6,2},{8,4},{10,6},{12,8},{14,10},{13,12},{15,14... | collective-permute-start | bytes 712712 | tf_op jit(solution)/shard_map/rows_behind/ppermute | solution.py:297
  25.8 0.2 collective-permute-start.7
  26.0 2.2 %collective-permute-done.12.refs_1_ = bf16[16,7424]{1,0:T(8,128)(2,1)S(1)} collective-permute-done((bf16[16,7424]{1,0:T(8,128)(2,1)S(1)}, bf16[16,7424]{1,0:T(8,128)(2,1)S(1)}, u32[]{:S(2)}, u32[]{:S(2)}) %collective-permute-start.12) | collective-permute-done | bytes 237600 | tf_op jit(solution)/shard_map/rows_behind/ppermute | solution.py:297
  28.1 1.9 %collective-permute-start.14 = (bf16[16,7424]{1,0:T(8,128)(2,1)S(1)}, bf16[16,7424]{1,0:T(8,128)(2,1)S(1)}, u32[]{:S(2)}, u32[]{:S(2)}) collective-permute-start(bf16[16,7424]{1,0:T(8,128)(2,1)S(1)} %collective-permute-done.12.refs_1_), channel_id=1, source_target_pairs={{0,1},{2,3},{4,0},{6,2},{8,4},{10,6},{12,8},{14,10},{13,12},{15,14... | collective-permute-start | bytes 712712 | tf_op jit(solution)/shard_map/rows_behind/ppermute | solution.py:297
  30.1 0.0 collective-permute-done.13.refs_2_
  30.1 0.1 collective-permute-start.15
  30.2 3.0 %collective-permute-done.10.refs_7_ = bf16[16,7424]{1,0:T(8,128)(2,1)S(1)} collective-permute-done((bf16[16,7424]{1,0:T(8,128)(2,1)S(1)}, bf16[16,7424]{1,0:T(8,128)(2,1)S(1)}, u32[]{:S(2)}, u32[]{:S(2)}) %collective-permute-start.10) | collective-permute-done | bytes 237600 | tf_op jit(solution)/shard_map/rows_behind/ppermute | solution.py:297
  33.2 1.9 %collective-permute-start.11 = (bf16[16,7424]{1,0:T(8,128)(2,1)S(1)}, bf16[16,7424]{1,0:T(8,128)(2,1)S(1)}, u32[]{:S(2)}, u32[]{:S(2)}) collective-permute-start(bf16[16,7424]{1,0:T(8,128)(2,1)S(1)} %collective-permute-done.10.refs_7_), channel_id=1, source_target_pairs={{0,1},{2,3},{4,0},{6,2},{8,4},{10,6},{12,8},{14,10},{13,12},{15,14... | collective-permute-start | bytes 712712 | tf_op jit(solution)/shard_map/rows_behind/ppermute | solution.py:297
  35.2 0.0 collective-permute-done.7.refs_4_
  35.2 0.1 collective-permute-start.8
  35.3 3.0 %collective-permute-done.14.refs_5_ = bf16[16,7424]{1,0:T(8,128)(2,1)S(1)} collective-permute-done((bf16[16,7424]{1,0:T(8,128)(2,1)S(1)}, bf16[16,7424]{1,0:T(8,128)(2,1)S(1)}, u32[]{:S(2)}, u32[]{:S(2)}) %collective-permute-start.14) | collective-permute-done | bytes 237600 | tf_op jit(solution)/shard_map/rows_behind/ppermute | solution.py:297
  38.3 2.0 %collective-permute-done.15.refs_6_ = bf16[16,7424]{1,0:T(8,128)(2,1)S(1)} collective-permute-done((bf16[16,7424]{1,0:T(8,128)(2,1)S(1)}, bf16[16,7424]{1,0:T(8,128)(2,1)S(1)}, u32[]{:S(2)}, u32[]{:S(2)}) %collective-permute-start.15) | collective-permute-done | bytes 237600 | tf_op jit(solution)/shard_map/rows_ahead/ppermute | solution.py:297
  40.3 4.1 %shard_map.59 = (f32[128,128]{1,0:T(8,128)S(1)}, f32[128,128]{1,0:T(8,128)S(1)}, f32[128,128]{1,0:T(8,128)S(1)}) custom-call(s32[4]{0:T(128)S(1)} %pad_add_fusion.spot, bf16[16,7424]{1,0:T(8,128)(2,1)S(1)} %collective-permute-done.2.refs_0_, bf16[16,7424]{1,0:T(8,128)(2,1)S(1)} %collective-permute-done.12.refs_1_, ...), custom_call_target="tpu_custom_call" | custom-call | flops 956301312 | bytes 5603328 | tf_op jit(solution)/shard_map/pallas_call | solution.py:175
  44.4 0.1 collective-permute-done.8.refs_0_
  44.5 3.1 %shard_map.60 = (f32[2,256,128]{2,1,0:T(8,128)S(1)}, f32[256,128]{1,0:T(8,128)S(1)}) custom-call(s32[4]{0:T(128)S(1)} %pad_add_fusion.spot, bf16[16,7424]{1,0:T(8,128)(2,1)S(1)} %collective-permute-done.8.refs_0_, bf16[16,7424]{1,0:T(8,128)(2,1)S(1)} %collective-permute-done.11.refs_1_, f32[1,7296]{1,0:T(1,128)S(1)} %broadcast_in_dim.3.refs_6_.refs_8_.refs_2_, ...), custom_call_target="tpu_custom_call" | custom-call | flops 956301312 | bytes 4202496 | tf_op jit(solution)/shard_map/pallas_call | solution.py:175
  47.6 0.0 collective-permute-start.16
  47.7 1.5 %collective-permute-done.16.mate = f32[2,256,128]{2,1,0:T(8,128)S(1)} collective-permute-done((f32[2,256,128]{2,1,0:T(8,128)S(1)}, f32[2,256,128]{2,1,0:T(8,128)S(1)}, u32[]{:S(2)}, u32[]{:S(2)}) %collective-permute-start.16) | collective-permute-done | bytes 262176 | tf_op jit(solution)/shard_map/ppermute | solution.py:373
  49.2 0.9 %shard_map.61 = (f32[128,128]{1,0:T(8,128)S(1)}, f32[128,128]{1,0:T(8,128)S(1)}, f32[8,128]{1,0:T(8,128)S(1)}) custom-call(s32[4]{0:T(128)S(1)} %pad_add_fusion.spot, f32[2,256,128]{2,1,0:T(8,128)S(1)} %get-tuple-element.46.partial, f32[2,256,128]{2,1,0:T(8,128)S(1)} %collective-permute-done.16.mate, f32[256,128]{1,0:T(8,128)S(1)} %get-tuple-element.47.facts), custom_call_target="tpu_custom_call" | custom-call | tf_op jit(solution)/shard_map/pallas_call | solution.py:374
  50.1 1.6 %collective-permute-start.17 = (f32[8,128]{1,0:T(8,128)S(1)}, f32[8,128]{1,0:T(8,128)S(1)}, u32[]{:S(2)}, u32[]{:S(2)}) collective-permute-start(f32[8,128]{1,0:T(8,128)S(1)} %get-tuple-element.48), channel_id=1, source_target_pairs={{0,1},{1,0},{2,3},{3,2},{4,5},{5,4},{6,7},{7,6},{8,9},{9,8},{10,11... | collective-permute-start | bytes 12296 | tf_op jit(solution)/shard_map/ppermute | solution.py:386
  51.7 0.4 collective-permute-start.19
  52.1 1.6 %collective-permute-done.17 = f32[8,128]{1,0:T(8,128)S(1)} collective-permute-done((f32[8,128]{1,0:T(8,128)S(1)}, f32[8,128]{1,0:T(8,128)S(1)}, u32[]{:S(2)}, u32[]{:S(2)}) %collective-permute-start.17) | collective-permute-done | bytes 4128 | tf_op jit(solution)/shard_map/ppermute | solution.py:386
  53.7 1.2 %collective-permute-start.18 = (f32[8,128]{1,0:T(8,128)S(1)}, f32[8,128]{1,0:T(8,128)S(1)}, u32[]{:S(2)}, u32[]{:S(2)}) collective-permute-start(f32[8,128]{1,0:T(8,128)S(1)} %select_maximum_fusion.refs_0_), channel_id=1, source_target_pairs={{0,4},{2,10},{4,0},{6,14},{8,12},{10,2},{12,8},{14,6},{1,5},{3,11}... | collective-permute-start | bytes 12296 | tf_op jit(solution)/shard_map/ppermute | solution.py:404
  54.9 2.5 %collective-permute-start.21 = (f32[8,128]{1,0:T(8,128)S(1)}, f32[8,128]{1,0:T(8,128)S(1)}, u32[]{:S(2)}, u32[]{:S(2)}) collective-permute-start(f32[8,128]{1,0:T(8,128)S(1)} %select_maximum_fusion.refs_0_), channel_id=1, source_target_pairs={{0,12},{2,14},{4,8},{6,10},{8,4},{10,6},{12,0},{14,2},{1,13},{3,15... | collective-permute-start | bytes 12296 | tf_op jit(solution)/shard_map/ppermute | solution.py:405
  57.4 1.1 %shard_map.62 = (f32[128,256]{1,0:T(8,128)S(1)}, f32[128,128]{1,0:T(8,128)S(1)}, f32[8,128]{1,0:T(8,128)S(1)}) custom-call(s32[4]{0:T(128)S(1)} %pad_add_fusion.spot, f32[128,128]{1,0:T(8,128)S(1)} %get-tuple-element.49.mine, f32[128,128]{1,0:T(8,128)S(1)} %collective-permute-done.19.across, f32[256,128]{1,0:T(8,128)S(1)} %get-tuple-element.47.facts), custom_call_target="tpu_custom_call" | custom-call | tf_op jit(solution)/shard_map/pallas_call | solution.py:392
  58.5 0.1 collective-permute-start.20
  58.6 1.8 %collective-permute-done.21.refs_3_ = f32[8,128]{1,0:T(8,128)S(1)} collective-permute-done((f32[8,128]{1,0:T(8,128)S(1)}, f32[8,128]{1,0:T(8,128)S(1)}, u32[]{:S(2)}, u32[]{:S(2)}) %collective-permute-start.21) | collective-permute-done | bytes 4128 | tf_op jit(solution)/shard_map/ppermute | solution.py:405
  60.3 0.8 %shard_map.63 = f32[128,256]{1,0:T(8,128)} custom-call(f32[8,128]{1,0:T(8,128)S(1)} %select_maximum_fusion.refs_0_, f32[8,128]{1,0:T(8,128)S(1)} %collective-permute-done.18.refs_1_, f32[8,128]{1,0:T(8,128)S(1)} %collective-permute-done.20.refs_2_, f32[8,128]{1,0:T(8,128)S(1)} %collective-permute-done.21.refs_3_, f32[8,128]{1,0:T(8,128)S(1)} %get-tuple-element.54.refs_4_, ...), custom_call_target="tpu_custom_call" | custom-call | tf_op jit(solution)/shard_map/pallas_call | solution.py:413
  (15 shorter events, 0.1 us)
Async XLA Ops:
  3.1 5.2 %collective-permute-start.1 = (bf16[16,7424]{1,0:T(8,128)(2,1)S(1)}, bf16[16,7424]{1,0:T(8,128)(2,1)S(1)}, u32[]{:S(2)}, u32[]{:S(2)}) collective-permute-start(bf16[16,7424]{1,0:T(8,128)(2,1)S(1)} %get-tuple-element.32), channel_id=1, source_target_pairs={{0,2},{2,0},{4,6},{6,4},{8,10},{10,8},{12,14},{14,12},{1,3},{3,1},... | collective-permute-start | bytes 712712 | tf_op jit(solution)/shard_map/mate_rows/ppermute | solution.py:315
  3.6 8.8 %collective-permute-start.5 = (bf16[16,7424]{1,0:T(8,128)(2,1)S(1)}, bf16[16,7424]{1,0:T(8,128)(2,1)S(1)}, u32[]{:S(2)}, u32[]{:S(2)}) collective-permute-start(bf16[16,7424]{1,0:T(8,128)(2,1)S(1)} %get-tuple-element.32), channel_id=1, source_target_pairs={{0,3},{2,1},{4,2},{6,0},{8,6},{10,4},{12,10},{14,8},{13,14},{15,12... | collective-permute-start | bytes 712712 | tf_op jit(solution)/shard_map/rows_behind/ppermute | solution.py:297
  6.2 8.6 %collective-permute-start = (bf16[16,7424]{1,0:T(8,128)(2,1)S(1)}, bf16[16,7424]{1,0:T(8,128)(2,1)S(1)}, u32[]{:S(2)}, u32[]{:S(2)}) collective-permute-start(bf16[16,7424]{1,0:T(8,128)(2,1)S(1)} %get-tuple-element.31.refs_0_), channel_id=1, source_target_pairs={{0,4},{2,6},{4,8},{6,10},{8,12},{10,14},{12,13},{14,15},{13,9},{15... | collective-permute-start | bytes 712712 | tf_op jit(solution)/shard_map/rows_ahead/ppermute | solution.py:297
  6.3 11.6 %collective-permute-start.3 = (bf16[16,7424]{1,0:T(8,128)(2,1)S(1)}, bf16[16,7424]{1,0:T(8,128)(2,1)S(1)}, u32[]{:S(2)}, u32[]{:S(2)}) collective-permute-start(bf16[16,7424]{1,0:T(8,128)(2,1)S(1)} %get-tuple-element.31.refs_0_), channel_id=1, source_target_pairs={{0,1},{2,3},{4,0},{6,2},{8,4},{10,6},{12,8},{14,10},{13,12},{15,14... | collective-permute-start | bytes 712712 | tf_op jit(solution)/shard_map/rows_behind/ppermute | solution.py:297
  8.2 11.7 %collective-permute-start.4 = (bf16[16,7424]{1,0:T(8,128)(2,1)S(1)}, bf16[16,7424]{1,0:T(8,128)(2,1)S(1)}, u32[]{:S(2)}, u32[]{:S(2)}) collective-permute-start(bf16[16,7424]{1,0:T(8,128)(2,1)S(1)} %get-tuple-element.32), channel_id=1, source_target_pairs={{0,6},{2,4},{4,10},{6,8},{8,14},{10,12},{12,15},{14,13},{13,11},{1... | collective-permute-start | bytes 712712 | tf_op jit(solution)/shard_map/rows_ahead/ppermute | solution.py:297
  11.5 8.5 %collective-permute-start.6 = (bf16[128,7296]{1,0:T(8,128)(2,1)S(1)}, bf16[128,7296]{1,0:T(8,128)(2,1)S(1)}, u32[]{:S(2)}, u32[]{:S(2)}) collective-permute-start(bf16[128,7296]{1,0:T(8,128)(2,1)S(1)} %get-tuple-element.36), channel_id=1, source_target_pairs={{0,2},{2,0},{4,6},{6,4},{8,10},{10,8},{12,14},{14,12},{1,3},{3,1},... | collective-permute-start | bytes 5603336 | tf_op jit(solution)/shard_map/mate_panel/ppermute | solution.py:328
  12.4 11.5 %collective-permute-start.9 = (bf16[16,7424]{1,0:T(8,128)(2,1)S(1)}, bf16[16,7424]{1,0:T(8,128)(2,1)S(1)}, u32[]{:S(2)}, u32[]{:S(2)}) collective-permute-start(bf16[16,7424]{1,0:T(8,128)(2,1)S(1)} %collective-permute-done.5.refs_5_), channel_id=1, source_target_pairs={{0,1},{2,3},{4,0},{6,2},{8,4},{10,6},{12,8},{14,10},{13,12},{15,14... | collective-permute-start | bytes 712712 | tf_op jit(solution)/shard_map/rows_behind/ppermute | solution.py:297
  13.9 1.0 %copy-start = (f32[7296]{0:T(1024)S(1)}, f32[7296]{0:T(1024)}, u32[]{:S(2)}) copy-start(f32[7296]{0:T(1024)} %param.8) | copy-start | bytes 87556
  14.8 11.0 %collective-permute-start.2 = (bf16[16,7424]{1,0:T(8,128)(2,1)S(1)}, bf16[16,7424]{1,0:T(8,128)(2,1)S(1)}, u32[]{:S(2)}, u32[]{:S(2)}) collective-permute-start(bf16[16,7424]{1,0:T(8,128)(2,1)S(1)} %collective-permute-done.refs_2_), channel_id=1, source_target_pairs={{0,4},{2,6},{4,8},{6,10},{8,12},{10,14},{12,13},{14,15},{13,9},{15... | collective-permute-start | bytes 712712 | tf_op jit(solution)/shard_map/rows_ahead/ppermute | solution.py:297
  18.0 10.2 %collective-permute-start.12 = (bf16[16,7424]{1,0:T(8,128)(2,1)S(1)}, bf16[16,7424]{1,0:T(8,128)(2,1)S(1)}, u32[]{:S(2)}, u32[]{:S(2)}) collective-permute-start(bf16[16,7424]{1,0:T(8,128)(2,1)S(1)} %collective-permute-done.3.refs_3_), channel_id=1, source_target_pairs={{0,1},{2,3},{4,0},{6,2},{8,4},{10,6},{12,8},{14,10},{13,12},{15,14... | collective-permute-start | bytes 712712 | tf_op jit(solution)/shard_map/rows_behind/ppermute | solution.py:297
  19.9 10.2 %collective-permute-start.13 = (bf16[16,7424]{1,0:T(8,128)(2,1)S(1)}, bf16[16,7424]{1,0:T(8,128)(2,1)S(1)}, u32[]{:S(2)}, u32[]{:S(2)}) collective-permute-start(bf16[16,7424]{1,0:T(8,128)(2,1)S(1)} %collective-permute-done.4.refs_4_), channel_id=1, source_target_pairs={{0,4},{2,6},{4,8},{6,10},{8,12},{10,14},{12,13},{14,15},{13,9},{15... | collective-permute-start | bytes 712712 | tf_op jit(solution)/shard_map/rows_ahead/ppermute | solution.py:297
  23.8 9.4 %collective-permute-start.10 = (bf16[16,7424]{1,0:T(8,128)(2,1)S(1)}, bf16[16,7424]{1,0:T(8,128)(2,1)S(1)}, u32[]{:S(2)}, u32[]{:S(2)}) collective-permute-start(bf16[16,7424]{1,0:T(8,128)(2,1)S(1)} %collective-permute-done.9.refs_3_), channel_id=1, source_target_pairs={{0,1},{2,3},{4,0},{6,2},{8,4},{10,6},{12,8},{14,10},{13,12},{15,14... | collective-permute-start | bytes 712712 | tf_op jit(solution)/shard_map/rows_behind/ppermute | solution.py:297
  25.8 9.4 %collective-permute-start.7 = (bf16[16,7424]{1,0:T(8,128)(2,1)S(1)}, bf16[16,7424]{1,0:T(8,128)(2,1)S(1)}, u32[]{:S(2)}, u32[]{:S(2)}) collective-permute-start(bf16[16,7424]{1,0:T(8,128)(2,1)S(1)} %collective-permute-done.2.refs_0_), channel_id=1, source_target_pairs={{0,4},{2,6},{4,8},{6,10},{8,12},{10,14},{12,13},{14,15},{13,9},{15... | collective-permute-start | bytes 712712 | tf_op jit(solution)/shard_map/rows_ahead/ppermute | solution.py:297
  28.1 10.2 %collective-permute-start.14 = (bf16[16,7424]{1,0:T(8,128)(2,1)S(1)}, bf16[16,7424]{1,0:T(8,128)(2,1)S(1)}, u32[]{:S(2)}, u32[]{:S(2)}) collective-permute-start(bf16[16,7424]{1,0:T(8,128)(2,1)S(1)} %collective-permute-done.12.refs_1_), channel_id=1, source_target_pairs={{0,1},{2,3},{4,0},{6,2},{8,4},{10,6},{12,8},{14,10},{13,12},{15,14... | collective-permute-start | bytes 712712 | tf_op jit(solution)/shard_map/rows_behind/ppermute | solution.py:297
  30.1 10.2 %collective-permute-start.15 = (bf16[16,7424]{1,0:T(8,128)(2,1)S(1)}, bf16[16,7424]{1,0:T(8,128)(2,1)S(1)}, u32[]{:S(2)}, u32[]{:S(2)}) collective-permute-start(bf16[16,7424]{1,0:T(8,128)(2,1)S(1)} %collective-permute-done.13.refs_2_), channel_id=1, source_target_pairs={{0,4},{2,6},{4,8},{6,10},{8,12},{10,14},{12,13},{14,15},{13,9},{15... | collective-permute-start | bytes 712712 | tf_op jit(solution)/shard_map/rows_ahead/ppermute | solution.py:297
  33.2 11.2 %collective-permute-start.11 = (bf16[16,7424]{1,0:T(8,128)(2,1)S(1)}, bf16[16,7424]{1,0:T(8,128)(2,1)S(1)}, u32[]{:S(2)}, u32[]{:S(2)}) collective-permute-start(bf16[16,7424]{1,0:T(8,128)(2,1)S(1)} %collective-permute-done.10.refs_7_), channel_id=1, source_target_pairs={{0,1},{2,3},{4,0},{6,2},{8,4},{10,6},{12,8},{14,10},{13,12},{15,14... | collective-permute-start | bytes 712712 | tf_op jit(solution)/shard_map/rows_behind/ppermute | solution.py:297
  35.2 9.3 %collective-permute-start.8 = (bf16[16,7424]{1,0:T(8,128)(2,1)S(1)}, bf16[16,7424]{1,0:T(8,128)(2,1)S(1)}, u32[]{:S(2)}, u32[]{:S(2)}) collective-permute-start(bf16[16,7424]{1,0:T(8,128)(2,1)S(1)} %collective-permute-done.7.refs_4_), channel_id=1, source_target_pairs={{0,4},{2,6},{4,8},{6,10},{8,12},{10,14},{12,13},{14,15},{13,9},{15... | collective-permute-start | bytes 712712 | tf_op jit(solution)/shard_map/rows_ahead/ppermute | solution.py:297
  47.6 1.6 %collective-permute-start.16 = (f32[2,256,128]{2,1,0:T(8,128)S(1)}, f32[2,256,128]{2,1,0:T(8,128)S(1)}, u32[]{:S(2)}, u32[]{:S(2)}) collective-permute-start(f32[2,256,128]{2,1,0:T(8,128)S(1)} %get-tuple-element.46.partial), channel_id=1, source_target_pairs={{0,2},{2,0},{4,6},{6,4},{8,10},{10,8},{12,14},{14,12},{1,3},{3,1},... | collective-permute-start | bytes 786440 | tf_op jit(solution)/shard_map/ppermute | solution.py:373
  50.1 3.6 %collective-permute-start.17 = (f32[8,128]{1,0:T(8,128)S(1)}, f32[8,128]{1,0:T(8,128)S(1)}, u32[]{:S(2)}, u32[]{:S(2)}) collective-permute-start(f32[8,128]{1,0:T(8,128)S(1)} %get-tuple-element.48), channel_id=1, source_target_pairs={{0,1},{1,0},{2,3},{3,2},{4,5},{5,4},{6,7},{7,6},{8,9},{9,8},{10,11... | collective-permute-start | bytes 12296 | tf_op jit(solution)/shard_map/ppermute | solution.py:386
  51.7 5.7 %collective-permute-start.19 = (f32[128,128]{1,0:T(8,128)S(1)}, f32[128,128]{1,0:T(8,128)S(1)}, u32[]{:S(2)}, u32[]{:S(2)}) collective-permute-start(f32[128,128]{1,0:T(8,128)S(1)} %get-tuple-element.51), channel_id=1, source_target_pairs={{0,1},{1,0},{2,3},{3,2},{4,5},{5,4},{6,7},{7,6},{8,9},{9,8},{10,11... | collective-permute-start | bytes 196616 | tf_op jit(solution)/shard_map/ppermute | solution.py:388
  53.7 4.8 %collective-permute-start.18 = (f32[8,128]{1,0:T(8,128)S(1)}, f32[8,128]{1,0:T(8,128)S(1)}, u32[]{:S(2)}, u32[]{:S(2)}) collective-permute-start(f32[8,128]{1,0:T(8,128)S(1)} %select_maximum_fusion.refs_0_), channel_id=1, source_target_pairs={{0,4},{2,10},{4,0},{6,14},{8,12},{10,2},{12,8},{14,6},{1,5},{3,11}... | collective-permute-start | bytes 12296 | tf_op jit(solution)/shard_map/ppermute | solution.py:404
  54.9 5.4 %collective-permute-start.21 = (f32[8,128]{1,0:T(8,128)S(1)}, f32[8,128]{1,0:T(8,128)S(1)}, u32[]{:S(2)}, u32[]{:S(2)}) collective-permute-start(f32[8,128]{1,0:T(8,128)S(1)} %select_maximum_fusion.refs_0_), channel_id=1, source_target_pairs={{0,12},{2,14},{4,8},{6,10},{8,4},{10,6},{12,0},{14,2},{1,13},{3,15... | collective-permute-start | bytes 12296 | tf_op jit(solution)/shard_map/ppermute | solution.py:405
  58.5 1.9 %collective-permute-start.20 = (f32[8,128]{1,0:T(8,128)S(1)}, f32[8,128]{1,0:T(8,128)S(1)}, u32[]{:S(2)}, u32[]{:S(2)}) collective-permute-start(f32[8,128]{1,0:T(8,128)S(1)} %collective-permute-done.18.refs_1_), channel_id=1, source_target_pairs={{0,2},{2,0},{4,6},{6,4},{8,10},{10,8},{12,14},{14,12},{1,3},{3,1},... | collective-permute-start | bytes 12296 | tf_op jit(solution)/shard_map/ppermute | solution.py:407

commit v19 on v15

--- a/solution.py
+++ b/solution.py
@@ -193,15 +193,21 @@
     return jnp.max(jnp.where(match, 1.0, 0.0), axis=1, keepdims=True) > 0.0
 
 
-def chip_kernel(search, spot, partial, mate, facts, mine, across, stats):
-    group, core, place = spot[0], spot[2], spot[3]
+def mask_kernel(search, spot, facts, masks):
+    core, place = spot[2], spot[3]
+    for block in range(2):
+        named = names_block(facts[...], search, place - core + block)
+        masks[block] = jnp.broadcast_to(jnp.where(named, 1.0, 0.0), masks.shape[1:])
+
+
+def chip_kernel(spot, partial, mate, masks, mine, across, stats):
+    group, core = spot[0], spot[2]
     count = mine.shape[0]
     lane = lax.broadcasted_iota(jnp.int32, (count, LANES), 1)
     pairs = []
     for relative in range(2):
         side = group if relative == 0 else 1 - group
         window = pl.ds(pl.multiple_of(side * count, count), count)
-        listed = facts[window, :]
         masked = []
         for crossed in range(2):
             block = core if crossed == 0 else 1 - core
@@ -209,8 +215,7 @@
             if crossed == 0:
                 out = mine if relative == 0 else across
                 out[...] = scores
-            named = names_block(listed, search, place - core + block)
-            masked.append(jnp.where(named, scores, FLOOR))
+            masked.append(jnp.where(masks[block, window, :] > 0.0, scores, FLOOR))
         top = jnp.max(jnp.maximum(*masked), axis=1, keepdims=True)
         terms = [jnp.where(m > FLOOR, jnp.exp(m - top), 0.0) for m in masked]
         total = jnp.sum(terms[0] + terms[1], axis=1, keepdims=True)
@@ -373,8 +378,15 @@
     )
 
     mate_partial = lax.ppermute(partial, "orient", mate_pairs)
+    masks = pl.pallas_call(
+        functools.partial(mask_kernel, local_search),
+        in_specs=[smem, vmem],
+        out_specs=vmem,
+        out_shape=jax.ShapeDtypeStruct((2, 2 * everyone, orientations), jnp.float32),
+        compiler_params=params,
+    )(spot, all_facts)
     mine, across, stats = pl.pallas_call(
-        functools.partial(chip_kernel, local_search),
+        chip_kernel,
         in_specs=[smem] + [vmem] * 3,
         out_specs=[vmem] * 3,
         out_shape=[
@@ -383,7 +395,7 @@
             jax.ShapeDtypeStruct((8, everyone), jnp.float32),
         ],
         compiler_params=params,
-    )(spot, partial, mate_partial, all_facts)
+    )(spot, partial, mate_partial, masks)
 
     x_stats = lax.ppermute(stats, "cls", x_pairs)
     across, _ = lax.optimization_barrier((across, stats))

time: 61.3 us -> 61.2 us (level)
  waiting for transfers between devices: 15.8 us -> 15.1 us
    ppermute x1, waiting for transfers between devices: 1.52 us -> 0.83 us  [chip_shards(): mate_partial = lax.ppermute(partial, 'orient', mate_pairs)]
    pallas_call x1 -> x2, Pallas kernels: 0.88 us -> 1.48 us  [the longest x1 0.79 us: chip_shards(): pl.pallas_call(chip_kernel, in_specs=[smem] + [vmem] * 3, out_specs=[vmem...]
  transfers between devices with their start and end apart: 22 -> 22, of which waited for: 10 -> 10; matrix products, arithmetic and copies ran while one was open for 4% -> 4% of each run, Pallas kernels for 16% -> 17%
where the time goes in v19:
time: 61.2 us; the launch traced here: 60.9 us
  starting transfers between devices  24.9 us (41%)
  Pallas kernels  15.9 us (26%)
  waiting for transfers between devices  15.1 us (25%)
  local copies, waits for them, and re-layouts  3.52 us (6%)
  other arithmetic  1.45 us (2%)
    ppermute x14, starting transfers between devices, forward(): return lax.ppermute(values, ('orient', 'cls'), pairs)  17.1 us
    pallas_call x3, Pallas kernels, score_call(): pl.pallas_call(kernel, in_specs=[pl.BlockSpec(memory_space=pltpu.SMEM)] +...  11 us
    ppermute x14, waiting for transfers between devices, forward(): return lax.ppermute(values, ('orient', 'cls'), pairs)  10.9 us
    ppermute x1, starting transfers between devices, chip_shards(): far = lax.ppermute(pair, 'orient', [(d, d ^ 6) for d in range(devices)])  2.47 us
    optimization_barrier x1, local copies, waits for them, and re-layouts, chip_shards(): _, panels = lax.optimization_barrier((kept, panels))  2.42 us
    ppermute x1, waiting for transfers between devices, chip_shards(): far = lax.ppermute(pair, 'orient', [(d, d ^ 6) for d in range(devices)])  1.77 us
    ppermute x1, starting transfers between devices, chip_shards(): x_stats = lax.ppermute(stats, 'cls', x_pairs)  1.61 us
    ppermute x1, waiting for transfers between devices, chip_shards(): x_stats = lax.ppermute(stats, 'cls', x_pairs)  1.58 us
  transfers between devices with their start and end apart: 22, of which 10 were waited for; matrix products, arithmetic and copies ran while one was open for 4% of the time, Pallas kernels for 17%

profile of v19, /device:TPU:0, one launch (start us, length us, event | category | flops | bytes accessed | tf_op | source)
XLA Modules:
  0.0 60.9 jit_solution(11753984457621284660)
XLA Ops:
  0.0 1.1 %copy.11 = bf16[1,16,2,7296]{3,1,2,0:T(8,128)(2,1)S(1)} copy(bf16[1,16,2,7296]{3,2,1,0:T(2,128)(2,1)} %param.5) | data formatting | bytes 933888 | tf_op args[0]
  1.1 0.7 %convert_bitcast_fusion = bf16[4,16]{1,0:T(4,128)(2,1)S(1)} fusion(s32[1,16,4]{1,2,0:T(4,128)} %param.7), kind=kLoop, calls=%fused_computation.12 | loop fusion | flops 64 | bytes 384 | tf_op jit(solution)/shard_map/convert_element_type | solution.py:308
  1.8 0.7 %fusion.5.facts = bf16[16,128]{1,0:T(8,128)(2,1)S(1)} fusion(bf16[4,16]{1,0:T(4,128)(2,1)S(1)} %convert_bitcast_fusion, bf16[1,16]{1,0:T(2,128)(2,1)} %param.6), kind=kLoop, calls=%fused_computation.9 | loop fusion | flops 22528 | bytes 4256 | tf_op jit(solution)/shard_map/concatenate | solution.py:308
  2.4 0.1 pad_add_fusion.spot
  2.5 0.6 shard_map.55
  3.1 2.4 %collective-permute-start.5 = (bf16[16,7424]{1,0:T(8,128)(2,1)S(1)}, bf16[16,7424]{1,0:T(8,128)(2,1)S(1)}, u32[]{:S(2)}, u32[]{:S(2)}) collective-permute-start(bf16[16,7424]{1,0:T(8,128)(2,1)S(1)} %get-tuple-element.37), channel_id=1, source_target_pairs={{0,3},{2,1},{4,2},{6,0},{8,6},{10,4},{12,10},{14,8},{13,14},{15,12... | collective-permute-start | bytes 712712 | tf_op jit(solution)/shard_map/rows_behind/ppermute | solution.py:302
  5.5 0.7 %collective-permute-start = (bf16[16,7424]{1,0:T(8,128)(2,1)S(1)}, bf16[16,7424]{1,0:T(8,128)(2,1)S(1)}, u32[]{:S(2)}, u32[]{:S(2)}) collective-permute-start(bf16[16,7424]{1,0:T(8,128)(2,1)S(1)} %get-tuple-element.32.refs_0_), channel_id=1, source_target_pairs={{0,4},{2,6},{4,8},{6,10},{8,12},{10,14},{12,13},{14,15},{13,9},{15... | collective-permute-start | bytes 712712 | tf_op jit(solution)/shard_map/rows_ahead/ppermute | solution.py:302
  6.2 1.3 %collective-permute-start.3 = (bf16[16,7424]{1,0:T(8,128)(2,1)S(1)}, bf16[16,7424]{1,0:T(8,128)(2,1)S(1)}, u32[]{:S(2)}, u32[]{:S(2)}) collective-permute-start(bf16[16,7424]{1,0:T(8,128)(2,1)S(1)} %get-tuple-element.32.refs_0_), channel_id=1, source_target_pairs={{0,1},{2,3},{4,0},{6,2},{8,4},{10,6},{12,8},{14,10},{13,12},{15,14... | collective-permute-start | bytes 712712 | tf_op jit(solution)/shard_map/rows_behind/ppermute | solution.py:302
  7.5 0.1 collective-permute-start.4
  7.6 2.4 %copy.10 = bf16[1,1,128,2,7296]{4,2,3,1,0:T(8,128)(2,1)S(1)} copy(bf16[1,1,128,2,7296]{4,3,2,1,0:T(2,128)(2,1)} %param.9) | data formatting | bytes 7471104 | tf_op jit(solution)/shard_map/optimization_barrier | solution.py:319
  10.1 0.8 %shard_map.56 = (bf16[128,7296]{1,0:T(8,128)(2,1)S(1)}, bf16[128,7296]{1,0:T(8,128)(2,1)S(1)}) custom-call(s32[4]{0:T(128)S(1)} %pad_add_fusion.spot, bf16[2,128,7296]{2,1,0:T(8,128)(2,1)S(1)} %bitcast.19), custom_call_target="tpu_custom_call" | custom-call | tf_op jit(solution)/shard_map/pallas_call | solution.py:322
  10.9 0.8 %collective-permute-start.6 = (bf16[128,7296]{1,0:T(8,128)(2,1)S(1)}, bf16[128,7296]{1,0:T(8,128)(2,1)S(1)}, u32[]{:S(2)}, u32[]{:S(2)}) collective-permute-start(bf16[128,7296]{1,0:T(8,128)(2,1)S(1)} %get-tuple-element.38), channel_id=1, source_target_pairs={{0,2},{2,0},{4,6},{6,4},{8,10},{10,8},{12,14},{14,12},{1,3},{3,1},... | collective-permute-start | bytes 5603336 | tf_op jit(solution)/shard_map/mate_panel/ppermute | solution.py:330
  11.7 0.0 collective-permute-done.5.refs_5_
  11.7 1.2 %collective-permute-start.2 = (bf16[16,7424]{1,0:T(8,128)(2,1)S(1)}, bf16[16,7424]{1,0:T(8,128)(2,1)S(1)}, u32[]{:S(2)}, u32[]{:S(2)}) collective-permute-start(bf16[16,7424]{1,0:T(8,128)(2,1)S(1)} %get-tuple-element.37), channel_id=1, source_target_pairs={{0,2},{2,0},{4,6},{6,4},{8,10},{10,8},{12,14},{14,12},{1,3},{3,1},... | collective-permute-start | bytes 712712 | tf_op jit(solution)/shard_map/mate_rows/ppermute | solution.py:370
  12.9 0.1 shard_map.57.refs_8_.refs_10_.refs_4_
  13.0 1.2 %collective-permute-done.refs_2_ = bf16[16,7424]{1,0:T(8,128)(2,1)S(1)} collective-permute-done((bf16[16,7424]{1,0:T(8,128)(2,1)S(1)}, bf16[16,7424]{1,0:T(8,128)(2,1)S(1)}, u32[]{:S(2)}, u32[]{:S(2)}) %collective-permute-start) | collective-permute-done | bytes 237600 | tf_op jit(solution)/shard_map/rows_ahead/ppermute | solution.py:302
  14.2 1.6 %collective-permute-start.9 = (bf16[16,7424]{1,0:T(8,128)(2,1)S(1)}, bf16[16,7424]{1,0:T(8,128)(2,1)S(1)}, u32[]{:S(2)}, u32[]{:S(2)}) collective-permute-start(bf16[16,7424]{1,0:T(8,128)(2,1)S(1)} %collective-permute-done.5.refs_5_), channel_id=1, source_target_pairs={{0,1},{2,3},{4,0},{6,2},{8,4},{10,6},{12,8},{14,10},{13,12},{15,14... | collective-permute-start | bytes 712712 | tf_op jit(solution)/shard_map/rows_behind/ppermute | solution.py:302
  15.7 1.3 %collective-permute-start.1 = (bf16[16,7424]{1,0:T(8,128)(2,1)S(1)}, bf16[16,7424]{1,0:T(8,128)(2,1)S(1)}, u32[]{:S(2)}, u32[]{:S(2)}) collective-permute-start(bf16[16,7424]{1,0:T(8,128)(2,1)S(1)} %collective-permute-done.refs_2_), channel_id=1, source_target_pairs={{0,4},{2,6},{4,8},{6,10},{8,12},{10,14},{12,13},{14,15},{13,9},{15... | collective-permute-start | bytes 712712 | tf_op jit(solution)/shard_map/rows_ahead/ppermute | solution.py:302
  17.1 0.6 %collective-permute-done.3.refs_3_ = bf16[16,7424]{1,0:T(8,128)(2,1)S(1)} collective-permute-done((bf16[16,7424]{1,0:T(8,128)(2,1)S(1)}, bf16[16,7424]{1,0:T(8,128)(2,1)S(1)}, u32[]{:S(2)}, u32[]{:S(2)}) %collective-permute-start.3) | collective-permute-done | bytes 237600 | tf_op jit(solution)/shard_map/rows_behind/ppermute | solution.py:302
  17.7 1.6 %collective-permute-start.12 = (bf16[16,7424]{1,0:T(8,128)(2,1)S(1)}, bf16[16,7424]{1,0:T(8,128)(2,1)S(1)}, u32[]{:S(2)}, u32[]{:S(2)}) collective-permute-start(bf16[16,7424]{1,0:T(8,128)(2,1)S(1)} %collective-permute-done.3.refs_3_), channel_id=1, source_target_pairs={{0,1},{2,3},{4,0},{6,2},{8,4},{10,6},{12,8},{14,10},{13,12},{15,14... | collective-permute-start | bytes 712712 | tf_op jit(solution)/shard_map/rows_behind/ppermute | solution.py:302
  19.3 0.5 collective-permute-start.13
  19.7 3.8 %shard_map.58 = (f32[96,128]{1,0:T(8,128)S(1)}, f32[96,128]{1,0:T(8,128)S(1)}, f32[96,128]{1,0:T(8,128)S(1)}) custom-call(s32[4]{0:T(128)S(1)} %pad_add_fusion.spot, bf16[16,7424]{1,0:T(8,128)(2,1)S(1)} %get-tuple-element.32.refs_0_, bf16[16,7424]{1,0:T(8,128)(2,1)S(1)} %collective-permute-done.2.refs_1_, bf16[16,7424]{1,0:T(8,128)(2,1)S(1)} %collective-permute-done.refs_2_, ...), custom_call_target="tpu_custom_call" | custom-call | flops 956301312 | bytes 5136384 | tf_op jit(solution)/shard_map/pallas_call | solution.py:175
  23.6 1.6 %collective-permute-start.10 = (bf16[16,7424]{1,0:T(8,128)(2,1)S(1)}, bf16[16,7424]{1,0:T(8,128)(2,1)S(1)}, u32[]{:S(2)}, u32[]{:S(2)}) collective-permute-start(bf16[16,7424]{1,0:T(8,128)(2,1)S(1)} %collective-permute-done.9.refs_3_), channel_id=1, source_target_pairs={{0,1},{2,3},{4,0},{6,2},{8,4},{10,6},{12,8},{14,10},{13,12},{15,14... | collective-permute-start | bytes 712712 | tf_op jit(solution)/shard_map/rows_behind/ppermute | solution.py:302
  25.2 0.5 collective-permute-start.7
  25.7 2.3 %collective-permute-done.12.refs_1_ = bf16[16,7424]{1,0:T(8,128)(2,1)S(1)} collective-permute-done((bf16[16,7424]{1,0:T(8,128)(2,1)S(1)}, bf16[16,7424]{1,0:T(8,128)(2,1)S(1)}, u32[]{:S(2)}, u32[]{:S(2)}) %collective-permute-start.12) | collective-permute-done | bytes 237600 | tf_op jit(solution)/shard_map/rows_behind/ppermute | solution.py:302
  28.0 1.6 %collective-permute-start.14 = (bf16[16,7424]{1,0:T(8,128)(2,1)S(1)}, bf16[16,7424]{1,0:T(8,128)(2,1)S(1)}, u32[]{:S(2)}, u32[]{:S(2)}) collective-permute-start(bf16[16,7424]{1,0:T(8,128)(2,1)S(1)} %collective-permute-done.12.refs_1_), channel_id=1, source_target_pairs={{0,1},{2,3},{4,0},{6,2},{8,4},{10,6},{12,8},{14,10},{13,12},{15,14... | collective-permute-start | bytes 712712 | tf_op jit(solution)/shard_map/rows_behind/ppermute | solution.py:302
  29.6 1.2 %collective-permute-start.15 = (bf16[16,7424]{1,0:T(8,128)(2,1)S(1)}, bf16[16,7424]{1,0:T(8,128)(2,1)S(1)}, u32[]{:S(2)}, u32[]{:S(2)}) collective-permute-start(bf16[16,7424]{1,0:T(8,128)(2,1)S(1)} %collective-permute-done.13.refs_2_), channel_id=1, source_target_pairs={{0,4},{2,6},{4,8},{6,10},{8,12},{10,14},{12,13},{14,15},{13,9},{15... | collective-permute-start | bytes 712712 | tf_op jit(solution)/shard_map/rows_ahead/ppermute | solution.py:302
  30.7 2.3 %collective-permute-done.10.refs_7_ = bf16[16,7424]{1,0:T(8,128)(2,1)S(1)} collective-permute-done((bf16[16,7424]{1,0:T(8,128)(2,1)S(1)}, bf16[16,7424]{1,0:T(8,128)(2,1)S(1)}, u32[]{:S(2)}, u32[]{:S(2)}) %collective-permute-start.10) | collective-permute-done | bytes 237600 | tf_op jit(solution)/shard_map/rows_behind/ppermute | solution.py:302
  33.1 1.6 %collective-permute-start.11 = (bf16[16,7424]{1,0:T(8,128)(2,1)S(1)}, bf16[16,7424]{1,0:T(8,128)(2,1)S(1)}, u32[]{:S(2)}, u32[]{:S(2)}) collective-permute-start(bf16[16,7424]{1,0:T(8,128)(2,1)S(1)} %collective-permute-done.10.refs_7_), channel_id=1, source_target_pairs={{0,1},{2,3},{4,0},{6,2},{8,4},{10,6},{12,8},{14,10},{13,12},{15,14... | collective-permute-start | bytes 712712 | tf_op jit(solution)/shard_map/rows_behind/ppermute | solution.py:302
  34.7 1.2 %collective-permute-start.8 = (bf16[16,7424]{1,0:T(8,128)(2,1)S(1)}, bf16[16,7424]{1,0:T(8,128)(2,1)S(1)}, u32[]{:S(2)}, u32[]{:S(2)}) collective-permute-start(bf16[16,7424]{1,0:T(8,128)(2,1)S(1)} %collective-permute-done.7.refs_4_), channel_id=1, source_target_pairs={{0,4},{2,6},{4,8},{6,10},{8,12},{10,14},{12,13},{14,15},{13,9},{15... | collective-permute-start | bytes 712712 | tf_op jit(solution)/shard_map/rows_ahead/ppermute | solution.py:302
  35.8 2.3 %collective-permute-done.14.refs_5_ = bf16[16,7424]{1,0:T(8,128)(2,1)S(1)} collective-permute-done((bf16[16,7424]{1,0:T(8,128)(2,1)S(1)}, bf16[16,7424]{1,0:T(8,128)(2,1)S(1)}, u32[]{:S(2)}, u32[]{:S(2)}) %collective-permute-start.14) | collective-permute-done | bytes 237600 | tf_op jit(solution)/shard_map/rows_behind/ppermute | solution.py:302
  38.2 1.6 %collective-permute-done.15.refs_6_ = bf16[16,7424]{1,0:T(8,128)(2,1)S(1)} collective-permute-done((bf16[16,7424]{1,0:T(8,128)(2,1)S(1)}, bf16[16,7424]{1,0:T(8,128)(2,1)S(1)}, u32[]{:S(2)}, u32[]{:S(2)}) %collective-permute-start.15) | collective-permute-done | bytes 237600 | tf_op jit(solution)/shard_map/rows_ahead/ppermute | solution.py:302
  39.7 4.1 %shard_map.59 = (f32[128,128]{1,0:T(8,128)S(1)}, f32[128,128]{1,0:T(8,128)S(1)}, f32[128,128]{1,0:T(8,128)S(1)}) custom-call(s32[4]{0:T(128)S(1)} %pad_add_fusion.spot, bf16[16,7424]{1,0:T(8,128)(2,1)S(1)} %collective-permute-done.1.refs_0_, bf16[16,7424]{1,0:T(8,128)(2,1)S(1)} %collective-permute-done.12.refs_1_, ...), custom_call_target="tpu_custom_call" | custom-call | flops 956301312 | bytes 5603328 | tf_op jit(solution)/shard_map/pallas_call | solution.py:175
  43.9 0.5 collective-permute-done.8.refs_0_
  44.4 3.1 %shard_map.60 = (f32[2,256,128]{2,1,0:T(8,128)S(1)}, f32[256,128]{1,0:T(8,128)S(1)}) custom-call(s32[4]{0:T(128)S(1)} %pad_add_fusion.spot, bf16[16,7424]{1,0:T(8,128)(2,1)S(1)} %collective-permute-done.8.refs_0_, bf16[16,7424]{1,0:T(8,128)(2,1)S(1)} %collective-permute-done.11.refs_1_, f32[1,7296]{1,0:T(1,128)S(1)} %broadcast_in_dim.3.refs_6_.refs_8_.refs_2_, ...), custom_call_target="tpu_custom_call" | custom-call | flops 956301312 | bytes 4202496 | tf_op jit(solution)/shard_map/pallas_call | solution.py:175
  47.5 0.0 collective-permute-start.16
  47.6 0.7 %shard_map.61.masks = f32[2,256,128]{2,1,0:T(8,128)S(1)} custom-call(s32[4]{0:T(128)S(1)} %pad_add_fusion.spot, f32[256,128]{1,0:T(8,128)S(1)} %get-tuple-element.49.facts), custom_call_target="tpu_custom_call" | custom-call | tf_op jit(solution)/shard_map/pallas_call | solution.py:381
  48.3 0.8 %collective-permute-done.16.mate = f32[2,256,128]{2,1,0:T(8,128)S(1)} collective-permute-done((f32[2,256,128]{2,1,0:T(8,128)S(1)}, f32[2,256,128]{2,1,0:T(8,128)S(1)}, u32[]{:S(2)}, u32[]{:S(2)}) %collective-permute-start.16) | collective-permute-done | bytes 262176 | tf_op jit(solution)/shard_map/ppermute | solution.py:380
  49.1 0.8 %shard_map.62 = (f32[128,128]{1,0:T(8,128)S(1)}, f32[128,128]{1,0:T(8,128)S(1)}, f32[8,128]{1,0:T(8,128)S(1)}) custom-call(s32[4]{0:T(128)S(1)} %pad_add_fusion.spot, f32[2,256,128]{2,1,0:T(8,128)S(1)} %get-tuple-element.48.partial, f32[2,256,128]{2,1,0:T(8,128)S(1)} %collective-permute-done.16.mate, f32[2,256,128]{2,1,0:T(8,128)S(1)} %shard_map.61.masks), custom_call_target="tpu_custom_call" | custom-call | tf_op jit(solution)/shard_map/pallas_call | solution.py:388
  49.9 1.6 %collective-permute-start.17 = (f32[8,128]{1,0:T(8,128)S(1)}, f32[8,128]{1,0:T(8,128)S(1)}, u32[]{:S(2)}, u32[]{:S(2)}) collective-permute-start(f32[8,128]{1,0:T(8,128)S(1)} %get-tuple-element.50), channel_id=1, source_target_pairs={{0,1},{1,0},{2,3},{3,2},{4,5},{5,4},{6,7},{7,6},{8,9},{9,8},{10,11... | collective-permute-start | bytes 12296 | tf_op jit(solution)/shard_map/ppermute | solution.py:400
  51.5 0.4 collective-permute-start.19
  52.0 1.6 %collective-permute-done.17 = f32[8,128]{1,0:T(8,128)S(1)} collective-permute-done((f32[8,128]{1,0:T(8,128)S(1)}, f32[8,128]{1,0:T(8,128)S(1)}, u32[]{:S(2)}, u32[]{:S(2)}) %collective-permute-start.17) | collective-permute-done | bytes 4128 | tf_op jit(solution)/shard_map/ppermute | solution.py:400
  53.6 1.2 %collective-permute-start.18 = (f32[8,128]{1,0:T(8,128)S(1)}, f32[8,128]{1,0:T(8,128)S(1)}, u32[]{:S(2)}, u32[]{:S(2)}) collective-permute-start(f32[8,128]{1,0:T(8,128)S(1)} %select_maximum_fusion.refs_0_), channel_id=1, source_target_pairs={{0,4},{2,10},{4,0},{6,14},{8,12},{10,2},{12,8},{14,6},{1,5},{3,11}... | collective-permute-start | bytes 12296 | tf_op jit(solution)/shard_map/ppermute | solution.py:418
  54.8 2.5 %collective-permute-start.21 = (f32[8,128]{1,0:T(8,128)S(1)}, f32[8,128]{1,0:T(8,128)S(1)}, u32[]{:S(2)}, u32[]{:S(2)}) collective-permute-start(f32[8,128]{1,0:T(8,128)S(1)} %select_maximum_fusion.refs_0_), channel_id=1, source_target_pairs={{0,12},{2,14},{4,8},{6,10},{8,4},{10,6},{12,0},{14,2},{1,13},{3,15... | collective-permute-start | bytes 12296 | tf_op jit(solution)/shard_map/ppermute | solution.py:419
  57.2 1.1 %shard_map.63 = (f32[128,256]{1,0:T(8,128)S(1)}, f32[128,128]{1,0:T(8,128)S(1)}, f32[8,128]{1,0:T(8,128)S(1)}) custom-call(s32[4]{0:T(128)S(1)} %pad_add_fusion.spot, f32[128,128]{1,0:T(8,128)S(1)} %get-tuple-element.51.mine, f32[128,128]{1,0:T(8,128)S(1)} %collective-permute-done.19.across, f32[256,128]{1,0:T(8,128)S(1)} %get-tuple-element.49.facts), custom_call_target="tpu_custom_call" | custom-call | tf_op jit(solution)/shard_map/pallas_call | solution.py:406
  58.3 0.1 collective-permute-start.20
  58.4 1.8 %collective-permute-done.21.refs_3_ = f32[8,128]{1,0:T(8,128)S(1)} collective-permute-done((f32[8,128]{1,0:T(8,128)S(1)}, f32[8,128]{1,0:T(8,128)S(1)}, u32[]{:S(2)}, u32[]{:S(2)}) %collective-permute-start.21) | collective-permute-done | bytes 4128 | tf_op jit(solution)/shard_map/ppermute | solution.py:419
  60.2 0.8 %shard_map.64 = f32[128,256]{1,0:T(8,128)} custom-call(f32[8,128]{1,0:T(8,128)S(1)} %select_maximum_fusion.refs_0_, f32[8,128]{1,0:T(8,128)S(1)} %collective-permute-done.18.refs_1_, f32[8,128]{1,0:T(8,128)S(1)} %collective-permute-done.20.refs_2_, f32[8,128]{1,0:T(8,128)S(1)} %collective-permute-done.21.refs_3_, f32[8,128]{1,0:T(8,128)S(1)} %get-tuple-element.56.refs_4_, ...), custom_call_target="tpu_custom_call" | custom-call | tf_op jit(solution)/shard_map/pallas_call | solution.py:427
  (16 shorter events, 0.1 us)
Async XLA Ops:
  3.1 8.6 %collective-permute-start.5 = (bf16[16,7424]{1,0:T(8,128)(2,1)S(1)}, bf16[16,7424]{1,0:T(8,128)(2,1)S(1)}, u32[]{:S(2)}, u32[]{:S(2)}) collective-permute-start(bf16[16,7424]{1,0:T(8,128)(2,1)S(1)} %get-tuple-element.37), channel_id=1, source_target_pairs={{0,3},{2,1},{4,2},{6,0},{8,6},{10,4},{12,10},{14,8},{13,14},{15,12... | collective-permute-start | bytes 712712 | tf_op jit(solution)/shard_map/rows_behind/ppermute | solution.py:302
  5.5 8.7 %collective-permute-start = (bf16[16,7424]{1,0:T(8,128)(2,1)S(1)}, bf16[16,7424]{1,0:T(8,128)(2,1)S(1)}, u32[]{:S(2)}, u32[]{:S(2)}) collective-permute-start(bf16[16,7424]{1,0:T(8,128)(2,1)S(1)} %get-tuple-element.32.refs_0_), channel_id=1, source_target_pairs={{0,4},{2,6},{4,8},{6,10},{8,12},{10,14},{12,13},{14,15},{13,9},{15... | collective-permute-start | bytes 712712 | tf_op jit(solution)/shard_map/rows_ahead/ppermute | solution.py:302
  6.2 11.5 %collective-permute-start.3 = (bf16[16,7424]{1,0:T(8,128)(2,1)S(1)}, bf16[16,7424]{1,0:T(8,128)(2,1)S(1)}, u32[]{:S(2)}, u32[]{:S(2)}) collective-permute-start(bf16[16,7424]{1,0:T(8,128)(2,1)S(1)} %get-tuple-element.32.refs_0_), channel_id=1, source_target_pairs={{0,1},{2,3},{4,0},{6,2},{8,4},{10,6},{12,8},{14,10},{13,12},{15,14... | collective-permute-start | bytes 712712 | tf_op jit(solution)/shard_map/rows_behind/ppermute | solution.py:302
  7.5 11.7 %collective-permute-start.4 = (bf16[16,7424]{1,0:T(8,128)(2,1)S(1)}, bf16[16,7424]{1,0:T(8,128)(2,1)S(1)}, u32[]{:S(2)}, u32[]{:S(2)}) collective-permute-start(bf16[16,7424]{1,0:T(8,128)(2,1)S(1)} %get-tuple-element.37), channel_id=1, source_target_pairs={{0,6},{2,4},{4,10},{6,8},{8,14},{10,12},{12,15},{14,13},{13,11},{1... | collective-permute-start | bytes 712712 | tf_op jit(solution)/shard_map/rows_ahead/ppermute | solution.py:302
  10.9 8.9 %collective-permute-start.6 = (bf16[128,7296]{1,0:T(8,128)(2,1)S(1)}, bf16[128,7296]{1,0:T(8,128)(2,1)S(1)}, u32[]{:S(2)}, u32[]{:S(2)}) collective-permute-start(bf16[128,7296]{1,0:T(8,128)(2,1)S(1)} %get-tuple-element.38), channel_id=1, source_target_pairs={{0,2},{2,0},{4,6},{6,4},{8,10},{10,8},{12,14},{14,12},{1,3},{3,1},... | collective-permute-start | bytes 5603336 | tf_op jit(solution)/shard_map/mate_panel/ppermute | solution.py:330
  11.7 4.1 %collective-permute-start.2 = (bf16[16,7424]{1,0:T(8,128)(2,1)S(1)}, bf16[16,7424]{1,0:T(8,128)(2,1)S(1)}, u32[]{:S(2)}, u32[]{:S(2)}) collective-permute-start(bf16[16,7424]{1,0:T(8,128)(2,1)S(1)} %get-tuple-element.37), channel_id=1, source_target_pairs={{0,2},{2,0},{4,6},{6,4},{8,10},{10,8},{12,14},{14,12},{1,3},{3,1},... | collective-permute-start | bytes 712712 | tf_op jit(solution)/shard_map/mate_rows/ppermute | solution.py:370
  12.9 4.2 %copy-start = (f32[7296]{0:T(1024)S(1)}, f32[7296]{0:T(1024)}, u32[]{:S(2)}) copy-start(f32[7296]{0:T(1024)} %param.8) | copy-start | bytes 87556
  14.2 9.4 %collective-permute-start.9 = (bf16[16,7424]{1,0:T(8,128)(2,1)S(1)}, bf16[16,7424]{1,0:T(8,128)(2,1)S(1)}, u32[]{:S(2)}, u32[]{:S(2)}) collective-permute-start(bf16[16,7424]{1,0:T(8,128)(2,1)S(1)} %collective-permute-done.5.refs_5_), channel_id=1, source_target_pairs={{0,1},{2,3},{4,0},{6,2},{8,4},{10,6},{12,8},{14,10},{13,12},{15,14... | collective-permute-start | bytes 712712 | tf_op jit(solution)/shard_map/rows_behind/ppermute | solution.py:302
  15.7 9.4 %collective-permute-start.1 = (bf16[16,7424]{1,0:T(8,128)(2,1)S(1)}, bf16[16,7424]{1,0:T(8,128)(2,1)S(1)}, u32[]{:S(2)}, u32[]{:S(2)}) collective-permute-start(bf16[16,7424]{1,0:T(8,128)(2,1)S(1)} %collective-permute-done.refs_2_), channel_id=1, source_target_pairs={{0,4},{2,6},{4,8},{6,10},{8,12},{10,14},{12,13},{14,15},{13,9},{15... | collective-permute-start | bytes 712712 | tf_op jit(solution)/shard_map/rows_ahead/ppermute | solution.py:302
  17.7 10.3 %collective-permute-start.12 = (bf16[16,7424]{1,0:T(8,128)(2,1)S(1)}, bf16[16,7424]{1,0:T(8,128)(2,1)S(1)}, u32[]{:S(2)}, u32[]{:S(2)}) collective-permute-start(bf16[16,7424]{1,0:T(8,128)(2,1)S(1)} %collective-permute-done.3.refs_3_), channel_id=1, source_target_pairs={{0,1},{2,3},{4,0},{6,2},{8,4},{10,6},{12,8},{14,10},{13,12},{15,14... | collective-permute-start | bytes 712712 | tf_op jit(solution)/shard_map/rows_behind/ppermute | solution.py:302
  19.3 10.3 %collective-permute-start.13 = (bf16[16,7424]{1,0:T(8,128)(2,1)S(1)}, bf16[16,7424]{1,0:T(8,128)(2,1)S(1)}, u32[]{:S(2)}, u32[]{:S(2)}) collective-permute-start(bf16[16,7424]{1,0:T(8,128)(2,1)S(1)} %collective-permute-done.4.refs_4_), channel_id=1, source_target_pairs={{0,4},{2,6},{4,8},{6,10},{8,12},{10,14},{12,13},{14,15},{13,9},{15... | collective-permute-start | bytes 712712 | tf_op jit(solution)/shard_map/rows_ahead/ppermute | solution.py:302
  23.6 9.5 %collective-permute-start.10 = (bf16[16,7424]{1,0:T(8,128)(2,1)S(1)}, bf16[16,7424]{1,0:T(8,128)(2,1)S(1)}, u32[]{:S(2)}, u32[]{:S(2)}) collective-permute-start(bf16[16,7424]{1,0:T(8,128)(2,1)S(1)} %collective-permute-done.9.refs_3_), channel_id=1, source_target_pairs={{0,1},{2,3},{4,0},{6,2},{8,4},{10,6},{12,8},{14,10},{13,12},{15,14... | collective-permute-start | bytes 712712 | tf_op jit(solution)/shard_map/rows_behind/ppermute | solution.py:302
  25.2 9.5 %collective-permute-start.7 = (bf16[16,7424]{1,0:T(8,128)(2,1)S(1)}, bf16[16,7424]{1,0:T(8,128)(2,1)S(1)}, u32[]{:S(2)}, u32[]{:S(2)}) collective-permute-start(bf16[16,7424]{1,0:T(8,128)(2,1)S(1)} %collective-permute-done.1.refs_0_), channel_id=1, source_target_pairs={{0,4},{2,6},{4,8},{6,10},{8,12},{10,14},{12,13},{14,15},{13,9},{15... | collective-permute-start | bytes 712712 | tf_op jit(solution)/shard_map/rows_ahead/ppermute | solution.py:302
  28.0 10.2 %collective-permute-start.14 = (bf16[16,7424]{1,0:T(8,128)(2,1)S(1)}, bf16[16,7424]{1,0:T(8,128)(2,1)S(1)}, u32[]{:S(2)}, u32[]{:S(2)}) collective-permute-start(bf16[16,7424]{1,0:T(8,128)(2,1)S(1)} %collective-permute-done.12.refs_1_), channel_id=1, source_target_pairs={{0,1},{2,3},{4,0},{6,2},{8,4},{10,6},{12,8},{14,10},{13,12},{15,14... | collective-permute-start | bytes 712712 | tf_op jit(solution)/shard_map/rows_behind/ppermute | solution.py:302
  29.6 10.2 %collective-permute-start.15 = (bf16[16,7424]{1,0:T(8,128)(2,1)S(1)}, bf16[16,7424]{1,0:T(8,128)(2,1)S(1)}, u32[]{:S(2)}, u32[]{:S(2)}) collective-permute-start(bf16[16,7424]{1,0:T(8,128)(2,1)S(1)} %collective-permute-done.13.refs_2_), channel_id=1, source_target_pairs={{0,4},{2,6},{4,8},{6,10},{8,12},{10,14},{12,13},{14,15},{13,9},{15... | collective-permute-start | bytes 712712 | tf_op jit(solution)/shard_map/rows_ahead/ppermute | solution.py:302
  33.1 10.8 %collective-permute-start.11 = (bf16[16,7424]{1,0:T(8,128)(2,1)S(1)}, bf16[16,7424]{1,0:T(8,128)(2,1)S(1)}, u32[]{:S(2)}, u32[]{:S(2)}) collective-permute-start(bf16[16,7424]{1,0:T(8,128)(2,1)S(1)} %collective-permute-done.10.refs_7_), channel_id=1, source_target_pairs={{0,1},{2,3},{4,0},{6,2},{8,4},{10,6},{12,8},{14,10},{13,12},{15,14... | collective-permute-start | bytes 712712 | tf_op jit(solution)/shard_map/rows_behind/ppermute | solution.py:302
  34.7 9.8 %collective-permute-start.8 = (bf16[16,7424]{1,0:T(8,128)(2,1)S(1)}, bf16[16,7424]{1,0:T(8,128)(2,1)S(1)}, u32[]{:S(2)}, u32[]{:S(2)}) collective-permute-start(bf16[16,7424]{1,0:T(8,128)(2,1)S(1)} %collective-permute-done.7.refs_4_), channel_id=1, source_target_pairs={{0,4},{2,6},{4,8},{6,10},{8,12},{10,14},{12,13},{14,15},{13,9},{15... | collective-permute-start | bytes 712712 | tf_op jit(solution)/shard_map/rows_ahead/ppermute | solution.py:302
  47.5 1.6 %collective-permute-start.16 = (f32[2,256,128]{2,1,0:T(8,128)S(1)}, f32[2,256,128]{2,1,0:T(8,128)S(1)}, u32[]{:S(2)}, u32[]{:S(2)}) collective-permute-start(f32[2,256,128]{2,1,0:T(8,128)S(1)} %get-tuple-element.48.partial), channel_id=1, source_target_pairs={{0,2},{2,0},{4,6},{6,4},{8,10},{10,8},{12,14},{14,12},{1,3},{3,1},... | collective-permute-start | bytes 786440 | tf_op jit(solution)/shard_map/ppermute | solution.py:380
  49.9 3.6 %collective-permute-start.17 = (f32[8,128]{1,0:T(8,128)S(1)}, f32[8,128]{1,0:T(8,128)S(1)}, u32[]{:S(2)}, u32[]{:S(2)}) collective-permute-start(f32[8,128]{1,0:T(8,128)S(1)} %get-tuple-element.50), channel_id=1, source_target_pairs={{0,1},{1,0},{2,3},{3,2},{4,5},{5,4},{6,7},{7,6},{8,9},{9,8},{10,11... | collective-permute-start | bytes 12296 | tf_op jit(solution)/shard_map/ppermute | solution.py:400
  51.5 5.7 %collective-permute-start.19 = (f32[128,128]{1,0:T(8,128)S(1)}, f32[128,128]{1,0:T(8,128)S(1)}, u32[]{:S(2)}, u32[]{:S(2)}) collective-permute-start(f32[128,128]{1,0:T(8,128)S(1)} %get-tuple-element.53), channel_id=1, source_target_pairs={{0,1},{1,0},{2,3},{3,2},{4,5},{5,4},{6,7},{7,6},{8,9},{9,8},{10,11... | collective-permute-start | bytes 196616 | tf_op jit(solution)/shard_map/ppermute | solution.py:402
  53.6 4.8 %collective-permute-start.18 = (f32[8,128]{1,0:T(8,128)S(1)}, f32[8,128]{1,0:T(8,128)S(1)}, u32[]{:S(2)}, u32[]{:S(2)}) collective-permute-start(f32[8,128]{1,0:T(8,128)S(1)} %select_maximum_fusion.refs_0_), channel_id=1, source_target_pairs={{0,4},{2,10},{4,0},{6,14},{8,12},{10,2},{12,8},{14,6},{1,5},{3,11}... | collective-permute-start | bytes 12296 | tf_op jit(solution)/shard_map/ppermute | solution.py:418
  54.8 5.4 %collective-permute-start.21 = (f32[8,128]{1,0:T(8,128)S(1)}, f32[8,128]{1,0:T(8,128)S(1)}, u32[]{:S(2)}, u32[]{:S(2)}) collective-permute-start(f32[8,128]{1,0:T(8,128)S(1)} %select_maximum_fusion.refs_0_), channel_id=1, source_target_pairs={{0,12},{2,14},{4,8},{6,10},{8,4},{10,6},{12,0},{14,2},{1,13},{3,15... | collective-permute-start | bytes 12296 | tf_op jit(solution)/shard_map/ppermute | solution.py:419
  58.3 1.9 %collective-permute-start.20 = (f32[8,128]{1,0:T(8,128)S(1)}, f32[8,128]{1,0:T(8,128)S(1)}, u32[]{:S(2)}, u32[]{:S(2)}) collective-permute-start(f32[8,128]{1,0:T(8,128)S(1)} %collective-permute-done.18.refs_1_), channel_id=1, source_target_pairs={{0,2},{2,0},{4,6},{6,4},{8,10},{10,8},{12,14},{14,12},{1,3},{3,1},... | collective-permute-start | bytes 12296 | tf_op jit(solution)/shard_map/ppermute | solution.py:421

commit v20 on v19

--- a/solution.py
+++ b/solution.py
@@ -316,7 +316,10 @@
         compiler_params=params,
     )(spot, planes, facts)
 
-    _, panels = lax.optimization_barrier((kept, panels))
+    with jax.named_scope("mate_rows"):
+        got = lax.ppermute(given, "orient", mate_pairs)
+
+    _, panels = lax.optimization_barrier((got, panels))
     sides = lax.optimization_barrier(jnp.transpose(panels[0, 0], (1, 0, 2)))
     panel_shape = jax.ShapeDtypeStruct(sides.shape[1:], sides.dtype)
     own_panel, given_panel = pl.pallas_call(
@@ -330,7 +333,7 @@
         mate_panel = lax.ppermute(given_panel, "orient", mate_pairs)
 
     noise = noise_weight[None, :]
-    waiting = []
+    waiting = [((0, False), kept), ((0, True), got)]
     ahead = {False: kept, True: given}
     behind = {False: kept, True: given}
     orders, earlier, late = [], [], []
@@ -351,7 +354,7 @@
             for chain, c in ((ahead, False), (behind, True)):
                 chain[c] = lax.optimization_barrier((chain[c], earlier[-1][2]))[0]
         if step == 2:
-            for chain, c in ((ahead, False), (behind, True)):
+            for chain, c in ((ahead, False), (behind, False)):
                 chain[c] = lax.optimization_barrier((chain[c], squares))[0]
         waiting = waiting + late
         late = []
@@ -364,11 +367,6 @@
                 with jax.named_scope("rows_behind"):
                     behind[crossed] = forward(behind[crossed], -1, int(crossed and step == 1))
                 late.append(((step, crossed), behind[crossed]))
-        if step == 1:
-            late_given, _ = lax.optimization_barrier((given, kept))
-            with jax.named_scope("mate_rows"):
-                got = lax.ppermute(late_given, "orient", mate_pairs)
-            late = [((0, False), kept), ((0, True), got)] + late
     orders.append([key for key, _ in waiting])
     earlier.append(score([c for _, c in waiting]))
     waiting = late

time: 61.2 us -> 61.3 us (level)
  waiting for transfers between devices: 15.1 us -> 19 us
  starting transfers between devices: 24.9 us -> 21.1 us
    ppermute x14, waiting for transfers between devices: 10.9 us -> 14.8 us  [forward(): return lax.ppermute(values, ('orient', 'cls'), pairs)]
    ppermute x14, starting transfers between devices: 17.1 us -> 14.4 us  [forward(): return lax.ppermute(values, ('orient', 'cls'), pairs)]
    ppermute x1, starting transfers between devices: 1.2 us -> 0.52 us  [chip_shards(): got = lax.ppermute(given, 'orient', mate_pairs)]
  transfers between devices with their start and end apart: 22 -> 22, of which waited for: 10 -> 11; matrix products, arithmetic and copies ran while one was open for 4% -> 4% of each run, Pallas kernels for 17% -> 17%
where the time goes in v20:
time: 61.3 us; the launch traced here: 61 us
  starting transfers between devices  21.1 us (34%)
  waiting for transfers between devices  19 us (31%)
  Pallas kernels  15.9 us (26%)
  local copies, waits for them, and re-layouts  3.52 us (6%)
  other arithmetic  1.45 us (2%)
    ppermute x14, waiting for transfers between devices, forward(): return lax.ppermute(values, ('orient', 'cls'), pairs)  14.8 us
    ppermute x14, starting transfers between devices, forward(): return lax.ppermute(values, ('orient', 'cls'), pairs)  14.4 us
    pallas_call x3, Pallas kernels, score_call(): pl.pallas_call(kernel, in_specs=[pl.BlockSpec(memory_space=pltpu.SMEM)] +...  11.1 us
    ppermute x1, starting transfers between devices, chip_shards(): far = lax.ppermute(pair, 'orient', [(d, d ^ 6) for d in range(devices)])  2.47 us
    optimization_barrier x1, local copies, waits for them, and re-layouts, chip_shards(): _, panels = lax.optimization_barrier((got, panels))  2.42 us
    ppermute x1, waiting for transfers between devices, chip_shards(): far = lax.ppermute(pair, 'orient', [(d, d ^ 6) for d in range(devices)])  1.77 us
    ppermute x1, starting transfers between devices, chip_shards(): x_stats = lax.ppermute(stats, 'cls', x_pairs)  1.61 us
    ppermute x1, waiting for transfers between devices, chip_shards(): x_stats = lax.ppermute(stats, 'cls', x_pairs)  1.58 us
  transfers between devices with their start and end apart: 22, of which 11 were waited for; matrix products, arithmetic and copies ran while one was open for 4% of the time, Pallas kernels for 17%

profile of v20, /device:TPU:0, one launch (start us, length us, event | category | flops | bytes accessed | tf_op | source)
XLA Modules:
  0.0 61.0 jit_solution(6857333745694008148)
XLA Ops:
  0.0 1.1 %copy.11 = bf16[1,16,2,7296]{3,1,2,0:T(8,128)(2,1)S(1)} copy(bf16[1,16,2,7296]{3,2,1,0:T(2,128)(2,1)} %param.5) | data formatting | bytes 933888 | tf_op args[0]
  1.1 0.7 %convert_bitcast_fusion = bf16[4,16]{1,0:T(4,128)(2,1)S(1)} fusion(s32[1,16,4]{1,2,0:T(4,128)} %param.7), kind=kLoop, calls=%fused_computation.12 | loop fusion | flops 64 | bytes 384 | tf_op jit(solution)/shard_map/convert_element_type | solution.py:308
  1.8 0.7 %fusion.5.facts = bf16[16,128]{1,0:T(8,128)(2,1)S(1)} fusion(bf16[4,16]{1,0:T(4,128)(2,1)S(1)} %convert_bitcast_fusion, bf16[1,16]{1,0:T(2,128)(2,1)} %param.6), kind=kLoop, calls=%fused_computation.9 | loop fusion | flops 22528 | bytes 4256 | tf_op jit(solution)/shard_map/concatenate | solution.py:308
  2.4 0.1 pad_add_fusion.spot
  2.5 0.6 shard_map.55
  3.1 0.5 collective-permute-start.1
  3.6 2.6 %collective-permute-start.5 = (bf16[16,7424]{1,0:T(8,128)(2,1)S(1)}, bf16[16,7424]{1,0:T(8,128)(2,1)S(1)}, u32[]{:S(2)}, u32[]{:S(2)}) collective-permute-start(bf16[16,7424]{1,0:T(8,128)(2,1)S(1)} %get-tuple-element.32), channel_id=1, source_target_pairs={{0,3},{2,1},{4,2},{6,0},{8,6},{10,4},{12,10},{14,8},{13,14},{15,12... | collective-permute-start | bytes 712712 | tf_op jit(solution)/shard_map/rows_behind/ppermute | solution.py:302
  6.2 0.1 collective-permute-start
  6.3 1.9 %collective-permute-start.3 = (bf16[16,7424]{1,0:T(8,128)(2,1)S(1)}, bf16[16,7424]{1,0:T(8,128)(2,1)S(1)}, u32[]{:S(2)}, u32[]{:S(2)}) collective-permute-start(bf16[16,7424]{1,0:T(8,128)(2,1)S(1)} %get-tuple-element.31.refs_0_), channel_id=1, source_target_pairs={{0,1},{2,3},{4,0},{6,2},{8,4},{10,6},{12,8},{14,10},{13,12},{15,14... | collective-permute-start | bytes 712712 | tf_op jit(solution)/shard_map/rows_behind/ppermute | solution.py:302
  8.2 2.4 %copy.10 = bf16[1,1,128,2,7296]{4,2,3,1,0:T(8,128)(2,1)S(1)} copy(bf16[1,1,128,2,7296]{4,3,2,1,0:T(2,128)(2,1)} %param.9) | data formatting | bytes 7471104 | tf_op jit(solution)/shard_map/optimization_barrier | solution.py:322
  10.7 0.8 %shard_map.56 = (bf16[128,7296]{1,0:T(8,128)(2,1)S(1)}, bf16[128,7296]{1,0:T(8,128)(2,1)S(1)}) custom-call(s32[4]{0:T(128)S(1)} %pad_add_fusion.spot, bf16[2,128,7296]{2,1,0:T(8,128)(2,1)S(1)} %bitcast.19), custom_call_target="tpu_custom_call" | custom-call | tf_op jit(solution)/shard_map/pallas_call | solution.py:325
  11.5 0.3 collective-permute-start.6
  11.8 0.6 %collective-permute-done.5.refs_5_ = bf16[16,7424]{1,0:T(8,128)(2,1)S(1)} collective-permute-done((bf16[16,7424]{1,0:T(8,128)(2,1)S(1)}, bf16[16,7424]{1,0:T(8,128)(2,1)S(1)}, u32[]{:S(2)}, u32[]{:S(2)}) %collective-permute-start.5) | collective-permute-done | bytes 237600 | tf_op jit(solution)/shard_map/rows_behind/ppermute | solution.py:302
  12.4 1.5 %collective-permute-start.9 = (bf16[16,7424]{1,0:T(8,128)(2,1)S(1)}, bf16[16,7424]{1,0:T(8,128)(2,1)S(1)}, u32[]{:S(2)}, u32[]{:S(2)}) collective-permute-start(bf16[16,7424]{1,0:T(8,128)(2,1)S(1)} %collective-permute-done.5.refs_5_), channel_id=1, source_target_pairs={{0,1},{2,3},{4,0},{6,2},{8,4},{10,6},{12,8},{14,10},{13,12},{15,14... | collective-permute-start | bytes 712712 | tf_op jit(solution)/shard_map/rows_behind/ppermute | solution.py:302
  13.9 0.1 shard_map.57.refs_8_.refs_10_.refs_4_
  14.0 0.8 %collective-permute-done.refs_2_ = bf16[16,7424]{1,0:T(8,128)(2,1)S(1)} collective-permute-done((bf16[16,7424]{1,0:T(8,128)(2,1)S(1)}, bf16[16,7424]{1,0:T(8,128)(2,1)S(1)}, u32[]{:S(2)}, u32[]{:S(2)}) %collective-permute-start) | collective-permute-done | bytes 237600 | tf_op jit(solution)/shard_map/rows_ahead/ppermute | solution.py:302
  14.8 0.1 collective-permute-start.2
  15.0 3.0 %collective-permute-done.3.refs_3_ = bf16[16,7424]{1,0:T(8,128)(2,1)S(1)} collective-permute-done((bf16[16,7424]{1,0:T(8,128)(2,1)S(1)}, bf16[16,7424]{1,0:T(8,128)(2,1)S(1)}, u32[]{:S(2)}, u32[]{:S(2)}) %collective-permute-start.3) | collective-permute-done | bytes 237600 | tf_op jit(solution)/shard_map/rows_behind/ppermute | solution.py:302
  18.0 1.9 %collective-permute-start.12 = (bf16[16,7424]{1,0:T(8,128)(2,1)S(1)}, bf16[16,7424]{1,0:T(8,128)(2,1)S(1)}, u32[]{:S(2)}, u32[]{:S(2)}) collective-permute-start(bf16[16,7424]{1,0:T(8,128)(2,1)S(1)} %collective-permute-done.3.refs_3_), channel_id=1, source_target_pairs={{0,1},{2,3},{4,0},{6,2},{8,4},{10,6},{12,8},{14,10},{13,12},{15,14... | collective-permute-start | bytes 712712 | tf_op jit(solution)/shard_map/rows_behind/ppermute | solution.py:302
  19.9 0.1 collective-permute-start.13
  20.0 3.8 %shard_map.58 = (f32[96,128]{1,0:T(8,128)S(1)}, f32[96,128]{1,0:T(8,128)S(1)}, f32[96,128]{1,0:T(8,128)S(1)}) custom-call(s32[4]{0:T(128)S(1)} %pad_add_fusion.spot, bf16[16,7424]{1,0:T(8,128)(2,1)S(1)} %get-tuple-element.31.refs_0_, bf16[16,7424]{1,0:T(8,128)(2,1)S(1)} %collective-permute-done.1.refs_1_, bf16[16,7424]{1,0:T(8,128)(2,1)S(1)} %collective-permute-done.refs_2_, ...), custom_call_target="tpu_custom_call" | custom-call | flops 956301312 | bytes 5136384 | tf_op jit(solution)/shard_map/pallas_call | solution.py:175
  23.8 2.0 %collective-permute-start.10 = (bf16[16,7424]{1,0:T(8,128)(2,1)S(1)}, bf16[16,7424]{1,0:T(8,128)(2,1)S(1)}, u32[]{:S(2)}, u32[]{:S(2)}) collective-permute-start(bf16[16,7424]{1,0:T(8,128)(2,1)S(1)} %collective-permute-done.9.refs_3_), channel_id=1, source_target_pairs={{0,1},{2,3},{4,0},{6,2},{8,4},{10,6},{12,8},{14,10},{13,12},{15,14... | collective-permute-start | bytes 712712 | tf_op jit(solution)/shard_map/rows_behind/ppermute | solution.py:302
  25.8 0.2 collective-permute-start.7
  26.0 2.2 %collective-permute-done.12.refs_1_ = bf16[16,7424]{1,0:T(8,128)(2,1)S(1)} collective-permute-done((bf16[16,7424]{1,0:T(8,128)(2,1)S(1)}, bf16[16,7424]{1,0:T(8,128)(2,1)S(1)}, u32[]{:S(2)}, u32[]{:S(2)}) %collective-permute-start.12) | collective-permute-done | bytes 237600 | tf_op jit(solution)/shard_map/rows_behind/ppermute | solution.py:302
  28.1 1.9 %collective-permute-start.14 = (bf16[16,7424]{1,0:T(8,128)(2,1)S(1)}, bf16[16,7424]{1,0:T(8,128)(2,1)S(1)}, u32[]{:S(2)}, u32[]{:S(2)}) collective-permute-start(bf16[16,7424]{1,0:T(8,128)(2,1)S(1)} %collective-permute-done.12.refs_1_), channel_id=1, source_target_pairs={{0,1},{2,3},{4,0},{6,2},{8,4},{10,6},{12,8},{14,10},{13,12},{15,14... | collective-permute-start | bytes 712712 | tf_op jit(solution)/shard_map/rows_behind/ppermute | solution.py:302
  30.1 0.0 collective-permute-done.13.refs_2_
  30.1 0.1 collective-permute-start.15
  30.2 3.0 %collective-permute-done.10.refs_7_ = bf16[16,7424]{1,0:T(8,128)(2,1)S(1)} collective-permute-done((bf16[16,7424]{1,0:T(8,128)(2,1)S(1)}, bf16[16,7424]{1,0:T(8,128)(2,1)S(1)}, u32[]{:S(2)}, u32[]{:S(2)}) %collective-permute-start.10) | collective-permute-done | bytes 237600 | tf_op jit(solution)/shard_map/rows_behind/ppermute | solution.py:302
  33.2 1.9 %collective-permute-start.11 = (bf16[16,7424]{1,0:T(8,128)(2,1)S(1)}, bf16[16,7424]{1,0:T(8,128)(2,1)S(1)}, u32[]{:S(2)}, u32[]{:S(2)}) collective-permute-start(bf16[16,7424]{1,0:T(8,128)(2,1)S(1)} %collective-permute-done.10.refs_7_), channel_id=1, source_target_pairs={{0,1},{2,3},{4,0},{6,2},{8,4},{10,6},{12,8},{14,10},{13,12},{15,14... | collective-permute-start | bytes 712712 | tf_op jit(solution)/shard_map/rows_behind/ppermute | solution.py:302
  35.2 0.1 collective-permute-start.8
  35.3 3.0 %collective-permute-done.14.refs_5_ = bf16[16,7424]{1,0:T(8,128)(2,1)S(1)} collective-permute-done((bf16[16,7424]{1,0:T(8,128)(2,1)S(1)}, bf16[16,7424]{1,0:T(8,128)(2,1)S(1)}, u32[]{:S(2)}, u32[]{:S(2)}) %collective-permute-start.14) | collective-permute-done | bytes 237600 | tf_op jit(solution)/shard_map/rows_behind/ppermute | solution.py:302
  38.3 2.0 %collective-permute-done.15.refs_6_ = bf16[16,7424]{1,0:T(8,128)(2,1)S(1)} collective-permute-done((bf16[16,7424]{1,0:T(8,128)(2,1)S(1)}, bf16[16,7424]{1,0:T(8,128)(2,1)S(1)}, u32[]{:S(2)}, u32[]{:S(2)}) %collective-permute-start.15) | collective-permute-done | bytes 237600 | tf_op jit(solution)/shard_map/rows_ahead/ppermute | solution.py:302
  40.3 4.1 %shard_map.59 = (f32[128,128]{1,0:T(8,128)S(1)}, f32[128,128]{1,0:T(8,128)S(1)}, f32[128,128]{1,0:T(8,128)S(1)}) custom-call(s32[4]{0:T(128)S(1)} %pad_add_fusion.spot, bf16[16,7424]{1,0:T(8,128)(2,1)S(1)} %collective-permute-done.2.refs_0_, bf16[16,7424]{1,0:T(8,128)(2,1)S(1)} %collective-permute-done.12.refs_1_, ...), custom_call_target="tpu_custom_call" | custom-call | flops 956301312 | bytes 5603328 | tf_op jit(solution)/shard_map/pallas_call | solution.py:175
  44.4 0.1 collective-permute-done.8.refs_0_
  44.5 3.1 %shard_map.60 = (f32[2,256,128]{2,1,0:T(8,128)S(1)}, f32[256,128]{1,0:T(8,128)S(1)}) custom-call(s32[4]{0:T(128)S(1)} %pad_add_fusion.spot, bf16[16,7424]{1,0:T(8,128)(2,1)S(1)} %collective-permute-done.8.refs_0_, bf16[16,7424]{1,0:T(8,128)(2,1)S(1)} %collective-permute-done.11.refs_1_, f32[1,7296]{1,0:T(1,128)S(1)} %broadcast_in_dim.3.refs_6_.refs_8_.refs_2_, ...), custom_call_target="tpu_custom_call" | custom-call | flops 956301312 | bytes 4202496 | tf_op jit(solution)/shard_map/pallas_call | solution.py:175
  47.6 0.0 collective-permute-start.16
  47.7 0.7 %shard_map.61.masks = f32[2,256,128]{2,1,0:T(8,128)S(1)} custom-call(s32[4]{0:T(128)S(1)} %pad_add_fusion.spot, f32[256,128]{1,0:T(8,128)S(1)} %get-tuple-element.47.facts), custom_call_target="tpu_custom_call" | custom-call | tf_op jit(solution)/shard_map/pallas_call | solution.py:379
  48.4 0.8 %collective-permute-done.16.mate = f32[2,256,128]{2,1,0:T(8,128)S(1)} collective-permute-done((f32[2,256,128]{2,1,0:T(8,128)S(1)}, f32[2,256,128]{2,1,0:T(8,128)S(1)}, u32[]{:S(2)}, u32[]{:S(2)}) %collective-permute-start.16) | collective-permute-done | bytes 262176 | tf_op jit(solution)/shard_map/ppermute | solution.py:378
  49.2 0.8 %shard_map.62 = (f32[128,128]{1,0:T(8,128)S(1)}, f32[128,128]{1,0:T(8,128)S(1)}, f32[8,128]{1,0:T(8,128)S(1)}) custom-call(s32[4]{0:T(128)S(1)} %pad_add_fusion.spot, f32[2,256,128]{2,1,0:T(8,128)S(1)} %get-tuple-element.46.partial, f32[2,256,128]{2,1,0:T(8,128)S(1)} %collective-permute-done.16.mate, f32[2,256,128]{2,1,0:T(8,128)S(1)} %shard_map.61.masks), custom_call_target="tpu_custom_call" | custom-call | tf_op jit(solution)/shard_map/pallas_call | solution.py:386
  50.0 1.6 %collective-permute-start.17 = (f32[8,128]{1,0:T(8,128)S(1)}, f32[8,128]{1,0:T(8,128)S(1)}, u32[]{:S(2)}, u32[]{:S(2)}) collective-permute-start(f32[8,128]{1,0:T(8,128)S(1)} %get-tuple-element.48), channel_id=1, source_target_pairs={{0,1},{1,0},{2,3},{3,2},{4,5},{5,4},{6,7},{7,6},{8,9},{9,8},{10,11... | collective-permute-start | bytes 12296 | tf_op jit(solution)/shard_map/ppermute | solution.py:398
  51.6 0.4 collective-permute-start.19
  52.0 1.6 %collective-permute-done.17 = f32[8,128]{1,0:T(8,128)S(1)} collective-permute-done((f32[8,128]{1,0:T(8,128)S(1)}, f32[8,128]{1,0:T(8,128)S(1)}, u32[]{:S(2)}, u32[]{:S(2)}) %collective-permute-start.17) | collective-permute-done | bytes 4128 | tf_op jit(solution)/shard_map/ppermute | solution.py:398
  53.6 1.2 %collective-permute-start.18 = (f32[8,128]{1,0:T(8,128)S(1)}, f32[8,128]{1,0:T(8,128)S(1)}, u32[]{:S(2)}, u32[]{:S(2)}) collective-permute-start(f32[8,128]{1,0:T(8,128)S(1)} %select_maximum_fusion.refs_0_), channel_id=1, source_target_pairs={{0,4},{2,10},{4,0},{6,14},{8,12},{10,2},{12,8},{14,6},{1,5},{3,11}... | collective-permute-start | bytes 12296 | tf_op jit(solution)/shard_map/ppermute | solution.py:416
  54.8 2.5 %collective-permute-start.21 = (f32[8,128]{1,0:T(8,128)S(1)}, f32[8,128]{1,0:T(8,128)S(1)}, u32[]{:S(2)}, u32[]{:S(2)}) collective-permute-start(f32[8,128]{1,0:T(8,128)S(1)} %select_maximum_fusion.refs_0_), channel_id=1, source_target_pairs={{0,12},{2,14},{4,8},{6,10},{8,4},{10,6},{12,0},{14,2},{1,13},{3,15... | collective-permute-start | bytes 12296 | tf_op jit(solution)/shard_map/ppermute | solution.py:417
  57.3 1.1 %shard_map.63 = (f32[128,256]{1,0:T(8,128)S(1)}, f32[128,128]{1,0:T(8,128)S(1)}, f32[8,128]{1,0:T(8,128)S(1)}) custom-call(s32[4]{0:T(128)S(1)} %pad_add_fusion.spot, f32[128,128]{1,0:T(8,128)S(1)} %get-tuple-element.49.mine, f32[128,128]{1,0:T(8,128)S(1)} %collective-permute-done.19.across, f32[256,128]{1,0:T(8,128)S(1)} %get-tuple-element.47.facts), custom_call_target="tpu_custom_call" | custom-call | tf_op jit(solution)/shard_map/pallas_call | solution.py:404
  58.4 0.1 collective-permute-start.20
  58.5 1.8 %collective-permute-done.21.refs_3_ = f32[8,128]{1,0:T(8,128)S(1)} collective-permute-done((f32[8,128]{1,0:T(8,128)S(1)}, f32[8,128]{1,0:T(8,128)S(1)}, u32[]{:S(2)}, u32[]{:S(2)}) %collective-permute-start.21) | collective-permute-done | bytes 4128 | tf_op jit(solution)/shard_map/ppermute | solution.py:417
  60.3 0.8 %shard_map.64 = f32[128,256]{1,0:T(8,128)} custom-call(f32[8,128]{1,0:T(8,128)S(1)} %select_maximum_fusion.refs_0_, f32[8,128]{1,0:T(8,128)S(1)} %collective-permute-done.18.refs_1_, f32[8,128]{1,0:T(8,128)S(1)} %collective-permute-done.20.refs_2_, f32[8,128]{1,0:T(8,128)S(1)} %collective-permute-done.21.refs_3_, f32[8,128]{1,0:T(8,128)S(1)} %get-tuple-element.54.refs_4_, ...), custom_call_target="tpu_custom_call" | custom-call | tf_op jit(solution)/shard_map/pallas_call | solution.py:425
  (16 shorter events, 0.1 us)
Async XLA Ops:
  3.1 5.2 %collective-permute-start.1 = (bf16[16,7424]{1,0:T(8,128)(2,1)S(1)}, bf16[16,7424]{1,0:T(8,128)(2,1)S(1)}, u32[]{:S(2)}, u32[]{:S(2)}) collective-permute-start(bf16[16,7424]{1,0:T(8,128)(2,1)S(1)} %get-tuple-element.32), channel_id=1, source_target_pairs={{0,2},{2,0},{4,6},{6,4},{8,10},{10,8},{12,14},{14,12},{1,3},{3,1},... | collective-permute-start | bytes 712712 | tf_op jit(solution)/shard_map/mate_rows/ppermute | solution.py:320
  3.6 8.8 %collective-permute-start.5 = (bf16[16,7424]{1,0:T(8,128)(2,1)S(1)}, bf16[16,7424]{1,0:T(8,128)(2,1)S(1)}, u32[]{:S(2)}, u32[]{:S(2)}) collective-permute-start(bf16[16,7424]{1,0:T(8,128)(2,1)S(1)} %get-tuple-element.32), channel_id=1, source_target_pairs={{0,3},{2,1},{4,2},{6,0},{8,6},{10,4},{12,10},{14,8},{13,14},{15,12... | collective-permute-start | bytes 712712 | tf_op jit(solution)/shard_map/rows_behind/ppermute | solution.py:302
  6.2 8.6 %collective-permute-start = (bf16[16,7424]{1,0:T(8,128)(2,1)S(1)}, bf16[16,7424]{1,0:T(8,128)(2,1)S(1)}, u32[]{:S(2)}, u32[]{:S(2)}) collective-permute-start(bf16[16,7424]{1,0:T(8,128)(2,1)S(1)} %get-tuple-element.31.refs_0_), channel_id=1, source_target_pairs={{0,4},{2,6},{4,8},{6,10},{8,12},{10,14},{12,13},{14,15},{13,9},{15... | collective-permute-start | bytes 712712 | tf_op jit(solution)/shard_map/rows_ahead/ppermute | solution.py:302
  6.3 11.6 %collective-permute-start.3 = (bf16[16,7424]{1,0:T(8,128)(2,1)S(1)}, bf16[16,7424]{1,0:T(8,128)(2,1)S(1)}, u32[]{:S(2)}, u32[]{:S(2)}) collective-permute-start(bf16[16,7424]{1,0:T(8,128)(2,1)S(1)} %get-tuple-element.31.refs_0_), channel_id=1, source_target_pairs={{0,1},{2,3},{4,0},{6,2},{8,4},{10,6},{12,8},{14,10},{13,12},{15,14... | collective-permute-start | bytes 712712 | tf_op jit(solution)/shard_map/rows_behind/ppermute | solution.py:302
  8.2 11.7 %collective-permute-start.4 = (bf16[16,7424]{1,0:T(8,128)(2,1)S(1)}, bf16[16,7424]{1,0:T(8,128)(2,1)S(1)}, u32[]{:S(2)}, u32[]{:S(2)}) collective-permute-start(bf16[16,7424]{1,0:T(8,128)(2,1)S(1)} %get-tuple-element.32), channel_id=1, source_target_pairs={{0,6},{2,4},{4,10},{6,8},{8,14},{10,12},{12,15},{14,13},{13,11},{1... | collective-permute-start | bytes 712712 | tf_op jit(solution)/shard_map/rows_ahead/ppermute | solution.py:302
  11.5 8.5 %collective-permute-start.6 = (bf16[128,7296]{1,0:T(8,128)(2,1)S(1)}, bf16[128,7296]{1,0:T(8,128)(2,1)S(1)}, u32[]{:S(2)}, u32[]{:S(2)}) collective-permute-start(bf16[128,7296]{1,0:T(8,128)(2,1)S(1)} %get-tuple-element.36), channel_id=1, source_target_pairs={{0,2},{2,0},{4,6},{6,4},{8,10},{10,8},{12,14},{14,12},{1,3},{3,1},... | collective-permute-start | bytes 5603336 | tf_op jit(solution)/shard_map/mate_panel/ppermute | solution.py:333
  12.4 11.5 %collective-permute-start.9 = (bf16[16,7424]{1,0:T(8,128)(2,1)S(1)}, bf16[16,7424]{1,0:T(8,128)(2,1)S(1)}, u32[]{:S(2)}, u32[]{:S(2)}) collective-permute-start(bf16[16,7424]{1,0:T(8,128)(2,1)S(1)} %collective-permute-done.5.refs_5_), channel_id=1, source_target_pairs={{0,1},{2,3},{4,0},{6,2},{8,4},{10,6},{12,8},{14,10},{13,12},{15,14... | collective-permute-start | bytes 712712 | tf_op jit(solution)/shard_map/rows_behind/ppermute | solution.py:302
  13.9 1.0 %copy-start = (f32[7296]{0:T(1024)S(1)}, f32[7296]{0:T(1024)}, u32[]{:S(2)}) copy-start(f32[7296]{0:T(1024)} %param.8) | copy-start | bytes 87556
  14.8 11.0 %collective-permute-start.2 = (bf16[16,7424]{1,0:T(8,128)(2,1)S(1)}, bf16[16,7424]{1,0:T(8,128)(2,1)S(1)}, u32[]{:S(2)}, u32[]{:S(2)}) collective-permute-start(bf16[16,7424]{1,0:T(8,128)(2,1)S(1)} %collective-permute-done.refs_2_), channel_id=1, source_target_pairs={{0,4},{2,6},{4,8},{6,10},{8,12},{10,14},{12,13},{14,15},{13,9},{15... | collective-permute-start | bytes 712712 | tf_op jit(solution)/shard_map/rows_ahead/ppermute | solution.py:302
  18.0 10.2 %collective-permute-start.12 = (bf16[16,7424]{1,0:T(8,128)(2,1)S(1)}, bf16[16,7424]{1,0:T(8,128)(2,1)S(1)}, u32[]{:S(2)}, u32[]{:S(2)}) collective-permute-start(bf16[16,7424]{1,0:T(8,128)(2,1)S(1)} %collective-permute-done.3.refs_3_), channel_id=1, source_target_pairs={{0,1},{2,3},{4,0},{6,2},{8,4},{10,6},{12,8},{14,10},{13,12},{15,14... | collective-permute-start | bytes 712712 | tf_op jit(solution)/shard_map/rows_behind/ppermute | solution.py:302
  19.9 10.2 %collective-permute-start.13 = (bf16[16,7424]{1,0:T(8,128)(2,1)S(1)}, bf16[16,7424]{1,0:T(8,128)(2,1)S(1)}, u32[]{:S(2)}, u32[]{:S(2)}) collective-permute-start(bf16[16,7424]{1,0:T(8,128)(2,1)S(1)} %collective-permute-done.4.refs_4_), channel_id=1, source_target_pairs={{0,4},{2,6},{4,8},{6,10},{8,12},{10,14},{12,13},{14,15},{13,9},{15... | collective-permute-start | bytes 712712 | tf_op jit(solution)/shard_map/rows_ahead/ppermute | solution.py:302
  23.8 9.4 %collective-permute-start.10 = (bf16[16,7424]{1,0:T(8,128)(2,1)S(1)}, bf16[16,7424]{1,0:T(8,128)(2,1)S(1)}, u32[]{:S(2)}, u32[]{:S(2)}) collective-permute-start(bf16[16,7424]{1,0:T(8,128)(2,1)S(1)} %collective-permute-done.9.refs_3_), channel_id=1, source_target_pairs={{0,1},{2,3},{4,0},{6,2},{8,4},{10,6},{12,8},{14,10},{13,12},{15,14... | collective-permute-start | bytes 712712 | tf_op jit(solution)/shard_map/rows_behind/ppermute | solution.py:302
  25.8 9.4 %collective-permute-start.7 = (bf16[16,7424]{1,0:T(8,128)(2,1)S(1)}, bf16[16,7424]{1,0:T(8,128)(2,1)S(1)}, u32[]{:S(2)}, u32[]{:S(2)}) collective-permute-start(bf16[16,7424]{1,0:T(8,128)(2,1)S(1)} %collective-permute-done.2.refs_0_), channel_id=1, source_target_pairs={{0,4},{2,6},{4,8},{6,10},{8,12},{10,14},{12,13},{14,15},{13,9},{15... | collective-permute-start | bytes 712712 | tf_op jit(solution)/shard_map/rows_ahead/ppermute | solution.py:302
  28.1 10.2 %collective-permute-start.14 = (bf16[16,7424]{1,0:T(8,128)(2,1)S(1)}, bf16[16,7424]{1,0:T(8,128)(2,1)S(1)}, u32[]{:S(2)}, u32[]{:S(2)}) collective-permute-start(bf16[16,7424]{1,0:T(8,128)(2,1)S(1)} %collective-permute-done.12.refs_1_), channel_id=1, source_target_pairs={{0,1},{2,3},{4,0},{6,2},{8,4},{10,6},{12,8},{14,10},{13,12},{15,14... | collective-permute-start | bytes 712712 | tf_op jit(solution)/shard_map/rows_behind/ppermute | solution.py:302
  30.1 10.2 %collective-permute-start.15 = (bf16[16,7424]{1,0:T(8,128)(2,1)S(1)}, bf16[16,7424]{1,0:T(8,128)(2,1)S(1)}, u32[]{:S(2)}, u32[]{:S(2)}) collective-permute-start(bf16[16,7424]{1,0:T(8,128)(2,1)S(1)} %collective-permute-done.13.refs_2_), channel_id=1, source_target_pairs={{0,4},{2,6},{4,8},{6,10},{8,12},{10,14},{12,13},{14,15},{13,9},{15... | collective-permute-start | bytes 712712 | tf_op jit(solution)/shard_map/rows_ahead/ppermute | solution.py:302
  33.2 11.2 %collective-permute-start.11 = (bf16[16,7424]{1,0:T(8,128)(2,1)S(1)}, bf16[16,7424]{1,0:T(8,128)(2,1)S(1)}, u32[]{:S(2)}, u32[]{:S(2)}) collective-permute-start(bf16[16,7424]{1,0:T(8,128)(2,1)S(1)} %collective-permute-done.10.refs_7_), channel_id=1, source_target_pairs={{0,1},{2,3},{4,0},{6,2},{8,4},{10,6},{12,8},{14,10},{13,12},{15,14... | collective-permute-start | bytes 712712 | tf_op jit(solution)/shard_map/rows_behind/ppermute | solution.py:302
  35.2 9.3 %collective-permute-start.8 = (bf16[16,7424]{1,0:T(8,128)(2,1)S(1)}, bf16[16,7424]{1,0:T(8,128)(2,1)S(1)}, u32[]{:S(2)}, u32[]{:S(2)}) collective-permute-start(bf16[16,7424]{1,0:T(8,128)(2,1)S(1)} %collective-permute-done.7.refs_4_), channel_id=1, source_target_pairs={{0,4},{2,6},{4,8},{6,10},{8,12},{10,14},{12,13},{14,15},{13,9},{15... | collective-permute-start | bytes 712712 | tf_op jit(solution)/shard_map/rows_ahead/ppermute | solution.py:302
  47.6 1.6 %collective-permute-start.16 = (f32[2,256,128]{2,1,0:T(8,128)S(1)}, f32[2,256,128]{2,1,0:T(8,128)S(1)}, u32[]{:S(2)}, u32[]{:S(2)}) collective-permute-start(f32[2,256,128]{2,1,0:T(8,128)S(1)} %get-tuple-element.46.partial), channel_id=1, source_target_pairs={{0,2},{2,0},{4,6},{6,4},{8,10},{10,8},{12,14},{14,12},{1,3},{3,1},... | collective-permute-start | bytes 786440 | tf_op jit(solution)/shard_map/ppermute | solution.py:378
  50.0 3.6 %collective-permute-start.17 = (f32[8,128]{1,0:T(8,128)S(1)}, f32[8,128]{1,0:T(8,128)S(1)}, u32[]{:S(2)}, u32[]{:S(2)}) collective-permute-start(f32[8,128]{1,0:T(8,128)S(1)} %get-tuple-element.48), channel_id=1, source_target_pairs={{0,1},{1,0},{2,3},{3,2},{4,5},{5,4},{6,7},{7,6},{8,9},{9,8},{10,11... | collective-permute-start | bytes 12296 | tf_op jit(solution)/shard_map/ppermute | solution.py:398
  51.6 5.7 %collective-permute-start.19 = (f32[128,128]{1,0:T(8,128)S(1)}, f32[128,128]{1,0:T(8,128)S(1)}, u32[]{:S(2)}, u32[]{:S(2)}) collective-permute-start(f32[128,128]{1,0:T(8,128)S(1)} %get-tuple-element.51), channel_id=1, source_target_pairs={{0,1},{1,0},{2,3},{3,2},{4,5},{5,4},{6,7},{7,6},{8,9},{9,8},{10,11... | collective-permute-start | bytes 196616 | tf_op jit(solution)/shard_map/ppermute | solution.py:400
  53.6 4.8 %collective-permute-start.18 = (f32[8,128]{1,0:T(8,128)S(1)}, f32[8,128]{1,0:T(8,128)S(1)}, u32[]{:S(2)}, u32[]{:S(2)}) collective-permute-start(f32[8,128]{1,0:T(8,128)S(1)} %select_maximum_fusion.refs_0_), channel_id=1, source_target_pairs={{0,4},{2,10},{4,0},{6,14},{8,12},{10,2},{12,8},{14,6},{1,5},{3,11}... | collective-permute-start | bytes 12296 | tf_op jit(solution)/shard_map/ppermute | solution.py:416
  54.8 5.4 %collective-permute-start.21 = (f32[8,128]{1,0:T(8,128)S(1)}, f32[8,128]{1,0:T(8,128)S(1)}, u32[]{:S(2)}, u32[]{:S(2)}) collective-permute-start(f32[8,128]{1,0:T(8,128)S(1)} %select_maximum_fusion.refs_0_), channel_id=1, source_target_pairs={{0,12},{2,14},{4,8},{6,10},{8,4},{10,6},{12,0},{14,2},{1,13},{3,15... | collective-permute-start | bytes 12296 | tf_op jit(solution)/shard_map/ppermute | solution.py:417
  58.4 1.9 %collective-permute-start.20 = (f32[8,128]{1,0:T(8,128)S(1)}, f32[8,128]{1,0:T(8,128)S(1)}, u32[]{:S(2)}, u32[]{:S(2)}) collective-permute-start(f32[8,128]{1,0:T(8,128)S(1)} %collective-permute-done.18.refs_1_), channel_id=1, source_target_pairs={{0,2},{2,0},{4,6},{6,4},{8,10},{10,8},{12,14},{14,12},{1,3},{3,1},... | collective-permute-start | bytes 12296 | tf_op jit(solution)/shard_map/ppermute | solution.py:419
